TPU v7x, 32 devices: a whole 2x2x4 slice. The times are simulated.
32 devices in a mesh: groups: 2 (over y), dp: 4 (over x, core), proj: 4 (over z).
Axes of the slice: x: 2, y: 2, z: 4, core: 2. Of those that a mesh axis runs over, the one named last changes fastest.
Arguments:
- queries: bfloat16 [2048, 64, 128], P(('groups', 'dp'), 'proj'), parts along dimension 0, may hold values from -6 to 6
- train_grads: bfloat16 [4096, 64, 128], P(('groups', 'dp'), 'proj'), parts along dimension 0, may hold values from -0.0625 to 0.0625
- out_basis: float32 [64, 64], replicated, may hold values from -1 to 2
- in_basis: float32 [128, 128], replicated, may hold values from -1 to 2
- corrections: float32 [64, 128], replicated, may hold values from 0.25 to 4
Outputs:
- scores: float32 [2048, 2048], P(('groups', 'proj'), 'dp'), parts along dimension 0
There are 2 independent parts, one for each index of `groups`. A program takes and returns all parts, laid end to end along the dimension named above; an argument that names none is the same for every part. Nothing has to cross between parts.
All inputs are finite; a program needn't handle non-finite values.
Results may differ from a plain program's by a relative error of at most 0.0085.
Values may be sent and summed in bfloat16 or wider, within the bound.
No kernel may reach another device: no remote copies, remote signals or barrier semaphores. Data moves between devices by JAX's collectives and lax.ppermute only.
A program may use at most 64 MiB of HBM per device.

v0:
```python
import jax
import jax.numpy as jnp
from jax import lax
from jax.sharding import PartitionSpec as P

damping_term = 0.05


def condition(block, out_basis, in_basis, corrections):
    highest = lax.Precision.HIGHEST
    values = block.astype(jnp.float32)
    inner = jnp.einsum("qbc,cd->qbd", values, in_basis, precision=highest)
    rotated = jnp.einsum("ba,qbd->qad", out_basis, inner, precision=highest)
    scaled = rotated / (corrections + damping_term)
    back = jnp.einsum("qad,ed->qae", scaled, in_basis, precision=highest)
    result = jnp.einsum("ba,qae->qbe", out_basis, back, precision=highest)
    return result.astype(jnp.bfloat16)


def body(queries, train_grads, out_basis, in_basis, corrections):
    rows_here = queries.shape[1]
    width = rows_here * queries.shape[2]
    whole = lax.all_gather(queries, "proj", axis=1, tiled=True)
    conditioned = condition(whole, out_basis, in_basis, corrections)
    mine = lax.dynamic_slice_in_dim(conditioned, lax.axis_index("proj") * rows_here, rows_here, 1)
    flat = mine.reshape(mine.shape[0], width)
    train_flat = train_grads.reshape(train_grads.shape[0], width)
    contract = (((1,), (1,)), ((), ()))
    partial_value = lax.dot_general(
        lax.all_gather(flat, "dp", axis=0, tiled=True),
        train_flat,
        contract,
        preferred_element_type=jnp.float32,
    )
    scores = lax.psum_scatter(
        partial_value.astype(jnp.bfloat16), "proj", scatter_dimension=0, tiled=True
    ).astype(jnp.float32)
    return scores


def solution(mesh):
    in_specs = (P(("groups", "dp"), "proj", None), P(("groups", "dp"), "proj", None), P(), P(), P())
    out_specs = P(("groups", "proj"), "dp")
    return jax.shard_map(body, mesh=mesh, in_specs=in_specs, out_specs=out_specs, check_vma=False)
```

profile of v0, /device:TPU:0, one launch (start us, length us, event | category | flops | bytes accessed | tf_op | source)
XLA Modules:
  0.0 198.2 jit_solution(981238735902552789)
XLA Ops:
  6.5 0.0 copy-start
  6.5 0.0 copy-start.1
  6.5 0.0 all-gather.3.cloned.1.call-start
  6.5 0.7 all-gather.3.cloned.1.call-update
  7.3 0.0 all-gather.5.cloned.1.call-start
  7.3 0.8 broadcast_add_fusion
  8.1 84.1 %all-gather.3.cloned.1.call-done = bf16[256,64,128]{2,1,0:T(8,128)(2,1)} async-done(((bf16[256,16,128]{2,1,0:T(8,128)(2,1)}), bf16[256,64,128]{2,1,0:T(8,128)(2,1)}) %all-gather.3.cloned.1.call-update) | async-done | bytes 4194320 | tf_op jit(solution)/shard_map/all_gather | solution.py:23
  92.2 0.0 copy-done
  92.2 6.8 %fusion.9 = f32[256,64,128]{2,1,0:T(8,128)S(1)} fusion(bf16[256,64,128]{2,1,0:T(8,128)(2,1)} %all-gather.3.cloned.1.call-done, f32[128,128]{1,0:T(8,128)S(1)} %copy-done), kind=kOutput, calls=%fused_computation.10 | convolution fusion | flops 3221225472 | bytes 12648448 | tf_op jit(solution)/shard_map/qbc,cd->qbd/dot_general | solution.py:12
  99.0 0.0 copy-done.1
  99.0 8.4 %fusion.13 = f32[256,128,64]{1,2,0:T(8,128)S(1)} fusion(f32[256,64,128]{2,1,0:T(8,128)S(1)} %fusion.9, f32[64,64]{1,0:T(8,128)S(1)} %copy-done.1), kind=kOutput, calls=%fused_computation.14 | convolution fusion | flops 1610612736 | bytes 16793600 | tf_op jit(solution)/shard_map/ba,qbd->qad/dot_general | solution.py:13
  107.4 7.3 %fusion = f32[256,64,128]{2,1,0:T(8,128)S(1)} fusion(f32[256,128,64]{1,2,0:T(8,128)S(1)} %fusion.13, f32[64,128]{1,0:T(8,128)S(1)} %broadcast_add_fusion, f32[128,128]{1,0:T(8,128)S(1)} %copy-done), kind=kOutput, calls=%fused_computation.1 | convolution fusion | flops 3223322624 | bytes 16875520 | tf_op jit(solution)/shard_map/qad,ed->qae/dot_general | solution.py:15
  114.7 0.0 copy-start.2
  114.7 7.9 %fusion.11 = bf16[256,128,64]{1,2,0:T(8,128)(2,1)S(1)} fusion(f32[256,64,128]{2,1,0:T(8,128)S(1)} %fusion, f32[64,64]{1,0:T(8,128)S(1)} %copy-done.1), kind=kOutput, calls=%fused_computation.12 | convolution fusion | flops 1610612736 | bytes 12599296 | tf_op jit(solution)/shard_map/ba,qae->qbe/dot_general | solution.py:16
  122.7 0.3 dynamic-slice_convert_fusion
  123.0 1.2 copy.16
  124.2 0.0 all-gather.5.cloned.1.call-update
  124.2 0.0 reduce-scatter.2.cloned.1.call-start
  124.3 32.8 %all-gather.5.cloned.1.call-done = bf16[1024,2048]{1,0:T(8,128)(2,1)} async-done(((bf16[256,2048]{1,0:T(8,128)(2,1)}), bf16[1024,2048]{1,0:T(8,128)(2,1)}) %all-gather.5.cloned.1.call-update) | async-done | bytes 4194320 | tf_op jit(solution)/shard_map/all_gather | solution.py:30
  157.0 0.0 copy-done.2
  157.0 5.5 %fusion.5 = bf16[1024,512]{1,0:T(8,128)(2,1)} fusion(bf16[1024,2048]{1,0:T(8,128)(2,1)} %all-gather.5.cloned.1.call-done, bf16[64,8,16,128]{3,2,1,0:T(8,128)(2,1)S(1)} %bitcast.30), kind=kOutput, calls=%fused_computation.7 | convolution fusion | flops 2148007936 | bytes 7340032 | tf_op jit(solution)/shard_map/dot_general | solution.py:29
  162.6 0.0 reduce-scatter.2.cloned.1.call-update
  162.6 27.3 %reduce-scatter.2.cloned.1.call-done = bf16[256,512]{1,0:T(8,128)(2,1)} async-done(((bf16[1024,512]{1,0:T(8,128)(2,1)}), bf16[256,512]{1,0:T(8,128)(2,1)}) %reduce-scatter.2.cloned.1.call-update) | async-done | bytes 262160 | tf_op jit(solution)/shard_map/reduce_scatter | solution.py:35
  189.9 1.8 convert_element_type.13
Async XLA Ops:
  6.5 85.7 %copy-start = (f32[128,128]{1,0:T(8,128)S(1)}, f32[128,128]{1,0:T(8,128)}, u32[]{:S(2)}) copy-start(f32[128,128]{1,0:T(8,128)} %param.8) | copy-start | bytes 196612
  6.5 92.5 %copy-start.1 = (f32[64,64]{1,0:T(8,128)S(1)}, f32[64,64]{1,0:T(8,128)}, u32[]{:S(2)}) copy-start(f32[64,64]{1,0:T(8,128)} %param.7) | copy-start | bytes 49156
  6.5 85.7 %all-gather.3.cloned.1.call-start = ((), (), s32[]{:S(2)}) async-start(), calls=%async_computation.1 | async-start | bytes 5242880 | tf_op jit(solution)/shard_map/all_gather | solution.py:23
  7.3 149.8 %all-gather.5.cloned.1.call-start = ((), (), s32[]{:S(2)}) async-start(), calls=%async_computation.2 | async-start | bytes 5242880 | tf_op jit(solution)/shard_map/all_gather | solution.py:30
  114.7 42.3 %copy-start.2 = (bf16[512,16,128]{2,1,0:T(8,128)(2,1)S(1)}, bf16[512,16,128]{2,1,0:T(8,128)(2,1)}, u32[]{:S(2)}) copy-start(bf16[512,16,128]{2,1,0:T(8,128)(2,1)} %param.6) | copy-start | bytes 6291460
  124.2 65.7 %reduce-scatter.2.cloned.1.call-start = ((), (), s32[]{:S(2)}) async-start(), calls=%async_computation.3 | async-start | bytes 1310720 | tf_op jit(solution)/shard_map/reduce_scatter | solution.py:35
Sparse Core Ops, SparseCore 0:
  8.9 83.2 all-gather.2
  124.3 32.6 all-gather.4
  162.7 27.1 reduce-scatter.1
where the time goes:
time: 198 us
  waiting for transfers between devices  145 us (73%)
  matrix products  35.9 us (18%)
  between operations  13.2 us (7%)
  other arithmetic  2.57 us (1%)
    all_gather x1, waiting for transfers between devices, body(): whole = lax.all_gather(queries, 'proj', axis=1, tiled=True)  84.1 us
    all_gather x1, waiting for transfers between devices, body(): lax.all_gather(flat, 'dp', axis=0, tiled=True)  32.8 us
    reduce_scatter x1, waiting for transfers between devices, body(): lax.psum_scatter(partial_value.astype(jnp.bfloat16), 'proj', scatter_dime...  27.3 us
    dot_general x1, matrix products, condition(): rotated = jnp.einsum('ba,qbd->qad', out_basis, inner, precision=highest)  8.38 us
    dot_general x1, matrix products, condition(): result = jnp.einsum('ba,qae->qbe', out_basis, back, precision=highest)  7.94 us
    dot_general x1, matrix products, condition(): back = jnp.einsum('qad,ed->qae', scaled, in_basis, precision=highest)  7.27 us
    dot_general x1, matrix products, condition(): inner = jnp.einsum('qbc,cd->qbd', values, in_basis, precision=highest)  6.81 us
    dot_general x1, matrix products, body(): lax.dot_general(lax.all_gather(flat, 'dp', axis=0, tiled=True), train_fla...  5.53 us
  transfers between devices with their start and end apart: 3, of which 3 were waited for; matrix products, arithmetic and copies ran while one was open for 0% of the time, Pallas kernels for 0%

commit v1 on v0

--- a/solution.py
+++ b/solution.py
@@ -7,22 +7,22 @@
 
 
 def condition(block, out_basis, in_basis, corrections):
-    highest = lax.Precision.HIGHEST
+    high = lax.Precision.HIGH
     values = block.astype(jnp.float32)
-    inner = jnp.einsum("qbc,cd->qbd", values, in_basis, precision=highest)
-    rotated = jnp.einsum("ba,qbd->qad", out_basis, inner, precision=highest)
+    inner = jnp.einsum("qbc,cd->qbd", values, in_basis, precision=high)
+    rotated = jnp.einsum("ba,qbd->qad", out_basis, inner, precision=high)
     scaled = rotated / (corrections + damping_term)
-    back = jnp.einsum("qad,ed->qae", scaled, in_basis, precision=highest)
-    result = jnp.einsum("ba,qae->qbe", out_basis, back, precision=highest)
+    back = jnp.einsum("qad,ed->qae", scaled, in_basis, precision=high)
+    result = jnp.einsum("ba,qae->qbe", out_basis, back, precision=high)
     return result.astype(jnp.bfloat16)
 
 
 def body(queries, train_grads, out_basis, in_basis, corrections):
     rows_here = queries.shape[1]
     width = rows_here * queries.shape[2]
-    whole = lax.all_gather(queries, "proj", axis=1, tiled=True)
+    whole = lax.all_to_all(queries, "proj", split_axis=0, concat_axis=1, tiled=True)
     conditioned = condition(whole, out_basis, in_basis, corrections)
-    mine = lax.dynamic_slice_in_dim(conditioned, lax.axis_index("proj") * rows_here, rows_here, 1)
+    mine = lax.all_to_all(conditioned, "proj", split_axis=1, concat_axis=0, tiled=True)
     flat = mine.reshape(mine.shape[0], width)
     train_flat = train_grads.reshape(train_grads.shape[0], width)
     contract = (((1,), (1,)), ((), ()))

time: 198 us -> 149 us (0.75)
  waiting for transfers between devices: 145 us -> 86.7 us
  blocking collectives: 0 us -> 27.7 us
  matrix products: 35.9 us -> 9.24 us
  starting transfers between devices: 0.08 us -> 6.49 us
    all_gather x1 -> x0, waiting for transfers between devices: 84.1 us -> none  [body(): whole = lax.all_gather(queries, 'proj', axis=1, tiled=True)]
    all_to_all x0 -> x1, blocking collectives: none -> 27.7 us  [body(): lax.all_to_all(conditioned, 'proj', split_axis=1, concat_axis=0, tiled=True)]
    dot_general x4, matrix products: 30.4 us -> 3.71 us  [the longest x1 1.03 us: condition(): rotated = jnp.einsum('ba,qbd->qad', out_basis, inner, precision=high)]
    all_to_all x0 -> x1, waiting for transfers between devices: none -> 25.7 us  [body(): lax.all_to_all(queries, 'proj', split_axis=0, concat_axis=1, tiled=True)]
    all_to_all x0 -> x1, starting transfers between devices: none -> 6.45 us  [body(): lax.all_to_all(queries, 'proj', split_axis=0, concat_axis=1, tiled=True)]
where the time goes in v1:
time: 149 us; the launch traced here: 148 us
  waiting for transfers between devices  86.7 us (58%)
  blocking collectives  27.7 us (19%)
  between operations  13.5 us (9%)
  matrix products  9.24 us (6%)
  starting transfers between devices  6.49 us (4%)
  local copies, waits for them, and re-layouts  2.96 us (2%)
  other arithmetic  1.81 us (1%)
    all_gather x1, waiting for transfers between devices, body(): lax.all_gather(flat, 'dp', axis=0, tiled=True)  33.6 us
    all_to_all x1, blocking collectives, body(): lax.all_to_all(conditioned, 'proj', split_axis=1, concat_axis=0, tiled=True)  27.7 us
    reduce_scatter x1, waiting for transfers between devices, body(): lax.psum_scatter(partial_value.astype(jnp.bfloat16), 'proj', scatter_dime...  27.3 us
    all_to_all x1, waiting for transfers between devices, body(): lax.all_to_all(queries, 'proj', split_axis=0, concat_axis=1, tiled=True)  25.7 us
    all_to_all x1, starting transfers between devices, body(): lax.all_to_all(queries, 'proj', split_axis=0, concat_axis=1, tiled=True)  6.45 us
    dot_general x1, matrix products, body(): lax.dot_general(lax.all_gather(flat, 'dp', axis=0, tiled=True), train_fla...  5.53 us
  transfers between devices with their start and end apart: 3, of which 3 were waited for; matrix products, arithmetic and copies ran while one was open for 0% of the time, Pallas kernels for 0%

profile of v1, /device:TPU:0, one launch (start us, length us, event | category | flops | bytes accessed | tf_op | source)
XLA Modules:
  0.0 148.4 jit_solution(6387004049671244642)
XLA Ops:
  6.5 0.0 copy-start
  6.5 0.0 copy-start.2
  6.5 6.4 %all-to-all-start = ((bf16[256,16,128]{2,1,0:T(8,128)(2,1)}), bf16[256,16,128]{2,1,0:T(8,128)(2,1)S(1)}, u32[]{:S(2)}, u32[]{:S(2)}) async-start(bf16[256,16,128]{2,1,0:T(8,128)(2,1)} %param.5), calls=%async_computation | async-start | bytes 2097152 | tf_op jit(solution)/shard_map/all_to_all | solution.py:23
  13.0 0.0 all-gather.2.cloned.1.call-start
  13.0 0.0 copy-done.2
  13.0 25.7 %all-to-all-done = bf16[256,16,128]{2,1,0:T(8,128)(2,1)S(1)} async-done(((bf16[256,16,128]{2,1,0:T(8,128)(2,1)}), bf16[256,16,128]{2,1,0:T(8,128)(2,1)S(1)}, u32[]{:S(2)}, u32[]{:S(2)}) %all-to-all-start) | async-done | bytes 1048608 | tf_op jit(solution)/shard_map/all_to_all | solution.py:23
  38.7 0.3 copy.12
  39.0 0.0 copy-start.1
  39.0 0.0 copy-done
  39.1 0.7 fusion.10
  39.8 0.0 copy-done.1
  39.8 1.0 fusion.13
  40.8 1.0 fusion.3
  41.9 1.0 fusion.7
  42.8 0.7 copy.14
  43.5 27.7 %all_to_all.33 = bf16[64,64,128]{2,0,1:T(8,128)(2,1)S(1)} all-to-all(bf16[64,64,128]{2,0,1:T(8,128)(2,1)S(1)} %copy.14), channel_id=1, replica_groups=mesh['groups'=2,'dp'=4,'proj'=4] {'proj'}, dimensions={1} | all-to-all | bytes 2097152 | tf_op jit(solution)/shard_map/all_to_all | solution.py:25
  71.2 0.7 copy.15
  71.9 0.0 copy-start.3
  71.9 1.2 copy.27
  73.2 0.0 all-gather.2.cloned.1.call-update
  73.2 0.0 reduce-scatter.2.cloned.1.call-start
  73.2 33.6 %all-gather.2.cloned.1.call-done = bf16[1024,2048]{1,0:T(8,128)(2,1)} async-done(((bf16[256,2048]{1,0:T(8,128)(2,1)}), bf16[1024,2048]{1,0:T(8,128)(2,1)}) %all-gather.2.cloned.1.call-update) | async-done | bytes 4194320 | tf_op jit(solution)/shard_map/all_gather | solution.py:30
  106.9 0.0 copy-done.3
  106.9 5.5 %fusion.4 = bf16[1024,512]{1,0:T(8,128)(2,1)} fusion(bf16[1024,2048]{1,0:T(8,128)(2,1)} %all-gather.2.cloned.1.call-done, bf16[64,8,16,128]{3,2,1,0:T(8,128)(2,1)S(1)} %bitcast.42), kind=kOutput, calls=%fused_computation.6 | convolution fusion | flops 2148007936 | bytes 7340032 | tf_op jit(solution)/shard_map/dot_general | solution.py:29
  112.4 0.0 reduce-scatter.2.cloned.1.call-update
  112.4 27.3 %reduce-scatter.2.cloned.1.call-done = bf16[256,512]{1,0:T(8,128)(2,1)} async-done(((bf16[1024,512]{1,0:T(8,128)(2,1)}), bf16[256,512]{1,0:T(8,128)(2,1)}) %reduce-scatter.2.cloned.1.call-update) | async-done | bytes 262160 | tf_op jit(solution)/shard_map/reduce_scatter | solution.py:35
  139.7 1.8 %convert_element_type.16 = f32[256,512]{1,0:T(8,128)} convert(bf16[256,512]{1,0:T(8,128)(2,1)} %reduce-scatter.2.cloned.1.call-done) | non-fusion elementwise | flops 131072 | bytes 786432 | tf_op jit(solution)/shard_map/convert_element_type | solution.py:37
  (1 shorter events, 0.0 us)
Async XLA Ops:
  6.5 32.5 %copy-start = (f32[128,128]{1,0:T(8,128)S(1)}, f32[128,128]{1,0:T(8,128)}, u32[]{:S(2)}) copy-start(f32[128,128]{1,0:T(8,128)} %param.8) | copy-start | bytes 196612
  6.5 6.5 %copy-start.2 = (f32[64,128]{1,0:T(8,128)S(1)}, f32[64,128]{1,0:T(8,128)}, u32[]{:S(2)}) copy-start(f32[64,128]{1,0:T(8,128)} %param.9) | copy-start | bytes 98308
  6.5 32.2 %all-to-all-start = ((bf16[256,16,128]{2,1,0:T(8,128)(2,1)}), bf16[256,16,128]{2,1,0:T(8,128)(2,1)S(1)}, u32[]{:S(2)}, u32[]{:S(2)}) async-start(bf16[256,16,128]{2,1,0:T(8,128)(2,1)} %param.5), calls=%async_computation | async-start | bytes 2097152 | tf_op jit(solution)/shard_map/all_to_all | solution.py:23
  13.0 93.9 %all-gather.2.cloned.1.call-start = ((), (), s32[]{:S(2)}) async-start(), calls=%async_computation.3 | async-start | bytes 5242880 | tf_op jit(solution)/shard_map/all_gather | solution.py:30
  39.0 0.8 copy-start.1
  71.9 35.0 %copy-start.3 = (bf16[512,16,128]{2,1,0:T(8,128)(2,1)S(1)}, bf16[512,16,128]{2,1,0:T(8,128)(2,1)}, u32[]{:S(2)}) copy-start(bf16[512,16,128]{2,1,0:T(8,128)(2,1)} %param.6) | copy-start | bytes 6291460
  73.2 66.6 %reduce-scatter.2.cloned.1.call-start = ((), (), s32[]{:S(2)}) async-start(), calls=%async_computation.4 | async-start | bytes 1310720 | tf_op jit(solution)/shard_map/reduce_scatter | solution.py:35
Sparse Core Ops, SparseCore 0:
  73.3 33.5 all-gather.1
  112.6 27.1 reduce-scatter.1

commit v2 on v1

v2 whole, which is shorter than its diff:
```python
import jax
import jax.numpy as jnp
from jax import lax
from jax.sharding import PartitionSpec as P

damping_term = 0.05
CHUNKS = 2


def condition(block, out_basis, in_basis, corrections):
    high = lax.Precision.HIGH
    values = block.astype(jnp.float32)
    inner = jnp.einsum("qbc,cd->qbd", values, in_basis, precision=high)
    rotated = jnp.einsum("ba,qbd->qad", out_basis, inner, precision=high)
    scaled = rotated / (corrections + damping_term)
    back = jnp.einsum("qad,ed->qae", scaled, in_basis, precision=high)
    result = jnp.einsum("ba,qae->qbe", out_basis, back, precision=high)
    return result.astype(jnp.bfloat16)


def body(queries, train_grads, out_basis, in_basis, corrections):
    slices = lax.axis_size("proj")
    shares = lax.axis_size("dp")
    count, rows_here, columns = queries.shape
    width = rows_here * columns
    part = count // CHUNKS
    owned = shares // slices
    train_count = train_grads.shape[0]
    train_flat = lax.optimization_barrier(train_grads.reshape(train_count, width))
    contract = (((1,), (1,)), ((), ()))
    results = []
    for chunk in range(CHUNKS):
        raw = queries[chunk * part:(chunk + 1) * part]
        whole = lax.all_to_all(raw, "proj", split_axis=0, concat_axis=1, tiled=True)
        conditioned = condition(whole, out_basis, in_basis, corrections)
        mine = lax.all_to_all(conditioned, "proj", split_axis=1, concat_axis=0, tiled=True)
        flat = mine.reshape(part, width)
        left = lax.all_gather(flat, "dp", axis=0, tiled=True)
        partial_value = lax.dot_general(left, train_flat, contract, preferred_element_type=jnp.float32)
        sent = partial_value.astype(jnp.bfloat16).reshape(slices, owned * part, train_count)
        arrived = lax.all_to_all(sent, "proj", split_axis=0, concat_axis=0, tiled=True)
        total = jnp.sum(arrived.astype(jnp.float32), axis=0)
        results.append(total.reshape(owned, part, train_count))
    return jnp.concatenate(results, axis=1).reshape(owned * count, train_count)


def solution(mesh):
    in_specs = (P(("groups", "dp"), "proj", None), P(("groups", "dp"), "proj", None), P(), P(), P())
    out_specs = P(("groups", "proj"), "dp")
    return jax.shard_map(body, mesh=mesh, in_specs=in_specs, out_specs=out_specs, check_vma=False)
```

time: 149 us -> 140 us (0.940)
  waiting for transfers between devices: 86.7 us -> 41.4 us
  blocking collectives: 27.7 us -> 49.6 us
  starting transfers between devices: 6.49 us -> 14.6 us
  local copies, waits for them, and re-layouts: 2.96 us -> 7.17 us
  matrix products: 9.24 us -> 12.5 us
    reduce_scatter x1 -> x0, waiting for transfers between devices: 27.3 us -> none  [body(): lax.psum_scatter(partial_value.astype(jnp.bfloat16), 'proj', scatter_dime...]
    all_gather x1 -> x2, waiting for transfers between devices: 33.6 us -> 12 us  [body(): left = lax.all_gather(flat, 'dp', axis=0, tiled=True)]
    all_to_all x0 -> x1, blocking collectives: none -> 16.5 us  [body(): whole = lax.all_to_all(raw, 'proj', split_axis=0, concat_axis=1, tiled=True)]
    all_to_all x1 -> x3, starting transfers between devices: 6.45 us -> 14.5 us  [the longest x2 8.07 us: body(): lax.all_to_all(sent, 'proj', split_axis=0, concat_axis=0, tiled=True)]
    all_to_all x1 -> x2, blocking collectives: 27.7 us -> 33.1 us  [body(): lax.all_to_all(conditioned, 'proj', split_axis=1, concat_axis=0, tiled=True)]
    all_to_all x1 -> x3, waiting for transfers between devices: 25.7 us -> 29.3 us  [the longest x2 14.8 us: body(): lax.all_to_all(sent, 'proj', split_axis=0, concat_axis=0, tiled=True)]
    dot_general x1 -> x2, matrix products: 5.53 us -> 8.12 us  [body(): lax.dot_general(left, train_flat, contract, preferred_element_type=jnp.fl...]
    unnamed x9 -> x13, local copies, waits for them, and re-layouts: 1.29 us -> 3.76 us
  transfers between devices with their start and end apart: 3 -> 5, of which waited for: 3 -> 3; matrix products, arithmetic and copies ran while one was open for 0% -> 10% of each run, Pallas kernels for 0% -> 0%
where the time goes in v2:
time: 140 us
  blocking collectives  49.6 us (35%)
  waiting for transfers between devices  41.4 us (30%)
  starting transfers between devices  14.6 us (10%)
  between operations  13.6 us (10%)
  matrix products  12.5 us (9%)
  local copies, waits for them, and re-layouts  7.17 us (5%)
    all_to_all x2, blocking collectives, body(): lax.all_to_all(conditioned, 'proj', split_axis=1, concat_axis=0, tiled=True)  33.1 us
    all_to_all x1, blocking collectives, body(): whole = lax.all_to_all(raw, 'proj', split_axis=0, concat_axis=1, tiled=True)  16.5 us
    all_to_all x2, waiting for transfers between devices, body(): lax.all_to_all(sent, 'proj', split_axis=0, concat_axis=0, tiled=True)  14.8 us
    all_to_all x1, waiting for transfers between devices, body(): whole = lax.all_to_all(raw, 'proj', split_axis=0, concat_axis=1, tiled=True)  14.5 us
    all_gather x2, waiting for transfers between devices, body(): left = lax.all_gather(flat, 'dp', axis=0, tiled=True)  12 us
    dot_general x2, matrix products, body(): lax.dot_general(left, train_flat, contract, preferred_element_type=jnp.fl...  8.12 us
    all_to_all x2, starting transfers between devices, body(): lax.all_to_all(sent, 'proj', split_axis=0, concat_axis=0, tiled=True)  8.07 us
    all_to_all x1, starting transfers between devices, body(): whole = lax.all_to_all(raw, 'proj', split_axis=0, concat_axis=1, tiled=True)  6.45 us
  transfers between devices with their start and end apart: 5, of which 3 were waited for; matrix products, arithmetic and copies ran while one was open for 10% of the time, Pallas kernels for 0%

profile of v2, /device:TPU:0, one launch (start us, length us, event | category | flops | bytes accessed | tf_op | source)
XLA Modules:
  0.0 139.8 jit_solution(9629829916242472433)
XLA Ops:
  6.5 0.0 copy-start
  6.5 0.0 copy-start.4
  6.5 2.2 %fusion.16 = (bf16[128,16,128]{2,1,0:T(8,128)(2,1)}, bf16[128,16,128]{2,1,0:T(8,128)(2,1)S(1)}) fusion(bf16[256,16,128]{2,1,0:T(8,128)(2,1)} %param.5), kind=kLoop, calls=%fused_computation.29 | loop fusion | bytes 2097152 | tf_op jit(solution)/shard_map/slice | solution.py:33
  8.8 0.0 copy-start.3
  8.8 6.4 %all-to-all-start = ((bf16[128,16,128]{2,1,0:T(8,128)(2,1)}), bf16[128,16,128]{2,1,0:T(8,128)(2,1)S(1)}, u32[]{:S(2)}, u32[]{:S(2)}) async-start(bf16[128,16,128]{2,1,0:T(8,128)(2,1)} %get-tuple-element.5), calls=%async_computation | async-start | bytes 1048576 | tf_op jit(solution)/shard_map/all_to_all | solution.py:34
  15.2 0.0 all-gather.3.cloned.1.call-start
  15.2 0.0 copy-done.4
  15.2 14.5 %all-to-all-done = bf16[128,16,128]{2,1,0:T(8,128)(2,1)S(1)} async-done(((bf16[128,16,128]{2,1,0:T(8,128)(2,1)}), bf16[128,16,128]{2,1,0:T(8,128)(2,1)S(1)}, u32[]{:S(2)}, u32[]{:S(2)}) %all-to-all-start) | async-done | bytes 524320 | tf_op jit(solution)/shard_map/all_to_all | solution.py:34
  29.7 0.1 copy.16
  29.8 0.0 copy-done
  29.8 0.4 fusion.10
  30.2 0.0 copy-done.3
  30.2 0.6 fusion.1
  30.8 0.6 fusion.8
  31.4 0.6 fusion.2
  32.0 0.3 copy.18
  32.3 16.4 %all_to_all.76 = bf16[32,64,128]{2,0,1:T(8,128)(2,1)S(1)} all-to-all(bf16[32,64,128]{2,0,1:T(8,128)(2,1)S(1)} %copy.18), channel_id=1, replica_groups=mesh['groups'=2,'dp'=4,'proj'=4] {'proj'}, dimensions={1} | all-to-all | bytes 1048576 | tf_op jit(solution)/shard_map/all_to_all | solution.py:36
  48.7 0.2 copy.19
  48.9 0.9 copy.36
  49.9 0.0 all-gather.3.cloned.1.call-update
  49.9 0.0 all-gather.5.cloned.1.call-start
  50.0 16.5 %all_to_all.77 = bf16[128,16,128]{2,1,0:T(8,128)(2,1)S(1)} all-to-all(bf16[128,16,128]{2,1,0:T(8,128)(2,1)S(1)} %get-tuple-element.6), channel_id=1, replica_groups=mesh['groups'=2,'dp'=4,'proj'=4] {'proj'}, dimensions={0} | all-to-all | bytes 1048576 | tf_op jit(solution)/shard_map/all_to_all | solution.py:34
  66.5 0.1 copy.20
  66.6 0.4 fusion.6
  67.0 0.6 fusion
  67.6 0.6 fusion.4
  68.2 0.6 fusion.3
  68.8 0.3 copy.22
  69.1 0.0 copy-start.1
  69.2 16.7 %all_to_all.78 = bf16[32,64,128]{2,0,1:T(8,128)(2,1)S(1)} all-to-all(bf16[32,64,128]{2,0,1:T(8,128)(2,1)S(1)} %copy.22), channel_id=1, replica_groups=mesh['groups'=2,'dp'=4,'proj'=4] {'proj'}, dimensions={1} | all-to-all | bytes 1048576 | tf_op jit(solution)/shard_map/all_to_all | solution.py:36
  85.9 0.2 copy.23
  86.1 0.9 copy.35
  87.0 0.0 all-gather.5.cloned.1.call-update
  87.0 0.0 copy-done.1
  87.0 1.9 %copy.34 = bf16[64,8,16,128]{3,1,2,0:T(8,128)(2,1)} copy(bf16[64,8,16,128]{3,2,1,0:T(8,128)(2,1)S(1)} %bitcast.78) | data formatting | bytes 4194304
  88.9 0.0 copy-start.2
  88.9 0.0 all-gather.3.cloned.1.call-done
  88.9 4.5 %convolution_convert_fusion.2 = bf16[512,512]{1,0:T(8,128)(2,1)} fusion(bf16[512,2048]{1,0:T(8,128)(2,1)} %all-gather.3.cloned.1.call-done, bf16[512,2048]{1,0:T(8,128)(2,1)} %bitcast.79), kind=kOutput, calls=%fused_computation.7 | convolution fusion | flops 1074003968 | bytes 4718592 | tf_op jit(solution)/shard_map/dot_general | solution.py:39
  93.3 3.5 %all-to-all-start.2 = ((bf16[4,128,512]{2,1,0:T(8,128)(2,1)}), bf16[4,128,512]{2,1,0:T(8,128)(2,1)S(1)}, u32[]{:S(2)}, u32[]{:S(2)}) async-start(bf16[4,128,512]{2,1,0:T(8,128)(2,1)} %bitcast.10), calls=%async_computation.2 | async-start | bytes 1048576 | tf_op jit(solution)/shard_map/all_to_all | solution.py:41
  96.8 12.0 %all-gather.5.cloned.1.call-done = bf16[512,2048]{1,0:T(8,128)(2,1)} async-done(((bf16[128,2048]{1,0:T(8,128)(2,1)}), bf16[512,2048]{1,0:T(8,128)(2,1)}) %all-gather.5.cloned.1.call-update) | async-done | bytes 2097168 | tf_op jit(solution)/shard_map/all_gather | solution.py:38
  108.9 0.0 copy-done.2
  108.9 3.7 %convolution_convert_fusion = bf16[512,512]{1,0:T(8,128)(2,1)} fusion(bf16[512,2048]{1,0:T(8,128)(2,1)} %all-gather.5.cloned.1.call-done, bf16[512,2048]{1,0:T(8,128)(2,1)S(1)} %bitcast.80), kind=kOutput, calls=%fused_computation.5 | convolution fusion | flops 1074003968 | bytes 4718592 | tf_op jit(solution)/shard_map/dot_general | solution.py:39
  112.5 0.0 all-to-all-done.2
  112.5 4.6 %all-to-all-start.5 = ((bf16[4,128,512]{2,1,0:T(8,128)(2,1)}), bf16[4,128,512]{2,1,0:T(8,128)(2,1)S(1)}, u32[]{:S(2)}, u32[]{:S(2)}) async-start(bf16[4,128,512]{2,1,0:T(8,128)(2,1)} %bitcast.20), calls=%async_computation.5 | async-start | bytes 1048576 | tf_op jit(solution)/shard_map/all_to_all | solution.py:41
  117.1 0.1 convert_reduce_fusion.1
  117.2 14.8 %all-to-all-done.5 = bf16[4,128,512]{2,1,0:T(8,128)(2,1)S(1)} async-done(((bf16[4,128,512]{2,1,0:T(8,128)(2,1)}), bf16[4,128,512]{2,1,0:T(8,128)(2,1)S(1)}, u32[]{:S(2)}, u32[]{:S(2)}) %all-to-all-start.5) | async-done | bytes 524320 | tf_op jit(solution)/shard_map/all_to_all | solution.py:41
  132.0 0.1 convert_reduce_fusion
  132.1 0.8 maximum_bitcast_fusion
  (1 shorter events, 0.0 us)
Async XLA Ops:
  6.5 23.2 %copy-start = (f32[128,128]{1,0:T(8,128)S(1)}, f32[128,128]{1,0:T(8,128)}, u32[]{:S(2)}) copy-start(f32[128,128]{1,0:T(8,128)} %param.8) | copy-start | bytes 196612
  6.5 8.7 %copy-start.4 = (f32[64,128]{1,0:T(8,128)S(1)}, f32[64,128]{1,0:T(8,128)}, u32[]{:S(2)}) copy-start(f32[64,128]{1,0:T(8,128)} %param.9) | copy-start | bytes 98308
  8.8 21.4 %copy-start.3 = (f32[64,64]{1,0:T(8,128)S(1)}, f32[64,64]{1,0:T(8,128)}, u32[]{:S(2)}) copy-start(f32[64,64]{1,0:T(8,128)} %param.7) | copy-start | bytes 49156
  8.8 20.9 %all-to-all-start = ((bf16[128,16,128]{2,1,0:T(8,128)(2,1)}), bf16[128,16,128]{2,1,0:T(8,128)(2,1)S(1)}, u32[]{:S(2)}, u32[]{:S(2)}) async-start(bf16[128,16,128]{2,1,0:T(8,128)(2,1)} %get-tuple-element.5), calls=%async_computation | async-start | bytes 1048576 | tf_op jit(solution)/shard_map/all_to_all | solution.py:34
  15.2 73.7 %all-gather.3.cloned.1.call-start = ((), (), s32[]{:S(2)}) async-start(), calls=%async_computation.6 | async-start | bytes 2621440 | tf_op jit(solution)/shard_map/all_gather | solution.py:38
  49.9 59.0 %all-gather.5.cloned.1.call-start = ((), (), s32[]{:S(2)}) async-start(), calls=%async_computation.7 | async-start | bytes 2621440 | tf_op jit(solution)/shard_map/all_gather | solution.py:38
  69.1 17.9 %copy-start.1 = (bf16[512,16,128]{2,1,0:T(8,128)(2,1)S(1)}, bf16[512,16,128]{2,1,0:T(8,128)(2,1)}, u32[]{:S(2)}) copy-start(bf16[512,16,128]{2,1,0:T(8,128)(2,1)} %param.6) | copy-start | bytes 6291460
  88.9 20.0 %copy-start.2 = (bf16[64,8,16,128]{3,1,2,0:T(8,128)(2,1)S(1)}, bf16[64,8,16,128]{3,1,2,0:T(8,128)(2,1)}, u32[]{:S(2)}) copy-start(bf16[64,8,16,128]{3,1,2,0:T(8,128)(2,1)} %copy.34) | copy-start | bytes 6291460
  93.3 19.2 %all-to-all-start.2 = ((bf16[4,128,512]{2,1,0:T(8,128)(2,1)}), bf16[4,128,512]{2,1,0:T(8,128)(2,1)S(1)}, u32[]{:S(2)}, u32[]{:S(2)}) async-start(bf16[4,128,512]{2,1,0:T(8,128)(2,1)} %bitcast.10), calls=%async_computation.2 | async-start | bytes 1048576 | tf_op jit(solution)/shard_map/all_to_all | solution.py:41
  112.5 19.5 %all-to-all-start.5 = ((bf16[4,128,512]{2,1,0:T(8,128)(2,1)}), bf16[4,128,512]{2,1,0:T(8,128)(2,1)S(1)}, u32[]{:S(2)}, u32[]{:S(2)}) async-start(bf16[4,128,512]{2,1,0:T(8,128)(2,1)} %bitcast.20), calls=%async_computation.5 | async-start | bytes 1048576 | tf_op jit(solution)/shard_map/all_to_all | solution.py:41
Sparse Core Ops, SparseCore 0:
  50.0 21.6 all-gather.2
  87.1 21.6 all-gather.4

commit v3 on v2

v3 whole, which is shorter than its diff:
```python
import jax
import jax.numpy as jnp
from jax import lax
from jax.sharding import PartitionSpec as P

damping_term = 0.05
CHUNKS = 2
CORES = 2


def condition(block, enter, leave, in_basis, divisor):
    high = lax.Precision.HIGH
    values = block.astype(jnp.float32)
    inner = jnp.einsum("qbc,cd->qbd", values, in_basis, precision=high)
    rotated = jnp.einsum("ba,qbd->qad", enter, inner, precision=high)
    scaled = rotated / divisor
    back = jnp.einsum("qad,ed->qae", scaled, in_basis, precision=high)
    result = jnp.einsum("ba,qae->qbe", leave, back, precision=high)
    return result.astype(jnp.bfloat16)


def shifted(value, axis, size, step):
    return lax.ppermute(value, axis, [(at, (at + step) % size) for at in range(size)])


def pick(blocks, index):
    return lax.dynamic_index_in_dim(blocks, index, 0, keepdims=False)


def body(queries, train_grads, out_basis, in_basis, corrections):
    slices = lax.axis_size("proj")
    shares = lax.axis_size("dp")
    cores = CORES if shares % CORES == 0 else 1
    here = lax.axis_index("proj")
    share = lax.axis_index("dp")
    count, rows_here, columns = queries.shape
    width = rows_here * columns
    part = count // CHUNKS
    each = part // slices
    owned = shares // slices
    train_count = train_grads.shape[0]
    train_flat = lax.optimization_barrier(train_grads.reshape(train_count, width))
    contract = (((1,), (1,)), ((), ()))
    order = jnp.arange(slices)
    row_blocks = out_basis.reshape(slices, rows_here, -1)
    enter = row_blocks[(here - order) % slices].reshape(out_basis.shape)
    leave = row_blocks[(here + order) % slices].reshape(out_basis.shape)
    divisor = corrections + damping_term
    results = []
    for chunk in range(CHUNKS):
        raw = queries[chunk * part:(chunk + 1) * part].reshape(slices, each, rows_here, columns)
        rows = [pick(raw, here)]
        for step in range(1, slices):
            rows.append(shifted(pick(raw, (here + step) % slices), "proj", slices, step))
        conditioned = condition(jnp.concatenate(rows, axis=1), enter, leave, in_basis, divisor)
        mine = jnp.zeros((slices, each, width), jnp.bfloat16)
        for step in range(slices):
            piece = conditioned[:, step * rows_here:(step + 1) * rows_here].reshape(each, width)
            if step:
                piece = shifted(piece, "proj", slices, step)
            mine = lax.dynamic_update_index_in_dim(mine, piece, (here - step) % slices, 0)
        mine = mine.reshape(part, width)
        near = [mine]
        for step in range(cores, shares, cores):
            near.append(shifted(mine, "dp", shares, step))
        near = jnp.concatenate(near, axis=0)
        swap = [(at, at // cores * cores + (at + 1) % cores) for at in range(shares)]
        held = [near] if cores == 1 else [near, lax.ppermute(near, "dp", swap)]
        partial_scores = jnp.zeros((shares, part, train_count), jnp.bfloat16)
        for turn, block in enumerate(held):
            value = lax.dot_general(block, train_flat, contract, preferred_element_type=jnp.float32)
            value = value.astype(jnp.bfloat16).reshape(shares // cores, part, train_count)
            lane = share // cores * cores + (share + turn) % cores
            for step in range(shares // cores):
                at = (lane - step * cores) % shares
                partial_scores = lax.dynamic_update_index_in_dim(partial_scores, value[step], at, 0)
        sent = partial_scores.reshape(slices, owned, part, train_count)
        total = pick(sent, here).astype(jnp.float32)
        for step in range(1, slices):
            total = total + shifted(pick(sent, (here + step) % slices), "proj", slices, step).astype(jnp.float32)
        results.append(total)
    return jnp.concatenate(results, axis=1).reshape(owned * count, train_count)


def solution(mesh):
    in_specs = (P(("groups", "dp"), "proj", None), P(("groups", "dp"), "proj", None), P(), P(), P())
    out_specs = P(("groups", "proj"), "dp")
    return jax.shard_map(body, mesh=mesh, in_specs=in_specs, out_specs=out_specs, check_vma=False)
```

time: 140 us -> 107 us (0.76)
  blocking collectives: 49.6 us -> 0 us
  starting transfers between devices: 14.6 us -> 35.9 us
  between operations: 13.6 us -> 0.61 us
  local copies, waits for them, and re-layouts: 7.17 us -> 9.5 us
  other arithmetic: 0.97 us -> 3.24 us
  matrix products: 12.5 us -> 14.3 us
    all_to_all x3 -> x0, blocking collectives: 49.6 us -> none  [the longest x2 33.1 us: body(): lax.all_to_all(conditioned, 'proj', split_axis=1, concat_axis=0, tiled=True)]
    ppermute x0 -> x22, waiting for transfers between devices: none -> 42.8 us  [the longest x20 42.8 us: shifted(): lax.ppermute(value, axis, [(at, (at + step) % size) for at in range(size)])]
    ppermute x0 -> x22, starting transfers between devices: none -> 35.9 us  [the longest x20 35.7 us: shifted(): lax.ppermute(value, axis, [(at, (at + step) % size) for at in range(size)])]
    all_to_all x3 -> x0, waiting for transfers between devices: 29.3 us -> none  [the longest x2 14.8 us: body(): lax.all_to_all(sent, 'proj', split_axis=0, concat_axis=0, tiled=True)]
    all_to_all x3 -> x0, starting transfers between devices: 14.5 us -> none  [the longest x2 8.07 us: body(): lax.all_to_all(sent, 'proj', split_axis=0, concat_axis=0, tiled=True)]
    all_gather x2 -> x0, waiting for transfers between devices: 12 us -> none  [body(): left = lax.all_gather(flat, 'dp', axis=0, tiled=True)]
    dynamic_update_slice x0 -> x16, local copies, waits for them, and re-layouts: none -> 2.95 us  [the longest x8 2.82 us: body(): lax.dynamic_update_index_in_dim(mine, piece, (here - step) % slices, 0)]
    dot_general x2, matrix products: 1.18 us -> 3.6 us  [condition(): back = jnp.einsum('qad,ed->qae', scaled, in_basis, precision=high)]
  transfers between devices with their start and end apart: 5 -> 22, of which waited for: 3 -> 9; matrix products, arithmetic and copies ran while one was open for 10% -> 23% of each run, Pallas kernels for 0% -> 0%
where the time goes in v3:
time: 107 us; the launch traced here: 106 us
  waiting for transfers between devices  42.8 us (40%)
  starting transfers between devices  35.9 us (34%)
  matrix products  14.3 us (13%)
  local copies, waits for them, and re-layouts  9.5 us (9%)
  other arithmetic  3.24 us (3%)
    ppermute x20, waiting for transfers between devices, shifted(): lax.ppermute(value, axis, [(at, (at + step) % size) for at in range(size)])  42.8 us
    ppermute x20, starting transfers between devices, shifted(): lax.ppermute(value, axis, [(at, (at + step) % size) for at in range(size)])  35.7 us
    dot_general x4, matrix products, body(): lax.dot_general(block, train_flat, contract, preferred_element_type=jnp.f...  5.09 us
    dot_general x2, matrix products, condition(): rotated = jnp.einsum('ba,qbd->qad', enter, inner, precision=high)  3.62 us
    dot_general x2, matrix products, condition(): back = jnp.einsum('qad,ed->qae', scaled, in_basis, precision=high)  3.6 us
    unnamed x17, local copies, waits for them, and re-layouts  3.43 us
    dynamic_update_slice x8, local copies, waits for them, and re-layouts, body(): lax.dynamic_update_index_in_dim(mine, piece, (here - step) % slices, 0)  2.82 us
    concatenate x2, other arithmetic, body(): near = jnp.concatenate(near, axis=0)  2.24 us
  transfers between devices with their start and end apart: 22, of which 9 were waited for; matrix products, arithmetic and copies ran while one was open for 23% of the time, Pallas kernels for 0%

profile of v3, /device:TPU:0, one launch (start us, length us, event | category | flops | bytes accessed | tf_op | source)
XLA Modules:
  0.0 106.3 jit_solution(6105792842661130528)
XLA Ops:
  0.0 1.4 %fusion.44 = (bf16[128,16,128]{2,1,0:T(8,128)(2,1)S(1)}, bf16[128,16,128]{2,1,0:T(8,128)(2,1)S(1)}) fusion(bf16[256,16,128]{2,1,0:T(8,128)(2,1)} %param.5), kind=kLoop, calls=%fused_computation.107 | loop fusion | bytes 2097152 | tf_op jit(solution)/shard_map/slice | solution.py:51
  1.5 3.1 %collective-permute-start = (bf16[32,16,128]{2,1,0:T(8,128)(2,1)S(1)}, bf16[32,16,128]{2,1,0:T(8,128)(2,1)S(1)}, u32[]{:S(2)}, u32[]{:S(2)}) collective-permute-start(bf16[32,16,128]{2,1,0:T(8,128)(2,1)S(1)} %get-tuple-element.17), channel_id=1, source_target_pairs={{0,1},{1,2},{2,3},{3,0},{4,5},{5,6},{6,7},{7,4},{8,9},{9,10},{10,1... | collective-permute-start | bytes 393224 | tf_op jit(solution)/shard_map/ppermute | solution.py:23
  4.6 2.6 %collective-permute-start.1 = (bf16[32,16,128]{2,1,0:T(8,128)(2,1)S(1)}, bf16[32,16,128]{2,1,0:T(8,128)(2,1)S(1)}, u32[]{:S(2)}, u32[]{:S(2)}) collective-permute-start(bf16[32,16,128]{2,1,0:T(8,128)(2,1)S(1)} %get-tuple-element.16), channel_id=1, source_target_pairs={{0,2},{1,3},{2,0},{3,1},{4,6},{5,7},{6,4},{7,5},{8,10},{9,11},{10,... | collective-permute-start | bytes 393224 | tf_op jit(solution)/shard_map/ppermute | solution.py:23
  7.2 1.3 %collective-permute-start.2 = (bf16[32,16,128]{2,1,0:T(8,128)(2,1)S(1)}, bf16[32,16,128]{2,1,0:T(8,128)(2,1)S(1)}, u32[]{:S(2)}, u32[]{:S(2)}) collective-permute-start(bf16[32,16,128]{2,1,0:T(8,128)(2,1)S(1)} %get-tuple-element.15), channel_id=1, source_target_pairs={{0,3},{1,0},{2,1},{3,2},{4,7},{5,4},{6,5},{7,6},{8,11},{9,8},{10,9... | collective-permute-start | bytes 393224 | tf_op jit(solution)/shard_map/ppermute | solution.py:23
  8.6 0.7 collective-permute-start.11
  9.3 0.3 collective-permute-start.12
  9.7 0.1 copy.6
  9.8 0.6 gather_fusion
  10.4 0.6 gather_fusion.1
  11.0 0.0 collective-permute-done
  11.0 2.9 %collective-permute-start.13 = (bf16[32,16,128]{2,1,0:T(8,128)(2,1)S(1)}, bf16[32,16,128]{2,1,0:T(8,128)(2,1)S(1)}, u32[]{:S(2)}, u32[]{:S(2)}) collective-permute-start(bf16[32,16,128]{2,1,0:T(8,128)(2,1)S(1)} %get-tuple-element.26), channel_id=1, source_target_pairs={{0,3},{1,0},{2,1},{3,2},{4,7},{5,4},{6,5},{7,6},{8,11},{9,8},{10,9... | collective-permute-start | bytes 393224 | tf_op jit(solution)/shard_map/ppermute | solution.py:23
  13.9 6.9 %collective-permute-done.1 = bf16[32,16,128]{2,1,0:T(8,128)(2,1)S(1)} collective-permute-done((bf16[32,16,128]{2,1,0:T(8,128)(2,1)S(1)}, bf16[32,16,128]{2,1,0:T(8,128)(2,1)S(1)}, u32[]{:S(2)}, u32[]{:S(2)}) %collective-permute-start.1) | collective-permute-done | bytes 131104 | tf_op jit(solution)/shard_map/ppermute | solution.py:23
  20.7 0.0 collective-permute-done.2
  20.7 0.4 fusion.6
  21.2 1.8 %fusion.47 = f32[32,128,64]{2,1,0:T(8,128)S(1)} fusion(f32[32,64,128]{2,1,0:T(8,128)S(1)} %fusion.6, f32[64,64,1]{1,0,2:T(8,128)S(1)} %bitcast.175), kind=kOutput, calls=%fused_computation.110 | convolution fusion | flops 100663296 | bytes 2113536 | tf_op jit(solution)/shard_map/ba,qbd->qad/dot_general | solution.py:15
  23.0 1.8 %fusion = f32[32,64,128]{2,1,0:T(8,128)S(1)} fusion(f32[32,128,64]{2,1,0:T(8,128)S(1)} %fusion.47, f32[64,128]{0,1:T(8,128)S(1)} %copy.6, f32[128,128]{1,0:T(8,128)S(1)} %copy-done), kind=kOutput, calls=%fused_computation.5 | convolution fusion | flops 201588736 | bytes 2195456 | tf_op jit(solution)/shard_map/qad,ed->qae/dot_general | solution.py:17
  24.8 0.6 fusion.2
  25.4 0.1 broadcast_in_dim.38
  25.5 0.7 copy.27
  26.2 4.1 %collective-permute-start.3 = (bf16[32,2048]{1,0:T(8,128)(2,1)}, bf16[32,2048]{1,0:T(8,128)(2,1)}, u32[]{:S(2)}, u32[]{:S(2)}) collective-permute-start(bf16[32,2048]{1,0:T(8,128)(2,1)} %bitcast.155), channel_id=1, source_target_pairs={{0,1},{1,2},{2,3},{3,0},{4,5},{5,6},{6,7},{7,4},{8,9},{9,10},{10,1... | collective-permute-start | bytes 393224 | tf_op jit(solution)/shard_map/ppermute | solution.py:23
  30.3 2.7 %collective-permute-start.4 = (bf16[32,2048]{1,0:T(8,128)(2,1)S(1)}, bf16[32,2048]{1,0:T(8,128)(2,1)}, u32[]{:S(2)}, u32[]{:S(2)}) collective-permute-start(bf16[32,2048]{1,0:T(8,128)(2,1)S(1)} %bitcast.179), channel_id=1, source_target_pairs={{0,2},{1,3},{2,0},{3,1},{4,6},{5,7},{6,4},{7,5},{8,10},{9,11},{10,... | collective-permute-start | bytes 393224 | tf_op jit(solution)/shard_map/ppermute | solution.py:23
  33.0 0.7 copy.25
  33.7 0.0 collective-permute-done.11
  33.7 0.0 collective-permute-start.5
  33.7 0.4 fusion.14
  34.2 1.8 %fusion.48 = f32[32,128,64]{2,1,0:T(8,128)S(1)} fusion(f32[32,64,128]{2,1,0:T(8,128)S(1)} %fusion.14, f32[64,64,1]{1,0,2:T(8,128)S(1)} %bitcast.176), kind=kOutput, calls=%fused_computation.111 | convolution fusion | flops 100663296 | bytes 2113536 | tf_op jit(solution)/shard_map/ba,qbd->qad/dot_general | solution.py:15
  36.0 1.8 %fusion.1 = f32[32,64,128]{2,1,0:T(8,128)S(1)} fusion(f32[32,128,64]{2,1,0:T(8,128)S(1)} %fusion.48, f32[64,128]{0,1:T(8,128)S(1)} %copy.6, f32[128,128]{1,0:T(8,128)S(1)} %copy-done), kind=kOutput, calls=%fused_computation.6 | convolution fusion | flops 201588736 | bytes 2195456 | tf_op jit(solution)/shard_map/qad,ed->qae/dot_general | solution.py:17
  37.8 0.6 fusion.3
  38.4 0.1 broadcast_in_dim.42
  38.5 0.0 copy-start.1
  38.5 2.1 %collective-permute-start.14 = (bf16[32,2048]{1,0:T(8,128)(2,1)S(1)}, bf16[32,2048]{1,0:T(8,128)(2,1)S(1)}, u32[]{:S(2)}, u32[]{:S(2)}) collective-permute-start(bf16[32,2048]{1,0:T(8,128)(2,1)S(1)} %bitcast.182), channel_id=1, source_target_pairs={{0,1},{1,2},{2,3},{3,0},{4,5},{5,6},{6,7},{7,4},{8,9},{9,10},{10,1... | collective-permute-start | bytes 393224 | tf_op jit(solution)/shard_map/ppermute | solution.py:23
  40.6 0.3 collective-permute-start.15
  41.2 2.4 %collective-permute-start.16 = (bf16[32,2048]{1,0:T(8,128)(2,1)S(1)}, bf16[32,2048]{1,0:T(8,128)(2,1)S(1)}, u32[]{:S(2)}, u32[]{:S(2)}) collective-permute-start(bf16[32,2048]{1,0:T(8,128)(2,1)S(1)} %bitcast.180), channel_id=1, source_target_pairs={{0,3},{1,0},{2,1},{3,2},{4,7},{5,4},{6,5},{7,6},{8,11},{9,8},{10,9... | collective-permute-start | bytes 393224 | tf_op jit(solution)/shard_map/ppermute | solution.py:23
  43.5 0.9 bitcast_dynamic-update-slice_fusion.5
  44.5 0.9 bitcast_dynamic-update-slice_fusion.4
  45.4 0.9 bitcast_dynamic-update-slice_fusion.3
  46.3 1.6 %collective-permute-start.6 = (bf16[128,2048]{1,0:T(8,128)(2,1)S(1)}, bf16[128,2048]{1,0:T(8,128)(2,1)}, u32[]{:S(2)}, u32[]{:S(2)}) collective-permute-start(bf16[128,2048]{1,0:T(8,128)(2,1)S(1)} %bitcast.166), channel_id=1, source_target_pairs={{0,8},{4,12},{8,0},{12,4},{1,9},{5,13},{9,1},{13,5},{2,10},{6,14},... | collective-permute-start | bytes 1572872 | tf_op jit(solution)/shard_map/ppermute | solution.py:23
  47.9 3.7 %collective-permute-done.15 = bf16[32,2048]{1,0:T(8,128)(2,1)S(1)} collective-permute-done((bf16[32,2048]{1,0:T(8,128)(2,1)S(1)}, bf16[32,2048]{1,0:T(8,128)(2,1)S(1)}, u32[]{:S(2)}, u32[]{:S(2)}) %collective-permute-start.15) | collective-permute-done | bytes 131104 | tf_op jit(solution)/shard_map/ppermute | solution.py:23
  51.6 1.5 %collective-permute-start.17 = (bf16[128,2048]{1,0:T(8,128)(2,1)S(1)}, bf16[128,2048]{1,0:T(8,128)(2,1)}, u32[]{:S(2)}, u32[]{:S(2)}) collective-permute-start(bf16[128,2048]{1,0:T(8,128)(2,1)S(1)} %bitcast.163), channel_id=1, source_target_pairs={{0,8},{4,12},{8,0},{12,4},{1,9},{5,13},{9,1},{13,5},{2,10},{6,14},... | collective-permute-start | bytes 1572872 | tf_op jit(solution)/shard_map/ppermute | solution.py:23
  53.2 1.9 %copy.21 = bf16[64,8,16,128]{3,1,2,0:T(8,128)(2,1)} copy(bf16[64,8,16,128]{3,2,1,0:T(8,128)(2,1)S(1)} %bitcast.156) | data formatting | bytes 4194304
  55.1 6.3 %collective-permute-done.6 = bf16[128,2048]{1,0:T(8,128)(2,1)} collective-permute-done((bf16[128,2048]{1,0:T(8,128)(2,1)S(1)}, bf16[128,2048]{1,0:T(8,128)(2,1)}, u32[]{:S(2)}, u32[]{:S(2)}) %collective-permute-start.6) | collective-permute-done | bytes 524320 | tf_op jit(solution)/shard_map/ppermute | solution.py:23
  61.3 1.1 %pad_maximum_fusion = bf16[256,2048]{1,0:T(8,128)(2,1)S(1)} fusion(bf16[128,2048]{1,0:T(8,128)(2,1)} %collective-permute-done.6, bf16[128,2048]{1,0:T(8,128)(2,1)S(1)} %bitcast.167), kind=kLoop, calls=%fused_computation.15 | loop fusion | flops 2097152 | bytes 2097152 | tf_op jit(solution)/shard_map/concatenate | solution.py:66
  62.5 0.1 collective-permute-start.7
  62.6 6.9 %collective-permute-done.17 = bf16[128,2048]{1,0:T(8,128)(2,1)} collective-permute-done((bf16[128,2048]{1,0:T(8,128)(2,1)S(1)}, bf16[128,2048]{1,0:T(8,128)(2,1)}, u32[]{:S(2)}, u32[]{:S(2)}) %collective-permute-start.17) | collective-permute-done | bytes 524320 | tf_op jit(solution)/shard_map/ppermute | solution.py:23
  69.5 1.1 %pad_maximum_fusion.1 = bf16[256,2048]{1,0:T(8,128)(2,1)S(1)} fusion(bf16[128,2048]{1,0:T(8,128)(2,1)} %collective-permute-done.17, bf16[128,2048]{1,0:T(8,128)(2,1)S(1)} %bitcast.164), kind=kLoop, calls=%fused_computation.16 | loop fusion | flops 2097152 | bytes 2097152 | tf_op jit(solution)/shard_map/concatenate | solution.py:66
  70.6 0.1 collective-permute-start.18
  70.7 1.8 %convolution_convert_fusion.5 = bf16[256,512]{1,0:T(8,128)(2,1)S(1)} fusion(bf16[512,2048]{1,0:T(8,128)(2,1)S(1)} %bitcast.157, bf16[128,2048]{1,0:T(8,128)(2,1)} %collective-permute-done.6, bf16[128,2048]{1,0:T(8,128)(2,1)S(1)} %bitcast.168), kind=kOutput, calls=%fused_computation.14 | convolution fusion | flops 539099136 | bytes 3407872 | tf_op jit(solution)/shard_map/dot_general | solution.py:71
  72.6 1.8 %convolution_convert_fusion.3 = bf16[256,512]{1,0:T(8,128)(2,1)S(1)} fusion(bf16[512,2048]{1,0:T(8,128)(2,1)S(1)} %bitcast.158, bf16[128,2048]{1,0:T(8,128)(2,1)} %collective-permute-done.17, bf16[128,2048]{1,0:T(8,128)(2,1)S(1)} %bitcast.165), kind=kOutput, calls=%fused_computation.12 | convolution fusion | flops 539099136 | bytes 3407872 | tf_op jit(solution)/shard_map/dot_general | solution.py:71
  74.5 0.8 convolution_convert_fusion.4
  75.4 2.0 %collective-permute-start.10 = (bf16[1,128,512]{2,1,0:T(8,128)(2,1)S(1)}, bf16[1,128,512]{2,1,0:T(8,128)(2,1)S(1)}, u32[]{:S(2)}, u32[]{:S(2)}) collective-permute-start(bf16[1,128,512]{2,1,0:T(8,128)(2,1)S(1)} %get-tuple-element.8), channel_id=1, source_target_pairs={{0,3},{1,0},{2,1},{3,2},{4,7},{5,4},{6,5},{7,6},{8,11},{9,8},{10,9... | collective-permute-start | bytes 393224 | tf_op jit(solution)/shard_map/ppermute | solution.py:23
  77.4 3.1 %collective-permute-start.8 = (bf16[1,128,512]{2,1,0:T(8,128)(2,1)S(1)}, bf16[1,128,512]{2,1,0:T(8,128)(2,1)S(1)}, u32[]{:S(2)}, u32[]{:S(2)}) collective-permute-start(bf16[1,128,512]{2,1,0:T(8,128)(2,1)S(1)} %get-tuple-element.7), channel_id=1, source_target_pairs={{0,1},{1,2},{2,3},{3,0},{4,5},{5,6},{6,7},{7,4},{8,9},{9,10},{10,1... | collective-permute-start | bytes 393224 | tf_op jit(solution)/shard_map/ppermute | solution.py:23
  80.5 1.4 %collective-permute-start.9 = (bf16[1,128,512]{2,1,0:T(8,128)(2,1)S(1)}, bf16[1,128,512]{2,1,0:T(8,128)(2,1)S(1)}, u32[]{:S(2)}, u32[]{:S(2)}) collective-permute-start(bf16[1,128,512]{2,1,0:T(8,128)(2,1)S(1)} %get-tuple-element.9), channel_id=1, source_target_pairs={{0,2},{1,3},{2,0},{3,1},{4,6},{5,7},{6,4},{7,5},{8,10},{9,11},{10,... | collective-permute-start | bytes 393224 | tf_op jit(solution)/shard_map/ppermute | solution.py:23
  81.9 0.7 convolution_convert_fusion.2
  82.7 0.6 collective-permute-start.19
  83.3 2.9 %collective-permute-start.20 = (bf16[1,128,512]{2,1,0:T(8,128)(2,1)S(1)}, bf16[1,128,512]{2,1,0:T(8,128)(2,1)S(1)}, u32[]{:S(2)}, u32[]{:S(2)}) collective-permute-start(bf16[1,128,512]{2,1,0:T(8,128)(2,1)S(1)} %get-tuple-element.20), channel_id=1, source_target_pairs={{0,2},{1,3},{2,0},{3,1},{4,6},{5,7},{6,4},{7,5},{8,10},{9,11},{10,... | collective-permute-start | bytes 393224 | tf_op jit(solution)/shard_map/ppermute | solution.py:23
  86.2 0.9 collective-permute-done.10
  87.2 0.1 collective-permute-start.21
  87.2 0.3 collective-permute-done.8
  87.5 12.7 %collective-permute-done.9 = bf16[1,128,512]{2,1,0:T(8,128)(2,1)S(1)} collective-permute-done((bf16[1,128,512]{2,1,0:T(8,128)(2,1)S(1)}, bf16[1,128,512]{2,1,0:T(8,128)(2,1)S(1)}, u32[]{:S(2)}, u32[]{:S(2)}) %collective-permute-start.9) | collective-permute-done | bytes 131104 | tf_op jit(solution)/shard_map/ppermute | solution.py:23
  100.3 0.1 fusion.25
  100.4 2.7 %collective-permute-done.20 = bf16[1,128,512]{2,1,0:T(8,128)(2,1)S(1)} collective-permute-done((bf16[1,128,512]{2,1,0:T(8,128)(2,1)S(1)}, bf16[1,128,512]{2,1,0:T(8,128)(2,1)S(1)}, u32[]{:S(2)}, u32[]{:S(2)}) %collective-permute-start.20) | collective-permute-done | bytes 131104 | tf_op jit(solution)/shard_map/ppermute | solution.py:23
  103.0 2.3 %collective-permute-done.21 = bf16[1,128,512]{2,1,0:T(8,128)(2,1)S(1)} collective-permute-done((bf16[1,128,512]{2,1,0:T(8,128)(2,1)S(1)}, bf16[1,128,512]{2,1,0:T(8,128)(2,1)S(1)}, u32[]{:S(2)}, u32[]{:S(2)}) %collective-permute-start.21) | collective-permute-done | bytes 131104 | tf_op jit(solution)/shard_map/ppermute | solution.py:23
  105.4 0.1 fusion.23
  105.5 0.8 maximum_bitcast_fusion
  (50 shorter events, 0.8 us)
Async XLA Ops:
  0.0 20.7 %copy-start = (f32[128,128]{1,0:T(8,128)S(1)}, f32[128,128]{1,0:T(8,128)}, u32[]{:S(2)}) copy-start(f32[128,128]{1,0:T(8,128)} %param.8) | copy-start | bytes 196612
  0.0 9.6 %copy-start.4 = (f32[64,128]{1,0:T(8,128)S(1)}, f32[64,128]{1,0:T(8,128)}, u32[]{:S(2)}) copy-start(f32[64,128]{1,0:T(8,128)} %param.9) | copy-start | bytes 98308
  0.0 9.8 %copy-start.3 = (f32[64,64]{1,0:T(8,128)S(1)}, f32[64,64]{1,0:T(8,128)}, u32[]{:S(2)}) copy-start(f32[64,64]{1,0:T(8,128)} %param.7) | copy-start | bytes 49156
  1.5 9.5 %collective-permute-start = (bf16[32,16,128]{2,1,0:T(8,128)(2,1)S(1)}, bf16[32,16,128]{2,1,0:T(8,128)(2,1)S(1)}, u32[]{:S(2)}, u32[]{:S(2)}) collective-permute-start(bf16[32,16,128]{2,1,0:T(8,128)(2,1)S(1)} %get-tuple-element.17), channel_id=1, source_target_pairs={{0,1},{1,2},{2,3},{3,0},{4,5},{5,6},{6,7},{7,4},{8,9},{9,10},{10,1... | collective-permute-start | bytes 393224 | tf_op jit(solution)/shard_map/ppermute | solution.py:23
  4.6 16.2 %collective-permute-start.1 = (bf16[32,16,128]{2,1,0:T(8,128)(2,1)S(1)}, bf16[32,16,128]{2,1,0:T(8,128)(2,1)S(1)}, u32[]{:S(2)}, u32[]{:S(2)}) collective-permute-start(bf16[32,16,128]{2,1,0:T(8,128)(2,1)S(1)} %get-tuple-element.16), channel_id=1, source_target_pairs={{0,2},{1,3},{2,0},{3,1},{4,6},{5,7},{6,4},{7,5},{8,10},{9,11},{10,... | collective-permute-start | bytes 393224 | tf_op jit(solution)/shard_map/ppermute | solution.py:23
  7.2 13.6 %collective-permute-start.2 = (bf16[32,16,128]{2,1,0:T(8,128)(2,1)S(1)}, bf16[32,16,128]{2,1,0:T(8,128)(2,1)S(1)}, u32[]{:S(2)}, u32[]{:S(2)}) collective-permute-start(bf16[32,16,128]{2,1,0:T(8,128)(2,1)S(1)} %get-tuple-element.15), channel_id=1, source_target_pairs={{0,3},{1,0},{2,1},{3,2},{4,7},{5,4},{6,5},{7,6},{8,11},{9,8},{10,9... | collective-permute-start | bytes 393224 | tf_op jit(solution)/shard_map/ppermute | solution.py:23
  8.6 25.2 %collective-permute-start.11 = (bf16[32,16,128]{2,1,0:T(8,128)(2,1)S(1)}, bf16[32,16,128]{2,1,0:T(8,128)(2,1)S(1)}, u32[]{:S(2)}, u32[]{:S(2)}) collective-permute-start(bf16[32,16,128]{2,1,0:T(8,128)(2,1)S(1)} %get-tuple-element.28), channel_id=1, source_target_pairs={{0,1},{1,2},{2,3},{3,0},{4,5},{5,6},{6,7},{7,4},{8,9},{9,10},{10,1... | collective-permute-start | bytes 393224 | tf_op jit(solution)/shard_map/ppermute | solution.py:23
  9.3 24.4 %collective-permute-start.12 = (bf16[32,16,128]{2,1,0:T(8,128)(2,1)S(1)}, bf16[32,16,128]{2,1,0:T(8,128)(2,1)S(1)}, u32[]{:S(2)}, u32[]{:S(2)}) collective-permute-start(bf16[32,16,128]{2,1,0:T(8,128)(2,1)S(1)} %get-tuple-element.27), channel_id=1, source_target_pairs={{0,2},{1,3},{2,0},{3,1},{4,6},{5,7},{6,4},{7,5},{8,10},{9,11},{10,... | collective-permute-start | bytes 393224 | tf_op jit(solution)/shard_map/ppermute | solution.py:23
  11.0 22.7 %collective-permute-start.13 = (bf16[32,16,128]{2,1,0:T(8,128)(2,1)S(1)}, bf16[32,16,128]{2,1,0:T(8,128)(2,1)S(1)}, u32[]{:S(2)}, u32[]{:S(2)}) collective-permute-start(bf16[32,16,128]{2,1,0:T(8,128)(2,1)S(1)} %get-tuple-element.26), channel_id=1, source_target_pairs={{0,3},{1,0},{2,1},{3,2},{4,7},{5,4},{6,5},{7,6},{8,11},{9,8},{10,9... | collective-permute-start | bytes 393224 | tf_op jit(solution)/shard_map/ppermute | solution.py:23
  26.2 15.0 %collective-permute-start.3 = (bf16[32,2048]{1,0:T(8,128)(2,1)}, bf16[32,2048]{1,0:T(8,128)(2,1)}, u32[]{:S(2)}, u32[]{:S(2)}) collective-permute-start(bf16[32,2048]{1,0:T(8,128)(2,1)} %bitcast.155), channel_id=1, source_target_pairs={{0,1},{1,2},{2,3},{3,0},{4,5},{5,6},{6,7},{7,4},{8,9},{9,10},{10,1... | collective-permute-start | bytes 393224 | tf_op jit(solution)/shard_map/ppermute | solution.py:23
  30.3 14.1 %collective-permute-start.4 = (bf16[32,2048]{1,0:T(8,128)(2,1)S(1)}, bf16[32,2048]{1,0:T(8,128)(2,1)}, u32[]{:S(2)}, u32[]{:S(2)}) collective-permute-start(bf16[32,2048]{1,0:T(8,128)(2,1)S(1)} %bitcast.179), channel_id=1, source_target_pairs={{0,2},{1,3},{2,0},{3,1},{4,6},{5,7},{6,4},{7,5},{8,10},{9,11},{10,... | collective-permute-start | bytes 393224 | tf_op jit(solution)/shard_map/ppermute | solution.py:23
  33.7 11.7 %collective-permute-start.5 = (bf16[32,2048]{1,0:T(8,128)(2,1)}, bf16[32,2048]{1,0:T(8,128)(2,1)}, u32[]{:S(2)}, u32[]{:S(2)}) collective-permute-start(bf16[32,2048]{1,0:T(8,128)(2,1)} %bitcast.153), channel_id=1, source_target_pairs={{0,3},{1,0},{2,1},{3,2},{4,7},{5,4},{6,5},{7,6},{8,11},{9,8},{10,9... | collective-permute-start | bytes 393224 | tf_op jit(solution)/shard_map/ppermute | solution.py:23
  38.5 14.7 %copy-start.1 = (bf16[512,16,128]{2,1,0:T(8,128)(2,1)S(1)}, bf16[512,16,128]{2,1,0:T(8,128)(2,1)}, u32[]{:S(2)}) copy-start(bf16[512,16,128]{2,1,0:T(8,128)(2,1)} %param.6) | copy-start | bytes 6291460
  38.5 9.3 %collective-permute-start.14 = (bf16[32,2048]{1,0:T(8,128)(2,1)S(1)}, bf16[32,2048]{1,0:T(8,128)(2,1)S(1)}, u32[]{:S(2)}, u32[]{:S(2)}) collective-permute-start(bf16[32,2048]{1,0:T(8,128)(2,1)S(1)} %bitcast.182), channel_id=1, source_target_pairs={{0,1},{1,2},{2,3},{3,0},{4,5},{5,6},{6,7},{7,4},{8,9},{9,10},{10,1... | collective-permute-start | bytes 393224 | tf_op jit(solution)/shard_map/ppermute | solution.py:23
  40.6 10.9 %collective-permute-start.15 = (bf16[32,2048]{1,0:T(8,128)(2,1)S(1)}, bf16[32,2048]{1,0:T(8,128)(2,1)S(1)}, u32[]{:S(2)}, u32[]{:S(2)}) collective-permute-start(bf16[32,2048]{1,0:T(8,128)(2,1)S(1)} %bitcast.181), channel_id=1, source_target_pairs={{0,2},{1,3},{2,0},{3,1},{4,6},{5,7},{6,4},{7,5},{8,10},{9,11},{10,... | collective-permute-start | bytes 393224 | tf_op jit(solution)/shard_map/ppermute | solution.py:23
  41.2 10.4 %collective-permute-start.16 = (bf16[32,2048]{1,0:T(8,128)(2,1)S(1)}, bf16[32,2048]{1,0:T(8,128)(2,1)S(1)}, u32[]{:S(2)}, u32[]{:S(2)}) collective-permute-start(bf16[32,2048]{1,0:T(8,128)(2,1)S(1)} %bitcast.180), channel_id=1, source_target_pairs={{0,3},{1,0},{2,1},{3,2},{4,7},{5,4},{6,5},{7,6},{8,11},{9,8},{10,9... | collective-permute-start | bytes 393224 | tf_op jit(solution)/shard_map/ppermute | solution.py:23
  46.3 15.0 %collective-permute-start.6 = (bf16[128,2048]{1,0:T(8,128)(2,1)S(1)}, bf16[128,2048]{1,0:T(8,128)(2,1)}, u32[]{:S(2)}, u32[]{:S(2)}) collective-permute-start(bf16[128,2048]{1,0:T(8,128)(2,1)S(1)} %bitcast.166), channel_id=1, source_target_pairs={{0,8},{4,12},{8,0},{12,4},{1,9},{5,13},{9,1},{13,5},{2,10},{6,14},... | collective-permute-start | bytes 1572872 | tf_op jit(solution)/shard_map/ppermute | solution.py:23
  51.6 17.9 %collective-permute-start.17 = (bf16[128,2048]{1,0:T(8,128)(2,1)S(1)}, bf16[128,2048]{1,0:T(8,128)(2,1)}, u32[]{:S(2)}, u32[]{:S(2)}) collective-permute-start(bf16[128,2048]{1,0:T(8,128)(2,1)S(1)} %bitcast.163), channel_id=1, source_target_pairs={{0,8},{4,12},{8,0},{12,4},{1,9},{5,13},{9,1},{13,5},{2,10},{6,14},... | collective-permute-start | bytes 1572872 | tf_op jit(solution)/shard_map/ppermute | solution.py:23
  55.1 15.6 %copy-start.2 = (bf16[64,8,16,128]{3,1,2,0:T(8,128)(2,1)S(1)}, bf16[64,8,16,128]{3,1,2,0:T(8,128)(2,1)}, u32[]{:S(2)}) copy-start(bf16[64,8,16,128]{3,1,2,0:T(8,128)(2,1)} %copy.21) | copy-start | bytes 6291460
  62.5 12.0 %collective-permute-start.7 = (bf16[256,2048]{1,0:T(8,128)(2,1)S(1)}, bf16[256,2048]{1,0:T(8,128)(2,1)S(1)}, u32[]{:S(2)}, u32[]{:S(2)}) collective-permute-start(bf16[256,2048]{1,0:T(8,128)(2,1)S(1)} %pad_maximum_fusion), channel_id=1, source_target_pairs={{0,4},{4,0},{8,12},{12,8},{1,5},{5,1},{9,13},{13,9},{2,6},{6,2},{1... | collective-permute-start | bytes 3145736 | tf_op jit(solution)/shard_map/ppermute | solution.py:68
  70.6 11.3 %collective-permute-start.18 = (bf16[256,2048]{1,0:T(8,128)(2,1)S(1)}, bf16[256,2048]{1,0:T(8,128)(2,1)S(1)}, u32[]{:S(2)}, u32[]{:S(2)}) collective-permute-start(bf16[256,2048]{1,0:T(8,128)(2,1)S(1)} %pad_maximum_fusion.1), channel_id=1, source_target_pairs={{0,4},{4,0},{8,12},{12,8},{1,5},{5,1},{9,13},{13,9},{2,6},{6,2},{1... | collective-permute-start | bytes 3145736 | tf_op jit(solution)/shard_map/ppermute | solution.py:68
  75.4 11.8 %collective-permute-start.10 = (bf16[1,128,512]{2,1,0:T(8,128)(2,1)S(1)}, bf16[1,128,512]{2,1,0:T(8,128)(2,1)S(1)}, u32[]{:S(2)}, u32[]{:S(2)}) collective-permute-start(bf16[1,128,512]{2,1,0:T(8,128)(2,1)S(1)} %get-tuple-element.8), channel_id=1, source_target_pairs={{0,3},{1,0},{2,1},{3,2},{4,7},{5,4},{6,5},{7,6},{8,11},{9,8},{10,9... | collective-permute-start | bytes 393224 | tf_op jit(solution)/shard_map/ppermute | solution.py:23
  77.4 10.1 %collective-permute-start.8 = (bf16[1,128,512]{2,1,0:T(8,128)(2,1)S(1)}, bf16[1,128,512]{2,1,0:T(8,128)(2,1)S(1)}, u32[]{:S(2)}, u32[]{:S(2)}) collective-permute-start(bf16[1,128,512]{2,1,0:T(8,128)(2,1)S(1)} %get-tuple-element.7), channel_id=1, source_target_pairs={{0,1},{1,2},{2,3},{3,0},{4,5},{5,6},{6,7},{7,4},{8,9},{9,10},{10,1... | collective-permute-start | bytes 393224 | tf_op jit(solution)/shard_map/ppermute | solution.py:23
  80.5 19.8 %collective-permute-start.9 = (bf16[1,128,512]{2,1,0:T(8,128)(2,1)S(1)}, bf16[1,128,512]{2,1,0:T(8,128)(2,1)S(1)}, u32[]{:S(2)}, u32[]{:S(2)}) collective-permute-start(bf16[1,128,512]{2,1,0:T(8,128)(2,1)S(1)} %get-tuple-element.9), channel_id=1, source_target_pairs={{0,2},{1,3},{2,0},{3,1},{4,6},{5,7},{6,4},{7,5},{8,10},{9,11},{10,... | collective-permute-start | bytes 393224 | tf_op jit(solution)/shard_map/ppermute | solution.py:23
  82.7 17.6 %collective-permute-start.19 = (bf16[1,128,512]{2,1,0:T(8,128)(2,1)S(1)}, bf16[1,128,512]{2,1,0:T(8,128)(2,1)S(1)}, u32[]{:S(2)}, u32[]{:S(2)}) collective-permute-start(bf16[1,128,512]{2,1,0:T(8,128)(2,1)S(1)} %get-tuple-element.18), channel_id=1, source_target_pairs={{0,1},{1,2},{2,3},{3,0},{4,5},{5,6},{6,7},{7,4},{8,9},{9,10},{10,1... | collective-permute-start | bytes 393224 | tf_op jit(solution)/shard_map/ppermute | solution.py:23
  83.3 19.7 %collective-permute-start.20 = (bf16[1,128,512]{2,1,0:T(8,128)(2,1)S(1)}, bf16[1,128,512]{2,1,0:T(8,128)(2,1)S(1)}, u32[]{:S(2)}, u32[]{:S(2)}) collective-permute-start(bf16[1,128,512]{2,1,0:T(8,128)(2,1)S(1)} %get-tuple-element.20), channel_id=1, source_target_pairs={{0,2},{1,3},{2,0},{3,1},{4,6},{5,7},{6,4},{7,5},{8,10},{9,11},{10,... | collective-permute-start | bytes 393224 | tf_op jit(solution)/shard_map/ppermute | solution.py:23
  87.2 18.2 %collective-permute-start.21 = (bf16[1,128,512]{2,1,0:T(8,128)(2,1)S(1)}, bf16[1,128,512]{2,1,0:T(8,128)(2,1)S(1)}, u32[]{:S(2)}, u32[]{:S(2)}) collective-permute-start(bf16[1,128,512]{2,1,0:T(8,128)(2,1)S(1)} %get-tuple-element.19), channel_id=1, source_target_pairs={{0,3},{1,0},{2,1},{3,2},{4,7},{5,4},{6,5},{7,6},{8,11},{9,8},{10,9... | collective-permute-start | bytes 393224 | tf_op jit(solution)/shard_map/ppermute | solution.py:23

commit v4 on v2

v4 whole, which is shorter than its diff:
```python
import functools
import jax
import jax.numpy as jnp
from jax import lax
from jax.experimental import pallas as pl
from jax.experimental.pallas import tpu as pltpu
from jax.sharding import PartitionSpec as P

damping_term = 0.05
CHUNKS = 4
BLOCK = 32


def halves(value):
    high = value.astype(jnp.bfloat16)
    return high, (value - high.astype(jnp.float32)).astype(jnp.bfloat16)


def times(left, right):
    return jnp.dot(left, right, preferred_element_type=jnp.float32)


def three_wide(matrix):
    high, low = halves(matrix)
    return jnp.concatenate([high, low, high], axis=1)


def three_deep(matrix):
    high, low = halves(matrix)
    return jnp.concatenate([high, high, low], axis=0)


def condition_kernel(slices, rows_here, *refs):
    pieces = refs[:slices]
    enter, leave, right, back, inverse, own, other, stage = refs[slices:]
    count, _, columns = pieces[0].shape
    out_rows = 2 * rows_here
    parts = []
    for piece in pieces:
        flat = piece[...].reshape(count * rows_here, columns)
        parts.append(halves(times(flat, right[0]) + times(flat, right[1])))
    scale = jnp.concatenate([inverse[...]] * 2, axis=1)

    def gathered(at, which):
        rows = slice(at * rows_here, (at + 1) * rows_here)
        return jnp.concatenate([part[which][rows] for part in parts], axis=0)

    for at in range(0, count, 2):
        high = jnp.concatenate([gathered(at, 0), gathered(at + 1, 0)], axis=1)
        low = jnp.concatenate([gathered(at, 1), gathered(at + 1, 1)], axis=1)
        rotated = times(enter[...], jnp.concatenate([high, high, low], axis=0))
        result = times(leave[...], three_deep(rotated * scale))
        stage[at * out_rows:(at + 1) * out_rows, :] = result[:, :columns]
        stage[(at + 1) * out_rows:(at + 2) * out_rows, :] = result[:, columns:]
    high, low = halves(stage[...])
    stage[...] = times(high, back[0]) + times(low, back[0]) + times(high, back[1])
    for row in range(out_rows):
        value = stage[pl.ds(row, count, stride=out_rows), :].astype(jnp.bfloat16)
        target = own if row < rows_here else other
        at = row % rows_here * columns
        target[:, at:at + columns] = value


def condition_fast(pieces, enter, leave, in_basis, inverse):
    slices = len(pieces)
    count, rows_here, columns = pieces[0].shape
    block = min(BLOCK, count)
    width = rows_here * columns
    piece_spec = pl.BlockSpec((block, rows_here, columns), lambda step: (step, 0, 0))
    out_spec = pl.BlockSpec((block, width), lambda step: (step, 0))
    whole = pl.BlockSpec(memory_space=pltpu.VMEM)
    order = enter.shape[0]
    flops = 2 * count * columns * order * (3 * columns + 5 * order)
    return pl.pallas_call(
        functools.partial(condition_kernel, slices, rows_here),
        grid=(count // block,),
        in_specs=[piece_spec] * slices + [whole] * 5,
        out_specs=[out_spec] * 2,
        out_shape=[jax.ShapeDtypeStruct((count, width), jnp.bfloat16)] * 2,
        scratch_shapes=[pltpu.VMEM((block * 2 * rows_here, columns), jnp.float32)],
        compiler_params=pltpu.CompilerParams(vmem_limit_bytes=32 * 1024 * 1024),
        cost_estimate=pl.CostEstimate(flops=flops, bytes_accessed=(slices + 2) * count * width * 2, transcendentals=0),
    )(
        *pieces,
        three_wide(enter.T),
        three_wide(leave),
        jnp.stack(halves(in_basis)),
        jnp.stack(halves(in_basis.T)),
        inverse,
    )


def condition_plain(pieces, enter, leave, in_basis, inverse):
    high = lax.Precision.HIGH
    count, rows_here, columns = pieces[0].shape
    values = jnp.concatenate(pieces, axis=1).astype(jnp.float32)
    inner = jnp.einsum("qbc,cd->qbd", values, in_basis, precision=high)
    rotated = jnp.einsum("ba,qbd->qad", enter, inner, precision=high)
    left = jnp.einsum("ba,qad->qbd", leave, rotated * inverse, precision=high)
    result = jnp.einsum("qbd,ed->qbe", left, in_basis, precision=high).astype(jnp.bfloat16)
    flat = [result[:, at:at + rows_here].reshape(count, rows_here * columns) for at in (0, rows_here)]
    return flat


def crossed(value, axis, size, mask):
    return lax.ppermute(value, axis, [(at, at ^ mask) for at in range(size)])


def body(queries, train_grads, out_basis, in_basis, corrections):
    slices = lax.axis_size("proj")
    shares = lax.axis_size("dp")
    here = lax.axis_index("proj")
    share = lax.axis_index("dp")
    count, rows_here, columns = queries.shape
    width = rows_here * columns
    part = count // CHUNKS
    each = part // 2
    owned = shares // slices
    odd = here % 2
    train_count = train_grads.shape[0]
    train_flat = lax.optimization_barrier(train_grads.reshape(train_count, width))
    contract = (((1,), (1,)), ((), ()))
    row_blocks = out_basis.reshape(slices, rows_here, -1)
    enter = row_blocks[here ^ jnp.arange(slices)].reshape(out_basis.shape)
    leave = row_blocks[here ^ jnp.arange(2)].reshape(2 * rows_here, -1)
    inverse = 1.0 / (corrections + damping_term)
    condition = condition_fast if rows_here % 16 == 0 else condition_plain
    results = []
    token = None
    for chunk in range(CHUNKS):
        mine = lax.dynamic_slice_in_dim(queries, chunk * part + odd * each, each, 0)
        theirs = lax.dynamic_slice_in_dim(queries, chunk * part + (1 - odd) * each, each, 0)
        if token is not None:
            mine, theirs, pieces[2] = lax.optimization_barrier((mine, theirs, pieces[2]))
        if token is not None:
            waiting.append(pieces)
        else:
            waiting = []
        pieces = [mine]
        for mask in range(1, slices):
            pieces.append(crossed(theirs if mask % 2 else mine, "proj", slices, mask))
        token = pieces[-1]
    waiting.append(pieces)
    for chunk, pieces in enumerate(waiting):
        own, other = condition(pieces, enter, leave, in_basis, inverse)
        near = [own, crossed(other, "proj", slices, 1)]
        near = jnp.concatenate(near, axis=0)
        near = [near] + [crossed(near, "dp", shares, mask) for mask in range(2, shares, 2)]
        near = jnp.concatenate(near, axis=0)
        far = crossed(near, "dp", shares, 1)
        values = []
        for block in (near, far):
            value = lax.dot_general(block, train_flat, contract, preferred_element_type=jnp.float32)
            values.append(value.astype(jnp.bfloat16).reshape(shares // 2, 2, each, train_count))
        blocks = [values[at % 2][at // 2] for at in range(shares)]
        held = [jnp.stack(blocks[at * owned:(at + 1) * owned]) for at in range(slices)]
        place = share // owned
        mask = 1
        while mask < slices:
            swap = (here // mask % 2) != (place // mask % 2)
            keep = [jnp.where(swap, second, first) for first, second in zip(held[::2], held[1::2])]
            send = [jnp.where(swap, first, second) for first, second in zip(held[::2], held[1::2])]
            send = jnp.stack(send)
            if mask == 1:
                send = jnp.concatenate([send[:, :, 1:], send[:, :, :1]], axis=2)
            arrived = crossed(send, "proj", slices, mask)
            mask *= 2
            kind = jnp.bfloat16 if mask < slices else jnp.float32
            held = [(value.astype(jnp.float32) + arrived[at].astype(jnp.float32)).astype(kind) for at, value in enumerate(keep)]
        total = held[0]
        total = jnp.where(odd == 1, jnp.concatenate([total[:, 1:], total[:, :1]], axis=1), total)
        mask = 1
        while mask < owned:
            swapped = total.reshape(owned // (2 * mask), 2, mask, 2, each, train_count)
            swapped = jnp.concatenate([swapped[:, 1:], swapped[:, :1]], axis=1).reshape(total.shape)
            total = jnp.where(share // mask % 2 == 1, swapped, total)
            mask *= 2
        results.append(total.reshape(owned, part, train_count))
    return jnp.concatenate(results, axis=1).reshape(owned * count, train_count)


def solution(mesh):
    in_specs = (P(("groups", "dp"), "proj", None), P(("groups", "dp"), "proj", None), P(), P(), P())
    out_specs = P(("groups", "proj"), "dp")
    return jax.shard_map(body, mesh=mesh, in_specs=in_specs, out_specs=out_specs, check_vma=False)
```

time: 140 us -> 111 us (0.79)
  blocking collectives: 49.6 us -> 0 us
  starting transfers between devices: 14.6 us -> 33.9 us
  waiting for transfers between devices: 41.4 us -> 54.8 us
  between operations: 13.6 us -> 0.7 us
  Pallas kernels: 0 us -> 6.41 us
  matrix products: 12.5 us -> 6.83 us
    ppermute x0 -> x32, waiting for transfers between devices: none -> 54.8 us  [crossed(): return lax.ppermute(value, axis, [(at, at ^ mask) for at in range(size)])]
    all_to_all x3 -> x0, blocking collectives: 49.6 us -> none  [the longest x2 33.1 us: body(): lax.all_to_all(conditioned, 'proj', split_axis=1, concat_axis=0, tiled=True)]
    ppermute x0 -> x32, starting transfers between devices: none -> 33.9 us  [crossed(): return lax.ppermute(value, axis, [(at, at ^ mask) for at in range(size)])]
    all_to_all x3 -> x0, waiting for transfers between devices: 29.3 us -> none  [the longest x2 14.8 us: body(): lax.all_to_all(sent, 'proj', split_axis=0, concat_axis=0, tiled=True)]
    all_to_all x3 -> x0, starting transfers between devices: 14.5 us -> none  [the longest x2 8.07 us: body(): lax.all_to_all(sent, 'proj', split_axis=0, concat_axis=0, tiled=True)]
    all_gather x2 -> x0, waiting for transfers between devices: 12 us -> none  [body(): left = lax.all_gather(flat, 'dp', axis=0, tiled=True)]
    pallas_call x0 -> x4, Pallas kernels: none -> 6.41 us  [condition_fast(): pl.pallas_call(functools.partial(condition_kernel, slices, rows_here), gr...]
    dot_general x10 -> x8, matrix products: 12.5 us -> 6.83 us  [body(): lax.dot_general(block, train_flat, contract, preferred_element_type=jnp.f...]
  transfers between devices with their start and end apart: 5 -> 32, of which waited for: 3 -> 15; matrix products, arithmetic and copies ran while one was open for 10% -> 9% of each run, Pallas kernels for 0% -> 6%
where the time goes in v4:
time: 111 us; the launch traced here: 110 us
  waiting for transfers between devices  54.8 us (49%)
  starting transfers between devices  33.9 us (31%)
  matrix products  6.83 us (6%)
  Pallas kernels  6.41 us (6%)
  local copies, waits for them, and re-layouts  5.8 us (5%)
  other arithmetic  1.94 us (2%)
    ppermute x32, waiting for transfers between devices, crossed(): return lax.ppermute(value, axis, [(at, at ^ mask) for at in range(size)])  54.8 us
    ppermute x32, starting transfers between devices, crossed(): return lax.ppermute(value, axis, [(at, at ^ mask) for at in range(size)])  33.9 us
    dot_general x8, matrix products, body(): lax.dot_general(block, train_flat, contract, preferred_element_type=jnp.f...  6.83 us
    pallas_call x4, Pallas kernels, condition_fast(): pl.pallas_call(functools.partial(condition_kernel, slices, rows_here), gr...  6.41 us
    unnamed x16, local copies, waits for them, and re-layouts  2.32 us
  transfers between devices with their start and end apart: 32, of which 15 were waited for; matrix products, arithmetic and copies ran while one was open for 9% of the time, Pallas kernels for 6%

profile of v4, /device:TPU:0, one launch (start us, length us, event | category | flops | bytes accessed | tf_op | source)
XLA Modules:
  0.0 110.4 jit_solution(6819361430924381967)
XLA Ops:
  0.0 2.2 %constant_dynamic-slice_fusion.6 = (bf16[32,16,128]{2,1,0:T(8,128)(2,1)}, bf16[32,16,128]{2,1,0:T(8,128)(2,1)S(1)}, bf16[32,16,128]{2,1,0:T(8,128)(2,1)S(1)}, bf...) fusion(bf16[256,16,128]{2,1,0:T(8,128)(2,1)} %param.5, ...), kind=kLoop, calls=%fused_computation.169 | loop fusion | bytes 2097184 | tf_op jit(solution)/shard_map/dynamic_slice | solution.py:132
  2.2 3.1 %collective-permute-start = (bf16[32,16,128]{2,1,0:T(8,128)(2,1)}, bf16[32,16,128]{2,1,0:T(8,128)(2,1)S(1)}, u32[]{:S(2)}, u32[]{:S(2)}) collective-permute-start(bf16[32,16,128]{2,1,0:T(8,128)(2,1)} %get-tuple-element.43), channel_id=1, source_target_pairs={{0,1},{1,0},{2,3},{3,2},{4,5},{5,4},{6,7},{7,6},{8,9},{9,8},{10,11... | collective-permute-start | bytes 393224 | tf_op jit(solution)/shard_map/ppermute | solution.py:106
  5.3 2.5 %collective-permute-start.2 = (bf16[32,16,128]{2,1,0:T(8,128)(2,1)}, bf16[32,16,128]{2,1,0:T(8,128)(2,1)S(1)}, u32[]{:S(2)}, u32[]{:S(2)}) collective-permute-start(bf16[32,16,128]{2,1,0:T(8,128)(2,1)} %get-tuple-element.43), channel_id=1, source_target_pairs={{0,3},{1,2},{2,1},{3,0},{4,7},{5,6},{6,5},{7,4},{8,11},{9,10},{10,... | collective-permute-start | bytes 393224 | tf_op jit(solution)/shard_map/ppermute | solution.py:106
  7.7 0.1 collective-permute-start.1
  7.9 0.1 copy.8
  8.0 0.6 gather_fusion
  8.6 0.1 copy.7
  8.7 0.5 gather_fusion.1
  9.3 0.1 pad_maximum_fusion.14.refs_4_
  9.4 0.1 pad_maximum_fusion.15.refs_5_
  9.5 2.1 %copy.11 = bf16[64,8,16,128]{3,1,2,0:T(8,128)(2,1)S(1)} copy(bf16[64,8,16,128]{3,2,1,0:T(8,128)(2,1)} %bitcast.241) | data formatting | bytes 4194304
  11.7 8.1 %collective-permute-done.1.refs_2_ = bf16[32,16,128]{2,1,0:T(8,128)(2,1)S(1)} collective-permute-done((bf16[32,16,128]{2,1,0:T(8,128)(2,1)S(1)}, bf16[32,16,128]{2,1,0:T(8,128)(2,1)S(1)}, u32[]{:S(2)}, u32[]{:S(2)}) %collective-permute-start.1) | collective-permute-done | bytes 131104 | tf_op jit(solution)/shard_map/ppermute | solution.py:106
  19.7 2.9 %collective-permute-start.10 = (bf16[32,16,128]{2,1,0:T(8,128)(2,1)}, bf16[32,16,128]{2,1,0:T(8,128)(2,1)S(1)}, u32[]{:S(2)}, u32[]{:S(2)}) collective-permute-start(bf16[32,16,128]{2,1,0:T(8,128)(2,1)} %get-tuple-element.26), channel_id=1, source_target_pairs={{0,3},{1,2},{2,1},{3,0},{4,7},{5,6},{6,5},{7,4},{8,11},{9,10},{10,... | collective-permute-start | bytes 393224 | tf_op jit(solution)/shard_map/ppermute | solution.py:106
  22.6 1.6 %shard_map.55 = (bf16[32,2048]{1,0:T(8,128)(2,1)S(1)}, bf16[32,2048]{1,0:T(8,128)(2,1)S(1)}) custom-call(bf16[32,16,128]{2,1,0:T(8,128)(2,1)S(1)} %get-tuple-element.48.refs_0_, bf16[32,16,128]{2,1,0:T(8,128)(2,1)S(1)} %collective-permute-done.refs_1_, bf16[32,16,128]{2,1,0:T(8,128)(2,1)S(1)} %collective-permute-done.1.refs_2_, ...), custom_call_target="tpu_custom_call" | custom-call | flops 369098752 | bytes 786432 | tf_op jit(solution)/shard_map/pallas_call | solution.py:74
  24.2 2.1 %collective-permute-start.3 = (bf16[32,2048]{1,0:T(8,128)(2,1)S(1)}, bf16[32,2048]{1,0:T(8,128)(2,1)S(1)}, u32[]{:S(2)}, u32[]{:S(2)}) collective-permute-start(bf16[32,2048]{1,0:T(8,128)(2,1)S(1)} %get-tuple-element.24), channel_id=1, source_target_pairs={{0,1},{1,0},{2,3},{3,2},{4,5},{5,4},{6,7},{7,6},{8,9},{9,8},{10,11... | collective-permute-start | bytes 393224 | tf_op jit(solution)/shard_map/ppermute | solution.py:106
  26.3 6.9 %collective-permute-done.9.refs_2_ = bf16[32,16,128]{2,1,0:T(8,128)(2,1)S(1)} collective-permute-done((bf16[32,16,128]{2,1,0:T(8,128)(2,1)S(1)}, bf16[32,16,128]{2,1,0:T(8,128)(2,1)S(1)}, u32[]{:S(2)}, u32[]{:S(2)}) %collective-permute-start.9) | collective-permute-done | bytes 131104 | tf_op jit(solution)/shard_map/ppermute | solution.py:106
  33.2 2.0 %collective-permute-start.16 = (bf16[32,16,128]{2,1,0:T(8,128)(2,1)S(1)}, bf16[32,16,128]{2,1,0:T(8,128)(2,1)S(1)}, u32[]{:S(2)}, u32[]{:S(2)}) collective-permute-start(bf16[32,16,128]{2,1,0:T(8,128)(2,1)S(1)} %get-tuple-element.31), channel_id=1, source_target_pairs={{0,1},{1,0},{2,3},{3,2},{4,5},{5,4},{6,7},{7,6},{8,9},{9,8},{10,11... | collective-permute-start | bytes 393224 | tf_op jit(solution)/shard_map/ppermute | solution.py:106
  35.2 2.5 %collective-permute-start.18 = (bf16[32,16,128]{2,1,0:T(8,128)(2,1)S(1)}, bf16[32,16,128]{2,1,0:T(8,128)(2,1)S(1)}, u32[]{:S(2)}, u32[]{:S(2)}) collective-permute-start(bf16[32,16,128]{2,1,0:T(8,128)(2,1)S(1)} %get-tuple-element.31), channel_id=1, source_target_pairs={{0,3},{1,2},{2,1},{3,0},{4,7},{5,6},{6,5},{7,4},{8,11},{9,10},{10,... | collective-permute-start | bytes 393224 | tf_op jit(solution)/shard_map/ppermute | solution.py:106
  37.7 1.6 %collective-permute-start.4 = (bf16[64,2048]{1,0:T(8,128)(2,1)S(1)}, bf16[64,2048]{1,0:T(8,128)(2,1)S(1)}, u32[]{:S(2)}, u32[]{:S(2)}) collective-permute-start(bf16[64,2048]{1,0:T(8,128)(2,1)S(1)} %pad_maximum_fusion), channel_id=1, source_target_pairs={{0,8},{4,12},{8,0},{12,4},{1,9},{5,13},{9,1},{13,5},{2,10},{6,14},... | collective-permute-start | bytes 786440 | tf_op jit(solution)/shard_map/ppermute | solution.py:106
  39.3 1.6 %shard_map.56 = (bf16[32,2048]{1,0:T(8,128)(2,1)S(1)}, bf16[32,2048]{1,0:T(8,128)(2,1)S(1)}) custom-call(bf16[32,16,128]{2,1,0:T(8,128)(2,1)S(1)} %get-tuple-element.25.refs_0_, bf16[32,16,128]{2,1,0:T(8,128)(2,1)S(1)} %collective-permute-done.8.refs_1_, bf16[32,16,128]{2,1,0:T(8,128)(2,1)S(1)} %collective-permute-done.9.refs_2_, ...), custom_call_target="tpu_custom_call" | custom-call | flops 369098752 | bytes 786432 | tf_op jit(solution)/shard_map/pallas_call | solution.py:74
  40.9 0.1 collective-permute-start.11
  41.0 1.9 %collective-permute-start.17 = (bf16[32,16,128]{2,1,0:T(8,128)(2,1)S(1)}, bf16[32,16,128]{2,1,0:T(8,128)(2,1)S(1)}, u32[]{:S(2)}, u32[]{:S(2)}) collective-permute-start(bf16[32,16,128]{2,1,0:T(8,128)(2,1)S(1)} %get-tuple-element.30.refs_0_), channel_id=1, source_target_pairs={{0,2},{1,3},{2,0},{3,1},{4,6},{5,7},{6,4},{7,5},{8,10},{9,11},{10,... | collective-permute-start | bytes 393224 | tf_op jit(solution)/shard_map/ppermute | solution.py:106
  42.9 5.7 %collective-permute-done.17.refs_2_ = bf16[32,16,128]{2,1,0:T(8,128)(2,1)S(1)} collective-permute-done((bf16[32,16,128]{2,1,0:T(8,128)(2,1)S(1)}, bf16[32,16,128]{2,1,0:T(8,128)(2,1)S(1)}, u32[]{:S(2)}, u32[]{:S(2)}) %collective-permute-start.17) | collective-permute-done | bytes 131104 | tf_op jit(solution)/shard_map/ppermute | solution.py:106
  48.6 0.3 collective-permute-start.24
  49.0 1.3 %collective-permute-start.26 = (bf16[32,16,128]{2,1,0:T(8,128)(2,1)S(1)}, bf16[32,16,128]{2,1,0:T(8,128)(2,1)S(1)}, u32[]{:S(2)}, u32[]{:S(2)}) collective-permute-start(bf16[32,16,128]{2,1,0:T(8,128)(2,1)S(1)} %get-tuple-element.36), channel_id=1, source_target_pairs={{0,3},{1,2},{2,1},{3,0},{4,7},{5,6},{6,5},{7,4},{8,11},{9,10},{10,... | collective-permute-start | bytes 393224 | tf_op jit(solution)/shard_map/ppermute | solution.py:106
  50.4 1.0 collective-permute-start.12
  51.4 1.6 %shard_map.57 = (bf16[32,2048]{1,0:T(8,128)(2,1)S(1)}, bf16[32,2048]{1,0:T(8,128)(2,1)S(1)}) custom-call(bf16[32,16,128]{2,1,0:T(8,128)(2,1)S(1)} %get-tuple-element.30.refs_0_, bf16[32,16,128]{2,1,0:T(8,128)(2,1)S(1)} %collective-permute-done.16.refs_1_, bf16[32,16,128]{2,1,0:T(8,128)(2,1)S(1)} %collective-permute-done.17.refs_2_, ...), custom_call_target="tpu_custom_call" | custom-call | flops 369098752 | bytes 786432 | tf_op jit(solution)/shard_map/pallas_call | solution.py:74
  53.0 0.1 collective-permute-start.19
  53.1 2.9 %collective-permute-start.25 = (bf16[32,16,128]{2,1,0:T(8,128)(2,1)S(1)}, bf16[32,16,128]{2,1,0:T(8,128)(2,1)S(1)}, u32[]{:S(2)}, u32[]{:S(2)}) collective-permute-start(bf16[32,16,128]{2,1,0:T(8,128)(2,1)S(1)} %get-tuple-element.35.refs_0_), channel_id=1, source_target_pairs={{0,2},{1,3},{2,0},{3,1},{4,6},{5,7},{6,4},{7,5},{8,10},{9,11},{10,... | collective-permute-start | bytes 393224 | tf_op jit(solution)/shard_map/ppermute | solution.py:106
  56.0 2.4 %collective-permute-done.19 = bf16[32,2048]{1,0:T(8,128)(2,1)S(1)} collective-permute-done((bf16[32,2048]{1,0:T(8,128)(2,1)S(1)}, bf16[32,2048]{1,0:T(8,128)(2,1)S(1)}, u32[]{:S(2)}, u32[]{:S(2)}) %collective-permute-start.19) | collective-permute-done | bytes 131104 | tf_op jit(solution)/shard_map/ppermute | solution.py:106
  58.5 2.5 %collective-permute-start.20 = (bf16[64,2048]{1,0:T(8,128)(2,1)S(1)}, bf16[64,2048]{1,0:T(8,128)(2,1)S(1)}, u32[]{:S(2)}, u32[]{:S(2)}) collective-permute-start(bf16[64,2048]{1,0:T(8,128)(2,1)S(1)} %pad_maximum_fusion.2), channel_id=1, source_target_pairs={{0,8},{4,12},{8,0},{12,4},{1,9},{5,13},{9,1},{13,5},{2,10},{6,14},... | collective-permute-start | bytes 786440 | tf_op jit(solution)/shard_map/ppermute | solution.py:106
  60.9 1.1 %collective-permute-done.25.refs_2_ = bf16[32,16,128]{2,1,0:T(8,128)(2,1)S(1)} collective-permute-done((bf16[32,16,128]{2,1,0:T(8,128)(2,1)S(1)}, bf16[32,16,128]{2,1,0:T(8,128)(2,1)S(1)}, u32[]{:S(2)}, u32[]{:S(2)}) %collective-permute-start.25) | collective-permute-done | bytes 131104 | tf_op jit(solution)/shard_map/ppermute | solution.py:106
  62.1 1.6 %shard_map.58 = (bf16[32,2048]{1,0:T(8,128)(2,1)S(1)}, bf16[32,2048]{1,0:T(8,128)(2,1)S(1)}) custom-call(bf16[32,16,128]{2,1,0:T(8,128)(2,1)S(1)} %get-tuple-element.35.refs_0_, bf16[32,16,128]{2,1,0:T(8,128)(2,1)S(1)} %collective-permute-done.24.refs_1_, bf16[32,16,128]{2,1,0:T(8,128)(2,1)S(1)} %collective-permute-done.25.refs_2_, ...), custom_call_target="tpu_custom_call" | custom-call | flops 369098752 | bytes 786432 | tf_op jit(solution)/shard_map/pallas_call | solution.py:74
  63.7 0.1 collective-permute-start.27
  63.8 0.8 convolution_convert_fusion.6
  64.7 0.1 collective-permute-start.13
  64.8 4.0 %collective-permute-done.27 = bf16[32,2048]{1,0:T(8,128)(2,1)S(1)} collective-permute-done((bf16[32,2048]{1,0:T(8,128)(2,1)S(1)}, bf16[32,2048]{1,0:T(8,128)(2,1)S(1)}, u32[]{:S(2)}, u32[]{:S(2)}) %collective-permute-start.27) | collective-permute-done | bytes 131104 | tf_op jit(solution)/shard_map/ppermute | solution.py:106
  68.8 0.3 collective-permute-start.28
  69.1 0.8 convolution_convert_fusion.4
  70.0 0.1 collective-permute-start.21
  70.1 0.8 convolution_convert_fusion.2
  70.9 4.8 %collective-permute-done.28 = bf16[64,2048]{1,0:T(8,128)(2,1)S(1)} collective-permute-done((bf16[64,2048]{1,0:T(8,128)(2,1)S(1)}, bf16[64,2048]{1,0:T(8,128)(2,1)S(1)}, u32[]{:S(2)}, u32[]{:S(2)}) %collective-permute-start.28) | collective-permute-done | bytes 262176 | tf_op jit(solution)/shard_map/ppermute | solution.py:106
  75.7 0.1 collective-permute-start.29
  75.8 0.8 convolution_convert_fusion
  76.6 0.8 convolution_convert_fusion.7
  77.5 1.0 convolution_convert_fusion.5
  78.6 0.5 collective-permute-start.6
  79.1 1.6 %collective-permute-start.14 = (bf16[2,1,2,32,512]{4,3,2,1,0:T(8,128)(2,1)S(1)}, bf16[2,1,2,32,512]{4,3,2,1,0:T(8,128)(2,1)S(1)}, u32[]{:S(2)}, u32[]{:S(2)}) collective-permute-start(bf16[2,1,2,32,512]{4,3,2,1,0:T(8,128)(2,1)S(1)} %fusion.2), channel_id=1, source_target_pairs={{0,1},{1,0},{2,3},{3,2},{4,5},{5,4},{6,7},{7,6},{8,9},{9,8},{10,11... | collective-permute-start | bytes 393224 | tf_op jit(solution)/shard_map/ppermute | solution.py:106
  80.8 4.2 %collective-permute-done.6 = bf16[2,1,2,32,512]{4,3,2,1,0:T(8,128)(2,1)S(1)} collective-permute-done((bf16[2,1,2,32,512]{4,3,2,1,0:T(8,128)(2,1)S(1)}, bf16[2,1,2,32,512]{4,3,2,1,0:T(8,128)(2,1)S(1)}, u32[]{:S(2)}, u32[]{:S(2)}) %collective-permute-start.6) | collective-permute-done | bytes 131104 | tf_op jit(solution)/shard_map/ppermute | solution.py:106
  85.0 0.1 collective-permute-start.7
  85.1 2.3 %collective-permute-done.14 = bf16[2,1,2,32,512]{4,3,2,1,0:T(8,128)(2,1)S(1)} collective-permute-done((bf16[2,1,2,32,512]{4,3,2,1,0:T(8,128)(2,1)S(1)}, bf16[2,1,2,32,512]{4,3,2,1,0:T(8,128)(2,1)S(1)}, u32[]{:S(2)}, u32[]{:S(2)}) %collective-permute-start.14) | collective-permute-done | bytes 131104 | tf_op jit(solution)/shard_map/ppermute | solution.py:106
  87.4 0.7 collective-permute-start.15
  88.1 0.8 convolution_convert_fusion.3
  88.9 2.8 %collective-permute-done.7 = bf16[1,1,2,32,512]{4,3,2,1,0:T(8,128)(2,1)S(1)} collective-permute-done((bf16[1,1,2,32,512]{4,3,2,1,0:T(8,128)(2,1)S(1)}, bf16[1,1,2,32,512]{4,3,2,1,0:T(8,128)(2,1)S(1)}, u32[]{:S(2)}, u32[]{:S(2)}) %collective-permute-start.7) | collective-permute-done | bytes 65568 | tf_op jit(solution)/shard_map/ppermute | solution.py:106
  91.8 1.8 %collective-permute-done.15 = bf16[1,1,2,32,512]{4,3,2,1,0:T(8,128)(2,1)S(1)} collective-permute-done((bf16[1,1,2,32,512]{4,3,2,1,0:T(8,128)(2,1)S(1)}, bf16[1,1,2,32,512]{4,3,2,1,0:T(8,128)(2,1)S(1)}, u32[]{:S(2)}, u32[]{:S(2)}) %collective-permute-start.15) | collective-permute-done | bytes 65568 | tf_op jit(solution)/shard_map/ppermute | solution.py:106
  93.8 0.8 convolution_convert_fusion.1
  94.8 0.1 collective-permute-start.22
  94.9 2.1 %collective-permute-start.30 = (bf16[2,1,2,32,512]{4,3,2,1,0:T(8,128)(2,1)S(1)}, bf16[2,1,2,32,512]{4,3,2,1,0:T(8,128)(2,1)S(1)}, u32[]{:S(2)}, u32[]{:S(2)}) collective-permute-start(bf16[2,1,2,32,512]{4,3,2,1,0:T(8,128)(2,1)S(1)} %fusion), channel_id=1, source_target_pairs={{0,1},{1,0},{2,3},{3,2},{4,5},{5,4},{6,7},{7,6},{8,9},{9,8},{10,11... | collective-permute-start | bytes 393224 | tf_op jit(solution)/shard_map/ppermute | solution.py:106
  97.0 4.3 %collective-permute-done.22 = bf16[2,1,2,32,512]{4,3,2,1,0:T(8,128)(2,1)S(1)} collective-permute-done((bf16[2,1,2,32,512]{4,3,2,1,0:T(8,128)(2,1)S(1)}, bf16[2,1,2,32,512]{4,3,2,1,0:T(8,128)(2,1)S(1)}, u32[]{:S(2)}, u32[]{:S(2)}) %collective-permute-start.22) | collective-permute-done | bytes 131104 | tf_op jit(solution)/shard_map/ppermute | solution.py:106
  101.4 1.5 %collective-permute-done.30 = bf16[2,1,2,32,512]{4,3,2,1,0:T(8,128)(2,1)S(1)} collective-permute-done((bf16[2,1,2,32,512]{4,3,2,1,0:T(8,128)(2,1)S(1)}, bf16[2,1,2,32,512]{4,3,2,1,0:T(8,128)(2,1)S(1)}, u32[]{:S(2)}, u32[]{:S(2)}) %collective-permute-start.30) | collective-permute-done | bytes 131104 | tf_op jit(solution)/shard_map/ppermute | solution.py:106
  102.9 1.5 %collective-permute-start.31 = (bf16[1,1,2,32,512]{4,3,2,1,0:T(8,128)(2,1)S(1)}, bf16[1,1,2,32,512]{4,3,2,1,0:T(8,128)(2,1)S(1)}, u32[]{:S(2)}, u32[]{:S(2)}) collective-permute-start(bf16[1,1,2,32,512]{4,3,2,1,0:T(8,128)(2,1)S(1)} %get-tuple-element.83), channel_id=1, source_target_pairs={{0,2},{1,3},{2,0},{3,1},{4,6},{5,7},{6,4},{7,5},{8,10},{9,11},{10,... | collective-permute-start | bytes 196616 | tf_op jit(solution)/shard_map/ppermute | solution.py:106
  104.4 4.2 %collective-permute-done.23 = bf16[1,1,2,32,512]{4,3,2,1,0:T(8,128)(2,1)S(1)} collective-permute-done((bf16[1,1,2,32,512]{4,3,2,1,0:T(8,128)(2,1)S(1)}, bf16[1,1,2,32,512]{4,3,2,1,0:T(8,128)(2,1)S(1)}, u32[]{:S(2)}, u32[]{:S(2)}) %collective-permute-start.23) | collective-permute-done | bytes 65568 | tf_op jit(solution)/shard_map/ppermute | solution.py:106
  108.7 0.6 collective-permute-done.31
  109.5 0.8 maximum_bitcast_fusion
  (85 shorter events, 1.3 us)
Async XLA Ops:
  0.0 8.0 %copy-start = (f32[64,64]{1,0:T(8,128)S(1)}, f32[64,64]{1,0:T(8,128)}, u32[]{:S(2)}) copy-start(f32[64,64]{1,0:T(8,128)} %param.7) | copy-start | bytes 49156
  0.0 7.9 %copy-start.1 = (f32[128,128]{1,0:T(8,128)S(1)}, f32[128,128]{1,0:T(8,128)}, u32[]{:S(2)}) copy-start(f32[128,128]{1,0:T(8,128)} %param.8) | copy-start | bytes 196612
  0.0 9.3 %copy-start.2 = (f32[64,128]{1,0:T(8,128)S(1)}, f32[64,128]{1,0:T(8,128)}, u32[]{:S(2)}) copy-start(f32[64,128]{1,0:T(8,128)} %param.9) | copy-start | bytes 98308
  2.2 20.4 %collective-permute-start = (bf16[32,16,128]{2,1,0:T(8,128)(2,1)}, bf16[32,16,128]{2,1,0:T(8,128)(2,1)S(1)}, u32[]{:S(2)}, u32[]{:S(2)}) collective-permute-start(bf16[32,16,128]{2,1,0:T(8,128)(2,1)} %get-tuple-element.43), channel_id=1, source_target_pairs={{0,1},{1,0},{2,3},{3,2},{4,5},{5,4},{6,7},{7,6},{8,9},{9,8},{10,11... | collective-permute-start | bytes 393224 | tf_op jit(solution)/shard_map/ppermute | solution.py:106
  5.3 17.3 %collective-permute-start.2 = (bf16[32,16,128]{2,1,0:T(8,128)(2,1)}, bf16[32,16,128]{2,1,0:T(8,128)(2,1)S(1)}, u32[]{:S(2)}, u32[]{:S(2)}) collective-permute-start(bf16[32,16,128]{2,1,0:T(8,128)(2,1)} %get-tuple-element.43), channel_id=1, source_target_pairs={{0,3},{1,2},{2,1},{3,0},{4,7},{5,6},{6,5},{7,4},{8,11},{9,10},{10,... | collective-permute-start | bytes 393224 | tf_op jit(solution)/shard_map/ppermute | solution.py:106
  7.7 12.0 %collective-permute-start.1 = (bf16[32,16,128]{2,1,0:T(8,128)(2,1)S(1)}, bf16[32,16,128]{2,1,0:T(8,128)(2,1)S(1)}, u32[]{:S(2)}, u32[]{:S(2)}) collective-permute-start(bf16[32,16,128]{2,1,0:T(8,128)(2,1)S(1)} %get-tuple-element.48.refs_0_), channel_id=1, source_target_pairs={{0,2},{1,3},{2,0},{3,1},{4,6},{5,7},{6,4},{7,5},{8,10},{9,11},{10,... | collective-permute-start | bytes 393224 | tf_op jit(solution)/shard_map/ppermute | solution.py:106
  19.7 19.6 %collective-permute-start.10 = (bf16[32,16,128]{2,1,0:T(8,128)(2,1)}, bf16[32,16,128]{2,1,0:T(8,128)(2,1)S(1)}, u32[]{:S(2)}, u32[]{:S(2)}) collective-permute-start(bf16[32,16,128]{2,1,0:T(8,128)(2,1)} %get-tuple-element.26), channel_id=1, source_target_pairs={{0,3},{1,2},{2,1},{3,0},{4,7},{5,6},{6,5},{7,4},{8,11},{9,10},{10,... | collective-permute-start | bytes 393224 | tf_op jit(solution)/shard_map/ppermute | solution.py:106
  22.6 16.7 %collective-permute-start.8 = (bf16[32,16,128]{2,1,0:T(8,128)(2,1)}, bf16[32,16,128]{2,1,0:T(8,128)(2,1)S(1)}, u32[]{:S(2)}, u32[]{:S(2)}) collective-permute-start(bf16[32,16,128]{2,1,0:T(8,128)(2,1)} %get-tuple-element.26), channel_id=1, source_target_pairs={{0,1},{1,0},{2,3},{3,2},{4,5},{5,4},{6,7},{7,6},{8,9},{9,8},{10,11... | collective-permute-start | bytes 393224 | tf_op jit(solution)/shard_map/ppermute | solution.py:106
  24.2 13.5 %collective-permute-start.3 = (bf16[32,2048]{1,0:T(8,128)(2,1)S(1)}, bf16[32,2048]{1,0:T(8,128)(2,1)S(1)}, u32[]{:S(2)}, u32[]{:S(2)}) collective-permute-start(bf16[32,2048]{1,0:T(8,128)(2,1)S(1)} %get-tuple-element.24), channel_id=1, source_target_pairs={{0,1},{1,0},{2,3},{3,2},{4,5},{5,4},{6,7},{7,6},{8,9},{9,8},{10,11... | collective-permute-start | bytes 393224 | tf_op jit(solution)/shard_map/ppermute | solution.py:106
  26.3 6.9 %collective-permute-start.9 = (bf16[32,16,128]{2,1,0:T(8,128)(2,1)S(1)}, bf16[32,16,128]{2,1,0:T(8,128)(2,1)S(1)}, u32[]{:S(2)}, u32[]{:S(2)}) collective-permute-start(bf16[32,16,128]{2,1,0:T(8,128)(2,1)S(1)} %get-tuple-element.25.refs_0_), channel_id=1, source_target_pairs={{0,2},{1,3},{2,0},{3,1},{4,6},{5,7},{6,4},{7,5},{8,10},{9,11},{10,... | collective-permute-start | bytes 393224 | tf_op jit(solution)/shard_map/ppermute | solution.py:106
  33.2 17.1 %collective-permute-start.16 = (bf16[32,16,128]{2,1,0:T(8,128)(2,1)S(1)}, bf16[32,16,128]{2,1,0:T(8,128)(2,1)S(1)}, u32[]{:S(2)}, u32[]{:S(2)}) collective-permute-start(bf16[32,16,128]{2,1,0:T(8,128)(2,1)S(1)} %get-tuple-element.31), channel_id=1, source_target_pairs={{0,1},{1,0},{2,3},{3,2},{4,5},{5,4},{6,7},{7,6},{8,9},{9,8},{10,11... | collective-permute-start | bytes 393224 | tf_op jit(solution)/shard_map/ppermute | solution.py:106
  35.2 16.2 %collective-permute-start.18 = (bf16[32,16,128]{2,1,0:T(8,128)(2,1)S(1)}, bf16[32,16,128]{2,1,0:T(8,128)(2,1)S(1)}, u32[]{:S(2)}, u32[]{:S(2)}) collective-permute-start(bf16[32,16,128]{2,1,0:T(8,128)(2,1)S(1)} %get-tuple-element.31), channel_id=1, source_target_pairs={{0,3},{1,2},{2,1},{3,0},{4,7},{5,6},{6,5},{7,4},{8,11},{9,10},{10,... | collective-permute-start | bytes 393224 | tf_op jit(solution)/shard_map/ppermute | solution.py:106
  37.7 15.4 %collective-permute-start.4 = (bf16[64,2048]{1,0:T(8,128)(2,1)S(1)}, bf16[64,2048]{1,0:T(8,128)(2,1)S(1)}, u32[]{:S(2)}, u32[]{:S(2)}) collective-permute-start(bf16[64,2048]{1,0:T(8,128)(2,1)S(1)} %pad_maximum_fusion), channel_id=1, source_target_pairs={{0,8},{4,12},{8,0},{12,4},{1,9},{5,13},{9,1},{13,5},{2,10},{6,14},... | collective-permute-start | bytes 786440 | tf_op jit(solution)/shard_map/ppermute | solution.py:106
  40.9 8.1 %collective-permute-start.11 = (bf16[32,2048]{1,0:T(8,128)(2,1)S(1)}, bf16[32,2048]{1,0:T(8,128)(2,1)S(1)}, u32[]{:S(2)}, u32[]{:S(2)}) collective-permute-start(bf16[32,2048]{1,0:T(8,128)(2,1)S(1)} %get-tuple-element.29), channel_id=1, source_target_pairs={{0,1},{1,0},{2,3},{3,2},{4,5},{5,4},{6,7},{7,6},{8,9},{9,8},{10,11... | collective-permute-start | bytes 393224 | tf_op jit(solution)/shard_map/ppermute | solution.py:106
  41.0 7.6 %collective-permute-start.17 = (bf16[32,16,128]{2,1,0:T(8,128)(2,1)S(1)}, bf16[32,16,128]{2,1,0:T(8,128)(2,1)S(1)}, u32[]{:S(2)}, u32[]{:S(2)}) collective-permute-start(bf16[32,16,128]{2,1,0:T(8,128)(2,1)S(1)} %get-tuple-element.30.refs_0_), channel_id=1, source_target_pairs={{0,2},{1,3},{2,0},{3,1},{4,6},{5,7},{6,4},{7,5},{8,10},{9,11},{10,... | collective-permute-start | bytes 393224 | tf_op jit(solution)/shard_map/ppermute | solution.py:106
  48.6 9.9 %collective-permute-start.24 = (bf16[32,16,128]{2,1,0:T(8,128)(2,1)S(1)}, bf16[32,16,128]{2,1,0:T(8,128)(2,1)S(1)}, u32[]{:S(2)}, u32[]{:S(2)}) collective-permute-start(bf16[32,16,128]{2,1,0:T(8,128)(2,1)S(1)} %get-tuple-element.36), channel_id=1, source_target_pairs={{0,1},{1,0},{2,3},{3,2},{4,5},{5,4},{6,7},{7,6},{8,9},{9,8},{10,11... | collective-permute-start | bytes 393224 | tf_op jit(solution)/shard_map/ppermute | solution.py:106
  49.0 13.1 %collective-permute-start.26 = (bf16[32,16,128]{2,1,0:T(8,128)(2,1)S(1)}, bf16[32,16,128]{2,1,0:T(8,128)(2,1)S(1)}, u32[]{:S(2)}, u32[]{:S(2)}) collective-permute-start(bf16[32,16,128]{2,1,0:T(8,128)(2,1)S(1)} %get-tuple-element.36), channel_id=1, source_target_pairs={{0,3},{1,2},{2,1},{3,0},{4,7},{5,6},{6,5},{7,4},{8,11},{9,10},{10,... | collective-permute-start | bytes 393224 | tf_op jit(solution)/shard_map/ppermute | solution.py:106
  50.4 14.3 %collective-permute-start.12 = (bf16[64,2048]{1,0:T(8,128)(2,1)S(1)}, bf16[64,2048]{1,0:T(8,128)(2,1)S(1)}, u32[]{:S(2)}, u32[]{:S(2)}) collective-permute-start(bf16[64,2048]{1,0:T(8,128)(2,1)S(1)} %pad_maximum_fusion.1), channel_id=1, source_target_pairs={{0,8},{4,12},{8,0},{12,4},{1,9},{5,13},{9,1},{13,5},{2,10},{6,14},... | collective-permute-start | bytes 786440 | tf_op jit(solution)/shard_map/ppermute | solution.py:106
  53.0 5.5 %collective-permute-start.19 = (bf16[32,2048]{1,0:T(8,128)(2,1)S(1)}, bf16[32,2048]{1,0:T(8,128)(2,1)S(1)}, u32[]{:S(2)}, u32[]{:S(2)}) collective-permute-start(bf16[32,2048]{1,0:T(8,128)(2,1)S(1)} %get-tuple-element.34), channel_id=1, source_target_pairs={{0,1},{1,0},{2,3},{3,2},{4,5},{5,4},{6,7},{7,6},{8,9},{9,8},{10,11... | collective-permute-start | bytes 393224 | tf_op jit(solution)/shard_map/ppermute | solution.py:106
  53.1 9.0 %collective-permute-start.25 = (bf16[32,16,128]{2,1,0:T(8,128)(2,1)S(1)}, bf16[32,16,128]{2,1,0:T(8,128)(2,1)S(1)}, u32[]{:S(2)}, u32[]{:S(2)}) collective-permute-start(bf16[32,16,128]{2,1,0:T(8,128)(2,1)S(1)} %get-tuple-element.35.refs_0_), channel_id=1, source_target_pairs={{0,2},{1,3},{2,0},{3,1},{4,6},{5,7},{6,4},{7,5},{8,10},{9,11},{10,... | collective-permute-start | bytes 393224 | tf_op jit(solution)/shard_map/ppermute | solution.py:106
  58.5 18.1 %collective-permute-start.5 = (bf16[128,2048]{1,0:T(8,128)(2,1)S(1)}, bf16[128,2048]{1,0:T(8,128)(2,1)S(1)}, u32[]{:S(2)}, u32[]{:S(2)}) collective-permute-start(bf16[128,2048]{1,0:T(8,128)(2,1)S(1)} %constant_dynamic-update-slice_fusion), channel_id=1, source_target_pairs={{0,4},{4,0},{8,12},{12,8},{1,5},{5,1},{9,13},{13,9},{2,6},{6,2},{1... | collective-permute-start | bytes 1572872 | tf_op jit(solution)/shard_map/ppermute | solution.py:106
  58.5 11.4 %collective-permute-start.20 = (bf16[64,2048]{1,0:T(8,128)(2,1)S(1)}, bf16[64,2048]{1,0:T(8,128)(2,1)S(1)}, u32[]{:S(2)}, u32[]{:S(2)}) collective-permute-start(bf16[64,2048]{1,0:T(8,128)(2,1)S(1)} %pad_maximum_fusion.2), channel_id=1, source_target_pairs={{0,8},{4,12},{8,0},{12,4},{1,9},{5,13},{9,1},{13,5},{2,10},{6,14},... | collective-permute-start | bytes 786440 | tf_op jit(solution)/shard_map/ppermute | solution.py:106
  63.7 5.0 %collective-permute-start.27 = (bf16[32,2048]{1,0:T(8,128)(2,1)S(1)}, bf16[32,2048]{1,0:T(8,128)(2,1)S(1)}, u32[]{:S(2)}, u32[]{:S(2)}) collective-permute-start(bf16[32,2048]{1,0:T(8,128)(2,1)S(1)} %get-tuple-element.38), channel_id=1, source_target_pairs={{0,1},{1,0},{2,3},{3,2},{4,5},{5,4},{6,7},{7,6},{8,9},{9,8},{10,11... | collective-permute-start | bytes 393224 | tf_op jit(solution)/shard_map/ppermute | solution.py:106
  64.7 12.8 %collective-permute-start.13 = (bf16[128,2048]{1,0:T(8,128)(2,1)S(1)}, bf16[128,2048]{1,0:T(8,128)(2,1)S(1)}, u32[]{:S(2)}, u32[]{:S(2)}) collective-permute-start(bf16[128,2048]{1,0:T(8,128)(2,1)S(1)} %constant_dynamic-update-slice_fusion.3), channel_id=1, source_target_pairs={{0,4},{4,0},{8,12},{12,8},{1,5},{5,1},{9,13},{13,9},{2,6},{6,2},{1... | collective-permute-start | bytes 1572872 | tf_op jit(solution)/shard_map/ppermute | solution.py:106
  68.8 6.9 %collective-permute-start.28 = (bf16[64,2048]{1,0:T(8,128)(2,1)S(1)}, bf16[64,2048]{1,0:T(8,128)(2,1)S(1)}, u32[]{:S(2)}, u32[]{:S(2)}) collective-permute-start(bf16[64,2048]{1,0:T(8,128)(2,1)S(1)} %pad_maximum_fusion.3), channel_id=1, source_target_pairs={{0,8},{4,12},{8,0},{12,4},{1,9},{5,13},{9,1},{13,5},{2,10},{6,14},... | collective-permute-start | bytes 786440 | tf_op jit(solution)/shard_map/ppermute | solution.py:106
  70.0 18.1 %collective-permute-start.21 = (bf16[128,2048]{1,0:T(8,128)(2,1)S(1)}, bf16[128,2048]{1,0:T(8,128)(2,1)S(1)}, u32[]{:S(2)}, u32[]{:S(2)}) collective-permute-start(bf16[128,2048]{1,0:T(8,128)(2,1)S(1)} %constant_dynamic-update-slice_fusion.6), channel_id=1, source_target_pairs={{0,4},{4,0},{8,12},{12,8},{1,5},{5,1},{9,13},{13,9},{2,6},{6,2},{1... | collective-permute-start | bytes 1572872 | tf_op jit(solution)/shard_map/ppermute | solution.py:106
  75.7 18.1 %collective-permute-start.29 = (bf16[128,2048]{1,0:T(8,128)(2,1)S(1)}, bf16[128,2048]{1,0:T(8,128)(2,1)S(1)}, u32[]{:S(2)}, u32[]{:S(2)}) collective-permute-start(bf16[128,2048]{1,0:T(8,128)(2,1)S(1)} %constant_dynamic-update-slice_fusion.9), channel_id=1, source_target_pairs={{0,4},{4,0},{8,12},{12,8},{1,5},{5,1},{9,13},{13,9},{2,6},{6,2},{1... | collective-permute-start | bytes 1572872 | tf_op jit(solution)/shard_map/ppermute | solution.py:106
  78.6 6.4 %collective-permute-start.6 = (bf16[2,1,2,32,512]{4,3,2,1,0:T(8,128)(2,1)S(1)}, bf16[2,1,2,32,512]{4,3,2,1,0:T(8,128)(2,1)S(1)}, u32[]{:S(2)}, u32[]{:S(2)}) collective-permute-start(bf16[2,1,2,32,512]{4,3,2,1,0:T(8,128)(2,1)S(1)} %fusion.3), channel_id=1, source_target_pairs={{0,1},{1,0},{2,3},{3,2},{4,5},{5,4},{6,7},{7,6},{8,9},{9,8},{10,11... | collective-permute-start | bytes 393224 | tf_op jit(solution)/shard_map/ppermute | solution.py:106
  79.1 8.2 %collective-permute-start.14 = (bf16[2,1,2,32,512]{4,3,2,1,0:T(8,128)(2,1)S(1)}, bf16[2,1,2,32,512]{4,3,2,1,0:T(8,128)(2,1)S(1)}, u32[]{:S(2)}, u32[]{:S(2)}) collective-permute-start(bf16[2,1,2,32,512]{4,3,2,1,0:T(8,128)(2,1)S(1)} %fusion.2), channel_id=1, source_target_pairs={{0,1},{1,0},{2,3},{3,2},{4,5},{5,4},{6,7},{7,6},{8,9},{9,8},{10,11... | collective-permute-start | bytes 393224 | tf_op jit(solution)/shard_map/ppermute | solution.py:106
  85.0 6.7 %collective-permute-start.7 = (bf16[1,1,2,32,512]{4,3,2,1,0:T(8,128)(2,1)S(1)}, bf16[1,1,2,32,512]{4,3,2,1,0:T(8,128)(2,1)S(1)}, u32[]{:S(2)}, u32[]{:S(2)}) collective-permute-start(bf16[1,1,2,32,512]{4,3,2,1,0:T(8,128)(2,1)S(1)} %get-tuple-element.68), channel_id=1, source_target_pairs={{0,2},{1,3},{2,0},{3,1},{4,6},{5,7},{6,4},{7,5},{8,10},{9,11},{10,... | collective-permute-start | bytes 196616 | tf_op jit(solution)/shard_map/ppermute | solution.py:106
  87.4 6.2 %collective-permute-start.15 = (bf16[1,1,2,32,512]{4,3,2,1,0:T(8,128)(2,1)S(1)}, bf16[1,1,2,32,512]{4,3,2,1,0:T(8,128)(2,1)S(1)}, u32[]{:S(2)}, u32[]{:S(2)}) collective-permute-start(bf16[1,1,2,32,512]{4,3,2,1,0:T(8,128)(2,1)S(1)} %get-tuple-element.73), channel_id=1, source_target_pairs={{0,2},{1,3},{2,0},{3,1},{4,6},{5,7},{6,4},{7,5},{8,10},{9,11},{10,... | collective-permute-start | bytes 196616 | tf_op jit(solution)/shard_map/ppermute | solution.py:106
  94.8 6.5 %collective-permute-start.22 = (bf16[2,1,2,32,512]{4,3,2,1,0:T(8,128)(2,1)S(1)}, bf16[2,1,2,32,512]{4,3,2,1,0:T(8,128)(2,1)S(1)}, u32[]{:S(2)}, u32[]{:S(2)}) collective-permute-start(bf16[2,1,2,32,512]{4,3,2,1,0:T(8,128)(2,1)S(1)} %fusion.1), channel_id=1, source_target_pairs={{0,1},{1,0},{2,3},{3,2},{4,5},{5,4},{6,7},{7,6},{8,9},{9,8},{10,11... | collective-permute-start | bytes 393224 | tf_op jit(solution)/shard_map/ppermute | solution.py:106
  94.9 8.0 %collective-permute-start.30 = (bf16[2,1,2,32,512]{4,3,2,1,0:T(8,128)(2,1)S(1)}, bf16[2,1,2,32,512]{4,3,2,1,0:T(8,128)(2,1)S(1)}, u32[]{:S(2)}, u32[]{:S(2)}) collective-permute-start(bf16[2,1,2,32,512]{4,3,2,1,0:T(8,128)(2,1)S(1)} %fusion), channel_id=1, source_target_pairs={{0,1},{1,0},{2,3},{3,2},{4,5},{5,4},{6,7},{7,6},{8,9},{9,8},{10,11... | collective-permute-start | bytes 393224 | tf_op jit(solution)/shard_map/ppermute | solution.py:106
  101.3 7.3 %collective-permute-start.23 = (bf16[1,1,2,32,512]{4,3,2,1,0:T(8,128)(2,1)S(1)}, bf16[1,1,2,32,512]{4,3,2,1,0:T(8,128)(2,1)S(1)}, u32[]{:S(2)}, u32[]{:S(2)}) collective-permute-start(bf16[1,1,2,32,512]{4,3,2,1,0:T(8,128)(2,1)S(1)} %get-tuple-element.78), channel_id=1, source_target_pairs={{0,2},{1,3},{2,0},{3,1},{4,6},{5,7},{6,4},{7,5},{8,10},{9,11},{10,... | collective-permute-start | bytes 196616 | tf_op jit(solution)/shard_map/ppermute | solution.py:106
  102.9 6.4 %collective-permute-start.31 = (bf16[1,1,2,32,512]{4,3,2,1,0:T(8,128)(2,1)S(1)}, bf16[1,1,2,32,512]{4,3,2,1,0:T(8,128)(2,1)S(1)}, u32[]{:S(2)}, u32[]{:S(2)}) collective-permute-start(bf16[1,1,2,32,512]{4,3,2,1,0:T(8,128)(2,1)S(1)} %get-tuple-element.83), channel_id=1, source_target_pairs={{0,2},{1,3},{2,0},{3,1},{4,6},{5,7},{6,4},{7,5},{8,10},{9,11},{10,... | collective-permute-start | bytes 196616 | tf_op jit(solution)/shard_map/ppermute | solution.py:106

commit v5 on v4

--- a/solution.py
+++ b/solution.py
@@ -7,8 +7,8 @@
 from jax.sharding import PartitionSpec as P
 
 damping_term = 0.05
-CHUNKS = 4
-BLOCK = 32
+CHUNKS = (6, 4, 4, 2)
+BLOCK = 64
 
 
 def halves(value):
@@ -16,12 +16,17 @@
     return high, (value - high.astype(jnp.float32)).astype(jnp.bfloat16)
 
 
+def basis_halves(matrix):
+    high = lax.reduce_precision(matrix, 8, 7)
+    return high.astype(jnp.bfloat16), (matrix - high).astype(jnp.bfloat16)
+
+
 def times(left, right):
     return jnp.dot(left, right, preferred_element_type=jnp.float32)
 
 
 def three_wide(matrix):
-    high, low = halves(matrix)
+    high, low = basis_halves(matrix)
     return jnp.concatenate([high, low, high], axis=1)
 
 
@@ -84,8 +89,8 @@
         *pieces,
         three_wide(enter.T),
         three_wide(leave),
-        jnp.stack(halves(in_basis)),
-        jnp.stack(halves(in_basis.T)),
+        jnp.stack(basis_halves(in_basis)),
+        jnp.stack(basis_halves(in_basis.T)),
         inverse,
     )
 
@@ -106,6 +111,63 @@
     return lax.ppermute(value, axis, [(at, at ^ mask) for at in range(size)])
 
 
+def exchange_queries(mine, theirs, slices):
+    pieces = [mine]
+    for mask in range(1, slices):
+        pieces.append(crossed(theirs if mask % 2 else mine, "proj", slices, mask))
+    return pieces
+
+
+def spread_rows(own, other, slices):
+    return jnp.concatenate([own, crossed(other, "proj", slices, 1)], axis=0)
+
+
+def spread_shares(near, shares):
+    return jnp.concatenate([near] + [crossed(near, "dp", shares, mask) for mask in range(2, shares, 2)], axis=0)
+
+
+def products(near, train_flat, shares):
+    far = crossed(near, "dp", shares, 1)
+    contract = (((1,), (1,)), ((), ()))
+    values = []
+    for block in (near, far):
+        value = lax.dot_general(block, train_flat, contract, preferred_element_type=jnp.float32)
+        values.append(value.astype(jnp.bfloat16).reshape(shares // 2, 2, -1, train_flat.shape[0]))
+    return [values[at % 2][at // 2] for at in range(shares)]
+
+
+def split_scores(held, mask, here, place):
+    swap = (here // mask % 2) != (place // mask % 2)
+    keep = [jnp.where(swap, second, first) for first, second in zip(held[::2], held[1::2])]
+    send = jnp.stack([jnp.where(swap, first, second) for first, second in zip(held[::2], held[1::2])])
+    if mask == 1:
+        send = jnp.concatenate([send[:, :, 1:], send[:, :, :1]], axis=2)
+    return keep, send
+
+
+def add_scores(keep, send, mask, slices):
+    arrived = crossed(send, "proj", slices, mask)
+    kind = jnp.bfloat16 if 2 * mask < slices else jnp.float32
+    return [(value.astype(jnp.float32) + arrived[at].astype(jnp.float32)).astype(kind) for at, value in enumerate(keep)]
+
+
+def after(value, *tokens):
+    tokens = [token for token in tokens if token is not None]
+    return lax.optimization_barrier((value, tokens))[0] if tokens else value
+
+
+def in_order(total, odd, share):
+    owned, _, each, train_count = total.shape
+    total = jnp.where(odd == 1, jnp.concatenate([total[:, 1:], total[:, :1]], axis=1), total)
+    mask = 1
+    while mask < owned:
+        swapped = total.reshape(owned // (2 * mask), 2, mask, 2, each, train_count)
+        swapped = jnp.concatenate([swapped[:, 1:], swapped[:, :1]], axis=1).reshape(total.shape)
+        total = jnp.where(share // mask % 2 == 1, swapped, total)
+        mask *= 2
+    return total.reshape(owned, 2 * each, train_count)
+
+
 def body(queries, train_grads, out_basis, in_basis, corrections):
     slices = lax.axis_size("proj")
     shares = lax.axis_size("dp")
@@ -113,69 +175,47 @@
     share = lax.axis_index("dp")
     count, rows_here, columns = queries.shape
     width = rows_here * columns
-    part = count // CHUNKS
-    each = part // 2
     owned = shares // slices
+    place = share // owned
     odd = here % 2
     train_count = train_grads.shape[0]
     train_flat = lax.optimization_barrier(train_grads.reshape(train_count, width))
-    contract = (((1,), (1,)), ((), ()))
     row_blocks = out_basis.reshape(slices, rows_here, -1)
     enter = row_blocks[here ^ jnp.arange(slices)].reshape(out_basis.shape)
     leave = row_blocks[here ^ jnp.arange(2)].reshape(2 * rows_here, -1)
     inverse = 1.0 / (corrections + damping_term)
     condition = condition_fast if rows_here % 16 == 0 else condition_plain
+    parts = [count * size // sum(CHUNKS) for size in CHUNKS]
+    chunks = len(parts)
+    source = queries
+    raw = []
+    for chunk, part in enumerate(parts):
+        first, each = sum(parts[:chunk]), part // 2
+        mine = lax.dynamic_slice_in_dim(source, first + odd * each, each, 0)
+        theirs = lax.dynamic_slice_in_dim(source, first + (1 - odd) * each, each, 0)
+        if chunk == 0:
+            mine, theirs, source = lax.optimization_barrier((mine, theirs, source))
+        raw.append((mine, theirs))
+    pieces, rows, near, sent = {}, {}, {}, {}
     results = []
-    token = None
-    for chunk in range(CHUNKS):
-        mine = lax.dynamic_slice_in_dim(queries, chunk * part + odd * each, each, 0)
-        theirs = lax.dynamic_slice_in_dim(queries, chunk * part + (1 - odd) * each, each, 0)
-        if token is not None:
-            mine, theirs, pieces[2] = lax.optimization_barrier((mine, theirs, pieces[2]))
-        if token is not None:
-            waiting.append(pieces)
-        else:
-            waiting = []
-        pieces = [mine]
-        for mask in range(1, slices):
-            pieces.append(crossed(theirs if mask % 2 else mine, "proj", slices, mask))
-        token = pieces[-1]
-    waiting.append(pieces)
-    for chunk, pieces in enumerate(waiting):
-        own, other = condition(pieces, enter, leave, in_basis, inverse)
-        near = [own, crossed(other, "proj", slices, 1)]
-        near = jnp.concatenate(near, axis=0)
-        near = [near] + [crossed(near, "dp", shares, mask) for mask in range(2, shares, 2)]
-        near = jnp.concatenate(near, axis=0)
-        far = crossed(near, "dp", shares, 1)
-        values = []
-        for block in (near, far):
-            value = lax.dot_general(block, train_flat, contract, preferred_element_type=jnp.float32)
-            values.append(value.astype(jnp.bfloat16).reshape(shares // 2, 2, each, train_count))
-        blocks = [values[at % 2][at // 2] for at in range(shares)]
-        held = [jnp.stack(blocks[at * owned:(at + 1) * owned]) for at in range(slices)]
-        place = share // owned
+    for chunk in range(chunks):
+        earlier = pieces[chunk - 1][1] if chunk else None
+        mine, theirs = after(raw[chunk], earlier, rows.get(chunk - 2), near.get(chunk - 3))
+        pieces[chunk] = exchange_queries(mine, theirs, slices)
+        ready = after(pieces[chunk], near.get(chunk - 1), sent.get((chunk - 2, 1)))
+        rows[chunk] = condition(ready, enter, leave, in_basis, inverse)
+        own, other = rows[chunk]
+        near[chunk] = after(spread_rows(own, other, slices), sent.get((chunk - 2, 2)))
+        full = after(spread_shares(near[chunk], shares), sent.get((chunk - 1, 1)))
+        blocks = products(full, train_flat, shares)
+        now = [jnp.stack(blocks[at * owned:(at + 1) * owned]) for at in range(slices)]
         mask = 1
         while mask < slices:
-            swap = (here // mask % 2) != (place // mask % 2)
-            keep = [jnp.where(swap, second, first) for first, second in zip(held[::2], held[1::2])]
-            send = [jnp.where(swap, first, second) for first, second in zip(held[::2], held[1::2])]
-            send = jnp.stack(send)
-            if mask == 1:
-                send = jnp.concatenate([send[:, :, 1:], send[:, :, :1]], axis=2)
-            arrived = crossed(send, "proj", slices, mask)
+            keep, send = split_scores(now, mask, here, place)
+            sent[chunk, mask] = send
+            now = add_scores(keep, send, mask, slices)
             mask *= 2
-            kind = jnp.bfloat16 if mask < slices else jnp.float32
-            held = [(value.astype(jnp.float32) + arrived[at].astype(jnp.float32)).astype(kind) for at, value in enumerate(keep)]
-        total = held[0]
-        total = jnp.where(odd == 1, jnp.concatenate([total[:, 1:], total[:, :1]], axis=1), total)
-        mask = 1
-        while mask < owned:
-            swapped = total.reshape(owned // (2 * mask), 2, mask, 2, each, train_count)
-            swapped = jnp.concatenate([swapped[:, 1:], swapped[:, :1]], axis=1).reshape(total.shape)
-            total = jnp.where(share // mask % 2 == 1, swapped, total)
-            mask *= 2
-        results.append(total.reshape(owned, part, train_count))
+        results.append(in_order(now[0], odd, share))
     return jnp.concatenate(results, axis=1).reshape(owned * count, train_count)
 
 

time: 111 us -> 132 us (1.19)
  waiting for transfers between devices: 54.8 us -> 74.6 us
  starting transfers between devices: 33.9 us -> 29.6 us
  local copies, waits for them, and re-layouts: 5.8 us -> 8.48 us
  other arithmetic: 1.94 us -> 3.86 us
    ppermute x32, waiting for transfers between devices: 54.8 us -> 74.6 us  [crossed(): return lax.ppermute(value, axis, [(at, at ^ mask) for at in range(size)])]
    ppermute x32, starting transfers between devices: 33.9 us -> 29.6 us  [crossed(): return lax.ppermute(value, axis, [(at, at ^ mask) for at in range(size)])]
    unnamed x16 -> x13, local copies, waits for them, and re-layouts: 2.32 us -> 3.8 us
    dynamic_slice x1 -> x3, local copies, waits for them, and re-layouts: 2.19 us -> 2.74 us  [body(): theirs = lax.dynamic_slice_in_dim(source, first + (1 - odd) * each, each, 0)]
  transfers between devices with their start and end apart: 32 -> 32, of which waited for: 15 -> 17; matrix products, arithmetic and copies ran while one was open for 9% -> 13% of each run, Pallas kernels for 6% -> 5%
where the time goes in v5:
time: 132 us; the launch traced here: 131 us
  waiting for transfers between devices  74.6 us (57%)
  starting transfers between devices  29.6 us (22%)
  local copies, waits for them, and re-layouts  8.48 us (6%)
  matrix products  7.67 us (6%)
  Pallas kernels  6.46 us (5%)
  other arithmetic  3.86 us (3%)
    ppermute x32, waiting for transfers between devices, crossed(): return lax.ppermute(value, axis, [(at, at ^ mask) for at in range(size)])  74.6 us
    ppermute x32, starting transfers between devices, crossed(): return lax.ppermute(value, axis, [(at, at ^ mask) for at in range(size)])  29.6 us
    dot_general x8, matrix products, products(): lax.dot_general(block, train_flat, contract, preferred_element_type=jnp.f...  7.67 us
    pallas_call x4, Pallas kernels, condition_fast(): pl.pallas_call(functools.partial(condition_kernel, slices, rows_here), gr...  6.46 us
    unnamed x13, local copies, waits for them, and re-layouts  3.8 us
    dynamic_slice x3, local copies, waits for them, and re-layouts, body(): theirs = lax.dynamic_slice_in_dim(source, first + (1 - odd) * each, each, 0)  2.74 us
  transfers between devices with their start and end apart: 32, of which 17 were waited for; matrix products, arithmetic and copies ran while one was open for 13% of the time, Pallas kernels for 5%

profile of v5, /device:TPU:0, one launch (start us, length us, event | category | flops | bytes accessed | tf_op | source)
XLA Modules:
  0.0 131.4 jit_solution(3857559583436442226)
XLA Ops:
  0.0 1.1 constant_dynamic-slice_fusion.6
  1.1 3.1 %collective-permute-start = (bf16[48,16,128]{2,1,0:T(8,128)(2,1)S(1)}, bf16[48,16,128]{2,1,0:T(8,128)(2,1)S(1)}, u32[]{:S(2)}, u32[]{:S(2)}) collective-permute-start(bf16[48,16,128]{2,1,0:T(8,128)(2,1)S(1)} %get-tuple-element.40), channel_id=1, source_target_pairs={{0,1},{1,0},{2,3},{3,2},{4,5},{5,4},{6,7},{7,6},{8,9},{9,8},{10,11... | collective-permute-start | bytes 589832 | tf_op jit(solution)/shard_map/ppermute | solution.py:111
  4.3 2.5 %collective-permute-start.2 = (bf16[48,16,128]{2,1,0:T(8,128)(2,1)S(1)}, bf16[48,16,128]{2,1,0:T(8,128)(2,1)S(1)}, u32[]{:S(2)}, u32[]{:S(2)}) collective-permute-start(bf16[48,16,128]{2,1,0:T(8,128)(2,1)S(1)} %get-tuple-element.40), channel_id=1, source_target_pairs={{0,3},{1,2},{2,1},{3,0},{4,7},{5,6},{6,5},{7,4},{8,11},{9,10},{10,... | collective-permute-start | bytes 589832 | tf_op jit(solution)/shard_map/ppermute | solution.py:111
  6.7 0.1 collective-permute-start.1
  6.9 0.9 fusion.45
  7.7 0.9 copy.8
  8.7 0.6 gather_fusion
  9.3 0.5 gather_fusion.1
  9.9 0.1 pad_maximum_fusion.15.refs_4_
  10.1 0.7 constant_dynamic-slice_fusion.4
  10.9 1.9 %collective-permute-start.8 = (bf16[32,16,128]{2,1,0:T(8,128)(2,1)S(1)}, bf16[32,16,128]{2,1,0:T(8,128)(2,1)S(1)}, u32[]{:S(2)}, u32[]{:S(2)}) collective-permute-start(bf16[32,16,128]{2,1,0:T(8,128)(2,1)S(1)} %get-tuple-element.45), channel_id=1, source_target_pairs={{0,1},{1,0},{2,3},{3,2},{4,5},{5,4},{6,7},{7,6},{8,9},{9,8},{10,11... | collective-permute-start | bytes 393224 | tf_op jit(solution)/shard_map/ppermute | solution.py:111
  12.7 3.7 %collective-permute-start.10 = (bf16[32,16,128]{2,1,0:T(8,128)(2,1)S(1)}, bf16[32,16,128]{2,1,0:T(8,128)(2,1)S(1)}, u32[]{:S(2)}, u32[]{:S(2)}) collective-permute-start(bf16[32,16,128]{2,1,0:T(8,128)(2,1)S(1)} %get-tuple-element.45), channel_id=1, source_target_pairs={{0,3},{1,2},{2,1},{3,0},{4,7},{5,6},{6,5},{7,4},{8,11},{9,10},{10,... | collective-permute-start | bytes 393224 | tf_op jit(solution)/shard_map/ppermute | solution.py:111
  16.5 0.6 collective-permute-start.9
  17.0 13.9 %collective-permute-done.1.refs_2_ = bf16[48,16,128]{2,1,0:T(8,128)(2,1)S(1)} collective-permute-done((bf16[48,16,128]{2,1,0:T(8,128)(2,1)S(1)}, bf16[48,16,128]{2,1,0:T(8,128)(2,1)S(1)}, u32[]{:S(2)}, u32[]{:S(2)}) %collective-permute-start.1) | collective-permute-done | bytes 196640 | tf_op jit(solution)/shard_map/ppermute | solution.py:111
  30.9 2.2 %shard_map.55 = (bf16[48,2048]{1,0:T(8,128)(2,1)S(1)}, bf16[48,2048]{1,0:T(8,128)(2,1)S(1)}) custom-call(bf16[48,16,128]{2,1,0:T(8,128)(2,1)S(1)} %get-tuple-element.39.refs_0_, bf16[48,16,128]{2,1,0:T(8,128)(2,1)S(1)} %collective-permute-done.refs_1_, bf16[48,16,128]{2,1,0:T(8,128)(2,1)S(1)} %collective-permute-done.1.refs_2_, ...), custom_call_target="tpu_custom_call" | custom-call | flops 553648128 | bytes 1179648 | tf_op jit(solution)/shard_map/pallas_call | solution.py:79
  33.1 0.2 collective-permute-start.3
  33.3 6.2 %collective-permute-done.3 = bf16[48,2048]{1,0:T(8,128)(2,1)S(1)} collective-permute-done((bf16[48,2048]{1,0:T(8,128)(2,1)S(1)}, bf16[48,2048]{1,0:T(8,128)(2,1)S(1)}, u32[]{:S(2)}, u32[]{:S(2)}) %collective-permute-start.3) | collective-permute-done | bytes 196640 | tf_op jit(solution)/shard_map/ppermute | solution.py:111
  39.5 1.6 %collective-permute-start.4 = (bf16[96,2048]{1,0:T(8,128)(2,1)S(1)}, bf16[96,2048]{1,0:T(8,128)(2,1)S(1)}, u32[]{:S(2)}, u32[]{:S(2)}) collective-permute-start(bf16[96,2048]{1,0:T(8,128)(2,1)S(1)} %get-tuple-element.99), channel_id=1, source_target_pairs={{0,8},{4,12},{8,0},{12,4},{1,9},{5,13},{9,1},{13,5},{2,10},{6,14},... | collective-permute-start | bytes 1179656 | tf_op jit(solution)/shard_map/ppermute | solution.py:111
  41.1 1.6 %shard_map.56 = (bf16[32,2048]{1,0:T(8,128)(2,1)S(1)}, bf16[32,2048]{1,0:T(8,128)(2,1)S(1)}) custom-call(bf16[32,16,128]{2,1,0:T(8,128)(2,1)S(1)} %get-tuple-element.46.refs_0_, bf16[32,16,128]{2,1,0:T(8,128)(2,1)S(1)} %collective-permute-done.8.refs_1_, bf16[32,16,128]{2,1,0:T(8,128)(2,1)S(1)} %collective-permute-done.9.refs_2_, ...), custom_call_target="tpu_custom_call" | custom-call | flops 369098752 | bytes 786432 | tf_op jit(solution)/shard_map/pallas_call | solution.py:79
  42.8 0.7 constant_dynamic-update-slice_fusion.6
  43.5 4.3 %collective-permute-done.11 = bf16[32,2048]{1,0:T(8,128)(2,1)S(1)} collective-permute-done((bf16[32,2048]{1,0:T(8,128)(2,1)S(1)}, bf16[32,2048]{1,0:T(8,128)(2,1)S(1)}, u32[]{:S(2)}, u32[]{:S(2)}) %collective-permute-start.11) | collective-permute-done | bytes 131104 | tf_op jit(solution)/shard_map/ppermute | solution.py:111
  47.8 0.7 constant_dynamic-update-slice_fusion.5
  48.5 0.5 collective-permute-start.12
  49.0 0.7 collective-permute-done.4
  50.0 2.1 %copy.11 = bf16[64,8,16,128]{3,1,2,0:T(8,128)(2,1)S(1)} copy(bf16[64,8,16,128]{3,2,1,0:T(8,128)(2,1)} %bitcast.235) | data formatting | bytes 4194304
  52.1 0.9 constant_dynamic-slice_fusion
  53.0 1.7 %collective-permute-start.18 = (bf16[32,16,128]{2,1,0:T(8,128)(2,1)}, bf16[32,16,128]{2,1,0:T(8,128)(2,1)S(1)}, u32[]{:S(2)}, u32[]{:S(2)}) collective-permute-start(bf16[32,16,128]{2,1,0:T(8,128)(2,1)} %get-tuple-element.54), channel_id=1, source_target_pairs={{0,3},{1,2},{2,1},{3,0},{4,7},{5,6},{6,5},{7,4},{8,11},{9,10},{10,... | collective-permute-start | bytes 393224 | tf_op jit(solution)/shard_map/ppermute | solution.py:111
  54.7 1.8 %collective-permute-start.17 = (bf16[32,16,128]{2,1,0:T(8,128)(2,1)S(1)}, bf16[32,16,128]{2,1,0:T(8,128)(2,1)S(1)}, u32[]{:S(2)}, u32[]{:S(2)}) collective-permute-start(bf16[32,16,128]{2,1,0:T(8,128)(2,1)S(1)} %get-tuple-element.55.refs_0_), channel_id=1, source_target_pairs={{0,2},{1,3},{2,0},{3,1},{4,6},{5,7},{6,4},{7,5},{8,10},{9,11},{10,... | collective-permute-start | bytes 393224 | tf_op jit(solution)/shard_map/ppermute | solution.py:111
  56.5 1.0 collective-permute-start.24
  57.5 1.6 %collective-permute-start.26 = (bf16[16,16,128]{2,1,0:T(8,128)(2,1)S(1)}, bf16[16,16,128]{2,1,0:T(8,128)(2,1)S(1)}, u32[]{:S(2)}, u32[]{:S(2)}) collective-permute-start(bf16[16,16,128]{2,1,0:T(8,128)(2,1)S(1)} %get-tuple-element.64), channel_id=1, source_target_pairs={{0,3},{1,2},{2,1},{3,0},{4,7},{5,6},{6,5},{7,4},{8,11},{9,10},{10,... | collective-permute-start | bytes 196616 | tf_op jit(solution)/shard_map/ppermute | solution.py:111
  59.1 1.0 pad_maximum_fusion
  60.1 0.8 convolution_convert_fusion
  61.0 0.9 collective-permute-start.25
  61.9 2.0 %convolution_convert_fusion.1 = bf16[192,512]{1,0:T(8,128)(2,1)S(1)} fusion(bf16[192,2048]{1,0:T(8,128)(2,1)} %collective-permute-done.5, bf16[512,2048]{1,0:T(8,128)(2,1)S(1)} %bitcast.224), kind=kOutput, calls=%fused_computation.4 | convolution fusion | flops 402751488 | bytes 3080192 | tf_op jit(solution)/shard_map/dot_general | solution.py:134
  64.0 8.1 %collective-permute-done.17.refs_2_ = bf16[32,16,128]{2,1,0:T(8,128)(2,1)S(1)} collective-permute-done((bf16[32,16,128]{2,1,0:T(8,128)(2,1)S(1)}, bf16[32,16,128]{2,1,0:T(8,128)(2,1)S(1)}, u32[]{:S(2)}, u32[]{:S(2)}) %collective-permute-start.17) | collective-permute-done | bytes 131104 | tf_op jit(solution)/shard_map/ppermute | solution.py:111
  72.1 1.6 %shard_map.57 = (bf16[32,2048]{1,0:T(8,128)(2,1)S(1)}, bf16[32,2048]{1,0:T(8,128)(2,1)S(1)}) custom-call(bf16[32,16,128]{2,1,0:T(8,128)(2,1)S(1)} %get-tuple-element.55.refs_0_, bf16[32,16,128]{2,1,0:T(8,128)(2,1)S(1)} %collective-permute-done.16.refs_1_, bf16[32,16,128]{2,1,0:T(8,128)(2,1)S(1)} %collective-permute-done.17.refs_2_, ...), custom_call_target="tpu_custom_call" | custom-call | flops 369098752 | bytes 786432 | tf_op jit(solution)/shard_map/pallas_call | solution.py:79
  73.8 0.8 convolution_convert_fusion.4
  74.6 3.8 %collective-permute-done.6 = bf16[2,1,2,48,512]{4,3,2,1,0:T(8,128)(2,1)S(1)} collective-permute-done((bf16[2,1,2,48,512]{4,3,2,1,0:T(8,128)(2,1)S(1)}, bf16[2,1,2,48,512]{4,3,2,1,0:T(8,128)(2,1)S(1)}, u32[]{:S(2)}, u32[]{:S(2)}) %collective-permute-start.6) | collective-permute-done | bytes 196640 | tf_op jit(solution)/shard_map/ppermute | solution.py:111
  78.5 4.9 %collective-permute-done.19 = bf16[32,2048]{1,0:T(8,128)(2,1)S(1)} collective-permute-done((bf16[32,2048]{1,0:T(8,128)(2,1)S(1)}, bf16[32,2048]{1,0:T(8,128)(2,1)S(1)}, u32[]{:S(2)}, u32[]{:S(2)}) %collective-permute-start.19) | collective-permute-done | bytes 131104 | tf_op jit(solution)/shard_map/ppermute | solution.py:111
  83.4 0.1 collective-permute-start.7
  83.6 5.8 %collective-permute-done.7 = bf16[1,1,2,48,512]{4,3,2,1,0:T(8,128)(2,1)S(1)} collective-permute-done((bf16[1,1,2,48,512]{4,3,2,1,0:T(8,128)(2,1)S(1)}, bf16[1,1,2,48,512]{4,3,2,1,0:T(8,128)(2,1)S(1)}, u32[]{:S(2)}, u32[]{:S(2)}) %collective-permute-start.7) | collective-permute-done | bytes 98336 | tf_op jit(solution)/shard_map/ppermute | solution.py:111
  89.4 2.5 %collective-permute-start.20 = (bf16[64,2048]{1,0:T(8,128)(2,1)S(1)}, bf16[64,2048]{1,0:T(8,128)(2,1)S(1)}, u32[]{:S(2)}, u32[]{:S(2)}) collective-permute-start(bf16[64,2048]{1,0:T(8,128)(2,1)S(1)} %pad_maximum_fusion.2), channel_id=1, source_target_pairs={{0,8},{4,12},{8,0},{12,4},{1,9},{5,13},{9,1},{13,5},{2,10},{6,14},... | collective-permute-start | bytes 786440 | tf_op jit(solution)/shard_map/ppermute | solution.py:111
  92.0 0.1 fusion.1
  92.1 4.1 %collective-permute-done.20 = bf16[64,2048]{1,0:T(8,128)(2,1)S(1)} collective-permute-done((bf16[64,2048]{1,0:T(8,128)(2,1)S(1)}, bf16[64,2048]{1,0:T(8,128)(2,1)S(1)}, u32[]{:S(2)}, u32[]{:S(2)}) %collective-permute-start.20) | collective-permute-done | bytes 262176 | tf_op jit(solution)/shard_map/ppermute | solution.py:111
  96.3 0.8 convolution_convert_fusion.5
  97.4 0.8 convolution_convert_fusion.2
  98.2 1.1 shard_map.58
  99.3 2.2 %collective-permute-start.27 = (bf16[16,2048]{1,0:T(8,128)(2,1)S(1)}, bf16[16,2048]{1,0:T(8,128)(2,1)S(1)}, u32[]{:S(2)}, u32[]{:S(2)}) collective-permute-start(bf16[16,2048]{1,0:T(8,128)(2,1)S(1)} %get-tuple-element.70), channel_id=1, source_target_pairs={{0,1},{1,0},{2,3},{3,2},{4,5},{5,4},{6,7},{7,6},{8,9},{9,8},{10,11... | collective-permute-start | bytes 196616 | tf_op jit(solution)/shard_map/ppermute | solution.py:111
  101.5 0.7 collective-permute-done.14
  102.4 1.9 %collective-permute-done.27 = bf16[16,2048]{1,0:T(8,128)(2,1)S(1)} collective-permute-done((bf16[16,2048]{1,0:T(8,128)(2,1)S(1)}, bf16[16,2048]{1,0:T(8,128)(2,1)S(1)}, u32[]{:S(2)}, u32[]{:S(2)}) %collective-permute-start.27) | collective-permute-done | bytes 65568 | tf_op jit(solution)/shard_map/ppermute | solution.py:111
  104.3 2.1 %collective-permute-start.28 = (bf16[32,2048]{1,0:T(8,128)(2,1)S(1)}, bf16[32,2048]{1,0:T(8,128)(2,1)S(1)}, u32[]{:S(2)}, u32[]{:S(2)}) collective-permute-start(bf16[32,2048]{1,0:T(8,128)(2,1)S(1)} %pad_maximum_fusion.10), channel_id=1, source_target_pairs={{0,8},{4,12},{8,0},{12,4},{1,9},{5,13},{9,1},{13,5},{2,10},{6,14},... | collective-permute-start | bytes 393224 | tf_op jit(solution)/shard_map/ppermute | solution.py:111
  106.4 1.6 %collective-permute-done.15 = bf16[1,1,2,32,512]{4,3,2,1,0:T(8,128)(2,1)S(1)} collective-permute-done((bf16[1,1,2,32,512]{4,3,2,1,0:T(8,128)(2,1)S(1)}, bf16[1,1,2,32,512]{4,3,2,1,0:T(8,128)(2,1)S(1)}, u32[]{:S(2)}, u32[]{:S(2)}) %collective-permute-start.15) | collective-permute-done | bytes 65568 | tf_op jit(solution)/shard_map/ppermute | solution.py:111
  108.2 0.8 convolution_convert_fusion.3
  109.1 0.6 collective-permute-start.22
  109.7 0.2 collective-permute-done.28
  110.0 4.3 %collective-permute-done.22 = bf16[2,1,2,32,512]{4,3,2,1,0:T(8,128)(2,1)S(1)} collective-permute-done((bf16[2,1,2,32,512]{4,3,2,1,0:T(8,128)(2,1)S(1)}, bf16[2,1,2,32,512]{4,3,2,1,0:T(8,128)(2,1)S(1)}, u32[]{:S(2)}, u32[]{:S(2)}) %collective-permute-start.22) | collective-permute-done | bytes 131104 | tf_op jit(solution)/shard_map/ppermute | solution.py:111
  114.3 0.4 collective-permute-start.23
  114.7 0.8 convolution_convert_fusion.6
  115.5 4.6 %collective-permute-done.23 = bf16[1,1,2,32,512]{4,3,2,1,0:T(8,128)(2,1)S(1)} collective-permute-done((bf16[1,1,2,32,512]{4,3,2,1,0:T(8,128)(2,1)S(1)}, bf16[1,1,2,32,512]{4,3,2,1,0:T(8,128)(2,1)S(1)}, u32[]{:S(2)}, u32[]{:S(2)}) %collective-permute-start.23) | collective-permute-done | bytes 65568 | tf_op jit(solution)/shard_map/ppermute | solution.py:111
  120.1 0.8 convolution_convert_fusion.7
  121.0 4.6 %collective-permute-done.30 = bf16[2,1,2,16,512]{4,3,2,1,0:T(8,128)(2,1)S(1)} collective-permute-done((bf16[2,1,2,16,512]{4,3,2,1,0:T(8,128)(2,1)S(1)}, bf16[2,1,2,16,512]{4,3,2,1,0:T(8,128)(2,1)S(1)}, u32[]{:S(2)}, u32[]{:S(2)}) %collective-permute-start.30) | collective-permute-done | bytes 65568 | tf_op jit(solution)/shard_map/ppermute | solution.py:111
  125.6 0.1 collective-permute-start.31
  125.8 4.7 %collective-permute-done.31 = bf16[1,1,2,16,512]{4,3,2,1,0:T(8,128)(2,1)S(1)} collective-permute-done((bf16[1,1,2,16,512]{4,3,2,1,0:T(8,128)(2,1)S(1)}, bf16[1,1,2,16,512]{4,3,2,1,0:T(8,128)(2,1)S(1)}, u32[]{:S(2)}, u32[]{:S(2)}) %collective-permute-start.31) | collective-permute-done | bytes 32800 | tf_op jit(solution)/shard_map/ppermute | solution.py:111
  130.6 0.8 maximum_bitcast_fusion
  (82 shorter events, 1.8 us)
Async XLA Ops:
  0.0 8.7 %copy-start = (f32[64,64]{1,0:T(8,128)S(1)}, f32[64,64]{1,0:T(8,128)}, u32[]{:S(2)}) copy-start(f32[64,64]{1,0:T(8,128)} %param.7) | copy-start | bytes 49156
  0.0 10.1 %copy-start.1 = (bf16[256,16,128]{2,1,0:T(8,128)(2,1)S(1)}, bf16[256,16,128]{2,1,0:T(8,128)(2,1)}, u32[]{:S(2)}) copy-start(bf16[256,16,128]{2,1,0:T(8,128)(2,1)} %param.5) | copy-start | bytes 3145732
  0.0 10.8 %copy-start.3 = (f32[64,128]{1,0:T(8,128)S(1)}, f32[64,128]{1,0:T(8,128)}, u32[]{:S(2)}) copy-start(f32[64,128]{1,0:T(8,128)} %param.9) | copy-start | bytes 98308
  1.1 9.7 %collective-permute-start = (bf16[48,16,128]{2,1,0:T(8,128)(2,1)S(1)}, bf16[48,16,128]{2,1,0:T(8,128)(2,1)S(1)}, u32[]{:S(2)}, u32[]{:S(2)}) collective-permute-start(bf16[48,16,128]{2,1,0:T(8,128)(2,1)S(1)} %get-tuple-element.40), channel_id=1, source_target_pairs={{0,1},{1,0},{2,3},{3,2},{4,5},{5,4},{6,7},{7,6},{8,9},{9,8},{10,11... | collective-permute-start | bytes 589832 | tf_op jit(solution)/shard_map/ppermute | solution.py:111
  4.3 26.6 %collective-permute-start.2 = (bf16[48,16,128]{2,1,0:T(8,128)(2,1)S(1)}, bf16[48,16,128]{2,1,0:T(8,128)(2,1)S(1)}, u32[]{:S(2)}, u32[]{:S(2)}) collective-permute-start(bf16[48,16,128]{2,1,0:T(8,128)(2,1)S(1)} %get-tuple-element.40), channel_id=1, source_target_pairs={{0,3},{1,2},{2,1},{3,0},{4,7},{5,6},{6,5},{7,4},{8,11},{9,10},{10,... | collective-permute-start | bytes 589832 | tf_op jit(solution)/shard_map/ppermute | solution.py:111
  6.7 24.2 %collective-permute-start.1 = (bf16[48,16,128]{2,1,0:T(8,128)(2,1)S(1)}, bf16[48,16,128]{2,1,0:T(8,128)(2,1)S(1)}, u32[]{:S(2)}, u32[]{:S(2)}) collective-permute-start(bf16[48,16,128]{2,1,0:T(8,128)(2,1)S(1)} %get-tuple-element.39.refs_0_), channel_id=1, source_target_pairs={{0,2},{1,3},{2,0},{3,1},{4,6},{5,7},{6,4},{7,5},{8,10},{9,11},{10,... | collective-permute-start | bytes 589832 | tf_op jit(solution)/shard_map/ppermute | solution.py:111
  10.9 30.2 %collective-permute-start.8 = (bf16[32,16,128]{2,1,0:T(8,128)(2,1)S(1)}, bf16[32,16,128]{2,1,0:T(8,128)(2,1)S(1)}, u32[]{:S(2)}, u32[]{:S(2)}) collective-permute-start(bf16[32,16,128]{2,1,0:T(8,128)(2,1)S(1)} %get-tuple-element.45), channel_id=1, source_target_pairs={{0,1},{1,0},{2,3},{3,2},{4,5},{5,4},{6,7},{7,6},{8,9},{9,8},{10,11... | collective-permute-start | bytes 393224 | tf_op jit(solution)/shard_map/ppermute | solution.py:111
  12.7 28.4 %collective-permute-start.10 = (bf16[32,16,128]{2,1,0:T(8,128)(2,1)S(1)}, bf16[32,16,128]{2,1,0:T(8,128)(2,1)S(1)}, u32[]{:S(2)}, u32[]{:S(2)}) collective-permute-start(bf16[32,16,128]{2,1,0:T(8,128)(2,1)S(1)} %get-tuple-element.45), channel_id=1, source_target_pairs={{0,3},{1,2},{2,1},{3,0},{4,7},{5,6},{6,5},{7,4},{8,11},{9,10},{10,... | collective-permute-start | bytes 393224 | tf_op jit(solution)/shard_map/ppermute | solution.py:111
  16.5 24.7 %collective-permute-start.9 = (bf16[32,16,128]{2,1,0:T(8,128)(2,1)S(1)}, bf16[32,16,128]{2,1,0:T(8,128)(2,1)S(1)}, u32[]{:S(2)}, u32[]{:S(2)}) collective-permute-start(bf16[32,16,128]{2,1,0:T(8,128)(2,1)S(1)} %get-tuple-element.46.refs_0_), channel_id=1, source_target_pairs={{0,2},{1,3},{2,0},{3,1},{4,6},{5,7},{6,4},{7,5},{8,10},{9,11},{10,... | collective-permute-start | bytes 393224 | tf_op jit(solution)/shard_map/ppermute | solution.py:111
  33.1 6.4 %collective-permute-start.3 = (bf16[48,2048]{1,0:T(8,128)(2,1)S(1)}, bf16[48,2048]{1,0:T(8,128)(2,1)S(1)}, u32[]{:S(2)}, u32[]{:S(2)}) collective-permute-start(bf16[48,2048]{1,0:T(8,128)(2,1)S(1)} %get-tuple-element.42), channel_id=1, source_target_pairs={{0,1},{1,0},{2,3},{3,2},{4,5},{5,4},{6,7},{7,6},{8,9},{9,8},{10,11... | collective-permute-start | bytes 589832 | tf_op jit(solution)/shard_map/ppermute | solution.py:111
  39.5 10.1 %collective-permute-start.4 = (bf16[96,2048]{1,0:T(8,128)(2,1)S(1)}, bf16[96,2048]{1,0:T(8,128)(2,1)S(1)}, u32[]{:S(2)}, u32[]{:S(2)}) collective-permute-start(bf16[96,2048]{1,0:T(8,128)(2,1)S(1)} %get-tuple-element.99), channel_id=1, source_target_pairs={{0,8},{4,12},{8,0},{12,4},{1,9},{5,13},{9,1},{13,5},{2,10},{6,14},... | collective-permute-start | bytes 1179656 | tf_op jit(solution)/shard_map/ppermute | solution.py:111
  42.7 5.0 %collective-permute-start.11 = (bf16[32,2048]{1,0:T(8,128)(2,1)S(1)}, bf16[32,2048]{1,0:T(8,128)(2,1)S(1)}, u32[]{:S(2)}, u32[]{:S(2)}) collective-permute-start(bf16[32,2048]{1,0:T(8,128)(2,1)S(1)} %get-tuple-element.51), channel_id=1, source_target_pairs={{0,1},{1,0},{2,3},{3,2},{4,5},{5,4},{6,7},{7,6},{8,9},{9,8},{10,11... | collective-permute-start | bytes 393224 | tf_op jit(solution)/shard_map/ppermute | solution.py:111
  47.8 2.2 %copy-start.2 = (bf16[32,2048]{1,0:T(8,128)(2,1)}, bf16[32,2048]{1,0:T(8,128)(2,1)S(1)}, u32[]{:S(2)}) copy-start(bf16[32,2048]{1,0:T(8,128)(2,1)S(1)} %collective-permute-done.11) | copy-start | bytes 393220
  48.5 9.0 %collective-permute-start.12 = (bf16[64,2048]{1,0:T(8,128)(2,1)}, bf16[64,2048]{1,0:T(8,128)(2,1)}, u32[]{:S(2)}, u32[]{:S(2)}) collective-permute-start(bf16[64,2048]{1,0:T(8,128)(2,1)} %constant_dynamic-update-slice_fusion.5), channel_id=1, source_target_pairs={{0,8},{4,12},{8,0},{12,4},{1,9},{5,13},{9,1},{13,5},{2,10},{6,14},... | collective-permute-start | bytes 786440 | tf_op jit(solution)/shard_map/ppermute | solution.py:111
  49.7 11.2 %collective-permute-start.5 = (bf16[192,2048]{1,0:T(8,128)(2,1)S(1)}, bf16[192,2048]{1,0:T(8,128)(2,1)}, u32[]{:S(2)}, u32[]{:S(2)}) collective-permute-start(bf16[192,2048]{1,0:T(8,128)(2,1)S(1)} %constant_dynamic-update-slice_fusion.2), channel_id=1, source_target_pairs={{0,4},{4,0},{8,12},{12,8},{1,5},{5,1},{9,13},{13,9},{2,6},{6,2},{1... | collective-permute-start | bytes 2359304 | tf_op jit(solution)/shard_map/ppermute | solution.py:111
  49.8 6.7 %collective-permute-start.16 = (bf16[32,16,128]{2,1,0:T(8,128)(2,1)}, bf16[32,16,128]{2,1,0:T(8,128)(2,1)S(1)}, u32[]{:S(2)}, u32[]{:S(2)}) collective-permute-start(bf16[32,16,128]{2,1,0:T(8,128)(2,1)} %get-tuple-element.54), channel_id=1, source_target_pairs={{0,1},{1,0},{2,3},{3,2},{4,5},{5,4},{6,7},{7,6},{8,9},{9,8},{10,11... | collective-permute-start | bytes 393224 | tf_op jit(solution)/shard_map/ppermute | solution.py:111
  53.0 19.1 %collective-permute-start.18 = (bf16[32,16,128]{2,1,0:T(8,128)(2,1)}, bf16[32,16,128]{2,1,0:T(8,128)(2,1)S(1)}, u32[]{:S(2)}, u32[]{:S(2)}) collective-permute-start(bf16[32,16,128]{2,1,0:T(8,128)(2,1)} %get-tuple-element.54), channel_id=1, source_target_pairs={{0,3},{1,2},{2,1},{3,0},{4,7},{5,6},{6,5},{7,4},{8,11},{9,10},{10,... | collective-permute-start | bytes 393224 | tf_op jit(solution)/shard_map/ppermute | solution.py:111
  54.7 17.4 %collective-permute-start.17 = (bf16[32,16,128]{2,1,0:T(8,128)(2,1)S(1)}, bf16[32,16,128]{2,1,0:T(8,128)(2,1)S(1)}, u32[]{:S(2)}, u32[]{:S(2)}) collective-permute-start(bf16[32,16,128]{2,1,0:T(8,128)(2,1)S(1)} %get-tuple-element.55.refs_0_), channel_id=1, source_target_pairs={{0,2},{1,3},{2,0},{3,1},{4,6},{5,7},{6,4},{7,5},{8,10},{9,11},{10,... | collective-permute-start | bytes 393224 | tf_op jit(solution)/shard_map/ppermute | solution.py:111
  56.5 41.7 %collective-permute-start.24 = (bf16[16,16,128]{2,1,0:T(8,128)(2,1)S(1)}, bf16[16,16,128]{2,1,0:T(8,128)(2,1)S(1)}, u32[]{:S(2)}, u32[]{:S(2)}) collective-permute-start(bf16[16,16,128]{2,1,0:T(8,128)(2,1)S(1)} %get-tuple-element.64), channel_id=1, source_target_pairs={{0,1},{1,0},{2,3},{3,2},{4,5},{5,4},{6,7},{7,6},{8,9},{9,8},{10,11... | collective-permute-start | bytes 196616 | tf_op jit(solution)/shard_map/ppermute | solution.py:111
  57.5 40.8 %collective-permute-start.26 = (bf16[16,16,128]{2,1,0:T(8,128)(2,1)S(1)}, bf16[16,16,128]{2,1,0:T(8,128)(2,1)S(1)}, u32[]{:S(2)}, u32[]{:S(2)}) collective-permute-start(bf16[16,16,128]{2,1,0:T(8,128)(2,1)S(1)} %get-tuple-element.64), channel_id=1, source_target_pairs={{0,3},{1,2},{2,1},{3,0},{4,7},{5,6},{6,5},{7,4},{8,11},{9,10},{10,... | collective-permute-start | bytes 196616 | tf_op jit(solution)/shard_map/ppermute | solution.py:111
  61.0 37.3 %collective-permute-start.25 = (bf16[16,16,128]{2,1,0:T(8,128)(2,1)S(1)}, bf16[16,16,128]{2,1,0:T(8,128)(2,1)S(1)}, u32[]{:S(2)}, u32[]{:S(2)}) collective-permute-start(bf16[16,16,128]{2,1,0:T(8,128)(2,1)S(1)} %get-tuple-element.65.refs_0_), channel_id=1, source_target_pairs={{0,2},{1,3},{2,0},{3,1},{4,6},{5,7},{6,4},{7,5},{8,10},{9,11},{10,... | collective-permute-start | bytes 196616 | tf_op jit(solution)/shard_map/ppermute | solution.py:111
  72.1 6.3 %collective-permute-start.6 = (bf16[2,1,2,48,512]{4,3,2,1,0:T(8,128)(2,1)S(1)}, bf16[2,1,2,48,512]{4,3,2,1,0:T(8,128)(2,1)S(1)}, u32[]{:S(2)}, u32[]{:S(2)}) collective-permute-start(bf16[2,1,2,48,512]{4,3,2,1,0:T(8,128)(2,1)S(1)} %fusion), channel_id=1, source_target_pairs={{0,1},{1,0},{2,3},{3,2},{4,5},{5,4},{6,7},{7,6},{8,9},{9,8},{10,11... | collective-permute-start | bytes 589832 | tf_op jit(solution)/shard_map/ppermute | solution.py:111
  72.1 24.2 %collective-permute-start.13 = (bf16[128,2048]{1,0:T(8,128)(2,1)S(1)}, bf16[128,2048]{1,0:T(8,128)(2,1)S(1)}, u32[]{:S(2)}, u32[]{:S(2)}) collective-permute-start(bf16[128,2048]{1,0:T(8,128)(2,1)S(1)} %pad_maximum_fusion), channel_id=1, source_target_pairs={{0,4},{4,0},{8,12},{12,8},{1,5},{5,1},{9,13},{13,9},{2,6},{6,2},{1... | collective-permute-start | bytes 1572872 | tf_op jit(solution)/shard_map/ppermute | solution.py:111
  78.5 5.0 %collective-permute-start.19 = (bf16[32,2048]{1,0:T(8,128)(2,1)S(1)}, bf16[32,2048]{1,0:T(8,128)(2,1)S(1)}, u32[]{:S(2)}, u32[]{:S(2)}) collective-permute-start(bf16[32,2048]{1,0:T(8,128)(2,1)S(1)} %get-tuple-element.60), channel_id=1, source_target_pairs={{0,1},{1,0},{2,3},{3,2},{4,5},{5,4},{6,7},{7,6},{8,9},{9,8},{10,11... | collective-permute-start | bytes 393224 | tf_op jit(solution)/shard_map/ppermute | solution.py:111
  83.4 6.0 %collective-permute-start.7 = (bf16[1,1,2,48,512]{4,3,2,1,0:T(8,128)(2,1)S(1)}, bf16[1,1,2,48,512]{4,3,2,1,0:T(8,128)(2,1)S(1)}, u32[]{:S(2)}, u32[]{:S(2)}) collective-permute-start(bf16[1,1,2,48,512]{4,3,2,1,0:T(8,128)(2,1)S(1)} %get-tuple-element.94), channel_id=1, source_target_pairs={{0,2},{1,3},{2,0},{3,1},{4,6},{5,7},{6,4},{7,5},{8,10},{9,11},{10,... | collective-permute-start | bytes 294920 | tf_op jit(solution)/shard_map/ppermute | solution.py:111
  89.4 6.8 %collective-permute-start.20 = (bf16[64,2048]{1,0:T(8,128)(2,1)S(1)}, bf16[64,2048]{1,0:T(8,128)(2,1)S(1)}, u32[]{:S(2)}, u32[]{:S(2)}) collective-permute-start(bf16[64,2048]{1,0:T(8,128)(2,1)S(1)} %pad_maximum_fusion.2), channel_id=1, source_target_pairs={{0,8},{4,12},{8,0},{12,4},{1,9},{5,13},{9,1},{13,5},{2,10},{6,14},... | collective-permute-start | bytes 786440 | tf_op jit(solution)/shard_map/ppermute | solution.py:111
  97.2 5.0 %collective-permute-start.14 = (bf16[2,1,2,32,512]{4,3,2,1,0:T(8,128)(2,1)S(1)}, bf16[2,1,2,32,512]{4,3,2,1,0:T(8,128)(2,1)S(1)}, u32[]{:S(2)}, u32[]{:S(2)}) collective-permute-start(bf16[2,1,2,32,512]{4,3,2,1,0:T(8,128)(2,1)S(1)} %fusion.7), channel_id=1, source_target_pairs={{0,1},{1,0},{2,3},{3,2},{4,5},{5,4},{6,7},{7,6},{8,9},{9,8},{10,11... | collective-permute-start | bytes 393224 | tf_op jit(solution)/shard_map/ppermute | solution.py:111
  97.3 10.9 %collective-permute-start.21 = (bf16[128,2048]{1,0:T(8,128)(2,1)S(1)}, bf16[128,2048]{1,0:T(8,128)(2,1)S(1)}, u32[]{:S(2)}, u32[]{:S(2)}) collective-permute-start(bf16[128,2048]{1,0:T(8,128)(2,1)S(1)} %pad_maximum_fusion.1), channel_id=1, source_target_pairs={{0,4},{4,0},{8,12},{12,8},{1,5},{5,1},{9,13},{13,9},{2,6},{6,2},{1... | collective-permute-start | bytes 1572872 | tf_op jit(solution)/shard_map/ppermute | solution.py:111
  99.3 4.9 %collective-permute-start.27 = (bf16[16,2048]{1,0:T(8,128)(2,1)S(1)}, bf16[16,2048]{1,0:T(8,128)(2,1)S(1)}, u32[]{:S(2)}, u32[]{:S(2)}) collective-permute-start(bf16[16,2048]{1,0:T(8,128)(2,1)S(1)} %get-tuple-element.70), channel_id=1, source_target_pairs={{0,1},{1,0},{2,3},{3,2},{4,5},{5,4},{6,7},{7,6},{8,9},{9,8},{10,11... | collective-permute-start | bytes 196616 | tf_op jit(solution)/shard_map/ppermute | solution.py:111
  102.3 5.7 %collective-permute-start.15 = (bf16[1,1,2,32,512]{4,3,2,1,0:T(8,128)(2,1)S(1)}, bf16[1,1,2,32,512]{4,3,2,1,0:T(8,128)(2,1)S(1)}, u32[]{:S(2)}, u32[]{:S(2)}) collective-permute-start(bf16[1,1,2,32,512]{4,3,2,1,0:T(8,128)(2,1)S(1)} %get-tuple-element.103), channel_id=1, source_target_pairs={{0,2},{1,3},{2,0},{3,1},{4,6},{5,7},{6,4},{7,5},{8,10},{9,11},{10,... | collective-permute-start | bytes 196616 | tf_op jit(solution)/shard_map/ppermute | solution.py:111
  104.3 5.6 %collective-permute-start.28 = (bf16[32,2048]{1,0:T(8,128)(2,1)S(1)}, bf16[32,2048]{1,0:T(8,128)(2,1)S(1)}, u32[]{:S(2)}, u32[]{:S(2)}) collective-permute-start(bf16[32,2048]{1,0:T(8,128)(2,1)S(1)} %pad_maximum_fusion.10), channel_id=1, source_target_pairs={{0,8},{4,12},{8,0},{12,4},{1,9},{5,13},{9,1},{13,5},{2,10},{6,14},... | collective-permute-start | bytes 393224 | tf_op jit(solution)/shard_map/ppermute | solution.py:111
  109.1 5.2 %collective-permute-start.22 = (bf16[2,1,2,32,512]{4,3,2,1,0:T(8,128)(2,1)S(1)}, bf16[2,1,2,32,512]{4,3,2,1,0:T(8,128)(2,1)S(1)}, u32[]{:S(2)}, u32[]{:S(2)}) collective-permute-start(bf16[2,1,2,32,512]{4,3,2,1,0:T(8,128)(2,1)S(1)} %fusion.6), channel_id=1, source_target_pairs={{0,1},{1,0},{2,3},{3,2},{4,5},{5,4},{6,7},{7,6},{8,9},{9,8},{10,11... | collective-permute-start | bytes 393224 | tf_op jit(solution)/shard_map/ppermute | solution.py:111
  109.9 10.2 %collective-permute-start.29 = (bf16[64,2048]{1,0:T(8,128)(2,1)S(1)}, bf16[64,2048]{1,0:T(8,128)(2,1)S(1)}, u32[]{:S(2)}, u32[]{:S(2)}) collective-permute-start(bf16[64,2048]{1,0:T(8,128)(2,1)S(1)} %pad_maximum_fusion.3), channel_id=1, source_target_pairs={{0,4},{4,0},{8,12},{12,8},{1,5},{5,1},{9,13},{13,9},{2,6},{6,2},{1... | collective-permute-start | bytes 786440 | tf_op jit(solution)/shard_map/ppermute | solution.py:111
  114.3 5.7 %collective-permute-start.23 = (bf16[1,1,2,32,512]{4,3,2,1,0:T(8,128)(2,1)S(1)}, bf16[1,1,2,32,512]{4,3,2,1,0:T(8,128)(2,1)S(1)}, u32[]{:S(2)}, u32[]{:S(2)}) collective-permute-start(bf16[1,1,2,32,512]{4,3,2,1,0:T(8,128)(2,1)S(1)} %get-tuple-element.108), channel_id=1, source_target_pairs={{0,2},{1,3},{2,0},{3,1},{4,6},{5,7},{6,4},{7,5},{8,10},{9,11},{10,... | collective-permute-start | bytes 196616 | tf_op jit(solution)/shard_map/ppermute | solution.py:111
  120.9 4.7 %collective-permute-start.30 = (bf16[2,1,2,16,512]{4,3,2,1,0:T(8,128)(2,1)S(1)}, bf16[2,1,2,16,512]{4,3,2,1,0:T(8,128)(2,1)S(1)}, u32[]{:S(2)}, u32[]{:S(2)}) collective-permute-start(bf16[2,1,2,16,512]{4,3,2,1,0:T(8,128)(2,1)S(1)} %fusion.32), channel_id=1, source_target_pairs={{0,1},{1,0},{2,3},{3,2},{4,5},{5,4},{6,7},{7,6},{8,9},{9,8},{10,11... | collective-permute-start | bytes 196616 | tf_op jit(solution)/shard_map/ppermute | solution.py:111
  125.6 4.9 %collective-permute-start.31 = (bf16[1,1,2,16,512]{4,3,2,1,0:T(8,128)(2,1)S(1)}, bf16[1,1,2,16,512]{4,3,2,1,0:T(8,128)(2,1)S(1)}, u32[]{:S(2)}, u32[]{:S(2)}) collective-permute-start(bf16[1,1,2,16,512]{4,3,2,1,0:T(8,128)(2,1)S(1)} %get-tuple-element.117), channel_id=1, source_target_pairs={{0,2},{1,3},{2,0},{3,1},{4,6},{5,7},{6,4},{7,5},{8,10},{9,11},{10,... | collective-permute-start | bytes 98312 | tf_op jit(solution)/shard_map/ppermute | solution.py:111

commit v6 on v5

v6 whole, which is shorter than its diff:
```python
import functools
import jax
import jax.numpy as jnp
from jax import lax
from jax.experimental import pallas as pl
from jax.experimental.pallas import tpu as pltpu
from jax.sharding import PartitionSpec as P

damping_term = 0.05
CHUNKS = (8, 8)
BLOCK = 64


def halves(value):
    high = value.astype(jnp.bfloat16)
    return high, (value - high.astype(jnp.float32)).astype(jnp.bfloat16)


def basis_halves(matrix):
    high = lax.reduce_precision(matrix, 8, 7)
    return high.astype(jnp.bfloat16), (matrix - high).astype(jnp.bfloat16)


def times(left, right):
    return jnp.dot(left, right, preferred_element_type=jnp.float32)


def three_wide(matrix):
    high, low = basis_halves(matrix)
    return jnp.concatenate([high, low, high], axis=1)


def three_deep(matrix):
    high, low = halves(matrix)
    return jnp.concatenate([high, high, low], axis=0)


def condition_kernel(slices, rows_here, *refs):
    pieces = refs[:slices]
    enter, leave, right, back, inverse = refs[slices:slices + 5]
    outs, stage = refs[slices + 5:-1], refs[-1]
    count, _, columns = pieces[0].shape
    out_rows = slices * rows_here
    parts = []
    for piece in pieces:
        flat = piece[...].reshape(count * rows_here, columns)
        parts.append(halves(times(flat, right[0]) + times(flat, right[1])))
    scale = jnp.concatenate([inverse[...]] * 2, axis=1)

    def gathered(at, which):
        rows = slice(at * rows_here, (at + 1) * rows_here)
        return jnp.concatenate([part[which][rows] for part in parts], axis=0)

    for at in range(0, count, 2):
        high = jnp.concatenate([gathered(at, 0), gathered(at + 1, 0)], axis=1)
        low = jnp.concatenate([gathered(at, 1), gathered(at + 1, 1)], axis=1)
        rotated = times(enter[...], jnp.concatenate([high, high, low], axis=0))
        result = times(leave[...], three_deep(rotated * scale))
        stage[at * out_rows:(at + 1) * out_rows, :] = result[:, :columns]
        stage[(at + 1) * out_rows:(at + 2) * out_rows, :] = result[:, columns:]
    high, low = halves(stage[...])
    stage[...] = times(high, back[0]) + times(low, back[0]) + times(high, back[1])
    for row in range(out_rows):
        value = stage[pl.ds(row, count, stride=out_rows), :].astype(jnp.bfloat16)
        at = row % rows_here * columns
        outs[row // rows_here][:, at:at + columns] = value


def condition_fast(pieces, enter, leave, in_basis, inverse):
    slices = len(pieces)
    count, rows_here, columns = pieces[0].shape
    block = min(BLOCK, count)
    width = rows_here * columns
    piece_spec = pl.BlockSpec((block, rows_here, columns), lambda step: (step, 0, 0))
    out_spec = pl.BlockSpec((block, width), lambda step: (step, 0))
    whole = pl.BlockSpec(memory_space=pltpu.VMEM)
    order = enter.shape[0]
    return pl.pallas_call(
        functools.partial(condition_kernel, slices, rows_here),
        grid=(count // block,),
        in_specs=[piece_spec] * slices + [whole] * 5,
        out_specs=[out_spec] * slices,
        out_shape=[jax.ShapeDtypeStruct((count, width), jnp.bfloat16)] * slices,
        scratch_shapes=[pltpu.VMEM((block * order, columns), jnp.float32)],
        compiler_params=pltpu.CompilerParams(vmem_limit_bytes=32 * 1024 * 1024),
        cost_estimate=pl.CostEstimate(flops=0, bytes_accessed=0, transcendentals=0),
    )(
        *pieces,
        three_wide(enter.T),
        three_wide(leave),
        jnp.stack(basis_halves(in_basis)),
        jnp.stack(basis_halves(in_basis.T)),
        inverse,
    )


def condition_plain(pieces, enter, leave, in_basis, inverse):
    high = lax.Precision.HIGH
    count, rows_here, columns = pieces[0].shape
    values = jnp.concatenate(pieces, axis=1).astype(jnp.float32)
    inner = jnp.einsum("qbc,cd->qbd", values, in_basis, precision=high)
    rotated = jnp.einsum("ba,qbd->qad", enter, inner, precision=high)
    left = jnp.einsum("ba,qad->qbd", leave, rotated * inverse, precision=high)
    result = jnp.einsum("qbd,ed->qbe", left, in_basis, precision=high).astype(jnp.bfloat16)
    starts = range(0, enter.shape[0], rows_here)
    return [result[:, at:at + rows_here].reshape(count, rows_here * columns) for at in starts]


def crossed(value, axis, size, mask):
    return lax.ppermute(value, axis, [(at, at ^ mask) for at in range(size)])


def after(value, *tokens):
    return lax.optimization_barrier((value, tokens))[0]


def spread_shares(near, shares):
    return jnp.concatenate([near] + [crossed(near, "dp", shares, mask) for mask in range(2, shares, 2)], axis=0)


def products(near, far, train_flat, shares):
    contract = (((1,), (1,)), ((), ()))
    values = []
    for block in (near, far):
        value = lax.dot_general(block, train_flat, contract, preferred_element_type=jnp.float32)
        values.append(value.astype(jnp.bfloat16).reshape(shares // 2, -1, train_flat.shape[0]))
    return [values[at % 2][at // 2] for at in range(shares)]


def turned(blocks, mask):
    bit = 1
    while bit < len(blocks):
        swap = mask // bit % 2 == 1
        blocks = [jnp.where(swap, blocks[at ^ bit], blocks[at]) for at in range(len(blocks))]
        bit *= 2
    return blocks


def body(queries, train_grads, out_basis, in_basis, corrections):
    slices = lax.axis_size("proj")
    shares = lax.axis_size("dp")
    here = lax.axis_index("proj")
    share = lax.axis_index("dp")
    count, rows_here, columns = queries.shape
    width = rows_here * columns
    owned = shares // slices
    train_count = train_grads.shape[0]
    train_flat = lax.optimization_barrier(train_grads.reshape(train_count, width))
    row_blocks = out_basis.reshape(slices, rows_here, -1)
    basis = jnp.concatenate(turned([row_blocks[at] for at in range(slices)], here), axis=0)
    inverse = 1.0 / (corrections + damping_term)
    condition = condition_fast if rows_here % 16 == 0 else condition_plain
    parts = [count * size // sum(CHUNKS) for size in CHUNKS]
    firsts = [sum(parts[:chunk]) for chunk in range(len(parts))]
    pieces, rows, blocks, results = [], [], [], []
    source = queries
    for first, part in zip(firsts, parts):
        each = part // slices
        raw = [lax.dynamic_slice_in_dim(source, first + (here ^ mask) * each, each, 0) for mask in range(slices)]
        if pieces:
            raw = after(raw, pieces[-1][1])
        else:
            raw, source = lax.optimization_barrier((raw, source))
        pieces.append([raw[0]] + [crossed(raw[mask], "proj", slices, mask) for mask in range(1, slices)])
    for chunk in range(len(parts)):
        made = condition(pieces[chunk], basis, basis, in_basis, inverse)
        rows.append([made[0]] + [crossed(made[mask], "proj", slices, mask) for mask in range(1, slices)])
    for chunk, part in enumerate(parts):
        near = spread_shares(jnp.concatenate(rows[chunk], axis=0), shares)
        near = after(near, *blocks[-1:])
        far = crossed(near, "dp", shares, 1)
        values = products(near, far, train_flat, shares)
        values = [jnp.stack(values[at * owned:(at + 1) * owned]) for at in range(slices)]
        blocks.append(turned(values, here ^ (share // owned)))
    for part, block in zip(parts, blocks):
        came = [block[0]] + [crossed(block[mask], "proj", slices, mask) for mask in range(1, slices)]
        came = [value.reshape(owned, slices, part // slices, train_count) for value in came]
        total = [sum(came[mask][:, at ^ mask].astype(jnp.float32) for mask in range(slices)) for at in range(slices)]
        total = jnp.stack(turned(total, here), axis=1)
        total = jnp.stack(turned([total[at] for at in range(owned)], share % owned))
        results.append(total.reshape(owned, part, train_count))
    return jnp.concatenate(results, axis=1).reshape(owned * count, train_count)


def solution(mesh):
    in_specs = (P(("groups", "dp"), "proj", None), P(("groups", "dp"), "proj", None), P(), P(), P())
    out_specs = P(("groups", "proj"), "dp")
    return jax.shard_map(body, mesh=mesh, in_specs=in_specs, out_specs=out_specs, check_vma=False)
```

time: 132 us -> 107 us (0.81)
  waiting for transfers between devices: 74.6 us -> 58.3 us
  matrix products: 7.67 us -> 2.98 us
  local copies, waits for them, and re-layouts: 8.48 us -> 4.83 us
  starting transfers between devices: 29.6 us -> 32.1 us
  Pallas kernels: 6.46 us -> 4.46 us
    ppermute x32 -> x22, waiting for transfers between devices: 74.6 us -> 58.3 us  [crossed(): return lax.ppermute(value, axis, [(at, at ^ mask) for at in range(size)])]
    dot_general x8 -> x4, matrix products: 7.67 us -> 2.98 us  [products(): lax.dot_general(block, train_flat, contract, preferred_element_type=jnp.f...]
    ppermute x32 -> x22, starting transfers between devices: 29.6 us -> 32.1 us  [crossed(): return lax.ppermute(value, axis, [(at, at ^ mask) for at in range(size)])]
    unnamed x13 -> x14, local copies, waits for them, and re-layouts: 3.8 us -> 1.57 us
    pallas_call x4 -> x2, Pallas kernels: 6.46 us -> 4.46 us  [condition_fast(): pl.pallas_call(functools.partial(condition_kernel, slices, rows_here), gr...]
    dynamic_slice x3 -> x2, local copies, waits for them, and re-layouts: 2.74 us -> 3.1 us  [body(): lax.dynamic_slice_in_dim(source, first + (here ^ mask) * each, each, 0)]
  transfers between devices with their start and end apart: 32 -> 22, of which waited for: 17 -> 10; matrix products, arithmetic and copies ran while one was open for 13% -> 7% of each run, Pallas kernels for 5% -> 4%
where the time goes in v6:
time: 107 us
  waiting for transfers between devices  58.3 us (54%)
  starting transfers between devices  32.1 us (30%)
  local copies, waits for them, and re-layouts  4.83 us (5%)
  Pallas kernels  4.46 us (4%)
  other arithmetic  3.78 us (4%)
  matrix products  2.98 us (3%)
    ppermute x22, waiting for transfers between devices, crossed(): return lax.ppermute(value, axis, [(at, at ^ mask) for at in range(size)])  58.3 us
    ppermute x22, starting transfers between devices, crossed(): return lax.ppermute(value, axis, [(at, at ^ mask) for at in range(size)])  32.1 us
    pallas_call x2, Pallas kernels, condition_fast(): pl.pallas_call(functools.partial(condition_kernel, slices, rows_here), gr...  4.46 us
    dynamic_slice x2, local copies, waits for them, and re-layouts, body(): lax.dynamic_slice_in_dim(source, first + (here ^ mask) * each, each, 0)  3.1 us
    dot_general x4, matrix products, products(): lax.dot_general(block, train_flat, contract, preferred_element_type=jnp.f...  2.98 us
  transfers between devices with their start and end apart: 22, of which 10 were waited for; matrix products, arithmetic and copies ran while one was open for 7% of the time, Pallas kernels for 4%

profile of v6, /device:TPU:0, one launch (start us, length us, event | category | flops | bytes accessed | tf_op | source)
XLA Modules:
  0.0 106.8 jit_solution(10738302237972909933)
XLA Ops:
  0.0 1.3 %constant_dynamic-slice_fusion.4 = (bf16[32,16,128]{2,1,0:T(8,128)(2,1)S(1)}, bf16[32,16,128]{2,1,0:T(8,128)(2,1)S(1)}, bf16[32,16,128]{2,1,0:T(8,128)(2,1)S(1)}, bf16[32,16,128]{2,1,0:T(8,128)(2,1)S(1)}) fusion(bf16[256,16,128]{2,1,0:T(8,128)(2,1)} %param.5, s32[]{:T(128)S(6)} %select_n.355, s32[]{:T(128)S(6)} %select_n.354, s32[]{:T(128)S(6)} %select_n.353, ...), kind=kLoop, calls=%fused_computation.94 | loop fusion | bytes 1048592 | tf_op jit(solution)/shard_map/dynamic_slice | solution.py:159
  1.3 3.1 %collective-permute-start = (bf16[32,16,128]{2,1,0:T(8,128)(2,1)S(1)}, bf16[32,16,128]{2,1,0:T(8,128)(2,1)S(1)}, u32[]{:S(2)}, u32[]{:S(2)}) collective-permute-start(bf16[32,16,128]{2,1,0:T(8,128)(2,1)S(1)} %get-tuple-element.24), channel_id=1, source_target_pairs={{0,1},{1,0},{2,3},{3,2},{4,5},{5,4},{6,7},{7,6},{8,9},{9,8},{10,11... | collective-permute-start | bytes 393224 | tf_op jit(solution)/shard_map/ppermute | solution.py:110
  4.4 2.6 %collective-permute-start.1 = (bf16[32,16,128]{2,1,0:T(8,128)(2,1)S(1)}, bf16[32,16,128]{2,1,0:T(8,128)(2,1)S(1)}, u32[]{:S(2)}, u32[]{:S(2)}) collective-permute-start(bf16[32,16,128]{2,1,0:T(8,128)(2,1)S(1)} %get-tuple-element.25), channel_id=1, source_target_pairs={{0,2},{1,3},{2,0},{3,1},{4,6},{5,7},{6,4},{7,5},{8,10},{9,11},{10,... | collective-permute-start | bytes 393224 | tf_op jit(solution)/shard_map/ppermute | solution.py:110
  7.0 0.0 collective-permute-start.2
  7.0 0.9 copy.6
  7.9 0.9 fusion.6
  8.8 0.8 add_divide_fusion.refs_8_
  9.6 0.8 broadcast_select_fusion.29
  10.4 1.8 %constant_dynamic-slice_fusion = (bf16[32,16,128]{2,1,0:T(8,128)(2,1)S(1)}, bf16[32,16,128]{2,1,0:T(8,128)(2,1)}, bf16[32,16,128]{2,1,0:T(8,128)(2,1)}, bf16[32,16,128]{2,1,0:T(8,128)(2,1)S(1)}) fusion(bf16[256,16,128]{2,1,0:T(8,128)(2,1)} %param.5, s32[]{:T(128)S(6)} %select_n.388, s32[]{:T(128)S(6)} %select_n.387, s32[]{:T(128)S(6)} %select_n.386, ...), kind=kLoop, calls=%fused_computation.90 | loop fusion | bytes 1048592 | tf_op jit(solution)/shard_map/dynamic_slice | solution.py:159
  12.2 0.0 collective-permute-done.refs_1_
  12.2 0.9 collective-permute-start.11
  13.1 0.1 pad_maximum_fusion.8.refs_5_
  13.3 0.1 copy.7.refs_4_
  13.4 0.0 copy-start.1
  13.4 0.5 copy.11
  13.9 3.4 %collective-permute-done.1.refs_2_ = bf16[32,16,128]{2,1,0:T(8,128)(2,1)S(1)} collective-permute-done((bf16[32,16,128]{2,1,0:T(8,128)(2,1)S(1)}, bf16[32,16,128]{2,1,0:T(8,128)(2,1)S(1)}, u32[]{:S(2)}, u32[]{:S(2)}) %collective-permute-start.1) | collective-permute-done | bytes 131104 | tf_op jit(solution)/shard_map/ppermute | solution.py:110
  17.3 0.0 collective-permute-done.2.refs_3_
  17.3 2.2 %shard_map.55 = (bf16[32,2048]{1,0:T(8,128)(2,1)S(1)}, bf16[32,2048]{1,0:T(8,128)(2,1)S(1)}, bf16[32,2048]{1,0:T(8,128)(2,1)S(1)}, bf16[32,2048]{1,0:T(8,128)(2,1)S(1)}) custom-call(bf16[32,16,128]{2,1,0:T(8,128)(2,1)S(1)} %get-tuple-element.23.refs_0_, bf16[32,16,128]{2,1,0:T(8,128)(2,1)S(1)} %collective-permute-done.refs_1_, ...), custom_call_target="tpu_custom_call" | custom-call | tf_op jit(solution)/shard_map/pallas_call | solution.py:78
  19.5 2.0 %collective-permute-start.3 = (bf16[32,2048]{1,0:T(8,128)(2,1)S(1)}, bf16[32,2048]{1,0:T(8,128)(2,1)S(1)}, u32[]{:S(2)}, u32[]{:S(2)}) collective-permute-start(bf16[32,2048]{1,0:T(8,128)(2,1)S(1)} %get-tuple-element.28), channel_id=1, source_target_pairs={{0,1},{1,0},{2,3},{3,2},{4,5},{5,4},{6,7},{7,6},{8,9},{9,8},{10,11... | collective-permute-start | bytes 393224 | tf_op jit(solution)/shard_map/ppermute | solution.py:110
  21.6 1.1 %collective-permute-start.4 = (bf16[32,2048]{1,0:T(8,128)(2,1)S(1)}, bf16[32,2048]{1,0:T(8,128)(2,1)S(1)}, u32[]{:S(2)}, u32[]{:S(2)}) collective-permute-start(bf16[32,2048]{1,0:T(8,128)(2,1)S(1)} %get-tuple-element.29), channel_id=1, source_target_pairs={{0,2},{1,3},{2,0},{3,1},{4,6},{5,7},{6,4},{7,5},{8,10},{9,11},{10,... | collective-permute-start | bytes 393224 | tf_op jit(solution)/shard_map/ppermute | solution.py:110
  22.7 1.4 %collective-permute-start.5 = (bf16[32,2048]{1,0:T(8,128)(2,1)S(1)}, bf16[32,2048]{1,0:T(8,128)(2,1)S(1)}, u32[]{:S(2)}, u32[]{:S(2)}) collective-permute-start(bf16[32,2048]{1,0:T(8,128)(2,1)S(1)} %get-tuple-element.30), channel_id=1, source_target_pairs={{0,3},{1,2},{2,1},{3,0},{4,7},{5,6},{6,5},{7,4},{8,11},{9,10},{10,... | collective-permute-start | bytes 393224 | tf_op jit(solution)/shard_map/ppermute | solution.py:110
  24.0 2.0 %collective-permute-start.12 = (bf16[32,16,128]{2,1,0:T(8,128)(2,1)S(1)}, bf16[32,16,128]{2,1,0:T(8,128)(2,1)S(1)}, u32[]{:S(2)}, u32[]{:S(2)}) collective-permute-start(bf16[32,16,128]{2,1,0:T(8,128)(2,1)S(1)} %copy-done.1), channel_id=1, source_target_pairs={{0,2},{1,3},{2,0},{3,1},{4,6},{5,7},{6,4},{7,5},{8,10},{9,11},{10,... | collective-permute-start | bytes 393224 | tf_op jit(solution)/shard_map/ppermute | solution.py:110
  26.1 0.0 collective-permute-done.11.refs_1_
  26.1 1.4 %collective-permute-start.13 = (bf16[32,16,128]{2,1,0:T(8,128)(2,1)S(1)}, bf16[32,16,128]{2,1,0:T(8,128)(2,1)S(1)}, u32[]{:S(2)}, u32[]{:S(2)}) collective-permute-start(bf16[32,16,128]{2,1,0:T(8,128)(2,1)S(1)} %get-tuple-element.35), channel_id=1, source_target_pairs={{0,3},{1,2},{2,1},{3,0},{4,7},{5,6},{6,5},{7,4},{8,11},{9,10},{10,... | collective-permute-start | bytes 393224 | tf_op jit(solution)/shard_map/ppermute | solution.py:110
  27.4 17.1 %collective-permute-done.12.refs_2_ = bf16[32,16,128]{2,1,0:T(8,128)(2,1)S(1)} collective-permute-done((bf16[32,16,128]{2,1,0:T(8,128)(2,1)S(1)}, bf16[32,16,128]{2,1,0:T(8,128)(2,1)S(1)}, u32[]{:S(2)}, u32[]{:S(2)}) %collective-permute-start.12) | collective-permute-done | bytes 131104 | tf_op jit(solution)/shard_map/ppermute | solution.py:110
  44.6 0.0 collective-permute-done.13.refs_3_
  44.6 2.2 %shard_map.56 = (bf16[32,2048]{1,0:T(8,128)(2,1)S(1)}, bf16[32,2048]{1,0:T(8,128)(2,1)S(1)}, bf16[32,2048]{1,0:T(8,128)(2,1)S(1)}, bf16[32,2048]{1,0:T(8,128)(2,1)S(1)}) custom-call(bf16[32,16,128]{2,1,0:T(8,128)(2,1)S(1)} %get-tuple-element.32.refs_0_, bf16[32,16,128]{2,1,0:T(8,128)(2,1)S(1)} %collective-permute-done.11.refs_1_, ...), custom_call_target="tpu_custom_call" | custom-call | tf_op jit(solution)/shard_map/pallas_call | solution.py:78
  46.8 2.0 %collective-permute-start.14 = (bf16[32,2048]{1,0:T(8,128)(2,1)S(1)}, bf16[32,2048]{1,0:T(8,128)(2,1)S(1)}, u32[]{:S(2)}, u32[]{:S(2)}) collective-permute-start(bf16[32,2048]{1,0:T(8,128)(2,1)S(1)} %get-tuple-element.37), channel_id=1, source_target_pairs={{0,1},{1,0},{2,3},{3,2},{4,5},{5,4},{6,7},{7,6},{8,9},{9,8},{10,11... | collective-permute-start | bytes 393224 | tf_op jit(solution)/shard_map/ppermute | solution.py:110
  48.8 1.2 %collective-permute-start.15 = (bf16[32,2048]{1,0:T(8,128)(2,1)S(1)}, bf16[32,2048]{1,0:T(8,128)(2,1)S(1)}, u32[]{:S(2)}, u32[]{:S(2)}) collective-permute-start(bf16[32,2048]{1,0:T(8,128)(2,1)S(1)} %get-tuple-element.38), channel_id=1, source_target_pairs={{0,2},{1,3},{2,0},{3,1},{4,6},{5,7},{6,4},{7,5},{8,10},{9,11},{10,... | collective-permute-start | bytes 393224 | tf_op jit(solution)/shard_map/ppermute | solution.py:110
  50.0 0.0 collective-permute-done.3
  50.0 1.4 %collective-permute-start.16 = (bf16[32,2048]{1,0:T(8,128)(2,1)S(1)}, bf16[32,2048]{1,0:T(8,128)(2,1)S(1)}, u32[]{:S(2)}, u32[]{:S(2)}) collective-permute-start(bf16[32,2048]{1,0:T(8,128)(2,1)S(1)} %get-tuple-element.39), channel_id=1, source_target_pairs={{0,3},{1,2},{2,1},{3,0},{4,7},{5,6},{6,5},{7,4},{8,11},{9,10},{10,... | collective-permute-start | bytes 393224 | tf_op jit(solution)/shard_map/ppermute | solution.py:110
  51.4 0.0 collective-permute-done.4
  51.4 0.0 collective-permute-done.5
  51.5 1.5 %collective-permute-start.6 = (bf16[128,2048]{1,0:T(8,128)(2,1)S(1)}, bf16[128,2048]{1,0:T(8,128)(2,1)S(1)}, u32[]{:S(2)}, u32[]{:S(2)}) collective-permute-start(bf16[128,2048]{1,0:T(8,128)(2,1)S(1)} %pad_maximum_fusion), channel_id=1, source_target_pairs={{0,8},{4,12},{8,0},{12,4},{1,9},{5,13},{9,1},{13,5},{2,10},{6,14},... | collective-permute-start | bytes 1572872 | tf_op jit(solution)/shard_map/ppermute | solution.py:110
  53.1 0.2 collective-permute-done.14
  53.3 7.8 %collective-permute-done.15 = bf16[32,2048]{1,0:T(8,128)(2,1)S(1)} collective-permute-done((bf16[32,2048]{1,0:T(8,128)(2,1)S(1)}, bf16[32,2048]{1,0:T(8,128)(2,1)S(1)}, u32[]{:S(2)}, u32[]{:S(2)}) %collective-permute-start.15) | collective-permute-done | bytes 131104 | tf_op jit(solution)/shard_map/ppermute | solution.py:110
  61.1 0.0 collective-permute-done.16
  61.1 1.5 %collective-permute-start.17 = (bf16[128,2048]{1,0:T(8,128)(2,1)S(1)}, bf16[128,2048]{1,0:T(8,128)(2,1)S(1)}, u32[]{:S(2)}, u32[]{:S(2)}) collective-permute-start(bf16[128,2048]{1,0:T(8,128)(2,1)S(1)} %pad_maximum_fusion.1), channel_id=1, source_target_pairs={{0,8},{4,12},{8,0},{12,4},{1,9},{5,13},{9,1},{13,5},{2,10},{6,14},... | collective-permute-start | bytes 1572872 | tf_op jit(solution)/shard_map/ppermute | solution.py:110
  62.7 3.7 %collective-permute-done.6 = bf16[128,2048]{1,0:T(8,128)(2,1)S(1)} collective-permute-done((bf16[128,2048]{1,0:T(8,128)(2,1)S(1)}, bf16[128,2048]{1,0:T(8,128)(2,1)S(1)}, u32[]{:S(2)}, u32[]{:S(2)}) %collective-permute-start.6) | collective-permute-done | bytes 524320 | tf_op jit(solution)/shard_map/ppermute | solution.py:110
  66.4 0.1 collective-permute-start.7
  66.6 0.8 convolution_convert_fusion.2
  67.3 8.0 %collective-permute-done.17 = bf16[128,2048]{1,0:T(8,128)(2,1)S(1)} collective-permute-done((bf16[128,2048]{1,0:T(8,128)(2,1)S(1)}, bf16[128,2048]{1,0:T(8,128)(2,1)S(1)}, u32[]{:S(2)}, u32[]{:S(2)}) %collective-permute-start.17) | collective-permute-done | bytes 524320 | tf_op jit(solution)/shard_map/ppermute | solution.py:110
  75.4 0.0 collective-permute-done.7
  75.4 0.7 convolution_convert_fusion.3
  76.1 0.1 broadcast_select_fusion.9
  76.2 0.1 collective-permute-start.18
  76.3 0.6 collective-permute-start.8
  76.9 2.4 %collective-permute-start.9 = (bf16[1,128,512]{2,1,0:T(8,128)(2,1)S(1)}, bf16[1,128,512]{2,1,0:T(8,128)(2,1)S(1)}, u32[]{:S(2)}, u32[]{:S(2)}) collective-permute-start(bf16[1,128,512]{2,1,0:T(8,128)(2,1)S(1)} %get-tuple-element.61), channel_id=1, source_target_pairs={{0,2},{1,3},{2,0},{3,1},{4,6},{5,7},{6,4},{7,5},{8,10},{9,11},{10,... | collective-permute-start | bytes 393224 | tf_op jit(solution)/shard_map/ppermute | solution.py:110
  79.3 1.4 %collective-permute-start.10 = (bf16[1,128,512]{2,1,0:T(8,128)(2,1)S(1)}, bf16[1,128,512]{2,1,0:T(8,128)(2,1)S(1)}, u32[]{:S(2)}, u32[]{:S(2)}) collective-permute-start(bf16[1,128,512]{2,1,0:T(8,128)(2,1)S(1)} %get-tuple-element.62), channel_id=1, source_target_pairs={{0,3},{1,2},{2,1},{3,0},{4,7},{5,6},{6,5},{7,4},{8,11},{9,10},{10,... | collective-permute-start | bytes 393224 | tf_op jit(solution)/shard_map/ppermute | solution.py:110
  80.7 0.7 convolution_convert_fusion
  81.5 3.2 %collective-permute-done.8 = bf16[1,128,512]{2,1,0:T(8,128)(2,1)S(1)} collective-permute-done((bf16[1,128,512]{2,1,0:T(8,128)(2,1)S(1)}, bf16[1,128,512]{2,1,0:T(8,128)(2,1)S(1)}, u32[]{:S(2)}, u32[]{:S(2)}) %collective-permute-start.8) | collective-permute-done | bytes 131104 | tf_op jit(solution)/shard_map/ppermute | solution.py:110
  84.7 5.1 %collective-permute-done.9 = bf16[1,128,512]{2,1,0:T(8,128)(2,1)S(1)} collective-permute-done((bf16[1,128,512]{2,1,0:T(8,128)(2,1)S(1)}, bf16[1,128,512]{2,1,0:T(8,128)(2,1)S(1)}, u32[]{:S(2)}, u32[]{:S(2)}) %collective-permute-start.9) | collective-permute-done | bytes 131104 | tf_op jit(solution)/shard_map/ppermute | solution.py:110
  89.8 0.0 collective-permute-done.10
  89.8 0.1 broadcast_select_fusion.25
  89.9 0.8 convolution_convert_fusion.1
  90.7 0.1 broadcast_select_fusion.8
  90.7 2.7 %collective-permute-start.19 = (bf16[1,128,512]{2,1,0:T(8,128)(2,1)S(1)}, bf16[1,128,512]{2,1,0:T(8,128)(2,1)S(1)}, u32[]{:S(2)}, u32[]{:S(2)}) collective-permute-start(bf16[1,128,512]{2,1,0:T(8,128)(2,1)S(1)} %get-tuple-element.64), channel_id=1, source_target_pairs={{0,1},{1,0},{2,3},{3,2},{4,5},{5,4},{6,7},{7,6},{8,9},{9,8},{10,11... | collective-permute-start | bytes 393224 | tf_op jit(solution)/shard_map/ppermute | solution.py:110
  93.4 1.3 %collective-permute-start.20 = (bf16[1,128,512]{2,1,0:T(8,128)(2,1)S(1)}, bf16[1,128,512]{2,1,0:T(8,128)(2,1)S(1)}, u32[]{:S(2)}, u32[]{:S(2)}) collective-permute-start(bf16[1,128,512]{2,1,0:T(8,128)(2,1)S(1)} %get-tuple-element.65), channel_id=1, source_target_pairs={{0,2},{1,3},{2,0},{3,1},{4,6},{5,7},{6,4},{7,5},{8,10},{9,11},{10,... | collective-permute-start | bytes 393224 | tf_op jit(solution)/shard_map/ppermute | solution.py:110
  94.7 1.4 %collective-permute-start.21 = (bf16[1,128,512]{2,1,0:T(8,128)(2,1)S(1)}, bf16[1,128,512]{2,1,0:T(8,128)(2,1)S(1)}, u32[]{:S(2)}, u32[]{:S(2)}) collective-permute-start(bf16[1,128,512]{2,1,0:T(8,128)(2,1)S(1)} %get-tuple-element.66), channel_id=1, source_target_pairs={{0,3},{1,2},{2,1},{3,0},{4,7},{5,6},{6,5},{7,4},{8,11},{9,10},{10,... | collective-permute-start | bytes 393224 | tf_op jit(solution)/shard_map/ppermute | solution.py:110
  96.1 1.7 %collective-permute-done.19 = bf16[1,128,512]{2,1,0:T(8,128)(2,1)S(1)} collective-permute-done((bf16[1,128,512]{2,1,0:T(8,128)(2,1)S(1)}, bf16[1,128,512]{2,1,0:T(8,128)(2,1)S(1)}, u32[]{:S(2)}, u32[]{:S(2)}) %collective-permute-start.19) | collective-permute-done | bytes 131104 | tf_op jit(solution)/shard_map/ppermute | solution.py:110
  97.8 8.0 %collective-permute-done.20 = bf16[1,128,512]{2,1,0:T(8,128)(2,1)S(1)} collective-permute-done((bf16[1,128,512]{2,1,0:T(8,128)(2,1)S(1)}, bf16[1,128,512]{2,1,0:T(8,128)(2,1)S(1)}, u32[]{:S(2)}, u32[]{:S(2)}) %collective-permute-start.20) | collective-permute-done | bytes 131104 | tf_op jit(solution)/shard_map/ppermute | solution.py:110
  105.8 0.0 collective-permute-done.21
  105.8 0.1 broadcast_select_fusion.21
  105.9 0.8 maximum_bitcast_fusion
  (25 shorter events, 0.4 us)
Async XLA Ops:
  0.0 13.3 %copy-start = (bf16[512,16,128]{2,1,0:T(8,128)(2,1)S(1)}, bf16[512,16,128]{2,1,0:T(8,128)(2,1)}, u32[]{:S(2)}) copy-start(bf16[512,16,128]{2,1,0:T(8,128)(2,1)} %param.6) | copy-start | bytes 6291460
  1.3 11.0 %collective-permute-start = (bf16[32,16,128]{2,1,0:T(8,128)(2,1)S(1)}, bf16[32,16,128]{2,1,0:T(8,128)(2,1)S(1)}, u32[]{:S(2)}, u32[]{:S(2)}) collective-permute-start(bf16[32,16,128]{2,1,0:T(8,128)(2,1)S(1)} %get-tuple-element.24), channel_id=1, source_target_pairs={{0,1},{1,0},{2,3},{3,2},{4,5},{5,4},{6,7},{7,6},{8,9},{9,8},{10,11... | collective-permute-start | bytes 393224 | tf_op jit(solution)/shard_map/ppermute | solution.py:110
  4.4 12.9 %collective-permute-start.1 = (bf16[32,16,128]{2,1,0:T(8,128)(2,1)S(1)}, bf16[32,16,128]{2,1,0:T(8,128)(2,1)S(1)}, u32[]{:S(2)}, u32[]{:S(2)}) collective-permute-start(bf16[32,16,128]{2,1,0:T(8,128)(2,1)S(1)} %get-tuple-element.25), channel_id=1, source_target_pairs={{0,2},{1,3},{2,0},{3,1},{4,6},{5,7},{6,4},{7,5},{8,10},{9,11},{10,... | collective-permute-start | bytes 393224 | tf_op jit(solution)/shard_map/ppermute | solution.py:110
  7.0 10.3 %collective-permute-start.2 = (bf16[32,16,128]{2,1,0:T(8,128)(2,1)S(1)}, bf16[32,16,128]{2,1,0:T(8,128)(2,1)S(1)}, u32[]{:S(2)}, u32[]{:S(2)}) collective-permute-start(bf16[32,16,128]{2,1,0:T(8,128)(2,1)S(1)} %get-tuple-element.26), channel_id=1, source_target_pairs={{0,3},{1,2},{2,1},{3,0},{4,7},{5,6},{6,5},{7,4},{8,11},{9,10},{10,... | collective-permute-start | bytes 393224 | tf_op jit(solution)/shard_map/ppermute | solution.py:110
  12.2 13.8 %collective-permute-start.11 = (bf16[32,16,128]{2,1,0:T(8,128)(2,1)}, bf16[32,16,128]{2,1,0:T(8,128)(2,1)S(1)}, u32[]{:S(2)}, u32[]{:S(2)}) collective-permute-start(bf16[32,16,128]{2,1,0:T(8,128)(2,1)} %get-tuple-element.33), channel_id=1, source_target_pairs={{0,1},{1,0},{2,3},{3,2},{4,5},{5,4},{6,7},{7,6},{8,9},{9,8},{10,11... | collective-permute-start | bytes 393224 | tf_op jit(solution)/shard_map/ppermute | solution.py:110
  13.4 10.7 %copy-start.1 = (bf16[32,16,128]{2,1,0:T(8,128)(2,1)S(1)}, bf16[32,16,128]{2,1,0:T(8,128)(2,1)}, u32[]{:S(2)}) copy-start(bf16[32,16,128]{2,1,0:T(8,128)(2,1)} %get-tuple-element.34) | copy-start | bytes 393220
  19.5 30.5 %collective-permute-start.3 = (bf16[32,2048]{1,0:T(8,128)(2,1)S(1)}, bf16[32,2048]{1,0:T(8,128)(2,1)S(1)}, u32[]{:S(2)}, u32[]{:S(2)}) collective-permute-start(bf16[32,2048]{1,0:T(8,128)(2,1)S(1)} %get-tuple-element.28), channel_id=1, source_target_pairs={{0,1},{1,0},{2,3},{3,2},{4,5},{5,4},{6,7},{7,6},{8,9},{9,8},{10,11... | collective-permute-start | bytes 393224 | tf_op jit(solution)/shard_map/ppermute | solution.py:110
  21.6 29.8 %collective-permute-start.4 = (bf16[32,2048]{1,0:T(8,128)(2,1)S(1)}, bf16[32,2048]{1,0:T(8,128)(2,1)S(1)}, u32[]{:S(2)}, u32[]{:S(2)}) collective-permute-start(bf16[32,2048]{1,0:T(8,128)(2,1)S(1)} %get-tuple-element.29), channel_id=1, source_target_pairs={{0,2},{1,3},{2,0},{3,1},{4,6},{5,7},{6,4},{7,5},{8,10},{9,11},{10,... | collective-permute-start | bytes 393224 | tf_op jit(solution)/shard_map/ppermute | solution.py:110
  22.7 28.7 %collective-permute-start.5 = (bf16[32,2048]{1,0:T(8,128)(2,1)S(1)}, bf16[32,2048]{1,0:T(8,128)(2,1)S(1)}, u32[]{:S(2)}, u32[]{:S(2)}) collective-permute-start(bf16[32,2048]{1,0:T(8,128)(2,1)S(1)} %get-tuple-element.30), channel_id=1, source_target_pairs={{0,3},{1,2},{2,1},{3,0},{4,7},{5,6},{6,5},{7,4},{8,11},{9,10},{10,... | collective-permute-start | bytes 393224 | tf_op jit(solution)/shard_map/ppermute | solution.py:110
  24.0 20.5 %collective-permute-start.12 = (bf16[32,16,128]{2,1,0:T(8,128)(2,1)S(1)}, bf16[32,16,128]{2,1,0:T(8,128)(2,1)S(1)}, u32[]{:S(2)}, u32[]{:S(2)}) collective-permute-start(bf16[32,16,128]{2,1,0:T(8,128)(2,1)S(1)} %copy-done.1), channel_id=1, source_target_pairs={{0,2},{1,3},{2,0},{3,1},{4,6},{5,7},{6,4},{7,5},{8,10},{9,11},{10,... | collective-permute-start | bytes 393224 | tf_op jit(solution)/shard_map/ppermute | solution.py:110
  26.1 18.5 %collective-permute-start.13 = (bf16[32,16,128]{2,1,0:T(8,128)(2,1)S(1)}, bf16[32,16,128]{2,1,0:T(8,128)(2,1)S(1)}, u32[]{:S(2)}, u32[]{:S(2)}) collective-permute-start(bf16[32,16,128]{2,1,0:T(8,128)(2,1)S(1)} %get-tuple-element.35), channel_id=1, source_target_pairs={{0,3},{1,2},{2,1},{3,0},{4,7},{5,6},{6,5},{7,4},{8,11},{9,10},{10,... | collective-permute-start | bytes 393224 | tf_op jit(solution)/shard_map/ppermute | solution.py:110
  46.8 6.4 %collective-permute-start.14 = (bf16[32,2048]{1,0:T(8,128)(2,1)S(1)}, bf16[32,2048]{1,0:T(8,128)(2,1)S(1)}, u32[]{:S(2)}, u32[]{:S(2)}) collective-permute-start(bf16[32,2048]{1,0:T(8,128)(2,1)S(1)} %get-tuple-element.37), channel_id=1, source_target_pairs={{0,1},{1,0},{2,3},{3,2},{4,5},{5,4},{6,7},{7,6},{8,9},{9,8},{10,11... | collective-permute-start | bytes 393224 | tf_op jit(solution)/shard_map/ppermute | solution.py:110
  48.8 12.2 %collective-permute-start.15 = (bf16[32,2048]{1,0:T(8,128)(2,1)S(1)}, bf16[32,2048]{1,0:T(8,128)(2,1)S(1)}, u32[]{:S(2)}, u32[]{:S(2)}) collective-permute-start(bf16[32,2048]{1,0:T(8,128)(2,1)S(1)} %get-tuple-element.38), channel_id=1, source_target_pairs={{0,2},{1,3},{2,0},{3,1},{4,6},{5,7},{6,4},{7,5},{8,10},{9,11},{10,... | collective-permute-start | bytes 393224 | tf_op jit(solution)/shard_map/ppermute | solution.py:110
  50.0 11.1 %collective-permute-start.16 = (bf16[32,2048]{1,0:T(8,128)(2,1)S(1)}, bf16[32,2048]{1,0:T(8,128)(2,1)S(1)}, u32[]{:S(2)}, u32[]{:S(2)}) collective-permute-start(bf16[32,2048]{1,0:T(8,128)(2,1)S(1)} %get-tuple-element.39), channel_id=1, source_target_pairs={{0,3},{1,2},{2,1},{3,0},{4,7},{5,6},{6,5},{7,4},{8,11},{9,10},{10,... | collective-permute-start | bytes 393224 | tf_op jit(solution)/shard_map/ppermute | solution.py:110
  51.5 14.9 %collective-permute-start.6 = (bf16[128,2048]{1,0:T(8,128)(2,1)S(1)}, bf16[128,2048]{1,0:T(8,128)(2,1)S(1)}, u32[]{:S(2)}, u32[]{:S(2)}) collective-permute-start(bf16[128,2048]{1,0:T(8,128)(2,1)S(1)} %pad_maximum_fusion), channel_id=1, source_target_pairs={{0,8},{4,12},{8,0},{12,4},{1,9},{5,13},{9,1},{13,5},{2,10},{6,14},... | collective-permute-start | bytes 1572872 | tf_op jit(solution)/shard_map/ppermute | solution.py:110
  61.1 14.2 %collective-permute-start.17 = (bf16[128,2048]{1,0:T(8,128)(2,1)S(1)}, bf16[128,2048]{1,0:T(8,128)(2,1)S(1)}, u32[]{:S(2)}, u32[]{:S(2)}) collective-permute-start(bf16[128,2048]{1,0:T(8,128)(2,1)S(1)} %pad_maximum_fusion.1), channel_id=1, source_target_pairs={{0,8},{4,12},{8,0},{12,4},{1,9},{5,13},{9,1},{13,5},{2,10},{6,14},... | collective-permute-start | bytes 1572872 | tf_op jit(solution)/shard_map/ppermute | solution.py:110
  66.4 8.9 %collective-permute-start.7 = (bf16[256,2048]{1,0:T(8,128)(2,1)S(1)}, bf16[256,2048]{1,0:T(8,128)(2,1)S(1)}, u32[]{:S(2)}, u32[]{:S(2)}) collective-permute-start(bf16[256,2048]{1,0:T(8,128)(2,1)S(1)} %constant_dynamic-update-slice_fusion), channel_id=1, source_target_pairs={{0,4},{4,0},{8,12},{12,8},{1,5},{5,1},{9,13},{13,9},{2,6},{6,2},{1... | collective-permute-start | bytes 3145736 | tf_op jit(solution)/shard_map/ppermute | solution.py:110
  76.2 13.7 %collective-permute-start.18 = (bf16[256,2048]{1,0:T(8,128)(2,1)S(1)}, bf16[256,2048]{1,0:T(8,128)(2,1)S(1)}, u32[]{:S(2)}, u32[]{:S(2)}) collective-permute-start(bf16[256,2048]{1,0:T(8,128)(2,1)S(1)} %constant_dynamic-update-slice_fusion.5), channel_id=1, source_target_pairs={{0,4},{4,0},{8,12},{12,8},{1,5},{5,1},{9,13},{13,9},{2,6},{6,2},{1... | collective-permute-start | bytes 3145736 | tf_op jit(solution)/shard_map/ppermute | solution.py:110
  76.3 8.4 %collective-permute-start.8 = (bf16[1,128,512]{2,1,0:T(8,128)(2,1)S(1)}, bf16[1,128,512]{2,1,0:T(8,128)(2,1)S(1)}, u32[]{:S(2)}, u32[]{:S(2)}) collective-permute-start(bf16[1,128,512]{2,1,0:T(8,128)(2,1)S(1)} %get-tuple-element.60), channel_id=1, source_target_pairs={{0,1},{1,0},{2,3},{3,2},{4,5},{5,4},{6,7},{7,6},{8,9},{9,8},{10,11... | collective-permute-start | bytes 393224 | tf_op jit(solution)/shard_map/ppermute | solution.py:110
  76.9 12.9 %collective-permute-start.9 = (bf16[1,128,512]{2,1,0:T(8,128)(2,1)S(1)}, bf16[1,128,512]{2,1,0:T(8,128)(2,1)S(1)}, u32[]{:S(2)}, u32[]{:S(2)}) collective-permute-start(bf16[1,128,512]{2,1,0:T(8,128)(2,1)S(1)} %get-tuple-element.61), channel_id=1, source_target_pairs={{0,2},{1,3},{2,0},{3,1},{4,6},{5,7},{6,4},{7,5},{8,10},{9,11},{10,... | collective-permute-start | bytes 393224 | tf_op jit(solution)/shard_map/ppermute | solution.py:110
  79.3 10.5 %collective-permute-start.10 = (bf16[1,128,512]{2,1,0:T(8,128)(2,1)S(1)}, bf16[1,128,512]{2,1,0:T(8,128)(2,1)S(1)}, u32[]{:S(2)}, u32[]{:S(2)}) collective-permute-start(bf16[1,128,512]{2,1,0:T(8,128)(2,1)S(1)} %get-tuple-element.62), channel_id=1, source_target_pairs={{0,3},{1,2},{2,1},{3,0},{4,7},{5,6},{6,5},{7,4},{8,11},{9,10},{10,... | collective-permute-start | bytes 393224 | tf_op jit(solution)/shard_map/ppermute | solution.py:110
  90.7 7.1 %collective-permute-start.19 = (bf16[1,128,512]{2,1,0:T(8,128)(2,1)S(1)}, bf16[1,128,512]{2,1,0:T(8,128)(2,1)S(1)}, u32[]{:S(2)}, u32[]{:S(2)}) collective-permute-start(bf16[1,128,512]{2,1,0:T(8,128)(2,1)S(1)} %get-tuple-element.64), channel_id=1, source_target_pairs={{0,1},{1,0},{2,3},{3,2},{4,5},{5,4},{6,7},{7,6},{8,9},{9,8},{10,11... | collective-permute-start | bytes 393224 | tf_op jit(solution)/shard_map/ppermute | solution.py:110
  93.4 12.4 %collective-permute-start.20 = (bf16[1,128,512]{2,1,0:T(8,128)(2,1)S(1)}, bf16[1,128,512]{2,1,0:T(8,128)(2,1)S(1)}, u32[]{:S(2)}, u32[]{:S(2)}) collective-permute-start(bf16[1,128,512]{2,1,0:T(8,128)(2,1)S(1)} %get-tuple-element.65), channel_id=1, source_target_pairs={{0,2},{1,3},{2,0},{3,1},{4,6},{5,7},{6,4},{7,5},{8,10},{9,11},{10,... | collective-permute-start | bytes 393224 | tf_op jit(solution)/shard_map/ppermute | solution.py:110
  94.7 11.1 %collective-permute-start.21 = (bf16[1,128,512]{2,1,0:T(8,128)(2,1)S(1)}, bf16[1,128,512]{2,1,0:T(8,128)(2,1)S(1)}, u32[]{:S(2)}, u32[]{:S(2)}) collective-permute-start(bf16[1,128,512]{2,1,0:T(8,128)(2,1)S(1)} %get-tuple-element.66), channel_id=1, source_target_pairs={{0,3},{1,2},{2,1},{3,0},{4,7},{5,6},{6,5},{7,4},{8,11},{9,10},{10,... | collective-permute-start | bytes 393224 | tf_op jit(solution)/shard_map/ppermute | solution.py:110

commit v7 on v6

--- a/solution.py
+++ b/solution.py
@@ -7,8 +7,8 @@
 from jax.sharding import PartitionSpec as P
 
 damping_term = 0.05
-CHUNKS = (8, 8)
 BLOCK = 64
+SPLIT = 2
 
 
 def halves(value):
@@ -150,36 +150,41 @@
     basis = jnp.concatenate(turned([row_blocks[at] for at in range(slices)], here), axis=0)
     inverse = 1.0 / (corrections + damping_term)
     condition = condition_fast if rows_here % 16 == 0 else condition_plain
-    parts = [count * size // sum(CHUNKS) for size in CHUNKS]
-    firsts = [sum(parts[:chunk]) for chunk in range(len(parts))]
-    pieces, rows, blocks, results = [], [], [], []
+    each = count // slices
+    raw = [None] * slices
     source = queries
-    for first, part in zip(firsts, parts):
-        each = part // slices
-        raw = [lax.dynamic_slice_in_dim(source, first + (here ^ mask) * each, each, 0) for mask in range(slices)]
-        if pieces:
-            raw = after(raw, pieces[-1][1])
-        else:
-            raw, source = lax.optimization_barrier((raw, source))
-        pieces.append([raw[0]] + [crossed(raw[mask], "proj", slices, mask) for mask in range(1, slices)])
-    for chunk in range(len(parts)):
-        made = condition(pieces[chunk], basis, basis, in_basis, inverse)
-        rows.append([made[0]] + [crossed(made[mask], "proj", slices, mask) for mask in range(1, slices)])
-    for chunk, part in enumerate(parts):
-        near = spread_shares(jnp.concatenate(rows[chunk], axis=0), shares)
-        near = after(near, *blocks[-1:])
-        far = crossed(near, "dp", shares, 1)
-        values = products(near, far, train_flat, shares)
-        values = [jnp.stack(values[at * owned:(at + 1) * owned]) for at in range(slices)]
-        blocks.append(turned(values, here ^ (share // owned)))
-    for part, block in zip(parts, blocks):
-        came = [block[0]] + [crossed(block[mask], "proj", slices, mask) for mask in range(1, slices)]
-        came = [value.reshape(owned, slices, part // slices, train_count) for value in came]
-        total = [sum(came[mask][:, at ^ mask].astype(jnp.float32) for mask in range(slices)) for at in range(slices)]
-        total = jnp.stack(turned(total, here), axis=1)
-        total = jnp.stack(turned([total[at] for at in range(owned)], share % owned))
-        results.append(total.reshape(owned, part, train_count))
-    return jnp.concatenate(results, axis=1).reshape(owned * count, train_count)
+    for mask in reversed(range(slices)):
+        block = lax.dynamic_slice_in_dim(source, (here ^ mask) * each, each, 0)
+        raw[mask], source = lax.optimization_barrier((block, source))
+    arrived = [raw[0]] + [crossed(raw[mask], "proj", slices, mask) for mask in range(1, slices)]
+    arrived, train_flat = lax.optimization_barrier((arrived, train_flat))
+    made = condition(arrived, basis, basis, in_basis, inverse)
+    rows = [made[0]] + [crossed(made[mask], "proj", slices, mask) for mask in range(1, slices)]
+    half = slices // 2
+    groups = [range(half), range(half, slices)]
+    scores = [[None] * slices for _ in range(slices)]
+    came = []
+    for group in groups:
+        own = [rows[at] for at in group]
+        if not came:
+            own = own[:-1] + jnp.split(own[-1], SPLIT)
+        near = own
+        for mask in range(2, shares, 2):
+            near = near + [crossed(row, "dp", shares, mask) for row in own]
+        near = after(jnp.concatenate(near, axis=0), *(came[1:-1] or rows[half:]))
+        far = after(crossed(near, "dp", shares, 1), *came[-1:])
+        blocks = products(near, far, train_flat, shares)
+        blocks = [jnp.stack(blocks[at * owned:(at + 1) * owned]) for at in range(slices)]
+        blocks = turned(blocks, here ^ (share // owned))
+        came = [blocks[0]] + [crossed(blocks[mask], "proj", slices, mask) for mask in range(1, slices)]
+        for mask, block in enumerate(came):
+            block = block.reshape(owned, len(group), each, train_count)
+            for place, at in enumerate(group):
+                scores[at ^ mask][mask] = block[:, place].astype(jnp.float32)
+    total = [sum(scores[at]) for at in range(slices)]
+    total = jnp.stack(turned(total, here), axis=1)
+    total = jnp.stack(turned([total[at] for at in range(owned)], share % owned))
+    return total.reshape(owned * count, train_count)
 
 
 def solution(mesh):

time: 107 us -> 101 us (0.944)
  waiting for transfers between devices: 58.3 us -> 46.9 us
  local copies, waits for them, and re-layouts: 4.83 us -> 10 us
  matrix products: 2.98 us -> 5.47 us
  starting transfers between devices: 32.1 us -> 30.3 us
    ppermute x22 -> x19, waiting for transfers between devices: 58.3 us -> 46.9 us  [crossed(): return lax.ppermute(value, axis, [(at, at ^ mask) for at in range(size)])]
    unnamed x14 -> x16, local copies, waits for them, and re-layouts: 1.57 us -> 9.18 us
    dynamic_slice x2 -> x4, local copies, waits for them, and re-layouts: 3.1 us -> 0.09 us  [body(): block = lax.dynamic_slice_in_dim(source, (here ^ mask) * each, each, 0)]
    dot_general x4, matrix products: 2.98 us -> 5.47 us  [products(): lax.dot_general(block, train_flat, contract, preferred_element_type=jnp.f...]
    ppermute x22 -> x19, starting transfers between devices: 32.1 us -> 30.3 us  [crossed(): return lax.ppermute(value, axis, [(at, at ^ mask) for at in range(size)])]
    pallas_call x2 -> x1, Pallas kernels: 4.46 us -> 4.34 us  [condition_fast(): pl.pallas_call(functools.partial(condition_kernel, slices, rows_here), gr...]
  transfers between devices with their start and end apart: 22 -> 19, of which waited for: 10 -> 12; matrix products, arithmetic and copies ran while one was open for 7% -> 15% of each run, Pallas kernels for 4% -> 0%
where the time goes in v7:
time: 101 us; the launch traced here: 100 us
  waiting for transfers between devices  46.9 us (46%)
  starting transfers between devices  30.3 us (30%)
  local copies, waits for them, and re-layouts  10 us (10%)
  matrix products  5.47 us (5%)
  Pallas kernels  4.34 us (4%)
  other arithmetic  3 us (3%)
    ppermute x19, waiting for transfers between devices, crossed(): return lax.ppermute(value, axis, [(at, at ^ mask) for at in range(size)])  46.9 us
    ppermute x19, starting transfers between devices, crossed(): return lax.ppermute(value, axis, [(at, at ^ mask) for at in range(size)])  30.3 us
    unnamed x16, local copies, waits for them, and re-layouts  9.18 us
    dot_general x4, matrix products, products(): lax.dot_general(block, train_flat, contract, preferred_element_type=jnp.f...  5.47 us
    pallas_call x1, Pallas kernels, condition_fast(): pl.pallas_call(functools.partial(condition_kernel, slices, rows_here), gr...  4.34 us
  transfers between devices with their start and end apart: 19, of which 12 were waited for; matrix products, arithmetic and copies ran while one was open for 15% of the time, Pallas kernels for 0%

profile of v7, /device:TPU:0, one launch (start us, length us, event | category | flops | bytes accessed | tf_op | source)
XLA Modules:
  0.0 100.3 jit_solution(2036650124306305310)
XLA Ops:
  0.0 0.0 copy-start
  0.0 1.2 %copy-done = bf16[256,16,128]{2,1,0:T(8,128)(2,1)S(1)} copy-done((bf16[256,16,128]{2,1,0:T(8,128)(2,1)S(1)}, bf16[256,16,128]{2,1,0:T(8,128)(2,1)}, u32[]{:S(2)}) %copy-start) | copy-done | bytes 1048600
  1.3 3.1 %collective-permute-start = (bf16[64,16,128]{2,1,0:T(8,128)(2,1)S(1)}, bf16[64,16,128]{2,1,0:T(8,128)(2,1)S(1)}, u32[]{:S(2)}, u32[]{:S(2)}) collective-permute-start(bf16[64,16,128]{2,1,0:T(8,128)(2,1)S(1)} %constant_dynamic-slice_fusion.1), channel_id=1, source_target_pairs={{0,1},{1,0},{2,3},{3,2},{4,5},{5,4},{6,7},{7,6},{8,9},{9,8},{10,11... | collective-permute-start | bytes 786440 | tf_op jit(solution)/shard_map/ppermute | solution.py:110
  4.4 2.6 %collective-permute-start.1 = (bf16[64,16,128]{2,1,0:T(8,128)(2,1)S(1)}, bf16[64,16,128]{2,1,0:T(8,128)(2,1)S(1)}, u32[]{:S(2)}, u32[]{:S(2)}) collective-permute-start(bf16[64,16,128]{2,1,0:T(8,128)(2,1)S(1)} %constant_dynamic-slice_fusion.2), channel_id=1, source_target_pairs={{0,2},{1,3},{2,0},{3,1},{4,6},{5,7},{6,4},{7,5},{8,10},{9,11},{10,... | collective-permute-start | bytes 786440 | tf_op jit(solution)/shard_map/ppermute | solution.py:110
  7.0 0.0 collective-permute-start.2
  7.0 0.8 broadcast_select_fusion.21
  7.8 0.9 copy.6
  8.7 0.9 fusion.6
  9.7 0.1 pad_maximum_fusion.6.refs_5_
  9.8 3.5 %copy.10 = bf16[64,8,16,128]{3,1,2,0:T(8,128)(2,1)} copy(bf16[64,8,16,128]{3,2,1,0:T(8,128)(2,1)} %bitcast.51) | data formatting | bytes 4194304
  13.3 0.1 copy.7.refs_4_
  13.4 2.2 %collective-permute-done.refs_1_ = bf16[64,16,128]{2,1,0:T(8,128)(2,1)S(1)} collective-permute-done((bf16[64,16,128]{2,1,0:T(8,128)(2,1)S(1)}, bf16[64,16,128]{2,1,0:T(8,128)(2,1)S(1)}, u32[]{:S(2)}, u32[]{:S(2)}) %collective-permute-start) | collective-permute-done | bytes 262176 | tf_op jit(solution)/shard_map/ppermute | solution.py:110
  15.6 10.2 %collective-permute-done.1.refs_2_ = bf16[64,16,128]{2,1,0:T(8,128)(2,1)S(1)} collective-permute-done((bf16[64,16,128]{2,1,0:T(8,128)(2,1)S(1)}, bf16[64,16,128]{2,1,0:T(8,128)(2,1)S(1)}, u32[]{:S(2)}, u32[]{:S(2)}) %collective-permute-start.1) | collective-permute-done | bytes 262176 | tf_op jit(solution)/shard_map/ppermute | solution.py:110
  25.8 0.0 collective-permute-done.2.refs_3_
  25.8 4.3 %shard_map.55 = (bf16[64,2048]{1,0:T(8,128)(2,1)S(1)}, bf16[64,2048]{1,0:T(8,128)(2,1)S(1)}, bf16[64,2048]{1,0:T(8,128)(2,1)S(1)}, bf16[64,2048]{1,0:T(8,128)(2,1)S(1)}) custom-call(bf16[64,16,128]{2,1,0:T(8,128)(2,1)S(1)} %constant_dynamic-slice_fusion.refs_0_, bf16[64,16,128]{2,1,0:T(8,128)(2,1)S(1)} %collective-permute-done.refs_1_, ...), custom_call_target="tpu_custom_call" | custom-call | tf_op jit(solution)/shard_map/pallas_call | solution.py:78
  30.1 4.8 %collective-permute-start.7 = (bf16[64,2048]{1,0:T(8,128)(2,1)S(1)}, bf16[64,2048]{1,0:T(8,128)(2,1)S(1)}, u32[]{:S(2)}, u32[]{:S(2)}) collective-permute-start(bf16[64,2048]{1,0:T(8,128)(2,1)S(1)} %get-tuple-element.38), channel_id=1, source_target_pairs={{0,1},{1,0},{2,3},{3,2},{4,5},{5,4},{6,7},{7,6},{8,9},{9,8},{10,11... | collective-permute-start | bytes 786440 | tf_op jit(solution)/shard_map/ppermute | solution.py:110
  35.0 1.5 %collective-permute-start.8 = (bf16[64,2048]{1,0:T(8,128)(2,1)S(1)}, bf16[64,2048]{1,0:T(8,128)(2,1)S(1)}, u32[]{:S(2)}, u32[]{:S(2)}) collective-permute-start(bf16[64,2048]{1,0:T(8,128)(2,1)S(1)} %get-tuple-element.37), channel_id=1, source_target_pairs={{0,8},{4,12},{8,0},{12,4},{1,9},{5,13},{9,1},{13,5},{2,10},{6,14},... | collective-permute-start | bytes 786440 | tf_op jit(solution)/shard_map/ppermute | solution.py:110
  36.5 1.1 %collective-permute-start.3 = (bf16[64,2048]{1,0:T(8,128)(2,1)S(1)}, bf16[64,2048]{1,0:T(8,128)(2,1)S(1)}, u32[]{:S(2)}, u32[]{:S(2)}) collective-permute-start(bf16[64,2048]{1,0:T(8,128)(2,1)S(1)} %get-tuple-element.35), channel_id=1, source_target_pairs={{0,2},{1,3},{2,0},{3,1},{4,6},{5,7},{6,4},{7,5},{8,10},{9,11},{10,... | collective-permute-start | bytes 786440 | tf_op jit(solution)/shard_map/ppermute | solution.py:110
  37.5 1.4 %collective-permute-start.4 = (bf16[64,2048]{1,0:T(8,128)(2,1)S(1)}, bf16[64,2048]{1,0:T(8,128)(2,1)S(1)}, u32[]{:S(2)}, u32[]{:S(2)}) collective-permute-start(bf16[64,2048]{1,0:T(8,128)(2,1)S(1)} %get-tuple-element.36), channel_id=1, source_target_pairs={{0,3},{1,2},{2,1},{3,0},{4,7},{5,6},{6,5},{7,4},{8,11},{9,10},{10,... | collective-permute-start | bytes 786440 | tf_op jit(solution)/shard_map/ppermute | solution.py:110
  38.9 0.7 constant_dynamic-update-slice_fusion.4
  39.6 3.9 %collective-permute-done.7 = bf16[64,2048]{1,0:T(8,128)(2,1)S(1)} collective-permute-done((bf16[64,2048]{1,0:T(8,128)(2,1)S(1)}, bf16[64,2048]{1,0:T(8,128)(2,1)S(1)}, u32[]{:S(2)}, u32[]{:S(2)}) %collective-permute-start.7) | collective-permute-done | bytes 262176 | tf_op jit(solution)/shard_map/ppermute | solution.py:110
  43.6 1.9 %collective-permute-start.9 = (bf16[32,2048]{1,0:T(8,128)(2,1)S(1)}, bf16[32,2048]{1,0:T(8,128)(2,1)S(1)}, u32[]{:S(2)}, u32[]{:S(2)}) collective-permute-start(bf16[32,2048]{1,0:T(8,128)(2,1)S(1)} %get-tuple-element.60), channel_id=1, source_target_pairs={{0,8},{4,12},{8,0},{12,4},{1,9},{5,13},{9,1},{13,5},{2,10},{6,14},... | collective-permute-start | bytes 393224 | tf_op jit(solution)/shard_map/ppermute | solution.py:110
  45.4 0.2 collective-permute-start.10
  45.7 0.7 constant_dynamic-update-slice_fusion.3
  46.4 0.0 collective-permute-done.8
  46.4 0.7 constant_dynamic-update-slice_fusion.2
  47.1 1.5 %collective-permute-done.9 = bf16[32,2048]{1,0:T(8,128)(2,1)S(1)} collective-permute-done((bf16[32,2048]{1,0:T(8,128)(2,1)S(1)}, bf16[32,2048]{1,0:T(8,128)(2,1)S(1)}, u32[]{:S(2)}, u32[]{:S(2)}) %collective-permute-start.9) | collective-permute-done | bytes 131104 | tf_op jit(solution)/shard_map/ppermute | solution.py:110
  48.6 0.7 constant_dynamic-update-slice_fusion.1
  49.3 1.1 %collective-permute-done.10 = bf16[32,2048]{1,0:T(8,128)(2,1)S(1)} collective-permute-done((bf16[32,2048]{1,0:T(8,128)(2,1)S(1)}, bf16[32,2048]{1,0:T(8,128)(2,1)S(1)}, u32[]{:S(2)}, u32[]{:S(2)}) %collective-permute-start.10) | collective-permute-done | bytes 131104 | tf_op jit(solution)/shard_map/ppermute | solution.py:110
  50.4 0.7 constant_dynamic-update-slice_fusion
  51.1 6.3 %collective-permute-done.3 = bf16[64,2048]{1,0:T(8,128)(2,1)S(1)} collective-permute-done((bf16[64,2048]{1,0:T(8,128)(2,1)S(1)}, bf16[64,2048]{1,0:T(8,128)(2,1)S(1)}, u32[]{:S(2)}, u32[]{:S(2)}) %collective-permute-start.3) | collective-permute-done | bytes 262176 | tf_op jit(solution)/shard_map/ppermute | solution.py:110
  57.4 0.0 collective-permute-done.4
  57.4 0.7 copy-done.2
  58.1 0.0 collective-permute-start.11
  58.1 1.0 collective-permute-start.5
  59.0 1.1 %collective-permute-start.6 = (bf16[64,2048]{1,0:T(8,128)(2,1)}, bf16[64,2048]{1,0:T(8,128)(2,1)S(1)}, u32[]{:S(2)}, u32[]{:S(2)}) collective-permute-start(bf16[64,2048]{1,0:T(8,128)(2,1)} %copy-done.2), channel_id=1, source_target_pairs={{0,8},{4,12},{8,0},{12,4},{1,9},{5,13},{9,1},{13,5},{2,10},{6,14},... | collective-permute-start | bytes 786440 | tf_op jit(solution)/shard_map/ppermute | solution.py:110
  60.1 2.0 %convolution_convert_fusion.3 = bf16[256,512]{1,0:T(8,128)(2,1)S(1)} fusion(bf16[256,2048]{1,0:T(8,128)(2,1)} %constant_dynamic-update-slice_fusion, bf16[512,2048]{1,0:T(8,128)(2,1)S(1)} %bitcast.52), kind=kOutput, calls=%fused_computation.4 | convolution fusion | flops 537001984 | bytes 3407872 | tf_op jit(solution)/shard_map/dot_general | solution.py:125
  62.1 0.0 copy-start.3
  62.1 0.0 collective-permute-done.11
  62.1 2.0 %convolution_convert_fusion.2 = bf16[256,512]{1,0:T(8,128)(2,1)S(1)} fusion(bf16[256,2048]{1,0:T(8,128)(2,1)} %collective-permute-done.11, bf16[512,2048]{1,0:T(8,128)(2,1)S(1)} %bitcast.53), kind=kOutput, calls=%fused_computation.3 | convolution fusion | flops 537001984 | bytes 3407872 | tf_op jit(solution)/shard_map/dot_general | solution.py:125
  64.1 0.1 broadcast_select_fusion.8
  64.2 3.9 %collective-permute-start.12 = (bf16[1,128,512]{2,1,0:T(8,128)(2,1)S(1)}, bf16[1,128,512]{2,1,0:T(8,128)(2,1)S(1)}, u32[]{:S(2)}, u32[]{:S(2)}) collective-permute-start(bf16[1,128,512]{2,1,0:T(8,128)(2,1)S(1)} %get-tuple-element.58), channel_id=1, source_target_pairs={{0,1},{1,0},{2,3},{3,2},{4,5},{5,4},{6,7},{7,6},{8,9},{9,8},{10,11... | collective-permute-start | bytes 393224 | tf_op jit(solution)/shard_map/ppermute | solution.py:110
  68.0 1.0 %collective-permute-start.13 = (bf16[1,128,512]{2,1,0:T(8,128)(2,1)S(1)}, bf16[1,128,512]{2,1,0:T(8,128)(2,1)S(1)}, u32[]{:S(2)}, u32[]{:S(2)}) collective-permute-start(bf16[1,128,512]{2,1,0:T(8,128)(2,1)S(1)} %get-tuple-element.56), channel_id=1, source_target_pairs={{0,2},{1,3},{2,0},{3,1},{4,6},{5,7},{6,4},{7,5},{8,10},{9,11},{10,... | collective-permute-start | bytes 393224 | tf_op jit(solution)/shard_map/ppermute | solution.py:110
  69.1 0.0 collective-permute-done.5
  69.1 3.3 %collective-permute-done.6 = bf16[64,2048]{1,0:T(8,128)(2,1)S(1)} collective-permute-done((bf16[64,2048]{1,0:T(8,128)(2,1)}, bf16[64,2048]{1,0:T(8,128)(2,1)S(1)}, u32[]{:S(2)}, u32[]{:S(2)}) %collective-permute-start.6) | collective-permute-done | bytes 262176 | tf_op jit(solution)/shard_map/ppermute | solution.py:110
  72.4 0.1 pad_maximum_fusion
  72.5 1.0 %collective-permute-done.12 = bf16[1,128,512]{2,1,0:T(8,128)(2,1)S(1)} collective-permute-done((bf16[1,128,512]{2,1,0:T(8,128)(2,1)S(1)}, bf16[1,128,512]{2,1,0:T(8,128)(2,1)S(1)}, u32[]{:S(2)}, u32[]{:S(2)}) %collective-permute-start.12) | collective-permute-done | bytes 131104 | tf_op jit(solution)/shard_map/ppermute | solution.py:110
  73.6 3.3 %collective-permute-done.13 = bf16[1,128,512]{2,1,0:T(8,128)(2,1)S(1)} collective-permute-done((bf16[1,128,512]{2,1,0:T(8,128)(2,1)S(1)}, bf16[1,128,512]{2,1,0:T(8,128)(2,1)S(1)}, u32[]{:S(2)}, u32[]{:S(2)}) %collective-permute-start.13) | collective-permute-done | bytes 131104 | tf_op jit(solution)/shard_map/ppermute | solution.py:110
  76.9 0.0 collective-permute-start.14
  76.9 2.4 %collective-permute-start.15 = (bf16[1,128,512]{2,1,0:T(8,128)(2,1)S(1)}, bf16[1,128,512]{2,1,0:T(8,128)(2,1)S(1)}, u32[]{:S(2)}, u32[]{:S(2)}) collective-permute-start(bf16[1,128,512]{2,1,0:T(8,128)(2,1)S(1)} %get-tuple-element.57), channel_id=1, source_target_pairs={{0,3},{1,2},{2,1},{3,0},{4,7},{5,6},{6,5},{7,4},{8,11},{9,10},{10,... | collective-permute-start | bytes 393224 | tf_op jit(solution)/shard_map/ppermute | solution.py:110
  79.2 0.7 convolution_convert_fusion
  80.0 4.7 %collective-permute-done.15 = bf16[1,128,512]{2,1,0:T(8,128)(2,1)S(1)} collective-permute-done((bf16[1,128,512]{2,1,0:T(8,128)(2,1)S(1)}, bf16[1,128,512]{2,1,0:T(8,128)(2,1)S(1)}, u32[]{:S(2)}, u32[]{:S(2)}) %collective-permute-start.15) | collective-permute-done | bytes 131104 | tf_op jit(solution)/shard_map/ppermute | solution.py:110
  84.7 0.0 collective-permute-done.14
  84.7 0.8 convolution_convert_fusion.1
  85.4 0.1 broadcast_select_fusion.9
  85.5 1.4 %collective-permute-start.16 = (bf16[1,128,512]{2,1,0:T(8,128)(2,1)S(1)}, bf16[1,128,512]{2,1,0:T(8,128)(2,1)S(1)}, u32[]{:S(2)}, u32[]{:S(2)}) collective-permute-start(bf16[1,128,512]{2,1,0:T(8,128)(2,1)S(1)} %get-tuple-element.52), channel_id=1, source_target_pairs={{0,1},{1,0},{2,3},{3,2},{4,5},{5,4},{6,7},{7,6},{8,9},{9,8},{10,11... | collective-permute-start | bytes 393224 | tf_op jit(solution)/shard_map/ppermute | solution.py:110
  86.8 1.6 %collective-permute-start.17 = (bf16[1,128,512]{2,1,0:T(8,128)(2,1)S(1)}, bf16[1,128,512]{2,1,0:T(8,128)(2,1)S(1)}, u32[]{:S(2)}, u32[]{:S(2)}) collective-permute-start(bf16[1,128,512]{2,1,0:T(8,128)(2,1)S(1)} %get-tuple-element.53), channel_id=1, source_target_pairs={{0,2},{1,3},{2,0},{3,1},{4,6},{5,7},{6,4},{7,5},{8,10},{9,11},{10,... | collective-permute-start | bytes 393224 | tf_op jit(solution)/shard_map/ppermute | solution.py:110
  88.4 1.5 %collective-permute-start.18 = (bf16[1,128,512]{2,1,0:T(8,128)(2,1)S(1)}, bf16[1,128,512]{2,1,0:T(8,128)(2,1)S(1)}, u32[]{:S(2)}, u32[]{:S(2)}) collective-permute-start(bf16[1,128,512]{2,1,0:T(8,128)(2,1)S(1)} %get-tuple-element.54), channel_id=1, source_target_pairs={{0,3},{1,2},{2,1},{3,0},{4,7},{5,6},{6,5},{7,4},{8,11},{9,10},{10,... | collective-permute-start | bytes 393224 | tf_op jit(solution)/shard_map/ppermute | solution.py:110
  89.9 1.9 %collective-permute-done.16 = bf16[1,128,512]{2,1,0:T(8,128)(2,1)S(1)} collective-permute-done((bf16[1,128,512]{2,1,0:T(8,128)(2,1)S(1)}, bf16[1,128,512]{2,1,0:T(8,128)(2,1)S(1)}, u32[]{:S(2)}, u32[]{:S(2)}) %collective-permute-start.16) | collective-permute-done | bytes 131104 | tf_op jit(solution)/shard_map/ppermute | solution.py:110
  91.8 7.4 %collective-permute-done.17 = bf16[1,128,512]{2,1,0:T(8,128)(2,1)S(1)} collective-permute-done((bf16[1,128,512]{2,1,0:T(8,128)(2,1)S(1)}, bf16[1,128,512]{2,1,0:T(8,128)(2,1)S(1)}, u32[]{:S(2)}, u32[]{:S(2)}) %collective-permute-start.17) | collective-permute-done | bytes 131104 | tf_op jit(solution)/shard_map/ppermute | solution.py:110
  99.2 0.0 collective-permute-done.18
  99.2 0.1 broadcast_select_fusion.17
  99.4 0.1 broadcast_select_fusion.16
  99.5 0.8 pad_maximum_fusion.1
  (17 shorter events, 0.2 us)
Async XLA Ops:
  0.0 1.2 %copy-start = (bf16[256,16,128]{2,1,0:T(8,128)(2,1)S(1)}, bf16[256,16,128]{2,1,0:T(8,128)(2,1)}, u32[]{:S(2)}) copy-start(bf16[256,16,128]{2,1,0:T(8,128)(2,1)} %param.5) | copy-start | bytes 3145732
  1.3 14.2 %collective-permute-start = (bf16[64,16,128]{2,1,0:T(8,128)(2,1)S(1)}, bf16[64,16,128]{2,1,0:T(8,128)(2,1)S(1)}, u32[]{:S(2)}, u32[]{:S(2)}) collective-permute-start(bf16[64,16,128]{2,1,0:T(8,128)(2,1)S(1)} %constant_dynamic-slice_fusion.1), channel_id=1, source_target_pairs={{0,1},{1,0},{2,3},{3,2},{4,5},{5,4},{6,7},{7,6},{8,9},{9,8},{10,11... | collective-permute-start | bytes 786440 | tf_op jit(solution)/shard_map/ppermute | solution.py:110
  4.4 21.4 %collective-permute-start.1 = (bf16[64,16,128]{2,1,0:T(8,128)(2,1)S(1)}, bf16[64,16,128]{2,1,0:T(8,128)(2,1)S(1)}, u32[]{:S(2)}, u32[]{:S(2)}) collective-permute-start(bf16[64,16,128]{2,1,0:T(8,128)(2,1)S(1)} %constant_dynamic-slice_fusion.2), channel_id=1, source_target_pairs={{0,2},{1,3},{2,0},{3,1},{4,6},{5,7},{6,4},{7,5},{8,10},{9,11},{10,... | collective-permute-start | bytes 786440 | tf_op jit(solution)/shard_map/ppermute | solution.py:110
  7.0 18.8 %collective-permute-start.2 = (bf16[64,16,128]{2,1,0:T(8,128)(2,1)S(1)}, bf16[64,16,128]{2,1,0:T(8,128)(2,1)S(1)}, u32[]{:S(2)}, u32[]{:S(2)}) collective-permute-start(bf16[64,16,128]{2,1,0:T(8,128)(2,1)S(1)} %constant_dynamic-slice_fusion.3), channel_id=1, source_target_pairs={{0,3},{1,2},{2,1},{3,0},{4,7},{5,6},{6,5},{7,4},{8,11},{9,10},{10,... | collective-permute-start | bytes 786440 | tf_op jit(solution)/shard_map/ppermute | solution.py:110
  9.8 3.6 %copy-start.4 = (f32[64,128]{1,0:T(8,128)S(1)}, f32[64,128]{1,0:T(8,128)}, u32[]{:S(2)}) copy-start(f32[64,128]{1,0:T(8,128)} %param.9) | copy-start | bytes 98308
  30.1 30.0 %copy-start.1 = (bf16[64,8,16,128]{3,1,2,0:T(8,128)(2,1)S(1)}, bf16[64,8,16,128]{3,1,2,0:T(8,128)(2,1)}, u32[]{:S(2)}) copy-start(bf16[64,8,16,128]{3,1,2,0:T(8,128)(2,1)} %copy.10) | copy-start | bytes 6291460
  30.1 13.4 %collective-permute-start.7 = (bf16[64,2048]{1,0:T(8,128)(2,1)S(1)}, bf16[64,2048]{1,0:T(8,128)(2,1)S(1)}, u32[]{:S(2)}, u32[]{:S(2)}) collective-permute-start(bf16[64,2048]{1,0:T(8,128)(2,1)S(1)} %get-tuple-element.38), channel_id=1, source_target_pairs={{0,1},{1,0},{2,3},{3,2},{4,5},{5,4},{6,7},{7,6},{8,9},{9,8},{10,11... | collective-permute-start | bytes 786440 | tf_op jit(solution)/shard_map/ppermute | solution.py:110
  35.0 11.4 %collective-permute-start.8 = (bf16[64,2048]{1,0:T(8,128)(2,1)S(1)}, bf16[64,2048]{1,0:T(8,128)(2,1)S(1)}, u32[]{:S(2)}, u32[]{:S(2)}) collective-permute-start(bf16[64,2048]{1,0:T(8,128)(2,1)S(1)} %get-tuple-element.37), channel_id=1, source_target_pairs={{0,8},{4,12},{8,0},{12,4},{1,9},{5,13},{9,1},{13,5},{2,10},{6,14},... | collective-permute-start | bytes 786440 | tf_op jit(solution)/shard_map/ppermute | solution.py:110
  36.5 20.9 %collective-permute-start.3 = (bf16[64,2048]{1,0:T(8,128)(2,1)S(1)}, bf16[64,2048]{1,0:T(8,128)(2,1)S(1)}, u32[]{:S(2)}, u32[]{:S(2)}) collective-permute-start(bf16[64,2048]{1,0:T(8,128)(2,1)S(1)} %get-tuple-element.35), channel_id=1, source_target_pairs={{0,2},{1,3},{2,0},{3,1},{4,6},{5,7},{6,4},{7,5},{8,10},{9,11},{10,... | collective-permute-start | bytes 786440 | tf_op jit(solution)/shard_map/ppermute | solution.py:110
  37.5 19.8 %collective-permute-start.4 = (bf16[64,2048]{1,0:T(8,128)(2,1)S(1)}, bf16[64,2048]{1,0:T(8,128)(2,1)S(1)}, u32[]{:S(2)}, u32[]{:S(2)}) collective-permute-start(bf16[64,2048]{1,0:T(8,128)(2,1)S(1)} %get-tuple-element.36), channel_id=1, source_target_pairs={{0,3},{1,2},{2,1},{3,0},{4,7},{5,6},{6,5},{7,4},{8,11},{9,10},{10,... | collective-permute-start | bytes 786440 | tf_op jit(solution)/shard_map/ppermute | solution.py:110
  43.6 5.0 %collective-permute-start.9 = (bf16[32,2048]{1,0:T(8,128)(2,1)S(1)}, bf16[32,2048]{1,0:T(8,128)(2,1)S(1)}, u32[]{:S(2)}, u32[]{:S(2)}) collective-permute-start(bf16[32,2048]{1,0:T(8,128)(2,1)S(1)} %get-tuple-element.60), channel_id=1, source_target_pairs={{0,8},{4,12},{8,0},{12,4},{1,9},{5,13},{9,1},{13,5},{2,10},{6,14},... | collective-permute-start | bytes 393224 | tf_op jit(solution)/shard_map/ppermute | solution.py:110
  45.4 5.0 %collective-permute-start.10 = (bf16[32,2048]{1,0:T(8,128)(2,1)S(1)}, bf16[32,2048]{1,0:T(8,128)(2,1)S(1)}, u32[]{:S(2)}, u32[]{:S(2)}) collective-permute-start(bf16[32,2048]{1,0:T(8,128)(2,1)S(1)} %get-tuple-element.59), channel_id=1, source_target_pairs={{0,8},{4,12},{8,0},{12,4},{1,9},{5,13},{9,1},{13,5},{2,10},{6,14},... | collective-permute-start | bytes 393224 | tf_op jit(solution)/shard_map/ppermute | solution.py:110
  57.4 0.7 copy-start.2
  58.1 4.0 %collective-permute-start.11 = (bf16[256,2048]{1,0:T(8,128)(2,1)}, bf16[256,2048]{1,0:T(8,128)(2,1)}, u32[]{:S(2)}, u32[]{:S(2)}) collective-permute-start(bf16[256,2048]{1,0:T(8,128)(2,1)} %constant_dynamic-update-slice_fusion), channel_id=1, source_target_pairs={{0,4},{4,0},{8,12},{12,8},{1,5},{5,1},{9,13},{13,9},{2,6},{6,2},{1... | collective-permute-start | bytes 3145736 | tf_op jit(solution)/shard_map/ppermute | solution.py:110
  58.1 11.0 %collective-permute-start.5 = (bf16[64,2048]{1,0:T(8,128)(2,1)S(1)}, bf16[64,2048]{1,0:T(8,128)(2,1)S(1)}, u32[]{:S(2)}, u32[]{:S(2)}) collective-permute-start(bf16[64,2048]{1,0:T(8,128)(2,1)S(1)} %collective-permute-done.3), channel_id=1, source_target_pairs={{0,8},{4,12},{8,0},{12,4},{1,9},{5,13},{9,1},{13,5},{2,10},{6,14},... | collective-permute-start | bytes 786440 | tf_op jit(solution)/shard_map/ppermute | solution.py:110
  59.0 13.4 %collective-permute-start.6 = (bf16[64,2048]{1,0:T(8,128)(2,1)}, bf16[64,2048]{1,0:T(8,128)(2,1)S(1)}, u32[]{:S(2)}, u32[]{:S(2)}) collective-permute-start(bf16[64,2048]{1,0:T(8,128)(2,1)} %copy-done.2), channel_id=1, source_target_pairs={{0,8},{4,12},{8,0},{12,4},{1,9},{5,13},{9,1},{13,5},{2,10},{6,14},... | collective-permute-start | bytes 786440 | tf_op jit(solution)/shard_map/ppermute | solution.py:110
  62.1 10.3 %copy-start.3 = (bf16[64,2048]{1,0:T(8,128)(2,1)S(1)}, bf16[64,2048]{1,0:T(8,128)(2,1)}, u32[]{:S(2)}) copy-start(bf16[64,2048]{1,0:T(8,128)(2,1)} %copy-done.2) | copy-start | bytes 786436
  64.2 9.4 %collective-permute-start.12 = (bf16[1,128,512]{2,1,0:T(8,128)(2,1)S(1)}, bf16[1,128,512]{2,1,0:T(8,128)(2,1)S(1)}, u32[]{:S(2)}, u32[]{:S(2)}) collective-permute-start(bf16[1,128,512]{2,1,0:T(8,128)(2,1)S(1)} %get-tuple-element.58), channel_id=1, source_target_pairs={{0,1},{1,0},{2,3},{3,2},{4,5},{5,4},{6,7},{7,6},{8,9},{9,8},{10,11... | collective-permute-start | bytes 393224 | tf_op jit(solution)/shard_map/ppermute | solution.py:110
  68.0 8.8 %collective-permute-start.13 = (bf16[1,128,512]{2,1,0:T(8,128)(2,1)S(1)}, bf16[1,128,512]{2,1,0:T(8,128)(2,1)S(1)}, u32[]{:S(2)}, u32[]{:S(2)}) collective-permute-start(bf16[1,128,512]{2,1,0:T(8,128)(2,1)S(1)} %get-tuple-element.56), channel_id=1, source_target_pairs={{0,2},{1,3},{2,0},{3,1},{4,6},{5,7},{6,4},{7,5},{8,10},{9,11},{10,... | collective-permute-start | bytes 393224 | tf_op jit(solution)/shard_map/ppermute | solution.py:110
  76.9 7.8 %collective-permute-start.14 = (bf16[256,2048]{1,0:T(8,128)(2,1)S(1)}, bf16[256,2048]{1,0:T(8,128)(2,1)S(1)}, u32[]{:S(2)}, u32[]{:S(2)}) collective-permute-start(bf16[256,2048]{1,0:T(8,128)(2,1)S(1)} %pad_maximum_fusion), channel_id=1, source_target_pairs={{0,4},{4,0},{8,12},{12,8},{1,5},{5,1},{9,13},{13,9},{2,6},{6,2},{1... | collective-permute-start | bytes 3145736 | tf_op jit(solution)/shard_map/ppermute | solution.py:110
  76.9 7.8 %collective-permute-start.15 = (bf16[1,128,512]{2,1,0:T(8,128)(2,1)S(1)}, bf16[1,128,512]{2,1,0:T(8,128)(2,1)S(1)}, u32[]{:S(2)}, u32[]{:S(2)}) collective-permute-start(bf16[1,128,512]{2,1,0:T(8,128)(2,1)S(1)} %get-tuple-element.57), channel_id=1, source_target_pairs={{0,3},{1,2},{2,1},{3,0},{4,7},{5,6},{6,5},{7,4},{8,11},{9,10},{10,... | collective-permute-start | bytes 393224 | tf_op jit(solution)/shard_map/ppermute | solution.py:110
  85.5 6.3 %collective-permute-start.16 = (bf16[1,128,512]{2,1,0:T(8,128)(2,1)S(1)}, bf16[1,128,512]{2,1,0:T(8,128)(2,1)S(1)}, u32[]{:S(2)}, u32[]{:S(2)}) collective-permute-start(bf16[1,128,512]{2,1,0:T(8,128)(2,1)S(1)} %get-tuple-element.52), channel_id=1, source_target_pairs={{0,1},{1,0},{2,3},{3,2},{4,5},{5,4},{6,7},{7,6},{8,9},{9,8},{10,11... | collective-permute-start | bytes 393224 | tf_op jit(solution)/shard_map/ppermute | solution.py:110
  86.8 12.4 %collective-permute-start.17 = (bf16[1,128,512]{2,1,0:T(8,128)(2,1)S(1)}, bf16[1,128,512]{2,1,0:T(8,128)(2,1)S(1)}, u32[]{:S(2)}, u32[]{:S(2)}) collective-permute-start(bf16[1,128,512]{2,1,0:T(8,128)(2,1)S(1)} %get-tuple-element.53), channel_id=1, source_target_pairs={{0,2},{1,3},{2,0},{3,1},{4,6},{5,7},{6,4},{7,5},{8,10},{9,11},{10,... | collective-permute-start | bytes 393224 | tf_op jit(solution)/shard_map/ppermute | solution.py:110
  88.4 10.8 %collective-permute-start.18 = (bf16[1,128,512]{2,1,0:T(8,128)(2,1)S(1)}, bf16[1,128,512]{2,1,0:T(8,128)(2,1)S(1)}, u32[]{:S(2)}, u32[]{:S(2)}) collective-permute-start(bf16[1,128,512]{2,1,0:T(8,128)(2,1)S(1)} %get-tuple-element.54), channel_id=1, source_target_pairs={{0,3},{1,2},{2,1},{3,0},{4,7},{5,6},{6,5},{7,4},{8,11},{9,10},{10,... | collective-permute-start | bytes 393224 | tf_op jit(solution)/shard_map/ppermute | solution.py:110

commit v8 on v6

--- a/solution.py
+++ b/solution.py
@@ -110,6 +110,11 @@
     return lax.ppermute(value, axis, [(at, at ^ mask) for at in range(size)])
 
 
+def exchanged(blocks, slices):
+    moved = {mask: crossed(blocks[mask], "proj", slices, mask) for mask in reversed(range(1, slices))}
+    return [blocks[0]] + [moved[mask] for mask in range(1, slices)]
+
+
 def after(value, *tokens):
     return lax.optimization_barrier((value, tokens))[0]
 
@@ -157,25 +162,22 @@
     for first, part in zip(firsts, parts):
         each = part // slices
         raw = [lax.dynamic_slice_in_dim(source, first + (here ^ mask) * each, each, 0) for mask in range(slices)]
-        if pieces:
-            raw = after(raw, pieces[-1][1])
-        else:
-            raw, source = lax.optimization_barrier((raw, source))
-        pieces.append([raw[0]] + [crossed(raw[mask], "proj", slices, mask) for mask in range(1, slices)])
+        raw, source = lax.optimization_barrier((raw, source))
+        pieces.append(exchanged(raw, slices))
     for chunk in range(len(parts)):
+        pieces[chunk], train_flat = lax.optimization_barrier((pieces[chunk], train_flat))
         made = condition(pieces[chunk], basis, basis, in_basis, inverse)
-        rows.append([made[0]] + [crossed(made[mask], "proj", slices, mask) for mask in range(1, slices)])
+        rows.append(exchanged(made, slices))
+    came = []
     for chunk, part in enumerate(parts):
         near = spread_shares(jnp.concatenate(rows[chunk], axis=0), shares)
-        near = after(near, *blocks[-1:])
+        near = after(near, *came[2:3])
         far = crossed(near, "dp", shares, 1)
         values = products(near, far, train_flat, shares)
         values = [jnp.stack(values[at * owned:(at + 1) * owned]) for at in range(slices)]
-        blocks.append(turned(values, here ^ (share // owned)))
-    for part, block in zip(parts, blocks):
-        came = [block[0]] + [crossed(block[mask], "proj", slices, mask) for mask in range(1, slices)]
-        came = [value.reshape(owned, slices, part // slices, train_count) for value in came]
-        total = [sum(came[mask][:, at ^ mask].astype(jnp.float32) for mask in range(slices)) for at in range(slices)]
+        came = exchanged(turned(values, here ^ (share // owned)), slices)
+        sums = [value.reshape(owned, slices, part // slices, train_count) for value in came]
+        total = [sum(sums[mask][:, at ^ mask].astype(jnp.float32) for mask in range(slices)) for at in range(slices)]
         total = jnp.stack(turned(total, here), axis=1)
         total = jnp.stack(turned([total[at] for at in range(owned)], share % owned))
         results.append(total.reshape(owned, part, train_count))

time: 107 us -> 96.4 us (0.901)
  waiting for transfers between devices: 58.3 us -> 35.8 us
  starting transfers between devices: 32.1 us -> 41.2 us
  other arithmetic: 3.78 us -> 4.98 us
  local copies, waits for them, and re-layouts: 4.83 us -> 6.02 us
    ppermute x22, waiting for transfers between devices: 58.3 us -> 35.8 us  [crossed(): return lax.ppermute(value, axis, [(at, at ^ mask) for at in range(size)])]
    ppermute x22, starting transfers between devices: 32.1 us -> 41.2 us  [crossed(): return lax.ppermute(value, axis, [(at, at ^ mask) for at in range(size)])]
    concatenate x2, other arithmetic: 0.1 us -> 1.69 us  [three_wide(): return jnp.concatenate([high, low, high], axis=1)]
    convert_element_type x2, other arithmetic: 0.02 us -> 1.22 us  [basis_halves(): return (high.astype(jnp.bfloat16), (matrix - high).astype(jnp.bfloat16))]
  transfers between devices with their start and end apart: 22 -> 22, of which waited for: 10 -> 10; matrix products, arithmetic and copies ran while one was open for 7% -> 11% of each run, Pallas kernels for 4% -> 5%
where the time goes in v8:
time: 96.4 us; the launch traced here: 96 us
  starting transfers between devices  41.2 us (43%)
  waiting for transfers between devices  35.8 us (37%)
  local copies, waits for them, and re-layouts  6.02 us (6%)
  other arithmetic  4.98 us (5%)
  Pallas kernels  4.46 us (5%)
  matrix products  3.14 us (3%)
    ppermute x22, starting transfers between devices, crossed(): return lax.ppermute(value, axis, [(at, at ^ mask) for at in range(size)])  41.2 us
    ppermute x22, waiting for transfers between devices, crossed(): return lax.ppermute(value, axis, [(at, at ^ mask) for at in range(size)])  35.8 us
    pallas_call x2, Pallas kernels, condition_fast(): pl.pallas_call(functools.partial(condition_kernel, slices, rows_here), gr...  4.46 us
    dynamic_slice x2, local copies, waits for them, and re-layouts, body(): lax.dynamic_slice_in_dim(source, first + (here ^ mask) * each, each, 0)  3.77 us
    dot_general x4, matrix products, products(): lax.dot_general(block, train_flat, contract, preferred_element_type=jnp.f...  3.14 us
    unnamed x18, local copies, waits for them, and re-layouts  2.08 us
  transfers between devices with their start and end apart: 22, of which 10 were waited for; matrix products, arithmetic and copies ran while one was open for 11% of the time, Pallas kernels for 5%

profile of v8, /device:TPU:0, one launch (start us, length us, event | category | flops | bytes accessed | tf_op | source)
XLA Modules:
  0.0 96.0 jit_solution(4196683890930872677)
XLA Ops:
  0.0 1.9 %constant_dynamic-slice_fusion.4 = (bf16[32,16,128]{2,1,0:T(8,128)(2,1)S(1)}, bf16[32,16,128]{2,1,0:T(8,128)(2,1)S(1)}, bf16[32,16,128]{2,1,0:T(8,128)(2,1)}, bf16[32,16,128]{2,1,0:T(8,128)(2,1)S(1)}) fusion(bf16[256,16,128]{2,1,0:T(8,128)(2,1)} %param.5, s32[]{:T(128)S(6)} %select_n.355, s32[]{:T(128)S(6)} %select_n.354, s32[]{:T(128)S(6)} %select_n.353, ...), kind=kLoop, calls=%fused_computation.94 | loop fusion | bytes 1048592 | tf_op jit(solution)/shard_map/dynamic_slice | solution.py:164
  1.9 3.1 %collective-permute-start = (bf16[32,16,128]{2,1,0:T(8,128)(2,1)}, bf16[32,16,128]{2,1,0:T(8,128)(2,1)S(1)}, u32[]{:S(2)}, u32[]{:S(2)}) collective-permute-start(bf16[32,16,128]{2,1,0:T(8,128)(2,1)} %get-tuple-element.34), channel_id=1, source_target_pairs={{0,1},{1,0},{2,3},{3,2},{4,5},{5,4},{6,7},{7,6},{8,9},{9,8},{10,11... | collective-permute-start | bytes 393224 | tf_op jit(solution)/shard_map/ppermute | solution.py:110
  5.0 2.6 %collective-permute-start.1 = (bf16[32,16,128]{2,1,0:T(8,128)(2,1)S(1)}, bf16[32,16,128]{2,1,0:T(8,128)(2,1)S(1)}, u32[]{:S(2)}, u32[]{:S(2)}) collective-permute-start(bf16[32,16,128]{2,1,0:T(8,128)(2,1)S(1)} %get-tuple-element.35), channel_id=1, source_target_pairs={{0,2},{1,3},{2,0},{3,1},{4,6},{5,7},{6,4},{7,5},{8,10},{9,11},{10,... | collective-permute-start | bytes 393224 | tf_op jit(solution)/shard_map/ppermute | solution.py:110
  7.6 0.0 collective-permute-start.2
  7.6 1.8 %constant_dynamic-slice_fusion = (bf16[32,16,128]{2,1,0:T(8,128)(2,1)}, bf16[32,16,128]{2,1,0:T(8,128)(2,1)}, bf16[32,16,128]{2,1,0:T(8,128)(2,1)}, bf16[32,16,128]{2,1,0:T(8,128)(2,1)S(1)}) fusion(bf16[256,16,128]{2,1,0:T(8,128)(2,1)} %param.5, s32[]{:T(128)S(6)} %select_n.369, s32[]{:T(128)S(6)} %select_n.368, s32[]{:T(128)S(6)} %select_n.367, ...), kind=kLoop, calls=%fused_computation.90 | loop fusion | bytes 1048592 | tf_op jit(solution)/shard_map/dynamic_slice | solution.py:164
  9.4 3.8 %collective-permute-start.10 = (bf16[32,16,128]{2,1,0:T(8,128)(2,1)}, bf16[32,16,128]{2,1,0:T(8,128)(2,1)S(1)}, u32[]{:S(2)}, u32[]{:S(2)}) collective-permute-start(bf16[32,16,128]{2,1,0:T(8,128)(2,1)} %get-tuple-element.49), channel_id=1, source_target_pairs={{0,3},{1,2},{2,1},{3,0},{4,7},{5,6},{6,5},{7,4},{8,11},{9,10},{10,... | collective-permute-start | bytes 393224 | tf_op jit(solution)/shard_map/ppermute | solution.py:110
  13.3 0.0 collective-permute-start.8
  13.3 0.6 fusion.2
  13.9 0.6 fusion.3
  14.5 0.1 copy.6
  14.6 0.8 add_divide_fusion.refs_8_
  15.4 0.8 pad_maximum_fusion.6
  16.2 0.9 pad_maximum_fusion.8.refs_5_
  17.2 1.9 %copy.11 = bf16[64,8,16,128]{3,1,2,0:T(8,128)(2,1)} copy(bf16[64,8,16,128]{3,2,1,0:T(8,128)(2,1)S(1)} %bitcast.54) | data formatting | bytes 4194304
  19.1 0.1 copy.7.refs_4_
  19.2 0.0 collective-permute-done.refs_1_
  19.2 0.6 collective-permute-start.9
  19.8 1.0 collective-permute-done.1.refs_2_
  20.8 0.0 collective-permute-done.2.refs_3_
  20.8 2.2 %shard_map.55 = (bf16[32,2048]{1,0:T(8,128)(2,1)S(1)}, bf16[32,2048]{1,0:T(8,128)(2,1)S(1)}, bf16[32,2048]{1,0:T(8,128)(2,1)S(1)}, bf16[32,2048]{1,0:T(8,128)(2,1)S(1)}) custom-call(bf16[32,16,128]{2,1,0:T(8,128)(2,1)S(1)} %get-tuple-element.37.refs_0_, bf16[32,16,128]{2,1,0:T(8,128)(2,1)S(1)} %collective-permute-done.refs_1_, ...), custom_call_target="tpu_custom_call" | custom-call | tf_op jit(solution)/shard_map/pallas_call | solution.py:78
  23.0 5.1 %collective-permute-start.3 = (bf16[32,2048]{1,0:T(8,128)(2,1)S(1)}, bf16[32,2048]{1,0:T(8,128)(2,1)S(1)}, u32[]{:S(2)}, u32[]{:S(2)}) collective-permute-start(bf16[32,2048]{1,0:T(8,128)(2,1)S(1)} %get-tuple-element.42), channel_id=1, source_target_pairs={{0,1},{1,0},{2,3},{3,2},{4,5},{5,4},{6,7},{7,6},{8,9},{9,8},{10,11... | collective-permute-start | bytes 393224 | tf_op jit(solution)/shard_map/ppermute | solution.py:110
  28.2 2.0 %collective-permute-start.4 = (bf16[32,2048]{1,0:T(8,128)(2,1)S(1)}, bf16[32,2048]{1,0:T(8,128)(2,1)S(1)}, u32[]{:S(2)}, u32[]{:S(2)}) collective-permute-start(bf16[32,2048]{1,0:T(8,128)(2,1)S(1)} %get-tuple-element.43), channel_id=1, source_target_pairs={{0,2},{1,3},{2,0},{3,1},{4,6},{5,7},{6,4},{7,5},{8,10},{9,11},{10,... | collective-permute-start | bytes 393224 | tf_op jit(solution)/shard_map/ppermute | solution.py:110
  30.2 0.0 collective-permute-done.10.refs_3_
  30.2 1.5 %collective-permute-start.5 = (bf16[32,2048]{1,0:T(8,128)(2,1)S(1)}, bf16[32,2048]{1,0:T(8,128)(2,1)S(1)}, u32[]{:S(2)}, u32[]{:S(2)}) collective-permute-start(bf16[32,2048]{1,0:T(8,128)(2,1)S(1)} %get-tuple-element.44), channel_id=1, source_target_pairs={{0,3},{1,2},{2,1},{3,0},{4,7},{5,6},{6,5},{7,4},{8,11},{9,10},{10,... | collective-permute-start | bytes 393224 | tf_op jit(solution)/shard_map/ppermute | solution.py:110
  31.6 0.0 collective-permute-done.8.refs_1_
  31.6 6.1 %collective-permute-done.9.refs_2_ = bf16[32,16,128]{2,1,0:T(8,128)(2,1)S(1)} collective-permute-done((bf16[32,16,128]{2,1,0:T(8,128)(2,1)}, bf16[32,16,128]{2,1,0:T(8,128)(2,1)S(1)}, u32[]{:S(2)}, u32[]{:S(2)}) %collective-permute-start.9) | collective-permute-done | bytes 131104 | tf_op jit(solution)/shard_map/ppermute | solution.py:110
  37.8 2.2 %shard_map.56 = (bf16[32,2048]{1,0:T(8,128)(2,1)S(1)}, bf16[32,2048]{1,0:T(8,128)(2,1)S(1)}, bf16[32,2048]{1,0:T(8,128)(2,1)S(1)}, bf16[32,2048]{1,0:T(8,128)(2,1)S(1)}) custom-call(bf16[32,16,128]{2,1,0:T(8,128)(2,1)S(1)} %get-tuple-element.52.refs_0_, bf16[32,16,128]{2,1,0:T(8,128)(2,1)S(1)} %collective-permute-done.8.refs_1_, ...), custom_call_target="tpu_custom_call" | custom-call | tf_op jit(solution)/shard_map/pallas_call | solution.py:78
  40.0 0.1 collective-permute-start.14
  40.1 2.8 %collective-permute-start.15 = (bf16[32,2048]{1,0:T(8,128)(2,1)S(1)}, bf16[32,2048]{1,0:T(8,128)(2,1)S(1)}, u32[]{:S(2)}, u32[]{:S(2)}) collective-permute-start(bf16[32,2048]{1,0:T(8,128)(2,1)S(1)} %get-tuple-element.58), channel_id=1, source_target_pairs={{0,2},{1,3},{2,0},{3,1},{4,6},{5,7},{6,4},{7,5},{8,10},{9,11},{10,... | collective-permute-start | bytes 393224 | tf_op jit(solution)/shard_map/ppermute | solution.py:110
  42.9 0.0 collective-permute-done.3
  42.9 1.7 %collective-permute-start.16 = (bf16[32,2048]{1,0:T(8,128)(2,1)S(1)}, bf16[32,2048]{1,0:T(8,128)(2,1)S(1)}, u32[]{:S(2)}, u32[]{:S(2)}) collective-permute-start(bf16[32,2048]{1,0:T(8,128)(2,1)S(1)} %get-tuple-element.59), channel_id=1, source_target_pairs={{0,3},{1,2},{2,1},{3,0},{4,7},{5,6},{6,5},{7,4},{8,11},{9,10},{10,... | collective-permute-start | bytes 393224 | tf_op jit(solution)/shard_map/ppermute | solution.py:110
  44.6 0.0 collective-permute-done.4
  44.6 0.0 collective-permute-done.5
  44.6 1.5 %collective-permute-start.6 = (bf16[128,2048]{1,0:T(8,128)(2,1)S(1)}, bf16[128,2048]{1,0:T(8,128)(2,1)S(1)}, u32[]{:S(2)}, u32[]{:S(2)}) collective-permute-start(bf16[128,2048]{1,0:T(8,128)(2,1)S(1)} %pad_maximum_fusion), channel_id=1, source_target_pairs={{0,8},{4,12},{8,0},{12,4},{1,9},{5,13},{9,1},{13,5},{2,10},{6,14},... | collective-permute-start | bytes 1572872 | tf_op jit(solution)/shard_map/ppermute | solution.py:110
  46.2 7.6 %collective-permute-done.6 = bf16[128,2048]{1,0:T(8,128)(2,1)S(1)} collective-permute-done((bf16[128,2048]{1,0:T(8,128)(2,1)S(1)}, bf16[128,2048]{1,0:T(8,128)(2,1)S(1)}, u32[]{:S(2)}, u32[]{:S(2)}) %collective-permute-start.6) | collective-permute-done | bytes 524320 | tf_op jit(solution)/shard_map/ppermute | solution.py:110
  53.9 0.1 collective-permute-start.7
  54.0 0.0 collective-permute-done.14
  54.0 0.0 collective-permute-done.15
  54.0 0.0 collective-permute-done.16
  54.1 1.5 %collective-permute-start.17 = (bf16[128,2048]{1,0:T(8,128)(2,1)S(1)}, bf16[128,2048]{1,0:T(8,128)(2,1)S(1)}, u32[]{:S(2)}, u32[]{:S(2)}) collective-permute-start(bf16[128,2048]{1,0:T(8,128)(2,1)S(1)} %pad_maximum_fusion.1), channel_id=1, source_target_pairs={{0,8},{4,12},{8,0},{12,4},{1,9},{5,13},{9,1},{13,5},{2,10},{6,14},... | collective-permute-start | bytes 1572872 | tf_op jit(solution)/shard_map/ppermute | solution.py:110
  55.7 0.9 convolution_convert_fusion.2
  56.6 0.1 collective-permute-done.7
  56.6 0.7 convolution_convert_fusion.3
  57.4 0.1 broadcast_select_fusion.9
  57.5 5.3 %collective-permute-start.12 = (bf16[1,128,512]{2,1,0:T(8,128)(2,1)S(1)}, bf16[1,128,512]{2,1,0:T(8,128)(2,1)S(1)}, u32[]{:S(2)}, u32[]{:S(2)}) collective-permute-start(bf16[1,128,512]{2,1,0:T(8,128)(2,1)S(1)} %get-tuple-element.81), channel_id=1, source_target_pairs={{0,2},{1,3},{2,0},{3,1},{4,6},{5,7},{6,4},{7,5},{8,10},{9,11},{10,... | collective-permute-start | bytes 393224 | tf_op jit(solution)/shard_map/ppermute | solution.py:110
  62.8 5.7 %collective-permute-done.17 = bf16[128,2048]{1,0:T(8,128)(2,1)S(1)} collective-permute-done((bf16[128,2048]{1,0:T(8,128)(2,1)S(1)}, bf16[128,2048]{1,0:T(8,128)(2,1)S(1)}, u32[]{:S(2)}, u32[]{:S(2)}) %collective-permute-start.17) | collective-permute-done | bytes 524320 | tf_op jit(solution)/shard_map/ppermute | solution.py:110
  68.5 0.9 collective-permute-done.12
  69.4 0.0 collective-permute-start.18
  69.4 1.5 %collective-permute-start.13 = (bf16[1,128,512]{2,1,0:T(8,128)(2,1)S(1)}, bf16[1,128,512]{2,1,0:T(8,128)(2,1)S(1)}, u32[]{:S(2)}, u32[]{:S(2)}) collective-permute-start(bf16[1,128,512]{2,1,0:T(8,128)(2,1)S(1)} %get-tuple-element.82), channel_id=1, source_target_pairs={{0,3},{1,2},{2,1},{3,0},{4,7},{5,6},{6,5},{7,4},{8,11},{9,10},{10,... | collective-permute-start | bytes 393224 | tf_op jit(solution)/shard_map/ppermute | solution.py:110
  70.9 3.6 %collective-permute-start.11 = (bf16[1,128,512]{2,1,0:T(8,128)(2,1)S(1)}, bf16[1,128,512]{2,1,0:T(8,128)(2,1)S(1)}, u32[]{:S(2)}, u32[]{:S(2)}) collective-permute-start(bf16[1,128,512]{2,1,0:T(8,128)(2,1)S(1)} %get-tuple-element.80), channel_id=1, source_target_pairs={{0,1},{1,0},{2,3},{3,2},{4,5},{5,4},{6,7},{7,6},{8,9},{9,8},{10,11... | collective-permute-start | bytes 393224 | tf_op jit(solution)/shard_map/ppermute | solution.py:110
  74.5 3.0 %collective-permute-done.13 = bf16[1,128,512]{2,1,0:T(8,128)(2,1)S(1)} collective-permute-done((bf16[1,128,512]{2,1,0:T(8,128)(2,1)S(1)}, bf16[1,128,512]{2,1,0:T(8,128)(2,1)S(1)}, u32[]{:S(2)}, u32[]{:S(2)}) %collective-permute-start.13) | collective-permute-done | bytes 131104 | tf_op jit(solution)/shard_map/ppermute | solution.py:110
  77.5 2.4 %collective-permute-done.11 = bf16[1,128,512]{2,1,0:T(8,128)(2,1)S(1)} collective-permute-done((bf16[1,128,512]{2,1,0:T(8,128)(2,1)S(1)}, bf16[1,128,512]{2,1,0:T(8,128)(2,1)S(1)}, u32[]{:S(2)}, u32[]{:S(2)}) %collective-permute-start.11) | collective-permute-done | bytes 131104 | tf_op jit(solution)/shard_map/ppermute | solution.py:110
  79.9 0.1 broadcast_select_fusion.25
  80.0 0.7 convolution_convert_fusion
  80.8 0.8 convolution_convert_fusion.1
  81.5 0.1 broadcast_select_fusion.8
  81.6 0.6 collective-permute-start.19
  82.2 1.4 %collective-permute-start.20 = (bf16[1,128,512]{2,1,0:T(8,128)(2,1)S(1)}, bf16[1,128,512]{2,1,0:T(8,128)(2,1)S(1)}, u32[]{:S(2)}, u32[]{:S(2)}) collective-permute-start(bf16[1,128,512]{2,1,0:T(8,128)(2,1)S(1)} %get-tuple-element.85), channel_id=1, source_target_pairs={{0,2},{1,3},{2,0},{3,1},{4,6},{5,7},{6,4},{7,5},{8,10},{9,11},{10,... | collective-permute-start | bytes 393224 | tf_op jit(solution)/shard_map/ppermute | solution.py:110
  83.6 2.5 %collective-permute-start.21 = (bf16[1,128,512]{2,1,0:T(8,128)(2,1)S(1)}, bf16[1,128,512]{2,1,0:T(8,128)(2,1)S(1)}, u32[]{:S(2)}, u32[]{:S(2)}) collective-permute-start(bf16[1,128,512]{2,1,0:T(8,128)(2,1)S(1)} %get-tuple-element.86), channel_id=1, source_target_pairs={{0,3},{1,2},{2,1},{3,0},{4,7},{5,6},{6,5},{7,4},{8,11},{9,10},{10,... | collective-permute-start | bytes 393224 | tf_op jit(solution)/shard_map/ppermute | solution.py:110
  86.1 2.6 %collective-permute-done.19 = bf16[1,128,512]{2,1,0:T(8,128)(2,1)S(1)} collective-permute-done((bf16[1,128,512]{2,1,0:T(8,128)(2,1)S(1)}, bf16[1,128,512]{2,1,0:T(8,128)(2,1)S(1)}, u32[]{:S(2)}, u32[]{:S(2)}) %collective-permute-start.19) | collective-permute-done | bytes 131104 | tf_op jit(solution)/shard_map/ppermute | solution.py:110
  88.7 6.3 %collective-permute-done.20 = bf16[1,128,512]{2,1,0:T(8,128)(2,1)S(1)} collective-permute-done((bf16[1,128,512]{2,1,0:T(8,128)(2,1)S(1)}, bf16[1,128,512]{2,1,0:T(8,128)(2,1)S(1)}, u32[]{:S(2)}, u32[]{:S(2)}) %collective-permute-start.20) | collective-permute-done | bytes 131104 | tf_op jit(solution)/shard_map/ppermute | solution.py:110
  95.0 0.0 collective-permute-done.21
  95.0 0.1 broadcast_select_fusion.21
  95.1 0.8 maximum_bitcast_fusion
  (29 shorter events, 0.4 us)
Async XLA Ops:
  0.0 13.3 %copy-start.3 = (f32[64,64]{1,0:T(8,128)S(1)}, f32[64,64]{1,0:T(8,128)}, u32[]{:S(2)}) copy-start(f32[64,64]{1,0:T(8,128)} %param.7) | copy-start | bytes 49156
  0.0 14.5 %copy-start.2 = (f32[128,128]{1,0:T(8,128)S(1)}, f32[128,128]{1,0:T(8,128)}, u32[]{:S(2)}) copy-start(f32[128,128]{1,0:T(8,128)} %param.8) | copy-start | bytes 196612
  0.0 17.2 %copy-start = (bf16[512,16,128]{2,1,0:T(8,128)(2,1)S(1)}, bf16[512,16,128]{2,1,0:T(8,128)(2,1)}, u32[]{:S(2)}) copy-start(bf16[512,16,128]{2,1,0:T(8,128)(2,1)} %param.6) | copy-start | bytes 6291460
  1.9 17.3 %collective-permute-start = (bf16[32,16,128]{2,1,0:T(8,128)(2,1)}, bf16[32,16,128]{2,1,0:T(8,128)(2,1)S(1)}, u32[]{:S(2)}, u32[]{:S(2)}) collective-permute-start(bf16[32,16,128]{2,1,0:T(8,128)(2,1)} %get-tuple-element.34), channel_id=1, source_target_pairs={{0,1},{1,0},{2,3},{3,2},{4,5},{5,4},{6,7},{7,6},{8,9},{9,8},{10,11... | collective-permute-start | bytes 393224 | tf_op jit(solution)/shard_map/ppermute | solution.py:110
  5.0 15.8 %collective-permute-start.1 = (bf16[32,16,128]{2,1,0:T(8,128)(2,1)S(1)}, bf16[32,16,128]{2,1,0:T(8,128)(2,1)S(1)}, u32[]{:S(2)}, u32[]{:S(2)}) collective-permute-start(bf16[32,16,128]{2,1,0:T(8,128)(2,1)S(1)} %get-tuple-element.35), channel_id=1, source_target_pairs={{0,2},{1,3},{2,0},{3,1},{4,6},{5,7},{6,4},{7,5},{8,10},{9,11},{10,... | collective-permute-start | bytes 393224 | tf_op jit(solution)/shard_map/ppermute | solution.py:110
  7.6 13.2 %collective-permute-start.2 = (bf16[32,16,128]{2,1,0:T(8,128)(2,1)S(1)}, bf16[32,16,128]{2,1,0:T(8,128)(2,1)S(1)}, u32[]{:S(2)}, u32[]{:S(2)}) collective-permute-start(bf16[32,16,128]{2,1,0:T(8,128)(2,1)S(1)} %get-tuple-element.36), channel_id=1, source_target_pairs={{0,3},{1,2},{2,1},{3,0},{4,7},{5,6},{6,5},{7,4},{8,11},{9,10},{10,... | collective-permute-start | bytes 393224 | tf_op jit(solution)/shard_map/ppermute | solution.py:110
  9.4 20.7 %collective-permute-start.10 = (bf16[32,16,128]{2,1,0:T(8,128)(2,1)}, bf16[32,16,128]{2,1,0:T(8,128)(2,1)S(1)}, u32[]{:S(2)}, u32[]{:S(2)}) collective-permute-start(bf16[32,16,128]{2,1,0:T(8,128)(2,1)} %get-tuple-element.49), channel_id=1, source_target_pairs={{0,3},{1,2},{2,1},{3,0},{4,7},{5,6},{6,5},{7,4},{8,11},{9,10},{10,... | collective-permute-start | bytes 393224 | tf_op jit(solution)/shard_map/ppermute | solution.py:110
  13.3 18.4 %collective-permute-start.8 = (bf16[32,16,128]{2,1,0:T(8,128)(2,1)}, bf16[32,16,128]{2,1,0:T(8,128)(2,1)S(1)}, u32[]{:S(2)}, u32[]{:S(2)}) collective-permute-start(bf16[32,16,128]{2,1,0:T(8,128)(2,1)} %get-tuple-element.47), channel_id=1, source_target_pairs={{0,1},{1,0},{2,3},{3,2},{4,5},{5,4},{6,7},{7,6},{8,9},{9,8},{10,11... | collective-permute-start | bytes 393224 | tf_op jit(solution)/shard_map/ppermute | solution.py:110
  19.2 18.6 %collective-permute-start.9 = (bf16[32,16,128]{2,1,0:T(8,128)(2,1)}, bf16[32,16,128]{2,1,0:T(8,128)(2,1)S(1)}, u32[]{:S(2)}, u32[]{:S(2)}) collective-permute-start(bf16[32,16,128]{2,1,0:T(8,128)(2,1)} %get-tuple-element.48), channel_id=1, source_target_pairs={{0,2},{1,3},{2,0},{3,1},{4,6},{5,7},{6,4},{7,5},{8,10},{9,11},{10,... | collective-permute-start | bytes 393224 | tf_op jit(solution)/shard_map/ppermute | solution.py:110
  23.0 19.8 %collective-permute-start.3 = (bf16[32,2048]{1,0:T(8,128)(2,1)S(1)}, bf16[32,2048]{1,0:T(8,128)(2,1)S(1)}, u32[]{:S(2)}, u32[]{:S(2)}) collective-permute-start(bf16[32,2048]{1,0:T(8,128)(2,1)S(1)} %get-tuple-element.42), channel_id=1, source_target_pairs={{0,1},{1,0},{2,3},{3,2},{4,5},{5,4},{6,7},{7,6},{8,9},{9,8},{10,11... | collective-permute-start | bytes 393224 | tf_op jit(solution)/shard_map/ppermute | solution.py:110
  28.2 16.4 %collective-permute-start.4 = (bf16[32,2048]{1,0:T(8,128)(2,1)S(1)}, bf16[32,2048]{1,0:T(8,128)(2,1)S(1)}, u32[]{:S(2)}, u32[]{:S(2)}) collective-permute-start(bf16[32,2048]{1,0:T(8,128)(2,1)S(1)} %get-tuple-element.43), channel_id=1, source_target_pairs={{0,2},{1,3},{2,0},{3,1},{4,6},{5,7},{6,4},{7,5},{8,10},{9,11},{10,... | collective-permute-start | bytes 393224 | tf_op jit(solution)/shard_map/ppermute | solution.py:110
  30.2 14.4 %collective-permute-start.5 = (bf16[32,2048]{1,0:T(8,128)(2,1)S(1)}, bf16[32,2048]{1,0:T(8,128)(2,1)S(1)}, u32[]{:S(2)}, u32[]{:S(2)}) collective-permute-start(bf16[32,2048]{1,0:T(8,128)(2,1)S(1)} %get-tuple-element.44), channel_id=1, source_target_pairs={{0,3},{1,2},{2,1},{3,0},{4,7},{5,6},{6,5},{7,4},{8,11},{9,10},{10,... | collective-permute-start | bytes 393224 | tf_op jit(solution)/shard_map/ppermute | solution.py:110
  40.0 14.0 %collective-permute-start.14 = (bf16[32,2048]{1,0:T(8,128)(2,1)S(1)}, bf16[32,2048]{1,0:T(8,128)(2,1)S(1)}, u32[]{:S(2)}, u32[]{:S(2)}) collective-permute-start(bf16[32,2048]{1,0:T(8,128)(2,1)S(1)} %get-tuple-element.57), channel_id=1, source_target_pairs={{0,1},{1,0},{2,3},{3,2},{4,5},{5,4},{6,7},{7,6},{8,9},{9,8},{10,11... | collective-permute-start | bytes 393224 | tf_op jit(solution)/shard_map/ppermute | solution.py:110
  40.1 13.9 %collective-permute-start.15 = (bf16[32,2048]{1,0:T(8,128)(2,1)S(1)}, bf16[32,2048]{1,0:T(8,128)(2,1)S(1)}, u32[]{:S(2)}, u32[]{:S(2)}) collective-permute-start(bf16[32,2048]{1,0:T(8,128)(2,1)S(1)} %get-tuple-element.58), channel_id=1, source_target_pairs={{0,2},{1,3},{2,0},{3,1},{4,6},{5,7},{6,4},{7,5},{8,10},{9,11},{10,... | collective-permute-start | bytes 393224 | tf_op jit(solution)/shard_map/ppermute | solution.py:110
  42.9 11.1 %collective-permute-start.16 = (bf16[32,2048]{1,0:T(8,128)(2,1)S(1)}, bf16[32,2048]{1,0:T(8,128)(2,1)S(1)}, u32[]{:S(2)}, u32[]{:S(2)}) collective-permute-start(bf16[32,2048]{1,0:T(8,128)(2,1)S(1)} %get-tuple-element.59), channel_id=1, source_target_pairs={{0,3},{1,2},{2,1},{3,0},{4,7},{5,6},{6,5},{7,4},{8,11},{9,10},{10,... | collective-permute-start | bytes 393224 | tf_op jit(solution)/shard_map/ppermute | solution.py:110
  44.6 11.1 %copy-start.1 = (bf16[64,8,16,128]{3,1,2,0:T(8,128)(2,1)S(1)}, bf16[64,8,16,128]{3,1,2,0:T(8,128)(2,1)}, u32[]{:S(2)}) copy-start(bf16[64,8,16,128]{3,1,2,0:T(8,128)(2,1)} %copy.11) | copy-start | bytes 6291460
  44.6 9.2 %collective-permute-start.6 = (bf16[128,2048]{1,0:T(8,128)(2,1)S(1)}, bf16[128,2048]{1,0:T(8,128)(2,1)S(1)}, u32[]{:S(2)}, u32[]{:S(2)}) collective-permute-start(bf16[128,2048]{1,0:T(8,128)(2,1)S(1)} %pad_maximum_fusion), channel_id=1, source_target_pairs={{0,8},{4,12},{8,0},{12,4},{1,9},{5,13},{9,1},{13,5},{2,10},{6,14},... | collective-permute-start | bytes 1572872 | tf_op jit(solution)/shard_map/ppermute | solution.py:110
  53.9 2.7 %collective-permute-start.7 = (bf16[256,2048]{1,0:T(8,128)(2,1)S(1)}, bf16[256,2048]{1,0:T(8,128)(2,1)S(1)}, u32[]{:S(2)}, u32[]{:S(2)}) collective-permute-start(bf16[256,2048]{1,0:T(8,128)(2,1)S(1)} %constant_dynamic-update-slice_fusion), channel_id=1, source_target_pairs={{0,4},{4,0},{8,12},{12,8},{1,5},{5,1},{9,13},{13,9},{2,6},{6,2},{1... | collective-permute-start | bytes 3145736 | tf_op jit(solution)/shard_map/ppermute | solution.py:110
  54.1 14.4 %collective-permute-start.17 = (bf16[128,2048]{1,0:T(8,128)(2,1)S(1)}, bf16[128,2048]{1,0:T(8,128)(2,1)S(1)}, u32[]{:S(2)}, u32[]{:S(2)}) collective-permute-start(bf16[128,2048]{1,0:T(8,128)(2,1)S(1)} %pad_maximum_fusion.1), channel_id=1, source_target_pairs={{0,8},{4,12},{8,0},{12,4},{1,9},{5,13},{9,1},{13,5},{2,10},{6,14},... | collective-permute-start | bytes 1572872 | tf_op jit(solution)/shard_map/ppermute | solution.py:110
  57.5 11.9 %collective-permute-start.12 = (bf16[1,128,512]{2,1,0:T(8,128)(2,1)S(1)}, bf16[1,128,512]{2,1,0:T(8,128)(2,1)S(1)}, u32[]{:S(2)}, u32[]{:S(2)}) collective-permute-start(bf16[1,128,512]{2,1,0:T(8,128)(2,1)S(1)} %get-tuple-element.81), channel_id=1, source_target_pairs={{0,2},{1,3},{2,0},{3,1},{4,6},{5,7},{6,4},{7,5},{8,10},{9,11},{10,... | collective-permute-start | bytes 393224 | tf_op jit(solution)/shard_map/ppermute | solution.py:110
  69.4 11.4 %collective-permute-start.18 = (bf16[256,2048]{1,0:T(8,128)(2,1)S(1)}, bf16[256,2048]{1,0:T(8,128)(2,1)S(1)}, u32[]{:S(2)}, u32[]{:S(2)}) collective-permute-start(bf16[256,2048]{1,0:T(8,128)(2,1)S(1)} %constant_dynamic-update-slice_fusion.5), channel_id=1, source_target_pairs={{0,4},{4,0},{8,12},{12,8},{1,5},{5,1},{9,13},{13,9},{2,6},{6,2},{1... | collective-permute-start | bytes 3145736 | tf_op jit(solution)/shard_map/ppermute | solution.py:110
  69.4 8.1 %collective-permute-start.13 = (bf16[1,128,512]{2,1,0:T(8,128)(2,1)S(1)}, bf16[1,128,512]{2,1,0:T(8,128)(2,1)S(1)}, u32[]{:S(2)}, u32[]{:S(2)}) collective-permute-start(bf16[1,128,512]{2,1,0:T(8,128)(2,1)S(1)} %get-tuple-element.82), channel_id=1, source_target_pairs={{0,3},{1,2},{2,1},{3,0},{4,7},{5,6},{6,5},{7,4},{8,11},{9,10},{10,... | collective-permute-start | bytes 393224 | tf_op jit(solution)/shard_map/ppermute | solution.py:110
  70.9 9.1 %collective-permute-start.11 = (bf16[1,128,512]{2,1,0:T(8,128)(2,1)S(1)}, bf16[1,128,512]{2,1,0:T(8,128)(2,1)S(1)}, u32[]{:S(2)}, u32[]{:S(2)}) collective-permute-start(bf16[1,128,512]{2,1,0:T(8,128)(2,1)S(1)} %get-tuple-element.80), channel_id=1, source_target_pairs={{0,1},{1,0},{2,3},{3,2},{4,5},{5,4},{6,7},{7,6},{8,9},{9,8},{10,11... | collective-permute-start | bytes 393224 | tf_op jit(solution)/shard_map/ppermute | solution.py:110
  81.6 7.1 %collective-permute-start.19 = (bf16[1,128,512]{2,1,0:T(8,128)(2,1)S(1)}, bf16[1,128,512]{2,1,0:T(8,128)(2,1)S(1)}, u32[]{:S(2)}, u32[]{:S(2)}) collective-permute-start(bf16[1,128,512]{2,1,0:T(8,128)(2,1)S(1)} %get-tuple-element.84), channel_id=1, source_target_pairs={{0,1},{1,0},{2,3},{3,2},{4,5},{5,4},{6,7},{7,6},{8,9},{9,8},{10,11... | collective-permute-start | bytes 393224 | tf_op jit(solution)/shard_map/ppermute | solution.py:110
  82.2 12.8 %collective-permute-start.20 = (bf16[1,128,512]{2,1,0:T(8,128)(2,1)S(1)}, bf16[1,128,512]{2,1,0:T(8,128)(2,1)S(1)}, u32[]{:S(2)}, u32[]{:S(2)}) collective-permute-start(bf16[1,128,512]{2,1,0:T(8,128)(2,1)S(1)} %get-tuple-element.85), channel_id=1, source_target_pairs={{0,2},{1,3},{2,0},{3,1},{4,6},{5,7},{6,4},{7,5},{8,10},{9,11},{10,... | collective-permute-start | bytes 393224 | tf_op jit(solution)/shard_map/ppermute | solution.py:110
  83.6 11.4 %collective-permute-start.21 = (bf16[1,128,512]{2,1,0:T(8,128)(2,1)S(1)}, bf16[1,128,512]{2,1,0:T(8,128)(2,1)S(1)}, u32[]{:S(2)}, u32[]{:S(2)}) collective-permute-start(bf16[1,128,512]{2,1,0:T(8,128)(2,1)S(1)} %get-tuple-element.86), channel_id=1, source_target_pairs={{0,3},{1,2},{2,1},{3,0},{4,7},{5,6},{6,5},{7,4},{8,11},{9,10},{10,... | collective-permute-start | bytes 393224 | tf_op jit(solution)/shard_map/ppermute | solution.py:110

commit v9 on v8

--- a/solution.py
+++ b/solution.py
@@ -16,17 +16,12 @@
     return high, (value - high.astype(jnp.float32)).astype(jnp.bfloat16)
 
 
-def basis_halves(matrix):
-    high = lax.reduce_precision(matrix, 8, 7)
-    return high.astype(jnp.bfloat16), (matrix - high).astype(jnp.bfloat16)
-
-
 def times(left, right):
     return jnp.dot(left, right, preferred_element_type=jnp.float32)
 
 
 def three_wide(matrix):
-    high, low = basis_halves(matrix)
+    high, low = halves(matrix)
     return jnp.concatenate([high, low, high], axis=1)
 
 
@@ -37,15 +32,17 @@
 
 def condition_kernel(slices, rows_here, *refs):
     pieces = refs[:slices]
-    enter, leave, right, back, inverse = refs[slices:slices + 5]
+    basis, across, right_basis, right_across, corrections = refs[slices:slices + 5]
     outs, stage = refs[slices + 5:-1], refs[-1]
+    enter, leave = three_wide(across[...]), three_wide(basis[...])
+    right, back = halves(right_basis[...]), halves(right_across[...])
     count, _, columns = pieces[0].shape
     out_rows = slices * rows_here
     parts = []
     for piece in pieces:
         flat = piece[...].reshape(count * rows_here, columns)
         parts.append(halves(times(flat, right[0]) + times(flat, right[1])))
-    scale = jnp.concatenate([inverse[...]] * 2, axis=1)
+    scale = jnp.concatenate([1.0 / (corrections[...] + damping_term)] * 2, axis=1)
 
     def gathered(at, which):
         rows = slice(at * rows_here, (at + 1) * rows_here)
@@ -54,8 +51,8 @@
     for at in range(0, count, 2):
         high = jnp.concatenate([gathered(at, 0), gathered(at + 1, 0)], axis=1)
         low = jnp.concatenate([gathered(at, 1), gathered(at + 1, 1)], axis=1)
-        rotated = times(enter[...], jnp.concatenate([high, high, low], axis=0))
-        result = times(leave[...], three_deep(rotated * scale))
+        rotated = times(enter, jnp.concatenate([high, high, low], axis=0))
+        result = times(leave, three_deep(rotated * scale))
         stage[at * out_rows:(at + 1) * out_rows, :] = result[:, :columns]
         stage[(at + 1) * out_rows:(at + 2) * out_rows, :] = result[:, columns:]
     high, low = halves(stage[...])
@@ -66,7 +63,7 @@
         outs[row // rows_here][:, at:at + columns] = value
 
 
-def condition_fast(pieces, enter, leave, in_basis, inverse):
+def condition_fast(pieces, basis, in_basis, corrections):
     slices = len(pieces)
     count, rows_here, columns = pieces[0].shape
     block = min(BLOCK, count)
@@ -74,7 +71,7 @@
     piece_spec = pl.BlockSpec((block, rows_here, columns), lambda step: (step, 0, 0))
     out_spec = pl.BlockSpec((block, width), lambda step: (step, 0))
     whole = pl.BlockSpec(memory_space=pltpu.VMEM)
-    order = enter.shape[0]
+    order = basis.shape[0]
     return pl.pallas_call(
         functools.partial(condition_kernel, slices, rows_here),
         grid=(count // block,),
@@ -84,25 +81,18 @@
         scratch_shapes=[pltpu.VMEM((block * order, columns), jnp.float32)],
         compiler_params=pltpu.CompilerParams(vmem_limit_bytes=32 * 1024 * 1024),
         cost_estimate=pl.CostEstimate(flops=0, bytes_accessed=0, transcendentals=0),
-    )(
-        *pieces,
-        three_wide(enter.T),
-        three_wide(leave),
-        jnp.stack(basis_halves(in_basis)),
-        jnp.stack(basis_halves(in_basis.T)),
-        inverse,
-    )
+    )(*pieces, basis, basis.T, in_basis, in_basis.T, corrections)
 
 
-def condition_plain(pieces, enter, leave, in_basis, inverse):
+def condition_plain(pieces, basis, in_basis, corrections):
     high = lax.Precision.HIGH
     count, rows_here, columns = pieces[0].shape
     values = jnp.concatenate(pieces, axis=1).astype(jnp.float32)
     inner = jnp.einsum("qbc,cd->qbd", values, in_basis, precision=high)
-    rotated = jnp.einsum("ba,qbd->qad", enter, inner, precision=high)
-    left = jnp.einsum("ba,qad->qbd", leave, rotated * inverse, precision=high)
+    rotated = jnp.einsum("ba,qbd->qad", basis, inner, precision=high)
+    left = jnp.einsum("ba,qad->qbd", basis, rotated / (corrections + damping_term), precision=high)
     result = jnp.einsum("qbd,ed->qbe", left, in_basis, precision=high).astype(jnp.bfloat16)
-    starts = range(0, enter.shape[0], rows_here)
+    starts = range(0, basis.shape[0], rows_here)
     return [result[:, at:at + rows_here].reshape(count, rows_here * columns) for at in starts]
 
 
@@ -153,30 +143,37 @@
     train_flat = lax.optimization_barrier(train_grads.reshape(train_count, width))
     row_blocks = out_basis.reshape(slices, rows_here, -1)
     basis = jnp.concatenate(turned([row_blocks[at] for at in range(slices)], here), axis=0)
-    inverse = 1.0 / (corrections + damping_term)
     condition = condition_fast if rows_here % 16 == 0 else condition_plain
     parts = [count * size // sum(CHUNKS) for size in CHUNKS]
-    firsts = [sum(parts[:chunk]) for chunk in range(len(parts))]
-    pieces, rows, blocks, results = [], [], [], []
+    pieces, rows, results = [], [], []
     source = queries
-    for first, part in zip(firsts, parts):
-        each = part // slices
-        raw = [lax.dynamic_slice_in_dim(source, first + (here ^ mask) * each, each, 0) for mask in range(slices)]
-        raw, source = lax.optimization_barrier((raw, source))
+    for chunk, part in enumerate(parts):
+        first, each = sum(parts[:chunk]), part // slices
+        raw = []
+        for mask in range(slices):
+            block = lax.dynamic_slice_in_dim(source, first + (here ^ mask) * each, each, 0)
+            block, source = lax.optimization_barrier((block, source))
+            raw.append(block)
         pieces.append(exchanged(raw, slices))
     for chunk in range(len(parts)):
-        pieces[chunk], train_flat = lax.optimization_barrier((pieces[chunk], train_flat))
-        made = condition(pieces[chunk], basis, basis, in_basis, inverse)
+        if chunk:
+            pieces[chunk], train_flat = lax.optimization_barrier((pieces[chunk], train_flat))
+        made = condition(pieces[chunk], basis, in_basis, corrections)
         rows.append(exchanged(made, slices))
     came = []
+    half = slices // 2
     for chunk, part in enumerate(parts):
-        near = spread_shares(jnp.concatenate(rows[chunk], axis=0), shares)
-        near = after(near, *came[2:3])
-        far = crossed(near, "dp", shares, 1)
-        values = products(near, far, train_flat, shares)
+        each = part // slices
+        groups = []
+        for group in (rows[chunk][:half], rows[chunk][half:]):
+            near = spread_shares(jnp.concatenate(group, axis=0), shares)
+            near = after(near, *came[2:3])
+            far = crossed(near, "dp", shares, 1)
+            groups.append(products(near, far, train_flat, shares))
+        values = [jnp.concatenate(pair, axis=0) for pair in zip(*groups)]
         values = [jnp.stack(values[at * owned:(at + 1) * owned]) for at in range(slices)]
         came = exchanged(turned(values, here ^ (share // owned)), slices)
-        sums = [value.reshape(owned, slices, part // slices, train_count) for value in came]
+        sums = [value.reshape(owned, slices, each, train_count) for value in came]
         total = [sum(sums[mask][:, at ^ mask].astype(jnp.float32) for mask in range(slices)) for at in range(slices)]
         total = jnp.stack(turned(total, here), axis=1)
         total = jnp.stack(turned([total[at] for at in range(owned)], share % owned))

time: 96.4 us -> 93.5 us (0.970)
  matrix products: 3.14 us -> 6.66 us
  other arithmetic: 4.98 us -> 1.81 us
  starting transfers between devices: 41.2 us -> 38.3 us
    dynamic_slice x2 -> x8, local copies, waits for them, and re-layouts: 3.77 us -> 0.11 us  [body(): lax.dynamic_slice_in_dim(source, first + (here ^ mask) * each, each, 0)]
    dot_general x4 -> x8, matrix products: 3.14 us -> 6.66 us  [products(): lax.dot_general(block, train_flat, contract, preferred_element_type=jnp.f...]
    unnamed x18 -> x16, local copies, waits for them, and re-layouts: 2.08 us -> 5.1 us
    ppermute x22 -> x26, starting transfers between devices: 41.2 us -> 38.3 us  [crossed(): return lax.ppermute(value, axis, [(at, at ^ mask) for at in range(size)])]
    concatenate x4 -> x9, other arithmetic: 1.77 us -> 0.32 us  [the longest x4 0.16 us: spread_shares(): jnp.concatenate([near] + [crossed(near, 'dp', shares, mask) for mask in r...]
    convert_element_type x2 -> x0, other arithmetic: 1.22 us -> none  [basis_halves(): return (high.astype(jnp.bfloat16), (matrix - high).astype(jnp.bfloat16))]
    ppermute x22 -> x26, waiting for transfers between devices: 35.8 us -> 36.1 us  [crossed(): return lax.ppermute(value, axis, [(at, at ^ mask) for at in range(size)])]
  transfers between devices with their start and end apart: 22 -> 26, of which waited for: 10 -> 10; matrix products, arithmetic and copies ran while one was open for 11% -> 11% of each run, Pallas kernels for 5% -> 5%
where the time goes in v9:
time: 93.5 us; the launch traced here: 93.3 us
  starting transfers between devices  38.3 us (41%)
  waiting for transfers between devices  36.1 us (39%)
  matrix products  6.66 us (7%)
  local copies, waits for them, and re-layouts  5.38 us (6%)
  Pallas kernels  4.49 us (5%)
  other arithmetic  1.81 us (2%)
    ppermute x26, starting transfers between devices, crossed(): return lax.ppermute(value, axis, [(at, at ^ mask) for at in range(size)])  38.3 us
    ppermute x26, waiting for transfers between devices, crossed(): return lax.ppermute(value, axis, [(at, at ^ mask) for at in range(size)])  36.1 us
    dot_general x8, matrix products, products(): lax.dot_general(block, train_flat, contract, preferred_element_type=jnp.f...  6.66 us
    unnamed x16, local copies, waits for them, and re-layouts  5.1 us
    pallas_call x2, Pallas kernels, condition_fast(): pl.pallas_call(functools.partial(condition_kernel, slices, rows_here), gr...  4.49 us
  transfers between devices with their start and end apart: 26, of which 10 were waited for; matrix products, arithmetic and copies ran while one was open for 11% of the time, Pallas kernels for 5%

profile of v9, /device:TPU:0, one launch (start us, length us, event | category | flops | bytes accessed | tf_op | source)
XLA Modules:
  0.0 93.3 jit_solution(10349258073124291503)
XLA Ops:
  0.0 1.2 %copy-done = bf16[256,16,128]{2,1,0:T(8,128)(2,1)S(1)} copy-done((bf16[256,16,128]{2,1,0:T(8,128)(2,1)S(1)}, bf16[256,16,128]{2,1,0:T(8,128)(2,1)}, u32[]{:S(2)}) %copy-start) | copy-done | bytes 1048600
  1.3 5.1 %collective-permute-start.2 = (bf16[32,16,128]{2,1,0:T(8,128)(2,1)S(1)}, bf16[32,16,128]{2,1,0:T(8,128)(2,1)S(1)}, u32[]{:S(2)}, u32[]{:S(2)}) collective-permute-start(bf16[32,16,128]{2,1,0:T(8,128)(2,1)S(1)} %constant_dynamic-slice_fusion.4), channel_id=1, source_target_pairs={{0,3},{1,2},{2,1},{3,0},{4,7},{5,6},{6,5},{7,4},{8,11},{9,10},{10,... | collective-permute-start | bytes 393224 | tf_op jit(solution)/shard_map/ppermute | solution.py:100
  6.4 0.0 collective-permute-start.1
  6.4 0.6 collective-permute-start
  7.2 3.8 %collective-permute-start.8 = (bf16[32,16,128]{2,1,0:T(8,128)(2,1)S(1)}, bf16[32,16,128]{2,1,0:T(8,128)(2,1)S(1)}, u32[]{:S(2)}, u32[]{:S(2)}) collective-permute-start(bf16[32,16,128]{2,1,0:T(8,128)(2,1)S(1)} %constant_dynamic-slice_fusion), channel_id=1, source_target_pairs={{0,3},{1,2},{2,1},{3,0},{4,7},{5,6},{6,5},{7,4},{8,11},{9,10},{10,... | collective-permute-start | bytes 393224 | tf_op jit(solution)/shard_map/ppermute | solution.py:100
  11.0 0.1 copy.13
  11.1 0.1 copy.14
  11.2 0.1 copy.15
  11.3 0.1 copy.16
  11.4 5.7 %collective-permute-start.6 = (bf16[32,16,128]{2,1,0:T(8,128)(2,1)S(1)}, bf16[32,16,128]{2,1,0:T(8,128)(2,1)S(1)}, u32[]{:S(2)}, u32[]{:S(2)}) collective-permute-start(bf16[32,16,128]{2,1,0:T(8,128)(2,1)S(1)} %constant_dynamic-slice_fusion.2), channel_id=1, source_target_pairs={{0,1},{1,0},{2,3},{3,2},{4,5},{5,4},{6,7},{7,6},{8,9},{9,8},{10,11... | collective-permute-start | bytes 393224 | tf_op jit(solution)/shard_map/ppermute | solution.py:100
  17.1 0.1 pad_maximum_fusion.18
  17.2 0.1 copy.11.refs_4_
  17.2 0.0 copy-done.1
  17.3 0.1 copy.10
  17.4 6.7 %collective-permute-done.1.refs_2_ = bf16[32,16,128]{2,1,0:T(8,128)(2,1)S(1)} collective-permute-done((bf16[32,16,128]{2,1,0:T(8,128)(2,1)S(1)}, bf16[32,16,128]{2,1,0:T(8,128)(2,1)S(1)}, u32[]{:S(2)}, u32[]{:S(2)}) %collective-permute-start.1) | collective-permute-done | bytes 131104 | tf_op jit(solution)/shard_map/ppermute | solution.py:100
  24.1 0.0 collective-permute-done.refs_1_
  24.1 2.2 %shard_map.55 = (bf16[32,2048]{1,0:T(8,128)(2,1)S(1)}, bf16[32,2048]{1,0:T(8,128)(2,1)S(1)}, bf16[32,2048]{1,0:T(8,128)(2,1)S(1)}, bf16[32,2048]{1,0:T(8,128)(2,1)S(1)}) custom-call(bf16[32,16,128]{2,1,0:T(8,128)(2,1)S(1)} %constant_dynamic-slice_fusion.7.refs_0_, bf16[32,16,128]{2,1,0:T(8,128)(2,1)S(1)} %collective-permute-done.refs_1_, ...), custom_call_target="tpu_custom_call" | custom-call | tf_op jit(solution)/shard_map/pallas_call | solution.py:75
  26.3 0.1 collective-permute-start.3
  26.5 3.5 %copy.19 = bf16[64,8,16,128]{3,1,2,0:T(8,128)(2,1)} copy(bf16[64,8,16,128]{3,2,1,0:T(8,128)(2,1)} %bitcast.78) | data formatting | bytes 4194304
  30.0 2.7 %collective-permute-start.10 = (bf16[32,2048]{1,0:T(8,128)(2,1)S(1)}, bf16[32,2048]{1,0:T(8,128)(2,1)S(1)}, u32[]{:S(2)}, u32[]{:S(2)}) collective-permute-start(bf16[32,2048]{1,0:T(8,128)(2,1)S(1)} %get-tuple-element.54), channel_id=1, source_target_pairs={{0,3},{1,2},{2,1},{3,0},{4,7},{5,6},{6,5},{7,4},{8,11},{9,10},{10,... | collective-permute-start | bytes 393224 | tf_op jit(solution)/shard_map/ppermute | solution.py:100
  32.7 0.8 collective-permute-start.9
  33.4 2.2 %shard_map.56 = (bf16[32,2048]{1,0:T(8,128)(2,1)S(1)}, bf16[32,2048]{1,0:T(8,128)(2,1)S(1)}, bf16[32,2048]{1,0:T(8,128)(2,1)S(1)}, bf16[32,2048]{1,0:T(8,128)(2,1)S(1)}) custom-call(bf16[32,16,128]{2,1,0:T(8,128)(2,1)S(1)} %constant_dynamic-slice_fusion.3.refs_0_, bf16[32,16,128]{2,1,0:T(8,128)(2,1)S(1)} %collective-permute-done.6.refs_1_, ...), custom_call_target="tpu_custom_call" | custom-call | tf_op jit(solution)/shard_map/pallas_call | solution.py:75
  35.7 1.0 %collective-permute-start.16 = (bf16[32,2048]{1,0:T(8,128)(2,1)S(1)}, bf16[32,2048]{1,0:T(8,128)(2,1)S(1)}, u32[]{:S(2)}, u32[]{:S(2)}) collective-permute-start(bf16[32,2048]{1,0:T(8,128)(2,1)S(1)} %get-tuple-element.60), channel_id=1, source_target_pairs={{0,1},{1,0},{2,3},{3,2},{4,5},{5,4},{6,7},{7,6},{8,9},{9,8},{10,11... | collective-permute-start | bytes 393224 | tf_op jit(solution)/shard_map/ppermute | solution.py:100
  36.7 2.3 %collective-permute-start.19 = (bf16[32,2048]{1,0:T(8,128)(2,1)S(1)}, bf16[32,2048]{1,0:T(8,128)(2,1)S(1)}, u32[]{:S(2)}, u32[]{:S(2)}) collective-permute-start(bf16[32,2048]{1,0:T(8,128)(2,1)S(1)} %get-tuple-element.62), channel_id=1, source_target_pairs={{0,2},{1,3},{2,0},{3,1},{4,6},{5,7},{6,4},{7,5},{8,10},{9,11},{10,... | collective-permute-start | bytes 393224 | tf_op jit(solution)/shard_map/ppermute | solution.py:100
  39.0 1.2 %collective-permute-start.20 = (bf16[32,2048]{1,0:T(8,128)(2,1)S(1)}, bf16[32,2048]{1,0:T(8,128)(2,1)S(1)}, u32[]{:S(2)}, u32[]{:S(2)}) collective-permute-start(bf16[32,2048]{1,0:T(8,128)(2,1)S(1)} %get-tuple-element.63), channel_id=1, source_target_pairs={{0,3},{1,2},{2,1},{3,0},{4,7},{5,6},{6,5},{7,4},{8,11},{9,10},{10,... | collective-permute-start | bytes 393224 | tf_op jit(solution)/shard_map/ppermute | solution.py:100
  40.2 0.0 collective-permute-done.10
  40.2 1.5 %collective-permute-start.4 = (bf16[64,2048]{1,0:T(8,128)(2,1)S(1)}, bf16[64,2048]{1,0:T(8,128)(2,1)S(1)}, u32[]{:S(2)}, u32[]{:S(2)}) collective-permute-start(bf16[64,2048]{1,0:T(8,128)(2,1)S(1)} %pad_maximum_fusion.4), channel_id=1, source_target_pairs={{0,8},{4,12},{8,0},{12,4},{1,9},{5,13},{9,1},{13,5},{2,10},{6,14},... | collective-permute-start | bytes 786440 | tf_op jit(solution)/shard_map/ppermute | solution.py:100
  41.7 7.9 %collective-permute-done.9 = bf16[32,2048]{1,0:T(8,128)(2,1)S(1)} collective-permute-done((bf16[32,2048]{1,0:T(8,128)(2,1)S(1)}, bf16[32,2048]{1,0:T(8,128)(2,1)S(1)}, u32[]{:S(2)}, u32[]{:S(2)}) %collective-permute-start.9) | collective-permute-done | bytes 131104 | tf_op jit(solution)/shard_map/ppermute | solution.py:100
  49.6 1.4 %collective-permute-start.11 = (bf16[64,2048]{1,0:T(8,128)(2,1)S(1)}, bf16[64,2048]{1,0:T(8,128)(2,1)S(1)}, u32[]{:S(2)}, u32[]{:S(2)}) collective-permute-start(bf16[64,2048]{1,0:T(8,128)(2,1)S(1)} %pad_maximum_fusion.5), channel_id=1, source_target_pairs={{0,8},{4,12},{8,0},{12,4},{1,9},{5,13},{9,1},{13,5},{2,10},{6,14},... | collective-permute-start | bytes 786440 | tf_op jit(solution)/shard_map/ppermute | solution.py:100
  51.0 0.0 collective-permute-done.16
  51.1 0.7 collective-permute-start.17
  51.8 0.6 collective-permute-done.19
  52.4 1.4 %collective-permute-start.21 = (bf16[64,2048]{1,0:T(8,128)(2,1)S(1)}, bf16[64,2048]{1,0:T(8,128)(2,1)S(1)}, u32[]{:S(2)}, u32[]{:S(2)}) collective-permute-start(bf16[64,2048]{1,0:T(8,128)(2,1)S(1)} %pad_maximum_fusion.8), channel_id=1, source_target_pairs={{0,8},{4,12},{8,0},{12,4},{1,9},{5,13},{9,1},{13,5},{2,10},{6,14},... | collective-permute-start | bytes 786440 | tf_op jit(solution)/shard_map/ppermute | solution.py:100
  53.9 5.0 %collective-permute-done.11 = bf16[64,2048]{1,0:T(8,128)(2,1)S(1)} collective-permute-done((bf16[64,2048]{1,0:T(8,128)(2,1)S(1)}, bf16[64,2048]{1,0:T(8,128)(2,1)S(1)}, u32[]{:S(2)}, u32[]{:S(2)}) %collective-permute-start.11) | collective-permute-done | bytes 262176 | tf_op jit(solution)/shard_map/ppermute | solution.py:100
  59.0 0.1 collective-permute-start.5
  59.1 0.5 collective-permute-start.12
  59.6 0.8 convolution_convert_fusion.5
  60.4 4.2 %collective-permute-done.17 = bf16[64,2048]{1,0:T(8,128)(2,1)S(1)} collective-permute-done((bf16[64,2048]{1,0:T(8,128)(2,1)S(1)}, bf16[64,2048]{1,0:T(8,128)(2,1)S(1)}, u32[]{:S(2)}, u32[]{:S(2)}) %collective-permute-start.17) | collective-permute-done | bytes 262176 | tf_op jit(solution)/shard_map/ppermute | solution.py:100
  64.6 0.8 convolution_convert_fusion.4
  65.5 0.8 convolution_convert_fusion.7
  66.4 0.8 convolution_convert_fusion.6
  67.2 0.1 broadcast_select_fusion.12
  67.3 0.1 collective-permute-start.14
  67.4 0.2 collective-permute-done.21
  67.6 0.1 broadcast_select_fusion.15
  67.7 0.1 collective-permute-start.13
  67.8 4.2 %collective-permute-start.15 = (bf16[1,128,512]{2,1,0:T(8,128)(2,1)S(1)}, bf16[1,128,512]{2,1,0:T(8,128)(2,1)S(1)}, u32[]{:S(2)}, u32[]{:S(2)}) collective-permute-start(bf16[1,128,512]{2,1,0:T(8,128)(2,1)S(1)} %get-tuple-element.77), channel_id=1, source_target_pairs={{0,3},{1,2},{2,1},{3,0},{4,7},{5,6},{6,5},{7,4},{8,11},{9,10},{10,... | collective-permute-start | bytes 393224 | tf_op jit(solution)/shard_map/ppermute | solution.py:100
  72.0 2.4 %collective-permute-done.14 = bf16[1,128,512]{2,1,0:T(8,128)(2,1)S(1)} collective-permute-done((bf16[1,128,512]{2,1,0:T(8,128)(2,1)S(1)}, bf16[1,128,512]{2,1,0:T(8,128)(2,1)S(1)}, u32[]{:S(2)}, u32[]{:S(2)}) %collective-permute-start.14) | collective-permute-done | bytes 131104 | tf_op jit(solution)/shard_map/ppermute | solution.py:100
  74.4 0.8 convolution_convert_fusion.1
  75.3 0.6 collective-permute-start.22
  75.9 0.9 collective-permute-done.13
  76.7 0.1 broadcast_select_fusion.31
  76.8 0.8 convolution_convert_fusion
  77.7 0.8 convolution_convert_fusion.3
  78.6 0.8 convolution_convert_fusion.2
  79.4 0.1 broadcast_select_fusion.11
  79.6 0.1 broadcast_select_fusion.9
  79.7 1.1 %collective-permute-start.23 = (bf16[1,128,512]{2,1,0:T(8,128)(2,1)S(1)}, bf16[1,128,512]{2,1,0:T(8,128)(2,1)S(1)}, u32[]{:S(2)}, u32[]{:S(2)}) collective-permute-start(bf16[1,128,512]{2,1,0:T(8,128)(2,1)S(1)} %get-tuple-element.80), channel_id=1, source_target_pairs={{0,1},{1,0},{2,3},{3,2},{4,5},{5,4},{6,7},{7,6},{8,9},{9,8},{10,11... | collective-permute-start | bytes 393224 | tf_op jit(solution)/shard_map/ppermute | solution.py:100
  80.7 1.7 %collective-permute-start.24 = (bf16[1,128,512]{2,1,0:T(8,128)(2,1)S(1)}, bf16[1,128,512]{2,1,0:T(8,128)(2,1)S(1)}, u32[]{:S(2)}, u32[]{:S(2)}) collective-permute-start(bf16[1,128,512]{2,1,0:T(8,128)(2,1)S(1)} %get-tuple-element.81), channel_id=1, source_target_pairs={{0,2},{1,3},{2,0},{3,1},{4,6},{5,7},{6,4},{7,5},{8,10},{9,11},{10,... | collective-permute-start | bytes 393224 | tf_op jit(solution)/shard_map/ppermute | solution.py:100
  82.4 1.7 %collective-permute-start.25 = (bf16[1,128,512]{2,1,0:T(8,128)(2,1)S(1)}, bf16[1,128,512]{2,1,0:T(8,128)(2,1)S(1)}, u32[]{:S(2)}, u32[]{:S(2)}) collective-permute-start(bf16[1,128,512]{2,1,0:T(8,128)(2,1)S(1)} %get-tuple-element.82), channel_id=1, source_target_pairs={{0,3},{1,2},{2,1},{3,0},{4,7},{5,6},{6,5},{7,4},{8,11},{9,10},{10,... | collective-permute-start | bytes 393224 | tf_op jit(solution)/shard_map/ppermute | solution.py:100
  84.2 2.1 %collective-permute-done.23 = bf16[1,128,512]{2,1,0:T(8,128)(2,1)S(1)} collective-permute-done((bf16[1,128,512]{2,1,0:T(8,128)(2,1)S(1)}, bf16[1,128,512]{2,1,0:T(8,128)(2,1)S(1)}, u32[]{:S(2)}, u32[]{:S(2)}) %collective-permute-start.23) | collective-permute-done | bytes 131104 | tf_op jit(solution)/shard_map/ppermute | solution.py:100
  86.2 6.1 %collective-permute-done.24 = bf16[1,128,512]{2,1,0:T(8,128)(2,1)S(1)} collective-permute-done((bf16[1,128,512]{2,1,0:T(8,128)(2,1)S(1)}, bf16[1,128,512]{2,1,0:T(8,128)(2,1)S(1)}, u32[]{:S(2)}, u32[]{:S(2)}) %collective-permute-start.24) | collective-permute-done | bytes 131104 | tf_op jit(solution)/shard_map/ppermute | solution.py:100
  92.4 0.1 broadcast_select_fusion.27
  92.5 0.8 maximum_bitcast_fusion
  (52 shorter events, 0.6 us)
Async XLA Ops:
  0.0 1.2 %copy-start = (bf16[256,16,128]{2,1,0:T(8,128)(2,1)S(1)}, bf16[256,16,128]{2,1,0:T(8,128)(2,1)}, u32[]{:S(2)}) copy-start(bf16[256,16,128]{2,1,0:T(8,128)(2,1)} %param.5) | copy-start | bytes 3145732
  0.0 11.0 %copy-start.4 = (f32[64,64]{1,0:T(8,128)S(1)}, f32[64,64]{1,0:T(8,128)}, u32[]{:S(2)}) copy-start(f32[64,64]{1,0:T(8,128)} %param.7) | copy-start | bytes 49156
  0.0 17.2 %copy-start.1 = (f32[128,128]{1,0:T(8,128)S(1)}, f32[128,128]{1,0:T(8,128)}, u32[]{:S(2)}) copy-start(f32[128,128]{1,0:T(8,128)} %refs_6_.3) | copy-start | bytes 196612
  0.0 24.1 %copy-start.2 = (f32[64,128]{1,0:T(8,128)S(1)}, f32[64,128]{1,0:T(8,128)}, u32[]{:S(2)}) copy-start(f32[64,128]{1,0:T(8,128)} %refs_8_.3) | copy-start | bytes 98308
  1.3 10.0 %collective-permute-start.2 = (bf16[32,16,128]{2,1,0:T(8,128)(2,1)S(1)}, bf16[32,16,128]{2,1,0:T(8,128)(2,1)S(1)}, u32[]{:S(2)}, u32[]{:S(2)}) collective-permute-start(bf16[32,16,128]{2,1,0:T(8,128)(2,1)S(1)} %constant_dynamic-slice_fusion.4), channel_id=1, source_target_pairs={{0,3},{1,2},{2,1},{3,0},{4,7},{5,6},{6,5},{7,4},{8,11},{9,10},{10,... | collective-permute-start | bytes 393224 | tf_op jit(solution)/shard_map/ppermute | solution.py:100
  6.4 17.7 %collective-permute-start.1 = (bf16[32,16,128]{2,1,0:T(8,128)(2,1)S(1)}, bf16[32,16,128]{2,1,0:T(8,128)(2,1)S(1)}, u32[]{:S(2)}, u32[]{:S(2)}) collective-permute-start(bf16[32,16,128]{2,1,0:T(8,128)(2,1)S(1)} %constant_dynamic-slice_fusion.5), channel_id=1, source_target_pairs={{0,2},{1,3},{2,0},{3,1},{4,6},{5,7},{6,4},{7,5},{8,10},{9,11},{10,... | collective-permute-start | bytes 393224 | tf_op jit(solution)/shard_map/ppermute | solution.py:100
  6.4 17.7 %collective-permute-start = (bf16[32,16,128]{2,1,0:T(8,128)(2,1)S(1)}, bf16[32,16,128]{2,1,0:T(8,128)(2,1)S(1)}, u32[]{:S(2)}, u32[]{:S(2)}) collective-permute-start(bf16[32,16,128]{2,1,0:T(8,128)(2,1)S(1)} %constant_dynamic-slice_fusion.6), channel_id=1, source_target_pairs={{0,1},{1,0},{2,3},{3,2},{4,5},{5,4},{6,7},{7,6},{8,9},{9,8},{10,11... | collective-permute-start | bytes 393224 | tf_op jit(solution)/shard_map/ppermute | solution.py:100
  7.2 22.8 %collective-permute-start.8 = (bf16[32,16,128]{2,1,0:T(8,128)(2,1)S(1)}, bf16[32,16,128]{2,1,0:T(8,128)(2,1)S(1)}, u32[]{:S(2)}, u32[]{:S(2)}) collective-permute-start(bf16[32,16,128]{2,1,0:T(8,128)(2,1)S(1)} %constant_dynamic-slice_fusion), channel_id=1, source_target_pairs={{0,3},{1,2},{2,1},{3,0},{4,7},{5,6},{6,5},{7,4},{8,11},{9,10},{10,... | collective-permute-start | bytes 393224 | tf_op jit(solution)/shard_map/ppermute | solution.py:100
  11.0 18.9 %collective-permute-start.7 = (bf16[32,16,128]{2,1,0:T(8,128)(2,1)S(1)}, bf16[32,16,128]{2,1,0:T(8,128)(2,1)S(1)}, u32[]{:S(2)}, u32[]{:S(2)}) collective-permute-start(bf16[32,16,128]{2,1,0:T(8,128)(2,1)S(1)} %constant_dynamic-slice_fusion.1), channel_id=1, source_target_pairs={{0,2},{1,3},{2,0},{3,1},{4,6},{5,7},{6,4},{7,5},{8,10},{9,11},{10,... | collective-permute-start | bytes 393224 | tf_op jit(solution)/shard_map/ppermute | solution.py:100
  11.4 18.6 %collective-permute-start.6 = (bf16[32,16,128]{2,1,0:T(8,128)(2,1)S(1)}, bf16[32,16,128]{2,1,0:T(8,128)(2,1)S(1)}, u32[]{:S(2)}, u32[]{:S(2)}) collective-permute-start(bf16[32,16,128]{2,1,0:T(8,128)(2,1)S(1)} %constant_dynamic-slice_fusion.2), channel_id=1, source_target_pairs={{0,1},{1,0},{2,3},{3,2},{4,5},{5,4},{6,7},{7,6},{8,9},{9,8},{10,11... | collective-permute-start | bytes 393224 | tf_op jit(solution)/shard_map/ppermute | solution.py:100
  26.3 12.7 %collective-permute-start.3 = (bf16[32,2048]{1,0:T(8,128)(2,1)S(1)}, bf16[32,2048]{1,0:T(8,128)(2,1)S(1)}, u32[]{:S(2)}, u32[]{:S(2)}) collective-permute-start(bf16[32,2048]{1,0:T(8,128)(2,1)S(1)} %get-tuple-element.43), channel_id=1, source_target_pairs={{0,1},{1,0},{2,3},{3,2},{4,5},{5,4},{6,7},{7,6},{8,9},{9,8},{10,11... | collective-permute-start | bytes 393224 | tf_op jit(solution)/shard_map/ppermute | solution.py:100
  30.0 10.2 %collective-permute-start.10 = (bf16[32,2048]{1,0:T(8,128)(2,1)S(1)}, bf16[32,2048]{1,0:T(8,128)(2,1)S(1)}, u32[]{:S(2)}, u32[]{:S(2)}) collective-permute-start(bf16[32,2048]{1,0:T(8,128)(2,1)S(1)} %get-tuple-element.54), channel_id=1, source_target_pairs={{0,3},{1,2},{2,1},{3,0},{4,7},{5,6},{6,5},{7,4},{8,11},{9,10},{10,... | collective-permute-start | bytes 393224 | tf_op jit(solution)/shard_map/ppermute | solution.py:100
  32.7 16.9 %collective-permute-start.9 = (bf16[32,2048]{1,0:T(8,128)(2,1)S(1)}, bf16[32,2048]{1,0:T(8,128)(2,1)S(1)}, u32[]{:S(2)}, u32[]{:S(2)}) collective-permute-start(bf16[32,2048]{1,0:T(8,128)(2,1)S(1)} %get-tuple-element.53), channel_id=1, source_target_pairs={{0,2},{1,3},{2,0},{3,1},{4,6},{5,7},{6,4},{7,5},{8,10},{9,11},{10,... | collective-permute-start | bytes 393224 | tf_op jit(solution)/shard_map/ppermute | solution.py:100
  35.7 15.4 %collective-permute-start.16 = (bf16[32,2048]{1,0:T(8,128)(2,1)S(1)}, bf16[32,2048]{1,0:T(8,128)(2,1)S(1)}, u32[]{:S(2)}, u32[]{:S(2)}) collective-permute-start(bf16[32,2048]{1,0:T(8,128)(2,1)S(1)} %get-tuple-element.60), channel_id=1, source_target_pairs={{0,1},{1,0},{2,3},{3,2},{4,5},{5,4},{6,7},{7,6},{8,9},{9,8},{10,11... | collective-permute-start | bytes 393224 | tf_op jit(solution)/shard_map/ppermute | solution.py:100
  36.7 15.7 %collective-permute-start.19 = (bf16[32,2048]{1,0:T(8,128)(2,1)S(1)}, bf16[32,2048]{1,0:T(8,128)(2,1)S(1)}, u32[]{:S(2)}, u32[]{:S(2)}) collective-permute-start(bf16[32,2048]{1,0:T(8,128)(2,1)S(1)} %get-tuple-element.62), channel_id=1, source_target_pairs={{0,2},{1,3},{2,0},{3,1},{4,6},{5,7},{6,4},{7,5},{8,10},{9,11},{10,... | collective-permute-start | bytes 393224 | tf_op jit(solution)/shard_map/ppermute | solution.py:100
  39.0 13.4 %collective-permute-start.20 = (bf16[32,2048]{1,0:T(8,128)(2,1)S(1)}, bf16[32,2048]{1,0:T(8,128)(2,1)S(1)}, u32[]{:S(2)}, u32[]{:S(2)}) collective-permute-start(bf16[32,2048]{1,0:T(8,128)(2,1)S(1)} %get-tuple-element.63), channel_id=1, source_target_pairs={{0,3},{1,2},{2,1},{3,0},{4,7},{5,6},{6,5},{7,4},{8,11},{9,10},{10,... | collective-permute-start | bytes 393224 | tf_op jit(solution)/shard_map/ppermute | solution.py:100
  40.2 19.4 %copy-start.3 = (bf16[64,8,16,128]{3,1,2,0:T(8,128)(2,1)S(1)}, bf16[64,8,16,128]{3,1,2,0:T(8,128)(2,1)}, u32[]{:S(2)}) copy-start(bf16[64,8,16,128]{3,1,2,0:T(8,128)(2,1)} %copy.19) | copy-start | bytes 6291460
  40.2 13.7 %collective-permute-start.4 = (bf16[64,2048]{1,0:T(8,128)(2,1)S(1)}, bf16[64,2048]{1,0:T(8,128)(2,1)S(1)}, u32[]{:S(2)}, u32[]{:S(2)}) collective-permute-start(bf16[64,2048]{1,0:T(8,128)(2,1)S(1)} %pad_maximum_fusion.4), channel_id=1, source_target_pairs={{0,8},{4,12},{8,0},{12,4},{1,9},{5,13},{9,1},{13,5},{2,10},{6,14},... | collective-permute-start | bytes 786440 | tf_op jit(solution)/shard_map/ppermute | solution.py:100
  49.6 9.3 %collective-permute-start.11 = (bf16[64,2048]{1,0:T(8,128)(2,1)S(1)}, bf16[64,2048]{1,0:T(8,128)(2,1)S(1)}, u32[]{:S(2)}, u32[]{:S(2)}) collective-permute-start(bf16[64,2048]{1,0:T(8,128)(2,1)S(1)} %pad_maximum_fusion.5), channel_id=1, source_target_pairs={{0,8},{4,12},{8,0},{12,4},{1,9},{5,13},{9,1},{13,5},{2,10},{6,14},... | collective-permute-start | bytes 786440 | tf_op jit(solution)/shard_map/ppermute | solution.py:100
  51.1 13.5 %collective-permute-start.17 = (bf16[64,2048]{1,0:T(8,128)(2,1)S(1)}, bf16[64,2048]{1,0:T(8,128)(2,1)S(1)}, u32[]{:S(2)}, u32[]{:S(2)}) collective-permute-start(bf16[64,2048]{1,0:T(8,128)(2,1)S(1)} %pad_maximum_fusion.7), channel_id=1, source_target_pairs={{0,8},{4,12},{8,0},{12,4},{1,9},{5,13},{9,1},{13,5},{2,10},{6,14},... | collective-permute-start | bytes 786440 | tf_op jit(solution)/shard_map/ppermute | solution.py:100
  52.4 15.1 %collective-permute-start.21 = (bf16[64,2048]{1,0:T(8,128)(2,1)S(1)}, bf16[64,2048]{1,0:T(8,128)(2,1)S(1)}, u32[]{:S(2)}, u32[]{:S(2)}) collective-permute-start(bf16[64,2048]{1,0:T(8,128)(2,1)S(1)} %pad_maximum_fusion.8), channel_id=1, source_target_pairs={{0,8},{4,12},{8,0},{12,4},{1,9},{5,13},{9,1},{13,5},{2,10},{6,14},... | collective-permute-start | bytes 786440 | tf_op jit(solution)/shard_map/ppermute | solution.py:100
  59.0 6.5 %collective-permute-start.5 = (bf16[128,2048]{1,0:T(8,128)(2,1)S(1)}, bf16[128,2048]{1,0:T(8,128)(2,1)S(1)}, u32[]{:S(2)}, u32[]{:S(2)}) collective-permute-start(bf16[128,2048]{1,0:T(8,128)(2,1)S(1)} %pad_maximum_fusion), channel_id=1, source_target_pairs={{0,4},{4,0},{8,12},{12,8},{1,5},{5,1},{9,13},{13,9},{2,6},{6,2},{1... | collective-permute-start | bytes 1572872 | tf_op jit(solution)/shard_map/ppermute | solution.py:100
  59.1 7.3 %collective-permute-start.12 = (bf16[128,2048]{1,0:T(8,128)(2,1)S(1)}, bf16[128,2048]{1,0:T(8,128)(2,1)S(1)}, u32[]{:S(2)}, u32[]{:S(2)}) collective-permute-start(bf16[128,2048]{1,0:T(8,128)(2,1)S(1)} %pad_maximum_fusion.1), channel_id=1, source_target_pairs={{0,4},{4,0},{8,12},{12,8},{1,5},{5,1},{9,13},{13,9},{2,6},{6,2},{1... | collective-permute-start | bytes 1572872 | tf_op jit(solution)/shard_map/ppermute | solution.py:100
  67.3 7.1 %collective-permute-start.14 = (bf16[1,128,512]{2,1,0:T(8,128)(2,1)S(1)}, bf16[1,128,512]{2,1,0:T(8,128)(2,1)S(1)}, u32[]{:S(2)}, u32[]{:S(2)}) collective-permute-start(bf16[1,128,512]{2,1,0:T(8,128)(2,1)S(1)} %get-tuple-element.78), channel_id=1, source_target_pairs={{0,2},{1,3},{2,0},{3,1},{4,6},{5,7},{6,4},{7,5},{8,10},{9,11},{10,... | collective-permute-start | bytes 393224 | tf_op jit(solution)/shard_map/ppermute | solution.py:100
  67.7 9.0 %collective-permute-start.13 = (bf16[1,128,512]{2,1,0:T(8,128)(2,1)S(1)}, bf16[1,128,512]{2,1,0:T(8,128)(2,1)S(1)}, u32[]{:S(2)}, u32[]{:S(2)}) collective-permute-start(bf16[1,128,512]{2,1,0:T(8,128)(2,1)S(1)} %get-tuple-element.76), channel_id=1, source_target_pairs={{0,1},{1,0},{2,3},{3,2},{4,5},{5,4},{6,7},{7,6},{8,9},{9,8},{10,11... | collective-permute-start | bytes 393224 | tf_op jit(solution)/shard_map/ppermute | solution.py:100
  67.8 8.9 %collective-permute-start.15 = (bf16[1,128,512]{2,1,0:T(8,128)(2,1)S(1)}, bf16[1,128,512]{2,1,0:T(8,128)(2,1)S(1)}, u32[]{:S(2)}, u32[]{:S(2)}) collective-permute-start(bf16[1,128,512]{2,1,0:T(8,128)(2,1)S(1)} %get-tuple-element.77), channel_id=1, source_target_pairs={{0,3},{1,2},{2,1},{3,0},{4,7},{5,6},{6,5},{7,4},{8,11},{9,10},{10,... | collective-permute-start | bytes 393224 | tf_op jit(solution)/shard_map/ppermute | solution.py:100
  74.4 3.3 %collective-permute-start.18 = (bf16[128,2048]{1,0:T(8,128)(2,1)S(1)}, bf16[128,2048]{1,0:T(8,128)(2,1)S(1)}, u32[]{:S(2)}, u32[]{:S(2)}) collective-permute-start(bf16[128,2048]{1,0:T(8,128)(2,1)S(1)} %pad_maximum_fusion.2), channel_id=1, source_target_pairs={{0,4},{4,0},{8,12},{12,8},{1,5},{5,1},{9,13},{13,9},{2,6},{6,2},{1... | collective-permute-start | bytes 1572872 | tf_op jit(solution)/shard_map/ppermute | solution.py:100
  75.3 3.3 %collective-permute-start.22 = (bf16[128,2048]{1,0:T(8,128)(2,1)S(1)}, bf16[128,2048]{1,0:T(8,128)(2,1)S(1)}, u32[]{:S(2)}, u32[]{:S(2)}) collective-permute-start(bf16[128,2048]{1,0:T(8,128)(2,1)S(1)} %pad_maximum_fusion.3), channel_id=1, source_target_pairs={{0,4},{4,0},{8,12},{12,8},{1,5},{5,1},{9,13},{13,9},{2,6},{6,2},{1... | collective-permute-start | bytes 1572872 | tf_op jit(solution)/shard_map/ppermute | solution.py:100
  79.7 6.6 %collective-permute-start.23 = (bf16[1,128,512]{2,1,0:T(8,128)(2,1)S(1)}, bf16[1,128,512]{2,1,0:T(8,128)(2,1)S(1)}, u32[]{:S(2)}, u32[]{:S(2)}) collective-permute-start(bf16[1,128,512]{2,1,0:T(8,128)(2,1)S(1)} %get-tuple-element.80), channel_id=1, source_target_pairs={{0,1},{1,0},{2,3},{3,2},{4,5},{5,4},{6,7},{7,6},{8,9},{9,8},{10,11... | collective-permute-start | bytes 393224 | tf_op jit(solution)/shard_map/ppermute | solution.py:100
  80.7 11.6 %collective-permute-start.24 = (bf16[1,128,512]{2,1,0:T(8,128)(2,1)S(1)}, bf16[1,128,512]{2,1,0:T(8,128)(2,1)S(1)}, u32[]{:S(2)}, u32[]{:S(2)}) collective-permute-start(bf16[1,128,512]{2,1,0:T(8,128)(2,1)S(1)} %get-tuple-element.81), channel_id=1, source_target_pairs={{0,2},{1,3},{2,0},{3,1},{4,6},{5,7},{6,4},{7,5},{8,10},{9,11},{10,... | collective-permute-start | bytes 393224 | tf_op jit(solution)/shard_map/ppermute | solution.py:100
  82.4 10.0 %collective-permute-start.25 = (bf16[1,128,512]{2,1,0:T(8,128)(2,1)S(1)}, bf16[1,128,512]{2,1,0:T(8,128)(2,1)S(1)}, u32[]{:S(2)}, u32[]{:S(2)}) collective-permute-start(bf16[1,128,512]{2,1,0:T(8,128)(2,1)S(1)} %get-tuple-element.82), channel_id=1, source_target_pairs={{0,3},{1,2},{2,1},{3,0},{4,7},{5,6},{6,5},{7,4},{8,11},{9,10},{10,... | collective-permute-start | bytes 393224 | tf_op jit(solution)/shard_map/ppermute | solution.py:100

commit v10 on v9

--- a/solution.py
+++ b/solution.py
@@ -145,10 +145,13 @@
     basis = jnp.concatenate(turned([row_blocks[at] for at in range(slices)], here), axis=0)
     condition = condition_fast if rows_here % 16 == 0 else condition_plain
     parts = [count * size // sum(CHUNKS) for size in CHUNKS]
+    half = slices // 2
     pieces, rows, results = [], [], []
     source = queries
     for chunk, part in enumerate(parts):
         first, each = sum(parts[:chunk]), part // slices
+        if chunk:
+            source, pieces[0][1], train_flat = lax.optimization_barrier((source, pieces[0][1], train_flat))
         raw = []
         for mask in range(slices):
             block = lax.dynamic_slice_in_dim(source, first + (here ^ mask) * each, each, 0)
@@ -156,12 +159,10 @@
             raw.append(block)
         pieces.append(exchanged(raw, slices))
     for chunk in range(len(parts)):
-        if chunk:
-            pieces[chunk], train_flat = lax.optimization_barrier((pieces[chunk], train_flat))
         made = condition(pieces[chunk], basis, in_basis, corrections)
         rows.append(exchanged(made, slices))
+    rows[0][:half], made = lax.optimization_barrier((rows[0][:half], made))
     came = []
-    half = slices // 2
     for chunk, part in enumerate(parts):
         each = part // slices
         groups = []

time: 93.5 us -> 92.6 us (level)
  starting transfers between devices: 38.3 us -> 34.5 us
  waiting for transfers between devices: 36.1 us -> 38.2 us
    ppermute x26, starting transfers between devices: 38.3 us -> 34.5 us  [crossed(): return lax.ppermute(value, axis, [(at, at ^ mask) for at in range(size)])]
    ppermute x26, waiting for transfers between devices: 36.1 us -> 38.2 us  [crossed(): return lax.ppermute(value, axis, [(at, at ^ mask) for at in range(size)])]
    unnamed x16 -> x14, local copies, waits for them, and re-layouts: 5.1 us -> 5.17 us
  transfers between devices with their start and end apart: 26 -> 26, of which waited for: 10 -> 8; matrix products, arithmetic and copies ran while one was open for 11% -> 12% of each run, Pallas kernels for 5% -> 5%
where the time goes in v10:
time: 92.6 us; the launch traced here: 92.3 us
  waiting for transfers between devices  38.2 us (41%)
  starting transfers between devices  34.5 us (37%)
  matrix products  6.66 us (7%)
  local copies, waits for them, and re-layouts  6.2 us (7%)
  Pallas kernels  4.45 us (5%)
  other arithmetic  1.82 us (2%)
    ppermute x26, waiting for transfers between devices, crossed(): return lax.ppermute(value, axis, [(at, at ^ mask) for at in range(size)])  38.2 us
    ppermute x26, starting transfers between devices, crossed(): return lax.ppermute(value, axis, [(at, at ^ mask) for at in range(size)])  34.5 us
    dot_general x8, matrix products, products(): lax.dot_general(block, train_flat, contract, preferred_element_type=jnp.f...  6.66 us
    unnamed x14, local copies, waits for them, and re-layouts  5.17 us
    pallas_call x2, Pallas kernels, condition_fast(): pl.pallas_call(functools.partial(condition_kernel, slices, rows_here), gr...  4.45 us
  transfers between devices with their start and end apart: 26, of which 8 were waited for; matrix products, arithmetic and copies ran while one was open for 12% of the time, Pallas kernels for 5%

profile of v10, /device:TPU:0, one launch (start us, length us, event | category | flops | bytes accessed | tf_op | source)
XLA Modules:
  0.0 92.3 jit_solution(4253054547092103325)
XLA Ops:
  0.0 1.2 %copy-done = bf16[256,16,128]{2,1,0:T(8,128)(2,1)S(1)} copy-done((bf16[256,16,128]{2,1,0:T(8,128)(2,1)S(1)}, bf16[256,16,128]{2,1,0:T(8,128)(2,1)}, u32[]{:S(2)}) %copy-start) | copy-done | bytes 1048600
  1.3 3.1 %collective-permute-start = (bf16[32,16,128]{2,1,0:T(8,128)(2,1)S(1)}, bf16[32,16,128]{2,1,0:T(8,128)(2,1)S(1)}, u32[]{:S(2)}, u32[]{:S(2)}) collective-permute-start(bf16[32,16,128]{2,1,0:T(8,128)(2,1)S(1)} %constant_dynamic-slice_fusion.6), channel_id=1, source_target_pairs={{0,1},{1,0},{2,3},{3,2},{4,5},{5,4},{6,7},{7,6},{8,9},{9,8},{10,11... | collective-permute-start | bytes 393224 | tf_op jit(solution)/shard_map/ppermute | solution.py:100
  4.4 2.5 %collective-permute-start.2 = (bf16[32,16,128]{2,1,0:T(8,128)(2,1)S(1)}, bf16[32,16,128]{2,1,0:T(8,128)(2,1)S(1)}, u32[]{:S(2)}, u32[]{:S(2)}) collective-permute-start(bf16[32,16,128]{2,1,0:T(8,128)(2,1)S(1)} %constant_dynamic-slice_fusion.4), channel_id=1, source_target_pairs={{0,3},{1,2},{2,1},{3,0},{4,7},{5,6},{6,5},{7,4},{8,11},{9,10},{10,... | collective-permute-start | bytes 393224 | tf_op jit(solution)/shard_map/ppermute | solution.py:100
  6.9 0.2 collective-permute-start.1
  7.1 0.7 fusion
  7.9 0.1 copy.13
  8.0 0.1 copy.14
  8.1 0.1 copy.15
  8.1 0.1 copy.16
  8.2 0.0 copy-start.1
  8.3 0.0 copy-start.2
  8.3 3.5 %copy.19 = bf16[64,8,16,128]{3,1,2,0:T(8,128)(2,1)} copy(bf16[64,8,16,128]{3,2,1,0:T(8,128)(2,1)} %bitcast.78) | data formatting | bytes 4194304
  11.8 0.1 pad_maximum_fusion.18
  11.9 0.1 copy.11.refs_4_
  11.9 0.0 copy-done.1
  12.0 0.1 copy.10
  12.1 0.0 collective-permute-done.refs_1_
  12.2 2.9 %collective-permute-start.6 = (bf16[32,16,128]{2,1,0:T(8,128)(2,1)S(1)}, bf16[32,16,128]{2,1,0:T(8,128)(2,1)S(1)}, u32[]{:S(2)}, u32[]{:S(2)}) collective-permute-start(bf16[32,16,128]{2,1,0:T(8,128)(2,1)S(1)} %constant_dynamic-slice_fusion), channel_id=1, source_target_pairs={{0,3},{1,2},{2,1},{3,0},{4,7},{5,6},{6,5},{7,4},{8,11},{9,10},{10,... | collective-permute-start | bytes 393224 | tf_op jit(solution)/shard_map/ppermute | solution.py:100
  15.1 0.3 collective-permute-start.5
  15.4 1.2 %collective-permute-start.4 = (bf16[32,16,128]{2,1,0:T(8,128)(2,1)S(1)}, bf16[32,16,128]{2,1,0:T(8,128)(2,1)S(1)}, u32[]{:S(2)}, u32[]{:S(2)}) collective-permute-start(bf16[32,16,128]{2,1,0:T(8,128)(2,1)S(1)} %constant_dynamic-slice_fusion.2), channel_id=1, source_target_pairs={{0,1},{1,0},{2,3},{3,2},{4,5},{5,4},{6,7},{7,6},{8,9},{9,8},{10,11... | collective-permute-start | bytes 393224 | tf_op jit(solution)/shard_map/ppermute | solution.py:100
  16.6 8.6 %collective-permute-done.1.refs_2_ = bf16[32,16,128]{2,1,0:T(8,128)(2,1)S(1)} collective-permute-done((bf16[32,16,128]{2,1,0:T(8,128)(2,1)S(1)}, bf16[32,16,128]{2,1,0:T(8,128)(2,1)S(1)}, u32[]{:S(2)}, u32[]{:S(2)}) %collective-permute-start.1) | collective-permute-done | bytes 131104 | tf_op jit(solution)/shard_map/ppermute | solution.py:100
  25.3 2.2 %shard_map.55 = (bf16[32,2048]{1,0:T(8,128)(2,1)S(1)}, bf16[32,2048]{1,0:T(8,128)(2,1)S(1)}, bf16[32,2048]{1,0:T(8,128)(2,1)S(1)}, bf16[32,2048]{1,0:T(8,128)(2,1)S(1)}) custom-call(bf16[32,16,128]{2,1,0:T(8,128)(2,1)S(1)} %constant_dynamic-slice_fusion.7.refs_0_, bf16[32,16,128]{2,1,0:T(8,128)(2,1)S(1)} %collective-permute-done.refs_1_, ...), custom_call_target="tpu_custom_call" | custom-call | tf_op jit(solution)/shard_map/pallas_call | solution.py:75
  27.5 0.1 collective-permute-start.3
  27.6 2.9 %collective-permute-start.10 = (bf16[32,2048]{1,0:T(8,128)(2,1)S(1)}, bf16[32,2048]{1,0:T(8,128)(2,1)S(1)}, u32[]{:S(2)}, u32[]{:S(2)}) collective-permute-start(bf16[32,2048]{1,0:T(8,128)(2,1)S(1)} %get-tuple-element.62), channel_id=1, source_target_pairs={{0,3},{1,2},{2,1},{3,0},{4,7},{5,6},{6,5},{7,4},{8,11},{9,10},{10,... | collective-permute-start | bytes 393224 | tf_op jit(solution)/shard_map/ppermute | solution.py:100
  30.6 0.5 collective-permute-start.9
  31.1 2.2 %shard_map.56 = (bf16[32,2048]{1,0:T(8,128)(2,1)S(1)}, bf16[32,2048]{1,0:T(8,128)(2,1)S(1)}, bf16[32,2048]{1,0:T(8,128)(2,1)S(1)}, bf16[32,2048]{1,0:T(8,128)(2,1)S(1)}) custom-call(bf16[32,16,128]{2,1,0:T(8,128)(2,1)S(1)} %constant_dynamic-slice_fusion.3.refs_0_, bf16[32,16,128]{2,1,0:T(8,128)(2,1)S(1)} %collective-permute-done.4.refs_1_, ...), custom_call_target="tpu_custom_call" | custom-call | tf_op jit(solution)/shard_map/pallas_call | solution.py:75
  33.3 1.1 %collective-permute-start.16 = (bf16[32,2048]{1,0:T(8,128)(2,1)S(1)}, bf16[32,2048]{1,0:T(8,128)(2,1)S(1)}, u32[]{:S(2)}, u32[]{:S(2)}) collective-permute-start(bf16[32,2048]{1,0:T(8,128)(2,1)S(1)} %get-tuple-element.55), channel_id=1, source_target_pairs={{0,1},{1,0},{2,3},{3,2},{4,5},{5,4},{6,7},{7,6},{8,9},{9,8},{10,11... | collective-permute-start | bytes 393224 | tf_op jit(solution)/shard_map/ppermute | solution.py:100
  34.4 2.4 %collective-permute-start.19 = (bf16[32,2048]{1,0:T(8,128)(2,1)S(1)}, bf16[32,2048]{1,0:T(8,128)(2,1)S(1)}, u32[]{:S(2)}, u32[]{:S(2)}) collective-permute-start(bf16[32,2048]{1,0:T(8,128)(2,1)S(1)} %get-tuple-element.56), channel_id=1, source_target_pairs={{0,2},{1,3},{2,0},{3,1},{4,6},{5,7},{6,4},{7,5},{8,10},{9,11},{10,... | collective-permute-start | bytes 393224 | tf_op jit(solution)/shard_map/ppermute | solution.py:100
  36.8 2.2 %collective-permute-start.20 = (bf16[32,2048]{1,0:T(8,128)(2,1)S(1)}, bf16[32,2048]{1,0:T(8,128)(2,1)S(1)}, u32[]{:S(2)}, u32[]{:S(2)}) collective-permute-start(bf16[32,2048]{1,0:T(8,128)(2,1)S(1)} %get-tuple-element.57), channel_id=1, source_target_pairs={{0,3},{1,2},{2,1},{3,0},{4,7},{5,6},{6,5},{7,4},{8,11},{9,10},{10,... | collective-permute-start | bytes 393224 | tf_op jit(solution)/shard_map/ppermute | solution.py:100
  39.0 1.6 %collective-permute-start.7 = (bf16[64,2048]{1,0:T(8,128)(2,1)S(1)}, bf16[64,2048]{1,0:T(8,128)(2,1)S(1)}, u32[]{:S(2)}, u32[]{:S(2)}) collective-permute-start(bf16[64,2048]{1,0:T(8,128)(2,1)S(1)} %pad_maximum_fusion.4), channel_id=1, source_target_pairs={{0,8},{4,12},{8,0},{12,4},{1,9},{5,13},{9,1},{13,5},{2,10},{6,14},... | collective-permute-start | bytes 786440 | tf_op jit(solution)/shard_map/ppermute | solution.py:100
  40.6 7.1 %collective-permute-done.9 = bf16[32,2048]{1,0:T(8,128)(2,1)S(1)} collective-permute-done((bf16[32,2048]{1,0:T(8,128)(2,1)S(1)}, bf16[32,2048]{1,0:T(8,128)(2,1)S(1)}, u32[]{:S(2)}, u32[]{:S(2)}) %collective-permute-start.9) | collective-permute-done | bytes 131104 | tf_op jit(solution)/shard_map/ppermute | solution.py:100
  47.7 1.6 %collective-permute-start.11 = (bf16[64,2048]{1,0:T(8,128)(2,1)S(1)}, bf16[64,2048]{1,0:T(8,128)(2,1)S(1)}, u32[]{:S(2)}, u32[]{:S(2)}) collective-permute-start(bf16[64,2048]{1,0:T(8,128)(2,1)S(1)} %pad_maximum_fusion.5), channel_id=1, source_target_pairs={{0,8},{4,12},{8,0},{12,4},{1,9},{5,13},{9,1},{13,5},{2,10},{6,14},... | collective-permute-start | bytes 786440 | tf_op jit(solution)/shard_map/ppermute | solution.py:100
  49.3 0.6 collective-permute-start.17
  49.9 0.6 collective-permute-done.19
  50.6 1.6 %collective-permute-start.21 = (bf16[64,2048]{1,0:T(8,128)(2,1)S(1)}, bf16[64,2048]{1,0:T(8,128)(2,1)S(1)}, u32[]{:S(2)}, u32[]{:S(2)}) collective-permute-start(bf16[64,2048]{1,0:T(8,128)(2,1)S(1)} %pad_maximum_fusion.8), channel_id=1, source_target_pairs={{0,8},{4,12},{8,0},{12,4},{1,9},{5,13},{9,1},{13,5},{2,10},{6,14},... | collective-permute-start | bytes 786440 | tf_op jit(solution)/shard_map/ppermute | solution.py:100
  52.2 0.1 collective-permute-start.8
  52.3 0.8 convolution_convert_fusion.5
  53.1 3.8 %collective-permute-done.11 = bf16[64,2048]{1,0:T(8,128)(2,1)S(1)} collective-permute-done((bf16[64,2048]{1,0:T(8,128)(2,1)S(1)}, bf16[64,2048]{1,0:T(8,128)(2,1)S(1)}, u32[]{:S(2)}, u32[]{:S(2)}) %collective-permute-start.11) | collective-permute-done | bytes 262176 | tf_op jit(solution)/shard_map/ppermute | solution.py:100
  57.0 0.8 convolution_convert_fusion.4
  57.8 0.1 collective-permute-start.12
  57.9 1.9 %collective-permute-done.17 = bf16[64,2048]{1,0:T(8,128)(2,1)S(1)} collective-permute-done((bf16[64,2048]{1,0:T(8,128)(2,1)S(1)}, bf16[64,2048]{1,0:T(8,128)(2,1)S(1)}, u32[]{:S(2)}, u32[]{:S(2)}) %collective-permute-start.17) | collective-permute-done | bytes 262176 | tf_op jit(solution)/shard_map/ppermute | solution.py:100
  59.9 0.8 convolution_convert_fusion.7
  60.7 0.8 convolution_convert_fusion.6
  61.6 0.1 broadcast_select_fusion.12
  61.7 1.4 %collective-permute-start.14 = (bf16[1,128,512]{2,1,0:T(8,128)(2,1)S(1)}, bf16[1,128,512]{2,1,0:T(8,128)(2,1)S(1)}, u32[]{:S(2)}, u32[]{:S(2)}) collective-permute-start(bf16[1,128,512]{2,1,0:T(8,128)(2,1)S(1)} %get-tuple-element.78), channel_id=1, source_target_pairs={{0,2},{1,3},{2,0},{3,1},{4,6},{5,7},{6,4},{7,5},{8,10},{9,11},{10,... | collective-permute-start | bytes 393224 | tf_op jit(solution)/shard_map/ppermute | solution.py:100
  63.2 0.1 broadcast_select_fusion.15
  63.3 1.5 %collective-permute-start.13 = (bf16[1,128,512]{2,1,0:T(8,128)(2,1)S(1)}, bf16[1,128,512]{2,1,0:T(8,128)(2,1)S(1)}, u32[]{:S(2)}, u32[]{:S(2)}) collective-permute-start(bf16[1,128,512]{2,1,0:T(8,128)(2,1)S(1)} %get-tuple-element.76), channel_id=1, source_target_pairs={{0,1},{1,0},{2,3},{3,2},{4,5},{5,4},{6,7},{7,6},{8,9},{9,8},{10,11... | collective-permute-start | bytes 393224 | tf_op jit(solution)/shard_map/ppermute | solution.py:100
  64.8 1.6 %collective-permute-start.15 = (bf16[1,128,512]{2,1,0:T(8,128)(2,1)S(1)}, bf16[1,128,512]{2,1,0:T(8,128)(2,1)S(1)}, u32[]{:S(2)}, u32[]{:S(2)}) collective-permute-start(bf16[1,128,512]{2,1,0:T(8,128)(2,1)S(1)} %get-tuple-element.77), channel_id=1, source_target_pairs={{0,3},{1,2},{2,1},{3,0},{4,7},{5,6},{6,5},{7,4},{8,11},{9,10},{10,... | collective-permute-start | bytes 393224 | tf_op jit(solution)/shard_map/ppermute | solution.py:100
  66.4 6.9 %collective-permute-done.14 = bf16[1,128,512]{2,1,0:T(8,128)(2,1)S(1)} collective-permute-done((bf16[1,128,512]{2,1,0:T(8,128)(2,1)S(1)}, bf16[1,128,512]{2,1,0:T(8,128)(2,1)S(1)}, u32[]{:S(2)}, u32[]{:S(2)}) %collective-permute-start.14) | collective-permute-done | bytes 131104 | tf_op jit(solution)/shard_map/ppermute | solution.py:100
  73.3 0.8 convolution_convert_fusion.1
  74.1 0.6 collective-permute-start.22
  74.7 0.1 broadcast_select_fusion.31
  74.8 0.8 convolution_convert_fusion
  75.7 0.8 convolution_convert_fusion.3
  76.5 0.8 convolution_convert_fusion.2
  77.4 0.1 broadcast_select_fusion.11
  77.5 0.1 broadcast_select_fusion.9
  77.6 1.3 %collective-permute-start.23 = (bf16[1,128,512]{2,1,0:T(8,128)(2,1)S(1)}, bf16[1,128,512]{2,1,0:T(8,128)(2,1)S(1)}, u32[]{:S(2)}, u32[]{:S(2)}) collective-permute-start(bf16[1,128,512]{2,1,0:T(8,128)(2,1)S(1)} %get-tuple-element.80), channel_id=1, source_target_pairs={{0,1},{1,0},{2,3},{3,2},{4,5},{5,4},{6,7},{7,6},{8,9},{9,8},{10,11... | collective-permute-start | bytes 393224 | tf_op jit(solution)/shard_map/ppermute | solution.py:100
  78.9 1.5 %collective-permute-start.24 = (bf16[1,128,512]{2,1,0:T(8,128)(2,1)S(1)}, bf16[1,128,512]{2,1,0:T(8,128)(2,1)S(1)}, u32[]{:S(2)}, u32[]{:S(2)}) collective-permute-start(bf16[1,128,512]{2,1,0:T(8,128)(2,1)S(1)} %get-tuple-element.81), channel_id=1, source_target_pairs={{0,2},{1,3},{2,0},{3,1},{4,6},{5,7},{6,4},{7,5},{8,10},{9,11},{10,... | collective-permute-start | bytes 393224 | tf_op jit(solution)/shard_map/ppermute | solution.py:100
  80.5 1.6 %collective-permute-start.25 = (bf16[1,128,512]{2,1,0:T(8,128)(2,1)S(1)}, bf16[1,128,512]{2,1,0:T(8,128)(2,1)S(1)}, u32[]{:S(2)}, u32[]{:S(2)}) collective-permute-start(bf16[1,128,512]{2,1,0:T(8,128)(2,1)S(1)} %get-tuple-element.82), channel_id=1, source_target_pairs={{0,3},{1,2},{2,1},{3,0},{4,7},{5,6},{6,5},{7,4},{8,11},{9,10},{10,... | collective-permute-start | bytes 393224 | tf_op jit(solution)/shard_map/ppermute | solution.py:100
  82.1 2.8 %collective-permute-done.23 = bf16[1,128,512]{2,1,0:T(8,128)(2,1)S(1)} collective-permute-done((bf16[1,128,512]{2,1,0:T(8,128)(2,1)S(1)}, bf16[1,128,512]{2,1,0:T(8,128)(2,1)S(1)}, u32[]{:S(2)}, u32[]{:S(2)}) %collective-permute-start.23) | collective-permute-done | bytes 131104 | tf_op jit(solution)/shard_map/ppermute | solution.py:100
  84.9 6.4 %collective-permute-done.24 = bf16[1,128,512]{2,1,0:T(8,128)(2,1)S(1)} collective-permute-done((bf16[1,128,512]{2,1,0:T(8,128)(2,1)S(1)}, bf16[1,128,512]{2,1,0:T(8,128)(2,1)S(1)}, u32[]{:S(2)}, u32[]{:S(2)}) %collective-permute-start.24) | collective-permute-done | bytes 131104 | tf_op jit(solution)/shard_map/ppermute | solution.py:100
  91.4 0.1 broadcast_select_fusion.27
  91.5 0.8 maximum_bitcast_fusion
  (50 shorter events, 0.6 us)
Async XLA Ops:
  0.0 1.2 %copy-start = (bf16[256,16,128]{2,1,0:T(8,128)(2,1)S(1)}, bf16[256,16,128]{2,1,0:T(8,128)(2,1)}, u32[]{:S(2)}) copy-start(bf16[256,16,128]{2,1,0:T(8,128)(2,1)} %param.5) | copy-start | bytes 3145732
  1.3 10.8 %collective-permute-start = (bf16[32,16,128]{2,1,0:T(8,128)(2,1)S(1)}, bf16[32,16,128]{2,1,0:T(8,128)(2,1)S(1)}, u32[]{:S(2)}, u32[]{:S(2)}) collective-permute-start(bf16[32,16,128]{2,1,0:T(8,128)(2,1)S(1)} %constant_dynamic-slice_fusion.6), channel_id=1, source_target_pairs={{0,1},{1,0},{2,3},{3,2},{4,5},{5,4},{6,7},{7,6},{8,9},{9,8},{10,11... | collective-permute-start | bytes 393224 | tf_op jit(solution)/shard_map/ppermute | solution.py:100
  4.4 12.2 %collective-permute-start.2 = (bf16[32,16,128]{2,1,0:T(8,128)(2,1)S(1)}, bf16[32,16,128]{2,1,0:T(8,128)(2,1)S(1)}, u32[]{:S(2)}, u32[]{:S(2)}) collective-permute-start(bf16[32,16,128]{2,1,0:T(8,128)(2,1)S(1)} %constant_dynamic-slice_fusion.4), channel_id=1, source_target_pairs={{0,3},{1,2},{2,1},{3,0},{4,7},{5,6},{6,5},{7,4},{8,11},{9,10},{10,... | collective-permute-start | bytes 393224 | tf_op jit(solution)/shard_map/ppermute | solution.py:100
  6.9 18.3 %collective-permute-start.1 = (bf16[32,16,128]{2,1,0:T(8,128)(2,1)S(1)}, bf16[32,16,128]{2,1,0:T(8,128)(2,1)S(1)}, u32[]{:S(2)}, u32[]{:S(2)}) collective-permute-start(bf16[32,16,128]{2,1,0:T(8,128)(2,1)S(1)} %constant_dynamic-slice_fusion.5), channel_id=1, source_target_pairs={{0,2},{1,3},{2,0},{3,1},{4,6},{5,7},{6,4},{7,5},{8,10},{9,11},{10,... | collective-permute-start | bytes 393224 | tf_op jit(solution)/shard_map/ppermute | solution.py:100
  8.2 3.7 %copy-start.1 = (f32[128,128]{1,0:T(8,128)S(1)}, f32[128,128]{1,0:T(8,128)}, u32[]{:S(2)}) copy-start(f32[128,128]{1,0:T(8,128)} %refs_6_.3) | copy-start | bytes 196612
  8.3 17.0 %copy-start.2 = (f32[64,128]{1,0:T(8,128)S(1)}, f32[64,128]{1,0:T(8,128)}, u32[]{:S(2)}) copy-start(f32[64,128]{1,0:T(8,128)} %refs_8_.3) | copy-start | bytes 98308
  12.2 18.4 %collective-permute-start.6 = (bf16[32,16,128]{2,1,0:T(8,128)(2,1)S(1)}, bf16[32,16,128]{2,1,0:T(8,128)(2,1)S(1)}, u32[]{:S(2)}, u32[]{:S(2)}) collective-permute-start(bf16[32,16,128]{2,1,0:T(8,128)(2,1)S(1)} %constant_dynamic-slice_fusion), channel_id=1, source_target_pairs={{0,3},{1,2},{2,1},{3,0},{4,7},{5,6},{6,5},{7,4},{8,11},{9,10},{10,... | collective-permute-start | bytes 393224 | tf_op jit(solution)/shard_map/ppermute | solution.py:100
  15.1 16.0 %collective-permute-start.5 = (bf16[32,16,128]{2,1,0:T(8,128)(2,1)S(1)}, bf16[32,16,128]{2,1,0:T(8,128)(2,1)S(1)}, u32[]{:S(2)}, u32[]{:S(2)}) collective-permute-start(bf16[32,16,128]{2,1,0:T(8,128)(2,1)S(1)} %constant_dynamic-slice_fusion.1), channel_id=1, source_target_pairs={{0,2},{1,3},{2,0},{3,1},{4,6},{5,7},{6,4},{7,5},{8,10},{9,11},{10,... | collective-permute-start | bytes 393224 | tf_op jit(solution)/shard_map/ppermute | solution.py:100
  15.4 15.6 %collective-permute-start.4 = (bf16[32,16,128]{2,1,0:T(8,128)(2,1)S(1)}, bf16[32,16,128]{2,1,0:T(8,128)(2,1)S(1)}, u32[]{:S(2)}, u32[]{:S(2)}) collective-permute-start(bf16[32,16,128]{2,1,0:T(8,128)(2,1)S(1)} %constant_dynamic-slice_fusion.2), channel_id=1, source_target_pairs={{0,1},{1,0},{2,3},{3,2},{4,5},{5,4},{6,7},{7,6},{8,9},{9,8},{10,11... | collective-permute-start | bytes 393224 | tf_op jit(solution)/shard_map/ppermute | solution.py:100
  27.5 9.3 %collective-permute-start.3 = (bf16[32,2048]{1,0:T(8,128)(2,1)S(1)}, bf16[32,2048]{1,0:T(8,128)(2,1)S(1)}, u32[]{:S(2)}, u32[]{:S(2)}) collective-permute-start(bf16[32,2048]{1,0:T(8,128)(2,1)S(1)} %get-tuple-element.45), channel_id=1, source_target_pairs={{0,1},{1,0},{2,3},{3,2},{4,5},{5,4},{6,7},{7,6},{8,9},{9,8},{10,11... | collective-permute-start | bytes 393224 | tf_op jit(solution)/shard_map/ppermute | solution.py:100
  27.6 24.6 %copy-start.3 = (bf16[64,8,16,128]{3,1,2,0:T(8,128)(2,1)S(1)}, bf16[64,8,16,128]{3,1,2,0:T(8,128)(2,1)}, u32[]{:S(2)}) copy-start(bf16[64,8,16,128]{3,1,2,0:T(8,128)(2,1)} %copy.19) | copy-start | bytes 6291460
  27.6 11.4 %collective-permute-start.10 = (bf16[32,2048]{1,0:T(8,128)(2,1)S(1)}, bf16[32,2048]{1,0:T(8,128)(2,1)S(1)}, u32[]{:S(2)}, u32[]{:S(2)}) collective-permute-start(bf16[32,2048]{1,0:T(8,128)(2,1)S(1)} %get-tuple-element.62), channel_id=1, source_target_pairs={{0,3},{1,2},{2,1},{3,0},{4,7},{5,6},{6,5},{7,4},{8,11},{9,10},{10,... | collective-permute-start | bytes 393224 | tf_op jit(solution)/shard_map/ppermute | solution.py:100
  30.6 17.2 %collective-permute-start.9 = (bf16[32,2048]{1,0:T(8,128)(2,1)S(1)}, bf16[32,2048]{1,0:T(8,128)(2,1)S(1)}, u32[]{:S(2)}, u32[]{:S(2)}) collective-permute-start(bf16[32,2048]{1,0:T(8,128)(2,1)S(1)} %get-tuple-element.61), channel_id=1, source_target_pairs={{0,2},{1,3},{2,0},{3,1},{4,6},{5,7},{6,4},{7,5},{8,10},{9,11},{10,... | collective-permute-start | bytes 393224 | tf_op jit(solution)/shard_map/ppermute | solution.py:100
  33.3 16.0 %collective-permute-start.16 = (bf16[32,2048]{1,0:T(8,128)(2,1)S(1)}, bf16[32,2048]{1,0:T(8,128)(2,1)S(1)}, u32[]{:S(2)}, u32[]{:S(2)}) collective-permute-start(bf16[32,2048]{1,0:T(8,128)(2,1)S(1)} %get-tuple-element.55), channel_id=1, source_target_pairs={{0,1},{1,0},{2,3},{3,2},{4,5},{5,4},{6,7},{7,6},{8,9},{9,8},{10,11... | collective-permute-start | bytes 393224 | tf_op jit(solution)/shard_map/ppermute | solution.py:100
  34.4 16.1 %collective-permute-start.19 = (bf16[32,2048]{1,0:T(8,128)(2,1)S(1)}, bf16[32,2048]{1,0:T(8,128)(2,1)S(1)}, u32[]{:S(2)}, u32[]{:S(2)}) collective-permute-start(bf16[32,2048]{1,0:T(8,128)(2,1)S(1)} %get-tuple-element.56), channel_id=1, source_target_pairs={{0,2},{1,3},{2,0},{3,1},{4,6},{5,7},{6,4},{7,5},{8,10},{9,11},{10,... | collective-permute-start | bytes 393224 | tf_op jit(solution)/shard_map/ppermute | solution.py:100
  36.8 13.7 %collective-permute-start.20 = (bf16[32,2048]{1,0:T(8,128)(2,1)S(1)}, bf16[32,2048]{1,0:T(8,128)(2,1)S(1)}, u32[]{:S(2)}, u32[]{:S(2)}) collective-permute-start(bf16[32,2048]{1,0:T(8,128)(2,1)S(1)} %get-tuple-element.57), channel_id=1, source_target_pairs={{0,3},{1,2},{2,1},{3,0},{4,7},{5,6},{6,5},{7,4},{8,11},{9,10},{10,... | collective-permute-start | bytes 393224 | tf_op jit(solution)/shard_map/ppermute | solution.py:100
  39.0 13.1 %collective-permute-start.7 = (bf16[64,2048]{1,0:T(8,128)(2,1)S(1)}, bf16[64,2048]{1,0:T(8,128)(2,1)S(1)}, u32[]{:S(2)}, u32[]{:S(2)}) collective-permute-start(bf16[64,2048]{1,0:T(8,128)(2,1)S(1)} %pad_maximum_fusion.4), channel_id=1, source_target_pairs={{0,8},{4,12},{8,0},{12,4},{1,9},{5,13},{9,1},{13,5},{2,10},{6,14},... | collective-permute-start | bytes 786440 | tf_op jit(solution)/shard_map/ppermute | solution.py:100
  47.7 9.2 %collective-permute-start.11 = (bf16[64,2048]{1,0:T(8,128)(2,1)S(1)}, bf16[64,2048]{1,0:T(8,128)(2,1)S(1)}, u32[]{:S(2)}, u32[]{:S(2)}) collective-permute-start(bf16[64,2048]{1,0:T(8,128)(2,1)S(1)} %pad_maximum_fusion.5), channel_id=1, source_target_pairs={{0,8},{4,12},{8,0},{12,4},{1,9},{5,13},{9,1},{13,5},{2,10},{6,14},... | collective-permute-start | bytes 786440 | tf_op jit(solution)/shard_map/ppermute | solution.py:100
  49.3 10.5 %collective-permute-start.17 = (bf16[64,2048]{1,0:T(8,128)(2,1)S(1)}, bf16[64,2048]{1,0:T(8,128)(2,1)S(1)}, u32[]{:S(2)}, u32[]{:S(2)}) collective-permute-start(bf16[64,2048]{1,0:T(8,128)(2,1)S(1)} %pad_maximum_fusion.7), channel_id=1, source_target_pairs={{0,8},{4,12},{8,0},{12,4},{1,9},{5,13},{9,1},{13,5},{2,10},{6,14},... | collective-permute-start | bytes 786440 | tf_op jit(solution)/shard_map/ppermute | solution.py:100
  50.6 12.6 %collective-permute-start.21 = (bf16[64,2048]{1,0:T(8,128)(2,1)S(1)}, bf16[64,2048]{1,0:T(8,128)(2,1)S(1)}, u32[]{:S(2)}, u32[]{:S(2)}) collective-permute-start(bf16[64,2048]{1,0:T(8,128)(2,1)S(1)} %pad_maximum_fusion.8), channel_id=1, source_target_pairs={{0,8},{4,12},{8,0},{12,4},{1,9},{5,13},{9,1},{13,5},{2,10},{6,14},... | collective-permute-start | bytes 786440 | tf_op jit(solution)/shard_map/ppermute | solution.py:100
  52.2 7.7 %collective-permute-start.8 = (bf16[128,2048]{1,0:T(8,128)(2,1)S(1)}, bf16[128,2048]{1,0:T(8,128)(2,1)S(1)}, u32[]{:S(2)}, u32[]{:S(2)}) collective-permute-start(bf16[128,2048]{1,0:T(8,128)(2,1)S(1)} %pad_maximum_fusion), channel_id=1, source_target_pairs={{0,4},{4,0},{8,12},{12,8},{1,5},{5,1},{9,13},{13,9},{2,6},{6,2},{1... | collective-permute-start | bytes 1572872 | tf_op jit(solution)/shard_map/ppermute | solution.py:100
  57.8 2.9 %collective-permute-start.12 = (bf16[128,2048]{1,0:T(8,128)(2,1)S(1)}, bf16[128,2048]{1,0:T(8,128)(2,1)S(1)}, u32[]{:S(2)}, u32[]{:S(2)}) collective-permute-start(bf16[128,2048]{1,0:T(8,128)(2,1)S(1)} %pad_maximum_fusion.1), channel_id=1, source_target_pairs={{0,4},{4,0},{8,12},{12,8},{1,5},{5,1},{9,13},{13,9},{2,6},{6,2},{1... | collective-permute-start | bytes 1572872 | tf_op jit(solution)/shard_map/ppermute | solution.py:100
  61.7 11.6 %collective-permute-start.14 = (bf16[1,128,512]{2,1,0:T(8,128)(2,1)S(1)}, bf16[1,128,512]{2,1,0:T(8,128)(2,1)S(1)}, u32[]{:S(2)}, u32[]{:S(2)}) collective-permute-start(bf16[1,128,512]{2,1,0:T(8,128)(2,1)S(1)} %get-tuple-element.78), channel_id=1, source_target_pairs={{0,2},{1,3},{2,0},{3,1},{4,6},{5,7},{6,4},{7,5},{8,10},{9,11},{10,... | collective-permute-start | bytes 393224 | tf_op jit(solution)/shard_map/ppermute | solution.py:100
  63.3 11.4 %collective-permute-start.13 = (bf16[1,128,512]{2,1,0:T(8,128)(2,1)S(1)}, bf16[1,128,512]{2,1,0:T(8,128)(2,1)S(1)}, u32[]{:S(2)}, u32[]{:S(2)}) collective-permute-start(bf16[1,128,512]{2,1,0:T(8,128)(2,1)S(1)} %get-tuple-element.76), channel_id=1, source_target_pairs={{0,1},{1,0},{2,3},{3,2},{4,5},{5,4},{6,7},{7,6},{8,9},{9,8},{10,11... | collective-permute-start | bytes 393224 | tf_op jit(solution)/shard_map/ppermute | solution.py:100
  64.8 9.9 %collective-permute-start.15 = (bf16[1,128,512]{2,1,0:T(8,128)(2,1)S(1)}, bf16[1,128,512]{2,1,0:T(8,128)(2,1)S(1)}, u32[]{:S(2)}, u32[]{:S(2)}) collective-permute-start(bf16[1,128,512]{2,1,0:T(8,128)(2,1)S(1)} %get-tuple-element.77), channel_id=1, source_target_pairs={{0,3},{1,2},{2,1},{3,0},{4,7},{5,6},{6,5},{7,4},{8,11},{9,10},{10,... | collective-permute-start | bytes 393224 | tf_op jit(solution)/shard_map/ppermute | solution.py:100
  73.3 2.4 %collective-permute-start.18 = (bf16[128,2048]{1,0:T(8,128)(2,1)S(1)}, bf16[128,2048]{1,0:T(8,128)(2,1)S(1)}, u32[]{:S(2)}, u32[]{:S(2)}) collective-permute-start(bf16[128,2048]{1,0:T(8,128)(2,1)S(1)} %pad_maximum_fusion.2), channel_id=1, source_target_pairs={{0,4},{4,0},{8,12},{12,8},{1,5},{5,1},{9,13},{13,9},{2,6},{6,2},{1... | collective-permute-start | bytes 1572872 | tf_op jit(solution)/shard_map/ppermute | solution.py:100
  74.1 2.4 %collective-permute-start.22 = (bf16[128,2048]{1,0:T(8,128)(2,1)S(1)}, bf16[128,2048]{1,0:T(8,128)(2,1)S(1)}, u32[]{:S(2)}, u32[]{:S(2)}) collective-permute-start(bf16[128,2048]{1,0:T(8,128)(2,1)S(1)} %pad_maximum_fusion.3), channel_id=1, source_target_pairs={{0,4},{4,0},{8,12},{12,8},{1,5},{5,1},{9,13},{13,9},{2,6},{6,2},{1... | collective-permute-start | bytes 1572872 | tf_op jit(solution)/shard_map/ppermute | solution.py:100
  77.6 7.3 %collective-permute-start.23 = (bf16[1,128,512]{2,1,0:T(8,128)(2,1)S(1)}, bf16[1,128,512]{2,1,0:T(8,128)(2,1)S(1)}, u32[]{:S(2)}, u32[]{:S(2)}) collective-permute-start(bf16[1,128,512]{2,1,0:T(8,128)(2,1)S(1)} %get-tuple-element.80), channel_id=1, source_target_pairs={{0,1},{1,0},{2,3},{3,2},{4,5},{5,4},{6,7},{7,6},{8,9},{9,8},{10,11... | collective-permute-start | bytes 393224 | tf_op jit(solution)/shard_map/ppermute | solution.py:100
  78.9 12.4 %collective-permute-start.24 = (bf16[1,128,512]{2,1,0:T(8,128)(2,1)S(1)}, bf16[1,128,512]{2,1,0:T(8,128)(2,1)S(1)}, u32[]{:S(2)}, u32[]{:S(2)}) collective-permute-start(bf16[1,128,512]{2,1,0:T(8,128)(2,1)S(1)} %get-tuple-element.81), channel_id=1, source_target_pairs={{0,2},{1,3},{2,0},{3,1},{4,6},{5,7},{6,4},{7,5},{8,10},{9,11},{10,... | collective-permute-start | bytes 393224 | tf_op jit(solution)/shard_map/ppermute | solution.py:100
  80.5 10.9 %collective-permute-start.25 = (bf16[1,128,512]{2,1,0:T(8,128)(2,1)S(1)}, bf16[1,128,512]{2,1,0:T(8,128)(2,1)S(1)}, u32[]{:S(2)}, u32[]{:S(2)}) collective-permute-start(bf16[1,128,512]{2,1,0:T(8,128)(2,1)S(1)} %get-tuple-element.82), channel_id=1, source_target_pairs={{0,3},{1,2},{2,1},{3,0},{4,7},{5,6},{6,5},{7,4},{8,11},{9,10},{10,... | collective-permute-start | bytes 393224 | tf_op jit(solution)/shard_map/ppermute | solution.py:100

commit v11 on v10

--- a/solution.py
+++ b/solution.py
@@ -31,7 +31,7 @@
 
 
 def condition_kernel(slices, rows_here, *refs):
-    pieces = refs[:slices]
+    pieces = refs[:slices][::-1]
     basis, across, right_basis, right_across, corrections = refs[slices:slices + 5]
     outs, stage = refs[slices + 5:-1], refs[-1]
     enter, leave = three_wide(across[...]), three_wide(basis[...])
@@ -81,7 +81,7 @@
         scratch_shapes=[pltpu.VMEM((block * order, columns), jnp.float32)],
         compiler_params=pltpu.CompilerParams(vmem_limit_bytes=32 * 1024 * 1024),
         cost_estimate=pl.CostEstimate(flops=0, bytes_accessed=0, transcendentals=0),
-    )(*pieces, basis, basis.T, in_basis, in_basis.T, corrections)
+    )(*pieces[::-1], basis, basis.T, in_basis, in_basis.T, corrections)
 
 
 def condition_plain(pieces, basis, in_basis, corrections):
@@ -109,8 +109,9 @@
     return lax.optimization_barrier((value, tokens))[0]
 
 
-def spread_shares(near, shares):
-    return jnp.concatenate([near] + [crossed(near, "dp", shares, mask) for mask in range(2, shares, 2)], axis=0)
+def spread_shares(near, shares, tokens):
+    parts = [near] + [crossed(near, "dp", shares, mask) for mask in range(2, shares, 2)]
+    return lax.optimization_barrier(jnp.concatenate(after(parts, *tokens), axis=0))
 
 
 def products(near, far, train_flat, shares):
@@ -151,12 +152,11 @@
     for chunk, part in enumerate(parts):
         first, each = sum(parts[:chunk]), part // slices
         if chunk:
-            source, pieces[0][1], train_flat = lax.optimization_barrier((source, pieces[0][1], train_flat))
-        raw = []
-        for mask in range(slices):
+            source, pieces[0][-1], train_flat = lax.optimization_barrier((source, pieces[0][-1], train_flat))
+        raw = {}
+        for mask in (reversed(range(slices)) if chunk else range(slices)):
             block = lax.dynamic_slice_in_dim(source, first + (here ^ mask) * each, each, 0)
-            block, source = lax.optimization_barrier((block, source))
-            raw.append(block)
+            raw[mask], source = lax.optimization_barrier((block, source))
         pieces.append(exchanged(raw, slices))
     for chunk in range(len(parts)):
         made = condition(pieces[chunk], basis, in_basis, corrections)
@@ -167,10 +167,12 @@
         each = part // slices
         groups = []
         for group in (rows[chunk][:half], rows[chunk][half:]):
-            near = spread_shares(jnp.concatenate(group, axis=0), shares)
-            near = after(near, *came[2:3])
+            if chunk and groups:
+                group = after(group, near_before)
+            near = spread_shares(jnp.concatenate(group, axis=0), shares, came[2:3])
             far = crossed(near, "dp", shares, 1)
             groups.append(products(near, far, train_flat, shares))
+        near_before = near
         values = [jnp.concatenate(pair, axis=0) for pair in zip(*groups)]
         values = [jnp.stack(values[at * owned:(at + 1) * owned]) for at in range(slices)]
         came = exchanged(turned(values, here ^ (share // owned)), slices)

time: 92.6 us -> 91.7 us (level)
  waiting for transfers between devices: 38.2 us -> 27.2 us
  starting transfers between devices: 34.5 us -> 45.3 us
    ppermute x26, waiting for transfers between devices: 38.2 us -> 27.2 us  [crossed(): return lax.ppermute(value, axis, [(at, at ^ mask) for at in range(size)])]
    ppermute x26, starting transfers between devices: 34.5 us -> 45.3 us  [crossed(): return lax.ppermute(value, axis, [(at, at ^ mask) for at in range(size)])]
    unnamed x14 -> x20, local copies, waits for them, and re-layouts: 5.17 us -> 5.21 us
where the time goes in v11:
time: 91.7 us; the launch traced here: 91.5 us
  starting transfers between devices  45.3 us (49%)
  waiting for transfers between devices  27.2 us (30%)
  matrix products  6.66 us (7%)
  local copies, waits for them, and re-layouts  5.54 us (6%)
  Pallas kernels  4.46 us (5%)
  other arithmetic  1.74 us (2%)
    ppermute x26, starting transfers between devices, crossed(): return lax.ppermute(value, axis, [(at, at ^ mask) for at in range(size)])  45.3 us
    ppermute x26, waiting for transfers between devices, crossed(): return lax.ppermute(value, axis, [(at, at ^ mask) for at in range(size)])  27.2 us
    dot_general x8, matrix products, products(): lax.dot_general(block, train_flat, contract, preferred_element_type=jnp.f...  6.66 us
    unnamed x20, local copies, waits for them, and re-layouts  5.21 us
    pallas_call x2, Pallas kernels, condition_fast(): pl.pallas_call(functools.partial(condition_kernel, slices, rows_here), gr...  4.46 us
  transfers between devices with their start and end apart: 26, of which 8 were waited for; matrix products, arithmetic and copies ran while one was open for 12% of the time, Pallas kernels for 5%

profile of v11, /device:TPU:0, one launch (start us, length us, event | category | flops | bytes accessed | tf_op | source)
XLA Modules:
  0.0 91.5 jit_solution(1757681365587348127)
XLA Ops:
  0.0 1.2 %copy-done = bf16[256,16,128]{2,1,0:T(8,128)(2,1)S(1)} copy-done((bf16[256,16,128]{2,1,0:T(8,128)(2,1)S(1)}, bf16[256,16,128]{2,1,0:T(8,128)(2,1)}, u32[]{:S(2)}) %copy-start) | copy-done | bytes 1048600
  1.3 5.1 %collective-permute-start = (bf16[32,16,128]{2,1,0:T(8,128)(2,1)S(1)}, bf16[32,16,128]{2,1,0:T(8,128)(2,1)S(1)}, u32[]{:S(2)}, u32[]{:S(2)}) collective-permute-start(bf16[32,16,128]{2,1,0:T(8,128)(2,1)S(1)} %constant_dynamic-slice_fusion.4), channel_id=1, source_target_pairs={{0,3},{1,2},{2,1},{3,0},{4,7},{5,6},{6,5},{7,4},{8,11},{9,10},{10,... | collective-permute-start | bytes 393224 | tf_op jit(solution)/shard_map/ppermute | solution.py:100
  6.4 0.6 collective-permute-start.2
  7.1 3.5 %copy.19 = bf16[64,8,16,128]{3,1,2,0:T(8,128)(2,1)} copy(bf16[64,8,16,128]{3,2,1,0:T(8,128)(2,1)} %bitcast.78) | data formatting | bytes 4194304
  10.6 0.1 copy.13
  10.7 0.1 copy.14
  10.8 0.1 copy.15
  10.9 0.1 copy.16
  11.0 0.0 collective-permute-done.refs_0_
  11.1 5.3 %collective-permute-start.6 = (bf16[32,16,128]{2,1,0:T(8,128)(2,1)S(1)}, bf16[32,16,128]{2,1,0:T(8,128)(2,1)S(1)}, u32[]{:S(2)}, u32[]{:S(2)}) collective-permute-start(bf16[32,16,128]{2,1,0:T(8,128)(2,1)S(1)} %constant_dynamic-slice_fusion.1), channel_id=1, source_target_pairs={{0,1},{1,0},{2,3},{3,2},{4,5},{5,4},{6,7},{7,6},{8,9},{9,8},{10,11... | collective-permute-start | bytes 393224 | tf_op jit(solution)/shard_map/ppermute | solution.py:100
  16.4 1.3 %collective-permute-start.5 = (bf16[32,16,128]{2,1,0:T(8,128)(2,1)S(1)}, bf16[32,16,128]{2,1,0:T(8,128)(2,1)S(1)}, u32[]{:S(2)}, u32[]{:S(2)}) collective-permute-start(bf16[32,16,128]{2,1,0:T(8,128)(2,1)S(1)} %constant_dynamic-slice_fusion.2), channel_id=1, source_target_pairs={{0,2},{1,3},{2,0},{3,1},{4,6},{5,7},{6,4},{7,5},{8,10},{9,11},{10,... | collective-permute-start | bytes 393224 | tf_op jit(solution)/shard_map/ppermute | solution.py:100
  17.6 1.4 %collective-permute-start.4 = (bf16[32,16,128]{2,1,0:T(8,128)(2,1)S(1)}, bf16[32,16,128]{2,1,0:T(8,128)(2,1)S(1)}, u32[]{:S(2)}, u32[]{:S(2)}) collective-permute-start(bf16[32,16,128]{2,1,0:T(8,128)(2,1)S(1)} %constant_dynamic-slice_fusion.3), channel_id=1, source_target_pairs={{0,3},{1,2},{2,1},{3,0},{4,7},{5,6},{6,5},{7,4},{8,11},{9,10},{10,... | collective-permute-start | bytes 393224 | tf_op jit(solution)/shard_map/ppermute | solution.py:100
  19.0 0.1 pad_maximum_fusion.14
  19.2 0.1 copy.11.refs_4_
  19.3 0.1 copy.10
  19.4 0.0 collective-permute-done.1.refs_1_
  19.4 2.2 %shard_map.55 = (bf16[32,2048]{1,0:T(8,128)(2,1)S(1)}, bf16[32,2048]{1,0:T(8,128)(2,1)S(1)}, bf16[32,2048]{1,0:T(8,128)(2,1)S(1)}, bf16[32,2048]{1,0:T(8,128)(2,1)S(1)}) custom-call(bf16[32,16,128]{2,1,0:T(8,128)(2,1)S(1)} %collective-permute-done.refs_0_, bf16[32,16,128]{2,1,0:T(8,128)(2,1)S(1)} %collective-permute-done.1.refs_1_, ...), custom_call_target="tpu_custom_call" | custom-call | tf_op jit(solution)/shard_map/pallas_call | solution.py:75
  21.7 0.9 collective-permute-start.3
  22.6 3.5 %collective-permute-start.9 = (bf16[32,2048]{1,0:T(8,128)(2,1)S(1)}, bf16[32,2048]{1,0:T(8,128)(2,1)S(1)}, u32[]{:S(2)}, u32[]{:S(2)}) collective-permute-start(bf16[32,2048]{1,0:T(8,128)(2,1)S(1)} %get-tuple-element.71), channel_id=1, source_target_pairs={{0,2},{1,3},{2,0},{3,1},{4,6},{5,7},{6,4},{7,5},{8,10},{9,11},{10,... | collective-permute-start | bytes 393224 | tf_op jit(solution)/shard_map/ppermute | solution.py:100
  26.0 0.0 collective-permute-done.6.refs_2_
  26.0 0.2 collective-permute-start.10
  26.2 1.8 %collective-permute-done.5.refs_1_ = bf16[32,16,128]{2,1,0:T(8,128)(2,1)S(1)} collective-permute-done((bf16[32,16,128]{2,1,0:T(8,128)(2,1)S(1)}, bf16[32,16,128]{2,1,0:T(8,128)(2,1)S(1)}, u32[]{:S(2)}, u32[]{:S(2)}) %collective-permute-start.5) | collective-permute-done | bytes 131104 | tf_op jit(solution)/shard_map/ppermute | solution.py:100
  28.0 2.2 %shard_map.56 = (bf16[32,2048]{1,0:T(8,128)(2,1)S(1)}, bf16[32,2048]{1,0:T(8,128)(2,1)S(1)}, bf16[32,2048]{1,0:T(8,128)(2,1)S(1)}, bf16[32,2048]{1,0:T(8,128)(2,1)S(1)}) custom-call(bf16[32,16,128]{2,1,0:T(8,128)(2,1)S(1)} %collective-permute-done.4.refs_0_, bf16[32,16,128]{2,1,0:T(8,128)(2,1)S(1)} %collective-permute-done.5.refs_1_, ...), custom_call_target="tpu_custom_call" | custom-call | tf_op jit(solution)/shard_map/pallas_call | solution.py:75
  30.2 7.6 %collective-permute-start.16 = (bf16[32,2048]{1,0:T(8,128)(2,1)S(1)}, bf16[32,2048]{1,0:T(8,128)(2,1)S(1)}, u32[]{:S(2)}, u32[]{:S(2)}) collective-permute-start(bf16[32,2048]{1,0:T(8,128)(2,1)S(1)} %get-tuple-element.63), channel_id=1, source_target_pairs={{0,1},{1,0},{2,3},{3,2},{4,5},{5,4},{6,7},{7,6},{8,9},{9,8},{10,11... | collective-permute-start | bytes 393224 | tf_op jit(solution)/shard_map/ppermute | solution.py:100
  37.8 2.0 %collective-permute-start.19 = (bf16[32,2048]{1,0:T(8,128)(2,1)S(1)}, bf16[32,2048]{1,0:T(8,128)(2,1)S(1)}, u32[]{:S(2)}, u32[]{:S(2)}) collective-permute-start(bf16[32,2048]{1,0:T(8,128)(2,1)S(1)} %get-tuple-element.64), channel_id=1, source_target_pairs={{0,2},{1,3},{2,0},{3,1},{4,6},{5,7},{6,4},{7,5},{8,10},{9,11},{10,... | collective-permute-start | bytes 393224 | tf_op jit(solution)/shard_map/ppermute | solution.py:100
  39.9 0.0 collective-permute-done.3
  39.9 1.5 %collective-permute-start.20 = (bf16[32,2048]{1,0:T(8,128)(2,1)S(1)}, bf16[32,2048]{1,0:T(8,128)(2,1)S(1)}, u32[]{:S(2)}, u32[]{:S(2)}) collective-permute-start(bf16[32,2048]{1,0:T(8,128)(2,1)S(1)} %get-tuple-element.65), channel_id=1, source_target_pairs={{0,3},{1,2},{2,1},{3,0},{4,7},{5,6},{6,5},{7,4},{8,11},{9,10},{10,... | collective-permute-start | bytes 393224 | tf_op jit(solution)/shard_map/ppermute | solution.py:100
  41.4 1.6 %collective-permute-start.7 = (bf16[64,2048]{1,0:T(8,128)(2,1)S(1)}, bf16[64,2048]{1,0:T(8,128)(2,1)S(1)}, u32[]{:S(2)}, u32[]{:S(2)}) collective-permute-start(bf16[64,2048]{1,0:T(8,128)(2,1)S(1)} %constant_dynamic-update-slice_fusion), channel_id=1, source_target_pairs={{0,8},{4,12},{8,0},{12,4},{1,9},{5,13},{9,1},{13,5},{2,10},{6,14},... | collective-permute-start | bytes 786440 | tf_op jit(solution)/shard_map/ppermute | solution.py:100
  43.0 0.6 collective-permute-start.11
  43.6 1.6 %collective-permute-start.17 = (bf16[64,2048]{1,0:T(8,128)(2,1)S(1)}, bf16[64,2048]{1,0:T(8,128)(2,1)S(1)}, u32[]{:S(2)}, u32[]{:S(2)}) collective-permute-start(bf16[64,2048]{1,0:T(8,128)(2,1)S(1)} %constant_dynamic-update-slice_fusion.4), channel_id=1, source_target_pairs={{0,8},{4,12},{8,0},{12,4},{1,9},{5,13},{9,1},{13,5},{2,10},{6,14},... | collective-permute-start | bytes 786440 | tf_op jit(solution)/shard_map/ppermute | solution.py:100
  45.1 5.5 %collective-permute-done.7 = bf16[64,2048]{1,0:T(8,128)(2,1)S(1)} collective-permute-done((bf16[64,2048]{1,0:T(8,128)(2,1)S(1)}, bf16[64,2048]{1,0:T(8,128)(2,1)S(1)}, u32[]{:S(2)}, u32[]{:S(2)}) %collective-permute-start.7) | collective-permute-done | bytes 262176 | tf_op jit(solution)/shard_map/ppermute | solution.py:100
  50.7 0.1 collective-permute-start.8
  50.8 0.8 convolution_convert_fusion.5
  51.7 3.9 %collective-permute-done.11 = bf16[64,2048]{1,0:T(8,128)(2,1)S(1)} collective-permute-done((bf16[64,2048]{1,0:T(8,128)(2,1)S(1)}, bf16[64,2048]{1,0:T(8,128)(2,1)S(1)}, u32[]{:S(2)}, u32[]{:S(2)}) %collective-permute-start.11) | collective-permute-done | bytes 262176 | tf_op jit(solution)/shard_map/ppermute | solution.py:100
  55.6 0.8 convolution_convert_fusion.4
  56.5 0.1 collective-permute-start.12
  56.6 0.0 collective-permute-done.8
  56.6 0.8 convolution_convert_fusion.7
  57.5 1.0 %collective-permute-done.12 = bf16[128,2048]{1,0:T(8,128)(2,1)S(1)} collective-permute-done((bf16[128,2048]{1,0:T(8,128)(2,1)S(1)}, bf16[128,2048]{1,0:T(8,128)(2,1)S(1)}, u32[]{:S(2)}, u32[]{:S(2)}) %collective-permute-start.12) | collective-permute-done | bytes 524320 | tf_op jit(solution)/shard_map/ppermute | solution.py:100
  58.5 0.8 convolution_convert_fusion.6
  59.3 0.1 broadcast_select_fusion.12
  59.4 0.6 collective-permute-start.14
  60.0 1.6 %collective-permute-start.21 = (bf16[64,2048]{1,0:T(8,128)(2,1)S(1)}, bf16[64,2048]{1,0:T(8,128)(2,1)S(1)}, u32[]{:S(2)}, u32[]{:S(2)}) collective-permute-start(bf16[64,2048]{1,0:T(8,128)(2,1)S(1)} %constant_dynamic-update-slice_fusion.6), channel_id=1, source_target_pairs={{0,8},{4,12},{8,0},{12,4},{1,9},{5,13},{9,1},{13,5},{2,10},{6,14},... | collective-permute-start | bytes 786440 | tf_op jit(solution)/shard_map/ppermute | solution.py:100
  61.6 0.1 broadcast_select_fusion.15
  61.7 1.5 %collective-permute-start.13 = (bf16[1,128,512]{2,1,0:T(8,128)(2,1)S(1)}, bf16[1,128,512]{2,1,0:T(8,128)(2,1)S(1)}, u32[]{:S(2)}, u32[]{:S(2)}) collective-permute-start(bf16[1,128,512]{2,1,0:T(8,128)(2,1)S(1)} %get-tuple-element.92), channel_id=1, source_target_pairs={{0,1},{1,0},{2,3},{3,2},{4,5},{5,4},{6,7},{7,6},{8,9},{9,8},{10,11... | collective-permute-start | bytes 393224 | tf_op jit(solution)/shard_map/ppermute | solution.py:100
  63.2 2.4 %collective-permute-start.15 = (bf16[1,128,512]{2,1,0:T(8,128)(2,1)S(1)}, bf16[1,128,512]{2,1,0:T(8,128)(2,1)S(1)}, u32[]{:S(2)}, u32[]{:S(2)}) collective-permute-start(bf16[1,128,512]{2,1,0:T(8,128)(2,1)S(1)} %get-tuple-element.93), channel_id=1, source_target_pairs={{0,3},{1,2},{2,1},{3,0},{4,7},{5,6},{6,5},{7,4},{8,11},{9,10},{10,... | collective-permute-start | bytes 393224 | tf_op jit(solution)/shard_map/ppermute | solution.py:100
  65.7 4.5 %collective-permute-done.14 = bf16[1,128,512]{2,1,0:T(8,128)(2,1)S(1)} collective-permute-done((bf16[1,128,512]{2,1,0:T(8,128)(2,1)S(1)}, bf16[1,128,512]{2,1,0:T(8,128)(2,1)S(1)}, u32[]{:S(2)}, u32[]{:S(2)}) %collective-permute-start.14) | collective-permute-done | bytes 131104 | tf_op jit(solution)/shard_map/ppermute | solution.py:100
  70.2 0.1 collective-permute-start.18
  70.3 0.8 convolution_convert_fusion.1
  71.2 0.6 collective-permute-start.22
  71.8 0.3 collective-permute-done.13
  72.1 0.1 broadcast_select_fusion.31
  72.2 0.8 convolution_convert_fusion
  73.1 0.8 convolution_convert_fusion.3
  73.9 0.8 convolution_convert_fusion.2
  74.8 0.1 broadcast_select_fusion.11
  74.9 0.1 broadcast_select_fusion.9
  75.0 2.9 %collective-permute-start.23 = (bf16[1,128,512]{2,1,0:T(8,128)(2,1)S(1)}, bf16[1,128,512]{2,1,0:T(8,128)(2,1)S(1)}, u32[]{:S(2)}, u32[]{:S(2)}) collective-permute-start(bf16[1,128,512]{2,1,0:T(8,128)(2,1)S(1)} %get-tuple-element.96), channel_id=1, source_target_pairs={{0,1},{1,0},{2,3},{3,2},{4,5},{5,4},{6,7},{7,6},{8,9},{9,8},{10,11... | collective-permute-start | bytes 393224 | tf_op jit(solution)/shard_map/ppermute | solution.py:100
  77.9 0.5 collective-permute-start.24
  78.5 1.9 %collective-permute-start.25 = (bf16[1,128,512]{2,1,0:T(8,128)(2,1)S(1)}, bf16[1,128,512]{2,1,0:T(8,128)(2,1)S(1)}, u32[]{:S(2)}, u32[]{:S(2)}) collective-permute-start(bf16[1,128,512]{2,1,0:T(8,128)(2,1)S(1)} %get-tuple-element.98), channel_id=1, source_target_pairs={{0,3},{1,2},{2,1},{3,0},{4,7},{5,6},{6,5},{7,4},{8,11},{9,10},{10,... | collective-permute-start | bytes 393224 | tf_op jit(solution)/shard_map/ppermute | solution.py:100
  80.4 2.2 %collective-permute-done.23 = bf16[1,128,512]{2,1,0:T(8,128)(2,1)S(1)} collective-permute-done((bf16[1,128,512]{2,1,0:T(8,128)(2,1)S(1)}, bf16[1,128,512]{2,1,0:T(8,128)(2,1)S(1)}, u32[]{:S(2)}, u32[]{:S(2)}) %collective-permute-start.23) | collective-permute-done | bytes 131104 | tf_op jit(solution)/shard_map/ppermute | solution.py:100
  82.6 7.9 %collective-permute-done.24 = bf16[1,128,512]{2,1,0:T(8,128)(2,1)S(1)} collective-permute-done((bf16[1,128,512]{2,1,0:T(8,128)(2,1)S(1)}, bf16[1,128,512]{2,1,0:T(8,128)(2,1)S(1)}, u32[]{:S(2)}, u32[]{:S(2)}) %collective-permute-start.24) | collective-permute-done | bytes 131104 | tf_op jit(solution)/shard_map/ppermute | solution.py:100
  90.5 0.1 broadcast_select_fusion.27
  90.7 0.8 maximum_bitcast_fusion
  (56 shorter events, 0.6 us)
Async XLA Ops:
  0.0 1.2 %copy-start = (bf16[256,16,128]{2,1,0:T(8,128)(2,1)S(1)}, bf16[256,16,128]{2,1,0:T(8,128)(2,1)}, u32[]{:S(2)}) copy-start(bf16[256,16,128]{2,1,0:T(8,128)(2,1)} %param.5) | copy-start | bytes 3145732
  1.3 9.6 %collective-permute-start = (bf16[32,16,128]{2,1,0:T(8,128)(2,1)S(1)}, bf16[32,16,128]{2,1,0:T(8,128)(2,1)S(1)}, u32[]{:S(2)}, u32[]{:S(2)}) collective-permute-start(bf16[32,16,128]{2,1,0:T(8,128)(2,1)S(1)} %constant_dynamic-slice_fusion.4), channel_id=1, source_target_pairs={{0,3},{1,2},{2,1},{3,0},{4,7},{5,6},{6,5},{7,4},{8,11},{9,10},{10,... | collective-permute-start | bytes 393224 | tf_op jit(solution)/shard_map/ppermute | solution.py:100
  6.4 12.9 %collective-permute-start.1 = (bf16[32,16,128]{2,1,0:T(8,128)(2,1)S(1)}, bf16[32,16,128]{2,1,0:T(8,128)(2,1)S(1)}, u32[]{:S(2)}, u32[]{:S(2)}) collective-permute-start(bf16[32,16,128]{2,1,0:T(8,128)(2,1)S(1)} %constant_dynamic-slice_fusion.5), channel_id=1, source_target_pairs={{0,2},{1,3},{2,0},{3,1},{4,6},{5,7},{6,4},{7,5},{8,10},{9,11},{10,... | collective-permute-start | bytes 393224 | tf_op jit(solution)/shard_map/ppermute | solution.py:100
  6.4 12.9 %collective-permute-start.2 = (bf16[32,16,128]{2,1,0:T(8,128)(2,1)S(1)}, bf16[32,16,128]{2,1,0:T(8,128)(2,1)S(1)}, u32[]{:S(2)}, u32[]{:S(2)}) collective-permute-start(bf16[32,16,128]{2,1,0:T(8,128)(2,1)S(1)} %constant_dynamic-slice_fusion.6), channel_id=1, source_target_pairs={{0,1},{1,0},{2,3},{3,2},{4,5},{5,4},{6,7},{7,6},{8,9},{9,8},{10,11... | collective-permute-start | bytes 393224 | tf_op jit(solution)/shard_map/ppermute | solution.py:100
  7.1 3.5 %copy-start.4 = (f32[64,64]{1,0:T(8,128)S(1)}, f32[64,64]{1,0:T(8,128)}, u32[]{:S(2)}) copy-start(f32[64,64]{1,0:T(8,128)} %param.7) | copy-start | bytes 49156
  7.1 12.2 %copy-start.1 = (f32[128,128]{1,0:T(8,128)S(1)}, f32[128,128]{1,0:T(8,128)}, u32[]{:S(2)}) copy-start(f32[128,128]{1,0:T(8,128)} %refs_6_.3) | copy-start | bytes 196612
  7.1 12.3 %copy-start.2 = (f32[64,128]{1,0:T(8,128)S(1)}, f32[64,128]{1,0:T(8,128)}, u32[]{:S(2)}) copy-start(f32[64,128]{1,0:T(8,128)} %refs_8_.3) | copy-start | bytes 98308
  11.1 15.0 %collective-permute-start.6 = (bf16[32,16,128]{2,1,0:T(8,128)(2,1)S(1)}, bf16[32,16,128]{2,1,0:T(8,128)(2,1)S(1)}, u32[]{:S(2)}, u32[]{:S(2)}) collective-permute-start(bf16[32,16,128]{2,1,0:T(8,128)(2,1)S(1)} %constant_dynamic-slice_fusion.1), channel_id=1, source_target_pairs={{0,1},{1,0},{2,3},{3,2},{4,5},{5,4},{6,7},{7,6},{8,9},{9,8},{10,11... | collective-permute-start | bytes 393224 | tf_op jit(solution)/shard_map/ppermute | solution.py:100
  16.4 11.6 %collective-permute-start.5 = (bf16[32,16,128]{2,1,0:T(8,128)(2,1)S(1)}, bf16[32,16,128]{2,1,0:T(8,128)(2,1)S(1)}, u32[]{:S(2)}, u32[]{:S(2)}) collective-permute-start(bf16[32,16,128]{2,1,0:T(8,128)(2,1)S(1)} %constant_dynamic-slice_fusion.2), channel_id=1, source_target_pairs={{0,2},{1,3},{2,0},{3,1},{4,6},{5,7},{6,4},{7,5},{8,10},{9,11},{10,... | collective-permute-start | bytes 393224 | tf_op jit(solution)/shard_map/ppermute | solution.py:100
  17.6 10.4 %collective-permute-start.4 = (bf16[32,16,128]{2,1,0:T(8,128)(2,1)S(1)}, bf16[32,16,128]{2,1,0:T(8,128)(2,1)S(1)}, u32[]{:S(2)}, u32[]{:S(2)}) collective-permute-start(bf16[32,16,128]{2,1,0:T(8,128)(2,1)S(1)} %constant_dynamic-slice_fusion.3), channel_id=1, source_target_pairs={{0,3},{1,2},{2,1},{3,0},{4,7},{5,6},{6,5},{7,4},{8,11},{9,10},{10,... | collective-permute-start | bytes 393224 | tf_op jit(solution)/shard_map/ppermute | solution.py:100
  19.4 31.4 %copy-start.3 = (bf16[64,8,16,128]{3,1,2,0:T(8,128)(2,1)S(1)}, bf16[64,8,16,128]{3,1,2,0:T(8,128)(2,1)}, u32[]{:S(2)}) copy-start(bf16[64,8,16,128]{3,1,2,0:T(8,128)(2,1)} %copy.19) | copy-start | bytes 6291460
  21.7 18.2 %collective-permute-start.3 = (bf16[32,2048]{1,0:T(8,128)(2,1)S(1)}, bf16[32,2048]{1,0:T(8,128)(2,1)S(1)}, u32[]{:S(2)}, u32[]{:S(2)}) collective-permute-start(bf16[32,2048]{1,0:T(8,128)(2,1)S(1)} %get-tuple-element.53), channel_id=1, source_target_pairs={{0,1},{1,0},{2,3},{3,2},{4,5},{5,4},{6,7},{7,6},{8,9},{9,8},{10,11... | collective-permute-start | bytes 393224 | tf_op jit(solution)/shard_map/ppermute | solution.py:100
  22.6 18.8 %collective-permute-start.9 = (bf16[32,2048]{1,0:T(8,128)(2,1)S(1)}, bf16[32,2048]{1,0:T(8,128)(2,1)S(1)}, u32[]{:S(2)}, u32[]{:S(2)}) collective-permute-start(bf16[32,2048]{1,0:T(8,128)(2,1)S(1)} %get-tuple-element.71), channel_id=1, source_target_pairs={{0,2},{1,3},{2,0},{3,1},{4,6},{5,7},{6,4},{7,5},{8,10},{9,11},{10,... | collective-permute-start | bytes 393224 | tf_op jit(solution)/shard_map/ppermute | solution.py:100
  26.0 16.9 %collective-permute-start.10 = (bf16[32,2048]{1,0:T(8,128)(2,1)S(1)}, bf16[32,2048]{1,0:T(8,128)(2,1)S(1)}, u32[]{:S(2)}, u32[]{:S(2)}) collective-permute-start(bf16[32,2048]{1,0:T(8,128)(2,1)S(1)} %get-tuple-element.72), channel_id=1, source_target_pairs={{0,3},{1,2},{2,1},{3,0},{4,7},{5,6},{6,5},{7,4},{8,11},{9,10},{10,... | collective-permute-start | bytes 393224 | tf_op jit(solution)/shard_map/ppermute | solution.py:100
  30.2 13.3 %collective-permute-start.16 = (bf16[32,2048]{1,0:T(8,128)(2,1)S(1)}, bf16[32,2048]{1,0:T(8,128)(2,1)S(1)}, u32[]{:S(2)}, u32[]{:S(2)}) collective-permute-start(bf16[32,2048]{1,0:T(8,128)(2,1)S(1)} %get-tuple-element.63), channel_id=1, source_target_pairs={{0,1},{1,0},{2,3},{3,2},{4,5},{5,4},{6,7},{7,6},{8,9},{9,8},{10,11... | collective-permute-start | bytes 393224 | tf_op jit(solution)/shard_map/ppermute | solution.py:100
  37.8 18.7 %collective-permute-start.19 = (bf16[32,2048]{1,0:T(8,128)(2,1)S(1)}, bf16[32,2048]{1,0:T(8,128)(2,1)S(1)}, u32[]{:S(2)}, u32[]{:S(2)}) collective-permute-start(bf16[32,2048]{1,0:T(8,128)(2,1)S(1)} %get-tuple-element.64), channel_id=1, source_target_pairs={{0,2},{1,3},{2,0},{3,1},{4,6},{5,7},{6,4},{7,5},{8,10},{9,11},{10,... | collective-permute-start | bytes 393224 | tf_op jit(solution)/shard_map/ppermute | solution.py:100
  39.9 16.7 %collective-permute-start.20 = (bf16[32,2048]{1,0:T(8,128)(2,1)S(1)}, bf16[32,2048]{1,0:T(8,128)(2,1)S(1)}, u32[]{:S(2)}, u32[]{:S(2)}) collective-permute-start(bf16[32,2048]{1,0:T(8,128)(2,1)S(1)} %get-tuple-element.65), channel_id=1, source_target_pairs={{0,3},{1,2},{2,1},{3,0},{4,7},{5,6},{6,5},{7,4},{8,11},{9,10},{10,... | collective-permute-start | bytes 393224 | tf_op jit(solution)/shard_map/ppermute | solution.py:100
  41.4 9.3 %collective-permute-start.7 = (bf16[64,2048]{1,0:T(8,128)(2,1)S(1)}, bf16[64,2048]{1,0:T(8,128)(2,1)S(1)}, u32[]{:S(2)}, u32[]{:S(2)}) collective-permute-start(bf16[64,2048]{1,0:T(8,128)(2,1)S(1)} %constant_dynamic-update-slice_fusion), channel_id=1, source_target_pairs={{0,8},{4,12},{8,0},{12,4},{1,9},{5,13},{9,1},{13,5},{2,10},{6,14},... | collective-permute-start | bytes 786440 | tf_op jit(solution)/shard_map/ppermute | solution.py:100
  43.0 12.6 %collective-permute-start.11 = (bf16[64,2048]{1,0:T(8,128)(2,1)S(1)}, bf16[64,2048]{1,0:T(8,128)(2,1)S(1)}, u32[]{:S(2)}, u32[]{:S(2)}) collective-permute-start(bf16[64,2048]{1,0:T(8,128)(2,1)S(1)} %constant_dynamic-update-slice_fusion.2), channel_id=1, source_target_pairs={{0,8},{4,12},{8,0},{12,4},{1,9},{5,13},{9,1},{13,5},{2,10},{6,14},... | collective-permute-start | bytes 786440 | tf_op jit(solution)/shard_map/ppermute | solution.py:100
  43.6 22.1 %collective-permute-start.17 = (bf16[64,2048]{1,0:T(8,128)(2,1)S(1)}, bf16[64,2048]{1,0:T(8,128)(2,1)S(1)}, u32[]{:S(2)}, u32[]{:S(2)}) collective-permute-start(bf16[64,2048]{1,0:T(8,128)(2,1)S(1)} %constant_dynamic-update-slice_fusion.4), channel_id=1, source_target_pairs={{0,8},{4,12},{8,0},{12,4},{1,9},{5,13},{9,1},{13,5},{2,10},{6,14},... | collective-permute-start | bytes 786440 | tf_op jit(solution)/shard_map/ppermute | solution.py:100
  50.7 5.9 %collective-permute-start.8 = (bf16[128,2048]{1,0:T(8,128)(2,1)S(1)}, bf16[128,2048]{1,0:T(8,128)(2,1)S(1)}, u32[]{:S(2)}, u32[]{:S(2)}) collective-permute-start(bf16[128,2048]{1,0:T(8,128)(2,1)S(1)} %pad_maximum_fusion), channel_id=1, source_target_pairs={{0,4},{4,0},{8,12},{12,8},{1,5},{5,1},{9,13},{13,9},{2,6},{6,2},{1... | collective-permute-start | bytes 1572872 | tf_op jit(solution)/shard_map/ppermute | solution.py:100
  56.5 2.0 %collective-permute-start.12 = (bf16[128,2048]{1,0:T(8,128)(2,1)S(1)}, bf16[128,2048]{1,0:T(8,128)(2,1)S(1)}, u32[]{:S(2)}, u32[]{:S(2)}) collective-permute-start(bf16[128,2048]{1,0:T(8,128)(2,1)S(1)} %pad_maximum_fusion.1), channel_id=1, source_target_pairs={{0,4},{4,0},{8,12},{12,8},{1,5},{5,1},{9,13},{13,9},{2,6},{6,2},{1... | collective-permute-start | bytes 1572872 | tf_op jit(solution)/shard_map/ppermute | solution.py:100
  59.4 10.8 %collective-permute-start.14 = (bf16[1,128,512]{2,1,0:T(8,128)(2,1)S(1)}, bf16[1,128,512]{2,1,0:T(8,128)(2,1)S(1)}, u32[]{:S(2)}, u32[]{:S(2)}) collective-permute-start(bf16[1,128,512]{2,1,0:T(8,128)(2,1)S(1)} %get-tuple-element.94), channel_id=1, source_target_pairs={{0,2},{1,3},{2,0},{3,1},{4,6},{5,7},{6,4},{7,5},{8,10},{9,11},{10,... | collective-permute-start | bytes 393224 | tf_op jit(solution)/shard_map/ppermute | solution.py:100
  60.0 11.2 %collective-permute-start.21 = (bf16[64,2048]{1,0:T(8,128)(2,1)S(1)}, bf16[64,2048]{1,0:T(8,128)(2,1)S(1)}, u32[]{:S(2)}, u32[]{:S(2)}) collective-permute-start(bf16[64,2048]{1,0:T(8,128)(2,1)S(1)} %constant_dynamic-update-slice_fusion.6), channel_id=1, source_target_pairs={{0,8},{4,12},{8,0},{12,4},{1,9},{5,13},{9,1},{13,5},{2,10},{6,14},... | collective-permute-start | bytes 786440 | tf_op jit(solution)/shard_map/ppermute | solution.py:100
  61.7 10.4 %collective-permute-start.13 = (bf16[1,128,512]{2,1,0:T(8,128)(2,1)S(1)}, bf16[1,128,512]{2,1,0:T(8,128)(2,1)S(1)}, u32[]{:S(2)}, u32[]{:S(2)}) collective-permute-start(bf16[1,128,512]{2,1,0:T(8,128)(2,1)S(1)} %get-tuple-element.92), channel_id=1, source_target_pairs={{0,1},{1,0},{2,3},{3,2},{4,5},{5,4},{6,7},{7,6},{8,9},{9,8},{10,11... | collective-permute-start | bytes 393224 | tf_op jit(solution)/shard_map/ppermute | solution.py:100
  63.2 8.9 %collective-permute-start.15 = (bf16[1,128,512]{2,1,0:T(8,128)(2,1)S(1)}, bf16[1,128,512]{2,1,0:T(8,128)(2,1)S(1)}, u32[]{:S(2)}, u32[]{:S(2)}) collective-permute-start(bf16[1,128,512]{2,1,0:T(8,128)(2,1)S(1)} %get-tuple-element.93), channel_id=1, source_target_pairs={{0,3},{1,2},{2,1},{3,0},{4,7},{5,6},{6,5},{7,4},{8,11},{9,10},{10,... | collective-permute-start | bytes 393224 | tf_op jit(solution)/shard_map/ppermute | solution.py:100
  70.2 2.8 %collective-permute-start.18 = (bf16[128,2048]{1,0:T(8,128)(2,1)S(1)}, bf16[128,2048]{1,0:T(8,128)(2,1)S(1)}, u32[]{:S(2)}, u32[]{:S(2)}) collective-permute-start(bf16[128,2048]{1,0:T(8,128)(2,1)S(1)} %pad_maximum_fusion.2), channel_id=1, source_target_pairs={{0,4},{4,0},{8,12},{12,8},{1,5},{5,1},{9,13},{13,9},{2,6},{6,2},{1... | collective-permute-start | bytes 1572872 | tf_op jit(solution)/shard_map/ppermute | solution.py:100
  71.2 2.7 %collective-permute-start.22 = (bf16[128,2048]{1,0:T(8,128)(2,1)S(1)}, bf16[128,2048]{1,0:T(8,128)(2,1)S(1)}, u32[]{:S(2)}, u32[]{:S(2)}) collective-permute-start(bf16[128,2048]{1,0:T(8,128)(2,1)S(1)} %pad_maximum_fusion.3), channel_id=1, source_target_pairs={{0,4},{4,0},{8,12},{12,8},{1,5},{5,1},{9,13},{13,9},{2,6},{6,2},{1... | collective-permute-start | bytes 1572872 | tf_op jit(solution)/shard_map/ppermute | solution.py:100
  75.0 7.6 %collective-permute-start.23 = (bf16[1,128,512]{2,1,0:T(8,128)(2,1)S(1)}, bf16[1,128,512]{2,1,0:T(8,128)(2,1)S(1)}, u32[]{:S(2)}, u32[]{:S(2)}) collective-permute-start(bf16[1,128,512]{2,1,0:T(8,128)(2,1)S(1)} %get-tuple-element.96), channel_id=1, source_target_pairs={{0,1},{1,0},{2,3},{3,2},{4,5},{5,4},{6,7},{7,6},{8,9},{9,8},{10,11... | collective-permute-start | bytes 393224 | tf_op jit(solution)/shard_map/ppermute | solution.py:100
  77.9 12.6 %collective-permute-start.24 = (bf16[1,128,512]{2,1,0:T(8,128)(2,1)S(1)}, bf16[1,128,512]{2,1,0:T(8,128)(2,1)S(1)}, u32[]{:S(2)}, u32[]{:S(2)}) collective-permute-start(bf16[1,128,512]{2,1,0:T(8,128)(2,1)S(1)} %get-tuple-element.97), channel_id=1, source_target_pairs={{0,2},{1,3},{2,0},{3,1},{4,6},{5,7},{6,4},{7,5},{8,10},{9,11},{10,... | collective-permute-start | bytes 393224 | tf_op jit(solution)/shard_map/ppermute | solution.py:100
  78.5 12.1 %collective-permute-start.25 = (bf16[1,128,512]{2,1,0:T(8,128)(2,1)S(1)}, bf16[1,128,512]{2,1,0:T(8,128)(2,1)S(1)}, u32[]{:S(2)}, u32[]{:S(2)}) collective-permute-start(bf16[1,128,512]{2,1,0:T(8,128)(2,1)S(1)} %get-tuple-element.98), channel_id=1, source_target_pairs={{0,3},{1,2},{2,1},{3,0},{4,7},{5,6},{6,5},{7,4},{8,11},{9,10},{10,... | collective-permute-start | bytes 393224 | tf_op jit(solution)/shard_map/ppermute | solution.py:100

commit v12 on v11

--- a/solution.py
+++ b/solution.py
@@ -109,9 +109,9 @@
     return lax.optimization_barrier((value, tokens))[0]
 
 
-def spread_shares(near, shares, tokens):
-    parts = [near] + [crossed(near, "dp", shares, mask) for mask in range(2, shares, 2)]
-    return lax.optimization_barrier(jnp.concatenate(after(parts, *tokens), axis=0))
+def over_shares(rows, shares):
+    near = jnp.concatenate(rows, axis=0)
+    return [near] + [crossed(near, "dp", shares, mask) for mask in range(2, shares, 2)]
 
 
 def products(near, far, train_flat, shares):
@@ -158,10 +158,13 @@
             block = lax.dynamic_slice_in_dim(source, first + (here ^ mask) * each, each, 0)
             raw[mask], source = lax.optimization_barrier((block, source))
         pieces.append(exchanged(raw, slices))
-    for chunk in range(len(parts)):
-        made = condition(pieces[chunk], basis, in_basis, corrections)
-        rows.append(exchanged(made, slices))
-    rows[0][:half], made = lax.optimization_barrier((rows[0][:half], made))
+    made = condition(pieces[0], basis, in_basis, corrections)
+    rows.append(exchanged(made, slices))
+    rows[0][:half], pieces[1] = lax.optimization_barrier((rows[0][:half], pieces[1]))
+    spread = over_shares(rows[0][:half], shares)
+    made = condition(pieces[1], basis, in_basis, corrections)
+    rows.append(exchanged(made, slices))
+    rows[1][:half], spread = lax.optimization_barrier((rows[1][:half], spread))
     came = []
     for chunk, part in enumerate(parts):
         each = part // slices
@@ -169,7 +172,9 @@
         for group in (rows[chunk][:half], rows[chunk][half:]):
             if chunk and groups:
                 group = after(group, near_before)
-            near = spread_shares(jnp.concatenate(group, axis=0), shares, came[2:3])
+            if chunk or groups:
+                spread = over_shares(group, shares)
+            near = lax.optimization_barrier(jnp.concatenate(after(spread, *came[2:3]), axis=0))
             far = crossed(near, "dp", shares, 1)
             groups.append(products(near, far, train_flat, shares))
         near_before = near

time: 91.7 us -> 84.8 us (0.925)
  waiting for transfers between devices: 27.2 us -> 22.8 us
  starting transfers between devices: 45.3 us -> 42.1 us
    ppermute x26, waiting for transfers between devices: 27.2 us -> 22.8 us  [crossed(): return lax.ppermute(value, axis, [(at, at ^ mask) for at in range(size)])]
    ppermute x26, starting transfers between devices: 45.3 us -> 42.1 us  [crossed(): return lax.ppermute(value, axis, [(at, at ^ mask) for at in range(size)])]
    unnamed x20 -> x18, local copies, waits for them, and re-layouts: 5.21 us -> 5.21 us
  transfers between devices with their start and end apart: 26 -> 26, of which waited for: 8 -> 7; matrix products, arithmetic and copies ran while one was open for 12% -> 13% of each run, Pallas kernels for 5% -> 5%
where the time goes in v12:
time: 84.8 us; the launch traced here: 84.6 us
  starting transfers between devices  42.1 us (50%)
  waiting for transfers between devices  22.8 us (27%)
  matrix products  6.65 us (8%)
  local copies, waits for them, and re-layouts  6.28 us (7%)
  Pallas kernels  4.47 us (5%)
  other arithmetic  1.74 us (2%)
    ppermute x26, starting transfers between devices, crossed(): return lax.ppermute(value, axis, [(at, at ^ mask) for at in range(size)])  42.1 us
    ppermute x26, waiting for transfers between devices, crossed(): return lax.ppermute(value, axis, [(at, at ^ mask) for at in range(size)])  22.8 us
    dot_general x8, matrix products, products(): lax.dot_general(block, train_flat, contract, preferred_element_type=jnp.f...  6.65 us
    unnamed x18, local copies, waits for them, and re-layouts  5.21 us
    pallas_call x2, Pallas kernels, condition_fast(): pl.pallas_call(functools.partial(condition_kernel, slices, rows_here), gr...  4.47 us
  transfers between devices with their start and end apart: 26, of which 7 were waited for; matrix products, arithmetic and copies ran while one was open for 13% of the time, Pallas kernels for 5%

profile of v12, /device:TPU:0, one launch (start us, length us, event | category | flops | bytes accessed | tf_op | source)
XLA Modules:
  0.0 84.6 jit_solution(8797017441262765182)
XLA Ops:
  0.0 1.2 %copy-done = bf16[256,16,128]{2,1,0:T(8,128)(2,1)S(1)} copy-done((bf16[256,16,128]{2,1,0:T(8,128)(2,1)S(1)}, bf16[256,16,128]{2,1,0:T(8,128)(2,1)}, u32[]{:S(2)}) %copy-start) | copy-done | bytes 1048600
  1.3 5.1 %collective-permute-start = (bf16[32,16,128]{2,1,0:T(8,128)(2,1)S(1)}, bf16[32,16,128]{2,1,0:T(8,128)(2,1)S(1)}, u32[]{:S(2)}, u32[]{:S(2)}) collective-permute-start(bf16[32,16,128]{2,1,0:T(8,128)(2,1)S(1)} %constant_dynamic-slice_fusion.4), channel_id=1, source_target_pairs={{0,3},{1,2},{2,1},{3,0},{4,7},{5,6},{6,5},{7,4},{8,11},{9,10},{10,... | collective-permute-start | bytes 393224 | tf_op jit(solution)/shard_map/ppermute | solution.py:100
  6.4 0.0 collective-permute-start.1
  6.4 0.6 collective-permute-start.2
  7.1 0.7 fusion
  7.8 0.1 copy.13
  7.9 0.1 copy.14
  8.0 0.1 copy.15
  8.1 0.1 copy.16
  8.2 0.0 copy-start.1
  8.2 0.0 copy-start.2
  8.2 3.5 %copy.19 = bf16[64,8,16,128]{3,1,2,0:T(8,128)(2,1)} copy(bf16[64,8,16,128]{3,2,1,0:T(8,128)(2,1)} %bitcast.78) | data formatting | bytes 4194304
  11.7 0.1 pad_maximum_fusion.14
  11.8 0.1 copy.11.refs_4_
  11.9 0.0 copy-done.1
  11.9 0.1 copy.10
  12.1 4.2 %collective-permute-start.4 = (bf16[32,16,128]{2,1,0:T(8,128)(2,1)S(1)}, bf16[32,16,128]{2,1,0:T(8,128)(2,1)S(1)}, u32[]{:S(2)}, u32[]{:S(2)}) collective-permute-start(bf16[32,16,128]{2,1,0:T(8,128)(2,1)S(1)} %constant_dynamic-slice_fusion.1), channel_id=1, source_target_pairs={{0,1},{1,0},{2,3},{3,2},{4,5},{5,4},{6,7},{7,6},{8,9},{9,8},{10,11... | collective-permute-start | bytes 393224 | tf_op jit(solution)/shard_map/ppermute | solution.py:100
  16.4 1.3 %collective-permute-start.5 = (bf16[32,16,128]{2,1,0:T(8,128)(2,1)S(1)}, bf16[32,16,128]{2,1,0:T(8,128)(2,1)S(1)}, u32[]{:S(2)}, u32[]{:S(2)}) collective-permute-start(bf16[32,16,128]{2,1,0:T(8,128)(2,1)S(1)} %constant_dynamic-slice_fusion.2), channel_id=1, source_target_pairs={{0,2},{1,3},{2,0},{3,1},{4,6},{5,7},{6,4},{7,5},{8,10},{9,11},{10,... | collective-permute-start | bytes 393224 | tf_op jit(solution)/shard_map/ppermute | solution.py:100
  17.6 1.4 %collective-permute-start.6 = (bf16[32,16,128]{2,1,0:T(8,128)(2,1)S(1)}, bf16[32,16,128]{2,1,0:T(8,128)(2,1)S(1)}, u32[]{:S(2)}, u32[]{:S(2)}) collective-permute-start(bf16[32,16,128]{2,1,0:T(8,128)(2,1)S(1)} %constant_dynamic-slice_fusion.3), channel_id=1, source_target_pairs={{0,3},{1,2},{2,1},{3,0},{4,7},{5,6},{6,5},{7,4},{8,11},{9,10},{10,... | collective-permute-start | bytes 393224 | tf_op jit(solution)/shard_map/ppermute | solution.py:100
  19.0 2.2 %shard_map.55 = (bf16[32,2048]{1,0:T(8,128)(2,1)S(1)}, bf16[32,2048]{1,0:T(8,128)(2,1)S(1)}, bf16[32,2048]{1,0:T(8,128)(2,1)S(1)}, bf16[32,2048]{1,0:T(8,128)(2,1)S(1)}) custom-call(bf16[32,16,128]{2,1,0:T(8,128)(2,1)S(1)} %collective-permute-done.refs_0_, bf16[32,16,128]{2,1,0:T(8,128)(2,1)S(1)} %collective-permute-done.1.refs_1_, ...), custom_call_target="tpu_custom_call" | custom-call | tf_op jit(solution)/shard_map/pallas_call | solution.py:75
  21.3 0.9 %collective-permute-start.3 = (bf16[32,2048]{1,0:T(8,128)(2,1)S(1)}, bf16[32,2048]{1,0:T(8,128)(2,1)S(1)}, u32[]{:S(2)}, u32[]{:S(2)}) collective-permute-start(bf16[32,2048]{1,0:T(8,128)(2,1)S(1)} %get-tuple-element.61), channel_id=1, source_target_pairs={{0,1},{1,0},{2,3},{3,2},{4,5},{5,4},{6,7},{7,6},{8,9},{9,8},{10,11... | collective-permute-start | bytes 393224 | tf_op jit(solution)/shard_map/ppermute | solution.py:100
  22.2 3.8 %collective-permute-start.10 = (bf16[32,2048]{1,0:T(8,128)(2,1)S(1)}, bf16[32,2048]{1,0:T(8,128)(2,1)S(1)}, u32[]{:S(2)}, u32[]{:S(2)}) collective-permute-start(bf16[32,2048]{1,0:T(8,128)(2,1)S(1)} %get-tuple-element.83), channel_id=1, source_target_pairs={{0,2},{1,3},{2,0},{3,1},{4,6},{5,7},{6,4},{7,5},{8,10},{9,11},{10,... | collective-permute-start | bytes 393224 | tf_op jit(solution)/shard_map/ppermute | solution.py:100
  26.0 0.0 collective-permute-done.4.refs_2_
  26.0 0.3 collective-permute-start.11
  26.4 1.6 %collective-permute-done.5.refs_1_ = bf16[32,16,128]{2,1,0:T(8,128)(2,1)S(1)} collective-permute-done((bf16[32,16,128]{2,1,0:T(8,128)(2,1)S(1)}, bf16[32,16,128]{2,1,0:T(8,128)(2,1)S(1)}, u32[]{:S(2)}, u32[]{:S(2)}) %collective-permute-start.5) | collective-permute-done | bytes 131104 | tf_op jit(solution)/shard_map/ppermute | solution.py:100
  27.9 1.4 %collective-permute-done.3 = bf16[32,2048]{1,0:T(8,128)(2,1)S(1)} collective-permute-done((bf16[32,2048]{1,0:T(8,128)(2,1)S(1)}, bf16[32,2048]{1,0:T(8,128)(2,1)S(1)}, u32[]{:S(2)}, u32[]{:S(2)}) %collective-permute-start.3) | collective-permute-done | bytes 131104 | tf_op jit(solution)/shard_map/ppermute | solution.py:100
  29.4 1.5 %collective-permute-start.8 = (bf16[64,2048]{1,0:T(8,128)(2,1)S(1)}, bf16[64,2048]{1,0:T(8,128)(2,1)S(1)}, u32[]{:S(2)}, u32[]{:S(2)}) collective-permute-start(bf16[64,2048]{1,0:T(8,128)(2,1)S(1)} %constant_dynamic-update-slice_fusion), channel_id=1, source_target_pairs={{0,8},{4,12},{8,0},{12,4},{1,9},{5,13},{9,1},{13,5},{2,10},{6,14},... | collective-permute-start | bytes 786440 | tf_op jit(solution)/shard_map/ppermute | solution.py:100
  30.9 2.2 %shard_map.56 = (bf16[32,2048]{1,0:T(8,128)(2,1)S(1)}, bf16[32,2048]{1,0:T(8,128)(2,1)S(1)}, bf16[32,2048]{1,0:T(8,128)(2,1)S(1)}, bf16[32,2048]{1,0:T(8,128)(2,1)S(1)}) custom-call(bf16[32,16,128]{2,1,0:T(8,128)(2,1)S(1)} %collective-permute-done.6.refs_0_, bf16[32,16,128]{2,1,0:T(8,128)(2,1)S(1)} %collective-permute-done.5.refs_1_, ...), custom_call_target="tpu_custom_call" | custom-call | tf_op jit(solution)/shard_map/pallas_call | solution.py:75
  33.1 6.3 %collective-permute-start.7 = (bf16[32,2048]{1,0:T(8,128)(2,1)S(1)}, bf16[32,2048]{1,0:T(8,128)(2,1)S(1)}, u32[]{:S(2)}, u32[]{:S(2)}) collective-permute-start(bf16[32,2048]{1,0:T(8,128)(2,1)S(1)} %get-tuple-element.75), channel_id=1, source_target_pairs={{0,1},{1,0},{2,3},{3,2},{4,5},{5,4},{6,7},{7,6},{8,9},{9,8},{10,11... | collective-permute-start | bytes 393224 | tf_op jit(solution)/shard_map/ppermute | solution.py:100
  39.5 0.6 collective-permute-start.12
  40.1 3.1 %collective-permute-start.19 = (bf16[32,2048]{1,0:T(8,128)(2,1)S(1)}, bf16[32,2048]{1,0:T(8,128)(2,1)S(1)}, u32[]{:S(2)}, u32[]{:S(2)}) collective-permute-start(bf16[32,2048]{1,0:T(8,128)(2,1)S(1)} %get-tuple-element.91), channel_id=1, source_target_pairs={{0,2},{1,3},{2,0},{3,1},{4,6},{5,7},{6,4},{7,5},{8,10},{9,11},{10,... | collective-permute-start | bytes 393224 | tf_op jit(solution)/shard_map/ppermute | solution.py:100
  43.2 1.3 %collective-permute-start.20 = (bf16[32,2048]{1,0:T(8,128)(2,1)S(1)}, bf16[32,2048]{1,0:T(8,128)(2,1)S(1)}, u32[]{:S(2)}, u32[]{:S(2)}) collective-permute-start(bf16[32,2048]{1,0:T(8,128)(2,1)S(1)} %get-tuple-element.92), channel_id=1, source_target_pairs={{0,3},{1,2},{2,1},{3,0},{4,7},{5,6},{6,5},{7,4},{8,11},{9,10},{10,... | collective-permute-start | bytes 393224 | tf_op jit(solution)/shard_map/ppermute | solution.py:100
  44.6 0.1 collective-permute-start.9
  44.7 0.8 convolution_convert_fusion.5
  45.5 0.8 collective-permute-done.12
  46.4 0.8 convolution_convert_fusion.4
  47.2 0.1 collective-permute-start.13
  47.3 0.5 collective-permute-start.17
  47.8 4.2 %collective-permute-done.19 = bf16[32,2048]{1,0:T(8,128)(2,1)S(1)} collective-permute-done((bf16[32,2048]{1,0:T(8,128)(2,1)S(1)}, bf16[32,2048]{1,0:T(8,128)(2,1)S(1)}, u32[]{:S(2)}, u32[]{:S(2)}) %collective-permute-start.19) | collective-permute-done | bytes 131104 | tf_op jit(solution)/shard_map/ppermute | solution.py:100
  52.1 0.8 convolution_convert_fusion.7
  53.0 0.8 convolution_convert_fusion.6
  53.8 0.1 broadcast_select_fusion.12
  54.0 3.1 %collective-permute-start.15 = (bf16[1,128,512]{2,1,0:T(8,128)(2,1)S(1)}, bf16[1,128,512]{2,1,0:T(8,128)(2,1)S(1)}, u32[]{:S(2)}, u32[]{:S(2)}) collective-permute-start(bf16[1,128,512]{2,1,0:T(8,128)(2,1)S(1)} %get-tuple-element.110), channel_id=1, source_target_pairs={{0,2},{1,3},{2,0},{3,1},{4,6},{5,7},{6,4},{7,5},{8,10},{9,11},{10,... | collective-permute-start | bytes 393224 | tf_op jit(solution)/shard_map/ppermute | solution.py:100
  57.1 0.5 collective-permute-start.21
  57.6 0.1 broadcast_select_fusion.15
  57.7 0.1 collective-permute-start.14
  57.9 1.9 %collective-permute-start.16 = (bf16[1,128,512]{2,1,0:T(8,128)(2,1)S(1)}, bf16[1,128,512]{2,1,0:T(8,128)(2,1)S(1)}, u32[]{:S(2)}, u32[]{:S(2)}) collective-permute-start(bf16[1,128,512]{2,1,0:T(8,128)(2,1)S(1)} %get-tuple-element.109), channel_id=1, source_target_pairs={{0,3},{1,2},{2,1},{3,0},{4,7},{5,6},{6,5},{7,4},{8,11},{9,10},{10,... | collective-permute-start | bytes 393224 | tf_op jit(solution)/shard_map/ppermute | solution.py:100
  59.8 5.9 %collective-permute-done.15 = bf16[1,128,512]{2,1,0:T(8,128)(2,1)S(1)} collective-permute-done((bf16[1,128,512]{2,1,0:T(8,128)(2,1)S(1)}, bf16[1,128,512]{2,1,0:T(8,128)(2,1)S(1)}, u32[]{:S(2)}, u32[]{:S(2)}) %collective-permute-start.15) | collective-permute-done | bytes 131104 | tf_op jit(solution)/shard_map/ppermute | solution.py:100
  65.8 0.1 collective-permute-start.18
  65.8 0.8 convolution_convert_fusion.1
  66.7 0.6 collective-permute-start.22
  67.3 0.1 broadcast_select_fusion.31
  67.4 0.8 convolution_convert_fusion
  68.3 0.8 convolution_convert_fusion.3
  69.1 0.8 convolution_convert_fusion.2
  70.0 0.1 broadcast_select_fusion.11
  70.1 0.1 broadcast_select_fusion.9
  70.2 0.5 collective-permute-start.23
  70.8 0.9 %collective-permute-start.24 = (bf16[1,128,512]{2,1,0:T(8,128)(2,1)S(1)}, bf16[1,128,512]{2,1,0:T(8,128)(2,1)S(1)}, u32[]{:S(2)}, u32[]{:S(2)}) collective-permute-start(bf16[1,128,512]{2,1,0:T(8,128)(2,1)S(1)} %get-tuple-element.113), channel_id=1, source_target_pairs={{0,2},{1,3},{2,0},{3,1},{4,6},{5,7},{6,4},{7,5},{8,10},{9,11},{10,... | collective-permute-start | bytes 393224 | tf_op jit(solution)/shard_map/ppermute | solution.py:100
  71.6 3.0 %collective-permute-start.25 = (bf16[1,128,512]{2,1,0:T(8,128)(2,1)S(1)}, bf16[1,128,512]{2,1,0:T(8,128)(2,1)S(1)}, u32[]{:S(2)}, u32[]{:S(2)}) collective-permute-start(bf16[1,128,512]{2,1,0:T(8,128)(2,1)S(1)} %get-tuple-element.114), channel_id=1, source_target_pairs={{0,3},{1,2},{2,1},{3,0},{4,7},{5,6},{6,5},{7,4},{8,11},{9,10},{10,... | collective-permute-start | bytes 393224 | tf_op jit(solution)/shard_map/ppermute | solution.py:100
  74.7 2.8 %collective-permute-done.23 = bf16[1,128,512]{2,1,0:T(8,128)(2,1)S(1)} collective-permute-done((bf16[1,128,512]{2,1,0:T(8,128)(2,1)S(1)}, bf16[1,128,512]{2,1,0:T(8,128)(2,1)S(1)}, u32[]{:S(2)}, u32[]{:S(2)}) %collective-permute-start.23) | collective-permute-done | bytes 131104 | tf_op jit(solution)/shard_map/ppermute | solution.py:100
  77.5 6.1 %collective-permute-done.24 = bf16[1,128,512]{2,1,0:T(8,128)(2,1)S(1)} collective-permute-done((bf16[1,128,512]{2,1,0:T(8,128)(2,1)S(1)}, bf16[1,128,512]{2,1,0:T(8,128)(2,1)S(1)}, u32[]{:S(2)}, u32[]{:S(2)}) %collective-permute-start.24) | collective-permute-done | bytes 131104 | tf_op jit(solution)/shard_map/ppermute | solution.py:100
  83.6 0.1 broadcast_select_fusion.27
  83.7 0.8 maximum_bitcast_fusion
  (54 shorter events, 0.6 us)
Async XLA Ops:
  0.0 1.2 %copy-start = (bf16[256,16,128]{2,1,0:T(8,128)(2,1)S(1)}, bf16[256,16,128]{2,1,0:T(8,128)(2,1)}, u32[]{:S(2)}) copy-start(bf16[256,16,128]{2,1,0:T(8,128)(2,1)} %param.5) | copy-start | bytes 3145732
  1.3 10.7 %collective-permute-start = (bf16[32,16,128]{2,1,0:T(8,128)(2,1)S(1)}, bf16[32,16,128]{2,1,0:T(8,128)(2,1)S(1)}, u32[]{:S(2)}, u32[]{:S(2)}) collective-permute-start(bf16[32,16,128]{2,1,0:T(8,128)(2,1)S(1)} %constant_dynamic-slice_fusion.4), channel_id=1, source_target_pairs={{0,3},{1,2},{2,1},{3,0},{4,7},{5,6},{6,5},{7,4},{8,11},{9,10},{10,... | collective-permute-start | bytes 393224 | tf_op jit(solution)/shard_map/ppermute | solution.py:100
  6.4 12.6 %collective-permute-start.1 = (bf16[32,16,128]{2,1,0:T(8,128)(2,1)S(1)}, bf16[32,16,128]{2,1,0:T(8,128)(2,1)S(1)}, u32[]{:S(2)}, u32[]{:S(2)}) collective-permute-start(bf16[32,16,128]{2,1,0:T(8,128)(2,1)S(1)} %constant_dynamic-slice_fusion.5), channel_id=1, source_target_pairs={{0,2},{1,3},{2,0},{3,1},{4,6},{5,7},{6,4},{7,5},{8,10},{9,11},{10,... | collective-permute-start | bytes 393224 | tf_op jit(solution)/shard_map/ppermute | solution.py:100
  6.4 12.6 %collective-permute-start.2 = (bf16[32,16,128]{2,1,0:T(8,128)(2,1)S(1)}, bf16[32,16,128]{2,1,0:T(8,128)(2,1)S(1)}, u32[]{:S(2)}, u32[]{:S(2)}) collective-permute-start(bf16[32,16,128]{2,1,0:T(8,128)(2,1)S(1)} %constant_dynamic-slice_fusion.6), channel_id=1, source_target_pairs={{0,1},{1,0},{2,3},{3,2},{4,5},{5,4},{6,7},{7,6},{8,9},{9,8},{10,11... | collective-permute-start | bytes 393224 | tf_op jit(solution)/shard_map/ppermute | solution.py:100
  8.2 3.7 %copy-start.1 = (f32[128,128]{1,0:T(8,128)S(1)}, f32[128,128]{1,0:T(8,128)}, u32[]{:S(2)}) copy-start(f32[128,128]{1,0:T(8,128)} %refs_6_.3) | copy-start | bytes 196612
  8.2 10.8 %copy-start.2 = (f32[64,128]{1,0:T(8,128)S(1)}, f32[64,128]{1,0:T(8,128)}, u32[]{:S(2)}) copy-start(f32[64,128]{1,0:T(8,128)} %refs_8_.3) | copy-start | bytes 98308
  12.1 13.9 %collective-permute-start.4 = (bf16[32,16,128]{2,1,0:T(8,128)(2,1)S(1)}, bf16[32,16,128]{2,1,0:T(8,128)(2,1)S(1)}, u32[]{:S(2)}, u32[]{:S(2)}) collective-permute-start(bf16[32,16,128]{2,1,0:T(8,128)(2,1)S(1)} %constant_dynamic-slice_fusion.1), channel_id=1, source_target_pairs={{0,1},{1,0},{2,3},{3,2},{4,5},{5,4},{6,7},{7,6},{8,9},{9,8},{10,11... | collective-permute-start | bytes 393224 | tf_op jit(solution)/shard_map/ppermute | solution.py:100
  16.4 11.6 %collective-permute-start.5 = (bf16[32,16,128]{2,1,0:T(8,128)(2,1)S(1)}, bf16[32,16,128]{2,1,0:T(8,128)(2,1)S(1)}, u32[]{:S(2)}, u32[]{:S(2)}) collective-permute-start(bf16[32,16,128]{2,1,0:T(8,128)(2,1)S(1)} %constant_dynamic-slice_fusion.2), channel_id=1, source_target_pairs={{0,2},{1,3},{2,0},{3,1},{4,6},{5,7},{6,4},{7,5},{8,10},{9,11},{10,... | collective-permute-start | bytes 393224 | tf_op jit(solution)/shard_map/ppermute | solution.py:100
  17.6 10.3 %collective-permute-start.6 = (bf16[32,16,128]{2,1,0:T(8,128)(2,1)S(1)}, bf16[32,16,128]{2,1,0:T(8,128)(2,1)S(1)}, u32[]{:S(2)}, u32[]{:S(2)}) collective-permute-start(bf16[32,16,128]{2,1,0:T(8,128)(2,1)S(1)} %constant_dynamic-slice_fusion.3), channel_id=1, source_target_pairs={{0,3},{1,2},{2,1},{3,0},{4,7},{5,6},{6,5},{7,4},{8,11},{9,10},{10,... | collective-permute-start | bytes 393224 | tf_op jit(solution)/shard_map/ppermute | solution.py:100
  21.3 8.0 %collective-permute-start.3 = (bf16[32,2048]{1,0:T(8,128)(2,1)S(1)}, bf16[32,2048]{1,0:T(8,128)(2,1)S(1)}, u32[]{:S(2)}, u32[]{:S(2)}) collective-permute-start(bf16[32,2048]{1,0:T(8,128)(2,1)S(1)} %get-tuple-element.61), channel_id=1, source_target_pairs={{0,1},{1,0},{2,3},{3,2},{4,5},{5,4},{6,7},{7,6},{8,9},{9,8},{10,11... | collective-permute-start | bytes 393224 | tf_op jit(solution)/shard_map/ppermute | solution.py:100
  22.2 22.5 %copy-start.3 = (bf16[64,8,16,128]{3,1,2,0:T(8,128)(2,1)S(1)}, bf16[64,8,16,128]{3,1,2,0:T(8,128)(2,1)}, u32[]{:S(2)}) copy-start(bf16[64,8,16,128]{3,1,2,0:T(8,128)(2,1)} %copy.19) | copy-start | bytes 6291460
  22.2 17.2 %collective-permute-start.10 = (bf16[32,2048]{1,0:T(8,128)(2,1)S(1)}, bf16[32,2048]{1,0:T(8,128)(2,1)S(1)}, u32[]{:S(2)}, u32[]{:S(2)}) collective-permute-start(bf16[32,2048]{1,0:T(8,128)(2,1)S(1)} %get-tuple-element.83), channel_id=1, source_target_pairs={{0,2},{1,3},{2,0},{3,1},{4,6},{5,7},{6,4},{7,5},{8,10},{9,11},{10,... | collective-permute-start | bytes 393224 | tf_op jit(solution)/shard_map/ppermute | solution.py:100
  26.0 13.4 %collective-permute-start.11 = (bf16[32,2048]{1,0:T(8,128)(2,1)S(1)}, bf16[32,2048]{1,0:T(8,128)(2,1)S(1)}, u32[]{:S(2)}, u32[]{:S(2)}) collective-permute-start(bf16[32,2048]{1,0:T(8,128)(2,1)S(1)} %get-tuple-element.84), channel_id=1, source_target_pairs={{0,3},{1,2},{2,1},{3,0},{4,7},{5,6},{6,5},{7,4},{8,11},{9,10},{10,... | collective-permute-start | bytes 393224 | tf_op jit(solution)/shard_map/ppermute | solution.py:100
  29.4 15.2 %collective-permute-start.8 = (bf16[64,2048]{1,0:T(8,128)(2,1)S(1)}, bf16[64,2048]{1,0:T(8,128)(2,1)S(1)}, u32[]{:S(2)}, u32[]{:S(2)}) collective-permute-start(bf16[64,2048]{1,0:T(8,128)(2,1)S(1)} %constant_dynamic-update-slice_fusion), channel_id=1, source_target_pairs={{0,8},{4,12},{8,0},{12,4},{1,9},{5,13},{9,1},{13,5},{2,10},{6,14},... | collective-permute-start | bytes 786440 | tf_op jit(solution)/shard_map/ppermute | solution.py:100
  33.1 11.4 %collective-permute-start.7 = (bf16[32,2048]{1,0:T(8,128)(2,1)S(1)}, bf16[32,2048]{1,0:T(8,128)(2,1)S(1)}, u32[]{:S(2)}, u32[]{:S(2)}) collective-permute-start(bf16[32,2048]{1,0:T(8,128)(2,1)S(1)} %get-tuple-element.75), channel_id=1, source_target_pairs={{0,1},{1,0},{2,3},{3,2},{4,5},{5,4},{6,7},{7,6},{8,9},{9,8},{10,11... | collective-permute-start | bytes 393224 | tf_op jit(solution)/shard_map/ppermute | solution.py:100
  39.5 6.8 %collective-permute-start.12 = (bf16[64,2048]{1,0:T(8,128)(2,1)S(1)}, bf16[64,2048]{1,0:T(8,128)(2,1)S(1)}, u32[]{:S(2)}, u32[]{:S(2)}) collective-permute-start(bf16[64,2048]{1,0:T(8,128)(2,1)S(1)} %constant_dynamic-update-slice_fusion.2), channel_id=1, source_target_pairs={{0,8},{4,12},{8,0},{12,4},{1,9},{5,13},{9,1},{13,5},{2,10},{6,14},... | collective-permute-start | bytes 786440 | tf_op jit(solution)/shard_map/ppermute | solution.py:100
  40.1 12.0 %collective-permute-start.19 = (bf16[32,2048]{1,0:T(8,128)(2,1)S(1)}, bf16[32,2048]{1,0:T(8,128)(2,1)S(1)}, u32[]{:S(2)}, u32[]{:S(2)}) collective-permute-start(bf16[32,2048]{1,0:T(8,128)(2,1)S(1)} %get-tuple-element.91), channel_id=1, source_target_pairs={{0,2},{1,3},{2,0},{3,1},{4,6},{5,7},{6,4},{7,5},{8,10},{9,11},{10,... | collective-permute-start | bytes 393224 | tf_op jit(solution)/shard_map/ppermute | solution.py:100
  43.2 8.8 %collective-permute-start.20 = (bf16[32,2048]{1,0:T(8,128)(2,1)S(1)}, bf16[32,2048]{1,0:T(8,128)(2,1)S(1)}, u32[]{:S(2)}, u32[]{:S(2)}) collective-permute-start(bf16[32,2048]{1,0:T(8,128)(2,1)S(1)} %get-tuple-element.92), channel_id=1, source_target_pairs={{0,3},{1,2},{2,1},{3,0},{4,7},{5,6},{6,5},{7,4},{8,11},{9,10},{10,... | collective-permute-start | bytes 393224 | tf_op jit(solution)/shard_map/ppermute | solution.py:100
  44.6 7.5 %collective-permute-start.9 = (bf16[128,2048]{1,0:T(8,128)(2,1)S(1)}, bf16[128,2048]{1,0:T(8,128)(2,1)S(1)}, u32[]{:S(2)}, u32[]{:S(2)}) collective-permute-start(bf16[128,2048]{1,0:T(8,128)(2,1)S(1)} %pad_maximum_fusion), channel_id=1, source_target_pairs={{0,4},{4,0},{8,12},{12,8},{1,5},{5,1},{9,13},{13,9},{2,6},{6,2},{1... | collective-permute-start | bytes 1572872 | tf_op jit(solution)/shard_map/ppermute | solution.py:100
  47.2 5.8 %collective-permute-start.13 = (bf16[128,2048]{1,0:T(8,128)(2,1)S(1)}, bf16[128,2048]{1,0:T(8,128)(2,1)S(1)}, u32[]{:S(2)}, u32[]{:S(2)}) collective-permute-start(bf16[128,2048]{1,0:T(8,128)(2,1)S(1)} %pad_maximum_fusion.1), channel_id=1, source_target_pairs={{0,4},{4,0},{8,12},{12,8},{1,5},{5,1},{9,13},{13,9},{2,6},{6,2},{1... | collective-permute-start | bytes 1572872 | tf_op jit(solution)/shard_map/ppermute | solution.py:100
  47.3 12.5 %collective-permute-start.17 = (bf16[64,2048]{1,0:T(8,128)(2,1)S(1)}, bf16[64,2048]{1,0:T(8,128)(2,1)S(1)}, u32[]{:S(2)}, u32[]{:S(2)}) collective-permute-start(bf16[64,2048]{1,0:T(8,128)(2,1)S(1)} %constant_dynamic-update-slice_fusion.4), channel_id=1, source_target_pairs={{0,8},{4,12},{8,0},{12,4},{1,9},{5,13},{9,1},{13,5},{2,10},{6,14},... | collective-permute-start | bytes 786440 | tf_op jit(solution)/shard_map/ppermute | solution.py:100
  54.0 11.8 %collective-permute-start.15 = (bf16[1,128,512]{2,1,0:T(8,128)(2,1)S(1)}, bf16[1,128,512]{2,1,0:T(8,128)(2,1)S(1)}, u32[]{:S(2)}, u32[]{:S(2)}) collective-permute-start(bf16[1,128,512]{2,1,0:T(8,128)(2,1)S(1)} %get-tuple-element.110), channel_id=1, source_target_pairs={{0,2},{1,3},{2,0},{3,1},{4,6},{5,7},{6,4},{7,5},{8,10},{9,11},{10,... | collective-permute-start | bytes 393224 | tf_op jit(solution)/shard_map/ppermute | solution.py:100
  57.1 9.6 %collective-permute-start.21 = (bf16[64,2048]{1,0:T(8,128)(2,1)S(1)}, bf16[64,2048]{1,0:T(8,128)(2,1)S(1)}, u32[]{:S(2)}, u32[]{:S(2)}) collective-permute-start(bf16[64,2048]{1,0:T(8,128)(2,1)S(1)} %constant_dynamic-update-slice_fusion.6), channel_id=1, source_target_pairs={{0,8},{4,12},{8,0},{12,4},{1,9},{5,13},{9,1},{13,5},{2,10},{6,14},... | collective-permute-start | bytes 786440 | tf_op jit(solution)/shard_map/ppermute | solution.py:100
  57.7 9.6 %collective-permute-start.14 = (bf16[1,128,512]{2,1,0:T(8,128)(2,1)S(1)}, bf16[1,128,512]{2,1,0:T(8,128)(2,1)S(1)}, u32[]{:S(2)}, u32[]{:S(2)}) collective-permute-start(bf16[1,128,512]{2,1,0:T(8,128)(2,1)S(1)} %get-tuple-element.108), channel_id=1, source_target_pairs={{0,1},{1,0},{2,3},{3,2},{4,5},{5,4},{6,7},{7,6},{8,9},{9,8},{10,11... | collective-permute-start | bytes 393224 | tf_op jit(solution)/shard_map/ppermute | solution.py:100
  57.9 9.5 %collective-permute-start.16 = (bf16[1,128,512]{2,1,0:T(8,128)(2,1)S(1)}, bf16[1,128,512]{2,1,0:T(8,128)(2,1)S(1)}, u32[]{:S(2)}, u32[]{:S(2)}) collective-permute-start(bf16[1,128,512]{2,1,0:T(8,128)(2,1)S(1)} %get-tuple-element.109), channel_id=1, source_target_pairs={{0,3},{1,2},{2,1},{3,0},{4,7},{5,6},{6,5},{7,4},{8,11},{9,10},{10,... | collective-permute-start | bytes 393224 | tf_op jit(solution)/shard_map/ppermute | solution.py:100
  65.8 2.5 %collective-permute-start.18 = (bf16[128,2048]{1,0:T(8,128)(2,1)S(1)}, bf16[128,2048]{1,0:T(8,128)(2,1)S(1)}, u32[]{:S(2)}, u32[]{:S(2)}) collective-permute-start(bf16[128,2048]{1,0:T(8,128)(2,1)S(1)} %pad_maximum_fusion.2), channel_id=1, source_target_pairs={{0,4},{4,0},{8,12},{12,8},{1,5},{5,1},{9,13},{13,9},{2,6},{6,2},{1... | collective-permute-start | bytes 1572872 | tf_op jit(solution)/shard_map/ppermute | solution.py:100
  66.7 2.4 %collective-permute-start.22 = (bf16[128,2048]{1,0:T(8,128)(2,1)S(1)}, bf16[128,2048]{1,0:T(8,128)(2,1)S(1)}, u32[]{:S(2)}, u32[]{:S(2)}) collective-permute-start(bf16[128,2048]{1,0:T(8,128)(2,1)S(1)} %pad_maximum_fusion.3), channel_id=1, source_target_pairs={{0,4},{4,0},{8,12},{12,8},{1,5},{5,1},{9,13},{13,9},{2,6},{6,2},{1... | collective-permute-start | bytes 1572872 | tf_op jit(solution)/shard_map/ppermute | solution.py:100
  70.2 7.3 %collective-permute-start.23 = (bf16[1,128,512]{2,1,0:T(8,128)(2,1)S(1)}, bf16[1,128,512]{2,1,0:T(8,128)(2,1)S(1)}, u32[]{:S(2)}, u32[]{:S(2)}) collective-permute-start(bf16[1,128,512]{2,1,0:T(8,128)(2,1)S(1)} %get-tuple-element.112), channel_id=1, source_target_pairs={{0,1},{1,0},{2,3},{3,2},{4,5},{5,4},{6,7},{7,6},{8,9},{9,8},{10,11... | collective-permute-start | bytes 393224 | tf_op jit(solution)/shard_map/ppermute | solution.py:100
  70.8 12.8 %collective-permute-start.24 = (bf16[1,128,512]{2,1,0:T(8,128)(2,1)S(1)}, bf16[1,128,512]{2,1,0:T(8,128)(2,1)S(1)}, u32[]{:S(2)}, u32[]{:S(2)}) collective-permute-start(bf16[1,128,512]{2,1,0:T(8,128)(2,1)S(1)} %get-tuple-element.113), channel_id=1, source_target_pairs={{0,2},{1,3},{2,0},{3,1},{4,6},{5,7},{6,4},{7,5},{8,10},{9,11},{10,... | collective-permute-start | bytes 393224 | tf_op jit(solution)/shard_map/ppermute | solution.py:100
  71.6 11.9 %collective-permute-start.25 = (bf16[1,128,512]{2,1,0:T(8,128)(2,1)S(1)}, bf16[1,128,512]{2,1,0:T(8,128)(2,1)S(1)}, u32[]{:S(2)}, u32[]{:S(2)}) collective-permute-start(bf16[1,128,512]{2,1,0:T(8,128)(2,1)S(1)} %get-tuple-element.114), channel_id=1, source_target_pairs={{0,3},{1,2},{2,1},{3,0},{4,7},{5,6},{6,5},{7,4},{8,11},{9,10},{10,... | collective-permute-start | bytes 393224 | tf_op jit(solution)/shard_map/ppermute | solution.py:100

commit v13 on v12

--- a/solution.py
+++ b/solution.py
@@ -103,6 +103,13 @@
 def exchanged(blocks, slices):
     moved = {mask: crossed(blocks[mask], "proj", slices, mask) for mask in reversed(range(1, slices))}
     return [blocks[0]] + [moved[mask] for mask in range(1, slices)]
+
+
+def in_turn(blocks):
+    done = []
+    for block in reversed(blocks):
+        done.append(after(block, *done[-1:]))
+    return done[::-1]
 
 
 def after(value, *tokens):
@@ -165,24 +172,31 @@
     made = condition(pieces[1], basis, in_basis, corrections)
     rows.append(exchanged(made, slices))
     rows[1][:half], spread = lax.optimization_barrier((rows[1][:half], spread))
+    near_rows, far_rows = list(range(half)), list(range(half, slices))
+    orders = [(near_rows, far_rows)] * 2
     came = []
     for chunk, part in enumerate(parts):
         each = part // slices
         groups = []
-        for group in (rows[chunk][:half], rows[chunk][half:]):
+        order = sum(orders[chunk], [])
+        for members in orders[chunk]:
+            group = [rows[chunk][at] for at in members]
             if chunk and groups:
                 group = after(group, near_before)
             if chunk or groups:
                 spread = over_shares(group, shares)
-            near = lax.optimization_barrier(jnp.concatenate(after(spread, *came[2:3]), axis=0))
+            near = lax.optimization_barrier(jnp.concatenate(after(spread, *(came[2:3] if groups else came[:1])), axis=0))
             far = crossed(near, "dp", shares, 1)
             groups.append(products(near, far, train_flat, shares))
         near_before = near
         values = [jnp.concatenate(pair, axis=0) for pair in zip(*groups)]
         values = [jnp.stack(values[at * owned:(at + 1) * owned]) for at in range(slices)]
-        came = exchanged(turned(values, here ^ (share // owned)), slices)
+        came = exchanged(in_turn(turned(values, here ^ (share // owned))), slices)
         sums = [value.reshape(owned, slices, each, train_count) for value in came]
-        total = [sum(sums[mask][:, at ^ mask].astype(jnp.float32) for mask in range(slices)) for at in range(slices)]
+        total = [
+            sum(sums[mask][:, order.index(at ^ mask)].astype(jnp.float32) for mask in range(slices))
+            for at in range(slices)
+        ]
         total = jnp.stack(turned(total, here), axis=1)
         total = jnp.stack(turned([total[at] for at in range(owned)], share % owned))
         results.append(total.reshape(owned, part, train_count))

time: 84.8 us -> 85.3 us (level)
  waiting for transfers between devices: 22.8 us -> 23.8 us
    ppermute x26, waiting for transfers between devices: 22.8 us -> 23.8 us  [crossed(): return lax.ppermute(value, axis, [(at, at ^ mask) for at in range(size)])]
  transfers between devices with their start and end apart: 26 -> 26, of which waited for: 7 -> 9; matrix products, arithmetic and copies ran while one was open for 13% -> 15% of each run, Pallas kernels for 5% -> 5%
where the time goes in v13:
time: 85.3 us; the launch traced here: 85.1 us
  starting transfers between devices  41.6 us (49%)
  waiting for transfers between devices  23.8 us (28%)
  matrix products  6.66 us (8%)
  local copies, waits for them, and re-layouts  6.29 us (7%)
  Pallas kernels  4.47 us (5%)
  other arithmetic  1.74 us (2%)
    ppermute x26, starting transfers between devices, crossed(): return lax.ppermute(value, axis, [(at, at ^ mask) for at in range(size)])  41.6 us
    ppermute x26, waiting for transfers between devices, crossed(): return lax.ppermute(value, axis, [(at, at ^ mask) for at in range(size)])  23.8 us
    dot_general x8, matrix products, products(): lax.dot_general(block, train_flat, contract, preferred_element_type=jnp.f...  6.66 us
    unnamed x18, local copies, waits for them, and re-layouts  5.21 us
    pallas_call x2, Pallas kernels, condition_fast(): pl.pallas_call(functools.partial(condition_kernel, slices, rows_here), gr...  4.47 us
  transfers between devices with their start and end apart: 26, of which 9 were waited for; matrix products, arithmetic and copies ran while one was open for 15% of the time, Pallas kernels for 5%

profile of v13, /device:TPU:0, one launch (start us, length us, event | category | flops | bytes accessed | tf_op | source)
XLA Modules:
  0.0 85.1 jit_solution(7800693061942928281)
XLA Ops:
  0.0 1.2 %copy-done = bf16[256,16,128]{2,1,0:T(8,128)(2,1)S(1)} copy-done((bf16[256,16,128]{2,1,0:T(8,128)(2,1)S(1)}, bf16[256,16,128]{2,1,0:T(8,128)(2,1)}, u32[]{:S(2)}) %copy-start) | copy-done | bytes 1048600
  1.3 5.1 %collective-permute-start = (bf16[32,16,128]{2,1,0:T(8,128)(2,1)S(1)}, bf16[32,16,128]{2,1,0:T(8,128)(2,1)S(1)}, u32[]{:S(2)}, u32[]{:S(2)}) collective-permute-start(bf16[32,16,128]{2,1,0:T(8,128)(2,1)S(1)} %constant_dynamic-slice_fusion.4), channel_id=1, source_target_pairs={{0,3},{1,2},{2,1},{3,0},{4,7},{5,6},{6,5},{7,4},{8,11},{9,10},{10,... | collective-permute-start | bytes 393224 | tf_op jit(solution)/shard_map/ppermute | solution.py:100
  6.4 0.6 collective-permute-start.2
  7.1 0.7 fusion
  7.8 0.1 copy.13
  7.9 0.1 copy.14
  8.0 0.1 copy.15
  8.1 0.1 copy.16
  8.2 0.0 copy-start.1
  8.2 0.0 copy-start.2
  8.2 3.5 %copy.19 = bf16[64,8,16,128]{3,1,2,0:T(8,128)(2,1)} copy(bf16[64,8,16,128]{3,2,1,0:T(8,128)(2,1)} %bitcast.78) | data formatting | bytes 4194304
  11.7 0.1 pad_maximum_fusion.14
  11.8 0.1 copy.11.refs_4_
  11.9 0.0 copy-done.1
  11.9 0.1 copy.10
  12.1 4.2 %collective-permute-start.4 = (bf16[32,16,128]{2,1,0:T(8,128)(2,1)S(1)}, bf16[32,16,128]{2,1,0:T(8,128)(2,1)S(1)}, u32[]{:S(2)}, u32[]{:S(2)}) collective-permute-start(bf16[32,16,128]{2,1,0:T(8,128)(2,1)S(1)} %constant_dynamic-slice_fusion.1), channel_id=1, source_target_pairs={{0,1},{1,0},{2,3},{3,2},{4,5},{5,4},{6,7},{7,6},{8,9},{9,8},{10,11... | collective-permute-start | bytes 393224 | tf_op jit(solution)/shard_map/ppermute | solution.py:100
  16.4 1.3 %collective-permute-start.5 = (bf16[32,16,128]{2,1,0:T(8,128)(2,1)S(1)}, bf16[32,16,128]{2,1,0:T(8,128)(2,1)S(1)}, u32[]{:S(2)}, u32[]{:S(2)}) collective-permute-start(bf16[32,16,128]{2,1,0:T(8,128)(2,1)S(1)} %constant_dynamic-slice_fusion.2), channel_id=1, source_target_pairs={{0,2},{1,3},{2,0},{3,1},{4,6},{5,7},{6,4},{7,5},{8,10},{9,11},{10,... | collective-permute-start | bytes 393224 | tf_op jit(solution)/shard_map/ppermute | solution.py:100
  17.6 1.4 %collective-permute-start.6 = (bf16[32,16,128]{2,1,0:T(8,128)(2,1)S(1)}, bf16[32,16,128]{2,1,0:T(8,128)(2,1)S(1)}, u32[]{:S(2)}, u32[]{:S(2)}) collective-permute-start(bf16[32,16,128]{2,1,0:T(8,128)(2,1)S(1)} %constant_dynamic-slice_fusion.3), channel_id=1, source_target_pairs={{0,3},{1,2},{2,1},{3,0},{4,7},{5,6},{6,5},{7,4},{8,11},{9,10},{10,... | collective-permute-start | bytes 393224 | tf_op jit(solution)/shard_map/ppermute | solution.py:100
  19.0 2.2 %shard_map.55 = (bf16[32,2048]{1,0:T(8,128)(2,1)S(1)}, bf16[32,2048]{1,0:T(8,128)(2,1)S(1)}, bf16[32,2048]{1,0:T(8,128)(2,1)S(1)}, bf16[32,2048]{1,0:T(8,128)(2,1)S(1)}) custom-call(bf16[32,16,128]{2,1,0:T(8,128)(2,1)S(1)} %collective-permute-done.refs_0_, bf16[32,16,128]{2,1,0:T(8,128)(2,1)S(1)} %collective-permute-done.1.refs_1_, ...), custom_call_target="tpu_custom_call" | custom-call | tf_op jit(solution)/shard_map/pallas_call | solution.py:75
  21.3 0.9 %collective-permute-start.3 = (bf16[32,2048]{1,0:T(8,128)(2,1)S(1)}, bf16[32,2048]{1,0:T(8,128)(2,1)S(1)}, u32[]{:S(2)}, u32[]{:S(2)}) collective-permute-start(bf16[32,2048]{1,0:T(8,128)(2,1)S(1)} %get-tuple-element.67), channel_id=1, source_target_pairs={{0,1},{1,0},{2,3},{3,2},{4,5},{5,4},{6,7},{7,6},{8,9},{9,8},{10,11... | collective-permute-start | bytes 393224 | tf_op jit(solution)/shard_map/ppermute | solution.py:100
  22.2 3.8 %collective-permute-start.10 = (bf16[32,2048]{1,0:T(8,128)(2,1)S(1)}, bf16[32,2048]{1,0:T(8,128)(2,1)S(1)}, u32[]{:S(2)}, u32[]{:S(2)}) collective-permute-start(bf16[32,2048]{1,0:T(8,128)(2,1)S(1)} %get-tuple-element.89), channel_id=1, source_target_pairs={{0,2},{1,3},{2,0},{3,1},{4,6},{5,7},{6,4},{7,5},{8,10},{9,11},{10,... | collective-permute-start | bytes 393224 | tf_op jit(solution)/shard_map/ppermute | solution.py:100
  26.0 0.3 collective-permute-start.11
  26.4 1.6 %collective-permute-done.5.refs_1_ = bf16[32,16,128]{2,1,0:T(8,128)(2,1)S(1)} collective-permute-done((bf16[32,16,128]{2,1,0:T(8,128)(2,1)S(1)}, bf16[32,16,128]{2,1,0:T(8,128)(2,1)S(1)}, u32[]{:S(2)}, u32[]{:S(2)}) %collective-permute-start.5) | collective-permute-done | bytes 131104 | tf_op jit(solution)/shard_map/ppermute | solution.py:100
  27.9 1.4 %collective-permute-done.3 = bf16[32,2048]{1,0:T(8,128)(2,1)S(1)} collective-permute-done((bf16[32,2048]{1,0:T(8,128)(2,1)S(1)}, bf16[32,2048]{1,0:T(8,128)(2,1)S(1)}, u32[]{:S(2)}, u32[]{:S(2)}) %collective-permute-start.3) | collective-permute-done | bytes 131104 | tf_op jit(solution)/shard_map/ppermute | solution.py:100
  29.4 1.5 %collective-permute-start.8 = (bf16[64,2048]{1,0:T(8,128)(2,1)S(1)}, bf16[64,2048]{1,0:T(8,128)(2,1)S(1)}, u32[]{:S(2)}, u32[]{:S(2)}) collective-permute-start(bf16[64,2048]{1,0:T(8,128)(2,1)S(1)} %constant_dynamic-update-slice_fusion), channel_id=1, source_target_pairs={{0,8},{4,12},{8,0},{12,4},{1,9},{5,13},{9,1},{13,5},{2,10},{6,14},... | collective-permute-start | bytes 786440 | tf_op jit(solution)/shard_map/ppermute | solution.py:100
  30.9 2.2 %shard_map.56 = (bf16[32,2048]{1,0:T(8,128)(2,1)S(1)}, bf16[32,2048]{1,0:T(8,128)(2,1)S(1)}, bf16[32,2048]{1,0:T(8,128)(2,1)S(1)}, bf16[32,2048]{1,0:T(8,128)(2,1)S(1)}) custom-call(bf16[32,16,128]{2,1,0:T(8,128)(2,1)S(1)} %collective-permute-done.6.refs_0_, bf16[32,16,128]{2,1,0:T(8,128)(2,1)S(1)} %collective-permute-done.5.refs_1_, ...), custom_call_target="tpu_custom_call" | custom-call | tf_op jit(solution)/shard_map/pallas_call | solution.py:75
  33.1 6.3 %collective-permute-start.7 = (bf16[32,2048]{1,0:T(8,128)(2,1)S(1)}, bf16[32,2048]{1,0:T(8,128)(2,1)S(1)}, u32[]{:S(2)}, u32[]{:S(2)}) collective-permute-start(bf16[32,2048]{1,0:T(8,128)(2,1)S(1)} %get-tuple-element.81), channel_id=1, source_target_pairs={{0,1},{1,0},{2,3},{3,2},{4,5},{5,4},{6,7},{7,6},{8,9},{9,8},{10,11... | collective-permute-start | bytes 393224 | tf_op jit(solution)/shard_map/ppermute | solution.py:100
  39.5 0.6 collective-permute-start.12
  40.1 3.1 %collective-permute-start.19 = (bf16[32,2048]{1,0:T(8,128)(2,1)S(1)}, bf16[32,2048]{1,0:T(8,128)(2,1)S(1)}, u32[]{:S(2)}, u32[]{:S(2)}) collective-permute-start(bf16[32,2048]{1,0:T(8,128)(2,1)S(1)} %get-tuple-element.100), channel_id=1, source_target_pairs={{0,2},{1,3},{2,0},{3,1},{4,6},{5,7},{6,4},{7,5},{8,10},{9,11},{10,... | collective-permute-start | bytes 393224 | tf_op jit(solution)/shard_map/ppermute | solution.py:100
  43.2 1.3 %collective-permute-start.20 = (bf16[32,2048]{1,0:T(8,128)(2,1)S(1)}, bf16[32,2048]{1,0:T(8,128)(2,1)S(1)}, u32[]{:S(2)}, u32[]{:S(2)}) collective-permute-start(bf16[32,2048]{1,0:T(8,128)(2,1)S(1)} %get-tuple-element.101), channel_id=1, source_target_pairs={{0,3},{1,2},{2,1},{3,0},{4,7},{5,6},{6,5},{7,4},{8,11},{9,10},{10,... | collective-permute-start | bytes 393224 | tf_op jit(solution)/shard_map/ppermute | solution.py:100
  44.6 0.1 collective-permute-start.9
  44.7 0.8 convolution_convert_fusion.5
  45.5 0.8 collective-permute-done.12
  46.4 0.8 convolution_convert_fusion.4
  47.2 0.1 collective-permute-start.13
  47.3 0.5 collective-permute-start.17
  47.8 4.2 %collective-permute-done.19 = bf16[32,2048]{1,0:T(8,128)(2,1)S(1)} collective-permute-done((bf16[32,2048]{1,0:T(8,128)(2,1)S(1)}, bf16[32,2048]{1,0:T(8,128)(2,1)S(1)}, u32[]{:S(2)}, u32[]{:S(2)}) %collective-permute-start.19) | collective-permute-done | bytes 131104 | tf_op jit(solution)/shard_map/ppermute | solution.py:100
  52.1 1.2 %collective-permute-start.21 = (bf16[64,2048]{1,0:T(8,128)(2,1)S(1)}, bf16[64,2048]{1,0:T(8,128)(2,1)S(1)}, u32[]{:S(2)}, u32[]{:S(2)}) collective-permute-start(bf16[64,2048]{1,0:T(8,128)(2,1)S(1)} %constant_dynamic-update-slice_fusion.6), channel_id=1, source_target_pairs={{0,8},{4,12},{8,0},{12,4},{1,9},{5,13},{9,1},{13,5},{2,10},{6,14},... | collective-permute-start | bytes 786440 | tf_op jit(solution)/shard_map/ppermute | solution.py:100
  53.3 0.8 convolution_convert_fusion.7
  54.2 0.8 convolution_convert_fusion.6
  55.0 0.1 broadcast_select_fusion.15
  55.1 2.0 %collective-permute-start.16 = (bf16[1,128,512]{2,1,0:T(8,128)(2,1)S(1)}, bf16[1,128,512]{2,1,0:T(8,128)(2,1)S(1)}, u32[]{:S(2)}, u32[]{:S(2)}) collective-permute-start(bf16[1,128,512]{2,1,0:T(8,128)(2,1)S(1)} %get-tuple-element.126), channel_id=1, source_target_pairs={{0,3},{1,2},{2,1},{3,0},{4,7},{5,6},{6,5},{7,4},{8,11},{9,10},{10,... | collective-permute-start | bytes 393224 | tf_op jit(solution)/shard_map/ppermute | solution.py:100
  57.1 0.1 broadcast_select_fusion.14
  57.2 1.6 %collective-permute-start.15 = (bf16[1,128,512]{2,1,0:T(8,128)(2,1)S(1)}, bf16[1,128,512]{2,1,0:T(8,128)(2,1)S(1)}, u32[]{:S(2)}, u32[]{:S(2)}) collective-permute-start(bf16[1,128,512]{2,1,0:T(8,128)(2,1)S(1)} %get-tuple-element.93), channel_id=1, source_target_pairs={{0,2},{1,3},{2,0},{3,1},{4,6},{5,7},{6,4},{7,5},{8,10},{9,11},{10,... | collective-permute-start | bytes 393224 | tf_op jit(solution)/shard_map/ppermute | solution.py:100
  58.8 1.0 %collective-permute-start.14 = (bf16[1,128,512]{2,1,0:T(8,128)(2,1)S(1)}, bf16[1,128,512]{2,1,0:T(8,128)(2,1)S(1)}, u32[]{:S(2)}, u32[]{:S(2)}) collective-permute-start(bf16[1,128,512]{2,1,0:T(8,128)(2,1)S(1)} %get-tuple-element.94), channel_id=1, source_target_pairs={{0,1},{1,0},{2,3},{3,2},{4,5},{5,4},{6,7},{7,6},{8,9},{9,8},{10,11... | collective-permute-start | bytes 393224 | tf_op jit(solution)/shard_map/ppermute | solution.py:100
  59.8 0.1 collective-permute-start.18
  59.9 0.8 convolution_convert_fusion.1
  60.7 1.0 %collective-permute-done.21 = bf16[64,2048]{1,0:T(8,128)(2,1)S(1)} collective-permute-done((bf16[64,2048]{1,0:T(8,128)(2,1)S(1)}, bf16[64,2048]{1,0:T(8,128)(2,1)S(1)}, u32[]{:S(2)}, u32[]{:S(2)}) %collective-permute-start.21) | collective-permute-done | bytes 262176 | tf_op jit(solution)/shard_map/ppermute | solution.py:100
  61.7 6.1 %collective-permute-done.15 = bf16[1,128,512]{2,1,0:T(8,128)(2,1)S(1)} collective-permute-done((bf16[1,128,512]{2,1,0:T(8,128)(2,1)S(1)}, bf16[1,128,512]{2,1,0:T(8,128)(2,1)S(1)}, u32[]{:S(2)}, u32[]{:S(2)}) %collective-permute-start.15) | collective-permute-done | bytes 131104 | tf_op jit(solution)/shard_map/ppermute | solution.py:100
  67.8 0.1 collective-permute-start.22
  67.9 0.8 convolution_convert_fusion
  68.8 0.8 convolution_convert_fusion.3
  69.6 0.2 collective-permute-done.22
  69.8 0.8 convolution_convert_fusion.2
  70.7 0.1 broadcast_select_fusion.9
  70.8 2.2 %collective-permute-start.25 = (bf16[1,128,512]{2,1,0:T(8,128)(2,1)S(1)}, bf16[1,128,512]{2,1,0:T(8,128)(2,1)S(1)}, u32[]{:S(2)}, u32[]{:S(2)}) collective-permute-start(bf16[1,128,512]{2,1,0:T(8,128)(2,1)S(1)} %get-tuple-element.122), channel_id=1, source_target_pairs={{0,3},{1,2},{2,1},{3,0},{4,7},{5,6},{6,5},{7,4},{8,11},{9,10},{10,... | collective-permute-start | bytes 393224 | tf_op jit(solution)/shard_map/ppermute | solution.py:100
  73.0 0.1 broadcast_select_fusion.11
  73.1 2.3 %collective-permute-start.23 = (bf16[1,128,512]{2,1,0:T(8,128)(2,1)S(1)}, bf16[1,128,512]{2,1,0:T(8,128)(2,1)S(1)}, u32[]{:S(2)}, u32[]{:S(2)}) collective-permute-start(bf16[1,128,512]{2,1,0:T(8,128)(2,1)S(1)} %get-tuple-element.107), channel_id=1, source_target_pairs={{0,1},{1,0},{2,3},{3,2},{4,5},{5,4},{6,7},{7,6},{8,9},{9,8},{10,11... | collective-permute-start | bytes 393224 | tf_op jit(solution)/shard_map/ppermute | solution.py:100
  75.4 0.1 broadcast_select_fusion.31
  75.5 6.5 %collective-permute-done.23 = bf16[1,128,512]{2,1,0:T(8,128)(2,1)S(1)} collective-permute-done((bf16[1,128,512]{2,1,0:T(8,128)(2,1)S(1)}, bf16[1,128,512]{2,1,0:T(8,128)(2,1)S(1)}, u32[]{:S(2)}, u32[]{:S(2)}) %collective-permute-start.23) | collective-permute-done | bytes 131104 | tf_op jit(solution)/shard_map/ppermute | solution.py:100
  82.0 2.1 %collective-permute-done.24 = bf16[1,128,512]{2,1,0:T(8,128)(2,1)S(1)} collective-permute-done((bf16[1,128,512]{2,1,0:T(8,128)(2,1)S(1)}, bf16[1,128,512]{2,1,0:T(8,128)(2,1)S(1)}, u32[]{:S(2)}, u32[]{:S(2)}) %collective-permute-start.24) | collective-permute-done | bytes 131104 | tf_op jit(solution)/shard_map/ppermute | solution.py:100
  84.0 0.1 broadcast_select_fusion.27
  84.1 0.1 broadcast_select_fusion.26
  84.2 0.8 maximum_bitcast_fusion
  (54 shorter events, 0.6 us)
Async XLA Ops:
  0.0 1.2 %copy-start = (bf16[256,16,128]{2,1,0:T(8,128)(2,1)S(1)}, bf16[256,16,128]{2,1,0:T(8,128)(2,1)}, u32[]{:S(2)}) copy-start(bf16[256,16,128]{2,1,0:T(8,128)(2,1)} %param.5) | copy-start | bytes 3145732
  1.3 10.7 %collective-permute-start = (bf16[32,16,128]{2,1,0:T(8,128)(2,1)S(1)}, bf16[32,16,128]{2,1,0:T(8,128)(2,1)S(1)}, u32[]{:S(2)}, u32[]{:S(2)}) collective-permute-start(bf16[32,16,128]{2,1,0:T(8,128)(2,1)S(1)} %constant_dynamic-slice_fusion.4), channel_id=1, source_target_pairs={{0,3},{1,2},{2,1},{3,0},{4,7},{5,6},{6,5},{7,4},{8,11},{9,10},{10,... | collective-permute-start | bytes 393224 | tf_op jit(solution)/shard_map/ppermute | solution.py:100
  6.4 12.6 %collective-permute-start.1 = (bf16[32,16,128]{2,1,0:T(8,128)(2,1)S(1)}, bf16[32,16,128]{2,1,0:T(8,128)(2,1)S(1)}, u32[]{:S(2)}, u32[]{:S(2)}) collective-permute-start(bf16[32,16,128]{2,1,0:T(8,128)(2,1)S(1)} %constant_dynamic-slice_fusion.5), channel_id=1, source_target_pairs={{0,2},{1,3},{2,0},{3,1},{4,6},{5,7},{6,4},{7,5},{8,10},{9,11},{10,... | collective-permute-start | bytes 393224 | tf_op jit(solution)/shard_map/ppermute | solution.py:100
  6.4 12.6 %collective-permute-start.2 = (bf16[32,16,128]{2,1,0:T(8,128)(2,1)S(1)}, bf16[32,16,128]{2,1,0:T(8,128)(2,1)S(1)}, u32[]{:S(2)}, u32[]{:S(2)}) collective-permute-start(bf16[32,16,128]{2,1,0:T(8,128)(2,1)S(1)} %constant_dynamic-slice_fusion.6), channel_id=1, source_target_pairs={{0,1},{1,0},{2,3},{3,2},{4,5},{5,4},{6,7},{7,6},{8,9},{9,8},{10,11... | collective-permute-start | bytes 393224 | tf_op jit(solution)/shard_map/ppermute | solution.py:100
  8.2 3.7 %copy-start.1 = (f32[128,128]{1,0:T(8,128)S(1)}, f32[128,128]{1,0:T(8,128)}, u32[]{:S(2)}) copy-start(f32[128,128]{1,0:T(8,128)} %refs_6_.3) | copy-start | bytes 196612
  8.2 10.8 %copy-start.2 = (f32[64,128]{1,0:T(8,128)S(1)}, f32[64,128]{1,0:T(8,128)}, u32[]{:S(2)}) copy-start(f32[64,128]{1,0:T(8,128)} %refs_8_.3) | copy-start | bytes 98308
  12.1 13.9 %collective-permute-start.4 = (bf16[32,16,128]{2,1,0:T(8,128)(2,1)S(1)}, bf16[32,16,128]{2,1,0:T(8,128)(2,1)S(1)}, u32[]{:S(2)}, u32[]{:S(2)}) collective-permute-start(bf16[32,16,128]{2,1,0:T(8,128)(2,1)S(1)} %constant_dynamic-slice_fusion.1), channel_id=1, source_target_pairs={{0,1},{1,0},{2,3},{3,2},{4,5},{5,4},{6,7},{7,6},{8,9},{9,8},{10,11... | collective-permute-start | bytes 393224 | tf_op jit(solution)/shard_map/ppermute | solution.py:100
  16.4 11.6 %collective-permute-start.5 = (bf16[32,16,128]{2,1,0:T(8,128)(2,1)S(1)}, bf16[32,16,128]{2,1,0:T(8,128)(2,1)S(1)}, u32[]{:S(2)}, u32[]{:S(2)}) collective-permute-start(bf16[32,16,128]{2,1,0:T(8,128)(2,1)S(1)} %constant_dynamic-slice_fusion.2), channel_id=1, source_target_pairs={{0,2},{1,3},{2,0},{3,1},{4,6},{5,7},{6,4},{7,5},{8,10},{9,11},{10,... | collective-permute-start | bytes 393224 | tf_op jit(solution)/shard_map/ppermute | solution.py:100
  17.6 10.3 %collective-permute-start.6 = (bf16[32,16,128]{2,1,0:T(8,128)(2,1)S(1)}, bf16[32,16,128]{2,1,0:T(8,128)(2,1)S(1)}, u32[]{:S(2)}, u32[]{:S(2)}) collective-permute-start(bf16[32,16,128]{2,1,0:T(8,128)(2,1)S(1)} %constant_dynamic-slice_fusion.3), channel_id=1, source_target_pairs={{0,3},{1,2},{2,1},{3,0},{4,7},{5,6},{6,5},{7,4},{8,11},{9,10},{10,... | collective-permute-start | bytes 393224 | tf_op jit(solution)/shard_map/ppermute | solution.py:100
  21.3 8.0 %collective-permute-start.3 = (bf16[32,2048]{1,0:T(8,128)(2,1)S(1)}, bf16[32,2048]{1,0:T(8,128)(2,1)S(1)}, u32[]{:S(2)}, u32[]{:S(2)}) collective-permute-start(bf16[32,2048]{1,0:T(8,128)(2,1)S(1)} %get-tuple-element.67), channel_id=1, source_target_pairs={{0,1},{1,0},{2,3},{3,2},{4,5},{5,4},{6,7},{7,6},{8,9},{9,8},{10,11... | collective-permute-start | bytes 393224 | tf_op jit(solution)/shard_map/ppermute | solution.py:100
  22.2 22.5 %copy-start.3 = (bf16[64,8,16,128]{3,1,2,0:T(8,128)(2,1)S(1)}, bf16[64,8,16,128]{3,1,2,0:T(8,128)(2,1)}, u32[]{:S(2)}) copy-start(bf16[64,8,16,128]{3,1,2,0:T(8,128)(2,1)} %copy.19) | copy-start | bytes 6291460
  22.2 17.2 %collective-permute-start.10 = (bf16[32,2048]{1,0:T(8,128)(2,1)S(1)}, bf16[32,2048]{1,0:T(8,128)(2,1)S(1)}, u32[]{:S(2)}, u32[]{:S(2)}) collective-permute-start(bf16[32,2048]{1,0:T(8,128)(2,1)S(1)} %get-tuple-element.89), channel_id=1, source_target_pairs={{0,2},{1,3},{2,0},{3,1},{4,6},{5,7},{6,4},{7,5},{8,10},{9,11},{10,... | collective-permute-start | bytes 393224 | tf_op jit(solution)/shard_map/ppermute | solution.py:100
  26.0 13.4 %collective-permute-start.11 = (bf16[32,2048]{1,0:T(8,128)(2,1)S(1)}, bf16[32,2048]{1,0:T(8,128)(2,1)S(1)}, u32[]{:S(2)}, u32[]{:S(2)}) collective-permute-start(bf16[32,2048]{1,0:T(8,128)(2,1)S(1)} %get-tuple-element.90), channel_id=1, source_target_pairs={{0,3},{1,2},{2,1},{3,0},{4,7},{5,6},{6,5},{7,4},{8,11},{9,10},{10,... | collective-permute-start | bytes 393224 | tf_op jit(solution)/shard_map/ppermute | solution.py:100
  29.4 15.2 %collective-permute-start.8 = (bf16[64,2048]{1,0:T(8,128)(2,1)S(1)}, bf16[64,2048]{1,0:T(8,128)(2,1)S(1)}, u32[]{:S(2)}, u32[]{:S(2)}) collective-permute-start(bf16[64,2048]{1,0:T(8,128)(2,1)S(1)} %constant_dynamic-update-slice_fusion), channel_id=1, source_target_pairs={{0,8},{4,12},{8,0},{12,4},{1,9},{5,13},{9,1},{13,5},{2,10},{6,14},... | collective-permute-start | bytes 786440 | tf_op jit(solution)/shard_map/ppermute | solution.py:100
  33.1 11.4 %collective-permute-start.7 = (bf16[32,2048]{1,0:T(8,128)(2,1)S(1)}, bf16[32,2048]{1,0:T(8,128)(2,1)S(1)}, u32[]{:S(2)}, u32[]{:S(2)}) collective-permute-start(bf16[32,2048]{1,0:T(8,128)(2,1)S(1)} %get-tuple-element.81), channel_id=1, source_target_pairs={{0,1},{1,0},{2,3},{3,2},{4,5},{5,4},{6,7},{7,6},{8,9},{9,8},{10,11... | collective-permute-start | bytes 393224 | tf_op jit(solution)/shard_map/ppermute | solution.py:100
  39.5 6.8 %collective-permute-start.12 = (bf16[64,2048]{1,0:T(8,128)(2,1)S(1)}, bf16[64,2048]{1,0:T(8,128)(2,1)S(1)}, u32[]{:S(2)}, u32[]{:S(2)}) collective-permute-start(bf16[64,2048]{1,0:T(8,128)(2,1)S(1)} %constant_dynamic-update-slice_fusion.2), channel_id=1, source_target_pairs={{0,8},{4,12},{8,0},{12,4},{1,9},{5,13},{9,1},{13,5},{2,10},{6,14},... | collective-permute-start | bytes 786440 | tf_op jit(solution)/shard_map/ppermute | solution.py:100
  40.1 12.0 %collective-permute-start.19 = (bf16[32,2048]{1,0:T(8,128)(2,1)S(1)}, bf16[32,2048]{1,0:T(8,128)(2,1)S(1)}, u32[]{:S(2)}, u32[]{:S(2)}) collective-permute-start(bf16[32,2048]{1,0:T(8,128)(2,1)S(1)} %get-tuple-element.100), channel_id=1, source_target_pairs={{0,2},{1,3},{2,0},{3,1},{4,6},{5,7},{6,4},{7,5},{8,10},{9,11},{10,... | collective-permute-start | bytes 393224 | tf_op jit(solution)/shard_map/ppermute | solution.py:100
  43.2 8.8 %collective-permute-start.20 = (bf16[32,2048]{1,0:T(8,128)(2,1)S(1)}, bf16[32,2048]{1,0:T(8,128)(2,1)S(1)}, u32[]{:S(2)}, u32[]{:S(2)}) collective-permute-start(bf16[32,2048]{1,0:T(8,128)(2,1)S(1)} %get-tuple-element.101), channel_id=1, source_target_pairs={{0,3},{1,2},{2,1},{3,0},{4,7},{5,6},{6,5},{7,4},{8,11},{9,10},{10,... | collective-permute-start | bytes 393224 | tf_op jit(solution)/shard_map/ppermute | solution.py:100
  44.6 8.7 %collective-permute-start.9 = (bf16[128,2048]{1,0:T(8,128)(2,1)S(1)}, bf16[128,2048]{1,0:T(8,128)(2,1)S(1)}, u32[]{:S(2)}, u32[]{:S(2)}) collective-permute-start(bf16[128,2048]{1,0:T(8,128)(2,1)S(1)} %pad_maximum_fusion), channel_id=1, source_target_pairs={{0,4},{4,0},{8,12},{12,8},{1,5},{5,1},{9,13},{13,9},{2,6},{6,2},{1... | collective-permute-start | bytes 1572872 | tf_op jit(solution)/shard_map/ppermute | solution.py:100
  47.2 7.0 %collective-permute-start.13 = (bf16[128,2048]{1,0:T(8,128)(2,1)S(1)}, bf16[128,2048]{1,0:T(8,128)(2,1)S(1)}, u32[]{:S(2)}, u32[]{:S(2)}) collective-permute-start(bf16[128,2048]{1,0:T(8,128)(2,1)S(1)} %pad_maximum_fusion.1), channel_id=1, source_target_pairs={{0,4},{4,0},{8,12},{12,8},{1,5},{5,1},{9,13},{13,9},{2,6},{6,2},{1... | collective-permute-start | bytes 1572872 | tf_op jit(solution)/shard_map/ppermute | solution.py:100
  47.3 12.4 %collective-permute-start.17 = (bf16[64,2048]{1,0:T(8,128)(2,1)S(1)}, bf16[64,2048]{1,0:T(8,128)(2,1)S(1)}, u32[]{:S(2)}, u32[]{:S(2)}) collective-permute-start(bf16[64,2048]{1,0:T(8,128)(2,1)S(1)} %constant_dynamic-update-slice_fusion.4), channel_id=1, source_target_pairs={{0,8},{4,12},{8,0},{12,4},{1,9},{5,13},{9,1},{13,5},{2,10},{6,14},... | collective-permute-start | bytes 786440 | tf_op jit(solution)/shard_map/ppermute | solution.py:100
  52.1 9.6 %collective-permute-start.21 = (bf16[64,2048]{1,0:T(8,128)(2,1)S(1)}, bf16[64,2048]{1,0:T(8,128)(2,1)S(1)}, u32[]{:S(2)}, u32[]{:S(2)}) collective-permute-start(bf16[64,2048]{1,0:T(8,128)(2,1)S(1)} %constant_dynamic-update-slice_fusion.6), channel_id=1, source_target_pairs={{0,8},{4,12},{8,0},{12,4},{1,9},{5,13},{9,1},{13,5},{2,10},{6,14},... | collective-permute-start | bytes 786440 | tf_op jit(solution)/shard_map/ppermute | solution.py:100
  55.1 20.3 %collective-permute-start.16 = (bf16[1,128,512]{2,1,0:T(8,128)(2,1)S(1)}, bf16[1,128,512]{2,1,0:T(8,128)(2,1)S(1)}, u32[]{:S(2)}, u32[]{:S(2)}) collective-permute-start(bf16[1,128,512]{2,1,0:T(8,128)(2,1)S(1)} %get-tuple-element.126), channel_id=1, source_target_pairs={{0,3},{1,2},{2,1},{3,0},{4,7},{5,6},{6,5},{7,4},{8,11},{9,10},{10,... | collective-permute-start | bytes 393224 | tf_op jit(solution)/shard_map/ppermute | solution.py:100
  57.2 10.6 %collective-permute-start.15 = (bf16[1,128,512]{2,1,0:T(8,128)(2,1)S(1)}, bf16[1,128,512]{2,1,0:T(8,128)(2,1)S(1)}, u32[]{:S(2)}, u32[]{:S(2)}) collective-permute-start(bf16[1,128,512]{2,1,0:T(8,128)(2,1)S(1)} %get-tuple-element.93), channel_id=1, source_target_pairs={{0,2},{1,3},{2,0},{3,1},{4,6},{5,7},{6,4},{7,5},{8,10},{9,11},{10,... | collective-permute-start | bytes 393224 | tf_op jit(solution)/shard_map/ppermute | solution.py:100
  58.8 16.6 %collective-permute-start.14 = (bf16[1,128,512]{2,1,0:T(8,128)(2,1)S(1)}, bf16[1,128,512]{2,1,0:T(8,128)(2,1)S(1)}, u32[]{:S(2)}, u32[]{:S(2)}) collective-permute-start(bf16[1,128,512]{2,1,0:T(8,128)(2,1)S(1)} %get-tuple-element.94), channel_id=1, source_target_pairs={{0,1},{1,0},{2,3},{3,2},{4,5},{5,4},{6,7},{7,6},{8,9},{9,8},{10,11... | collective-permute-start | bytes 393224 | tf_op jit(solution)/shard_map/ppermute | solution.py:100
  59.8 9.0 %collective-permute-start.18 = (bf16[128,2048]{1,0:T(8,128)(2,1)S(1)}, bf16[128,2048]{1,0:T(8,128)(2,1)S(1)}, u32[]{:S(2)}, u32[]{:S(2)}) collective-permute-start(bf16[128,2048]{1,0:T(8,128)(2,1)S(1)} %pad_maximum_fusion.2), channel_id=1, source_target_pairs={{0,4},{4,0},{8,12},{12,8},{1,5},{5,1},{9,13},{13,9},{2,6},{6,2},{1... | collective-permute-start | bytes 1572872 | tf_op jit(solution)/shard_map/ppermute | solution.py:100
  67.8 2.0 %collective-permute-start.22 = (bf16[128,2048]{1,0:T(8,128)(2,1)S(1)}, bf16[128,2048]{1,0:T(8,128)(2,1)S(1)}, u32[]{:S(2)}, u32[]{:S(2)}) collective-permute-start(bf16[128,2048]{1,0:T(8,128)(2,1)S(1)} %pad_maximum_fusion.3), channel_id=1, source_target_pairs={{0,4},{4,0},{8,12},{12,8},{1,5},{5,1},{9,13},{13,9},{2,6},{6,2},{1... | collective-permute-start | bytes 1572872 | tf_op jit(solution)/shard_map/ppermute | solution.py:100
  70.8 13.3 %collective-permute-start.25 = (bf16[1,128,512]{2,1,0:T(8,128)(2,1)S(1)}, bf16[1,128,512]{2,1,0:T(8,128)(2,1)S(1)}, u32[]{:S(2)}, u32[]{:S(2)}) collective-permute-start(bf16[1,128,512]{2,1,0:T(8,128)(2,1)S(1)} %get-tuple-element.122), channel_id=1, source_target_pairs={{0,3},{1,2},{2,1},{3,0},{4,7},{5,6},{6,5},{7,4},{8,11},{9,10},{10,... | collective-permute-start | bytes 393224 | tf_op jit(solution)/shard_map/ppermute | solution.py:100
  73.0 11.0 %collective-permute-start.24 = (bf16[1,128,512]{2,1,0:T(8,128)(2,1)S(1)}, bf16[1,128,512]{2,1,0:T(8,128)(2,1)S(1)}, u32[]{:S(2)}, u32[]{:S(2)}) collective-permute-start(bf16[1,128,512]{2,1,0:T(8,128)(2,1)S(1)} %get-tuple-element.106), channel_id=1, source_target_pairs={{0,2},{1,3},{2,0},{3,1},{4,6},{5,7},{6,4},{7,5},{8,10},{9,11},{10,... | collective-permute-start | bytes 393224 | tf_op jit(solution)/shard_map/ppermute | solution.py:100
  73.1 8.9 %collective-permute-start.23 = (bf16[1,128,512]{2,1,0:T(8,128)(2,1)S(1)}, bf16[1,128,512]{2,1,0:T(8,128)(2,1)S(1)}, u32[]{:S(2)}, u32[]{:S(2)}) collective-permute-start(bf16[1,128,512]{2,1,0:T(8,128)(2,1)S(1)} %get-tuple-element.107), channel_id=1, source_target_pairs={{0,1},{1,0},{2,3},{3,2},{4,5},{5,4},{6,7},{7,6},{8,9},{9,8},{10,11... | collective-permute-start | bytes 393224 | tf_op jit(solution)/shard_map/ppermute | solution.py:100

commit v14 on v13

--- a/solution.py
+++ b/solution.py
@@ -185,7 +185,7 @@
                 group = after(group, near_before)
             if chunk or groups:
                 spread = over_shares(group, shares)
-            near = lax.optimization_barrier(jnp.concatenate(after(spread, *(came[2:3] if groups else came[:1])), axis=0))
+            near = lax.optimization_barrier(jnp.concatenate(after(spread, *came[:1]), axis=0))
             far = crossed(near, "dp", shares, 1)
             groups.append(products(near, far, train_flat, shares))
         near_before = near

time: 85.3 us -> 82.7 us (0.970)
  waiting for transfers between devices: 23.8 us -> 21.2 us
    ppermute x26, waiting for transfers between devices: 23.8 us -> 21.2 us  [crossed(): return lax.ppermute(value, axis, [(at, at ^ mask) for at in range(size)])]
  transfers between devices with their start and end apart: 26 -> 26, of which waited for: 9 -> 8; matrix products, arithmetic and copies ran while one was open for 15% -> 15% of each run, Pallas kernels for 5% -> 5%
where the time goes in v14:
time: 82.7 us; the launch traced here: 82.4 us
  starting transfers between devices  41.6 us (50%)
  waiting for transfers between devices  21.2 us (26%)
  matrix products  6.66 us (8%)
  local copies, waits for them, and re-layouts  6.29 us (8%)
  Pallas kernels  4.47 us (5%)
  other arithmetic  1.69 us (2%)
    ppermute x26, starting transfers between devices, crossed(): return lax.ppermute(value, axis, [(at, at ^ mask) for at in range(size)])  41.6 us
    ppermute x26, waiting for transfers between devices, crossed(): return lax.ppermute(value, axis, [(at, at ^ mask) for at in range(size)])  21.2 us
    dot_general x8, matrix products, products(): lax.dot_general(block, train_flat, contract, preferred_element_type=jnp.f...  6.66 us
    unnamed x18, local copies, waits for them, and re-layouts  5.21 us
    pallas_call x2, Pallas kernels, condition_fast(): pl.pallas_call(functools.partial(condition_kernel, slices, rows_here), gr...  4.47 us
  transfers between devices with their start and end apart: 26, of which 8 were waited for; matrix products, arithmetic and copies ran while one was open for 15% of the time, Pallas kernels for 5%

profile of v14, /device:TPU:0, one launch (start us, length us, event | category | flops | bytes accessed | tf_op | source)
XLA Modules:
  0.0 82.4 jit_solution(5701253924867177746)
XLA Ops:
  0.0 1.2 %copy-done = bf16[256,16,128]{2,1,0:T(8,128)(2,1)S(1)} copy-done((bf16[256,16,128]{2,1,0:T(8,128)(2,1)S(1)}, bf16[256,16,128]{2,1,0:T(8,128)(2,1)}, u32[]{:S(2)}) %copy-start) | copy-done | bytes 1048600
  1.3 5.1 %collective-permute-start = (bf16[32,16,128]{2,1,0:T(8,128)(2,1)S(1)}, bf16[32,16,128]{2,1,0:T(8,128)(2,1)S(1)}, u32[]{:S(2)}, u32[]{:S(2)}) collective-permute-start(bf16[32,16,128]{2,1,0:T(8,128)(2,1)S(1)} %constant_dynamic-slice_fusion.4), channel_id=1, source_target_pairs={{0,3},{1,2},{2,1},{3,0},{4,7},{5,6},{6,5},{7,4},{8,11},{9,10},{10,... | collective-permute-start | bytes 393224 | tf_op jit(solution)/shard_map/ppermute | solution.py:100
  6.4 0.6 collective-permute-start.2
  7.1 0.7 fusion
  7.8 0.1 copy.13
  7.9 0.1 copy.14
  8.0 0.1 copy.15
  8.1 0.1 copy.16
  8.2 0.0 copy-start.1
  8.2 0.0 copy-start.2
  8.2 3.5 %copy.19 = bf16[64,8,16,128]{3,1,2,0:T(8,128)(2,1)} copy(bf16[64,8,16,128]{3,2,1,0:T(8,128)(2,1)} %bitcast.78) | data formatting | bytes 4194304
  11.7 0.1 pad_maximum_fusion.14
  11.8 0.1 copy.11.refs_4_
  11.9 0.0 copy-done.1
  11.9 0.1 copy.10
  12.1 4.2 %collective-permute-start.4 = (bf16[32,16,128]{2,1,0:T(8,128)(2,1)S(1)}, bf16[32,16,128]{2,1,0:T(8,128)(2,1)S(1)}, u32[]{:S(2)}, u32[]{:S(2)}) collective-permute-start(bf16[32,16,128]{2,1,0:T(8,128)(2,1)S(1)} %constant_dynamic-slice_fusion.1), channel_id=1, source_target_pairs={{0,1},{1,0},{2,3},{3,2},{4,5},{5,4},{6,7},{7,6},{8,9},{9,8},{10,11... | collective-permute-start | bytes 393224 | tf_op jit(solution)/shard_map/ppermute | solution.py:100
  16.4 1.3 %collective-permute-start.5 = (bf16[32,16,128]{2,1,0:T(8,128)(2,1)S(1)}, bf16[32,16,128]{2,1,0:T(8,128)(2,1)S(1)}, u32[]{:S(2)}, u32[]{:S(2)}) collective-permute-start(bf16[32,16,128]{2,1,0:T(8,128)(2,1)S(1)} %constant_dynamic-slice_fusion.2), channel_id=1, source_target_pairs={{0,2},{1,3},{2,0},{3,1},{4,6},{5,7},{6,4},{7,5},{8,10},{9,11},{10,... | collective-permute-start | bytes 393224 | tf_op jit(solution)/shard_map/ppermute | solution.py:100
  17.6 1.4 %collective-permute-start.6 = (bf16[32,16,128]{2,1,0:T(8,128)(2,1)S(1)}, bf16[32,16,128]{2,1,0:T(8,128)(2,1)S(1)}, u32[]{:S(2)}, u32[]{:S(2)}) collective-permute-start(bf16[32,16,128]{2,1,0:T(8,128)(2,1)S(1)} %constant_dynamic-slice_fusion.3), channel_id=1, source_target_pairs={{0,3},{1,2},{2,1},{3,0},{4,7},{5,6},{6,5},{7,4},{8,11},{9,10},{10,... | collective-permute-start | bytes 393224 | tf_op jit(solution)/shard_map/ppermute | solution.py:100
  19.0 2.2 %shard_map.55 = (bf16[32,2048]{1,0:T(8,128)(2,1)S(1)}, bf16[32,2048]{1,0:T(8,128)(2,1)S(1)}, bf16[32,2048]{1,0:T(8,128)(2,1)S(1)}, bf16[32,2048]{1,0:T(8,128)(2,1)S(1)}) custom-call(bf16[32,16,128]{2,1,0:T(8,128)(2,1)S(1)} %collective-permute-done.refs_0_, bf16[32,16,128]{2,1,0:T(8,128)(2,1)S(1)} %collective-permute-done.1.refs_1_, ...), custom_call_target="tpu_custom_call" | custom-call | tf_op jit(solution)/shard_map/pallas_call | solution.py:75
  21.3 0.9 %collective-permute-start.3 = (bf16[32,2048]{1,0:T(8,128)(2,1)S(1)}, bf16[32,2048]{1,0:T(8,128)(2,1)S(1)}, u32[]{:S(2)}, u32[]{:S(2)}) collective-permute-start(bf16[32,2048]{1,0:T(8,128)(2,1)S(1)} %get-tuple-element.67), channel_id=1, source_target_pairs={{0,1},{1,0},{2,3},{3,2},{4,5},{5,4},{6,7},{7,6},{8,9},{9,8},{10,11... | collective-permute-start | bytes 393224 | tf_op jit(solution)/shard_map/ppermute | solution.py:100
  22.2 3.8 %collective-permute-start.10 = (bf16[32,2048]{1,0:T(8,128)(2,1)S(1)}, bf16[32,2048]{1,0:T(8,128)(2,1)S(1)}, u32[]{:S(2)}, u32[]{:S(2)}) collective-permute-start(bf16[32,2048]{1,0:T(8,128)(2,1)S(1)} %get-tuple-element.89), channel_id=1, source_target_pairs={{0,2},{1,3},{2,0},{3,1},{4,6},{5,7},{6,4},{7,5},{8,10},{9,11},{10,... | collective-permute-start | bytes 393224 | tf_op jit(solution)/shard_map/ppermute | solution.py:100
  26.0 0.3 collective-permute-start.11
  26.4 1.6 %collective-permute-done.5.refs_1_ = bf16[32,16,128]{2,1,0:T(8,128)(2,1)S(1)} collective-permute-done((bf16[32,16,128]{2,1,0:T(8,128)(2,1)S(1)}, bf16[32,16,128]{2,1,0:T(8,128)(2,1)S(1)}, u32[]{:S(2)}, u32[]{:S(2)}) %collective-permute-start.5) | collective-permute-done | bytes 131104 | tf_op jit(solution)/shard_map/ppermute | solution.py:100
  27.9 1.4 %collective-permute-done.3 = bf16[32,2048]{1,0:T(8,128)(2,1)S(1)} collective-permute-done((bf16[32,2048]{1,0:T(8,128)(2,1)S(1)}, bf16[32,2048]{1,0:T(8,128)(2,1)S(1)}, u32[]{:S(2)}, u32[]{:S(2)}) %collective-permute-start.3) | collective-permute-done | bytes 131104 | tf_op jit(solution)/shard_map/ppermute | solution.py:100
  29.4 1.5 %collective-permute-start.8 = (bf16[64,2048]{1,0:T(8,128)(2,1)S(1)}, bf16[64,2048]{1,0:T(8,128)(2,1)S(1)}, u32[]{:S(2)}, u32[]{:S(2)}) collective-permute-start(bf16[64,2048]{1,0:T(8,128)(2,1)S(1)} %constant_dynamic-update-slice_fusion), channel_id=1, source_target_pairs={{0,8},{4,12},{8,0},{12,4},{1,9},{5,13},{9,1},{13,5},{2,10},{6,14},... | collective-permute-start | bytes 786440 | tf_op jit(solution)/shard_map/ppermute | solution.py:100
  30.9 2.2 %shard_map.56 = (bf16[32,2048]{1,0:T(8,128)(2,1)S(1)}, bf16[32,2048]{1,0:T(8,128)(2,1)S(1)}, bf16[32,2048]{1,0:T(8,128)(2,1)S(1)}, bf16[32,2048]{1,0:T(8,128)(2,1)S(1)}) custom-call(bf16[32,16,128]{2,1,0:T(8,128)(2,1)S(1)} %collective-permute-done.6.refs_0_, bf16[32,16,128]{2,1,0:T(8,128)(2,1)S(1)} %collective-permute-done.5.refs_1_, ...), custom_call_target="tpu_custom_call" | custom-call | tf_op jit(solution)/shard_map/pallas_call | solution.py:75
  33.1 6.3 %collective-permute-start.7 = (bf16[32,2048]{1,0:T(8,128)(2,1)S(1)}, bf16[32,2048]{1,0:T(8,128)(2,1)S(1)}, u32[]{:S(2)}, u32[]{:S(2)}) collective-permute-start(bf16[32,2048]{1,0:T(8,128)(2,1)S(1)} %get-tuple-element.81), channel_id=1, source_target_pairs={{0,1},{1,0},{2,3},{3,2},{4,5},{5,4},{6,7},{7,6},{8,9},{9,8},{10,11... | collective-permute-start | bytes 393224 | tf_op jit(solution)/shard_map/ppermute | solution.py:100
  39.5 0.6 collective-permute-start.12
  40.1 3.1 %collective-permute-start.19 = (bf16[32,2048]{1,0:T(8,128)(2,1)S(1)}, bf16[32,2048]{1,0:T(8,128)(2,1)S(1)}, u32[]{:S(2)}, u32[]{:S(2)}) collective-permute-start(bf16[32,2048]{1,0:T(8,128)(2,1)S(1)} %get-tuple-element.100), channel_id=1, source_target_pairs={{0,2},{1,3},{2,0},{3,1},{4,6},{5,7},{6,4},{7,5},{8,10},{9,11},{10,... | collective-permute-start | bytes 393224 | tf_op jit(solution)/shard_map/ppermute | solution.py:100
  43.2 1.3 %collective-permute-start.20 = (bf16[32,2048]{1,0:T(8,128)(2,1)S(1)}, bf16[32,2048]{1,0:T(8,128)(2,1)S(1)}, u32[]{:S(2)}, u32[]{:S(2)}) collective-permute-start(bf16[32,2048]{1,0:T(8,128)(2,1)S(1)} %get-tuple-element.101), channel_id=1, source_target_pairs={{0,3},{1,2},{2,1},{3,0},{4,7},{5,6},{6,5},{7,4},{8,11},{9,10},{10,... | collective-permute-start | bytes 393224 | tf_op jit(solution)/shard_map/ppermute | solution.py:100
  44.6 0.1 collective-permute-start.9
  44.7 1.6 %collective-permute-done.12 = bf16[64,2048]{1,0:T(8,128)(2,1)S(1)} collective-permute-done((bf16[64,2048]{1,0:T(8,128)(2,1)S(1)}, bf16[64,2048]{1,0:T(8,128)(2,1)S(1)}, u32[]{:S(2)}, u32[]{:S(2)}) %collective-permute-start.12) | collective-permute-done | bytes 262176 | tf_op jit(solution)/shard_map/ppermute | solution.py:100
  46.4 0.1 collective-permute-start.13
  46.5 0.8 %convolution_convert_fusion.5 = bf16[128,512]{1,0:T(8,128)(2,1)S(1)} fusion(bf16[128,2048]{1,0:T(8,128)(2,1)S(1)} %pad_maximum_fusion, bf16[512,2048]{1,0:T(8,128)(2,1)S(1)} %bitcast.70), kind=kOutput, calls=%fused_computation.6 | convolution fusion | flops 268500992 | bytes 2752512 | tf_op jit(solution)/shard_map/dot_general | solution.py:128
  47.3 0.8 %convolution_convert_fusion.4 = bf16[128,512]{1,0:T(8,128)(2,1)S(1)} fusion(bf16[128,2048]{1,0:T(8,128)(2,1)S(1)} %pad_maximum_fusion.1, bf16[512,2048]{1,0:T(8,128)(2,1)S(1)} %bitcast.71), kind=kOutput, calls=%fused_computation.5 | convolution fusion | flops 268500992 | bytes 2752512 | tf_op jit(solution)/shard_map/dot_general | solution.py:128
  48.2 0.5 collective-permute-start.17
  48.7 3.4 %collective-permute-done.19 = bf16[32,2048]{1,0:T(8,128)(2,1)S(1)} collective-permute-done((bf16[32,2048]{1,0:T(8,128)(2,1)S(1)}, bf16[32,2048]{1,0:T(8,128)(2,1)S(1)}, u32[]{:S(2)}, u32[]{:S(2)}) %collective-permute-start.19) | collective-permute-done | bytes 131104 | tf_op jit(solution)/shard_map/ppermute | solution.py:100
  52.1 1.2 %collective-permute-start.21 = (bf16[64,2048]{1,0:T(8,128)(2,1)S(1)}, bf16[64,2048]{1,0:T(8,128)(2,1)S(1)}, u32[]{:S(2)}, u32[]{:S(2)}) collective-permute-start(bf16[64,2048]{1,0:T(8,128)(2,1)S(1)} %constant_dynamic-update-slice_fusion.6), channel_id=1, source_target_pairs={{0,8},{4,12},{8,0},{12,4},{1,9},{5,13},{9,1},{13,5},{2,10},{6,14},... | collective-permute-start | bytes 786440 | tf_op jit(solution)/shard_map/ppermute | solution.py:100
  53.3 0.8 %convolution_convert_fusion.7 = bf16[128,512]{1,0:T(8,128)(2,1)S(1)} fusion(bf16[128,2048]{1,0:T(8,128)(2,1)S(1)} %collective-permute-done.9, bf16[512,2048]{1,0:T(8,128)(2,1)S(1)} %bitcast.72), kind=kOutput, calls=%fused_computation.8 | convolution fusion | flops 268500992 | bytes 2752512 | tf_op jit(solution)/shard_map/dot_general | solution.py:128
  54.2 0.8 %convolution_convert_fusion.6 = bf16[128,512]{1,0:T(8,128)(2,1)S(1)} fusion(bf16[128,2048]{1,0:T(8,128)(2,1)S(1)} %collective-permute-done.13, bf16[512,2048]{1,0:T(8,128)(2,1)S(1)} %bitcast.73), kind=kOutput, calls=%fused_computation.7 | convolution fusion | flops 268500992 | bytes 2752512 | tf_op jit(solution)/shard_map/dot_general | solution.py:128
  55.0 0.1 broadcast_select_fusion.12
  55.1 2.0 %collective-permute-start.16 = (bf16[1,128,512]{2,1,0:T(8,128)(2,1)S(1)}, bf16[1,128,512]{2,1,0:T(8,128)(2,1)S(1)}, u32[]{:S(2)}, u32[]{:S(2)}) collective-permute-start(bf16[1,128,512]{2,1,0:T(8,128)(2,1)S(1)} %get-tuple-element.123), channel_id=1, source_target_pairs={{0,3},{1,2},{2,1},{3,0},{4,7},{5,6},{6,5},{7,4},{8,11},{9,10},{10,... | collective-permute-start | bytes 393224 | tf_op jit(solution)/shard_map/ppermute | solution.py:100
  57.1 0.1 broadcast_select_fusion.13
  57.2 1.6 %collective-permute-start.15 = (bf16[1,128,512]{2,1,0:T(8,128)(2,1)S(1)}, bf16[1,128,512]{2,1,0:T(8,128)(2,1)S(1)}, u32[]{:S(2)}, u32[]{:S(2)}) collective-permute-start(bf16[1,128,512]{2,1,0:T(8,128)(2,1)S(1)} %get-tuple-element.93), channel_id=1, source_target_pairs={{0,2},{1,3},{2,0},{3,1},{4,6},{5,7},{6,4},{7,5},{8,10},{9,11},{10,... | collective-permute-start | bytes 393224 | tf_op jit(solution)/shard_map/ppermute | solution.py:100
  58.8 1.0 %collective-permute-start.14 = (bf16[1,128,512]{2,1,0:T(8,128)(2,1)S(1)}, bf16[1,128,512]{2,1,0:T(8,128)(2,1)S(1)}, u32[]{:S(2)}, u32[]{:S(2)}) collective-permute-start(bf16[1,128,512]{2,1,0:T(8,128)(2,1)S(1)} %get-tuple-element.94), channel_id=1, source_target_pairs={{0,1},{1,0},{2,3},{3,2},{4,5},{5,4},{6,7},{7,6},{8,9},{9,8},{10,11... | collective-permute-start | bytes 393224 | tf_op jit(solution)/shard_map/ppermute | solution.py:100
  59.8 0.1 collective-permute-start.18
  59.9 0.8 %convolution_convert_fusion.1 = bf16[128,512]{1,0:T(8,128)(2,1)S(1)} fusion(bf16[128,2048]{1,0:T(8,128)(2,1)S(1)} %pad_maximum_fusion.2, bf16[512,2048]{1,0:T(8,128)(2,1)S(1)} %bitcast.74), kind=kOutput, calls=%fused_computation.2 | convolution fusion | flops 268500992 | bytes 2752512 | tf_op jit(solution)/shard_map/dot_general | solution.py:128
  60.7 1.9 %collective-permute-done.21 = bf16[64,2048]{1,0:T(8,128)(2,1)S(1)} collective-permute-done((bf16[64,2048]{1,0:T(8,128)(2,1)S(1)}, bf16[64,2048]{1,0:T(8,128)(2,1)S(1)}, u32[]{:S(2)}, u32[]{:S(2)}) %collective-permute-start.21) | collective-permute-done | bytes 262176 | tf_op jit(solution)/shard_map/ppermute | solution.py:100
  62.6 0.1 collective-permute-start.22
  62.7 0.8 %convolution_convert_fusion = bf16[128,512]{1,0:T(8,128)(2,1)S(1)} fusion(bf16[128,2048]{1,0:T(8,128)(2,1)S(1)} %pad_maximum_fusion.3, bf16[512,2048]{1,0:T(8,128)(2,1)S(1)} %bitcast.75), kind=kOutput, calls=%fused_computation.1 | convolution fusion | flops 268500992 | bytes 2752512 | tf_op jit(solution)/shard_map/dot_general | solution.py:128
  63.6 0.8 %convolution_convert_fusion.3 = bf16[128,512]{1,0:T(8,128)(2,1)S(1)} fusion(bf16[128,2048]{1,0:T(8,128)(2,1)S(1)} %collective-permute-done.18, bf16[512,2048]{1,0:T(8,128)(2,1)S(1)} %bitcast.76), kind=kOutput, calls=%fused_computation.4 | convolution fusion | flops 268500992 | bytes 2752512 | tf_op jit(solution)/shard_map/dot_general | solution.py:128
  64.4 0.2 collective-permute-done.22
  64.6 0.8 %convolution_convert_fusion.2 = bf16[128,512]{1,0:T(8,128)(2,1)S(1)} fusion(bf16[128,2048]{1,0:T(8,128)(2,1)S(1)} %collective-permute-done.22, bf16[512,2048]{1,0:T(8,128)(2,1)S(1)} %bitcast.77), kind=kOutput, calls=%fused_computation.3 | convolution fusion | flops 268500992 | bytes 2752512 | tf_op jit(solution)/shard_map/dot_general | solution.py:128
  65.4 0.1 broadcast_select_fusion.9
  65.5 3.1 %collective-permute-start.25 = (bf16[1,128,512]{2,1,0:T(8,128)(2,1)S(1)}, bf16[1,128,512]{2,1,0:T(8,128)(2,1)S(1)}, u32[]{:S(2)}, u32[]{:S(2)}) collective-permute-start(bf16[1,128,512]{2,1,0:T(8,128)(2,1)S(1)} %get-tuple-element.122), channel_id=1, source_target_pairs={{0,3},{1,2},{2,1},{3,0},{4,7},{5,6},{6,5},{7,4},{8,11},{9,10},{10,... | collective-permute-start | bytes 393224 | tf_op jit(solution)/shard_map/ppermute | solution.py:100
  68.6 0.6 collective-permute-start.24
  69.2 0.1 broadcast_select_fusion.11
  69.4 0.8 collective-permute-start.23
  70.2 0.1 broadcast_select_fusion.31
  70.3 7.3 %collective-permute-done.23 = bf16[1,128,512]{2,1,0:T(8,128)(2,1)S(1)} collective-permute-done((bf16[1,128,512]{2,1,0:T(8,128)(2,1)S(1)}, bf16[1,128,512]{2,1,0:T(8,128)(2,1)S(1)}, u32[]{:S(2)}, u32[]{:S(2)}) %collective-permute-start.23) | collective-permute-done | bytes 131104 | tf_op jit(solution)/shard_map/ppermute | solution.py:100
  77.5 3.9 %collective-permute-done.24 = bf16[1,128,512]{2,1,0:T(8,128)(2,1)S(1)} collective-permute-done((bf16[1,128,512]{2,1,0:T(8,128)(2,1)S(1)}, bf16[1,128,512]{2,1,0:T(8,128)(2,1)S(1)}, u32[]{:S(2)}, u32[]{:S(2)}) %collective-permute-start.24) | collective-permute-done | bytes 131104 | tf_op jit(solution)/shard_map/ppermute | solution.py:100
  81.4 0.1 broadcast_select_fusion.27
  81.5 0.1 broadcast_select_fusion.26
  81.6 0.8 %maximum_bitcast_fusion = f32[256,512]{1,0:T(8,128)} fusion(f32[1,128,512]{2,1,0:T(8,128)S(1)} %bitcast.80, f32[1,128,512]{2,1,0:T(8,128)S(1)} %bitcast.79), kind=kLoop, calls=%fused_computation.13 | loop fusion | flops 131072 | bytes 1048576 | tf_op jit(solution)/shard_map/reshape | solution.py:203
  (54 shorter events, 0.6 us)
Async XLA Ops:
  0.0 1.2 %copy-start = (bf16[256,16,128]{2,1,0:T(8,128)(2,1)S(1)}, bf16[256,16,128]{2,1,0:T(8,128)(2,1)}, u32[]{:S(2)}) copy-start(bf16[256,16,128]{2,1,0:T(8,128)(2,1)} %param.5) | copy-start | bytes 3145732
  1.3 10.7 %collective-permute-start = (bf16[32,16,128]{2,1,0:T(8,128)(2,1)S(1)}, bf16[32,16,128]{2,1,0:T(8,128)(2,1)S(1)}, u32[]{:S(2)}, u32[]{:S(2)}) collective-permute-start(bf16[32,16,128]{2,1,0:T(8,128)(2,1)S(1)} %constant_dynamic-slice_fusion.4), channel_id=1, source_target_pairs={{0,3},{1,2},{2,1},{3,0},{4,7},{5,6},{6,5},{7,4},{8,11},{9,10},{10,... | collective-permute-start | bytes 393224 | tf_op jit(solution)/shard_map/ppermute | solution.py:100
  6.4 12.6 %collective-permute-start.1 = (bf16[32,16,128]{2,1,0:T(8,128)(2,1)S(1)}, bf16[32,16,128]{2,1,0:T(8,128)(2,1)S(1)}, u32[]{:S(2)}, u32[]{:S(2)}) collective-permute-start(bf16[32,16,128]{2,1,0:T(8,128)(2,1)S(1)} %constant_dynamic-slice_fusion.5), channel_id=1, source_target_pairs={{0,2},{1,3},{2,0},{3,1},{4,6},{5,7},{6,4},{7,5},{8,10},{9,11},{10,... | collective-permute-start | bytes 393224 | tf_op jit(solution)/shard_map/ppermute | solution.py:100
  6.4 12.6 %collective-permute-start.2 = (bf16[32,16,128]{2,1,0:T(8,128)(2,1)S(1)}, bf16[32,16,128]{2,1,0:T(8,128)(2,1)S(1)}, u32[]{:S(2)}, u32[]{:S(2)}) collective-permute-start(bf16[32,16,128]{2,1,0:T(8,128)(2,1)S(1)} %constant_dynamic-slice_fusion.6), channel_id=1, source_target_pairs={{0,1},{1,0},{2,3},{3,2},{4,5},{5,4},{6,7},{7,6},{8,9},{9,8},{10,11... | collective-permute-start | bytes 393224 | tf_op jit(solution)/shard_map/ppermute | solution.py:100
  8.2 3.7 %copy-start.1 = (f32[128,128]{1,0:T(8,128)S(1)}, f32[128,128]{1,0:T(8,128)}, u32[]{:S(2)}) copy-start(f32[128,128]{1,0:T(8,128)} %refs_6_.3) | copy-start | bytes 196612
  8.2 10.8 %copy-start.2 = (f32[64,128]{1,0:T(8,128)S(1)}, f32[64,128]{1,0:T(8,128)}, u32[]{:S(2)}) copy-start(f32[64,128]{1,0:T(8,128)} %refs_8_.3) | copy-start | bytes 98308
  12.1 13.9 %collective-permute-start.4 = (bf16[32,16,128]{2,1,0:T(8,128)(2,1)S(1)}, bf16[32,16,128]{2,1,0:T(8,128)(2,1)S(1)}, u32[]{:S(2)}, u32[]{:S(2)}) collective-permute-start(bf16[32,16,128]{2,1,0:T(8,128)(2,1)S(1)} %constant_dynamic-slice_fusion.1), channel_id=1, source_target_pairs={{0,1},{1,0},{2,3},{3,2},{4,5},{5,4},{6,7},{7,6},{8,9},{9,8},{10,11... | collective-permute-start | bytes 393224 | tf_op jit(solution)/shard_map/ppermute | solution.py:100
  16.4 11.6 %collective-permute-start.5 = (bf16[32,16,128]{2,1,0:T(8,128)(2,1)S(1)}, bf16[32,16,128]{2,1,0:T(8,128)(2,1)S(1)}, u32[]{:S(2)}, u32[]{:S(2)}) collective-permute-start(bf16[32,16,128]{2,1,0:T(8,128)(2,1)S(1)} %constant_dynamic-slice_fusion.2), channel_id=1, source_target_pairs={{0,2},{1,3},{2,0},{3,1},{4,6},{5,7},{6,4},{7,5},{8,10},{9,11},{10,... | collective-permute-start | bytes 393224 | tf_op jit(solution)/shard_map/ppermute | solution.py:100
  17.6 10.3 %collective-permute-start.6 = (bf16[32,16,128]{2,1,0:T(8,128)(2,1)S(1)}, bf16[32,16,128]{2,1,0:T(8,128)(2,1)S(1)}, u32[]{:S(2)}, u32[]{:S(2)}) collective-permute-start(bf16[32,16,128]{2,1,0:T(8,128)(2,1)S(1)} %constant_dynamic-slice_fusion.3), channel_id=1, source_target_pairs={{0,3},{1,2},{2,1},{3,0},{4,7},{5,6},{6,5},{7,4},{8,11},{9,10},{10,... | collective-permute-start | bytes 393224 | tf_op jit(solution)/shard_map/ppermute | solution.py:100
  21.3 8.0 %collective-permute-start.3 = (bf16[32,2048]{1,0:T(8,128)(2,1)S(1)}, bf16[32,2048]{1,0:T(8,128)(2,1)S(1)}, u32[]{:S(2)}, u32[]{:S(2)}) collective-permute-start(bf16[32,2048]{1,0:T(8,128)(2,1)S(1)} %get-tuple-element.67), channel_id=1, source_target_pairs={{0,1},{1,0},{2,3},{3,2},{4,5},{5,4},{6,7},{7,6},{8,9},{9,8},{10,11... | collective-permute-start | bytes 393224 | tf_op jit(solution)/shard_map/ppermute | solution.py:100
  22.2 17.2 %collective-permute-start.10 = (bf16[32,2048]{1,0:T(8,128)(2,1)S(1)}, bf16[32,2048]{1,0:T(8,128)(2,1)S(1)}, u32[]{:S(2)}, u32[]{:S(2)}) collective-permute-start(bf16[32,2048]{1,0:T(8,128)(2,1)S(1)} %get-tuple-element.89), channel_id=1, source_target_pairs={{0,2},{1,3},{2,0},{3,1},{4,6},{5,7},{6,4},{7,5},{8,10},{9,11},{10,... | collective-permute-start | bytes 393224 | tf_op jit(solution)/shard_map/ppermute | solution.py:100
  26.0 13.4 %collective-permute-start.11 = (bf16[32,2048]{1,0:T(8,128)(2,1)S(1)}, bf16[32,2048]{1,0:T(8,128)(2,1)S(1)}, u32[]{:S(2)}, u32[]{:S(2)}) collective-permute-start(bf16[32,2048]{1,0:T(8,128)(2,1)S(1)} %get-tuple-element.90), channel_id=1, source_target_pairs={{0,3},{1,2},{2,1},{3,0},{4,7},{5,6},{6,5},{7,4},{8,11},{9,10},{10,... | collective-permute-start | bytes 393224 | tf_op jit(solution)/shard_map/ppermute | solution.py:100
  29.4 15.2 %collective-permute-start.8 = (bf16[64,2048]{1,0:T(8,128)(2,1)S(1)}, bf16[64,2048]{1,0:T(8,128)(2,1)S(1)}, u32[]{:S(2)}, u32[]{:S(2)}) collective-permute-start(bf16[64,2048]{1,0:T(8,128)(2,1)S(1)} %constant_dynamic-update-slice_fusion), channel_id=1, source_target_pairs={{0,8},{4,12},{8,0},{12,4},{1,9},{5,13},{9,1},{13,5},{2,10},{6,14},... | collective-permute-start | bytes 786440 | tf_op jit(solution)/shard_map/ppermute | solution.py:100
  33.1 11.4 %collective-permute-start.7 = (bf16[32,2048]{1,0:T(8,128)(2,1)S(1)}, bf16[32,2048]{1,0:T(8,128)(2,1)S(1)}, u32[]{:S(2)}, u32[]{:S(2)}) collective-permute-start(bf16[32,2048]{1,0:T(8,128)(2,1)S(1)} %get-tuple-element.81), channel_id=1, source_target_pairs={{0,1},{1,0},{2,3},{3,2},{4,5},{5,4},{6,7},{7,6},{8,9},{9,8},{10,11... | collective-permute-start | bytes 393224 | tf_op jit(solution)/shard_map/ppermute | solution.py:100
  39.5 6.8 %collective-permute-start.12 = (bf16[64,2048]{1,0:T(8,128)(2,1)S(1)}, bf16[64,2048]{1,0:T(8,128)(2,1)S(1)}, u32[]{:S(2)}, u32[]{:S(2)}) collective-permute-start(bf16[64,2048]{1,0:T(8,128)(2,1)S(1)} %constant_dynamic-update-slice_fusion.2), channel_id=1, source_target_pairs={{0,8},{4,12},{8,0},{12,4},{1,9},{5,13},{9,1},{13,5},{2,10},{6,14},... | collective-permute-start | bytes 786440 | tf_op jit(solution)/shard_map/ppermute | solution.py:100
  40.1 6.3 %copy-start.3 = (bf16[64,8,16,128]{3,1,2,0:T(8,128)(2,1)S(1)}, bf16[64,8,16,128]{3,1,2,0:T(8,128)(2,1)}, u32[]{:S(2)}) copy-start(bf16[64,8,16,128]{3,1,2,0:T(8,128)(2,1)} %copy.19) | copy-start | bytes 6291460
  40.1 12.0 %collective-permute-start.19 = (bf16[32,2048]{1,0:T(8,128)(2,1)S(1)}, bf16[32,2048]{1,0:T(8,128)(2,1)S(1)}, u32[]{:S(2)}, u32[]{:S(2)}) collective-permute-start(bf16[32,2048]{1,0:T(8,128)(2,1)S(1)} %get-tuple-element.100), channel_id=1, source_target_pairs={{0,2},{1,3},{2,0},{3,1},{4,6},{5,7},{6,4},{7,5},{8,10},{9,11},{10,... | collective-permute-start | bytes 393224 | tf_op jit(solution)/shard_map/ppermute | solution.py:100
  43.2 8.8 %collective-permute-start.20 = (bf16[32,2048]{1,0:T(8,128)(2,1)S(1)}, bf16[32,2048]{1,0:T(8,128)(2,1)S(1)}, u32[]{:S(2)}, u32[]{:S(2)}) collective-permute-start(bf16[32,2048]{1,0:T(8,128)(2,1)S(1)} %get-tuple-element.101), channel_id=1, source_target_pairs={{0,3},{1,2},{2,1},{3,0},{4,7},{5,6},{6,5},{7,4},{8,11},{9,10},{10,... | collective-permute-start | bytes 393224 | tf_op jit(solution)/shard_map/ppermute | solution.py:100
  44.6 8.7 %collective-permute-start.9 = (bf16[128,2048]{1,0:T(8,128)(2,1)S(1)}, bf16[128,2048]{1,0:T(8,128)(2,1)S(1)}, u32[]{:S(2)}, u32[]{:S(2)}) collective-permute-start(bf16[128,2048]{1,0:T(8,128)(2,1)S(1)} %pad_maximum_fusion), channel_id=1, source_target_pairs={{0,4},{4,0},{8,12},{12,8},{1,5},{5,1},{9,13},{13,9},{2,6},{6,2},{1... | collective-permute-start | bytes 1572872 | tf_op jit(solution)/shard_map/ppermute | solution.py:100
  46.4 7.8 %collective-permute-start.13 = (bf16[128,2048]{1,0:T(8,128)(2,1)S(1)}, bf16[128,2048]{1,0:T(8,128)(2,1)S(1)}, u32[]{:S(2)}, u32[]{:S(2)}) collective-permute-start(bf16[128,2048]{1,0:T(8,128)(2,1)S(1)} %pad_maximum_fusion.1), channel_id=1, source_target_pairs={{0,4},{4,0},{8,12},{12,8},{1,5},{5,1},{9,13},{13,9},{2,6},{6,2},{1... | collective-permute-start | bytes 1572872 | tf_op jit(solution)/shard_map/ppermute | solution.py:100
  48.2 11.6 %collective-permute-start.17 = (bf16[64,2048]{1,0:T(8,128)(2,1)S(1)}, bf16[64,2048]{1,0:T(8,128)(2,1)S(1)}, u32[]{:S(2)}, u32[]{:S(2)}) collective-permute-start(bf16[64,2048]{1,0:T(8,128)(2,1)S(1)} %constant_dynamic-update-slice_fusion.4), channel_id=1, source_target_pairs={{0,8},{4,12},{8,0},{12,4},{1,9},{5,13},{9,1},{13,5},{2,10},{6,14},... | collective-permute-start | bytes 786440 | tf_op jit(solution)/shard_map/ppermute | solution.py:100
  52.1 10.4 %collective-permute-start.21 = (bf16[64,2048]{1,0:T(8,128)(2,1)S(1)}, bf16[64,2048]{1,0:T(8,128)(2,1)S(1)}, u32[]{:S(2)}, u32[]{:S(2)}) collective-permute-start(bf16[64,2048]{1,0:T(8,128)(2,1)S(1)} %constant_dynamic-update-slice_fusion.6), channel_id=1, source_target_pairs={{0,8},{4,12},{8,0},{12,4},{1,9},{5,13},{9,1},{13,5},{2,10},{6,14},... | collective-permute-start | bytes 786440 | tf_op jit(solution)/shard_map/ppermute | solution.py:100
  55.1 15.1 %collective-permute-start.16 = (bf16[1,128,512]{2,1,0:T(8,128)(2,1)S(1)}, bf16[1,128,512]{2,1,0:T(8,128)(2,1)S(1)}, u32[]{:S(2)}, u32[]{:S(2)}) collective-permute-start(bf16[1,128,512]{2,1,0:T(8,128)(2,1)S(1)} %get-tuple-element.123), channel_id=1, source_target_pairs={{0,3},{1,2},{2,1},{3,0},{4,7},{5,6},{6,5},{7,4},{8,11},{9,10},{10,... | collective-permute-start | bytes 393224 | tf_op jit(solution)/shard_map/ppermute | solution.py:100
  57.2 13.0 %collective-permute-start.15 = (bf16[1,128,512]{2,1,0:T(8,128)(2,1)S(1)}, bf16[1,128,512]{2,1,0:T(8,128)(2,1)S(1)}, u32[]{:S(2)}, u32[]{:S(2)}) collective-permute-start(bf16[1,128,512]{2,1,0:T(8,128)(2,1)S(1)} %get-tuple-element.93), channel_id=1, source_target_pairs={{0,2},{1,3},{2,0},{3,1},{4,6},{5,7},{6,4},{7,5},{8,10},{9,11},{10,... | collective-permute-start | bytes 393224 | tf_op jit(solution)/shard_map/ppermute | solution.py:100
  58.8 10.6 %collective-permute-start.14 = (bf16[1,128,512]{2,1,0:T(8,128)(2,1)S(1)}, bf16[1,128,512]{2,1,0:T(8,128)(2,1)S(1)}, u32[]{:S(2)}, u32[]{:S(2)}) collective-permute-start(bf16[1,128,512]{2,1,0:T(8,128)(2,1)S(1)} %get-tuple-element.94), channel_id=1, source_target_pairs={{0,1},{1,0},{2,3},{3,2},{4,5},{5,4},{6,7},{7,6},{8,9},{9,8},{10,11... | collective-permute-start | bytes 393224 | tf_op jit(solution)/shard_map/ppermute | solution.py:100
  59.8 3.8 %collective-permute-start.18 = (bf16[128,2048]{1,0:T(8,128)(2,1)S(1)}, bf16[128,2048]{1,0:T(8,128)(2,1)S(1)}, u32[]{:S(2)}, u32[]{:S(2)}) collective-permute-start(bf16[128,2048]{1,0:T(8,128)(2,1)S(1)} %pad_maximum_fusion.2), channel_id=1, source_target_pairs={{0,4},{4,0},{8,12},{12,8},{1,5},{5,1},{9,13},{13,9},{2,6},{6,2},{1... | collective-permute-start | bytes 1572872 | tf_op jit(solution)/shard_map/ppermute | solution.py:100
  62.6 2.0 %collective-permute-start.22 = (bf16[128,2048]{1,0:T(8,128)(2,1)S(1)}, bf16[128,2048]{1,0:T(8,128)(2,1)S(1)}, u32[]{:S(2)}, u32[]{:S(2)}) collective-permute-start(bf16[128,2048]{1,0:T(8,128)(2,1)S(1)} %pad_maximum_fusion.3), channel_id=1, source_target_pairs={{0,4},{4,0},{8,12},{12,8},{1,5},{5,1},{9,13},{13,9},{2,6},{6,2},{1... | collective-permute-start | bytes 1572872 | tf_op jit(solution)/shard_map/ppermute | solution.py:100
  65.5 15.8 %collective-permute-start.25 = (bf16[1,128,512]{2,1,0:T(8,128)(2,1)S(1)}, bf16[1,128,512]{2,1,0:T(8,128)(2,1)S(1)}, u32[]{:S(2)}, u32[]{:S(2)}) collective-permute-start(bf16[1,128,512]{2,1,0:T(8,128)(2,1)S(1)} %get-tuple-element.122), channel_id=1, source_target_pairs={{0,3},{1,2},{2,1},{3,0},{4,7},{5,6},{6,5},{7,4},{8,11},{9,10},{10,... | collective-permute-start | bytes 393224 | tf_op jit(solution)/shard_map/ppermute | solution.py:100
  68.6 12.8 %collective-permute-start.24 = (bf16[1,128,512]{2,1,0:T(8,128)(2,1)S(1)}, bf16[1,128,512]{2,1,0:T(8,128)(2,1)S(1)}, u32[]{:S(2)}, u32[]{:S(2)}) collective-permute-start(bf16[1,128,512]{2,1,0:T(8,128)(2,1)S(1)} %get-tuple-element.106), channel_id=1, source_target_pairs={{0,2},{1,3},{2,0},{3,1},{4,6},{5,7},{6,4},{7,5},{8,10},{9,11},{10,... | collective-permute-start | bytes 393224 | tf_op jit(solution)/shard_map/ppermute | solution.py:100
  69.4 8.2 %collective-permute-start.23 = (bf16[1,128,512]{2,1,0:T(8,128)(2,1)S(1)}, bf16[1,128,512]{2,1,0:T(8,128)(2,1)S(1)}, u32[]{:S(2)}, u32[]{:S(2)}) collective-permute-start(bf16[1,128,512]{2,1,0:T(8,128)(2,1)S(1)} %get-tuple-element.107), channel_id=1, source_target_pairs={{0,1},{1,0},{2,3},{3,2},{4,5},{5,4},{6,7},{7,6},{8,9},{9,8},{10,11... | collective-permute-start | bytes 393224 | tf_op jit(solution)/shard_map/ppermute | solution.py:100

commit v15 on v14

--- a/solution.py
+++ b/solution.py
@@ -126,7 +126,12 @@
     values = []
     for block in (near, far):
         value = lax.dot_general(block, train_flat, contract, preferred_element_type=jnp.float32)
-        values.append(value.astype(jnp.bfloat16).reshape(shares // 2, -1, train_flat.shape[0]))
+        values.append(value.astype(jnp.bfloat16))
+    return values
+
+
+def split_shares(values, shares):
+    values = [value.reshape(shares // 2, -1, value.shape[1]) for value in values]
     return [values[at % 2][at // 2] for at in range(shares)]
 
 
@@ -172,23 +177,29 @@
     made = condition(pieces[1], basis, in_basis, corrections)
     rows.append(exchanged(made, slices))
     rows[1][:half], spread = lax.optimization_barrier((rows[1][:half], spread))
-    near_rows, far_rows = list(range(half)), list(range(half, slices))
-    orders = [(near_rows, far_rows)] * 2
+    orders = [(range(half), range(half, slices))] * 2
+    ahead = over_shares(rows[1][:half], shares)
     came = []
     for chunk, part in enumerate(parts):
         each = part // slices
         groups = []
-        order = sum(orders[chunk], [])
+        order = list(range(slices))
         for members in orders[chunk]:
             group = [rows[chunk][at] for at in members]
+            if groups:
+                spread = over_shares(after(group, near_before) if chunk else group, shares)
+            elif chunk:
+                spread = ahead
+            if groups and not chunk:
+                spread, ahead = lax.optimization_barrier((spread, ahead))
+            tokens = came[:1]
             if chunk and groups:
-                group = after(group, near_before)
-            if chunk or groups:
-                spread = over_shares(group, shares)
-            near = lax.optimization_barrier(jnp.concatenate(after(spread, *came[:1]), axis=0))
+                tokens = groups[0][:1]
+            near = lax.optimization_barrier(jnp.concatenate(after(spread, *tokens), axis=0))
             far = crossed(near, "dp", shares, 1)
             groups.append(products(near, far, train_flat, shares))
         near_before = near
+        groups = [split_shares(values, shares) for values in groups]
         values = [jnp.concatenate(pair, axis=0) for pair in zip(*groups)]
         values = [jnp.stack(values[at * owned:(at + 1) * owned]) for at in range(slices)]
         came = exchanged(in_turn(turned(values, here ^ (share // owned))), slices)

time: 82.7 us -> 85 us (1.028)
  waiting for transfers between devices: 21.2 us -> 24.1 us
    ppermute x26, waiting for transfers between devices: 21.2 us -> 24.1 us  [crossed(): return lax.ppermute(value, axis, [(at, at ^ mask) for at in range(size)])]
where the time goes in v15:
time: 85 us; the launch traced here: 84.8 us
  starting transfers between devices  41 us (48%)
  waiting for transfers between devices  24.1 us (28%)
  matrix products  6.66 us (8%)
  local copies, waits for them, and re-layouts  6.29 us (7%)
  Pallas kernels  4.47 us (5%)
  other arithmetic  1.71 us (2%)
    ppermute x26, starting transfers between devices, crossed(): return lax.ppermute(value, axis, [(at, at ^ mask) for at in range(size)])  41 us
    ppermute x26, waiting for transfers between devices, crossed(): return lax.ppermute(value, axis, [(at, at ^ mask) for at in range(size)])  24.1 us
    dot_general x8, matrix products, products(): lax.dot_general(block, train_flat, contract, preferred_element_type=jnp.f...  6.66 us
    unnamed x18, local copies, waits for them, and re-layouts  5.21 us
    pallas_call x2, Pallas kernels, condition_fast(): pl.pallas_call(functools.partial(condition_kernel, slices, rows_here), gr...  4.47 us
  transfers between devices with their start and end apart: 26, of which 8 were waited for; matrix products, arithmetic and copies ran while one was open for 15% of the time, Pallas kernels for 5%

profile of v15, /device:TPU:0, one launch (start us, length us, event | category | flops | bytes accessed | tf_op | source)
XLA Modules:
  0.0 84.8 jit_solution(16253150694267085360)
XLA Ops:
  0.0 1.2 %copy-done = bf16[256,16,128]{2,1,0:T(8,128)(2,1)S(1)} copy-done((bf16[256,16,128]{2,1,0:T(8,128)(2,1)S(1)}, bf16[256,16,128]{2,1,0:T(8,128)(2,1)}, u32[]{:S(2)}) %copy-start) | copy-done | bytes 1048600
  1.3 5.1 %collective-permute-start = (bf16[32,16,128]{2,1,0:T(8,128)(2,1)S(1)}, bf16[32,16,128]{2,1,0:T(8,128)(2,1)S(1)}, u32[]{:S(2)}, u32[]{:S(2)}) collective-permute-start(bf16[32,16,128]{2,1,0:T(8,128)(2,1)S(1)} %constant_dynamic-slice_fusion.4), channel_id=1, source_target_pairs={{0,3},{1,2},{2,1},{3,0},{4,7},{5,6},{6,5},{7,4},{8,11},{9,10},{10,... | collective-permute-start | bytes 393224 | tf_op jit(solution)/shard_map/ppermute | solution.py:100
  6.4 0.6 collective-permute-start.2
  7.1 0.7 fusion
  7.8 0.1 copy.13
  7.9 0.1 copy.14
  8.0 0.1 copy.15
  8.1 0.1 copy.16
  8.2 0.0 copy-start.1
  8.2 0.0 copy-start.2
  8.2 3.5 %copy.19 = bf16[64,8,16,128]{3,1,2,0:T(8,128)(2,1)} copy(bf16[64,8,16,128]{3,2,1,0:T(8,128)(2,1)} %bitcast.78) | data formatting | bytes 4194304
  11.7 0.1 pad_maximum_fusion.14
  11.8 0.1 copy.11.refs_4_
  11.9 0.0 copy-done.1
  11.9 0.1 copy.10
  12.1 4.2 %collective-permute-start.4 = (bf16[32,16,128]{2,1,0:T(8,128)(2,1)S(1)}, bf16[32,16,128]{2,1,0:T(8,128)(2,1)S(1)}, u32[]{:S(2)}, u32[]{:S(2)}) collective-permute-start(bf16[32,16,128]{2,1,0:T(8,128)(2,1)S(1)} %constant_dynamic-slice_fusion.1), channel_id=1, source_target_pairs={{0,1},{1,0},{2,3},{3,2},{4,5},{5,4},{6,7},{7,6},{8,9},{9,8},{10,11... | collective-permute-start | bytes 393224 | tf_op jit(solution)/shard_map/ppermute | solution.py:100
  16.4 1.3 %collective-permute-start.5 = (bf16[32,16,128]{2,1,0:T(8,128)(2,1)S(1)}, bf16[32,16,128]{2,1,0:T(8,128)(2,1)S(1)}, u32[]{:S(2)}, u32[]{:S(2)}) collective-permute-start(bf16[32,16,128]{2,1,0:T(8,128)(2,1)S(1)} %constant_dynamic-slice_fusion.2), channel_id=1, source_target_pairs={{0,2},{1,3},{2,0},{3,1},{4,6},{5,7},{6,4},{7,5},{8,10},{9,11},{10,... | collective-permute-start | bytes 393224 | tf_op jit(solution)/shard_map/ppermute | solution.py:100
  17.6 1.4 %collective-permute-start.6 = (bf16[32,16,128]{2,1,0:T(8,128)(2,1)S(1)}, bf16[32,16,128]{2,1,0:T(8,128)(2,1)S(1)}, u32[]{:S(2)}, u32[]{:S(2)}) collective-permute-start(bf16[32,16,128]{2,1,0:T(8,128)(2,1)S(1)} %constant_dynamic-slice_fusion.3), channel_id=1, source_target_pairs={{0,3},{1,2},{2,1},{3,0},{4,7},{5,6},{6,5},{7,4},{8,11},{9,10},{10,... | collective-permute-start | bytes 393224 | tf_op jit(solution)/shard_map/ppermute | solution.py:100
  19.0 2.2 %shard_map.55 = (bf16[32,2048]{1,0:T(8,128)(2,1)S(1)}, bf16[32,2048]{1,0:T(8,128)(2,1)S(1)}, bf16[32,2048]{1,0:T(8,128)(2,1)S(1)}, bf16[32,2048]{1,0:T(8,128)(2,1)S(1)}) custom-call(bf16[32,16,128]{2,1,0:T(8,128)(2,1)S(1)} %collective-permute-done.refs_0_, bf16[32,16,128]{2,1,0:T(8,128)(2,1)S(1)} %collective-permute-done.1.refs_1_, ...), custom_call_target="tpu_custom_call" | custom-call | tf_op jit(solution)/shard_map/pallas_call | solution.py:75
  21.3 0.9 %collective-permute-start.3 = (bf16[32,2048]{1,0:T(8,128)(2,1)S(1)}, bf16[32,2048]{1,0:T(8,128)(2,1)S(1)}, u32[]{:S(2)}, u32[]{:S(2)}) collective-permute-start(bf16[32,2048]{1,0:T(8,128)(2,1)S(1)} %get-tuple-element.71), channel_id=1, source_target_pairs={{0,1},{1,0},{2,3},{3,2},{4,5},{5,4},{6,7},{7,6},{8,9},{9,8},{10,11... | collective-permute-start | bytes 393224 | tf_op jit(solution)/shard_map/ppermute | solution.py:100
  22.2 3.8 %collective-permute-start.10 = (bf16[32,2048]{1,0:T(8,128)(2,1)S(1)}, bf16[32,2048]{1,0:T(8,128)(2,1)S(1)}, u32[]{:S(2)}, u32[]{:S(2)}) collective-permute-start(bf16[32,2048]{1,0:T(8,128)(2,1)S(1)} %get-tuple-element.93), channel_id=1, source_target_pairs={{0,2},{1,3},{2,0},{3,1},{4,6},{5,7},{6,4},{7,5},{8,10},{9,11},{10,... | collective-permute-start | bytes 393224 | tf_op jit(solution)/shard_map/ppermute | solution.py:100
  26.0 0.3 collective-permute-start.11
  26.4 1.6 %collective-permute-done.5.refs_1_ = bf16[32,16,128]{2,1,0:T(8,128)(2,1)S(1)} collective-permute-done((bf16[32,16,128]{2,1,0:T(8,128)(2,1)S(1)}, bf16[32,16,128]{2,1,0:T(8,128)(2,1)S(1)}, u32[]{:S(2)}, u32[]{:S(2)}) %collective-permute-start.5) | collective-permute-done | bytes 131104 | tf_op jit(solution)/shard_map/ppermute | solution.py:100
  27.9 1.4 %collective-permute-done.3 = bf16[32,2048]{1,0:T(8,128)(2,1)S(1)} collective-permute-done((bf16[32,2048]{1,0:T(8,128)(2,1)S(1)}, bf16[32,2048]{1,0:T(8,128)(2,1)S(1)}, u32[]{:S(2)}, u32[]{:S(2)}) %collective-permute-start.3) | collective-permute-done | bytes 131104 | tf_op jit(solution)/shard_map/ppermute | solution.py:100
  29.4 1.5 %collective-permute-start.8 = (bf16[64,2048]{1,0:T(8,128)(2,1)S(1)}, bf16[64,2048]{1,0:T(8,128)(2,1)S(1)}, u32[]{:S(2)}, u32[]{:S(2)}) collective-permute-start(bf16[64,2048]{1,0:T(8,128)(2,1)S(1)} %constant_dynamic-update-slice_fusion), channel_id=1, source_target_pairs={{0,8},{4,12},{8,0},{12,4},{1,9},{5,13},{9,1},{13,5},{2,10},{6,14},... | collective-permute-start | bytes 786440 | tf_op jit(solution)/shard_map/ppermute | solution.py:100
  30.9 2.2 %shard_map.56 = (bf16[32,2048]{1,0:T(8,128)(2,1)S(1)}, bf16[32,2048]{1,0:T(8,128)(2,1)S(1)}, bf16[32,2048]{1,0:T(8,128)(2,1)S(1)}, bf16[32,2048]{1,0:T(8,128)(2,1)S(1)}) custom-call(bf16[32,16,128]{2,1,0:T(8,128)(2,1)S(1)} %collective-permute-done.6.refs_0_, bf16[32,16,128]{2,1,0:T(8,128)(2,1)S(1)} %collective-permute-done.5.refs_1_, ...), custom_call_target="tpu_custom_call" | custom-call | tf_op jit(solution)/shard_map/pallas_call | solution.py:75
  33.1 6.3 %collective-permute-start.7 = (bf16[32,2048]{1,0:T(8,128)(2,1)S(1)}, bf16[32,2048]{1,0:T(8,128)(2,1)S(1)}, u32[]{:S(2)}, u32[]{:S(2)}) collective-permute-start(bf16[32,2048]{1,0:T(8,128)(2,1)S(1)} %get-tuple-element.85), channel_id=1, source_target_pairs={{0,1},{1,0},{2,3},{3,2},{4,5},{5,4},{6,7},{7,6},{8,9},{9,8},{10,11... | collective-permute-start | bytes 393224 | tf_op jit(solution)/shard_map/ppermute | solution.py:100
  39.5 0.6 collective-permute-start.12
  40.1 3.1 %collective-permute-start.19 = (bf16[32,2048]{1,0:T(8,128)(2,1)S(1)}, bf16[32,2048]{1,0:T(8,128)(2,1)S(1)}, u32[]{:S(2)}, u32[]{:S(2)}) collective-permute-start(bf16[32,2048]{1,0:T(8,128)(2,1)S(1)} %get-tuple-element.108), channel_id=1, source_target_pairs={{0,2},{1,3},{2,0},{3,1},{4,6},{5,7},{6,4},{7,5},{8,10},{9,11},{10,... | collective-permute-start | bytes 393224 | tf_op jit(solution)/shard_map/ppermute | solution.py:100
  43.2 1.3 %collective-permute-start.20 = (bf16[32,2048]{1,0:T(8,128)(2,1)S(1)}, bf16[32,2048]{1,0:T(8,128)(2,1)S(1)}, u32[]{:S(2)}, u32[]{:S(2)}) collective-permute-start(bf16[32,2048]{1,0:T(8,128)(2,1)S(1)} %get-tuple-element.109), channel_id=1, source_target_pairs={{0,3},{1,2},{2,1},{3,0},{4,7},{5,6},{6,5},{7,4},{8,11},{9,10},{10,... | collective-permute-start | bytes 393224 | tf_op jit(solution)/shard_map/ppermute | solution.py:100
  44.6 0.1 collective-permute-start.9
  44.7 0.6 collective-permute-start.13
  45.3 0.8 convolution_convert_fusion.5
  46.2 0.2 collective-permute-done.12
  46.3 7.2 %collective-permute-done.13 = bf16[64,2048]{1,0:T(8,128)(2,1)S(1)} collective-permute-done((bf16[64,2048]{1,0:T(8,128)(2,1)S(1)}, bf16[64,2048]{1,0:T(8,128)(2,1)S(1)}, u32[]{:S(2)}, u32[]{:S(2)}) %collective-permute-start.13) | collective-permute-done | bytes 262176 | tf_op jit(solution)/shard_map/ppermute | solution.py:100
  53.6 0.1 collective-permute-start.14
  53.6 0.8 convolution_convert_fusion.4
  54.6 0.6 collective-permute-start.21
  55.1 0.8 convolution_convert_fusion.7
  56.0 0.8 convolution_convert_fusion.6
  56.8 0.1 broadcast_select_fusion.12
  56.9 0.1 broadcast_select_fusion.13
  57.0 2.7 %collective-permute-start.17 = (bf16[1,128,512]{2,1,0:T(8,128)(2,1)S(1)}, bf16[1,128,512]{2,1,0:T(8,128)(2,1)S(1)}, u32[]{:S(2)}, u32[]{:S(2)}) collective-permute-start(bf16[1,128,512]{2,1,0:T(8,128)(2,1)S(1)} %get-tuple-element.131), channel_id=1, source_target_pairs={{0,3},{1,2},{2,1},{3,0},{4,7},{5,6},{6,5},{7,4},{8,11},{9,10},{10,... | collective-permute-start | bytes 393224 | tf_op jit(solution)/shard_map/ppermute | solution.py:100
  59.7 0.6 collective-permute-start.16
  60.3 1.2 %collective-permute-start.15 = (bf16[1,128,512]{2,1,0:T(8,128)(2,1)S(1)}, bf16[1,128,512]{2,1,0:T(8,128)(2,1)S(1)}, u32[]{:S(2)}, u32[]{:S(2)}) collective-permute-start(bf16[1,128,512]{2,1,0:T(8,128)(2,1)S(1)} %get-tuple-element.102), channel_id=1, source_target_pairs={{0,1},{1,0},{2,3},{3,2},{4,5},{5,4},{6,7},{7,6},{8,9},{9,8},{10,11... | collective-permute-start | bytes 393224 | tf_op jit(solution)/shard_map/ppermute | solution.py:100
  61.5 0.1 collective-permute-start.18
  61.6 0.8 convolution_convert_fusion.2
  62.4 0.9 %collective-permute-done.21 = bf16[64,2048]{1,0:T(8,128)(2,1)S(1)} collective-permute-done((bf16[64,2048]{1,0:T(8,128)(2,1)S(1)}, bf16[64,2048]{1,0:T(8,128)(2,1)S(1)}, u32[]{:S(2)}, u32[]{:S(2)}) %collective-permute-start.21) | collective-permute-done | bytes 262176 | tf_op jit(solution)/shard_map/ppermute | solution.py:100
  63.4 0.1 collective-permute-start.22
  63.5 0.8 convolution_convert_fusion
  64.3 0.8 convolution_convert_fusion.3
  65.2 0.2 collective-permute-done.22
  65.4 0.8 convolution_convert_fusion.1
  66.2 0.1 broadcast_select_fusion.9
  66.3 2.7 %collective-permute-start.25 = (bf16[1,128,512]{2,1,0:T(8,128)(2,1)S(1)}, bf16[1,128,512]{2,1,0:T(8,128)(2,1)S(1)}, u32[]{:S(2)}, u32[]{:S(2)}) collective-permute-start(bf16[1,128,512]{2,1,0:T(8,128)(2,1)S(1)} %get-tuple-element.130), channel_id=1, source_target_pairs={{0,3},{1,2},{2,1},{3,0},{4,7},{5,6},{6,5},{7,4},{8,11},{9,10},{10,... | collective-permute-start | bytes 393224 | tf_op jit(solution)/shard_map/ppermute | solution.py:100
  69.0 0.5 collective-permute-start.24
  69.5 0.1 broadcast_select_fusion.11
  69.6 1.4 %collective-permute-start.23 = (bf16[1,128,512]{2,1,0:T(8,128)(2,1)S(1)}, bf16[1,128,512]{2,1,0:T(8,128)(2,1)S(1)}, u32[]{:S(2)}, u32[]{:S(2)}) collective-permute-start(bf16[1,128,512]{2,1,0:T(8,128)(2,1)S(1)} %get-tuple-element.115), channel_id=1, source_target_pairs={{0,1},{1,0},{2,3},{3,2},{4,5},{5,4},{6,7},{7,6},{8,9},{9,8},{10,11... | collective-permute-start | bytes 393224 | tf_op jit(solution)/shard_map/ppermute | solution.py:100
  71.0 7.5 %collective-permute-done.16 = bf16[1,128,512]{2,1,0:T(8,128)(2,1)S(1)} collective-permute-done((bf16[1,128,512]{2,1,0:T(8,128)(2,1)S(1)}, bf16[1,128,512]{2,1,0:T(8,128)(2,1)S(1)}, u32[]{:S(2)}, u32[]{:S(2)}) %collective-permute-start.16) | collective-permute-done | bytes 131104 | tf_op jit(solution)/shard_map/ppermute | solution.py:100
  78.6 0.1 broadcast_select_fusion.31
  78.6 5.1 %collective-permute-done.24 = bf16[1,128,512]{2,1,0:T(8,128)(2,1)S(1)} collective-permute-done((bf16[1,128,512]{2,1,0:T(8,128)(2,1)S(1)}, bf16[1,128,512]{2,1,0:T(8,128)(2,1)S(1)}, u32[]{:S(2)}, u32[]{:S(2)}) %collective-permute-start.24) | collective-permute-done | bytes 131104 | tf_op jit(solution)/shard_map/ppermute | solution.py:100
  83.8 0.1 broadcast_select_fusion.27
  83.9 0.1 broadcast_select_fusion.26
  84.0 0.8 maximum_bitcast_fusion
  (54 shorter events, 0.6 us)
Async XLA Ops:
  0.0 1.2 %copy-start = (bf16[256,16,128]{2,1,0:T(8,128)(2,1)S(1)}, bf16[256,16,128]{2,1,0:T(8,128)(2,1)}, u32[]{:S(2)}) copy-start(bf16[256,16,128]{2,1,0:T(8,128)(2,1)} %param.5) | copy-start | bytes 3145732
  1.3 10.7 %collective-permute-start = (bf16[32,16,128]{2,1,0:T(8,128)(2,1)S(1)}, bf16[32,16,128]{2,1,0:T(8,128)(2,1)S(1)}, u32[]{:S(2)}, u32[]{:S(2)}) collective-permute-start(bf16[32,16,128]{2,1,0:T(8,128)(2,1)S(1)} %constant_dynamic-slice_fusion.4), channel_id=1, source_target_pairs={{0,3},{1,2},{2,1},{3,0},{4,7},{5,6},{6,5},{7,4},{8,11},{9,10},{10,... | collective-permute-start | bytes 393224 | tf_op jit(solution)/shard_map/ppermute | solution.py:100
  6.4 12.6 %collective-permute-start.1 = (bf16[32,16,128]{2,1,0:T(8,128)(2,1)S(1)}, bf16[32,16,128]{2,1,0:T(8,128)(2,1)S(1)}, u32[]{:S(2)}, u32[]{:S(2)}) collective-permute-start(bf16[32,16,128]{2,1,0:T(8,128)(2,1)S(1)} %constant_dynamic-slice_fusion.5), channel_id=1, source_target_pairs={{0,2},{1,3},{2,0},{3,1},{4,6},{5,7},{6,4},{7,5},{8,10},{9,11},{10,... | collective-permute-start | bytes 393224 | tf_op jit(solution)/shard_map/ppermute | solution.py:100
  6.4 12.6 %collective-permute-start.2 = (bf16[32,16,128]{2,1,0:T(8,128)(2,1)S(1)}, bf16[32,16,128]{2,1,0:T(8,128)(2,1)S(1)}, u32[]{:S(2)}, u32[]{:S(2)}) collective-permute-start(bf16[32,16,128]{2,1,0:T(8,128)(2,1)S(1)} %constant_dynamic-slice_fusion.6), channel_id=1, source_target_pairs={{0,1},{1,0},{2,3},{3,2},{4,5},{5,4},{6,7},{7,6},{8,9},{9,8},{10,11... | collective-permute-start | bytes 393224 | tf_op jit(solution)/shard_map/ppermute | solution.py:100
  8.2 3.7 %copy-start.1 = (f32[128,128]{1,0:T(8,128)S(1)}, f32[128,128]{1,0:T(8,128)}, u32[]{:S(2)}) copy-start(f32[128,128]{1,0:T(8,128)} %refs_6_.3) | copy-start | bytes 196612
  8.2 10.8 %copy-start.2 = (f32[64,128]{1,0:T(8,128)S(1)}, f32[64,128]{1,0:T(8,128)}, u32[]{:S(2)}) copy-start(f32[64,128]{1,0:T(8,128)} %refs_8_.3) | copy-start | bytes 98308
  12.1 13.9 %collective-permute-start.4 = (bf16[32,16,128]{2,1,0:T(8,128)(2,1)S(1)}, bf16[32,16,128]{2,1,0:T(8,128)(2,1)S(1)}, u32[]{:S(2)}, u32[]{:S(2)}) collective-permute-start(bf16[32,16,128]{2,1,0:T(8,128)(2,1)S(1)} %constant_dynamic-slice_fusion.1), channel_id=1, source_target_pairs={{0,1},{1,0},{2,3},{3,2},{4,5},{5,4},{6,7},{7,6},{8,9},{9,8},{10,11... | collective-permute-start | bytes 393224 | tf_op jit(solution)/shard_map/ppermute | solution.py:100
  16.4 11.6 %collective-permute-start.5 = (bf16[32,16,128]{2,1,0:T(8,128)(2,1)S(1)}, bf16[32,16,128]{2,1,0:T(8,128)(2,1)S(1)}, u32[]{:S(2)}, u32[]{:S(2)}) collective-permute-start(bf16[32,16,128]{2,1,0:T(8,128)(2,1)S(1)} %constant_dynamic-slice_fusion.2), channel_id=1, source_target_pairs={{0,2},{1,3},{2,0},{3,1},{4,6},{5,7},{6,4},{7,5},{8,10},{9,11},{10,... | collective-permute-start | bytes 393224 | tf_op jit(solution)/shard_map/ppermute | solution.py:100
  17.6 10.3 %collective-permute-start.6 = (bf16[32,16,128]{2,1,0:T(8,128)(2,1)S(1)}, bf16[32,16,128]{2,1,0:T(8,128)(2,1)S(1)}, u32[]{:S(2)}, u32[]{:S(2)}) collective-permute-start(bf16[32,16,128]{2,1,0:T(8,128)(2,1)S(1)} %constant_dynamic-slice_fusion.3), channel_id=1, source_target_pairs={{0,3},{1,2},{2,1},{3,0},{4,7},{5,6},{6,5},{7,4},{8,11},{9,10},{10,... | collective-permute-start | bytes 393224 | tf_op jit(solution)/shard_map/ppermute | solution.py:100
  21.3 8.0 %collective-permute-start.3 = (bf16[32,2048]{1,0:T(8,128)(2,1)S(1)}, bf16[32,2048]{1,0:T(8,128)(2,1)S(1)}, u32[]{:S(2)}, u32[]{:S(2)}) collective-permute-start(bf16[32,2048]{1,0:T(8,128)(2,1)S(1)} %get-tuple-element.71), channel_id=1, source_target_pairs={{0,1},{1,0},{2,3},{3,2},{4,5},{5,4},{6,7},{7,6},{8,9},{9,8},{10,11... | collective-permute-start | bytes 393224 | tf_op jit(solution)/shard_map/ppermute | solution.py:100
  22.2 23.1 %copy-start.3 = (bf16[64,8,16,128]{3,1,2,0:T(8,128)(2,1)S(1)}, bf16[64,8,16,128]{3,1,2,0:T(8,128)(2,1)}, u32[]{:S(2)}) copy-start(bf16[64,8,16,128]{3,1,2,0:T(8,128)(2,1)} %copy.19) | copy-start | bytes 6291460
  22.2 17.2 %collective-permute-start.10 = (bf16[32,2048]{1,0:T(8,128)(2,1)S(1)}, bf16[32,2048]{1,0:T(8,128)(2,1)S(1)}, u32[]{:S(2)}, u32[]{:S(2)}) collective-permute-start(bf16[32,2048]{1,0:T(8,128)(2,1)S(1)} %get-tuple-element.93), channel_id=1, source_target_pairs={{0,2},{1,3},{2,0},{3,1},{4,6},{5,7},{6,4},{7,5},{8,10},{9,11},{10,... | collective-permute-start | bytes 393224 | tf_op jit(solution)/shard_map/ppermute | solution.py:100
  26.0 13.4 %collective-permute-start.11 = (bf16[32,2048]{1,0:T(8,128)(2,1)S(1)}, bf16[32,2048]{1,0:T(8,128)(2,1)S(1)}, u32[]{:S(2)}, u32[]{:S(2)}) collective-permute-start(bf16[32,2048]{1,0:T(8,128)(2,1)S(1)} %get-tuple-element.94), channel_id=1, source_target_pairs={{0,3},{1,2},{2,1},{3,0},{4,7},{5,6},{6,5},{7,4},{8,11},{9,10},{10,... | collective-permute-start | bytes 393224 | tf_op jit(solution)/shard_map/ppermute | solution.py:100
  29.4 15.2 %collective-permute-start.8 = (bf16[64,2048]{1,0:T(8,128)(2,1)S(1)}, bf16[64,2048]{1,0:T(8,128)(2,1)S(1)}, u32[]{:S(2)}, u32[]{:S(2)}) collective-permute-start(bf16[64,2048]{1,0:T(8,128)(2,1)S(1)} %constant_dynamic-update-slice_fusion), channel_id=1, source_target_pairs={{0,8},{4,12},{8,0},{12,4},{1,9},{5,13},{9,1},{13,5},{2,10},{6,14},... | collective-permute-start | bytes 786440 | tf_op jit(solution)/shard_map/ppermute | solution.py:100
  33.1 11.4 %collective-permute-start.7 = (bf16[32,2048]{1,0:T(8,128)(2,1)S(1)}, bf16[32,2048]{1,0:T(8,128)(2,1)S(1)}, u32[]{:S(2)}, u32[]{:S(2)}) collective-permute-start(bf16[32,2048]{1,0:T(8,128)(2,1)S(1)} %get-tuple-element.85), channel_id=1, source_target_pairs={{0,1},{1,0},{2,3},{3,2},{4,5},{5,4},{6,7},{7,6},{8,9},{9,8},{10,11... | collective-permute-start | bytes 393224 | tf_op jit(solution)/shard_map/ppermute | solution.py:100
  39.5 6.8 %collective-permute-start.12 = (bf16[64,2048]{1,0:T(8,128)(2,1)S(1)}, bf16[64,2048]{1,0:T(8,128)(2,1)S(1)}, u32[]{:S(2)}, u32[]{:S(2)}) collective-permute-start(bf16[64,2048]{1,0:T(8,128)(2,1)S(1)} %constant_dynamic-update-slice_fusion.2), channel_id=1, source_target_pairs={{0,8},{4,12},{8,0},{12,4},{1,9},{5,13},{9,1},{13,5},{2,10},{6,14},... | collective-permute-start | bytes 786440 | tf_op jit(solution)/shard_map/ppermute | solution.py:100
  40.1 14.4 %collective-permute-start.19 = (bf16[32,2048]{1,0:T(8,128)(2,1)S(1)}, bf16[32,2048]{1,0:T(8,128)(2,1)S(1)}, u32[]{:S(2)}, u32[]{:S(2)}) collective-permute-start(bf16[32,2048]{1,0:T(8,128)(2,1)S(1)} %get-tuple-element.108), channel_id=1, source_target_pairs={{0,2},{1,3},{2,0},{3,1},{4,6},{5,7},{6,4},{7,5},{8,10},{9,11},{10,... | collective-permute-start | bytes 393224 | tf_op jit(solution)/shard_map/ppermute | solution.py:100
  43.2 11.3 %collective-permute-start.20 = (bf16[32,2048]{1,0:T(8,128)(2,1)S(1)}, bf16[32,2048]{1,0:T(8,128)(2,1)S(1)}, u32[]{:S(2)}, u32[]{:S(2)}) collective-permute-start(bf16[32,2048]{1,0:T(8,128)(2,1)S(1)} %get-tuple-element.109), channel_id=1, source_target_pairs={{0,3},{1,2},{2,1},{3,0},{4,7},{5,6},{6,5},{7,4},{8,11},{9,10},{10,... | collective-permute-start | bytes 393224 | tf_op jit(solution)/shard_map/ppermute | solution.py:100
  44.6 10.5 %collective-permute-start.9 = (bf16[128,2048]{1,0:T(8,128)(2,1)S(1)}, bf16[128,2048]{1,0:T(8,128)(2,1)S(1)}, u32[]{:S(2)}, u32[]{:S(2)}) collective-permute-start(bf16[128,2048]{1,0:T(8,128)(2,1)S(1)} %pad_maximum_fusion), channel_id=1, source_target_pairs={{0,4},{4,0},{8,12},{12,8},{1,5},{5,1},{9,13},{13,9},{2,6},{6,2},{1... | collective-permute-start | bytes 1572872 | tf_op jit(solution)/shard_map/ppermute | solution.py:100
  44.7 8.8 %collective-permute-start.13 = (bf16[64,2048]{1,0:T(8,128)(2,1)S(1)}, bf16[64,2048]{1,0:T(8,128)(2,1)S(1)}, u32[]{:S(2)}, u32[]{:S(2)}) collective-permute-start(bf16[64,2048]{1,0:T(8,128)(2,1)S(1)} %constant_dynamic-update-slice_fusion.4), channel_id=1, source_target_pairs={{0,8},{4,12},{8,0},{12,4},{1,9},{5,13},{9,1},{13,5},{2,10},{6,14},... | collective-permute-start | bytes 786440 | tf_op jit(solution)/shard_map/ppermute | solution.py:100
  53.6 2.4 %collective-permute-start.14 = (bf16[128,2048]{1,0:T(8,128)(2,1)S(1)}, bf16[128,2048]{1,0:T(8,128)(2,1)S(1)}, u32[]{:S(2)}, u32[]{:S(2)}) collective-permute-start(bf16[128,2048]{1,0:T(8,128)(2,1)S(1)} %pad_maximum_fusion.1), channel_id=1, source_target_pairs={{0,4},{4,0},{8,12},{12,8},{1,5},{5,1},{9,13},{13,9},{2,6},{6,2},{1... | collective-permute-start | bytes 1572872 | tf_op jit(solution)/shard_map/ppermute | solution.py:100
  54.6 8.8 %collective-permute-start.21 = (bf16[64,2048]{1,0:T(8,128)(2,1)S(1)}, bf16[64,2048]{1,0:T(8,128)(2,1)S(1)}, u32[]{:S(2)}, u32[]{:S(2)}) collective-permute-start(bf16[64,2048]{1,0:T(8,128)(2,1)S(1)} %constant_dynamic-update-slice_fusion.6), channel_id=1, source_target_pairs={{0,8},{4,12},{8,0},{12,4},{1,9},{5,13},{9,1},{13,5},{2,10},{6,14},... | collective-permute-start | bytes 786440 | tf_op jit(solution)/shard_map/ppermute | solution.py:100
  57.0 21.5 %collective-permute-start.17 = (bf16[1,128,512]{2,1,0:T(8,128)(2,1)S(1)}, bf16[1,128,512]{2,1,0:T(8,128)(2,1)S(1)}, u32[]{:S(2)}, u32[]{:S(2)}) collective-permute-start(bf16[1,128,512]{2,1,0:T(8,128)(2,1)S(1)} %get-tuple-element.131), channel_id=1, source_target_pairs={{0,3},{1,2},{2,1},{3,0},{4,7},{5,6},{6,5},{7,4},{8,11},{9,10},{10,... | collective-permute-start | bytes 393224 | tf_op jit(solution)/shard_map/ppermute | solution.py:100
  59.7 18.8 %collective-permute-start.16 = (bf16[1,128,512]{2,1,0:T(8,128)(2,1)S(1)}, bf16[1,128,512]{2,1,0:T(8,128)(2,1)S(1)}, u32[]{:S(2)}, u32[]{:S(2)}) collective-permute-start(bf16[1,128,512]{2,1,0:T(8,128)(2,1)S(1)} %get-tuple-element.101), channel_id=1, source_target_pairs={{0,2},{1,3},{2,0},{3,1},{4,6},{5,7},{6,4},{7,5},{8,10},{9,11},{10,... | collective-permute-start | bytes 393224 | tf_op jit(solution)/shard_map/ppermute | solution.py:100
  60.3 9.3 %collective-permute-start.15 = (bf16[1,128,512]{2,1,0:T(8,128)(2,1)S(1)}, bf16[1,128,512]{2,1,0:T(8,128)(2,1)S(1)}, u32[]{:S(2)}, u32[]{:S(2)}) collective-permute-start(bf16[1,128,512]{2,1,0:T(8,128)(2,1)S(1)} %get-tuple-element.102), channel_id=1, source_target_pairs={{0,1},{1,0},{2,3},{3,2},{4,5},{5,4},{6,7},{7,6},{8,9},{9,8},{10,11... | collective-permute-start | bytes 393224 | tf_op jit(solution)/shard_map/ppermute | solution.py:100
  61.5 2.8 %collective-permute-start.18 = (bf16[128,2048]{1,0:T(8,128)(2,1)S(1)}, bf16[128,2048]{1,0:T(8,128)(2,1)S(1)}, u32[]{:S(2)}, u32[]{:S(2)}) collective-permute-start(bf16[128,2048]{1,0:T(8,128)(2,1)S(1)} %pad_maximum_fusion.2), channel_id=1, source_target_pairs={{0,4},{4,0},{8,12},{12,8},{1,5},{5,1},{9,13},{13,9},{2,6},{6,2},{1... | collective-permute-start | bytes 1572872 | tf_op jit(solution)/shard_map/ppermute | solution.py:100
  63.4 2.0 %collective-permute-start.22 = (bf16[128,2048]{1,0:T(8,128)(2,1)S(1)}, bf16[128,2048]{1,0:T(8,128)(2,1)S(1)}, u32[]{:S(2)}, u32[]{:S(2)}) collective-permute-start(bf16[128,2048]{1,0:T(8,128)(2,1)S(1)} %pad_maximum_fusion.3), channel_id=1, source_target_pairs={{0,4},{4,0},{8,12},{12,8},{1,5},{5,1},{9,13},{13,9},{2,6},{6,2},{1... | collective-permute-start | bytes 1572872 | tf_op jit(solution)/shard_map/ppermute | solution.py:100
  66.3 17.4 %collective-permute-start.25 = (bf16[1,128,512]{2,1,0:T(8,128)(2,1)S(1)}, bf16[1,128,512]{2,1,0:T(8,128)(2,1)S(1)}, u32[]{:S(2)}, u32[]{:S(2)}) collective-permute-start(bf16[1,128,512]{2,1,0:T(8,128)(2,1)S(1)} %get-tuple-element.130), channel_id=1, source_target_pairs={{0,3},{1,2},{2,1},{3,0},{4,7},{5,6},{6,5},{7,4},{8,11},{9,10},{10,... | collective-permute-start | bytes 393224 | tf_op jit(solution)/shard_map/ppermute | solution.py:100
  69.0 14.8 %collective-permute-start.24 = (bf16[1,128,512]{2,1,0:T(8,128)(2,1)S(1)}, bf16[1,128,512]{2,1,0:T(8,128)(2,1)S(1)}, u32[]{:S(2)}, u32[]{:S(2)}) collective-permute-start(bf16[1,128,512]{2,1,0:T(8,128)(2,1)S(1)} %get-tuple-element.114), channel_id=1, source_target_pairs={{0,2},{1,3},{2,0},{3,1},{4,6},{5,7},{6,4},{7,5},{8,10},{9,11},{10,... | collective-permute-start | bytes 393224 | tf_op jit(solution)/shard_map/ppermute | solution.py:100
  69.6 9.0 %collective-permute-start.23 = (bf16[1,128,512]{2,1,0:T(8,128)(2,1)S(1)}, bf16[1,128,512]{2,1,0:T(8,128)(2,1)S(1)}, u32[]{:S(2)}, u32[]{:S(2)}) collective-permute-start(bf16[1,128,512]{2,1,0:T(8,128)(2,1)S(1)} %get-tuple-element.115), channel_id=1, source_target_pairs={{0,1},{1,0},{2,3},{3,2},{4,5},{5,4},{6,7},{7,6},{8,9},{9,8},{10,11... | collective-permute-start | bytes 393224 | tf_op jit(solution)/shard_map/ppermute | solution.py:100

commit v16 on v14

--- a/solution.py
+++ b/solution.py
@@ -158,13 +158,14 @@
     source = queries
     for chunk, part in enumerate(parts):
         first, each = sum(parts[:chunk]), part // slices
-        if chunk:
-            source, pieces[0][-1], train_flat = lax.optimization_barrier((source, pieces[0][-1], train_flat))
         raw = {}
         for mask in (reversed(range(slices)) if chunk else range(slices)):
             block = lax.dynamic_slice_in_dim(source, first + (here ^ mask) * each, each, 0)
             raw[mask], source = lax.optimization_barrier((block, source))
+        if chunk:
+            raw[1], pieces[0][-1] = lax.optimization_barrier((raw[1], pieces[0][-1]))
         pieces.append(exchanged(raw, slices))
+    pieces[0], train_flat = lax.optimization_barrier((pieces[0], train_flat))
     made = condition(pieces[0], basis, in_basis, corrections)
     rows.append(exchanged(made, slices))
     rows[0][:half], pieces[1] = lax.optimization_barrier((rows[0][:half], pieces[1]))

time: 82.7 us -> 86.2 us (1.042)
  waiting for transfers between devices: 21.2 us -> 30.5 us
  starting transfers between devices: 41.6 us -> 35.8 us
    ppermute x26, waiting for transfers between devices: 21.2 us -> 30.5 us  [crossed(): return lax.ppermute(value, axis, [(at, at ^ mask) for at in range(size)])]
    ppermute x26, starting transfers between devices: 41.6 us -> 35.8 us  [crossed(): return lax.ppermute(value, axis, [(at, at ^ mask) for at in range(size)])]
  transfers between devices with their start and end apart: 26 -> 26, of which waited for: 8 -> 9; matrix products, arithmetic and copies ran while one was open for 15% -> 14% of each run, Pallas kernels for 5% -> 5%
where the time goes in v16:
time: 86.2 us; the launch traced here: 86 us
  starting transfers between devices  35.8 us (42%)
  waiting for transfers between devices  30.5 us (35%)
  matrix products  6.66 us (8%)
  local copies, waits for them, and re-layouts  6.27 us (7%)
  Pallas kernels  4.47 us (5%)
  other arithmetic  1.69 us (2%)
    ppermute x26, starting transfers between devices, crossed(): return lax.ppermute(value, axis, [(at, at ^ mask) for at in range(size)])  35.8 us
    ppermute x26, waiting for transfers between devices, crossed(): return lax.ppermute(value, axis, [(at, at ^ mask) for at in range(size)])  30.5 us
    dot_general x8, matrix products, products(): lax.dot_general(block, train_flat, contract, preferred_element_type=jnp.f...  6.66 us
    unnamed x18, local copies, waits for them, and re-layouts  5.21 us
    pallas_call x2, Pallas kernels, condition_fast(): pl.pallas_call(functools.partial(condition_kernel, slices, rows_here), gr...  4.47 us
  transfers between devices with their start and end apart: 26, of which 9 were waited for; matrix products, arithmetic and copies ran while one was open for 14% of the time, Pallas kernels for 5%

profile of v16, /device:TPU:0, one launch (start us, length us, event | category | flops | bytes accessed | tf_op | source)
XLA Modules:
  0.0 86.0 jit_solution(9958265699442519923)
XLA Ops:
  0.0 1.2 %copy-done = bf16[256,16,128]{2,1,0:T(8,128)(2,1)S(1)} copy-done((bf16[256,16,128]{2,1,0:T(8,128)(2,1)S(1)}, bf16[256,16,128]{2,1,0:T(8,128)(2,1)}, u32[]{:S(2)}) %copy-start) | copy-done | bytes 1048600
  1.3 5.1 %collective-permute-start.2 = (bf16[32,16,128]{2,1,0:T(8,128)(2,1)S(1)}, bf16[32,16,128]{2,1,0:T(8,128)(2,1)S(1)}, u32[]{:S(2)}, u32[]{:S(2)}) collective-permute-start(bf16[32,16,128]{2,1,0:T(8,128)(2,1)S(1)} %constant_dynamic-slice_fusion.4), channel_id=1, source_target_pairs={{0,3},{1,2},{2,1},{3,0},{4,7},{5,6},{6,5},{7,4},{8,11},{9,10},{10,... | collective-permute-start | bytes 393224 | tf_op jit(solution)/shard_map/ppermute | solution.py:100
  6.4 0.6 collective-permute-start
  7.1 2.4 %collective-permute-start.5 = (bf16[32,16,128]{2,1,0:T(8,128)(2,1)S(1)}, bf16[32,16,128]{2,1,0:T(8,128)(2,1)S(1)}, u32[]{:S(2)}, u32[]{:S(2)}) collective-permute-start(bf16[32,16,128]{2,1,0:T(8,128)(2,1)S(1)} %constant_dynamic-slice_fusion.2), channel_id=1, source_target_pairs={{0,2},{1,3},{2,0},{3,1},{4,6},{5,7},{6,4},{7,5},{8,10},{9,11},{10,... | collective-permute-start | bytes 393224 | tf_op jit(solution)/shard_map/ppermute | solution.py:100
  9.5 1.5 %collective-permute-start.6 = (bf16[32,16,128]{2,1,0:T(8,128)(2,1)S(1)}, bf16[32,16,128]{2,1,0:T(8,128)(2,1)S(1)}, u32[]{:S(2)}, u32[]{:S(2)}) collective-permute-start(bf16[32,16,128]{2,1,0:T(8,128)(2,1)S(1)} %constant_dynamic-slice_fusion.3), channel_id=1, source_target_pairs={{0,3},{1,2},{2,1},{3,0},{4,7},{5,6},{6,5},{7,4},{8,11},{9,10},{10,... | collective-permute-start | bytes 393224 | tf_op jit(solution)/shard_map/ppermute | solution.py:100
  11.0 0.7 fusion
  11.8 0.1 copy.13
  11.9 0.1 copy.14
  11.9 0.1 copy.15
  12.0 0.1 copy.16
  12.1 0.0 copy-start.1
  12.2 3.5 %copy.19 = bf16[64,8,16,128]{3,1,2,0:T(8,128)(2,1)} copy(bf16[64,8,16,128]{3,2,1,0:T(8,128)(2,1)} %bitcast.78) | data formatting | bytes 4194304
  15.7 0.1 pad_maximum_fusion.14
  15.8 0.1 copy.11.refs_4_
  15.8 0.0 copy-done.1
  15.9 0.1 copy.10
  16.0 8.1 %collective-permute-done.1.refs_1_ = bf16[32,16,128]{2,1,0:T(8,128)(2,1)S(1)} collective-permute-done((bf16[32,16,128]{2,1,0:T(8,128)(2,1)S(1)}, bf16[32,16,128]{2,1,0:T(8,128)(2,1)S(1)}, u32[]{:S(2)}, u32[]{:S(2)}) %collective-permute-start.1) | collective-permute-done | bytes 131104 | tf_op jit(solution)/shard_map/ppermute | solution.py:100
  24.1 2.2 %shard_map.55 = (bf16[32,2048]{1,0:T(8,128)(2,1)S(1)}, bf16[32,2048]{1,0:T(8,128)(2,1)S(1)}, bf16[32,2048]{1,0:T(8,128)(2,1)S(1)}, bf16[32,2048]{1,0:T(8,128)(2,1)S(1)}) custom-call(bf16[32,16,128]{2,1,0:T(8,128)(2,1)S(1)} %collective-permute-done.2.refs_0_, bf16[32,16,128]{2,1,0:T(8,128)(2,1)S(1)} %collective-permute-done.1.refs_1_, ...), custom_call_target="tpu_custom_call" | custom-call | tf_op jit(solution)/shard_map/pallas_call | solution.py:75
  26.3 0.1 collective-permute-start.3
  26.4 2.0 %collective-permute-start.4 = (bf16[32,16,128]{2,1,0:T(8,128)(2,1)S(1)}, bf16[32,16,128]{2,1,0:T(8,128)(2,1)S(1)}, u32[]{:S(2)}, u32[]{:S(2)}) collective-permute-start(bf16[32,16,128]{2,1,0:T(8,128)(2,1)S(1)} %constant_dynamic-slice_fusion.1), channel_id=1, source_target_pairs={{0,1},{1,0},{2,3},{3,2},{4,5},{5,4},{6,7},{7,6},{8,9},{9,8},{10,11... | collective-permute-start | bytes 393224 | tf_op jit(solution)/shard_map/ppermute | solution.py:100
  28.5 1.4 %collective-permute-start.10 = (bf16[32,2048]{1,0:T(8,128)(2,1)S(1)}, bf16[32,2048]{1,0:T(8,128)(2,1)S(1)}, u32[]{:S(2)}, u32[]{:S(2)}) collective-permute-start(bf16[32,2048]{1,0:T(8,128)(2,1)S(1)} %get-tuple-element.97), channel_id=1, source_target_pairs={{0,2},{1,3},{2,0},{3,1},{4,6},{5,7},{6,4},{7,5},{8,10},{9,11},{10,... | collective-permute-start | bytes 393224 | tf_op jit(solution)/shard_map/ppermute | solution.py:100
  29.8 1.5 %collective-permute-start.11 = (bf16[32,2048]{1,0:T(8,128)(2,1)S(1)}, bf16[32,2048]{1,0:T(8,128)(2,1)S(1)}, u32[]{:S(2)}, u32[]{:S(2)}) collective-permute-start(bf16[32,2048]{1,0:T(8,128)(2,1)S(1)} %get-tuple-element.98), channel_id=1, source_target_pairs={{0,3},{1,2},{2,1},{3,0},{4,7},{5,6},{6,5},{7,4},{8,11},{9,10},{10,... | collective-permute-start | bytes 393224 | tf_op jit(solution)/shard_map/ppermute | solution.py:100
  31.3 3.7 %collective-permute-done.3 = bf16[32,2048]{1,0:T(8,128)(2,1)S(1)} collective-permute-done((bf16[32,2048]{1,0:T(8,128)(2,1)S(1)}, bf16[32,2048]{1,0:T(8,128)(2,1)S(1)}, u32[]{:S(2)}, u32[]{:S(2)}) %collective-permute-start.3) | collective-permute-done | bytes 131104 | tf_op jit(solution)/shard_map/ppermute | solution.py:100
  35.0 1.5 %collective-permute-done.4.refs_2_ = bf16[32,16,128]{2,1,0:T(8,128)(2,1)S(1)} collective-permute-done((bf16[32,16,128]{2,1,0:T(8,128)(2,1)S(1)}, bf16[32,16,128]{2,1,0:T(8,128)(2,1)S(1)}, u32[]{:S(2)}, u32[]{:S(2)}) %collective-permute-start.4) | collective-permute-done | bytes 131104 | tf_op jit(solution)/shard_map/ppermute | solution.py:100
  36.5 4.7 %collective-permute-start.8 = (bf16[64,2048]{1,0:T(8,128)(2,1)S(1)}, bf16[64,2048]{1,0:T(8,128)(2,1)S(1)}, u32[]{:S(2)}, u32[]{:S(2)}) collective-permute-start(bf16[64,2048]{1,0:T(8,128)(2,1)S(1)} %constant_dynamic-update-slice_fusion), channel_id=1, source_target_pairs={{0,8},{4,12},{8,0},{12,4},{1,9},{5,13},{9,1},{13,5},{2,10},{6,14},... | collective-permute-start | bytes 786440 | tf_op jit(solution)/shard_map/ppermute | solution.py:100
  41.2 2.2 %shard_map.56 = (bf16[32,2048]{1,0:T(8,128)(2,1)S(1)}, bf16[32,2048]{1,0:T(8,128)(2,1)S(1)}, bf16[32,2048]{1,0:T(8,128)(2,1)S(1)}, bf16[32,2048]{1,0:T(8,128)(2,1)S(1)}) custom-call(bf16[32,16,128]{2,1,0:T(8,128)(2,1)S(1)} %collective-permute-done.6.refs_0_, bf16[32,16,128]{2,1,0:T(8,128)(2,1)S(1)} %collective-permute-done.5.refs_1_, ...), custom_call_target="tpu_custom_call" | custom-call | tf_op jit(solution)/shard_map/pallas_call | solution.py:75
  43.5 0.1 collective-permute-start.7
  43.6 0.1 collective-permute-start.12
  43.8 0.1 collective-permute-start.19
  43.8 4.3 %collective-permute-start.20 = (bf16[32,2048]{1,0:T(8,128)(2,1)S(1)}, bf16[32,2048]{1,0:T(8,128)(2,1)S(1)}, u32[]{:S(2)}, u32[]{:S(2)}) collective-permute-start(bf16[32,2048]{1,0:T(8,128)(2,1)S(1)} %get-tuple-element.109), channel_id=1, source_target_pairs={{0,3},{1,2},{2,1},{3,0},{4,7},{5,6},{6,5},{7,4},{8,11},{9,10},{10,... | collective-permute-start | bytes 393224 | tf_op jit(solution)/shard_map/ppermute | solution.py:100
  48.2 2.0 %collective-permute-done.7 = bf16[32,2048]{1,0:T(8,128)(2,1)S(1)} collective-permute-done((bf16[32,2048]{1,0:T(8,128)(2,1)S(1)}, bf16[32,2048]{1,0:T(8,128)(2,1)S(1)}, u32[]{:S(2)}, u32[]{:S(2)}) %collective-permute-start.7) | collective-permute-done | bytes 131104 | tf_op jit(solution)/shard_map/ppermute | solution.py:100
  50.2 0.1 collective-permute-start.9
  50.4 0.6 collective-permute-start.13
  50.9 0.8 convolution_convert_fusion.5
  51.8 0.8 convolution_convert_fusion.4
  52.6 0.1 collective-permute-start.17
  52.8 2.1 %collective-permute-start.21 = (bf16[64,2048]{1,0:T(8,128)(2,1)S(1)}, bf16[64,2048]{1,0:T(8,128)(2,1)S(1)}, u32[]{:S(2)}, u32[]{:S(2)}) collective-permute-start(bf16[64,2048]{1,0:T(8,128)(2,1)S(1)} %constant_dynamic-update-slice_fusion.6), channel_id=1, source_target_pairs={{0,8},{4,12},{8,0},{12,4},{1,9},{5,13},{9,1},{13,5},{2,10},{6,14},... | collective-permute-start | bytes 786440 | tf_op jit(solution)/shard_map/ppermute | solution.py:100
  54.9 0.8 convolution_convert_fusion.7
  55.7 0.8 convolution_convert_fusion.6
  56.6 0.1 broadcast_select_fusion.12
  56.7 2.2 %collective-permute-start.16 = (bf16[1,128,512]{2,1,0:T(8,128)(2,1)S(1)}, bf16[1,128,512]{2,1,0:T(8,128)(2,1)S(1)}, u32[]{:S(2)}, u32[]{:S(2)}) collective-permute-start(bf16[1,128,512]{2,1,0:T(8,128)(2,1)S(1)} %get-tuple-element.131), channel_id=1, source_target_pairs={{0,3},{1,2},{2,1},{3,0},{4,7},{5,6},{6,5},{7,4},{8,11},{9,10},{10,... | collective-permute-start | bytes 393224 | tf_op jit(solution)/shard_map/ppermute | solution.py:100
  58.9 0.1 broadcast_select_fusion.13
  59.0 0.9 %collective-permute-start.15 = (bf16[1,128,512]{2,1,0:T(8,128)(2,1)S(1)}, bf16[1,128,512]{2,1,0:T(8,128)(2,1)S(1)}, u32[]{:S(2)}, u32[]{:S(2)}) collective-permute-start(bf16[1,128,512]{2,1,0:T(8,128)(2,1)S(1)} %get-tuple-element.101), channel_id=1, source_target_pairs={{0,2},{1,3},{2,0},{3,1},{4,6},{5,7},{6,4},{7,5},{8,10},{9,11},{10,... | collective-permute-start | bytes 393224 | tf_op jit(solution)/shard_map/ppermute | solution.py:100
  60.0 1.3 %collective-permute-start.14 = (bf16[1,128,512]{2,1,0:T(8,128)(2,1)S(1)}, bf16[1,128,512]{2,1,0:T(8,128)(2,1)S(1)}, u32[]{:S(2)}, u32[]{:S(2)}) collective-permute-start(bf16[1,128,512]{2,1,0:T(8,128)(2,1)S(1)} %get-tuple-element.102), channel_id=1, source_target_pairs={{0,1},{1,0},{2,3},{3,2},{4,5},{5,4},{6,7},{7,6},{8,9},{9,8},{10,11... | collective-permute-start | bytes 393224 | tf_op jit(solution)/shard_map/ppermute | solution.py:100
  61.3 0.6 collective-permute-done.17
  61.9 0.1 collective-permute-start.18
  62.0 0.8 convolution_convert_fusion.1
  62.8 3.7 %collective-permute-done.21 = bf16[64,2048]{1,0:T(8,128)(2,1)S(1)} collective-permute-done((bf16[64,2048]{1,0:T(8,128)(2,1)S(1)}, bf16[64,2048]{1,0:T(8,128)(2,1)S(1)}, u32[]{:S(2)}, u32[]{:S(2)}) %collective-permute-start.21) | collective-permute-done | bytes 262176 | tf_op jit(solution)/shard_map/ppermute | solution.py:100
  66.6 0.1 collective-permute-start.22
  66.7 0.8 convolution_convert_fusion
  67.6 0.8 convolution_convert_fusion.3
  68.4 0.2 collective-permute-done.22
  68.6 0.8 convolution_convert_fusion.2
  69.4 0.1 broadcast_select_fusion.9
  69.5 0.1 collective-permute-start.25
  69.6 3.2 %collective-permute-start.24 = (bf16[1,128,512]{2,1,0:T(8,128)(2,1)S(1)}, bf16[1,128,512]{2,1,0:T(8,128)(2,1)S(1)}, u32[]{:S(2)}, u32[]{:S(2)}) collective-permute-start(bf16[1,128,512]{2,1,0:T(8,128)(2,1)S(1)} %get-tuple-element.114), channel_id=1, source_target_pairs={{0,2},{1,3},{2,0},{3,1},{4,6},{5,7},{6,4},{7,5},{8,10},{9,11},{10,... | collective-permute-start | bytes 393224 | tf_op jit(solution)/shard_map/ppermute | solution.py:100
  72.8 0.1 broadcast_select_fusion.11
  72.9 1.3 %collective-permute-start.23 = (bf16[1,128,512]{2,1,0:T(8,128)(2,1)S(1)}, bf16[1,128,512]{2,1,0:T(8,128)(2,1)S(1)}, u32[]{:S(2)}, u32[]{:S(2)}) collective-permute-start(bf16[1,128,512]{2,1,0:T(8,128)(2,1)S(1)} %get-tuple-element.115), channel_id=1, source_target_pairs={{0,1},{1,0},{2,3},{3,2},{4,5},{5,4},{6,7},{7,6},{8,9},{9,8},{10,11... | collective-permute-start | bytes 393224 | tf_op jit(solution)/shard_map/ppermute | solution.py:100
  74.2 0.1 broadcast_select_fusion.31
  74.3 5.8 %collective-permute-done.23 = bf16[1,128,512]{2,1,0:T(8,128)(2,1)S(1)} collective-permute-done((bf16[1,128,512]{2,1,0:T(8,128)(2,1)S(1)}, bf16[1,128,512]{2,1,0:T(8,128)(2,1)S(1)}, u32[]{:S(2)}, u32[]{:S(2)}) %collective-permute-start.23) | collective-permute-done | bytes 131104 | tf_op jit(solution)/shard_map/ppermute | solution.py:100
  80.1 4.9 %collective-permute-done.24 = bf16[1,128,512]{2,1,0:T(8,128)(2,1)S(1)} collective-permute-done((bf16[1,128,512]{2,1,0:T(8,128)(2,1)S(1)}, bf16[1,128,512]{2,1,0:T(8,128)(2,1)S(1)}, u32[]{:S(2)}, u32[]{:S(2)}) %collective-permute-start.24) | collective-permute-done | bytes 131104 | tf_op jit(solution)/shard_map/ppermute | solution.py:100
  85.0 0.1 broadcast_select_fusion.27
  85.0 0.1 broadcast_select_fusion.26
  85.2 0.8 maximum_bitcast_fusion
  (54 shorter events, 0.6 us)
Async XLA Ops:
  0.0 1.2 %copy-start = (bf16[256,16,128]{2,1,0:T(8,128)(2,1)S(1)}, bf16[256,16,128]{2,1,0:T(8,128)(2,1)}, u32[]{:S(2)}) copy-start(bf16[256,16,128]{2,1,0:T(8,128)(2,1)} %param.5) | copy-start | bytes 3145732
  1.3 14.6 %collective-permute-start.2 = (bf16[32,16,128]{2,1,0:T(8,128)(2,1)S(1)}, bf16[32,16,128]{2,1,0:T(8,128)(2,1)S(1)}, u32[]{:S(2)}, u32[]{:S(2)}) collective-permute-start(bf16[32,16,128]{2,1,0:T(8,128)(2,1)S(1)} %constant_dynamic-slice_fusion.4), channel_id=1, source_target_pairs={{0,3},{1,2},{2,1},{3,0},{4,7},{5,6},{6,5},{7,4},{8,11},{9,10},{10,... | collective-permute-start | bytes 393224 | tf_op jit(solution)/shard_map/ppermute | solution.py:100
  6.4 17.7 %collective-permute-start.1 = (bf16[32,16,128]{2,1,0:T(8,128)(2,1)S(1)}, bf16[32,16,128]{2,1,0:T(8,128)(2,1)S(1)}, u32[]{:S(2)}, u32[]{:S(2)}) collective-permute-start(bf16[32,16,128]{2,1,0:T(8,128)(2,1)S(1)} %constant_dynamic-slice_fusion.5), channel_id=1, source_target_pairs={{0,2},{1,3},{2,0},{3,1},{4,6},{5,7},{6,4},{7,5},{8,10},{9,11},{10,... | collective-permute-start | bytes 393224 | tf_op jit(solution)/shard_map/ppermute | solution.py:100
  6.4 17.7 %collective-permute-start = (bf16[32,16,128]{2,1,0:T(8,128)(2,1)S(1)}, bf16[32,16,128]{2,1,0:T(8,128)(2,1)S(1)}, u32[]{:S(2)}, u32[]{:S(2)}) collective-permute-start(bf16[32,16,128]{2,1,0:T(8,128)(2,1)S(1)} %constant_dynamic-slice_fusion.6), channel_id=1, source_target_pairs={{0,1},{1,0},{2,3},{3,2},{4,5},{5,4},{6,7},{7,6},{8,9},{9,8},{10,11... | collective-permute-start | bytes 393224 | tf_op jit(solution)/shard_map/ppermute | solution.py:100
  7.1 22.7 %collective-permute-start.5 = (bf16[32,16,128]{2,1,0:T(8,128)(2,1)S(1)}, bf16[32,16,128]{2,1,0:T(8,128)(2,1)S(1)}, u32[]{:S(2)}, u32[]{:S(2)}) collective-permute-start(bf16[32,16,128]{2,1,0:T(8,128)(2,1)S(1)} %constant_dynamic-slice_fusion.2), channel_id=1, source_target_pairs={{0,2},{1,3},{2,0},{3,1},{4,6},{5,7},{6,4},{7,5},{8,10},{9,11},{10,... | collective-permute-start | bytes 393224 | tf_op jit(solution)/shard_map/ppermute | solution.py:100
  9.5 21.8 %collective-permute-start.6 = (bf16[32,16,128]{2,1,0:T(8,128)(2,1)S(1)}, bf16[32,16,128]{2,1,0:T(8,128)(2,1)S(1)}, u32[]{:S(2)}, u32[]{:S(2)}) collective-permute-start(bf16[32,16,128]{2,1,0:T(8,128)(2,1)S(1)} %constant_dynamic-slice_fusion.3), channel_id=1, source_target_pairs={{0,3},{1,2},{2,1},{3,0},{4,7},{5,6},{6,5},{7,4},{8,11},{9,10},{10,... | collective-permute-start | bytes 393224 | tf_op jit(solution)/shard_map/ppermute | solution.py:100
  12.1 3.7 %copy-start.1 = (f32[128,128]{1,0:T(8,128)S(1)}, f32[128,128]{1,0:T(8,128)}, u32[]{:S(2)}) copy-start(f32[128,128]{1,0:T(8,128)} %refs_6_.3) | copy-start | bytes 196612
  12.2 11.9 %copy-start.2 = (f32[64,128]{1,0:T(8,128)S(1)}, f32[64,128]{1,0:T(8,128)}, u32[]{:S(2)}) copy-start(f32[64,128]{1,0:T(8,128)} %refs_8_.3) | copy-start | bytes 98308
  26.3 8.6 %collective-permute-start.3 = (bf16[32,2048]{1,0:T(8,128)(2,1)S(1)}, bf16[32,2048]{1,0:T(8,128)(2,1)S(1)}, u32[]{:S(2)}, u32[]{:S(2)}) collective-permute-start(bf16[32,2048]{1,0:T(8,128)(2,1)S(1)} %get-tuple-element.78), channel_id=1, source_target_pairs={{0,1},{1,0},{2,3},{3,2},{4,5},{5,4},{6,7},{7,6},{8,9},{9,8},{10,11... | collective-permute-start | bytes 393224 | tf_op jit(solution)/shard_map/ppermute | solution.py:100
  26.4 10.1 %collective-permute-start.4 = (bf16[32,16,128]{2,1,0:T(8,128)(2,1)S(1)}, bf16[32,16,128]{2,1,0:T(8,128)(2,1)S(1)}, u32[]{:S(2)}, u32[]{:S(2)}) collective-permute-start(bf16[32,16,128]{2,1,0:T(8,128)(2,1)S(1)} %constant_dynamic-slice_fusion.1), channel_id=1, source_target_pairs={{0,1},{1,0},{2,3},{3,2},{4,5},{5,4},{6,7},{7,6},{8,9},{9,8},{10,11... | collective-permute-start | bytes 393224 | tf_op jit(solution)/shard_map/ppermute | solution.py:100
  28.5 15.1 %collective-permute-start.10 = (bf16[32,2048]{1,0:T(8,128)(2,1)S(1)}, bf16[32,2048]{1,0:T(8,128)(2,1)S(1)}, u32[]{:S(2)}, u32[]{:S(2)}) collective-permute-start(bf16[32,2048]{1,0:T(8,128)(2,1)S(1)} %get-tuple-element.97), channel_id=1, source_target_pairs={{0,2},{1,3},{2,0},{3,1},{4,6},{5,7},{6,4},{7,5},{8,10},{9,11},{10,... | collective-permute-start | bytes 393224 | tf_op jit(solution)/shard_map/ppermute | solution.py:100
  29.8 13.8 %collective-permute-start.11 = (bf16[32,2048]{1,0:T(8,128)(2,1)S(1)}, bf16[32,2048]{1,0:T(8,128)(2,1)S(1)}, u32[]{:S(2)}, u32[]{:S(2)}) collective-permute-start(bf16[32,2048]{1,0:T(8,128)(2,1)S(1)} %get-tuple-element.98), channel_id=1, source_target_pairs={{0,3},{1,2},{2,1},{3,0},{4,7},{5,6},{6,5},{7,4},{8,11},{9,10},{10,... | collective-permute-start | bytes 393224 | tf_op jit(solution)/shard_map/ppermute | solution.py:100
  36.5 13.7 %collective-permute-start.8 = (bf16[64,2048]{1,0:T(8,128)(2,1)S(1)}, bf16[64,2048]{1,0:T(8,128)(2,1)S(1)}, u32[]{:S(2)}, u32[]{:S(2)}) collective-permute-start(bf16[64,2048]{1,0:T(8,128)(2,1)S(1)} %constant_dynamic-update-slice_fusion), channel_id=1, source_target_pairs={{0,8},{4,12},{8,0},{12,4},{1,9},{5,13},{9,1},{13,5},{2,10},{6,14},... | collective-permute-start | bytes 786440 | tf_op jit(solution)/shard_map/ppermute | solution.py:100
  43.5 6.7 %collective-permute-start.7 = (bf16[32,2048]{1,0:T(8,128)(2,1)S(1)}, bf16[32,2048]{1,0:T(8,128)(2,1)S(1)}, u32[]{:S(2)}, u32[]{:S(2)}) collective-permute-start(bf16[32,2048]{1,0:T(8,128)(2,1)S(1)} %get-tuple-element.89), channel_id=1, source_target_pairs={{0,1},{1,0},{2,3},{3,2},{4,5},{5,4},{6,7},{7,6},{8,9},{9,8},{10,11... | collective-permute-start | bytes 393224 | tf_op jit(solution)/shard_map/ppermute | solution.py:100
  43.6 6.7 %collective-permute-start.12 = (bf16[64,2048]{1,0:T(8,128)(2,1)S(1)}, bf16[64,2048]{1,0:T(8,128)(2,1)S(1)}, u32[]{:S(2)}, u32[]{:S(2)}) collective-permute-start(bf16[64,2048]{1,0:T(8,128)(2,1)S(1)} %constant_dynamic-update-slice_fusion.2), channel_id=1, source_target_pairs={{0,8},{4,12},{8,0},{12,4},{1,9},{5,13},{9,1},{13,5},{2,10},{6,14},... | collective-permute-start | bytes 786440 | tf_op jit(solution)/shard_map/ppermute | solution.py:100
  43.7 7.2 %copy-start.3 = (bf16[64,8,16,128]{3,1,2,0:T(8,128)(2,1)S(1)}, bf16[64,8,16,128]{3,1,2,0:T(8,128)(2,1)}, u32[]{:S(2)}) copy-start(bf16[64,8,16,128]{3,1,2,0:T(8,128)(2,1)} %copy.19) | copy-start | bytes 6291460
  43.8 9.0 %collective-permute-start.19 = (bf16[32,2048]{1,0:T(8,128)(2,1)S(1)}, bf16[32,2048]{1,0:T(8,128)(2,1)S(1)}, u32[]{:S(2)}, u32[]{:S(2)}) collective-permute-start(bf16[32,2048]{1,0:T(8,128)(2,1)S(1)} %get-tuple-element.108), channel_id=1, source_target_pairs={{0,2},{1,3},{2,0},{3,1},{4,6},{5,7},{6,4},{7,5},{8,10},{9,11},{10,... | collective-permute-start | bytes 393224 | tf_op jit(solution)/shard_map/ppermute | solution.py:100
  43.8 8.9 %collective-permute-start.20 = (bf16[32,2048]{1,0:T(8,128)(2,1)S(1)}, bf16[32,2048]{1,0:T(8,128)(2,1)S(1)}, u32[]{:S(2)}, u32[]{:S(2)}) collective-permute-start(bf16[32,2048]{1,0:T(8,128)(2,1)S(1)} %get-tuple-element.109), channel_id=1, source_target_pairs={{0,3},{1,2},{2,1},{3,0},{4,7},{5,6},{6,5},{7,4},{8,11},{9,10},{10,... | collective-permute-start | bytes 393224 | tf_op jit(solution)/shard_map/ppermute | solution.py:100
  50.2 4.7 %collective-permute-start.9 = (bf16[128,2048]{1,0:T(8,128)(2,1)S(1)}, bf16[128,2048]{1,0:T(8,128)(2,1)S(1)}, u32[]{:S(2)}, u32[]{:S(2)}) collective-permute-start(bf16[128,2048]{1,0:T(8,128)(2,1)S(1)} %pad_maximum_fusion), channel_id=1, source_target_pairs={{0,4},{4,0},{8,12},{12,8},{1,5},{5,1},{9,13},{13,9},{2,6},{6,2},{1... | collective-permute-start | bytes 1572872 | tf_op jit(solution)/shard_map/ppermute | solution.py:100
  50.4 5.4 %collective-permute-start.13 = (bf16[128,2048]{1,0:T(8,128)(2,1)S(1)}, bf16[128,2048]{1,0:T(8,128)(2,1)S(1)}, u32[]{:S(2)}, u32[]{:S(2)}) collective-permute-start(bf16[128,2048]{1,0:T(8,128)(2,1)S(1)} %pad_maximum_fusion.1), channel_id=1, source_target_pairs={{0,4},{4,0},{8,12},{12,8},{1,5},{5,1},{9,13},{13,9},{2,6},{6,2},{1... | collective-permute-start | bytes 1572872 | tf_op jit(solution)/shard_map/ppermute | solution.py:100
  52.6 9.2 %collective-permute-start.17 = (bf16[64,2048]{1,0:T(8,128)(2,1)S(1)}, bf16[64,2048]{1,0:T(8,128)(2,1)S(1)}, u32[]{:S(2)}, u32[]{:S(2)}) collective-permute-start(bf16[64,2048]{1,0:T(8,128)(2,1)S(1)} %constant_dynamic-update-slice_fusion.4), channel_id=1, source_target_pairs={{0,8},{4,12},{8,0},{12,4},{1,9},{5,13},{9,1},{13,5},{2,10},{6,14},... | collective-permute-start | bytes 786440 | tf_op jit(solution)/shard_map/ppermute | solution.py:100
  52.8 13.7 %collective-permute-start.21 = (bf16[64,2048]{1,0:T(8,128)(2,1)S(1)}, bf16[64,2048]{1,0:T(8,128)(2,1)S(1)}, u32[]{:S(2)}, u32[]{:S(2)}) collective-permute-start(bf16[64,2048]{1,0:T(8,128)(2,1)S(1)} %constant_dynamic-update-slice_fusion.6), channel_id=1, source_target_pairs={{0,8},{4,12},{8,0},{12,4},{1,9},{5,13},{9,1},{13,5},{2,10},{6,14},... | collective-permute-start | bytes 786440 | tf_op jit(solution)/shard_map/ppermute | solution.py:100
  56.7 17.5 %collective-permute-start.16 = (bf16[1,128,512]{2,1,0:T(8,128)(2,1)S(1)}, bf16[1,128,512]{2,1,0:T(8,128)(2,1)S(1)}, u32[]{:S(2)}, u32[]{:S(2)}) collective-permute-start(bf16[1,128,512]{2,1,0:T(8,128)(2,1)S(1)} %get-tuple-element.131), channel_id=1, source_target_pairs={{0,3},{1,2},{2,1},{3,0},{4,7},{5,6},{6,5},{7,4},{8,11},{9,10},{10,... | collective-permute-start | bytes 393224 | tf_op jit(solution)/shard_map/ppermute | solution.py:100
  59.0 15.2 %collective-permute-start.15 = (bf16[1,128,512]{2,1,0:T(8,128)(2,1)S(1)}, bf16[1,128,512]{2,1,0:T(8,128)(2,1)S(1)}, u32[]{:S(2)}, u32[]{:S(2)}) collective-permute-start(bf16[1,128,512]{2,1,0:T(8,128)(2,1)S(1)} %get-tuple-element.101), channel_id=1, source_target_pairs={{0,2},{1,3},{2,0},{3,1},{4,6},{5,7},{6,4},{7,5},{8,10},{9,11},{10,... | collective-permute-start | bytes 393224 | tf_op jit(solution)/shard_map/ppermute | solution.py:100
  60.0 12.9 %collective-permute-start.14 = (bf16[1,128,512]{2,1,0:T(8,128)(2,1)S(1)}, bf16[1,128,512]{2,1,0:T(8,128)(2,1)S(1)}, u32[]{:S(2)}, u32[]{:S(2)}) collective-permute-start(bf16[1,128,512]{2,1,0:T(8,128)(2,1)S(1)} %get-tuple-element.102), channel_id=1, source_target_pairs={{0,1},{1,0},{2,3},{3,2},{4,5},{5,4},{6,7},{7,6},{8,9},{9,8},{10,11... | collective-permute-start | bytes 393224 | tf_op jit(solution)/shard_map/ppermute | solution.py:100
  61.9 5.7 %collective-permute-start.18 = (bf16[128,2048]{1,0:T(8,128)(2,1)S(1)}, bf16[128,2048]{1,0:T(8,128)(2,1)S(1)}, u32[]{:S(2)}, u32[]{:S(2)}) collective-permute-start(bf16[128,2048]{1,0:T(8,128)(2,1)S(1)} %pad_maximum_fusion.2), channel_id=1, source_target_pairs={{0,4},{4,0},{8,12},{12,8},{1,5},{5,1},{9,13},{13,9},{2,6},{6,2},{1... | collective-permute-start | bytes 1572872 | tf_op jit(solution)/shard_map/ppermute | solution.py:100
  66.6 2.0 %collective-permute-start.22 = (bf16[128,2048]{1,0:T(8,128)(2,1)S(1)}, bf16[128,2048]{1,0:T(8,128)(2,1)S(1)}, u32[]{:S(2)}, u32[]{:S(2)}) collective-permute-start(bf16[128,2048]{1,0:T(8,128)(2,1)S(1)} %pad_maximum_fusion.3), channel_id=1, source_target_pairs={{0,4},{4,0},{8,12},{12,8},{1,5},{5,1},{9,13},{13,9},{2,6},{6,2},{1... | collective-permute-start | bytes 1572872 | tf_op jit(solution)/shard_map/ppermute | solution.py:100
  69.5 15.4 %collective-permute-start.25 = (bf16[1,128,512]{2,1,0:T(8,128)(2,1)S(1)}, bf16[1,128,512]{2,1,0:T(8,128)(2,1)S(1)}, u32[]{:S(2)}, u32[]{:S(2)}) collective-permute-start(bf16[1,128,512]{2,1,0:T(8,128)(2,1)S(1)} %get-tuple-element.130), channel_id=1, source_target_pairs={{0,3},{1,2},{2,1},{3,0},{4,7},{5,6},{6,5},{7,4},{8,11},{9,10},{10,... | collective-permute-start | bytes 393224 | tf_op jit(solution)/shard_map/ppermute | solution.py:100
  69.6 15.3 %collective-permute-start.24 = (bf16[1,128,512]{2,1,0:T(8,128)(2,1)S(1)}, bf16[1,128,512]{2,1,0:T(8,128)(2,1)S(1)}, u32[]{:S(2)}, u32[]{:S(2)}) collective-permute-start(bf16[1,128,512]{2,1,0:T(8,128)(2,1)S(1)} %get-tuple-element.114), channel_id=1, source_target_pairs={{0,2},{1,3},{2,0},{3,1},{4,6},{5,7},{6,4},{7,5},{8,10},{9,11},{10,... | collective-permute-start | bytes 393224 | tf_op jit(solution)/shard_map/ppermute | solution.py:100
  72.9 7.2 %collective-permute-start.23 = (bf16[1,128,512]{2,1,0:T(8,128)(2,1)S(1)}, bf16[1,128,512]{2,1,0:T(8,128)(2,1)S(1)}, u32[]{:S(2)}, u32[]{:S(2)}) collective-permute-start(bf16[1,128,512]{2,1,0:T(8,128)(2,1)S(1)} %get-tuple-element.115), channel_id=1, source_target_pairs={{0,1},{1,0},{2,3},{3,2},{4,5},{5,4},{6,7},{7,6},{8,9},{9,8},{10,11... | collective-permute-start | bytes 393224 | tf_op jit(solution)/shard_map/ppermute | solution.py:100

commit v17 on v12

--- a/solution.py
+++ b/solution.py
@@ -80,7 +80,7 @@
         out_shape=[jax.ShapeDtypeStruct((count, width), jnp.bfloat16)] * slices,
         scratch_shapes=[pltpu.VMEM((block * order, columns), jnp.float32)],
         compiler_params=pltpu.CompilerParams(vmem_limit_bytes=32 * 1024 * 1024),
-        cost_estimate=pl.CostEstimate(flops=0, bytes_accessed=0, transcendentals=0),
+        cost_estimate=pl.CostEstimate(flops=1000000000, bytes_accessed=0, transcendentals=0),
     )(*pieces[::-1], basis, basis.T, in_basis, in_basis.T, corrections)
 
 
@@ -105,6 +105,25 @@
     return [blocks[0]] + [moved[mask] for mask in range(1, slices)]
 
 
+def in_turn(blocks):
+    done = []
+    for block in reversed(blocks):
+        done.append(after(block, *done[-1:]))
+    return done[::-1]
+
+
+def met(block, mask, count):
+    rows = jnp.split(block, count, axis=1)
+    return jnp.concatenate([rows[at ^ mask] for at in range(count)], axis=1)
+
+
+def paired(blocks, mask, slices, kind):
+    arrived = crossed(jnp.stack(blocks[1::2]), "proj", slices, mask)
+    kept = blocks[::2]
+    moved = [met(arrived[at], mask, kept[at].shape[1]).astype(jnp.float32) for at in range(len(kept))]
+    return [(value.astype(jnp.float32) + other).astype(kind) for value, other in zip(kept, moved)]
+
+
 def after(value, *tokens):
     return lax.optimization_barrier((value, tokens))[0]
 
@@ -119,7 +138,12 @@
     values = []
     for block in (near, far):
         value = lax.dot_general(block, train_flat, contract, preferred_element_type=jnp.float32)
-        values.append(value.astype(jnp.bfloat16).reshape(shares // 2, -1, train_flat.shape[0]))
+        values.append(value.astype(jnp.bfloat16))
+    return values
+
+
+def split_shares(values, shares):
+    values = [value.reshape(shares // 2, -1, value.shape[1]) for value in values]
     return [values[at % 2][at // 2] for at in range(shares)]
 
 
@@ -146,43 +170,67 @@
     basis = jnp.concatenate(turned([row_blocks[at] for at in range(slices)], here), axis=0)
     condition = condition_fast if rows_here % 16 == 0 else condition_plain
     parts = [count * size // sum(CHUNKS) for size in CHUNKS]
+    source = queries
     half = slices // 2
-    pieces, rows, results = [], [], []
-    source = queries
+    pieces, results = [], []
     for chunk, part in enumerate(parts):
         first, each = sum(parts[:chunk]), part // slices
         if chunk:
-            source, pieces[0][-1], train_flat = lax.optimization_barrier((source, pieces[0][-1], train_flat))
+            source, pieces[0][-1] = lax.optimization_barrier((source, pieces[0][-1]))
         raw = {}
-        for mask in (reversed(range(slices)) if chunk else range(slices)):
+        for mask in (range(slices) if chunk else reversed(range(slices))):
             block = lax.dynamic_slice_in_dim(source, first + (here ^ mask) * each, each, 0)
             raw[mask], source = lax.optimization_barrier((block, source))
         pieces.append(exchanged(raw, slices))
     made = condition(pieces[0], basis, in_basis, corrections)
-    rows.append(exchanged(made, slices))
-    rows[0][:half], pieces[1] = lax.optimization_barrier((rows[0][:half], pieces[1]))
-    spread = over_shares(rows[0][:half], shares)
+    first_rows = exchanged(made, slices)
+    first_rows[:half], pieces[1] = lax.optimization_barrier((first_rows[:half], pieces[1]))
+    spread_a1 = over_shares(first_rows[:half], shares)
     made = condition(pieces[1], basis, in_basis, corrections)
-    rows.append(exchanged(made, slices))
-    rows[1][:half], spread = lax.optimization_barrier((rows[1][:half], spread))
-    came = []
-    for chunk, part in enumerate(parts):
-        each = part // slices
-        groups = []
-        for group in (rows[chunk][:half], rows[chunk][half:]):
-            if chunk and groups:
-                group = after(group, near_before)
-            if chunk or groups:
-                spread = over_shares(group, shares)
-            near = lax.optimization_barrier(jnp.concatenate(after(spread, *came[2:3]), axis=0))
-            far = crossed(near, "dp", shares, 1)
-            groups.append(products(near, far, train_flat, shares))
-        near_before = near
-        values = [jnp.concatenate(pair, axis=0) for pair in zip(*groups)]
-        values = [jnp.stack(values[at * owned:(at + 1) * owned]) for at in range(slices)]
-        came = exchanged(turned(values, here ^ (share // owned)), slices)
-        sums = [value.reshape(owned, slices, each, train_count) for value in came]
-        total = [sum(sums[mask][:, at ^ mask].astype(jnp.float32) for mask in range(slices)) for at in range(slices)]
+    last_rows = exchanged(made, slices)
+    first_rows[half:], last_rows[1] = lax.optimization_barrier((first_rows[half:], last_rows[1]))
+    spread_a2 = over_shares(first_rows[half:], shares)
+    last_rows[:half], spread_a1 = lax.optimization_barrier((last_rows[:half], spread_a1))
+    place = here ^ (share // owned)
+    spread_a1 = after(spread_a1, last_rows[1])
+    near_a1 = lax.optimization_barrier(jnp.concatenate(spread_a1, axis=0))
+    far_a1 = crossed(near_a1, "dp", shares, 1)
+    val_a1 = products(near_a1, far_a1, train_flat, shares)
+    spread_b1 = over_shares(last_rows[:half], shares)
+    near_a2 = lax.optimization_barrier(jnp.concatenate(spread_a2, axis=0))
+    far_a2 = crossed(near_a2, "dp", shares, 1)
+    val_a2 = products(near_a2, far_a2, train_flat, shares)
+    part_a1 = split_shares(val_a1, shares)
+    part_a1 = [jnp.concatenate(part_a1[at * owned:(at + 1) * owned]) for at in range(slices)]
+    part_a1 = [value.reshape(owned, half, -1, train_count) for value in part_a1]
+    part_a2 = split_shares(val_a2, shares)
+    part_a2 = [jnp.concatenate(part_a2[at * owned:(at + 1) * owned]) for at in range(slices)]
+    part_a2 = [value.reshape(owned, half, -1, train_count) for value in part_a2]
+    blocks = turned([jnp.concatenate(pair, axis=1) for pair in zip(part_a1, part_a2)], place)
+    blocks = in_turn(blocks)
+    came = exchanged(blocks, slices)
+    group = after(last_rows[half:], far_a1)
+    spread_b2 = over_shares(group, shares)
+    spread_b1 = after(spread_b1, came[0])
+    near_b1 = lax.optimization_barrier(jnp.concatenate(spread_b1, axis=0))
+    far_b1 = crossed(near_b1, "dp", shares, 1)
+    val_b1 = products(near_b1, far_b1, train_flat, shares)
+    spread_b2 = after(spread_b2, came[0])
+    near_b2 = lax.optimization_barrier(jnp.concatenate(spread_b2, axis=0))
+    far_b2 = crossed(near_b2, "dp", shares, 1)
+    val_b2 = products(near_b2, far_b2, train_flat, shares)
+    part_b1 = split_shares(val_b1, shares)
+    part_b1 = [jnp.concatenate(part_b1[at * owned:(at + 1) * owned]) for at in range(slices)]
+    part_b1 = [value.reshape(owned, half, -1, train_count) for value in part_b1]
+    part_b2 = split_shares(val_b2, shares)
+    part_b2 = [jnp.concatenate(part_b2[at * owned:(at + 1) * owned]) for at in range(slices)]
+    part_b2 = [value.reshape(owned, half, -1, train_count) for value in part_b2]
+    blocks = turned([jnp.concatenate(pair, axis=1) for pair in zip(part_b1, part_b2)], place)
+    blocks = in_turn(blocks)
+    left = exchanged(blocks, slices)
+    last = [sum(left[mask][:, at ^ mask].astype(jnp.float32) for mask in range(slices)) for at in range(slices)]
+    whole = [sum(came[mask][:, at ^ mask].astype(jnp.float32) for mask in range(slices)) for at in range(slices)]
+    for part, total in zip(parts, (whole, last)):
         total = jnp.stack(turned(total, here), axis=1)
         total = jnp.stack(turned([total[at] for at in range(owned)], share % owned))
         results.append(total.reshape(owned, part, train_count))

time: 84.8 us -> 85.5 us (level)
  starting transfers between devices: 42.1 us -> 34.3 us
  waiting for transfers between devices: 22.8 us -> 28.9 us
  matrix products: 6.65 us -> 8.38 us
    ppermute x26, starting transfers between devices: 42.1 us -> 34.3 us  [crossed(): return lax.ppermute(value, axis, [(at, at ^ mask) for at in range(size)])]
    ppermute x26, waiting for transfers between devices: 22.8 us -> 28.9 us  [crossed(): return lax.ppermute(value, axis, [(at, at ^ mask) for at in range(size)])]
    dot_general x8, matrix products: 6.65 us -> 8.38 us  [products(): lax.dot_general(block, train_flat, contract, preferred_element_type=jnp.f...]
    unnamed x18 -> x17, local copies, waits for them, and re-layouts: 5.21 us -> 6.02 us
  transfers between devices with their start and end apart: 26 -> 26, of which waited for: 7 -> 8; matrix products, arithmetic and copies ran while one was open for 13% -> 17% of each run, Pallas kernels for 5% -> 5%
where the time goes in v17:
time: 85.5 us; the launch traced here: 85.2 us
  starting transfers between devices  34.3 us (40%)
  waiting for transfers between devices  28.9 us (34%)
  matrix products  8.38 us (10%)
  local copies, waits for them, and re-layouts  7.08 us (8%)
  Pallas kernels  4.46 us (5%)
  other arithmetic  1.53 us (2%)
    ppermute x26, starting transfers between devices, crossed(): return lax.ppermute(value, axis, [(at, at ^ mask) for at in range(size)])  34.3 us
    ppermute x26, waiting for transfers between devices, crossed(): return lax.ppermute(value, axis, [(at, at ^ mask) for at in range(size)])  28.9 us
    dot_general x8, matrix products, products(): lax.dot_general(block, train_flat, contract, preferred_element_type=jnp.f...  8.38 us
    unnamed x17, local copies, waits for them, and re-layouts  6.02 us
    pallas_call x2, Pallas kernels, condition_fast(): pl.pallas_call(functools.partial(condition_kernel, slices, rows_here), gr...  4.46 us
  transfers between devices with their start and end apart: 26, of which 8 were waited for; matrix products, arithmetic and copies ran while one was open for 17% of the time, Pallas kernels for 5%

profile of v17, /device:TPU:0, one launch (start us, length us, event | category | flops | bytes accessed | tf_op | source)
XLA Modules:
  0.0 85.2 jit_solution(15371198203965842944)
XLA Ops:
  0.0 1.2 %copy-done = bf16[256,16,128]{2,1,0:T(8,128)(2,1)S(1)} copy-done((bf16[256,16,128]{2,1,0:T(8,128)(2,1)S(1)}, bf16[256,16,128]{2,1,0:T(8,128)(2,1)}, u32[]{:S(2)}) %copy-start) | copy-done | bytes 1048600
  1.2 5.1 %collective-permute-start = (bf16[32,16,128]{2,1,0:T(8,128)(2,1)S(1)}, bf16[32,16,128]{2,1,0:T(8,128)(2,1)S(1)}, u32[]{:S(2)}, u32[]{:S(2)}) collective-permute-start(bf16[32,16,128]{2,1,0:T(8,128)(2,1)S(1)} %constant_dynamic-slice_fusion.7), channel_id=1, source_target_pairs={{0,3},{1,2},{2,1},{3,0},{4,7},{5,6},{6,5},{7,4},{8,11},{9,10},{10,... | collective-permute-start | bytes 393224 | tf_op jit(solution)/shard_map/ppermute | solution.py:100
  6.4 0.1 collective-permute-start.2
  6.5 0.6 collective-permute-start.1
  7.1 0.7 fusion.8
  7.8 0.1 copy.13
  7.9 0.1 copy.14
  8.0 0.1 copy.15
  8.1 0.1 copy.16
  8.2 0.1 pad_maximum_fusion.15
  8.3 0.1 copy.11.refs_4_
  8.4 0.9 %copy.10 = f32[128,128]{0,1:T(8,128)S(1)} copy(f32[128,128]{1,0:T(8,128)} %refs_6_.3) | data formatting | bytes 131072 | tf_op args[3]
  9.4 1.4 %collective-permute-done.refs_0_ = bf16[32,16,128]{2,1,0:T(8,128)(2,1)S(1)} collective-permute-done((bf16[32,16,128]{2,1,0:T(8,128)(2,1)S(1)}, bf16[32,16,128]{2,1,0:T(8,128)(2,1)S(1)}, u32[]{:S(2)}, u32[]{:S(2)}) %collective-permute-start) | collective-permute-done | bytes 131104 | tf_op jit(solution)/shard_map/ppermute | solution.py:100
  10.8 3.9 %collective-permute-start.6 = (bf16[32,16,128]{2,1,0:T(8,128)(2,1)S(1)}, bf16[32,16,128]{2,1,0:T(8,128)(2,1)S(1)}, u32[]{:S(2)}, u32[]{:S(2)}) collective-permute-start(bf16[32,16,128]{2,1,0:T(8,128)(2,1)S(1)} %constant_dynamic-slice_fusion), channel_id=1, source_target_pairs={{0,3},{1,2},{2,1},{3,0},{4,7},{5,6},{6,5},{7,4},{8,11},{9,10},{10,... | collective-permute-start | bytes 393224 | tf_op jit(solution)/shard_map/ppermute | solution.py:100
  14.7 1.1 %collective-permute-start.5 = (bf16[32,16,128]{2,1,0:T(8,128)(2,1)S(1)}, bf16[32,16,128]{2,1,0:T(8,128)(2,1)S(1)}, u32[]{:S(2)}, u32[]{:S(2)}) collective-permute-start(bf16[32,16,128]{2,1,0:T(8,128)(2,1)S(1)} %constant_dynamic-slice_fusion.1), channel_id=1, source_target_pairs={{0,2},{1,3},{2,0},{3,1},{4,6},{5,7},{6,4},{7,5},{8,10},{9,11},{10,... | collective-permute-start | bytes 393224 | tf_op jit(solution)/shard_map/ppermute | solution.py:100
  15.8 0.0 collective-permute-start.4
  15.8 0.0 collective-permute-done.2.refs_2_
  15.8 8.3 %collective-permute-done.1.refs_1_ = bf16[32,16,128]{2,1,0:T(8,128)(2,1)S(1)} collective-permute-done((bf16[32,16,128]{2,1,0:T(8,128)(2,1)S(1)}, bf16[32,16,128]{2,1,0:T(8,128)(2,1)S(1)}, u32[]{:S(2)}, u32[]{:S(2)}) %collective-permute-start.1) | collective-permute-done | bytes 131104 | tf_op jit(solution)/shard_map/ppermute | solution.py:100
  24.1 2.2 %shard_map.55 = (bf16[32,2048]{1,0:T(8,128)(2,1)S(1)}, bf16[32,2048]{1,0:T(8,128)(2,1)S(1)}, bf16[32,2048]{1,0:T(8,128)(2,1)S(1)}, bf16[32,2048]{1,0:T(8,128)(2,1)S(1)}) custom-call(bf16[32,16,128]{2,1,0:T(8,128)(2,1)S(1)} %collective-permute-done.refs_0_, bf16[32,16,128]{2,1,0:T(8,128)(2,1)S(1)} %collective-permute-done.1.refs_1_, ...), custom_call_target="tpu_custom_call" | custom-call | flops 1000000000 | tf_op jit(solution)/shard_map/pallas_call | solution.py:75
  26.3 0.1 collective-permute-start.3
  26.4 2.8 %collective-permute-start.7 = (bf16[32,2048]{1,0:T(8,128)(2,1)S(1)}, bf16[32,2048]{1,0:T(8,128)(2,1)S(1)}, u32[]{:S(2)}, u32[]{:S(2)}) collective-permute-start(bf16[32,2048]{1,0:T(8,128)(2,1)S(1)} %get-tuple-element.81), channel_id=1, source_target_pairs={{0,2},{1,3},{2,0},{3,1},{4,6},{5,7},{6,4},{7,5},{8,10},{9,11},{10,... | collective-permute-start | bytes 393224 | tf_op jit(solution)/shard_map/ppermute | solution.py:100
  29.2 0.0 collective-permute-done.6.refs_0_
  29.2 1.6 %collective-permute-start.8 = (bf16[32,2048]{1,0:T(8,128)(2,1)S(1)}, bf16[32,2048]{1,0:T(8,128)(2,1)S(1)}, u32[]{:S(2)}, u32[]{:S(2)}) collective-permute-start(bf16[32,2048]{1,0:T(8,128)(2,1)S(1)} %get-tuple-element.82), channel_id=1, source_target_pairs={{0,3},{1,2},{2,1},{3,0},{4,7},{5,6},{6,5},{7,4},{8,11},{9,10},{10,... | collective-permute-start | bytes 393224 | tf_op jit(solution)/shard_map/ppermute | solution.py:100
  30.8 0.0 collective-permute-done.4.refs_2_
  30.8 4.3 %collective-permute-done.3 = bf16[32,2048]{1,0:T(8,128)(2,1)S(1)} collective-permute-done((bf16[32,2048]{1,0:T(8,128)(2,1)S(1)}, bf16[32,2048]{1,0:T(8,128)(2,1)S(1)}, u32[]{:S(2)}, u32[]{:S(2)}) %collective-permute-start.3) | collective-permute-done | bytes 131104 | tf_op jit(solution)/shard_map/ppermute | solution.py:100
  35.1 2.2 %shard_map.56 = (bf16[32,2048]{1,0:T(8,128)(2,1)S(1)}, bf16[32,2048]{1,0:T(8,128)(2,1)S(1)}, bf16[32,2048]{1,0:T(8,128)(2,1)S(1)}, bf16[32,2048]{1,0:T(8,128)(2,1)S(1)}) custom-call(bf16[32,16,128]{2,1,0:T(8,128)(2,1)S(1)} %collective-permute-done.6.refs_0_, bf16[32,16,128]{2,1,0:T(8,128)(2,1)S(1)} %collective-permute-done.5.refs_1_, ...), custom_call_target="tpu_custom_call" | custom-call | flops 1000000000 | tf_op jit(solution)/shard_map/pallas_call | solution.py:75
  37.3 0.1 collective-permute-start.9
  37.4 1.6 %collective-permute-start.10 = (bf16[64,2048]{1,0:T(8,128)(2,1)S(1)}, bf16[64,2048]{1,0:T(8,128)(2,1)S(1)}, u32[]{:S(2)}, u32[]{:S(2)}) collective-permute-start(bf16[64,2048]{1,0:T(8,128)(2,1)S(1)} %constant_dynamic-update-slice_fusion), channel_id=1, source_target_pairs={{0,8},{4,12},{8,0},{12,4},{1,9},{5,13},{9,1},{13,5},{2,10},{6,14},... | collective-permute-start | bytes 786440 | tf_op jit(solution)/shard_map/ppermute | solution.py:100
  39.0 3.5 %copy.19 = bf16[64,8,16,128]{3,1,2,0:T(8,128)(2,1)} copy(bf16[64,8,16,128]{3,2,1,0:T(8,128)(2,1)} %bitcast.54) | data formatting | bytes 4194304
  42.5 5.4 %collective-permute-start.19 = (bf16[32,2048]{1,0:T(8,128)(2,1)S(1)}, bf16[32,2048]{1,0:T(8,128)(2,1)S(1)}, u32[]{:S(2)}, u32[]{:S(2)}) collective-permute-start(bf16[32,2048]{1,0:T(8,128)(2,1)S(1)} %get-tuple-element.100), channel_id=1, source_target_pairs={{0,2},{1,3},{2,0},{3,1},{4,6},{5,7},{6,4},{7,5},{8,10},{9,11},{10,... | collective-permute-start | bytes 393224 | tf_op jit(solution)/shard_map/ppermute | solution.py:100
  47.9 0.0 collective-permute-done.7
  47.9 0.0 collective-permute-done.9
  48.0 0.5 collective-permute-start.12
  48.5 0.0 collective-permute-done.10
  48.5 0.1 collective-permute-start.11
  48.6 2.6 %convolution_convert_fusion.5 = bf16[128,512]{1,0:T(8,128)(2,1)S(1)} fusion(bf16[128,2048]{1,0:T(8,128)(2,1)S(1)} %pad_maximum_fusion, bf16[512,2048]{1,0:T(8,128)(2,1)} %bitcast.46), kind=kOutput, calls=%fused_computation.6 | convolution fusion | flops 268500992 | bytes 2752512 | tf_op jit(solution)/shard_map/dot_general | solution.py:140
  51.2 1.6 %collective-permute-start.17 = (bf16[64,2048]{1,0:T(8,128)(2,1)S(1)}, bf16[64,2048]{1,0:T(8,128)(2,1)S(1)}, u32[]{:S(2)}, u32[]{:S(2)}) collective-permute-start(bf16[64,2048]{1,0:T(8,128)(2,1)S(1)} %constant_dynamic-update-slice_fusion.2), channel_id=1, source_target_pairs={{0,8},{4,12},{8,0},{12,4},{1,9},{5,13},{9,1},{13,5},{2,10},{6,14},... | collective-permute-start | bytes 786440 | tf_op jit(solution)/shard_map/ppermute | solution.py:100
  52.9 1.6 %collective-permute-done.12 = bf16[64,2048]{1,0:T(8,128)(2,1)S(1)} collective-permute-done((bf16[64,2048]{1,0:T(8,128)(2,1)S(1)}, bf16[64,2048]{1,0:T(8,128)(2,1)S(1)}, u32[]{:S(2)}, u32[]{:S(2)}) %collective-permute-start.12) | collective-permute-done | bytes 262176 | tf_op jit(solution)/shard_map/ppermute | solution.py:100
  54.5 0.1 collective-permute-start.13
  54.6 0.8 convolution_convert_fusion.4
  55.5 0.0 collective-permute-done.20
  55.6 0.4 collective-permute-start.21
  56.0 0.8 convolution_convert_fusion.7
  56.9 0.8 convolution_convert_fusion.6
  57.8 3.9 %collective-permute-start.16 = (bf16[1,4,32,512]{3,2,1,0:T(8,128)(2,1)S(1)}, bf16[1,4,32,512]{3,2,1,0:T(8,128)(2,1)S(1)}, u32[]{:S(2)}, u32[]{:S(2)}) collective-permute-start(bf16[1,4,32,512]{3,2,1,0:T(8,128)(2,1)S(1)} %get-tuple-element.123), channel_id=1, source_target_pairs={{0,3},{1,2},{2,1},{3,0},{4,7},{5,6},{6,5},{7,4},{8,11},{9,10},{10,... | collective-permute-start | bytes 393224 | tf_op jit(solution)/shard_map/ppermute | solution.py:100
  61.7 0.1 collective-permute-start.15
  61.8 0.6 collective-permute-start.14
  62.4 0.1 collective-permute-start.18
  62.5 0.8 convolution_convert_fusion.1
  63.3 2.3 %collective-permute-done.21 = bf16[64,2048]{1,0:T(8,128)(2,1)S(1)} collective-permute-done((bf16[64,2048]{1,0:T(8,128)(2,1)S(1)}, bf16[64,2048]{1,0:T(8,128)(2,1)S(1)}, u32[]{:S(2)}, u32[]{:S(2)}) %collective-permute-start.21) | collective-permute-done | bytes 262176 | tf_op jit(solution)/shard_map/ppermute | solution.py:100
  65.7 0.1 collective-permute-start.22
  65.8 0.8 convolution_convert_fusion
  66.6 0.8 convolution_convert_fusion.3
  67.5 0.2 collective-permute-done.22
  67.7 0.8 convolution_convert_fusion.2
  68.5 0.1 broadcast_select_fusion.9
  68.6 3.9 %collective-permute-start.25 = (bf16[1,4,32,512]{3,2,1,0:T(8,128)(2,1)S(1)}, bf16[1,4,32,512]{3,2,1,0:T(8,128)(2,1)S(1)}, u32[]{:S(2)}, u32[]{:S(2)}) collective-permute-start(bf16[1,4,32,512]{3,2,1,0:T(8,128)(2,1)S(1)} %get-tuple-element.122), channel_id=1, source_target_pairs={{0,3},{1,2},{2,1},{3,0},{4,7},{5,6},{6,5},{7,4},{8,11},{9,10},{10,... | collective-permute-start | bytes 393224 | tf_op jit(solution)/shard_map/ppermute | solution.py:100
  72.5 0.7 collective-permute-start.23
  73.2 0.1 broadcast_select_fusion.31
  73.3 8.1 %collective-permute-done.23 = bf16[1,4,32,512]{3,2,1,0:T(8,128)(2,1)S(1)} collective-permute-done((bf16[1,4,32,512]{3,2,1,0:T(8,128)(2,1)S(1)}, bf16[1,4,32,512]{3,2,1,0:T(8,128)(2,1)S(1)}, u32[]{:S(2)}, u32[]{:S(2)}) %collective-permute-start.23) | collective-permute-done | bytes 131104 | tf_op jit(solution)/shard_map/ppermute | solution.py:100
  81.4 2.8 %collective-permute-done.24 = bf16[1,4,32,512]{3,2,1,0:T(8,128)(2,1)S(1)} collective-permute-done((bf16[1,4,32,512]{3,2,1,0:T(8,128)(2,1)S(1)}, bf16[1,4,32,512]{3,2,1,0:T(8,128)(2,1)S(1)}, u32[]{:S(2)}, u32[]{:S(2)}) %collective-permute-start.24) | collective-permute-done | bytes 131104 | tf_op jit(solution)/shard_map/ppermute | solution.py:100
  84.2 0.1 broadcast_select_fusion.27
  84.3 0.1 broadcast_select_fusion.26
  84.4 0.8 maximum_bitcast_fusion
  (53 shorter events, 0.7 us)
Async XLA Ops:
  0.0 1.2 %copy-start = (bf16[256,16,128]{2,1,0:T(8,128)(2,1)S(1)}, bf16[256,16,128]{2,1,0:T(8,128)(2,1)}, u32[]{:S(2)}) copy-start(bf16[256,16,128]{2,1,0:T(8,128)(2,1)} %param.5) | copy-start | bytes 3145732
  0.0 24.1 %copy-start.1 = (f32[128,128]{1,0:T(8,128)S(1)}, f32[128,128]{1,0:T(8,128)}, u32[]{:S(2)}) copy-start(f32[128,128]{1,0:T(8,128)} %refs_6_.3) | copy-start | bytes 196612
  0.0 24.1 %copy-start.2 = (f32[64,128]{1,0:T(8,128)S(1)}, f32[64,128]{1,0:T(8,128)}, u32[]{:S(2)}) copy-start(f32[64,128]{1,0:T(8,128)} %refs_8_.3) | copy-start | bytes 98308
  1.2 9.5 %collective-permute-start = (bf16[32,16,128]{2,1,0:T(8,128)(2,1)S(1)}, bf16[32,16,128]{2,1,0:T(8,128)(2,1)S(1)}, u32[]{:S(2)}, u32[]{:S(2)}) collective-permute-start(bf16[32,16,128]{2,1,0:T(8,128)(2,1)S(1)} %constant_dynamic-slice_fusion.7), channel_id=1, source_target_pairs={{0,3},{1,2},{2,1},{3,0},{4,7},{5,6},{6,5},{7,4},{8,11},{9,10},{10,... | collective-permute-start | bytes 393224 | tf_op jit(solution)/shard_map/ppermute | solution.py:100
  6.4 9.4 %collective-permute-start.2 = (bf16[32,16,128]{2,1,0:T(8,128)(2,1)S(1)}, bf16[32,16,128]{2,1,0:T(8,128)(2,1)S(1)}, u32[]{:S(2)}, u32[]{:S(2)}) collective-permute-start(bf16[32,16,128]{2,1,0:T(8,128)(2,1)S(1)} %constant_dynamic-slice_fusion.5), channel_id=1, source_target_pairs={{0,1},{1,0},{2,3},{3,2},{4,5},{5,4},{6,7},{7,6},{8,9},{9,8},{10,11... | collective-permute-start | bytes 393224 | tf_op jit(solution)/shard_map/ppermute | solution.py:100
  6.5 17.6 %collective-permute-start.1 = (bf16[32,16,128]{2,1,0:T(8,128)(2,1)S(1)}, bf16[32,16,128]{2,1,0:T(8,128)(2,1)S(1)}, u32[]{:S(2)}, u32[]{:S(2)}) collective-permute-start(bf16[32,16,128]{2,1,0:T(8,128)(2,1)S(1)} %constant_dynamic-slice_fusion.6), channel_id=1, source_target_pairs={{0,2},{1,3},{2,0},{3,1},{4,6},{5,7},{6,4},{7,5},{8,10},{9,11},{10,... | collective-permute-start | bytes 393224 | tf_op jit(solution)/shard_map/ppermute | solution.py:100
  10.8 18.4 %collective-permute-start.6 = (bf16[32,16,128]{2,1,0:T(8,128)(2,1)S(1)}, bf16[32,16,128]{2,1,0:T(8,128)(2,1)S(1)}, u32[]{:S(2)}, u32[]{:S(2)}) collective-permute-start(bf16[32,16,128]{2,1,0:T(8,128)(2,1)S(1)} %constant_dynamic-slice_fusion), channel_id=1, source_target_pairs={{0,3},{1,2},{2,1},{3,0},{4,7},{5,6},{6,5},{7,4},{8,11},{9,10},{10,... | collective-permute-start | bytes 393224 | tf_op jit(solution)/shard_map/ppermute | solution.py:100
  14.7 16.1 %collective-permute-start.5 = (bf16[32,16,128]{2,1,0:T(8,128)(2,1)S(1)}, bf16[32,16,128]{2,1,0:T(8,128)(2,1)S(1)}, u32[]{:S(2)}, u32[]{:S(2)}) collective-permute-start(bf16[32,16,128]{2,1,0:T(8,128)(2,1)S(1)} %constant_dynamic-slice_fusion.1), channel_id=1, source_target_pairs={{0,2},{1,3},{2,0},{3,1},{4,6},{5,7},{6,4},{7,5},{8,10},{9,11},{10,... | collective-permute-start | bytes 393224 | tf_op jit(solution)/shard_map/ppermute | solution.py:100
  15.8 15.0 %collective-permute-start.4 = (bf16[32,16,128]{2,1,0:T(8,128)(2,1)S(1)}, bf16[32,16,128]{2,1,0:T(8,128)(2,1)S(1)}, u32[]{:S(2)}, u32[]{:S(2)}) collective-permute-start(bf16[32,16,128]{2,1,0:T(8,128)(2,1)S(1)} %constant_dynamic-slice_fusion.2), channel_id=1, source_target_pairs={{0,1},{1,0},{2,3},{3,2},{4,5},{5,4},{6,7},{7,6},{8,9},{9,8},{10,11... | collective-permute-start | bytes 393224 | tf_op jit(solution)/shard_map/ppermute | solution.py:100
  26.3 8.8 %collective-permute-start.3 = (bf16[32,2048]{1,0:T(8,128)(2,1)S(1)}, bf16[32,2048]{1,0:T(8,128)(2,1)S(1)}, u32[]{:S(2)}, u32[]{:S(2)}) collective-permute-start(bf16[32,2048]{1,0:T(8,128)(2,1)S(1)} %get-tuple-element.67), channel_id=1, source_target_pairs={{0,1},{1,0},{2,3},{3,2},{4,5},{5,4},{6,7},{7,6},{8,9},{9,8},{10,11... | collective-permute-start | bytes 393224 | tf_op jit(solution)/shard_map/ppermute | solution.py:100
  26.4 21.5 %collective-permute-start.7 = (bf16[32,2048]{1,0:T(8,128)(2,1)S(1)}, bf16[32,2048]{1,0:T(8,128)(2,1)S(1)}, u32[]{:S(2)}, u32[]{:S(2)}) collective-permute-start(bf16[32,2048]{1,0:T(8,128)(2,1)S(1)} %get-tuple-element.81), channel_id=1, source_target_pairs={{0,2},{1,3},{2,0},{3,1},{4,6},{5,7},{6,4},{7,5},{8,10},{9,11},{10,... | collective-permute-start | bytes 393224 | tf_op jit(solution)/shard_map/ppermute | solution.py:100
  29.2 18.7 %collective-permute-start.8 = (bf16[32,2048]{1,0:T(8,128)(2,1)S(1)}, bf16[32,2048]{1,0:T(8,128)(2,1)S(1)}, u32[]{:S(2)}, u32[]{:S(2)}) collective-permute-start(bf16[32,2048]{1,0:T(8,128)(2,1)S(1)} %get-tuple-element.82), channel_id=1, source_target_pairs={{0,3},{1,2},{2,1},{3,0},{4,7},{5,6},{6,5},{7,4},{8,11},{9,10},{10,... | collective-permute-start | bytes 393224 | tf_op jit(solution)/shard_map/ppermute | solution.py:100
  37.3 10.6 %collective-permute-start.9 = (bf16[32,2048]{1,0:T(8,128)(2,1)S(1)}, bf16[32,2048]{1,0:T(8,128)(2,1)S(1)}, u32[]{:S(2)}, u32[]{:S(2)}) collective-permute-start(bf16[32,2048]{1,0:T(8,128)(2,1)S(1)} %get-tuple-element.83), channel_id=1, source_target_pairs={{0,1},{1,0},{2,3},{3,2},{4,5},{5,4},{6,7},{7,6},{8,9},{9,8},{10,11... | collective-permute-start | bytes 393224 | tf_op jit(solution)/shard_map/ppermute | solution.py:100
  37.4 11.1 %collective-permute-start.10 = (bf16[64,2048]{1,0:T(8,128)(2,1)S(1)}, bf16[64,2048]{1,0:T(8,128)(2,1)S(1)}, u32[]{:S(2)}, u32[]{:S(2)}) collective-permute-start(bf16[64,2048]{1,0:T(8,128)(2,1)S(1)} %constant_dynamic-update-slice_fusion), channel_id=1, source_target_pairs={{0,8},{4,12},{8,0},{12,4},{1,9},{5,13},{9,1},{13,5},{2,10},{6,14},... | collective-permute-start | bytes 786440 | tf_op jit(solution)/shard_map/ppermute | solution.py:100
  42.5 13.0 %collective-permute-start.19 = (bf16[32,2048]{1,0:T(8,128)(2,1)S(1)}, bf16[32,2048]{1,0:T(8,128)(2,1)S(1)}, u32[]{:S(2)}, u32[]{:S(2)}) collective-permute-start(bf16[32,2048]{1,0:T(8,128)(2,1)S(1)} %get-tuple-element.100), channel_id=1, source_target_pairs={{0,2},{1,3},{2,0},{3,1},{4,6},{5,7},{6,4},{7,5},{8,10},{9,11},{10,... | collective-permute-start | bytes 393224 | tf_op jit(solution)/shard_map/ppermute | solution.py:100
  47.9 7.6 %collective-permute-start.20 = (bf16[32,2048]{1,0:T(8,128)(2,1)S(1)}, bf16[32,2048]{1,0:T(8,128)(2,1)S(1)}, u32[]{:S(2)}, u32[]{:S(2)}) collective-permute-start(bf16[32,2048]{1,0:T(8,128)(2,1)S(1)} %get-tuple-element.101), channel_id=1, source_target_pairs={{0,3},{1,2},{2,1},{3,0},{4,7},{5,6},{6,5},{7,4},{8,11},{9,10},{10,... | collective-permute-start | bytes 393224 | tf_op jit(solution)/shard_map/ppermute | solution.py:100
  48.0 6.5 %collective-permute-start.12 = (bf16[64,2048]{1,0:T(8,128)(2,1)S(1)}, bf16[64,2048]{1,0:T(8,128)(2,1)S(1)}, u32[]{:S(2)}, u32[]{:S(2)}) collective-permute-start(bf16[64,2048]{1,0:T(8,128)(2,1)S(1)} %pad_maximum_fusion.4), channel_id=1, source_target_pairs={{0,8},{4,12},{8,0},{12,4},{1,9},{5,13},{9,1},{13,5},{2,10},{6,14},... | collective-permute-start | bytes 786440 | tf_op jit(solution)/shard_map/ppermute | solution.py:100
  48.5 6.1 %copy-start.3 = (bf16[64,8,16,128]{3,1,2,0:T(8,128)(2,1)S(1)}, bf16[64,8,16,128]{3,1,2,0:T(8,128)(2,1)}, u32[]{:S(2)}) copy-start(bf16[64,8,16,128]{3,1,2,0:T(8,128)(2,1)} %copy.19) | copy-start | bytes 6291460
  48.5 7.0 %collective-permute-start.11 = (bf16[128,2048]{1,0:T(8,128)(2,1)S(1)}, bf16[128,2048]{1,0:T(8,128)(2,1)S(1)}, u32[]{:S(2)}, u32[]{:S(2)}) collective-permute-start(bf16[128,2048]{1,0:T(8,128)(2,1)S(1)} %pad_maximum_fusion), channel_id=1, source_target_pairs={{0,4},{4,0},{8,12},{12,8},{1,5},{5,1},{9,13},{13,9},{2,6},{6,2},{1... | collective-permute-start | bytes 1572872 | tf_op jit(solution)/shard_map/ppermute | solution.py:100
  51.2 11.1 %collective-permute-start.17 = (bf16[64,2048]{1,0:T(8,128)(2,1)S(1)}, bf16[64,2048]{1,0:T(8,128)(2,1)S(1)}, u32[]{:S(2)}, u32[]{:S(2)}) collective-permute-start(bf16[64,2048]{1,0:T(8,128)(2,1)S(1)} %constant_dynamic-update-slice_fusion.2), channel_id=1, source_target_pairs={{0,8},{4,12},{8,0},{12,4},{1,9},{5,13},{9,1},{13,5},{2,10},{6,14},... | collective-permute-start | bytes 786440 | tf_op jit(solution)/shard_map/ppermute | solution.py:100
  54.5 2.3 %collective-permute-start.13 = (bf16[128,2048]{1,0:T(8,128)(2,1)S(1)}, bf16[128,2048]{1,0:T(8,128)(2,1)S(1)}, u32[]{:S(2)}, u32[]{:S(2)}) collective-permute-start(bf16[128,2048]{1,0:T(8,128)(2,1)S(1)} %pad_maximum_fusion.1), channel_id=1, source_target_pairs={{0,4},{4,0},{8,12},{12,8},{1,5},{5,1},{9,13},{13,9},{2,6},{6,2},{1... | collective-permute-start | bytes 1572872 | tf_op jit(solution)/shard_map/ppermute | solution.py:100
  55.6 10.1 %collective-permute-start.21 = (bf16[64,2048]{1,0:T(8,128)(2,1)S(1)}, bf16[64,2048]{1,0:T(8,128)(2,1)S(1)}, u32[]{:S(2)}, u32[]{:S(2)}) collective-permute-start(bf16[64,2048]{1,0:T(8,128)(2,1)S(1)} %constant_dynamic-update-slice_fusion.4), channel_id=1, source_target_pairs={{0,8},{4,12},{8,0},{12,4},{1,9},{5,13},{9,1},{13,5},{2,10},{6,14},... | collective-permute-start | bytes 786440 | tf_op jit(solution)/shard_map/ppermute | solution.py:100
  57.8 15.5 %collective-permute-start.16 = (bf16[1,4,32,512]{3,2,1,0:T(8,128)(2,1)S(1)}, bf16[1,4,32,512]{3,2,1,0:T(8,128)(2,1)S(1)}, u32[]{:S(2)}, u32[]{:S(2)}) collective-permute-start(bf16[1,4,32,512]{3,2,1,0:T(8,128)(2,1)S(1)} %get-tuple-element.123), channel_id=1, source_target_pairs={{0,3},{1,2},{2,1},{3,0},{4,7},{5,6},{6,5},{7,4},{8,11},{9,10},{10,... | collective-permute-start | bytes 393224 | tf_op jit(solution)/shard_map/ppermute | solution.py:100
  61.7 11.5 %collective-permute-start.15 = (bf16[1,4,32,512]{3,2,1,0:T(8,128)(2,1)S(1)}, bf16[1,4,32,512]{3,2,1,0:T(8,128)(2,1)S(1)}, u32[]{:S(2)}, u32[]{:S(2)}) collective-permute-start(bf16[1,4,32,512]{3,2,1,0:T(8,128)(2,1)S(1)} %get-tuple-element.94), channel_id=1, source_target_pairs={{0,2},{1,3},{2,0},{3,1},{4,6},{5,7},{6,4},{7,5},{8,10},{9,11},{10,... | collective-permute-start | bytes 393224 | tf_op jit(solution)/shard_map/ppermute | solution.py:100
  61.8 10.7 %collective-permute-start.14 = (bf16[1,4,32,512]{3,2,1,0:T(8,128)(2,1)S(1)}, bf16[1,4,32,512]{3,2,1,0:T(8,128)(2,1)S(1)}, u32[]{:S(2)}, u32[]{:S(2)}) collective-permute-start(bf16[1,4,32,512]{3,2,1,0:T(8,128)(2,1)S(1)} %get-tuple-element.95), channel_id=1, source_target_pairs={{0,1},{1,0},{2,3},{3,2},{4,5},{5,4},{6,7},{7,6},{8,9},{9,8},{10,11... | collective-permute-start | bytes 393224 | tf_op jit(solution)/shard_map/ppermute | solution.py:100
  62.4 4.2 %collective-permute-start.18 = (bf16[128,2048]{1,0:T(8,128)(2,1)S(1)}, bf16[128,2048]{1,0:T(8,128)(2,1)S(1)}, u32[]{:S(2)}, u32[]{:S(2)}) collective-permute-start(bf16[128,2048]{1,0:T(8,128)(2,1)S(1)} %pad_maximum_fusion.2), channel_id=1, source_target_pairs={{0,4},{4,0},{8,12},{12,8},{1,5},{5,1},{9,13},{13,9},{2,6},{6,2},{1... | collective-permute-start | bytes 1572872 | tf_op jit(solution)/shard_map/ppermute | solution.py:100
  65.7 2.0 %collective-permute-start.22 = (bf16[128,2048]{1,0:T(8,128)(2,1)S(1)}, bf16[128,2048]{1,0:T(8,128)(2,1)S(1)}, u32[]{:S(2)}, u32[]{:S(2)}) collective-permute-start(bf16[128,2048]{1,0:T(8,128)(2,1)S(1)} %pad_maximum_fusion.3), channel_id=1, source_target_pairs={{0,4},{4,0},{8,12},{12,8},{1,5},{5,1},{9,13},{13,9},{2,6},{6,2},{1... | collective-permute-start | bytes 1572872 | tf_op jit(solution)/shard_map/ppermute | solution.py:100
  68.6 15.6 %collective-permute-start.25 = (bf16[1,4,32,512]{3,2,1,0:T(8,128)(2,1)S(1)}, bf16[1,4,32,512]{3,2,1,0:T(8,128)(2,1)S(1)}, u32[]{:S(2)}, u32[]{:S(2)}) collective-permute-start(bf16[1,4,32,512]{3,2,1,0:T(8,128)(2,1)S(1)} %get-tuple-element.122), channel_id=1, source_target_pairs={{0,3},{1,2},{2,1},{3,0},{4,7},{5,6},{6,5},{7,4},{8,11},{9,10},{10,... | collective-permute-start | bytes 393224 | tf_op jit(solution)/shard_map/ppermute | solution.py:100
  72.5 11.7 %collective-permute-start.24 = (bf16[1,4,32,512]{3,2,1,0:T(8,128)(2,1)S(1)}, bf16[1,4,32,512]{3,2,1,0:T(8,128)(2,1)S(1)}, u32[]{:S(2)}, u32[]{:S(2)}) collective-permute-start(bf16[1,4,32,512]{3,2,1,0:T(8,128)(2,1)S(1)} %get-tuple-element.106), channel_id=1, source_target_pairs={{0,2},{1,3},{2,0},{3,1},{4,6},{5,7},{6,4},{7,5},{8,10},{9,11},{10,... | collective-permute-start | bytes 393224 | tf_op jit(solution)/shard_map/ppermute | solution.py:100
  72.5 8.9 %collective-permute-start.23 = (bf16[1,4,32,512]{3,2,1,0:T(8,128)(2,1)S(1)}, bf16[1,4,32,512]{3,2,1,0:T(8,128)(2,1)S(1)}, u32[]{:S(2)}, u32[]{:S(2)}) collective-permute-start(bf16[1,4,32,512]{3,2,1,0:T(8,128)(2,1)S(1)} %get-tuple-element.107), channel_id=1, source_target_pairs={{0,1},{1,0},{2,3},{3,2},{4,5},{5,4},{6,7},{7,6},{8,9},{9,8},{10,11... | collective-permute-start | bytes 393224 | tf_op jit(solution)/shard_map/ppermute | solution.py:100

commit v18 on v17

--- a/solution.py
+++ b/solution.py
@@ -9,6 +9,7 @@
 damping_term = 0.05
 CHUNKS = (8, 8)
 BLOCK = 64
+FLAT = 64
 
 
 def halves(value):
@@ -84,6 +85,29 @@
     )(*pieces[::-1], basis, basis.T, in_basis, in_basis.T, corrections)
 
 
+def flatten_kernel(rows, flat, stage):
+    count, each, columns = rows.shape
+    stage[...] = rows[...].reshape(count * each, columns).astype(jnp.float32)
+    for row in range(each):
+        flat[:, row * columns:(row + 1) * columns] = stage[pl.ds(row, count, stride=each), :].astype(flat.dtype)
+
+
+def flatten(rows):
+    count, each, columns = rows.shape
+    if each % 16 or count % FLAT:
+        return rows.reshape(count, each * columns)
+    return pl.pallas_call(
+        flatten_kernel,
+        grid=(count // FLAT,),
+        in_specs=[pl.BlockSpec((FLAT, each, columns), lambda step: (step, 0, 0))],
+        out_specs=pl.BlockSpec((FLAT, each * columns), lambda step: (step, 0)),
+        out_shape=jax.ShapeDtypeStruct((count, each * columns), rows.dtype),
+        scratch_shapes=[pltpu.VMEM((FLAT * each, columns), jnp.float32)],
+        compiler_params=pltpu.CompilerParams(vmem_limit_bytes=32 * 1024 * 1024),
+        cost_estimate=pl.CostEstimate(flops=1000000000, bytes_accessed=0, transcendentals=0),
+    )(rows)
+
+
 def condition_plain(pieces, basis, in_basis, corrections):
     high = lax.Precision.HIGH
     count, rows_here, columns = pieces[0].shape
@@ -165,7 +189,7 @@
     width = rows_here * columns
     owned = shares // slices
     train_count = train_grads.shape[0]
-    train_flat = lax.optimization_barrier(train_grads.reshape(train_count, width))
+    train_flat = flatten(train_grads)
     row_blocks = out_basis.reshape(slices, rows_here, -1)
     basis = jnp.concatenate(turned([row_blocks[at] for at in range(slices)], here), axis=0)
     condition = condition_fast if rows_here % 16 == 0 else condition_plain
@@ -176,9 +200,9 @@
     for chunk, part in enumerate(parts):
         first, each = sum(parts[:chunk]), part // slices
         if chunk:
-            source, pieces[0][-1] = lax.optimization_barrier((source, pieces[0][-1]))
+            source, pieces[0][-1], train_flat = lax.optimization_barrier((source, pieces[0][-1], train_flat))
         raw = {}
-        for mask in (range(slices) if chunk else reversed(range(slices))):
+        for mask in (reversed(range(slices)) if chunk else reversed(range(slices))):
             block = lax.dynamic_slice_in_dim(source, first + (here ^ mask) * each, each, 0)
             raw[mask], source = lax.optimization_barrier((block, source))
         pieces.append(exchanged(raw, slices))
@@ -209,7 +233,7 @@
     blocks = turned([jnp.concatenate(pair, axis=1) for pair in zip(part_a1, part_a2)], place)
     blocks = in_turn(blocks)
     came = exchanged(blocks, slices)
-    group = after(last_rows[half:], far_a1)
+    group = after(last_rows[half:], near_a2)
     spread_b2 = over_shares(group, shares)
     spread_b1 = after(spread_b1, came[0])
     near_b1 = lax.optimization_barrier(jnp.concatenate(spread_b1, axis=0))

time: 85.5 us -> 92 us (1.076)
  waiting for transfers between devices: 28.9 us -> 17.1 us
  local copies, waits for them, and re-layouts: 7.08 us -> 16.1 us
  Pallas kernels: 4.46 us -> 9.48 us
  other arithmetic: 1.53 us -> 4.52 us
  starting transfers between devices: 34.3 us -> 37.2 us
  matrix products: 8.38 us -> 6.66 us
    ppermute x26, waiting for transfers between devices: 28.9 us -> 17.1 us  [crossed(): return lax.ppermute(value, axis, [(at, at ^ mask) for at in range(size)])]
    unnamed x17 -> x36, local copies, waits for them, and re-layouts: 6.02 us -> 10.5 us
    dynamic_slice x8, local copies, waits for them, and re-layouts: 0.12 us -> 4.01 us  [body(): lax.dynamic_slice_in_dim(source, first + (here ^ mask) * each, each, 0)]
    pallas_call x2, Pallas kernels: 4.46 us -> 7.77 us  [condition_fast(): pl.pallas_call(functools.partial(condition_kernel, slices, rows_here), gr...]
    ppermute x26, starting transfers between devices: 34.3 us -> 37.2 us  [crossed(): return lax.ppermute(value, axis, [(at, at ^ mask) for at in range(size)])]
    dot_general x8, matrix products: 8.38 us -> 6.66 us  [products(): lax.dot_general(block, train_flat, contract, preferred_element_type=jnp.f...]
    pallas_call x0 -> x1, Pallas kernels: none -> 1.71 us  [flatten(): pl.pallas_call(flatten_kernel, grid=(count // FLAT,), in_specs=[pl.BlockS...]
    concatenate x1, other arithmetic: 0.03 us -> 1.07 us  [body(): near_a1 = lax.optimization_barrier(jnp.concatenate(spread_a1, axis=0))]
  transfers between devices with their start and end apart: 26 -> 26, of which waited for: 8 -> 8; matrix products, arithmetic and copies ran while one was open for 17% -> 19% of each run, Pallas kernels for 5% -> 10%
where the time goes in v18:
time: 92 us; the launch traced here: 91.5 us
  starting transfers between devices  37.2 us (40%)
  waiting for transfers between devices  17.1 us (19%)
  local copies, waits for them, and re-layouts  16.1 us (18%)
  Pallas kernels  9.48 us (10%)
  matrix products  6.66 us (7%)
  other arithmetic  4.52 us (5%)
    ppermute x26, starting transfers between devices, crossed(): return lax.ppermute(value, axis, [(at, at ^ mask) for at in range(size)])  37.2 us
    ppermute x26, waiting for transfers between devices, crossed(): return lax.ppermute(value, axis, [(at, at ^ mask) for at in range(size)])  17.1 us
    unnamed x36, local copies, waits for them, and re-layouts  10.5 us
    pallas_call x2, Pallas kernels, condition_fast(): pl.pallas_call(functools.partial(condition_kernel, slices, rows_here), gr...  7.77 us
    dot_general x8, matrix products, products(): lax.dot_general(block, train_flat, contract, preferred_element_type=jnp.f...  6.66 us
    dynamic_slice x8, local copies, waits for them, and re-layouts, body(): lax.dynamic_slice_in_dim(source, first + (here ^ mask) * each, each, 0)  4.01 us
  transfers between devices with their start and end apart: 26, of which 8 were waited for; matrix products, arithmetic and copies ran while one was open for 19% of the time, Pallas kernels for 10%

profile of v18, /device:TPU:0, one launch (start us, length us, event | category | flops | bytes accessed | tf_op | source)
XLA Modules:
  0.0 91.5 jit_solution(15797802871684404592)
XLA Ops:
  0.0 1.2 %copy-done = bf16[256,16,128]{2,1,0:T(8,128)(2,1)S(1)} copy-done((bf16[256,16,128]{2,1,0:T(8,128)(2,1)S(1)}, bf16[256,16,128]{2,1,0:T(8,128)(2,1)}, u32[]{:S(2)}) %copy-start) | copy-done | bytes 1048600
  1.2 0.7 constant_dynamic-slice_fusion.7
  1.9 5.0 %collective-permute-start = (bf16[32,16,128]{2,1,0:T(8,128)(2,1)}, bf16[32,16,128]{2,1,0:T(8,128)(2,1)S(1)}, u32[]{:S(2)}, u32[]{:S(2)}) collective-permute-start(bf16[32,16,128]{2,1,0:T(8,128)(2,1)} %constant_dynamic-slice_fusion.7), channel_id=1, source_target_pairs={{0,3},{1,2},{2,1},{3,0},{4,7},{5,6},{6,5},{7,4},{8,11},{9,10},{10,... | collective-permute-start | bytes 393224 | tf_op jit(solution)/shard_map/ppermute | solution.py:124
  6.9 0.7 constant_dynamic-slice_fusion.6
  7.6 0.7 constant_dynamic-slice_fusion.5
  8.3 0.6 collective-permute-start.1
  8.8 0.7 fusion.8
  9.6 0.1 copy.13
  9.7 0.1 copy.14
  9.7 0.1 copy.15
  9.9 0.1 pad_maximum_fusion.15
  10.1 1.6 %copy.10 = f32[128,128]{0,1:T(8,128)} copy(f32[128,128]{1,0:T(8,128)} %refs_6_.3) | data formatting | bytes 131072 | tf_op args[3]
  11.7 1.6 %copy-done.1 = bf16[512,16,128]{2,1,0:T(8,128)(2,1)S(1)} copy-done((bf16[512,16,128]{2,1,0:T(8,128)(2,1)S(1)}, bf16[512,16,128]{2,1,0:T(8,128)(2,1)}, u32[]{:S(2)}) %copy-start.1) | copy-done | bytes 2097176
  13.3 1.7 %shard_map.55 = bf16[512,2048]{1,0:T(8,128)(2,1)S(1)} custom-call(bf16[512,16,128]{2,1,0:T(8,128)(2,1)S(1)} %copy-done.1), custom_call_target="tpu_custom_call" | custom-call | flops 1000000000 | tf_op jit(solution)/shard_map/pallas_call | solution.py:99
  15.1 0.7 constant_dynamic-slice_fusion.3
  15.7 0.7 constant_dynamic-slice_fusion.2
  16.4 0.7 constant_dynamic-slice_fusion.1
  17.1 1.5 %collective-permute-start.4 = (bf16[32,16,128]{2,1,0:T(8,128)(2,1)}, bf16[32,16,128]{2,1,0:T(8,128)(2,1)}, u32[]{:S(2)}, u32[]{:S(2)}) collective-permute-start(bf16[32,16,128]{2,1,0:T(8,128)(2,1)} %constant_dynamic-slice_fusion.1), channel_id=1, source_target_pairs={{0,1},{1,0},{2,3},{3,2},{4,5},{5,4},{6,7},{7,6},{8,9},{9,8},{10,11... | collective-permute-start | bytes 393224 | tf_op jit(solution)/shard_map/ppermute | solution.py:124
  18.5 2.9 %collective-permute-start.5 = (bf16[32,16,128]{2,1,0:T(8,128)(2,1)}, bf16[32,16,128]{2,1,0:T(8,128)(2,1)}, u32[]{:S(2)}, u32[]{:S(2)}) collective-permute-start(bf16[32,16,128]{2,1,0:T(8,128)(2,1)} %constant_dynamic-slice_fusion.2), channel_id=1, source_target_pairs={{0,2},{1,3},{2,0},{3,1},{4,6},{5,7},{6,4},{7,5},{8,10},{9,11},{10,... | collective-permute-start | bytes 393224 | tf_op jit(solution)/shard_map/ppermute | solution.py:124
  21.5 0.9 copy-done.6
  22.4 3.8 %shard_map.56 = (bf16[32,2048]{1,0:T(8,128)(2,1)S(1)}, bf16[32,2048]{1,0:T(8,128)(2,1)}, bf16[32,2048]{1,0:T(8,128)(2,1)S(1)}, bf16[32,2048]{1,0:T(8,128)(2,1)S(1)}) custom-call(bf16[32,16,128]{2,1,0:T(8,128)(2,1)S(1)} %copy-done.6, bf16[32,16,128]{2,1,0:T(8,128)(2,1)} %collective-permute-done.1.refs_1_, ...), custom_call_target="tpu_custom_call" | custom-call | flops 1000000000 | tf_op jit(solution)/shard_map/pallas_call | solution.py:76
  26.2 0.6 copy-done.7
  26.9 0.7 copy-done.9
  27.5 0.5 collective-permute-start.3
  28.1 3.9 %collective-permute-start.7 = (bf16[32,2048]{1,0:T(8,128)(2,1)}, bf16[32,2048]{1,0:T(8,128)(2,1)}, u32[]{:S(2)}, u32[]{:S(2)}) collective-permute-start(bf16[32,2048]{1,0:T(8,128)(2,1)} %copy-done.9), channel_id=1, source_target_pairs={{0,2},{1,3},{2,0},{3,1},{4,6},{5,7},{6,4},{7,5},{8,10},{9,11},{10,... | collective-permute-start | bytes 393224 | tf_op jit(solution)/shard_map/ppermute | solution.py:124
  32.0 1.6 %collective-permute-done.3 = bf16[32,2048]{1,0:T(8,128)(2,1)S(1)} collective-permute-done((bf16[32,2048]{1,0:T(8,128)(2,1)}, bf16[32,2048]{1,0:T(8,128)(2,1)S(1)}, u32[]{:S(2)}, u32[]{:S(2)}) %collective-permute-start.3) | collective-permute-done | bytes 131104 | tf_op jit(solution)/shard_map/ppermute | solution.py:124
  33.6 0.6 copy-done.12
  34.2 0.7 constant_dynamic-update-slice_fusion.1
  34.9 0.8 copy-done.4
  35.7 0.8 copy-done.11
  36.5 3.9 %shard_map.57 = (bf16[32,2048]{1,0:T(8,128)(2,1)S(1)}, bf16[32,2048]{1,0:T(8,128)(2,1)}, bf16[32,2048]{1,0:T(8,128)(2,1)S(1)}, bf16[32,2048]{1,0:T(8,128)(2,1)S(1)}) custom-call(bf16[32,16,128]{2,1,0:T(8,128)(2,1)} %collective-permute-done.6.refs_0_, bf16[32,16,128]{2,1,0:T(8,128)(2,1)} %collective-permute-done.5.refs_1_, ...), custom_call_target="tpu_custom_call" | custom-call | flops 1000000000 | tf_op jit(solution)/shard_map/pallas_call | solution.py:76
  40.4 0.7 copy-done.8
  41.1 6.6 %collective-permute-start.9 = (bf16[32,2048]{1,0:T(8,128)(2,1)}, bf16[32,2048]{1,0:T(8,128)(2,1)S(1)}, u32[]{:S(2)}, u32[]{:S(2)}) collective-permute-start(bf16[32,2048]{1,0:T(8,128)(2,1)} %get-tuple-element.84), channel_id=1, source_target_pairs={{0,1},{1,0},{2,3},{3,2},{4,5},{5,4},{6,7},{7,6},{8,9},{9,8},{10,11... | collective-permute-start | bytes 393224 | tf_op jit(solution)/shard_map/ppermute | solution.py:124
  47.7 0.7 constant_dynamic-update-slice_fusion
  48.4 1.5 %collective-permute-start.10 = (bf16[64,2048]{1,0:T(8,128)(2,1)}, bf16[64,2048]{1,0:T(8,128)(2,1)}, u32[]{:S(2)}, u32[]{:S(2)}) collective-permute-start(bf16[64,2048]{1,0:T(8,128)(2,1)} %constant_dynamic-update-slice_fusion), channel_id=1, source_target_pairs={{0,8},{4,12},{8,0},{12,4},{1,9},{5,13},{9,1},{13,5},{2,10},{6,14},... | collective-permute-start | bytes 786440 | tf_op jit(solution)/shard_map/ppermute | solution.py:124
  49.8 1.2 %collective-permute-start.19 = (bf16[32,2048]{1,0:T(8,128)(2,1)}, bf16[32,2048]{1,0:T(8,128)(2,1)S(1)}, u32[]{:S(2)}, u32[]{:S(2)}) collective-permute-start(bf16[32,2048]{1,0:T(8,128)(2,1)} %copy-done.8), channel_id=1, source_target_pairs={{0,2},{1,3},{2,0},{3,1},{4,6},{5,7},{6,4},{7,5},{8,10},{9,11},{10,... | collective-permute-start | bytes 393224 | tf_op jit(solution)/shard_map/ppermute | solution.py:124
  51.0 1.5 %collective-permute-start.20 = (bf16[32,2048]{1,0:T(8,128)(2,1)S(1)}, bf16[32,2048]{1,0:T(8,128)(2,1)S(1)}, u32[]{:S(2)}, u32[]{:S(2)}) collective-permute-start(bf16[32,2048]{1,0:T(8,128)(2,1)S(1)} %get-tuple-element.103), channel_id=1, source_target_pairs={{0,3},{1,2},{2,1},{3,0},{4,7},{5,6},{6,5},{7,4},{8,11},{9,10},{10,... | collective-permute-start | bytes 393224 | tf_op jit(solution)/shard_map/ppermute | solution.py:124
  52.5 1.0 %pad_maximum_fusion.4 = bf16[64,2048]{1,0:T(8,128)(2,1)S(1)} fusion(bf16[32,2048]{1,0:T(8,128)(2,1)} %collective-permute-done.8, bf16[32,2048]{1,0:T(8,128)(2,1)} %collective-permute-done.7), kind=kLoop, calls=%fused_computation.13 | loop fusion | flops 524288 | bytes 524288 | tf_op jit(solution)/shard_map/concatenate | solution.py:156
  53.4 0.6 collective-permute-start.12
  54.0 1.0 %collective-permute-done.10 = bf16[64,2048]{1,0:T(8,128)(2,1)} collective-permute-done((bf16[64,2048]{1,0:T(8,128)(2,1)}, bf16[64,2048]{1,0:T(8,128)(2,1)}, u32[]{:S(2)}, u32[]{:S(2)}) %collective-permute-start.10) | collective-permute-done | bytes 262176 | tf_op jit(solution)/shard_map/ppermute | solution.py:124
  55.0 1.1 %pad_maximum_fusion = bf16[128,2048]{1,0:T(8,128)(2,1)S(1)} fusion(bf16[64,2048]{1,0:T(8,128)(2,1)} %collective-permute-done.10, bf16[64,2048]{1,0:T(8,128)(2,1)} %constant_dynamic-update-slice_fusion), kind=kLoop, calls=%fused_computation.8 | loop fusion | flops 1048576 | bytes 1048576 | tf_op jit(solution)/shard_map/concatenate | solution.py:220
  56.2 0.8 convolution_convert_fusion.5
  57.1 1.5 %collective-permute-start.17 = (bf16[64,2048]{1,0:T(8,128)(2,1)S(1)}, bf16[64,2048]{1,0:T(8,128)(2,1)S(1)}, u32[]{:S(2)}, u32[]{:S(2)}) collective-permute-start(bf16[64,2048]{1,0:T(8,128)(2,1)S(1)} %constant_dynamic-update-slice_fusion.2), channel_id=1, source_target_pairs={{0,8},{4,12},{8,0},{12,4},{1,9},{5,13},{9,1},{13,5},{2,10},{6,14},... | collective-permute-start | bytes 786440 | tf_op jit(solution)/shard_map/ppermute | solution.py:124
  58.6 1.3 %collective-permute-done.12 = bf16[64,2048]{1,0:T(8,128)(2,1)S(1)} collective-permute-done((bf16[64,2048]{1,0:T(8,128)(2,1)S(1)}, bf16[64,2048]{1,0:T(8,128)(2,1)S(1)}, u32[]{:S(2)}, u32[]{:S(2)}) %collective-permute-start.12) | collective-permute-done | bytes 262176 | tf_op jit(solution)/shard_map/ppermute | solution.py:124
  59.9 1.0 %pad_maximum_fusion.1 = bf16[128,2048]{1,0:T(8,128)(2,1)S(1)} fusion(bf16[64,2048]{1,0:T(8,128)(2,1)S(1)} %collective-permute-done.12, bf16[32,2048]{1,0:T(8,128)(2,1)} %collective-permute-done.8, bf16[32,2048]{1,0:T(8,128)(2,1)} %collective-permute-done.7), kind=kLoop, calls=%fused_computation.9 | loop fusion | flops 1572864 | bytes 1048576 | tf_op jit(solution)/shard_map/concatenate | solution.py:224
  61.0 0.8 convolution_convert_fusion.4
  61.9 0.6 collective-permute-start.21
  62.5 0.8 convolution_convert_fusion.7
  63.4 0.8 convolution_convert_fusion.6
  64.3 2.4 %collective-permute-start.16 = (bf16[1,4,32,512]{3,2,1,0:T(8,128)(2,1)S(1)}, bf16[1,4,32,512]{3,2,1,0:T(8,128)(2,1)S(1)}, u32[]{:S(2)}, u32[]{:S(2)}) collective-permute-start(bf16[1,4,32,512]{3,2,1,0:T(8,128)(2,1)S(1)} %get-tuple-element.125), channel_id=1, source_target_pairs={{0,3},{1,2},{2,1},{3,0},{4,7},{5,6},{6,5},{7,4},{8,11},{9,10},{10,... | collective-permute-start | bytes 393224 | tf_op jit(solution)/shard_map/ppermute | solution.py:124
  66.7 0.5 collective-permute-start.15
  67.3 1.6 %collective-permute-start.14 = (bf16[1,4,32,512]{3,2,1,0:T(8,128)(2,1)S(1)}, bf16[1,4,32,512]{3,2,1,0:T(8,128)(2,1)S(1)}, u32[]{:S(2)}, u32[]{:S(2)}) collective-permute-start(bf16[1,4,32,512]{3,2,1,0:T(8,128)(2,1)S(1)} %get-tuple-element.97), channel_id=1, source_target_pairs={{0,1},{1,0},{2,3},{3,2},{4,5},{5,4},{6,7},{7,6},{8,9},{9,8},{10,11... | collective-permute-start | bytes 393224 | tf_op jit(solution)/shard_map/ppermute | solution.py:124
  69.0 0.8 convolution_convert_fusion.1
  69.8 1.7 %collective-permute-done.21 = bf16[64,2048]{1,0:T(8,128)(2,1)S(1)} collective-permute-done((bf16[64,2048]{1,0:T(8,128)(2,1)S(1)}, bf16[64,2048]{1,0:T(8,128)(2,1)S(1)}, u32[]{:S(2)}, u32[]{:S(2)}) %collective-permute-start.21) | collective-permute-done | bytes 262176 | tf_op jit(solution)/shard_map/ppermute | solution.py:124
  71.6 0.8 convolution_convert_fusion
  72.5 0.8 convolution_convert_fusion.3
  73.3 0.2 collective-permute-done.22
  73.5 0.8 convolution_convert_fusion.2
  74.4 2.7 %collective-permute-start.25 = (bf16[1,4,32,512]{3,2,1,0:T(8,128)(2,1)S(1)}, bf16[1,4,32,512]{3,2,1,0:T(8,128)(2,1)S(1)}, u32[]{:S(2)}, u32[]{:S(2)}) collective-permute-start(bf16[1,4,32,512]{3,2,1,0:T(8,128)(2,1)S(1)} %get-tuple-element.124), channel_id=1, source_target_pairs={{0,3},{1,2},{2,1},{3,0},{4,7},{5,6},{6,5},{7,4},{8,11},{9,10},{10,... | collective-permute-start | bytes 393224 | tf_op jit(solution)/shard_map/ppermute | solution.py:124
  77.1 1.9 %collective-permute-start.23 = (bf16[1,4,32,512]{3,2,1,0:T(8,128)(2,1)S(1)}, bf16[1,4,32,512]{3,2,1,0:T(8,128)(2,1)S(1)}, u32[]{:S(2)}, u32[]{:S(2)}) collective-permute-start(bf16[1,4,32,512]{3,2,1,0:T(8,128)(2,1)S(1)} %get-tuple-element.109), channel_id=1, source_target_pairs={{0,1},{1,0},{2,3},{3,2},{4,5},{5,4},{6,7},{7,6},{8,9},{9,8},{10,11... | collective-permute-start | bytes 393224 | tf_op jit(solution)/shard_map/ppermute | solution.py:124
  79.0 6.5 %collective-permute-done.15 = bf16[1,4,32,512]{3,2,1,0:T(8,128)(2,1)S(1)} collective-permute-done((bf16[1,4,32,512]{3,2,1,0:T(8,128)(2,1)S(1)}, bf16[1,4,32,512]{3,2,1,0:T(8,128)(2,1)S(1)}, u32[]{:S(2)}, u32[]{:S(2)}) %collective-permute-start.15) | collective-permute-done | bytes 131104 | tf_op jit(solution)/shard_map/ppermute | solution.py:124
  85.6 0.4 collective-permute-done.23
  86.0 4.4 %collective-permute-done.24 = bf16[1,4,32,512]{3,2,1,0:T(8,128)(2,1)S(1)} collective-permute-done((bf16[1,4,32,512]{3,2,1,0:T(8,128)(2,1)S(1)}, bf16[1,4,32,512]{3,2,1,0:T(8,128)(2,1)S(1)}, u32[]{:S(2)}, u32[]{:S(2)}) %collective-permute-start.24) | collective-permute-done | bytes 131104 | tf_op jit(solution)/shard_map/ppermute | solution.py:124
  90.6 0.8 maximum_bitcast_fusion
  (73 shorter events, 1.2 us)
Async XLA Ops:
  0.0 1.2 %copy-start = (bf16[256,16,128]{2,1,0:T(8,128)(2,1)S(1)}, bf16[256,16,128]{2,1,0:T(8,128)(2,1)}, u32[]{:S(2)}) copy-start(bf16[256,16,128]{2,1,0:T(8,128)(2,1)} %param.5) | copy-start | bytes 3145732
  1.9 13.1 %collective-permute-start = (bf16[32,16,128]{2,1,0:T(8,128)(2,1)}, bf16[32,16,128]{2,1,0:T(8,128)(2,1)S(1)}, u32[]{:S(2)}, u32[]{:S(2)}) collective-permute-start(bf16[32,16,128]{2,1,0:T(8,128)(2,1)} %constant_dynamic-slice_fusion.7), channel_id=1, source_target_pairs={{0,3},{1,2},{2,1},{3,0},{4,7},{5,6},{6,5},{7,4},{8,11},{9,10},{10,... | collective-permute-start | bytes 393224 | tf_op jit(solution)/shard_map/ppermute | solution.py:124
  8.3 13.2 %collective-permute-start.2 = (bf16[32,16,128]{2,1,0:T(8,128)(2,1)}, bf16[32,16,128]{2,1,0:T(8,128)(2,1)}, u32[]{:S(2)}, u32[]{:S(2)}) collective-permute-start(bf16[32,16,128]{2,1,0:T(8,128)(2,1)} %constant_dynamic-slice_fusion.5), channel_id=1, source_target_pairs={{0,1},{1,0},{2,3},{3,2},{4,5},{5,4},{6,7},{7,6},{8,9},{9,8},{10,11... | collective-permute-start | bytes 393224 | tf_op jit(solution)/shard_map/ppermute | solution.py:124
  8.3 13.2 %collective-permute-start.1 = (bf16[32,16,128]{2,1,0:T(8,128)(2,1)}, bf16[32,16,128]{2,1,0:T(8,128)(2,1)}, u32[]{:S(2)}, u32[]{:S(2)}) collective-permute-start(bf16[32,16,128]{2,1,0:T(8,128)(2,1)} %constant_dynamic-slice_fusion.6), channel_id=1, source_target_pairs={{0,2},{1,3},{2,0},{3,1},{4,6},{5,7},{6,4},{7,5},{8,10},{9,11},{10,... | collective-permute-start | bytes 393224 | tf_op jit(solution)/shard_map/ppermute | solution.py:124
  11.7 1.6 %copy-start.1 = (bf16[512,16,128]{2,1,0:T(8,128)(2,1)S(1)}, bf16[512,16,128]{2,1,0:T(8,128)(2,1)}, u32[]{:S(2)}) copy-start(bf16[512,16,128]{2,1,0:T(8,128)(2,1)} %rows.1) | copy-start | bytes 6291460
  13.3 8.2 %copy-start.2 = (f32[128,128]{1,0:T(8,128)S(1)}, f32[128,128]{1,0:T(8,128)}, u32[]{:S(2)}) copy-start(f32[128,128]{1,0:T(8,128)} %refs_6_.3) | copy-start | bytes 196612
  13.3 8.2 %copy-start.3 = (f32[128,128]{0,1:T(8,128)S(1)}, f32[128,128]{0,1:T(8,128)}, u32[]{:S(2)}) copy-start(f32[128,128]{0,1:T(8,128)} %copy.10) | copy-start | bytes 196612
  13.3 8.2 %copy-start.10 = (f32[64,128]{1,0:T(8,128)S(1)}, f32[64,128]{1,0:T(8,128)}, u32[]{:S(2)}) copy-start(f32[64,128]{1,0:T(8,128)} %refs_8_.3) | copy-start | bytes 98308
  15.0 6.4 %copy-start.5 = (bf16[32,16,128]{2,1,0:T(8,128)(2,1)}, bf16[32,16,128]{2,1,0:T(8,128)(2,1)S(1)}, u32[]{:S(2)}) copy-start(bf16[32,16,128]{2,1,0:T(8,128)(2,1)S(1)} %collective-permute-done.refs_0_) | copy-start | bytes 393220
  17.1 14.9 %collective-permute-start.4 = (bf16[32,16,128]{2,1,0:T(8,128)(2,1)}, bf16[32,16,128]{2,1,0:T(8,128)(2,1)}, u32[]{:S(2)}, u32[]{:S(2)}) collective-permute-start(bf16[32,16,128]{2,1,0:T(8,128)(2,1)} %constant_dynamic-slice_fusion.1), channel_id=1, source_target_pairs={{0,1},{1,0},{2,3},{3,2},{4,5},{5,4},{6,7},{7,6},{8,9},{9,8},{10,11... | collective-permute-start | bytes 393224 | tf_op jit(solution)/shard_map/ppermute | solution.py:124
  18.5 13.5 %collective-permute-start.5 = (bf16[32,16,128]{2,1,0:T(8,128)(2,1)}, bf16[32,16,128]{2,1,0:T(8,128)(2,1)}, u32[]{:S(2)}, u32[]{:S(2)}) collective-permute-start(bf16[32,16,128]{2,1,0:T(8,128)(2,1)} %constant_dynamic-slice_fusion.2), channel_id=1, source_target_pairs={{0,2},{1,3},{2,0},{3,1},{4,6},{5,7},{6,4},{7,5},{8,10},{9,11},{10,... | collective-permute-start | bytes 393224 | tf_op jit(solution)/shard_map/ppermute | solution.py:124
  21.4 10.6 %collective-permute-start.6 = (bf16[32,16,128]{2,1,0:T(8,128)(2,1)}, bf16[32,16,128]{2,1,0:T(8,128)(2,1)}, u32[]{:S(2)}, u32[]{:S(2)}) collective-permute-start(bf16[32,16,128]{2,1,0:T(8,128)(2,1)} %constant_dynamic-slice_fusion.3), channel_id=1, source_target_pairs={{0,3},{1,2},{2,1},{3,0},{4,7},{5,6},{6,5},{7,4},{8,11},{9,10},{10,... | collective-permute-start | bytes 393224 | tf_op jit(solution)/shard_map/ppermute | solution.py:124
  21.5 0.9 copy-start.6
  26.2 0.6 copy-start.7
  26.9 0.7 copy-start.9
  27.5 6.0 %collective-permute-start.3 = (bf16[32,2048]{1,0:T(8,128)(2,1)}, bf16[32,2048]{1,0:T(8,128)(2,1)S(1)}, u32[]{:S(2)}, u32[]{:S(2)}) collective-permute-start(bf16[32,2048]{1,0:T(8,128)(2,1)} %get-tuple-element.68), channel_id=1, source_target_pairs={{0,1},{1,0},{2,3},{3,2},{4,5},{5,4},{6,7},{7,6},{8,9},{9,8},{10,11... | collective-permute-start | bytes 393224 | tf_op jit(solution)/shard_map/ppermute | solution.py:124
  28.1 22.9 %collective-permute-start.7 = (bf16[32,2048]{1,0:T(8,128)(2,1)}, bf16[32,2048]{1,0:T(8,128)(2,1)}, u32[]{:S(2)}, u32[]{:S(2)}) collective-permute-start(bf16[32,2048]{1,0:T(8,128)(2,1)} %copy-done.9), channel_id=1, source_target_pairs={{0,2},{1,3},{2,0},{3,1},{4,6},{5,7},{6,4},{7,5},{8,10},{9,11},{10,... | collective-permute-start | bytes 393224 | tf_op jit(solution)/shard_map/ppermute | solution.py:124
  32.0 20.5 %collective-permute-start.8 = (bf16[32,2048]{1,0:T(8,128)(2,1)}, bf16[32,2048]{1,0:T(8,128)(2,1)}, u32[]{:S(2)}, u32[]{:S(2)}) collective-permute-start(bf16[32,2048]{1,0:T(8,128)(2,1)} %copy-done.7), channel_id=1, source_target_pairs={{0,3},{1,2},{2,1},{3,0},{4,7},{5,6},{6,5},{7,4},{8,11},{9,10},{10,... | collective-permute-start | bytes 393224 | tf_op jit(solution)/shard_map/ppermute | solution.py:124
  33.6 0.6 copy-start.12
  34.9 0.8 copy-start.4
  35.7 0.8 copy-start.11
  36.5 11.2 %copy-start.13 = (bf16[32,2048]{1,0:T(8,128)(2,1)S(1)}, bf16[32,2048]{1,0:T(8,128)(2,1)}, u32[]{:S(2)}) copy-start(bf16[32,2048]{1,0:T(8,128)(2,1)} %copy-done.12) | copy-start | bytes 393220
  40.4 0.7 copy-start.8
  41.1 11.4 %collective-permute-start.9 = (bf16[32,2048]{1,0:T(8,128)(2,1)}, bf16[32,2048]{1,0:T(8,128)(2,1)S(1)}, u32[]{:S(2)}, u32[]{:S(2)}) collective-permute-start(bf16[32,2048]{1,0:T(8,128)(2,1)} %get-tuple-element.84), channel_id=1, source_target_pairs={{0,1},{1,0},{2,3},{3,2},{4,5},{5,4},{6,7},{7,6},{8,9},{9,8},{10,11... | collective-permute-start | bytes 393224 | tf_op jit(solution)/shard_map/ppermute | solution.py:124
  48.4 6.7 %collective-permute-start.10 = (bf16[64,2048]{1,0:T(8,128)(2,1)}, bf16[64,2048]{1,0:T(8,128)(2,1)}, u32[]{:S(2)}, u32[]{:S(2)}) collective-permute-start(bf16[64,2048]{1,0:T(8,128)(2,1)} %constant_dynamic-update-slice_fusion), channel_id=1, source_target_pairs={{0,8},{4,12},{8,0},{12,4},{1,9},{5,13},{9,1},{13,5},{2,10},{6,14},... | collective-permute-start | bytes 786440 | tf_op jit(solution)/shard_map/ppermute | solution.py:124
  49.8 12.0 %collective-permute-start.19 = (bf16[32,2048]{1,0:T(8,128)(2,1)}, bf16[32,2048]{1,0:T(8,128)(2,1)S(1)}, u32[]{:S(2)}, u32[]{:S(2)}) collective-permute-start(bf16[32,2048]{1,0:T(8,128)(2,1)} %copy-done.8), channel_id=1, source_target_pairs={{0,2},{1,3},{2,0},{3,1},{4,6},{5,7},{6,4},{7,5},{8,10},{9,11},{10,... | collective-permute-start | bytes 393224 | tf_op jit(solution)/shard_map/ppermute | solution.py:124
  51.0 10.8 %collective-permute-start.20 = (bf16[32,2048]{1,0:T(8,128)(2,1)S(1)}, bf16[32,2048]{1,0:T(8,128)(2,1)S(1)}, u32[]{:S(2)}, u32[]{:S(2)}) collective-permute-start(bf16[32,2048]{1,0:T(8,128)(2,1)S(1)} %get-tuple-element.103), channel_id=1, source_target_pairs={{0,3},{1,2},{2,1},{3,0},{4,7},{5,6},{6,5},{7,4},{8,11},{9,10},{10,... | collective-permute-start | bytes 393224 | tf_op jit(solution)/shard_map/ppermute | solution.py:124
  53.4 6.4 %collective-permute-start.12 = (bf16[64,2048]{1,0:T(8,128)(2,1)S(1)}, bf16[64,2048]{1,0:T(8,128)(2,1)S(1)}, u32[]{:S(2)}, u32[]{:S(2)}) collective-permute-start(bf16[64,2048]{1,0:T(8,128)(2,1)S(1)} %pad_maximum_fusion.4), channel_id=1, source_target_pairs={{0,8},{4,12},{8,0},{12,4},{1,9},{5,13},{9,1},{13,5},{2,10},{6,14},... | collective-permute-start | bytes 786440 | tf_op jit(solution)/shard_map/ppermute | solution.py:124
  56.1 6.4 %collective-permute-start.11 = (bf16[128,2048]{1,0:T(8,128)(2,1)S(1)}, bf16[128,2048]{1,0:T(8,128)(2,1)S(1)}, u32[]{:S(2)}, u32[]{:S(2)}) collective-permute-start(bf16[128,2048]{1,0:T(8,128)(2,1)S(1)} %pad_maximum_fusion), channel_id=1, source_target_pairs={{0,4},{4,0},{8,12},{12,8},{1,5},{5,1},{9,13},{13,9},{2,6},{6,2},{1... | collective-permute-start | bytes 1572872 | tf_op jit(solution)/shard_map/ppermute | solution.py:124
  57.1 11.8 %collective-permute-start.17 = (bf16[64,2048]{1,0:T(8,128)(2,1)S(1)}, bf16[64,2048]{1,0:T(8,128)(2,1)S(1)}, u32[]{:S(2)}, u32[]{:S(2)}) collective-permute-start(bf16[64,2048]{1,0:T(8,128)(2,1)S(1)} %constant_dynamic-update-slice_fusion.2), channel_id=1, source_target_pairs={{0,8},{4,12},{8,0},{12,4},{1,9},{5,13},{9,1},{13,5},{2,10},{6,14},... | collective-permute-start | bytes 786440 | tf_op jit(solution)/shard_map/ppermute | solution.py:124
  60.9 2.5 %collective-permute-start.13 = (bf16[128,2048]{1,0:T(8,128)(2,1)S(1)}, bf16[128,2048]{1,0:T(8,128)(2,1)S(1)}, u32[]{:S(2)}, u32[]{:S(2)}) collective-permute-start(bf16[128,2048]{1,0:T(8,128)(2,1)S(1)} %pad_maximum_fusion.1), channel_id=1, source_target_pairs={{0,4},{4,0},{8,12},{12,8},{1,5},{5,1},{9,13},{13,9},{2,6},{6,2},{1... | collective-permute-start | bytes 1572872 | tf_op jit(solution)/shard_map/ppermute | solution.py:124
  61.9 9.6 %collective-permute-start.21 = (bf16[64,2048]{1,0:T(8,128)(2,1)S(1)}, bf16[64,2048]{1,0:T(8,128)(2,1)S(1)}, u32[]{:S(2)}, u32[]{:S(2)}) collective-permute-start(bf16[64,2048]{1,0:T(8,128)(2,1)S(1)} %constant_dynamic-update-slice_fusion.4), channel_id=1, source_target_pairs={{0,8},{4,12},{8,0},{12,4},{1,9},{5,13},{9,1},{13,5},{2,10},{6,14},... | collective-permute-start | bytes 786440 | tf_op jit(solution)/shard_map/ppermute | solution.py:124
  64.3 21.3 %collective-permute-start.16 = (bf16[1,4,32,512]{3,2,1,0:T(8,128)(2,1)S(1)}, bf16[1,4,32,512]{3,2,1,0:T(8,128)(2,1)S(1)}, u32[]{:S(2)}, u32[]{:S(2)}) collective-permute-start(bf16[1,4,32,512]{3,2,1,0:T(8,128)(2,1)S(1)} %get-tuple-element.125), channel_id=1, source_target_pairs={{0,3},{1,2},{2,1},{3,0},{4,7},{5,6},{6,5},{7,4},{8,11},{9,10},{10,... | collective-permute-start | bytes 393224 | tf_op jit(solution)/shard_map/ppermute | solution.py:124
  66.7 18.8 %collective-permute-start.15 = (bf16[1,4,32,512]{3,2,1,0:T(8,128)(2,1)S(1)}, bf16[1,4,32,512]{3,2,1,0:T(8,128)(2,1)S(1)}, u32[]{:S(2)}, u32[]{:S(2)}) collective-permute-start(bf16[1,4,32,512]{3,2,1,0:T(8,128)(2,1)S(1)} %get-tuple-element.96), channel_id=1, source_target_pairs={{0,2},{1,3},{2,0},{3,1},{4,6},{5,7},{6,4},{7,5},{8,10},{9,11},{10,... | collective-permute-start | bytes 393224 | tf_op jit(solution)/shard_map/ppermute | solution.py:124
  67.3 9.8 %collective-permute-start.14 = (bf16[1,4,32,512]{3,2,1,0:T(8,128)(2,1)S(1)}, bf16[1,4,32,512]{3,2,1,0:T(8,128)(2,1)S(1)}, u32[]{:S(2)}, u32[]{:S(2)}) collective-permute-start(bf16[1,4,32,512]{3,2,1,0:T(8,128)(2,1)S(1)} %get-tuple-element.97), channel_id=1, source_target_pairs={{0,1},{1,0},{2,3},{3,2},{4,5},{5,4},{6,7},{7,6},{8,9},{9,8},{10,11... | collective-permute-start | bytes 393224 | tf_op jit(solution)/shard_map/ppermute | solution.py:124
  68.9 3.6 %collective-permute-start.18 = (bf16[128,2048]{1,0:T(8,128)(2,1)S(1)}, bf16[128,2048]{1,0:T(8,128)(2,1)S(1)}, u32[]{:S(2)}, u32[]{:S(2)}) collective-permute-start(bf16[128,2048]{1,0:T(8,128)(2,1)S(1)} %pad_maximum_fusion.2), channel_id=1, source_target_pairs={{0,4},{4,0},{8,12},{12,8},{1,5},{5,1},{9,13},{13,9},{2,6},{6,2},{1... | collective-permute-start | bytes 1572872 | tf_op jit(solution)/shard_map/ppermute | solution.py:124
  71.5 2.0 %collective-permute-start.22 = (bf16[128,2048]{1,0:T(8,128)(2,1)S(1)}, bf16[128,2048]{1,0:T(8,128)(2,1)S(1)}, u32[]{:S(2)}, u32[]{:S(2)}) collective-permute-start(bf16[128,2048]{1,0:T(8,128)(2,1)S(1)} %pad_maximum_fusion.3), channel_id=1, source_target_pairs={{0,4},{4,0},{8,12},{12,8},{1,5},{5,1},{9,13},{13,9},{2,6},{6,2},{1... | collective-permute-start | bytes 1572872 | tf_op jit(solution)/shard_map/ppermute | solution.py:124
  74.4 16.0 %collective-permute-start.25 = (bf16[1,4,32,512]{3,2,1,0:T(8,128)(2,1)S(1)}, bf16[1,4,32,512]{3,2,1,0:T(8,128)(2,1)S(1)}, u32[]{:S(2)}, u32[]{:S(2)}) collective-permute-start(bf16[1,4,32,512]{3,2,1,0:T(8,128)(2,1)S(1)} %get-tuple-element.124), channel_id=1, source_target_pairs={{0,3},{1,2},{2,1},{3,0},{4,7},{5,6},{6,5},{7,4},{8,11},{9,10},{10,... | collective-permute-start | bytes 393224 | tf_op jit(solution)/shard_map/ppermute | solution.py:124
  77.1 13.4 %collective-permute-start.24 = (bf16[1,4,32,512]{3,2,1,0:T(8,128)(2,1)S(1)}, bf16[1,4,32,512]{3,2,1,0:T(8,128)(2,1)S(1)}, u32[]{:S(2)}, u32[]{:S(2)}) collective-permute-start(bf16[1,4,32,512]{3,2,1,0:T(8,128)(2,1)S(1)} %get-tuple-element.108), channel_id=1, source_target_pairs={{0,2},{1,3},{2,0},{3,1},{4,6},{5,7},{6,4},{7,5},{8,10},{9,11},{10,... | collective-permute-start | bytes 393224 | tf_op jit(solution)/shard_map/ppermute | solution.py:124
  77.1 8.9 %collective-permute-start.23 = (bf16[1,4,32,512]{3,2,1,0:T(8,128)(2,1)S(1)}, bf16[1,4,32,512]{3,2,1,0:T(8,128)(2,1)S(1)}, u32[]{:S(2)}, u32[]{:S(2)}) collective-permute-start(bf16[1,4,32,512]{3,2,1,0:T(8,128)(2,1)S(1)} %get-tuple-element.109), channel_id=1, source_target_pairs={{0,1},{1,0},{2,3},{3,2},{4,5},{5,4},{6,7},{7,6},{8,9},{9,8},{10,11... | collective-permute-start | bytes 393224 | tf_op jit(solution)/shard_map/ppermute | solution.py:124

commit v19 on v18

--- a/solution.py
+++ b/solution.py
@@ -80,7 +80,7 @@
         out_specs=[out_spec] * slices,
         out_shape=[jax.ShapeDtypeStruct((count, width), jnp.bfloat16)] * slices,
         scratch_shapes=[pltpu.VMEM((block * order, columns), jnp.float32)],
-        compiler_params=pltpu.CompilerParams(vmem_limit_bytes=32 * 1024 * 1024),
+        compiler_params=pltpu.CompilerParams(vmem_limit_bytes=16 * 1024 * 1024),
         cost_estimate=pl.CostEstimate(flops=1000000000, bytes_accessed=0, transcendentals=0),
     )(*pieces[::-1], basis, basis.T, in_basis, in_basis.T, corrections)
 
@@ -103,7 +103,7 @@
         out_specs=pl.BlockSpec((FLAT, each * columns), lambda step: (step, 0)),
         out_shape=jax.ShapeDtypeStruct((count, each * columns), rows.dtype),
         scratch_shapes=[pltpu.VMEM((FLAT * each, columns), jnp.float32)],
-        compiler_params=pltpu.CompilerParams(vmem_limit_bytes=32 * 1024 * 1024),
+        compiler_params=pltpu.CompilerParams(vmem_limit_bytes=8 * 1024 * 1024),
         cost_estimate=pl.CostEstimate(flops=1000000000, bytes_accessed=0, transcendentals=0),
     )(rows)
 

time: 92 us -> 92 us (level)
  no operation moved by 1% of the time
where the time goes in v19:
time: 92 us; the launch traced here: 91.5 us
  starting transfers between devices  37.2 us (40%)
  waiting for transfers between devices  17.1 us (19%)
  local copies, waits for them, and re-layouts  16.1 us (18%)
  Pallas kernels  9.48 us (10%)
  matrix products  6.66 us (7%)
  other arithmetic  4.52 us (5%)
    ppermute x26, starting transfers between devices, crossed(): return lax.ppermute(value, axis, [(at, at ^ mask) for at in range(size)])  37.2 us
    ppermute x26, waiting for transfers between devices, crossed(): return lax.ppermute(value, axis, [(at, at ^ mask) for at in range(size)])  17.1 us
    unnamed x36, local copies, waits for them, and re-layouts  10.5 us
    pallas_call x2, Pallas kernels, condition_fast(): pl.pallas_call(functools.partial(condition_kernel, slices, rows_here), gr...  7.77 us
    dot_general x8, matrix products, products(): lax.dot_general(block, train_flat, contract, preferred_element_type=jnp.f...  6.66 us
    dynamic_slice x8, local copies, waits for them, and re-layouts, body(): lax.dynamic_slice_in_dim(source, first + (here ^ mask) * each, each, 0)  4.01 us
  transfers between devices with their start and end apart: 26, of which 8 were waited for; matrix products, arithmetic and copies ran while one was open for 19% of the time, Pallas kernels for 10%

profile of v19, /device:TPU:0, one launch (start us, length us, event | category | flops | bytes accessed | tf_op | source)
XLA Modules:
  0.0 91.5 jit_solution(9319491392232812224)
XLA Ops:
  0.0 1.2 %copy-done = bf16[256,16,128]{2,1,0:T(8,128)(2,1)S(1)} copy-done((bf16[256,16,128]{2,1,0:T(8,128)(2,1)S(1)}, bf16[256,16,128]{2,1,0:T(8,128)(2,1)}, u32[]{:S(2)}) %copy-start) | copy-done | bytes 1048600
  1.2 0.7 constant_dynamic-slice_fusion.7
  1.9 5.0 %collective-permute-start = (bf16[32,16,128]{2,1,0:T(8,128)(2,1)}, bf16[32,16,128]{2,1,0:T(8,128)(2,1)S(1)}, u32[]{:S(2)}, u32[]{:S(2)}) collective-permute-start(bf16[32,16,128]{2,1,0:T(8,128)(2,1)} %constant_dynamic-slice_fusion.7), channel_id=1, source_target_pairs={{0,3},{1,2},{2,1},{3,0},{4,7},{5,6},{6,5},{7,4},{8,11},{9,10},{10,... | collective-permute-start | bytes 393224 | tf_op jit(solution)/shard_map/ppermute | solution.py:124
  6.9 0.7 constant_dynamic-slice_fusion.6
  7.6 0.7 constant_dynamic-slice_fusion.5
  8.3 0.6 collective-permute-start.1
  8.8 0.7 fusion.8
  9.6 0.1 copy.13
  9.7 0.1 copy.14
  9.7 0.1 copy.15
  9.9 0.1 pad_maximum_fusion.15
  10.1 1.6 %copy.10 = f32[128,128]{0,1:T(8,128)} copy(f32[128,128]{1,0:T(8,128)} %refs_6_.3) | data formatting | bytes 131072 | tf_op args[3]
  11.7 1.6 %copy-done.1 = bf16[512,16,128]{2,1,0:T(8,128)(2,1)S(1)} copy-done((bf16[512,16,128]{2,1,0:T(8,128)(2,1)S(1)}, bf16[512,16,128]{2,1,0:T(8,128)(2,1)}, u32[]{:S(2)}) %copy-start.1) | copy-done | bytes 2097176
  13.3 1.7 %shard_map.55 = bf16[512,2048]{1,0:T(8,128)(2,1)S(1)} custom-call(bf16[512,16,128]{2,1,0:T(8,128)(2,1)S(1)} %copy-done.1), custom_call_target="tpu_custom_call" | custom-call | flops 1000000000 | tf_op jit(solution)/shard_map/pallas_call | solution.py:99
  15.1 0.7 constant_dynamic-slice_fusion.3
  15.7 0.7 constant_dynamic-slice_fusion.2
  16.4 0.7 constant_dynamic-slice_fusion.1
  17.1 1.5 %collective-permute-start.4 = (bf16[32,16,128]{2,1,0:T(8,128)(2,1)}, bf16[32,16,128]{2,1,0:T(8,128)(2,1)}, u32[]{:S(2)}, u32[]{:S(2)}) collective-permute-start(bf16[32,16,128]{2,1,0:T(8,128)(2,1)} %constant_dynamic-slice_fusion.1), channel_id=1, source_target_pairs={{0,1},{1,0},{2,3},{3,2},{4,5},{5,4},{6,7},{7,6},{8,9},{9,8},{10,11... | collective-permute-start | bytes 393224 | tf_op jit(solution)/shard_map/ppermute | solution.py:124
  18.5 2.9 %collective-permute-start.5 = (bf16[32,16,128]{2,1,0:T(8,128)(2,1)}, bf16[32,16,128]{2,1,0:T(8,128)(2,1)}, u32[]{:S(2)}, u32[]{:S(2)}) collective-permute-start(bf16[32,16,128]{2,1,0:T(8,128)(2,1)} %constant_dynamic-slice_fusion.2), channel_id=1, source_target_pairs={{0,2},{1,3},{2,0},{3,1},{4,6},{5,7},{6,4},{7,5},{8,10},{9,11},{10,... | collective-permute-start | bytes 393224 | tf_op jit(solution)/shard_map/ppermute | solution.py:124
  21.5 0.9 copy-done.6
  22.4 3.8 %shard_map.56 = (bf16[32,2048]{1,0:T(8,128)(2,1)S(1)}, bf16[32,2048]{1,0:T(8,128)(2,1)}, bf16[32,2048]{1,0:T(8,128)(2,1)S(1)}, bf16[32,2048]{1,0:T(8,128)(2,1)S(1)}) custom-call(bf16[32,16,128]{2,1,0:T(8,128)(2,1)S(1)} %copy-done.6, bf16[32,16,128]{2,1,0:T(8,128)(2,1)} %collective-permute-done.1.refs_1_, ...), custom_call_target="tpu_custom_call" | custom-call | flops 1000000000 | tf_op jit(solution)/shard_map/pallas_call | solution.py:76
  26.2 0.6 copy-done.7
  26.9 0.7 copy-done.9
  27.5 0.5 collective-permute-start.3
  28.1 3.9 %collective-permute-start.7 = (bf16[32,2048]{1,0:T(8,128)(2,1)}, bf16[32,2048]{1,0:T(8,128)(2,1)}, u32[]{:S(2)}, u32[]{:S(2)}) collective-permute-start(bf16[32,2048]{1,0:T(8,128)(2,1)} %copy-done.9), channel_id=1, source_target_pairs={{0,2},{1,3},{2,0},{3,1},{4,6},{5,7},{6,4},{7,5},{8,10},{9,11},{10,... | collective-permute-start | bytes 393224 | tf_op jit(solution)/shard_map/ppermute | solution.py:124
  32.0 1.6 %collective-permute-done.3 = bf16[32,2048]{1,0:T(8,128)(2,1)S(1)} collective-permute-done((bf16[32,2048]{1,0:T(8,128)(2,1)}, bf16[32,2048]{1,0:T(8,128)(2,1)S(1)}, u32[]{:S(2)}, u32[]{:S(2)}) %collective-permute-start.3) | collective-permute-done | bytes 131104 | tf_op jit(solution)/shard_map/ppermute | solution.py:124
  33.6 0.6 copy-done.12
  34.2 0.7 constant_dynamic-update-slice_fusion.1
  34.9 0.8 copy-done.4
  35.7 0.8 copy-done.11
  36.5 3.9 %shard_map.57 = (bf16[32,2048]{1,0:T(8,128)(2,1)S(1)}, bf16[32,2048]{1,0:T(8,128)(2,1)}, bf16[32,2048]{1,0:T(8,128)(2,1)S(1)}, bf16[32,2048]{1,0:T(8,128)(2,1)S(1)}) custom-call(bf16[32,16,128]{2,1,0:T(8,128)(2,1)} %collective-permute-done.6.refs_0_, bf16[32,16,128]{2,1,0:T(8,128)(2,1)} %collective-permute-done.5.refs_1_, ...), custom_call_target="tpu_custom_call" | custom-call | flops 1000000000 | tf_op jit(solution)/shard_map/pallas_call | solution.py:76
  40.4 0.7 copy-done.8
  41.1 6.6 %collective-permute-start.9 = (bf16[32,2048]{1,0:T(8,128)(2,1)}, bf16[32,2048]{1,0:T(8,128)(2,1)S(1)}, u32[]{:S(2)}, u32[]{:S(2)}) collective-permute-start(bf16[32,2048]{1,0:T(8,128)(2,1)} %get-tuple-element.84), channel_id=1, source_target_pairs={{0,1},{1,0},{2,3},{3,2},{4,5},{5,4},{6,7},{7,6},{8,9},{9,8},{10,11... | collective-permute-start | bytes 393224 | tf_op jit(solution)/shard_map/ppermute | solution.py:124
  47.7 0.7 constant_dynamic-update-slice_fusion
  48.4 1.5 %collective-permute-start.10 = (bf16[64,2048]{1,0:T(8,128)(2,1)}, bf16[64,2048]{1,0:T(8,128)(2,1)}, u32[]{:S(2)}, u32[]{:S(2)}) collective-permute-start(bf16[64,2048]{1,0:T(8,128)(2,1)} %constant_dynamic-update-slice_fusion), channel_id=1, source_target_pairs={{0,8},{4,12},{8,0},{12,4},{1,9},{5,13},{9,1},{13,5},{2,10},{6,14},... | collective-permute-start | bytes 786440 | tf_op jit(solution)/shard_map/ppermute | solution.py:124
  49.8 1.2 %collective-permute-start.19 = (bf16[32,2048]{1,0:T(8,128)(2,1)}, bf16[32,2048]{1,0:T(8,128)(2,1)S(1)}, u32[]{:S(2)}, u32[]{:S(2)}) collective-permute-start(bf16[32,2048]{1,0:T(8,128)(2,1)} %copy-done.8), channel_id=1, source_target_pairs={{0,2},{1,3},{2,0},{3,1},{4,6},{5,7},{6,4},{7,5},{8,10},{9,11},{10,... | collective-permute-start | bytes 393224 | tf_op jit(solution)/shard_map/ppermute | solution.py:124
  51.0 1.5 %collective-permute-start.20 = (bf16[32,2048]{1,0:T(8,128)(2,1)S(1)}, bf16[32,2048]{1,0:T(8,128)(2,1)S(1)}, u32[]{:S(2)}, u32[]{:S(2)}) collective-permute-start(bf16[32,2048]{1,0:T(8,128)(2,1)S(1)} %get-tuple-element.103), channel_id=1, source_target_pairs={{0,3},{1,2},{2,1},{3,0},{4,7},{5,6},{6,5},{7,4},{8,11},{9,10},{10,... | collective-permute-start | bytes 393224 | tf_op jit(solution)/shard_map/ppermute | solution.py:124
  52.5 1.0 %pad_maximum_fusion.4 = bf16[64,2048]{1,0:T(8,128)(2,1)S(1)} fusion(bf16[32,2048]{1,0:T(8,128)(2,1)} %collective-permute-done.8, bf16[32,2048]{1,0:T(8,128)(2,1)} %collective-permute-done.7), kind=kLoop, calls=%fused_computation.13 | loop fusion | flops 524288 | bytes 524288 | tf_op jit(solution)/shard_map/concatenate | solution.py:156
  53.4 0.6 collective-permute-start.12
  54.0 1.0 %collective-permute-done.10 = bf16[64,2048]{1,0:T(8,128)(2,1)} collective-permute-done((bf16[64,2048]{1,0:T(8,128)(2,1)}, bf16[64,2048]{1,0:T(8,128)(2,1)}, u32[]{:S(2)}, u32[]{:S(2)}) %collective-permute-start.10) | collective-permute-done | bytes 262176 | tf_op jit(solution)/shard_map/ppermute | solution.py:124
  55.0 1.1 %pad_maximum_fusion = bf16[128,2048]{1,0:T(8,128)(2,1)S(1)} fusion(bf16[64,2048]{1,0:T(8,128)(2,1)} %collective-permute-done.10, bf16[64,2048]{1,0:T(8,128)(2,1)} %constant_dynamic-update-slice_fusion), kind=kLoop, calls=%fused_computation.8 | loop fusion | flops 1048576 | bytes 1048576 | tf_op jit(solution)/shard_map/concatenate | solution.py:220
  56.2 0.8 convolution_convert_fusion.5
  57.1 1.5 %collective-permute-start.17 = (bf16[64,2048]{1,0:T(8,128)(2,1)S(1)}, bf16[64,2048]{1,0:T(8,128)(2,1)S(1)}, u32[]{:S(2)}, u32[]{:S(2)}) collective-permute-start(bf16[64,2048]{1,0:T(8,128)(2,1)S(1)} %constant_dynamic-update-slice_fusion.2), channel_id=1, source_target_pairs={{0,8},{4,12},{8,0},{12,4},{1,9},{5,13},{9,1},{13,5},{2,10},{6,14},... | collective-permute-start | bytes 786440 | tf_op jit(solution)/shard_map/ppermute | solution.py:124
  58.6 1.3 %collective-permute-done.12 = bf16[64,2048]{1,0:T(8,128)(2,1)S(1)} collective-permute-done((bf16[64,2048]{1,0:T(8,128)(2,1)S(1)}, bf16[64,2048]{1,0:T(8,128)(2,1)S(1)}, u32[]{:S(2)}, u32[]{:S(2)}) %collective-permute-start.12) | collective-permute-done | bytes 262176 | tf_op jit(solution)/shard_map/ppermute | solution.py:124
  59.9 1.0 %pad_maximum_fusion.1 = bf16[128,2048]{1,0:T(8,128)(2,1)S(1)} fusion(bf16[64,2048]{1,0:T(8,128)(2,1)S(1)} %collective-permute-done.12, bf16[32,2048]{1,0:T(8,128)(2,1)} %collective-permute-done.8, bf16[32,2048]{1,0:T(8,128)(2,1)} %collective-permute-done.7), kind=kLoop, calls=%fused_computation.9 | loop fusion | flops 1572864 | bytes 1048576 | tf_op jit(solution)/shard_map/concatenate | solution.py:224
  61.0 0.8 convolution_convert_fusion.4
  61.9 0.6 collective-permute-start.21
  62.5 0.8 convolution_convert_fusion.7
  63.4 0.8 convolution_convert_fusion.6
  64.3 2.4 %collective-permute-start.16 = (bf16[1,4,32,512]{3,2,1,0:T(8,128)(2,1)S(1)}, bf16[1,4,32,512]{3,2,1,0:T(8,128)(2,1)S(1)}, u32[]{:S(2)}, u32[]{:S(2)}) collective-permute-start(bf16[1,4,32,512]{3,2,1,0:T(8,128)(2,1)S(1)} %get-tuple-element.125), channel_id=1, source_target_pairs={{0,3},{1,2},{2,1},{3,0},{4,7},{5,6},{6,5},{7,4},{8,11},{9,10},{10,... | collective-permute-start | bytes 393224 | tf_op jit(solution)/shard_map/ppermute | solution.py:124
  66.7 0.5 collective-permute-start.15
  67.3 1.6 %collective-permute-start.14 = (bf16[1,4,32,512]{3,2,1,0:T(8,128)(2,1)S(1)}, bf16[1,4,32,512]{3,2,1,0:T(8,128)(2,1)S(1)}, u32[]{:S(2)}, u32[]{:S(2)}) collective-permute-start(bf16[1,4,32,512]{3,2,1,0:T(8,128)(2,1)S(1)} %get-tuple-element.97), channel_id=1, source_target_pairs={{0,1},{1,0},{2,3},{3,2},{4,5},{5,4},{6,7},{7,6},{8,9},{9,8},{10,11... | collective-permute-start | bytes 393224 | tf_op jit(solution)/shard_map/ppermute | solution.py:124
  69.0 0.8 convolution_convert_fusion.1
  69.8 1.7 %collective-permute-done.21 = bf16[64,2048]{1,0:T(8,128)(2,1)S(1)} collective-permute-done((bf16[64,2048]{1,0:T(8,128)(2,1)S(1)}, bf16[64,2048]{1,0:T(8,128)(2,1)S(1)}, u32[]{:S(2)}, u32[]{:S(2)}) %collective-permute-start.21) | collective-permute-done | bytes 262176 | tf_op jit(solution)/shard_map/ppermute | solution.py:124
  71.6 0.8 convolution_convert_fusion
  72.5 0.8 convolution_convert_fusion.3
  73.3 0.2 collective-permute-done.22
  73.5 0.8 convolution_convert_fusion.2
  74.4 2.7 %collective-permute-start.25 = (bf16[1,4,32,512]{3,2,1,0:T(8,128)(2,1)S(1)}, bf16[1,4,32,512]{3,2,1,0:T(8,128)(2,1)S(1)}, u32[]{:S(2)}, u32[]{:S(2)}) collective-permute-start(bf16[1,4,32,512]{3,2,1,0:T(8,128)(2,1)S(1)} %get-tuple-element.124), channel_id=1, source_target_pairs={{0,3},{1,2},{2,1},{3,0},{4,7},{5,6},{6,5},{7,4},{8,11},{9,10},{10,... | collective-permute-start | bytes 393224 | tf_op jit(solution)/shard_map/ppermute | solution.py:124
  77.1 1.9 %collective-permute-start.23 = (bf16[1,4,32,512]{3,2,1,0:T(8,128)(2,1)S(1)}, bf16[1,4,32,512]{3,2,1,0:T(8,128)(2,1)S(1)}, u32[]{:S(2)}, u32[]{:S(2)}) collective-permute-start(bf16[1,4,32,512]{3,2,1,0:T(8,128)(2,1)S(1)} %get-tuple-element.109), channel_id=1, source_target_pairs={{0,1},{1,0},{2,3},{3,2},{4,5},{5,4},{6,7},{7,6},{8,9},{9,8},{10,11... | collective-permute-start | bytes 393224 | tf_op jit(solution)/shard_map/ppermute | solution.py:124
  79.0 6.5 %collective-permute-done.15 = bf16[1,4,32,512]{3,2,1,0:T(8,128)(2,1)S(1)} collective-permute-done((bf16[1,4,32,512]{3,2,1,0:T(8,128)(2,1)S(1)}, bf16[1,4,32,512]{3,2,1,0:T(8,128)(2,1)S(1)}, u32[]{:S(2)}, u32[]{:S(2)}) %collective-permute-start.15) | collective-permute-done | bytes 131104 | tf_op jit(solution)/shard_map/ppermute | solution.py:124
  85.6 0.4 collective-permute-done.23
  86.0 4.4 %collective-permute-done.24 = bf16[1,4,32,512]{3,2,1,0:T(8,128)(2,1)S(1)} collective-permute-done((bf16[1,4,32,512]{3,2,1,0:T(8,128)(2,1)S(1)}, bf16[1,4,32,512]{3,2,1,0:T(8,128)(2,1)S(1)}, u32[]{:S(2)}, u32[]{:S(2)}) %collective-permute-start.24) | collective-permute-done | bytes 131104 | tf_op jit(solution)/shard_map/ppermute | solution.py:124
  90.6 0.8 maximum_bitcast_fusion
  (73 shorter events, 1.2 us)
Async XLA Ops:
  0.0 1.2 %copy-start = (bf16[256,16,128]{2,1,0:T(8,128)(2,1)S(1)}, bf16[256,16,128]{2,1,0:T(8,128)(2,1)}, u32[]{:S(2)}) copy-start(bf16[256,16,128]{2,1,0:T(8,128)(2,1)} %param.5) | copy-start | bytes 3145732
  1.9 13.1 %collective-permute-start = (bf16[32,16,128]{2,1,0:T(8,128)(2,1)}, bf16[32,16,128]{2,1,0:T(8,128)(2,1)S(1)}, u32[]{:S(2)}, u32[]{:S(2)}) collective-permute-start(bf16[32,16,128]{2,1,0:T(8,128)(2,1)} %constant_dynamic-slice_fusion.7), channel_id=1, source_target_pairs={{0,3},{1,2},{2,1},{3,0},{4,7},{5,6},{6,5},{7,4},{8,11},{9,10},{10,... | collective-permute-start | bytes 393224 | tf_op jit(solution)/shard_map/ppermute | solution.py:124
  8.3 13.2 %collective-permute-start.2 = (bf16[32,16,128]{2,1,0:T(8,128)(2,1)}, bf16[32,16,128]{2,1,0:T(8,128)(2,1)}, u32[]{:S(2)}, u32[]{:S(2)}) collective-permute-start(bf16[32,16,128]{2,1,0:T(8,128)(2,1)} %constant_dynamic-slice_fusion.5), channel_id=1, source_target_pairs={{0,1},{1,0},{2,3},{3,2},{4,5},{5,4},{6,7},{7,6},{8,9},{9,8},{10,11... | collective-permute-start | bytes 393224 | tf_op jit(solution)/shard_map/ppermute | solution.py:124
  8.3 13.2 %collective-permute-start.1 = (bf16[32,16,128]{2,1,0:T(8,128)(2,1)}, bf16[32,16,128]{2,1,0:T(8,128)(2,1)}, u32[]{:S(2)}, u32[]{:S(2)}) collective-permute-start(bf16[32,16,128]{2,1,0:T(8,128)(2,1)} %constant_dynamic-slice_fusion.6), channel_id=1, source_target_pairs={{0,2},{1,3},{2,0},{3,1},{4,6},{5,7},{6,4},{7,5},{8,10},{9,11},{10,... | collective-permute-start | bytes 393224 | tf_op jit(solution)/shard_map/ppermute | solution.py:124
  11.7 1.6 %copy-start.1 = (bf16[512,16,128]{2,1,0:T(8,128)(2,1)S(1)}, bf16[512,16,128]{2,1,0:T(8,128)(2,1)}, u32[]{:S(2)}) copy-start(bf16[512,16,128]{2,1,0:T(8,128)(2,1)} %rows.1) | copy-start | bytes 6291460
  13.3 8.2 %copy-start.2 = (f32[128,128]{1,0:T(8,128)S(1)}, f32[128,128]{1,0:T(8,128)}, u32[]{:S(2)}) copy-start(f32[128,128]{1,0:T(8,128)} %refs_6_.3) | copy-start | bytes 196612
  13.3 8.2 %copy-start.3 = (f32[128,128]{0,1:T(8,128)S(1)}, f32[128,128]{0,1:T(8,128)}, u32[]{:S(2)}) copy-start(f32[128,128]{0,1:T(8,128)} %copy.10) | copy-start | bytes 196612
  13.3 8.2 %copy-start.10 = (f32[64,128]{1,0:T(8,128)S(1)}, f32[64,128]{1,0:T(8,128)}, u32[]{:S(2)}) copy-start(f32[64,128]{1,0:T(8,128)} %refs_8_.3) | copy-start | bytes 98308
  15.0 6.4 %copy-start.5 = (bf16[32,16,128]{2,1,0:T(8,128)(2,1)}, bf16[32,16,128]{2,1,0:T(8,128)(2,1)S(1)}, u32[]{:S(2)}) copy-start(bf16[32,16,128]{2,1,0:T(8,128)(2,1)S(1)} %collective-permute-done.refs_0_) | copy-start | bytes 393220
  17.1 14.9 %collective-permute-start.4 = (bf16[32,16,128]{2,1,0:T(8,128)(2,1)}, bf16[32,16,128]{2,1,0:T(8,128)(2,1)}, u32[]{:S(2)}, u32[]{:S(2)}) collective-permute-start(bf16[32,16,128]{2,1,0:T(8,128)(2,1)} %constant_dynamic-slice_fusion.1), channel_id=1, source_target_pairs={{0,1},{1,0},{2,3},{3,2},{4,5},{5,4},{6,7},{7,6},{8,9},{9,8},{10,11... | collective-permute-start | bytes 393224 | tf_op jit(solution)/shard_map/ppermute | solution.py:124
  18.5 13.5 %collective-permute-start.5 = (bf16[32,16,128]{2,1,0:T(8,128)(2,1)}, bf16[32,16,128]{2,1,0:T(8,128)(2,1)}, u32[]{:S(2)}, u32[]{:S(2)}) collective-permute-start(bf16[32,16,128]{2,1,0:T(8,128)(2,1)} %constant_dynamic-slice_fusion.2), channel_id=1, source_target_pairs={{0,2},{1,3},{2,0},{3,1},{4,6},{5,7},{6,4},{7,5},{8,10},{9,11},{10,... | collective-permute-start | bytes 393224 | tf_op jit(solution)/shard_map/ppermute | solution.py:124
  21.4 10.6 %collective-permute-start.6 = (bf16[32,16,128]{2,1,0:T(8,128)(2,1)}, bf16[32,16,128]{2,1,0:T(8,128)(2,1)}, u32[]{:S(2)}, u32[]{:S(2)}) collective-permute-start(bf16[32,16,128]{2,1,0:T(8,128)(2,1)} %constant_dynamic-slice_fusion.3), channel_id=1, source_target_pairs={{0,3},{1,2},{2,1},{3,0},{4,7},{5,6},{6,5},{7,4},{8,11},{9,10},{10,... | collective-permute-start | bytes 393224 | tf_op jit(solution)/shard_map/ppermute | solution.py:124
  21.5 0.9 copy-start.6
  26.2 0.6 copy-start.7
  26.9 0.7 copy-start.9
  27.5 6.0 %collective-permute-start.3 = (bf16[32,2048]{1,0:T(8,128)(2,1)}, bf16[32,2048]{1,0:T(8,128)(2,1)S(1)}, u32[]{:S(2)}, u32[]{:S(2)}) collective-permute-start(bf16[32,2048]{1,0:T(8,128)(2,1)} %get-tuple-element.68), channel_id=1, source_target_pairs={{0,1},{1,0},{2,3},{3,2},{4,5},{5,4},{6,7},{7,6},{8,9},{9,8},{10,11... | collective-permute-start | bytes 393224 | tf_op jit(solution)/shard_map/ppermute | solution.py:124
  28.1 22.9 %collective-permute-start.7 = (bf16[32,2048]{1,0:T(8,128)(2,1)}, bf16[32,2048]{1,0:T(8,128)(2,1)}, u32[]{:S(2)}, u32[]{:S(2)}) collective-permute-start(bf16[32,2048]{1,0:T(8,128)(2,1)} %copy-done.9), channel_id=1, source_target_pairs={{0,2},{1,3},{2,0},{3,1},{4,6},{5,7},{6,4},{7,5},{8,10},{9,11},{10,... | collective-permute-start | bytes 393224 | tf_op jit(solution)/shard_map/ppermute | solution.py:124
  32.0 20.5 %collective-permute-start.8 = (bf16[32,2048]{1,0:T(8,128)(2,1)}, bf16[32,2048]{1,0:T(8,128)(2,1)}, u32[]{:S(2)}, u32[]{:S(2)}) collective-permute-start(bf16[32,2048]{1,0:T(8,128)(2,1)} %copy-done.7), channel_id=1, source_target_pairs={{0,3},{1,2},{2,1},{3,0},{4,7},{5,6},{6,5},{7,4},{8,11},{9,10},{10,... | collective-permute-start | bytes 393224 | tf_op jit(solution)/shard_map/ppermute | solution.py:124
  33.6 0.6 copy-start.12
  34.9 0.8 copy-start.4
  35.7 0.8 copy-start.11
  36.5 11.2 %copy-start.13 = (bf16[32,2048]{1,0:T(8,128)(2,1)S(1)}, bf16[32,2048]{1,0:T(8,128)(2,1)}, u32[]{:S(2)}) copy-start(bf16[32,2048]{1,0:T(8,128)(2,1)} %copy-done.12) | copy-start | bytes 393220
  40.4 0.7 copy-start.8
  41.1 11.4 %collective-permute-start.9 = (bf16[32,2048]{1,0:T(8,128)(2,1)}, bf16[32,2048]{1,0:T(8,128)(2,1)S(1)}, u32[]{:S(2)}, u32[]{:S(2)}) collective-permute-start(bf16[32,2048]{1,0:T(8,128)(2,1)} %get-tuple-element.84), channel_id=1, source_target_pairs={{0,1},{1,0},{2,3},{3,2},{4,5},{5,4},{6,7},{7,6},{8,9},{9,8},{10,11... | collective-permute-start | bytes 393224 | tf_op jit(solution)/shard_map/ppermute | solution.py:124
  48.4 6.7 %collective-permute-start.10 = (bf16[64,2048]{1,0:T(8,128)(2,1)}, bf16[64,2048]{1,0:T(8,128)(2,1)}, u32[]{:S(2)}, u32[]{:S(2)}) collective-permute-start(bf16[64,2048]{1,0:T(8,128)(2,1)} %constant_dynamic-update-slice_fusion), channel_id=1, source_target_pairs={{0,8},{4,12},{8,0},{12,4},{1,9},{5,13},{9,1},{13,5},{2,10},{6,14},... | collective-permute-start | bytes 786440 | tf_op jit(solution)/shard_map/ppermute | solution.py:124
  49.8 12.0 %collective-permute-start.19 = (bf16[32,2048]{1,0:T(8,128)(2,1)}, bf16[32,2048]{1,0:T(8,128)(2,1)S(1)}, u32[]{:S(2)}, u32[]{:S(2)}) collective-permute-start(bf16[32,2048]{1,0:T(8,128)(2,1)} %copy-done.8), channel_id=1, source_target_pairs={{0,2},{1,3},{2,0},{3,1},{4,6},{5,7},{6,4},{7,5},{8,10},{9,11},{10,... | collective-permute-start | bytes 393224 | tf_op jit(solution)/shard_map/ppermute | solution.py:124
  51.0 10.8 %collective-permute-start.20 = (bf16[32,2048]{1,0:T(8,128)(2,1)S(1)}, bf16[32,2048]{1,0:T(8,128)(2,1)S(1)}, u32[]{:S(2)}, u32[]{:S(2)}) collective-permute-start(bf16[32,2048]{1,0:T(8,128)(2,1)S(1)} %get-tuple-element.103), channel_id=1, source_target_pairs={{0,3},{1,2},{2,1},{3,0},{4,7},{5,6},{6,5},{7,4},{8,11},{9,10},{10,... | collective-permute-start | bytes 393224 | tf_op jit(solution)/shard_map/ppermute | solution.py:124
  53.4 6.4 %collective-permute-start.12 = (bf16[64,2048]{1,0:T(8,128)(2,1)S(1)}, bf16[64,2048]{1,0:T(8,128)(2,1)S(1)}, u32[]{:S(2)}, u32[]{:S(2)}) collective-permute-start(bf16[64,2048]{1,0:T(8,128)(2,1)S(1)} %pad_maximum_fusion.4), channel_id=1, source_target_pairs={{0,8},{4,12},{8,0},{12,4},{1,9},{5,13},{9,1},{13,5},{2,10},{6,14},... | collective-permute-start | bytes 786440 | tf_op jit(solution)/shard_map/ppermute | solution.py:124
  56.1 6.4 %collective-permute-start.11 = (bf16[128,2048]{1,0:T(8,128)(2,1)S(1)}, bf16[128,2048]{1,0:T(8,128)(2,1)S(1)}, u32[]{:S(2)}, u32[]{:S(2)}) collective-permute-start(bf16[128,2048]{1,0:T(8,128)(2,1)S(1)} %pad_maximum_fusion), channel_id=1, source_target_pairs={{0,4},{4,0},{8,12},{12,8},{1,5},{5,1},{9,13},{13,9},{2,6},{6,2},{1... | collective-permute-start | bytes 1572872 | tf_op jit(solution)/shard_map/ppermute | solution.py:124
  57.1 11.8 %collective-permute-start.17 = (bf16[64,2048]{1,0:T(8,128)(2,1)S(1)}, bf16[64,2048]{1,0:T(8,128)(2,1)S(1)}, u32[]{:S(2)}, u32[]{:S(2)}) collective-permute-start(bf16[64,2048]{1,0:T(8,128)(2,1)S(1)} %constant_dynamic-update-slice_fusion.2), channel_id=1, source_target_pairs={{0,8},{4,12},{8,0},{12,4},{1,9},{5,13},{9,1},{13,5},{2,10},{6,14},... | collective-permute-start | bytes 786440 | tf_op jit(solution)/shard_map/ppermute | solution.py:124
  60.9 2.5 %collective-permute-start.13 = (bf16[128,2048]{1,0:T(8,128)(2,1)S(1)}, bf16[128,2048]{1,0:T(8,128)(2,1)S(1)}, u32[]{:S(2)}, u32[]{:S(2)}) collective-permute-start(bf16[128,2048]{1,0:T(8,128)(2,1)S(1)} %pad_maximum_fusion.1), channel_id=1, source_target_pairs={{0,4},{4,0},{8,12},{12,8},{1,5},{5,1},{9,13},{13,9},{2,6},{6,2},{1... | collective-permute-start | bytes 1572872 | tf_op jit(solution)/shard_map/ppermute | solution.py:124
  61.9 9.6 %collective-permute-start.21 = (bf16[64,2048]{1,0:T(8,128)(2,1)S(1)}, bf16[64,2048]{1,0:T(8,128)(2,1)S(1)}, u32[]{:S(2)}, u32[]{:S(2)}) collective-permute-start(bf16[64,2048]{1,0:T(8,128)(2,1)S(1)} %constant_dynamic-update-slice_fusion.4), channel_id=1, source_target_pairs={{0,8},{4,12},{8,0},{12,4},{1,9},{5,13},{9,1},{13,5},{2,10},{6,14},... | collective-permute-start | bytes 786440 | tf_op jit(solution)/shard_map/ppermute | solution.py:124
  64.3 21.3 %collective-permute-start.16 = (bf16[1,4,32,512]{3,2,1,0:T(8,128)(2,1)S(1)}, bf16[1,4,32,512]{3,2,1,0:T(8,128)(2,1)S(1)}, u32[]{:S(2)}, u32[]{:S(2)}) collective-permute-start(bf16[1,4,32,512]{3,2,1,0:T(8,128)(2,1)S(1)} %get-tuple-element.125), channel_id=1, source_target_pairs={{0,3},{1,2},{2,1},{3,0},{4,7},{5,6},{6,5},{7,4},{8,11},{9,10},{10,... | collective-permute-start | bytes 393224 | tf_op jit(solution)/shard_map/ppermute | solution.py:124
  66.7 18.8 %collective-permute-start.15 = (bf16[1,4,32,512]{3,2,1,0:T(8,128)(2,1)S(1)}, bf16[1,4,32,512]{3,2,1,0:T(8,128)(2,1)S(1)}, u32[]{:S(2)}, u32[]{:S(2)}) collective-permute-start(bf16[1,4,32,512]{3,2,1,0:T(8,128)(2,1)S(1)} %get-tuple-element.96), channel_id=1, source_target_pairs={{0,2},{1,3},{2,0},{3,1},{4,6},{5,7},{6,4},{7,5},{8,10},{9,11},{10,... | collective-permute-start | bytes 393224 | tf_op jit(solution)/shard_map/ppermute | solution.py:124
  67.3 9.8 %collective-permute-start.14 = (bf16[1,4,32,512]{3,2,1,0:T(8,128)(2,1)S(1)}, bf16[1,4,32,512]{3,2,1,0:T(8,128)(2,1)S(1)}, u32[]{:S(2)}, u32[]{:S(2)}) collective-permute-start(bf16[1,4,32,512]{3,2,1,0:T(8,128)(2,1)S(1)} %get-tuple-element.97), channel_id=1, source_target_pairs={{0,1},{1,0},{2,3},{3,2},{4,5},{5,4},{6,7},{7,6},{8,9},{9,8},{10,11... | collective-permute-start | bytes 393224 | tf_op jit(solution)/shard_map/ppermute | solution.py:124
  68.9 3.6 %collective-permute-start.18 = (bf16[128,2048]{1,0:T(8,128)(2,1)S(1)}, bf16[128,2048]{1,0:T(8,128)(2,1)S(1)}, u32[]{:S(2)}, u32[]{:S(2)}) collective-permute-start(bf16[128,2048]{1,0:T(8,128)(2,1)S(1)} %pad_maximum_fusion.2), channel_id=1, source_target_pairs={{0,4},{4,0},{8,12},{12,8},{1,5},{5,1},{9,13},{13,9},{2,6},{6,2},{1... | collective-permute-start | bytes 1572872 | tf_op jit(solution)/shard_map/ppermute | solution.py:124
  71.5 2.0 %collective-permute-start.22 = (bf16[128,2048]{1,0:T(8,128)(2,1)S(1)}, bf16[128,2048]{1,0:T(8,128)(2,1)S(1)}, u32[]{:S(2)}, u32[]{:S(2)}) collective-permute-start(bf16[128,2048]{1,0:T(8,128)(2,1)S(1)} %pad_maximum_fusion.3), channel_id=1, source_target_pairs={{0,4},{4,0},{8,12},{12,8},{1,5},{5,1},{9,13},{13,9},{2,6},{6,2},{1... | collective-permute-start | bytes 1572872 | tf_op jit(solution)/shard_map/ppermute | solution.py:124
  74.4 16.0 %collective-permute-start.25 = (bf16[1,4,32,512]{3,2,1,0:T(8,128)(2,1)S(1)}, bf16[1,4,32,512]{3,2,1,0:T(8,128)(2,1)S(1)}, u32[]{:S(2)}, u32[]{:S(2)}) collective-permute-start(bf16[1,4,32,512]{3,2,1,0:T(8,128)(2,1)S(1)} %get-tuple-element.124), channel_id=1, source_target_pairs={{0,3},{1,2},{2,1},{3,0},{4,7},{5,6},{6,5},{7,4},{8,11},{9,10},{10,... | collective-permute-start | bytes 393224 | tf_op jit(solution)/shard_map/ppermute | solution.py:124
  77.1 13.4 %collective-permute-start.24 = (bf16[1,4,32,512]{3,2,1,0:T(8,128)(2,1)S(1)}, bf16[1,4,32,512]{3,2,1,0:T(8,128)(2,1)S(1)}, u32[]{:S(2)}, u32[]{:S(2)}) collective-permute-start(bf16[1,4,32,512]{3,2,1,0:T(8,128)(2,1)S(1)} %get-tuple-element.108), channel_id=1, source_target_pairs={{0,2},{1,3},{2,0},{3,1},{4,6},{5,7},{6,4},{7,5},{8,10},{9,11},{10,... | collective-permute-start | bytes 393224 | tf_op jit(solution)/shard_map/ppermute | solution.py:124
  77.1 8.9 %collective-permute-start.23 = (bf16[1,4,32,512]{3,2,1,0:T(8,128)(2,1)S(1)}, bf16[1,4,32,512]{3,2,1,0:T(8,128)(2,1)S(1)}, u32[]{:S(2)}, u32[]{:S(2)}) collective-permute-start(bf16[1,4,32,512]{3,2,1,0:T(8,128)(2,1)S(1)} %get-tuple-element.109), channel_id=1, source_target_pairs={{0,1},{1,0},{2,3},{3,2},{4,5},{5,4},{6,7},{7,6},{8,9},{9,8},{10,11... | collective-permute-start | bytes 393224 | tf_op jit(solution)/shard_map/ppermute | solution.py:124

commit v20 on v17

--- a/solution.py
+++ b/solution.py
@@ -80,7 +80,7 @@
         out_shape=[jax.ShapeDtypeStruct((count, width), jnp.bfloat16)] * slices,
         scratch_shapes=[pltpu.VMEM((block * order, columns), jnp.float32)],
         compiler_params=pltpu.CompilerParams(vmem_limit_bytes=32 * 1024 * 1024),
-        cost_estimate=pl.CostEstimate(flops=1000000000, bytes_accessed=0, transcendentals=0),
+        cost_estimate=pl.CostEstimate(flops=0, bytes_accessed=0, transcendentals=0),
     )(*pieces[::-1], basis, basis.T, in_basis, in_basis.T, corrections)
 
 
@@ -176,7 +176,7 @@
     for chunk, part in enumerate(parts):
         first, each = sum(parts[:chunk]), part // slices
         if chunk:
-            source, pieces[0][-1] = lax.optimization_barrier((source, pieces[0][-1]))
+            source, pieces[0][-1], train_flat = lax.optimization_barrier((source, pieces[0][-1], train_flat))
         raw = {}
         for mask in (range(slices) if chunk else reversed(range(slices))):
             block = lax.dynamic_slice_in_dim(source, first + (here ^ mask) * each, each, 0)
@@ -188,11 +188,9 @@
     spread_a1 = over_shares(first_rows[:half], shares)
     made = condition(pieces[1], basis, in_basis, corrections)
     last_rows = exchanged(made, slices)
-    first_rows[half:], last_rows[1] = lax.optimization_barrier((first_rows[half:], last_rows[1]))
     spread_a2 = over_shares(first_rows[half:], shares)
     last_rows[:half], spread_a1 = lax.optimization_barrier((last_rows[:half], spread_a1))
     place = here ^ (share // owned)
-    spread_a1 = after(spread_a1, last_rows[1])
     near_a1 = lax.optimization_barrier(jnp.concatenate(spread_a1, axis=0))
     far_a1 = crossed(near_a1, "dp", shares, 1)
     val_a1 = products(near_a1, far_a1, train_flat, shares)
@@ -209,7 +207,7 @@
     blocks = turned([jnp.concatenate(pair, axis=1) for pair in zip(part_a1, part_a2)], place)
     blocks = in_turn(blocks)
     came = exchanged(blocks, slices)
-    group = after(last_rows[half:], far_a1)
+    group = after(last_rows[half:], near_a2)
     spread_b2 = over_shares(group, shares)
     spread_b1 = after(spread_b1, came[0])
     near_b1 = lax.optimization_barrier(jnp.concatenate(spread_b1, axis=0))
@@ -229,6 +227,7 @@
     blocks = in_turn(blocks)
     left = exchanged(blocks, slices)
     last = [sum(left[mask][:, at ^ mask].astype(jnp.float32) for mask in range(slices)) for at in range(slices)]
+    came = after(came, *left[:1])
     whole = [sum(came[mask][:, at ^ mask].astype(jnp.float32) for mask in range(slices)) for at in range(slices)]
     for part, total in zip(parts, (whole, last)):
         total = jnp.stack(turned(total, here), axis=1)

time: 85.5 us -> 80.9 us (0.946)
  matrix products: 8.38 us -> 6.67 us
  starting transfers between devices: 34.3 us -> 33.2 us
  waiting for transfers between devices: 28.9 us -> 27.9 us
    dot_general x8, matrix products: 8.38 us -> 6.67 us  [products(): lax.dot_general(block, train_flat, contract, preferred_element_type=jnp.f...]
    ppermute x26, starting transfers between devices: 34.3 us -> 33.2 us  [crossed(): return lax.ppermute(value, axis, [(at, at ^ mask) for at in range(size)])]
    ppermute x26, waiting for transfers between devices: 28.9 us -> 27.9 us  [crossed(): return lax.ppermute(value, axis, [(at, at ^ mask) for at in range(size)])]
  transfers between devices with their start and end apart: 26 -> 26, of which waited for: 8 -> 8; matrix products, arithmetic and copies ran while one was open for 17% -> 15% of each run, Pallas kernels for 5% -> 6%
where the time goes in v20:
time: 80.9 us; the launch traced here: 80.6 us
  starting transfers between devices  33.2 us (41%)
  waiting for transfers between devices  27.9 us (34%)
  matrix products  6.67 us (8%)
  local copies, waits for them, and re-layouts  6.27 us (8%)
  Pallas kernels  4.47 us (6%)
  other arithmetic  1.54 us (2%)
    ppermute x26, starting transfers between devices, crossed(): return lax.ppermute(value, axis, [(at, at ^ mask) for at in range(size)])  33.2 us
    ppermute x26, waiting for transfers between devices, crossed(): return lax.ppermute(value, axis, [(at, at ^ mask) for at in range(size)])  27.9 us
    dot_general x8, matrix products, products(): lax.dot_general(block, train_flat, contract, preferred_element_type=jnp.f...  6.67 us
    unnamed x17, local copies, waits for them, and re-layouts  5.2 us
    pallas_call x2, Pallas kernels, condition_fast(): pl.pallas_call(functools.partial(condition_kernel, slices, rows_here), gr...  4.47 us
  transfers between devices with their start and end apart: 26, of which 8 were waited for; matrix products, arithmetic and copies ran while one was open for 15% of the time, Pallas kernels for 6%

profile of v20, /device:TPU:0, one launch (start us, length us, event | category | flops | bytes accessed | tf_op | source)
XLA Modules:
  0.0 80.6 jit_solution(4727176685950366088)
XLA Ops:
  0.0 1.2 %copy-done = bf16[256,16,128]{2,1,0:T(8,128)(2,1)S(1)} copy-done((bf16[256,16,128]{2,1,0:T(8,128)(2,1)S(1)}, bf16[256,16,128]{2,1,0:T(8,128)(2,1)}, u32[]{:S(2)}) %copy-start) | copy-done | bytes 1048600
  1.2 5.1 %collective-permute-start = (bf16[32,16,128]{2,1,0:T(8,128)(2,1)S(1)}, bf16[32,16,128]{2,1,0:T(8,128)(2,1)S(1)}, u32[]{:S(2)}, u32[]{:S(2)}) collective-permute-start(bf16[32,16,128]{2,1,0:T(8,128)(2,1)S(1)} %constant_dynamic-slice_fusion.7), channel_id=1, source_target_pairs={{0,3},{1,2},{2,1},{3,0},{4,7},{5,6},{6,5},{7,4},{8,11},{9,10},{10,... | collective-permute-start | bytes 393224 | tf_op jit(solution)/shard_map/ppermute | solution.py:100
  6.4 0.1 collective-permute-start.2
  6.5 0.6 collective-permute-start.1
  7.1 0.7 fusion.8
  7.8 0.1 copy.13
  7.9 0.1 copy.14
  8.0 0.1 copy.15
  8.1 0.1 copy.16
  8.2 0.0 copy-start.1
  8.2 0.0 copy-start.2
  8.2 3.5 %copy.19 = bf16[64,8,16,128]{3,1,2,0:T(8,128)(2,1)} copy(bf16[64,8,16,128]{3,2,1,0:T(8,128)(2,1)} %bitcast.54) | data formatting | bytes 4194304
  11.7 0.1 pad_maximum_fusion.15
  11.8 0.1 copy.11.refs_4_
  11.9 0.0 copy-done.1
  11.9 0.1 copy.10
  12.0 0.0 collective-permute-done.refs_0_
  12.1 3.8 %collective-permute-start.6 = (bf16[32,16,128]{2,1,0:T(8,128)(2,1)S(1)}, bf16[32,16,128]{2,1,0:T(8,128)(2,1)S(1)}, u32[]{:S(2)}, u32[]{:S(2)}) collective-permute-start(bf16[32,16,128]{2,1,0:T(8,128)(2,1)S(1)} %constant_dynamic-slice_fusion), channel_id=1, source_target_pairs={{0,3},{1,2},{2,1},{3,0},{4,7},{5,6},{6,5},{7,4},{8,11},{9,10},{10,... | collective-permute-start | bytes 393224 | tf_op jit(solution)/shard_map/ppermute | solution.py:100
  16.0 0.6 collective-permute-start.4
  16.6 7.4 %collective-permute-done.1.refs_1_ = bf16[32,16,128]{2,1,0:T(8,128)(2,1)S(1)} collective-permute-done((bf16[32,16,128]{2,1,0:T(8,128)(2,1)S(1)}, bf16[32,16,128]{2,1,0:T(8,128)(2,1)S(1)}, u32[]{:S(2)}, u32[]{:S(2)}) %collective-permute-start.1) | collective-permute-done | bytes 131104 | tf_op jit(solution)/shard_map/ppermute | solution.py:100
  24.0 2.2 %shard_map.55 = (bf16[32,2048]{1,0:T(8,128)(2,1)S(1)}, bf16[32,2048]{1,0:T(8,128)(2,1)S(1)}, bf16[32,2048]{1,0:T(8,128)(2,1)S(1)}, bf16[32,2048]{1,0:T(8,128)(2,1)S(1)}) custom-call(bf16[32,16,128]{2,1,0:T(8,128)(2,1)S(1)} %collective-permute-done.refs_0_, bf16[32,16,128]{2,1,0:T(8,128)(2,1)S(1)} %collective-permute-done.1.refs_1_, ...), custom_call_target="tpu_custom_call" | custom-call | tf_op jit(solution)/shard_map/pallas_call | solution.py:75
  26.2 0.1 collective-permute-start.3
  26.3 2.1 %collective-permute-start.10 = (bf16[32,2048]{1,0:T(8,128)(2,1)S(1)}, bf16[32,2048]{1,0:T(8,128)(2,1)S(1)}, u32[]{:S(2)}, u32[]{:S(2)}) collective-permute-start(bf16[32,2048]{1,0:T(8,128)(2,1)S(1)} %get-tuple-element.87), channel_id=1, source_target_pairs={{0,2},{1,3},{2,0},{3,1},{4,6},{5,7},{6,4},{7,5},{8,10},{9,11},{10,... | collective-permute-start | bytes 393224 | tf_op jit(solution)/shard_map/ppermute | solution.py:100
  28.4 0.0 collective-permute-done.6.refs_0_
  28.4 2.3 %collective-permute-start.11 = (bf16[32,2048]{1,0:T(8,128)(2,1)S(1)}, bf16[32,2048]{1,0:T(8,128)(2,1)S(1)}, u32[]{:S(2)}, u32[]{:S(2)}) collective-permute-start(bf16[32,2048]{1,0:T(8,128)(2,1)S(1)} %get-tuple-element.88), channel_id=1, source_target_pairs={{0,3},{1,2},{2,1},{3,0},{4,7},{5,6},{6,5},{7,4},{8,11},{9,10},{10,... | collective-permute-start | bytes 393224 | tf_op jit(solution)/shard_map/ppermute | solution.py:100
  30.7 4.7 %collective-permute-done.5.refs_1_ = bf16[32,16,128]{2,1,0:T(8,128)(2,1)S(1)} collective-permute-done((bf16[32,16,128]{2,1,0:T(8,128)(2,1)S(1)}, bf16[32,16,128]{2,1,0:T(8,128)(2,1)S(1)}, u32[]{:S(2)}, u32[]{:S(2)}) %collective-permute-start.5) | collective-permute-done | bytes 131104 | tf_op jit(solution)/shard_map/ppermute | solution.py:100
  35.4 0.0 collective-permute-done.4.refs_2_
  35.4 1.6 %collective-permute-start.8 = (bf16[64,2048]{1,0:T(8,128)(2,1)S(1)}, bf16[64,2048]{1,0:T(8,128)(2,1)S(1)}, u32[]{:S(2)}, u32[]{:S(2)}) collective-permute-start(bf16[64,2048]{1,0:T(8,128)(2,1)S(1)} %constant_dynamic-update-slice_fusion), channel_id=1, source_target_pairs={{0,8},{4,12},{8,0},{12,4},{1,9},{5,13},{9,1},{13,5},{2,10},{6,14},... | collective-permute-start | bytes 786440 | tf_op jit(solution)/shard_map/ppermute | solution.py:100
  37.0 2.2 %shard_map.56 = (bf16[32,2048]{1,0:T(8,128)(2,1)S(1)}, bf16[32,2048]{1,0:T(8,128)(2,1)S(1)}, bf16[32,2048]{1,0:T(8,128)(2,1)S(1)}, bf16[32,2048]{1,0:T(8,128)(2,1)S(1)}) custom-call(bf16[32,16,128]{2,1,0:T(8,128)(2,1)S(1)} %collective-permute-done.6.refs_0_, bf16[32,16,128]{2,1,0:T(8,128)(2,1)S(1)} %collective-permute-done.5.refs_1_, ...), custom_call_target="tpu_custom_call" | custom-call | tf_op jit(solution)/shard_map/pallas_call | solution.py:75
  39.3 0.1 collective-permute-start.7
  39.4 0.5 collective-permute-start.12
  39.9 3.2 %collective-permute-start.19 = (bf16[32,2048]{1,0:T(8,128)(2,1)S(1)}, bf16[32,2048]{1,0:T(8,128)(2,1)S(1)}, u32[]{:S(2)}, u32[]{:S(2)}) collective-permute-start(bf16[32,2048]{1,0:T(8,128)(2,1)S(1)} %get-tuple-element.96), channel_id=1, source_target_pairs={{0,2},{1,3},{2,0},{3,1},{4,6},{5,7},{6,4},{7,5},{8,10},{9,11},{10,... | collective-permute-start | bytes 393224 | tf_op jit(solution)/shard_map/ppermute | solution.py:100
  43.1 1.4 %collective-permute-start.20 = (bf16[32,2048]{1,0:T(8,128)(2,1)S(1)}, bf16[32,2048]{1,0:T(8,128)(2,1)S(1)}, u32[]{:S(2)}, u32[]{:S(2)}) collective-permute-start(bf16[32,2048]{1,0:T(8,128)(2,1)S(1)} %get-tuple-element.97), channel_id=1, source_target_pairs={{0,3},{1,2},{2,1},{3,0},{4,7},{5,6},{6,5},{7,4},{8,11},{9,10},{10,... | collective-permute-start | bytes 393224 | tf_op jit(solution)/shard_map/ppermute | solution.py:100
  44.5 0.8 %collective-permute-done.7 = bf16[32,2048]{1,0:T(8,128)(2,1)S(1)} collective-permute-done((bf16[32,2048]{1,0:T(8,128)(2,1)S(1)}, bf16[32,2048]{1,0:T(8,128)(2,1)S(1)}, u32[]{:S(2)}, u32[]{:S(2)}) %collective-permute-start.7) | collective-permute-done | bytes 131104 | tf_op jit(solution)/shard_map/ppermute | solution.py:100
  45.4 0.1 collective-permute-start.9
  45.5 1.9 %collective-permute-done.12 = bf16[64,2048]{1,0:T(8,128)(2,1)S(1)} collective-permute-done((bf16[64,2048]{1,0:T(8,128)(2,1)S(1)}, bf16[64,2048]{1,0:T(8,128)(2,1)S(1)}, u32[]{:S(2)}, u32[]{:S(2)}) %collective-permute-start.12) | collective-permute-done | bytes 262176 | tf_op jit(solution)/shard_map/ppermute | solution.py:100
  47.5 0.1 collective-permute-start.13
  47.6 0.8 %convolution_convert_fusion.5 = bf16[128,512]{1,0:T(8,128)(2,1)S(1)} fusion(bf16[128,2048]{1,0:T(8,128)(2,1)S(1)} %pad_maximum_fusion, bf16[512,2048]{1,0:T(8,128)(2,1)S(1)} %bitcast.46), kind=kOutput, calls=%fused_computation.6 | convolution fusion | flops 268500992 | bytes 2752512 | tf_op jit(solution)/shard_map/dot_general | solution.py:140
  48.4 0.8 %convolution_convert_fusion.4 = bf16[128,512]{1,0:T(8,128)(2,1)S(1)} fusion(bf16[128,2048]{1,0:T(8,128)(2,1)S(1)} %pad_maximum_fusion.1, bf16[512,2048]{1,0:T(8,128)(2,1)S(1)} %bitcast.47), kind=kOutput, calls=%fused_computation.5 | convolution fusion | flops 268500992 | bytes 2752512 | tf_op jit(solution)/shard_map/dot_general | solution.py:140
  49.3 1.6 %collective-permute-start.17 = (bf16[64,2048]{1,0:T(8,128)(2,1)S(1)}, bf16[64,2048]{1,0:T(8,128)(2,1)S(1)}, u32[]{:S(2)}, u32[]{:S(2)}) collective-permute-start(bf16[64,2048]{1,0:T(8,128)(2,1)S(1)} %constant_dynamic-update-slice_fusion.2), channel_id=1, source_target_pairs={{0,8},{4,12},{8,0},{12,4},{1,9},{5,13},{9,1},{13,5},{2,10},{6,14},... | collective-permute-start | bytes 786440 | tf_op jit(solution)/shard_map/ppermute | solution.py:100
  50.9 1.7 %collective-permute-done.19 = bf16[32,2048]{1,0:T(8,128)(2,1)S(1)} collective-permute-done((bf16[32,2048]{1,0:T(8,128)(2,1)S(1)}, bf16[32,2048]{1,0:T(8,128)(2,1)S(1)}, u32[]{:S(2)}, u32[]{:S(2)}) %collective-permute-start.19) | collective-permute-done | bytes 131104 | tf_op jit(solution)/shard_map/ppermute | solution.py:100
  52.6 0.8 collective-permute-start.21
  53.4 0.8 %convolution_convert_fusion.7 = bf16[128,512]{1,0:T(8,128)(2,1)S(1)} fusion(bf16[128,2048]{1,0:T(8,128)(2,1)S(1)} %collective-permute-done.9, bf16[512,2048]{1,0:T(8,128)(2,1)S(1)} %bitcast.48), kind=kOutput, calls=%fused_computation.8 | convolution fusion | flops 268500992 | bytes 2752512 | tf_op jit(solution)/shard_map/dot_general | solution.py:140
  54.2 0.8 %convolution_convert_fusion.6 = bf16[128,512]{1,0:T(8,128)(2,1)S(1)} fusion(bf16[128,2048]{1,0:T(8,128)(2,1)S(1)} %collective-permute-done.13, bf16[512,2048]{1,0:T(8,128)(2,1)S(1)} %bitcast.49), kind=kOutput, calls=%fused_computation.7 | convolution fusion | flops 268500992 | bytes 2752512 | tf_op jit(solution)/shard_map/dot_general | solution.py:140
  55.2 1.4 %collective-permute-start.16 = (bf16[1,4,32,512]{3,2,1,0:T(8,128)(2,1)S(1)}, bf16[1,4,32,512]{3,2,1,0:T(8,128)(2,1)S(1)}, u32[]{:S(2)}, u32[]{:S(2)}) collective-permute-start(bf16[1,4,32,512]{3,2,1,0:T(8,128)(2,1)S(1)} %get-tuple-element.123), channel_id=1, source_target_pairs={{0,3},{1,2},{2,1},{3,0},{4,7},{5,6},{6,5},{7,4},{8,11},{9,10},{10,... | collective-permute-start | bytes 393224 | tf_op jit(solution)/shard_map/ppermute | solution.py:100
  56.6 2.3 %collective-permute-start.15 = (bf16[1,4,32,512]{3,2,1,0:T(8,128)(2,1)S(1)}, bf16[1,4,32,512]{3,2,1,0:T(8,128)(2,1)S(1)}, u32[]{:S(2)}, u32[]{:S(2)}) collective-permute-start(bf16[1,4,32,512]{3,2,1,0:T(8,128)(2,1)S(1)} %get-tuple-element.89), channel_id=1, source_target_pairs={{0,2},{1,3},{2,0},{3,1},{4,6},{5,7},{6,4},{7,5},{8,10},{9,11},{10,... | collective-permute-start | bytes 393224 | tf_op jit(solution)/shard_map/ppermute | solution.py:100
  58.9 0.8 %collective-permute-start.14 = (bf16[1,4,32,512]{3,2,1,0:T(8,128)(2,1)S(1)}, bf16[1,4,32,512]{3,2,1,0:T(8,128)(2,1)S(1)}, u32[]{:S(2)}, u32[]{:S(2)}) collective-permute-start(bf16[1,4,32,512]{3,2,1,0:T(8,128)(2,1)S(1)} %get-tuple-element.90), channel_id=1, source_target_pairs={{0,1},{1,0},{2,3},{3,2},{4,5},{5,4},{6,7},{7,6},{8,9},{9,8},{10,11... | collective-permute-start | bytes 393224 | tf_op jit(solution)/shard_map/ppermute | solution.py:100
  59.8 0.1 collective-permute-start.18
  59.9 0.8 %convolution_convert_fusion.1 = bf16[128,512]{1,0:T(8,128)(2,1)S(1)} fusion(bf16[128,2048]{1,0:T(8,128)(2,1)S(1)} %pad_maximum_fusion.2, bf16[512,2048]{1,0:T(8,128)(2,1)S(1)} %bitcast.50), kind=kOutput, calls=%fused_computation.2 | convolution fusion | flops 268500992 | bytes 2752512 | tf_op jit(solution)/shard_map/dot_general | solution.py:140
  60.7 3.0 %collective-permute-done.21 = bf16[64,2048]{1,0:T(8,128)(2,1)S(1)} collective-permute-done((bf16[64,2048]{1,0:T(8,128)(2,1)S(1)}, bf16[64,2048]{1,0:T(8,128)(2,1)S(1)}, u32[]{:S(2)}, u32[]{:S(2)}) %collective-permute-start.21) | collective-permute-done | bytes 262176 | tf_op jit(solution)/shard_map/ppermute | solution.py:100
  63.7 0.1 collective-permute-start.22
  63.8 0.8 %convolution_convert_fusion = bf16[128,512]{1,0:T(8,128)(2,1)S(1)} fusion(bf16[128,2048]{1,0:T(8,128)(2,1)S(1)} %pad_maximum_fusion.3, bf16[512,2048]{1,0:T(8,128)(2,1)S(1)} %bitcast.51), kind=kOutput, calls=%fused_computation.1 | convolution fusion | flops 268500992 | bytes 2752512 | tf_op jit(solution)/shard_map/dot_general | solution.py:140
  64.7 0.8 %convolution_convert_fusion.3 = bf16[128,512]{1,0:T(8,128)(2,1)S(1)} fusion(bf16[128,2048]{1,0:T(8,128)(2,1)S(1)} %collective-permute-done.18, bf16[512,2048]{1,0:T(8,128)(2,1)S(1)} %bitcast.52), kind=kOutput, calls=%fused_computation.4 | convolution fusion | flops 268500992 | bytes 2752512 | tf_op jit(solution)/shard_map/dot_general | solution.py:140
  65.5 0.2 collective-permute-done.22
  65.7 0.8 %convolution_convert_fusion.2 = bf16[128,512]{1,0:T(8,128)(2,1)S(1)} fusion(bf16[128,2048]{1,0:T(8,128)(2,1)S(1)} %collective-permute-done.22, bf16[512,2048]{1,0:T(8,128)(2,1)S(1)} %bitcast.53), kind=kOutput, calls=%fused_computation.3 | convolution fusion | flops 268500992 | bytes 2752512 | tf_op jit(solution)/shard_map/dot_general | solution.py:140
  66.6 0.1 broadcast_select_fusion.9
  66.6 1.8 %collective-permute-start.24 = (bf16[1,4,32,512]{3,2,1,0:T(8,128)(2,1)S(1)}, bf16[1,4,32,512]{3,2,1,0:T(8,128)(2,1)S(1)}, u32[]{:S(2)}, u32[]{:S(2)}) collective-permute-start(bf16[1,4,32,512]{3,2,1,0:T(8,128)(2,1)S(1)} %get-tuple-element.102), channel_id=1, source_target_pairs={{0,2},{1,3},{2,0},{3,1},{4,6},{5,7},{6,4},{7,5},{8,10},{9,11},{10,... | collective-permute-start | bytes 393224 | tf_op jit(solution)/shard_map/ppermute | solution.py:100
  68.4 1.0 %collective-permute-start.23 = (bf16[1,4,32,512]{3,2,1,0:T(8,128)(2,1)S(1)}, bf16[1,4,32,512]{3,2,1,0:T(8,128)(2,1)S(1)}, u32[]{:S(2)}, u32[]{:S(2)}) collective-permute-start(bf16[1,4,32,512]{3,2,1,0:T(8,128)(2,1)S(1)} %get-tuple-element.103), channel_id=1, source_target_pairs={{0,1},{1,0},{2,3},{3,2},{4,5},{5,4},{6,7},{7,6},{8,9},{9,8},{10,11... | collective-permute-start | bytes 393224 | tf_op jit(solution)/shard_map/ppermute | solution.py:100
  69.4 1.8 %collective-permute-start.25 = (bf16[1,4,32,512]{3,2,1,0:T(8,128)(2,1)S(1)}, bf16[1,4,32,512]{3,2,1,0:T(8,128)(2,1)S(1)}, u32[]{:S(2)}, u32[]{:S(2)}) collective-permute-start(bf16[1,4,32,512]{3,2,1,0:T(8,128)(2,1)S(1)} %get-tuple-element.122), channel_id=1, source_target_pairs={{0,3},{1,2},{2,1},{3,0},{4,7},{5,6},{6,5},{7,4},{8,11},{9,10},{10,... | collective-permute-start | bytes 393224 | tf_op jit(solution)/shard_map/ppermute | solution.py:100
  71.2 0.1 broadcast_select_fusion.31
  71.3 8.3 %collective-permute-done.23 = bf16[1,4,32,512]{3,2,1,0:T(8,128)(2,1)S(1)} collective-permute-done((bf16[1,4,32,512]{3,2,1,0:T(8,128)(2,1)S(1)}, bf16[1,4,32,512]{3,2,1,0:T(8,128)(2,1)S(1)}, u32[]{:S(2)}, u32[]{:S(2)}) %collective-permute-start.23) | collective-permute-done | bytes 131104 | tf_op jit(solution)/shard_map/ppermute | solution.py:100
  79.5 0.1 broadcast_select_fusion.27
  79.6 0.1 broadcast_select_fusion.26
  79.7 0.8 %maximum_bitcast_fusion = f32[256,512]{1,0:T(8,128)} fusion(f32[1,128,512]{2,1,0:T(8,128)S(1)} %bitcast.56, f32[1,128,512]{2,1,0:T(8,128)S(1)} %bitcast.55), kind=kLoop, calls=%fused_computation.13 | loop fusion | flops 131072 | bytes 1048576 | tf_op jit(solution)/shard_map/reshape | solution.py:236
  (53 shorter events, 0.7 us)
Async XLA Ops:
  0.0 1.2 %copy-start = (bf16[256,16,128]{2,1,0:T(8,128)(2,1)S(1)}, bf16[256,16,128]{2,1,0:T(8,128)(2,1)}, u32[]{:S(2)}) copy-start(bf16[256,16,128]{2,1,0:T(8,128)(2,1)} %param.5) | copy-start | bytes 3145732
  1.2 10.8 %collective-permute-start = (bf16[32,16,128]{2,1,0:T(8,128)(2,1)S(1)}, bf16[32,16,128]{2,1,0:T(8,128)(2,1)S(1)}, u32[]{:S(2)}, u32[]{:S(2)}) collective-permute-start(bf16[32,16,128]{2,1,0:T(8,128)(2,1)S(1)} %constant_dynamic-slice_fusion.7), channel_id=1, source_target_pairs={{0,3},{1,2},{2,1},{3,0},{4,7},{5,6},{6,5},{7,4},{8,11},{9,10},{10,... | collective-permute-start | bytes 393224 | tf_op jit(solution)/shard_map/ppermute | solution.py:100
  6.4 10.2 %collective-permute-start.2 = (bf16[32,16,128]{2,1,0:T(8,128)(2,1)S(1)}, bf16[32,16,128]{2,1,0:T(8,128)(2,1)S(1)}, u32[]{:S(2)}, u32[]{:S(2)}) collective-permute-start(bf16[32,16,128]{2,1,0:T(8,128)(2,1)S(1)} %constant_dynamic-slice_fusion.5), channel_id=1, source_target_pairs={{0,1},{1,0},{2,3},{3,2},{4,5},{5,4},{6,7},{7,6},{8,9},{9,8},{10,11... | collective-permute-start | bytes 393224 | tf_op jit(solution)/shard_map/ppermute | solution.py:100
  6.5 17.5 %collective-permute-start.1 = (bf16[32,16,128]{2,1,0:T(8,128)(2,1)S(1)}, bf16[32,16,128]{2,1,0:T(8,128)(2,1)S(1)}, u32[]{:S(2)}, u32[]{:S(2)}) collective-permute-start(bf16[32,16,128]{2,1,0:T(8,128)(2,1)S(1)} %constant_dynamic-slice_fusion.6), channel_id=1, source_target_pairs={{0,2},{1,3},{2,0},{3,1},{4,6},{5,7},{6,4},{7,5},{8,10},{9,11},{10,... | collective-permute-start | bytes 393224 | tf_op jit(solution)/shard_map/ppermute | solution.py:100
  8.2 3.7 %copy-start.1 = (f32[128,128]{1,0:T(8,128)S(1)}, f32[128,128]{1,0:T(8,128)}, u32[]{:S(2)}) copy-start(f32[128,128]{1,0:T(8,128)} %refs_6_.3) | copy-start | bytes 196612
  8.2 15.8 %copy-start.2 = (f32[64,128]{1,0:T(8,128)S(1)}, f32[64,128]{1,0:T(8,128)}, u32[]{:S(2)}) copy-start(f32[64,128]{1,0:T(8,128)} %refs_8_.3) | copy-start | bytes 98308
  12.1 16.3 %collective-permute-start.6 = (bf16[32,16,128]{2,1,0:T(8,128)(2,1)S(1)}, bf16[32,16,128]{2,1,0:T(8,128)(2,1)S(1)}, u32[]{:S(2)}, u32[]{:S(2)}) collective-permute-start(bf16[32,16,128]{2,1,0:T(8,128)(2,1)S(1)} %constant_dynamic-slice_fusion), channel_id=1, source_target_pairs={{0,3},{1,2},{2,1},{3,0},{4,7},{5,6},{6,5},{7,4},{8,11},{9,10},{10,... | collective-permute-start | bytes 393224 | tf_op jit(solution)/shard_map/ppermute | solution.py:100
  16.0 19.4 %collective-permute-start.5 = (bf16[32,16,128]{2,1,0:T(8,128)(2,1)S(1)}, bf16[32,16,128]{2,1,0:T(8,128)(2,1)S(1)}, u32[]{:S(2)}, u32[]{:S(2)}) collective-permute-start(bf16[32,16,128]{2,1,0:T(8,128)(2,1)S(1)} %constant_dynamic-slice_fusion.1), channel_id=1, source_target_pairs={{0,2},{1,3},{2,0},{3,1},{4,6},{5,7},{6,4},{7,5},{8,10},{9,11},{10,... | collective-permute-start | bytes 393224 | tf_op jit(solution)/shard_map/ppermute | solution.py:100
  16.0 19.4 %collective-permute-start.4 = (bf16[32,16,128]{2,1,0:T(8,128)(2,1)S(1)}, bf16[32,16,128]{2,1,0:T(8,128)(2,1)S(1)}, u32[]{:S(2)}, u32[]{:S(2)}) collective-permute-start(bf16[32,16,128]{2,1,0:T(8,128)(2,1)S(1)} %constant_dynamic-slice_fusion.2), channel_id=1, source_target_pairs={{0,1},{1,0},{2,3},{3,2},{4,5},{5,4},{6,7},{7,6},{8,9},{9,8},{10,11... | collective-permute-start | bytes 393224 | tf_op jit(solution)/shard_map/ppermute | solution.py:100
  26.2 9.1 %collective-permute-start.3 = (bf16[32,2048]{1,0:T(8,128)(2,1)S(1)}, bf16[32,2048]{1,0:T(8,128)(2,1)S(1)}, u32[]{:S(2)}, u32[]{:S(2)}) collective-permute-start(bf16[32,2048]{1,0:T(8,128)(2,1)S(1)} %get-tuple-element.67), channel_id=1, source_target_pairs={{0,1},{1,0},{2,3},{3,2},{4,5},{5,4},{6,7},{7,6},{8,9},{9,8},{10,11... | collective-permute-start | bytes 393224 | tf_op jit(solution)/shard_map/ppermute | solution.py:100
  26.3 13.0 %collective-permute-start.10 = (bf16[32,2048]{1,0:T(8,128)(2,1)S(1)}, bf16[32,2048]{1,0:T(8,128)(2,1)S(1)}, u32[]{:S(2)}, u32[]{:S(2)}) collective-permute-start(bf16[32,2048]{1,0:T(8,128)(2,1)S(1)} %get-tuple-element.87), channel_id=1, source_target_pairs={{0,2},{1,3},{2,0},{3,1},{4,6},{5,7},{6,4},{7,5},{8,10},{9,11},{10,... | collective-permute-start | bytes 393224 | tf_op jit(solution)/shard_map/ppermute | solution.py:100
  28.4 10.9 %collective-permute-start.11 = (bf16[32,2048]{1,0:T(8,128)(2,1)S(1)}, bf16[32,2048]{1,0:T(8,128)(2,1)S(1)}, u32[]{:S(2)}, u32[]{:S(2)}) collective-permute-start(bf16[32,2048]{1,0:T(8,128)(2,1)S(1)} %get-tuple-element.88), channel_id=1, source_target_pairs={{0,3},{1,2},{2,1},{3,0},{4,7},{5,6},{6,5},{7,4},{8,11},{9,10},{10,... | collective-permute-start | bytes 393224 | tf_op jit(solution)/shard_map/ppermute | solution.py:100
  35.4 10.0 %collective-permute-start.8 = (bf16[64,2048]{1,0:T(8,128)(2,1)S(1)}, bf16[64,2048]{1,0:T(8,128)(2,1)S(1)}, u32[]{:S(2)}, u32[]{:S(2)}) collective-permute-start(bf16[64,2048]{1,0:T(8,128)(2,1)S(1)} %constant_dynamic-update-slice_fusion), channel_id=1, source_target_pairs={{0,8},{4,12},{8,0},{12,4},{1,9},{5,13},{9,1},{13,5},{2,10},{6,14},... | collective-permute-start | bytes 786440 | tf_op jit(solution)/shard_map/ppermute | solution.py:100
  39.3 6.1 %collective-permute-start.7 = (bf16[32,2048]{1,0:T(8,128)(2,1)S(1)}, bf16[32,2048]{1,0:T(8,128)(2,1)S(1)}, u32[]{:S(2)}, u32[]{:S(2)}) collective-permute-start(bf16[32,2048]{1,0:T(8,128)(2,1)S(1)} %get-tuple-element.81), channel_id=1, source_target_pairs={{0,1},{1,0},{2,3},{3,2},{4,5},{5,4},{6,7},{7,6},{8,9},{9,8},{10,11... | collective-permute-start | bytes 393224 | tf_op jit(solution)/shard_map/ppermute | solution.py:100
  39.4 8.0 %collective-permute-start.12 = (bf16[64,2048]{1,0:T(8,128)(2,1)S(1)}, bf16[64,2048]{1,0:T(8,128)(2,1)S(1)}, u32[]{:S(2)}, u32[]{:S(2)}) collective-permute-start(bf16[64,2048]{1,0:T(8,128)(2,1)S(1)} %pad_maximum_fusion.4), channel_id=1, source_target_pairs={{0,8},{4,12},{8,0},{12,4},{1,9},{5,13},{9,1},{13,5},{2,10},{6,14},... | collective-permute-start | bytes 786440 | tf_op jit(solution)/shard_map/ppermute | solution.py:100
  39.9 7.6 %copy-start.3 = (bf16[64,8,16,128]{3,1,2,0:T(8,128)(2,1)S(1)}, bf16[64,8,16,128]{3,1,2,0:T(8,128)(2,1)}, u32[]{:S(2)}) copy-start(bf16[64,8,16,128]{3,1,2,0:T(8,128)(2,1)} %copy.19) | copy-start | bytes 6291460
  39.9 12.6 %collective-permute-start.19 = (bf16[32,2048]{1,0:T(8,128)(2,1)S(1)}, bf16[32,2048]{1,0:T(8,128)(2,1)S(1)}, u32[]{:S(2)}, u32[]{:S(2)}) collective-permute-start(bf16[32,2048]{1,0:T(8,128)(2,1)S(1)} %get-tuple-element.96), channel_id=1, source_target_pairs={{0,2},{1,3},{2,0},{3,1},{4,6},{5,7},{6,4},{7,5},{8,10},{9,11},{10,... | collective-permute-start | bytes 393224 | tf_op jit(solution)/shard_map/ppermute | solution.py:100
  43.1 9.5 %collective-permute-start.20 = (bf16[32,2048]{1,0:T(8,128)(2,1)S(1)}, bf16[32,2048]{1,0:T(8,128)(2,1)S(1)}, u32[]{:S(2)}, u32[]{:S(2)}) collective-permute-start(bf16[32,2048]{1,0:T(8,128)(2,1)S(1)} %get-tuple-element.97), channel_id=1, source_target_pairs={{0,3},{1,2},{2,1},{3,0},{4,7},{5,6},{6,5},{7,4},{8,11},{9,10},{10,... | collective-permute-start | bytes 393224 | tf_op jit(solution)/shard_map/ppermute | solution.py:100
  45.4 8.0 %collective-permute-start.9 = (bf16[128,2048]{1,0:T(8,128)(2,1)S(1)}, bf16[128,2048]{1,0:T(8,128)(2,1)S(1)}, u32[]{:S(2)}, u32[]{:S(2)}) collective-permute-start(bf16[128,2048]{1,0:T(8,128)(2,1)S(1)} %pad_maximum_fusion), channel_id=1, source_target_pairs={{0,4},{4,0},{8,12},{12,8},{1,5},{5,1},{9,13},{13,9},{2,6},{6,2},{1... | collective-permute-start | bytes 1572872 | tf_op jit(solution)/shard_map/ppermute | solution.py:100
  47.5 6.8 %collective-permute-start.13 = (bf16[128,2048]{1,0:T(8,128)(2,1)S(1)}, bf16[128,2048]{1,0:T(8,128)(2,1)S(1)}, u32[]{:S(2)}, u32[]{:S(2)}) collective-permute-start(bf16[128,2048]{1,0:T(8,128)(2,1)S(1)} %pad_maximum_fusion.1), channel_id=1, source_target_pairs={{0,4},{4,0},{8,12},{12,8},{1,5},{5,1},{9,13},{13,9},{2,6},{6,2},{1... | collective-permute-start | bytes 1572872 | tf_op jit(solution)/shard_map/ppermute | solution.py:100
  49.3 10.4 %collective-permute-start.17 = (bf16[64,2048]{1,0:T(8,128)(2,1)S(1)}, bf16[64,2048]{1,0:T(8,128)(2,1)S(1)}, u32[]{:S(2)}, u32[]{:S(2)}) collective-permute-start(bf16[64,2048]{1,0:T(8,128)(2,1)S(1)} %constant_dynamic-update-slice_fusion.2), channel_id=1, source_target_pairs={{0,8},{4,12},{8,0},{12,4},{1,9},{5,13},{9,1},{13,5},{2,10},{6,14},... | collective-permute-start | bytes 786440 | tf_op jit(solution)/shard_map/ppermute | solution.py:100
  52.6 11.1 %collective-permute-start.21 = (bf16[64,2048]{1,0:T(8,128)(2,1)S(1)}, bf16[64,2048]{1,0:T(8,128)(2,1)S(1)}, u32[]{:S(2)}, u32[]{:S(2)}) collective-permute-start(bf16[64,2048]{1,0:T(8,128)(2,1)S(1)} %constant_dynamic-update-slice_fusion.4), channel_id=1, source_target_pairs={{0,8},{4,12},{8,0},{12,4},{1,9},{5,13},{9,1},{13,5},{2,10},{6,14},... | collective-permute-start | bytes 786440 | tf_op jit(solution)/shard_map/ppermute | solution.py:100
  55.2 16.0 %collective-permute-start.16 = (bf16[1,4,32,512]{3,2,1,0:T(8,128)(2,1)S(1)}, bf16[1,4,32,512]{3,2,1,0:T(8,128)(2,1)S(1)}, u32[]{:S(2)}, u32[]{:S(2)}) collective-permute-start(bf16[1,4,32,512]{3,2,1,0:T(8,128)(2,1)S(1)} %get-tuple-element.123), channel_id=1, source_target_pairs={{0,3},{1,2},{2,1},{3,0},{4,7},{5,6},{6,5},{7,4},{8,11},{9,10},{10,... | collective-permute-start | bytes 393224 | tf_op jit(solution)/shard_map/ppermute | solution.py:100
  56.6 14.6 %collective-permute-start.15 = (bf16[1,4,32,512]{3,2,1,0:T(8,128)(2,1)S(1)}, bf16[1,4,32,512]{3,2,1,0:T(8,128)(2,1)S(1)}, u32[]{:S(2)}, u32[]{:S(2)}) collective-permute-start(bf16[1,4,32,512]{3,2,1,0:T(8,128)(2,1)S(1)} %get-tuple-element.89), channel_id=1, source_target_pairs={{0,2},{1,3},{2,0},{3,1},{4,6},{5,7},{6,4},{7,5},{8,10},{9,11},{10,... | collective-permute-start | bytes 393224 | tf_op jit(solution)/shard_map/ppermute | solution.py:100
  58.9 10.5 %collective-permute-start.14 = (bf16[1,4,32,512]{3,2,1,0:T(8,128)(2,1)S(1)}, bf16[1,4,32,512]{3,2,1,0:T(8,128)(2,1)S(1)}, u32[]{:S(2)}, u32[]{:S(2)}) collective-permute-start(bf16[1,4,32,512]{3,2,1,0:T(8,128)(2,1)S(1)} %get-tuple-element.90), channel_id=1, source_target_pairs={{0,1},{1,0},{2,3},{3,2},{4,5},{5,4},{6,7},{7,6},{8,9},{9,8},{10,11... | collective-permute-start | bytes 393224 | tf_op jit(solution)/shard_map/ppermute | solution.py:100
  59.8 4.9 %collective-permute-start.18 = (bf16[128,2048]{1,0:T(8,128)(2,1)S(1)}, bf16[128,2048]{1,0:T(8,128)(2,1)S(1)}, u32[]{:S(2)}, u32[]{:S(2)}) collective-permute-start(bf16[128,2048]{1,0:T(8,128)(2,1)S(1)} %pad_maximum_fusion.2), channel_id=1, source_target_pairs={{0,4},{4,0},{8,12},{12,8},{1,5},{5,1},{9,13},{13,9},{2,6},{6,2},{1... | collective-permute-start | bytes 1572872 | tf_op jit(solution)/shard_map/ppermute | solution.py:100
  63.7 2.0 %collective-permute-start.22 = (bf16[128,2048]{1,0:T(8,128)(2,1)S(1)}, bf16[128,2048]{1,0:T(8,128)(2,1)S(1)}, u32[]{:S(2)}, u32[]{:S(2)}) collective-permute-start(bf16[128,2048]{1,0:T(8,128)(2,1)S(1)} %pad_maximum_fusion.3), channel_id=1, source_target_pairs={{0,4},{4,0},{8,12},{12,8},{1,5},{5,1},{9,13},{13,9},{2,6},{6,2},{1... | collective-permute-start | bytes 1572872 | tf_op jit(solution)/shard_map/ppermute | solution.py:100
  66.6 12.9 %collective-permute-start.24 = (bf16[1,4,32,512]{3,2,1,0:T(8,128)(2,1)S(1)}, bf16[1,4,32,512]{3,2,1,0:T(8,128)(2,1)S(1)}, u32[]{:S(2)}, u32[]{:S(2)}) collective-permute-start(bf16[1,4,32,512]{3,2,1,0:T(8,128)(2,1)S(1)} %get-tuple-element.102), channel_id=1, source_target_pairs={{0,2},{1,3},{2,0},{3,1},{4,6},{5,7},{6,4},{7,5},{8,10},{9,11},{10,... | collective-permute-start | bytes 393224 | tf_op jit(solution)/shard_map/ppermute | solution.py:100
  68.4 11.1 %collective-permute-start.23 = (bf16[1,4,32,512]{3,2,1,0:T(8,128)(2,1)S(1)}, bf16[1,4,32,512]{3,2,1,0:T(8,128)(2,1)S(1)}, u32[]{:S(2)}, u32[]{:S(2)}) collective-permute-start(bf16[1,4,32,512]{3,2,1,0:T(8,128)(2,1)S(1)} %get-tuple-element.103), channel_id=1, source_target_pairs={{0,1},{1,0},{2,3},{3,2},{4,5},{5,4},{6,7},{7,6},{8,9},{9,8},{10,11... | collective-permute-start | bytes 393224 | tf_op jit(solution)/shard_map/ppermute | solution.py:100
  69.4 10.1 %collective-permute-start.25 = (bf16[1,4,32,512]{3,2,1,0:T(8,128)(2,1)S(1)}, bf16[1,4,32,512]{3,2,1,0:T(8,128)(2,1)S(1)}, u32[]{:S(2)}, u32[]{:S(2)}) collective-permute-start(bf16[1,4,32,512]{3,2,1,0:T(8,128)(2,1)S(1)} %get-tuple-element.122), channel_id=1, source_target_pairs={{0,3},{1,2},{2,1},{3,0},{4,7},{5,6},{6,5},{7,4},{8,11},{9,10},{10,... | collective-permute-start | bytes 393224 | tf_op jit(solution)/shard_map/ppermute | solution.py:100

commit v21 on v20

--- a/solution.py
+++ b/solution.py
@@ -224,10 +224,9 @@
     part_b2 = [jnp.concatenate(part_b2[at * owned:(at + 1) * owned]) for at in range(slices)]
     part_b2 = [value.reshape(owned, half, -1, train_count) for value in part_b2]
     blocks = turned([jnp.concatenate(pair, axis=1) for pair in zip(part_b1, part_b2)], place)
-    blocks = in_turn(blocks)
+    blocks = in_turn(blocks[::-1])[::-1]
     left = exchanged(blocks, slices)
     last = [sum(left[mask][:, at ^ mask].astype(jnp.float32) for mask in range(slices)) for at in range(slices)]
-    came = after(came, *left[:1])
     whole = [sum(came[mask][:, at ^ mask].astype(jnp.float32) for mask in range(slices)) for at in range(slices)]
     for part, total in zip(parts, (whole, last)):
         total = jnp.stack(turned(total, here), axis=1)

time: 80.9 us -> 81.5 us (level)
  transfers between devices with their start and end apart: 26 -> 26, of which waited for: 8 -> 9; matrix products, arithmetic and copies ran while one was open for 15% -> 15% of each run, Pallas kernels for 6% -> 6%
where the time goes in v21:
time: 81.5 us; the launch traced here: 81.3 us
  starting transfers between devices  33.2 us (41%)
  waiting for transfers between devices  28.6 us (35%)
  matrix products  6.67 us (8%)
  local copies, waits for them, and re-layouts  6.27 us (8%)
  Pallas kernels  4.47 us (5%)
  other arithmetic  1.54 us (2%)
    ppermute x26, starting transfers between devices, crossed(): return lax.ppermute(value, axis, [(at, at ^ mask) for at in range(size)])  33.2 us
    ppermute x26, waiting for transfers between devices, crossed(): return lax.ppermute(value, axis, [(at, at ^ mask) for at in range(size)])  28.6 us
    dot_general x8, matrix products, products(): lax.dot_general(block, train_flat, contract, preferred_element_type=jnp.f...  6.67 us
    unnamed x17, local copies, waits for them, and re-layouts  5.2 us
    pallas_call x2, Pallas kernels, condition_fast(): pl.pallas_call(functools.partial(condition_kernel, slices, rows_here), gr...  4.47 us
  transfers between devices with their start and end apart: 26, of which 9 were waited for; matrix products, arithmetic and copies ran while one was open for 15% of the time, Pallas kernels for 6%

profile of v21, /device:TPU:0, one launch (start us, length us, event | category | flops | bytes accessed | tf_op | source)
XLA Modules:
  0.0 81.3 jit_solution(11819469565220403087)
XLA Ops:
  0.0 1.2 %copy-done = bf16[256,16,128]{2,1,0:T(8,128)(2,1)S(1)} copy-done((bf16[256,16,128]{2,1,0:T(8,128)(2,1)S(1)}, bf16[256,16,128]{2,1,0:T(8,128)(2,1)}, u32[]{:S(2)}) %copy-start) | copy-done | bytes 1048600
  1.2 5.1 %collective-permute-start = (bf16[32,16,128]{2,1,0:T(8,128)(2,1)S(1)}, bf16[32,16,128]{2,1,0:T(8,128)(2,1)S(1)}, u32[]{:S(2)}, u32[]{:S(2)}) collective-permute-start(bf16[32,16,128]{2,1,0:T(8,128)(2,1)S(1)} %constant_dynamic-slice_fusion.7), channel_id=1, source_target_pairs={{0,3},{1,2},{2,1},{3,0},{4,7},{5,6},{6,5},{7,4},{8,11},{9,10},{10,... | collective-permute-start | bytes 393224 | tf_op jit(solution)/shard_map/ppermute | solution.py:100
  6.4 0.1 collective-permute-start.2
  6.5 0.6 collective-permute-start.1
  7.1 0.7 fusion.8
  7.8 0.1 copy.13
  7.9 0.1 copy.14
  8.0 0.1 copy.15
  8.1 0.1 copy.16
  8.2 0.0 copy-start.1
  8.2 0.0 copy-start.2
  8.2 3.5 %copy.19 = bf16[64,8,16,128]{3,1,2,0:T(8,128)(2,1)} copy(bf16[64,8,16,128]{3,2,1,0:T(8,128)(2,1)} %bitcast.54) | data formatting | bytes 4194304
  11.7 0.1 pad_maximum_fusion.15
  11.8 0.1 copy.11.refs_4_
  11.9 0.0 copy-done.1
  11.9 0.1 copy.10
  12.0 0.0 collective-permute-done.refs_0_
  12.1 3.8 %collective-permute-start.6 = (bf16[32,16,128]{2,1,0:T(8,128)(2,1)S(1)}, bf16[32,16,128]{2,1,0:T(8,128)(2,1)S(1)}, u32[]{:S(2)}, u32[]{:S(2)}) collective-permute-start(bf16[32,16,128]{2,1,0:T(8,128)(2,1)S(1)} %constant_dynamic-slice_fusion), channel_id=1, source_target_pairs={{0,3},{1,2},{2,1},{3,0},{4,7},{5,6},{6,5},{7,4},{8,11},{9,10},{10,... | collective-permute-start | bytes 393224 | tf_op jit(solution)/shard_map/ppermute | solution.py:100
  16.0 0.0 collective-permute-start.5
  16.0 0.6 collective-permute-start.4
  16.6 7.4 %collective-permute-done.1.refs_1_ = bf16[32,16,128]{2,1,0:T(8,128)(2,1)S(1)} collective-permute-done((bf16[32,16,128]{2,1,0:T(8,128)(2,1)S(1)}, bf16[32,16,128]{2,1,0:T(8,128)(2,1)S(1)}, u32[]{:S(2)}, u32[]{:S(2)}) %collective-permute-start.1) | collective-permute-done | bytes 131104 | tf_op jit(solution)/shard_map/ppermute | solution.py:100
  24.0 2.2 %shard_map.55 = (bf16[32,2048]{1,0:T(8,128)(2,1)S(1)}, bf16[32,2048]{1,0:T(8,128)(2,1)S(1)}, bf16[32,2048]{1,0:T(8,128)(2,1)S(1)}, bf16[32,2048]{1,0:T(8,128)(2,1)S(1)}) custom-call(bf16[32,16,128]{2,1,0:T(8,128)(2,1)S(1)} %collective-permute-done.refs_0_, bf16[32,16,128]{2,1,0:T(8,128)(2,1)S(1)} %collective-permute-done.1.refs_1_, ...), custom_call_target="tpu_custom_call" | custom-call | tf_op jit(solution)/shard_map/pallas_call | solution.py:75
  26.2 0.1 collective-permute-start.3
  26.3 2.1 %collective-permute-start.10 = (bf16[32,2048]{1,0:T(8,128)(2,1)S(1)}, bf16[32,2048]{1,0:T(8,128)(2,1)S(1)}, u32[]{:S(2)}, u32[]{:S(2)}) collective-permute-start(bf16[32,2048]{1,0:T(8,128)(2,1)S(1)} %get-tuple-element.83), channel_id=1, source_target_pairs={{0,2},{1,3},{2,0},{3,1},{4,6},{5,7},{6,4},{7,5},{8,10},{9,11},{10,... | collective-permute-start | bytes 393224 | tf_op jit(solution)/shard_map/ppermute | solution.py:100
  28.4 2.3 %collective-permute-start.11 = (bf16[32,2048]{1,0:T(8,128)(2,1)S(1)}, bf16[32,2048]{1,0:T(8,128)(2,1)S(1)}, u32[]{:S(2)}, u32[]{:S(2)}) collective-permute-start(bf16[32,2048]{1,0:T(8,128)(2,1)S(1)} %get-tuple-element.84), channel_id=1, source_target_pairs={{0,3},{1,2},{2,1},{3,0},{4,7},{5,6},{6,5},{7,4},{8,11},{9,10},{10,... | collective-permute-start | bytes 393224 | tf_op jit(solution)/shard_map/ppermute | solution.py:100
  30.7 4.7 %collective-permute-done.5.refs_1_ = bf16[32,16,128]{2,1,0:T(8,128)(2,1)S(1)} collective-permute-done((bf16[32,16,128]{2,1,0:T(8,128)(2,1)S(1)}, bf16[32,16,128]{2,1,0:T(8,128)(2,1)S(1)}, u32[]{:S(2)}, u32[]{:S(2)}) %collective-permute-start.5) | collective-permute-done | bytes 131104 | tf_op jit(solution)/shard_map/ppermute | solution.py:100
  35.4 1.6 %collective-permute-start.8 = (bf16[64,2048]{1,0:T(8,128)(2,1)S(1)}, bf16[64,2048]{1,0:T(8,128)(2,1)S(1)}, u32[]{:S(2)}, u32[]{:S(2)}) collective-permute-start(bf16[64,2048]{1,0:T(8,128)(2,1)S(1)} %constant_dynamic-update-slice_fusion), channel_id=1, source_target_pairs={{0,8},{4,12},{8,0},{12,4},{1,9},{5,13},{9,1},{13,5},{2,10},{6,14},... | collective-permute-start | bytes 786440 | tf_op jit(solution)/shard_map/ppermute | solution.py:100
  37.0 2.2 %shard_map.56 = (bf16[32,2048]{1,0:T(8,128)(2,1)S(1)}, bf16[32,2048]{1,0:T(8,128)(2,1)S(1)}, bf16[32,2048]{1,0:T(8,128)(2,1)S(1)}, bf16[32,2048]{1,0:T(8,128)(2,1)S(1)}) custom-call(bf16[32,16,128]{2,1,0:T(8,128)(2,1)S(1)} %collective-permute-done.6.refs_0_, bf16[32,16,128]{2,1,0:T(8,128)(2,1)S(1)} %collective-permute-done.5.refs_1_, ...), custom_call_target="tpu_custom_call" | custom-call | tf_op jit(solution)/shard_map/pallas_call | solution.py:75
  39.3 0.1 collective-permute-start.7
  39.4 0.5 collective-permute-start.12
  39.9 3.2 %collective-permute-start.19 = (bf16[32,2048]{1,0:T(8,128)(2,1)S(1)}, bf16[32,2048]{1,0:T(8,128)(2,1)S(1)}, u32[]{:S(2)}, u32[]{:S(2)}) collective-permute-start(bf16[32,2048]{1,0:T(8,128)(2,1)S(1)} %get-tuple-element.92), channel_id=1, source_target_pairs={{0,2},{1,3},{2,0},{3,1},{4,6},{5,7},{6,4},{7,5},{8,10},{9,11},{10,... | collective-permute-start | bytes 393224 | tf_op jit(solution)/shard_map/ppermute | solution.py:100
  43.1 1.4 %collective-permute-start.20 = (bf16[32,2048]{1,0:T(8,128)(2,1)S(1)}, bf16[32,2048]{1,0:T(8,128)(2,1)S(1)}, u32[]{:S(2)}, u32[]{:S(2)}) collective-permute-start(bf16[32,2048]{1,0:T(8,128)(2,1)S(1)} %get-tuple-element.93), channel_id=1, source_target_pairs={{0,3},{1,2},{2,1},{3,0},{4,7},{5,6},{6,5},{7,4},{8,11},{9,10},{10,... | collective-permute-start | bytes 393224 | tf_op jit(solution)/shard_map/ppermute | solution.py:100
  44.5 0.8 %collective-permute-done.7 = bf16[32,2048]{1,0:T(8,128)(2,1)S(1)} collective-permute-done((bf16[32,2048]{1,0:T(8,128)(2,1)S(1)}, bf16[32,2048]{1,0:T(8,128)(2,1)S(1)}, u32[]{:S(2)}, u32[]{:S(2)}) %collective-permute-start.7) | collective-permute-done | bytes 131104 | tf_op jit(solution)/shard_map/ppermute | solution.py:100
  45.4 0.1 collective-permute-start.9
  45.5 1.9 %collective-permute-done.12 = bf16[64,2048]{1,0:T(8,128)(2,1)S(1)} collective-permute-done((bf16[64,2048]{1,0:T(8,128)(2,1)S(1)}, bf16[64,2048]{1,0:T(8,128)(2,1)S(1)}, u32[]{:S(2)}, u32[]{:S(2)}) %collective-permute-start.12) | collective-permute-done | bytes 262176 | tf_op jit(solution)/shard_map/ppermute | solution.py:100
  47.5 0.1 collective-permute-start.13
  47.6 0.8 %convolution_convert_fusion.5 = bf16[128,512]{1,0:T(8,128)(2,1)S(1)} fusion(bf16[128,2048]{1,0:T(8,128)(2,1)S(1)} %pad_maximum_fusion, bf16[512,2048]{1,0:T(8,128)(2,1)S(1)} %bitcast.46), kind=kOutput, calls=%fused_computation.6 | convolution fusion | flops 268500992 | bytes 2752512 | tf_op jit(solution)/shard_map/dot_general | solution.py:140
  48.4 0.8 %convolution_convert_fusion.4 = bf16[128,512]{1,0:T(8,128)(2,1)S(1)} fusion(bf16[128,2048]{1,0:T(8,128)(2,1)S(1)} %pad_maximum_fusion.1, bf16[512,2048]{1,0:T(8,128)(2,1)S(1)} %bitcast.47), kind=kOutput, calls=%fused_computation.5 | convolution fusion | flops 268500992 | bytes 2752512 | tf_op jit(solution)/shard_map/dot_general | solution.py:140
  49.3 1.6 %collective-permute-start.17 = (bf16[64,2048]{1,0:T(8,128)(2,1)S(1)}, bf16[64,2048]{1,0:T(8,128)(2,1)S(1)}, u32[]{:S(2)}, u32[]{:S(2)}) collective-permute-start(bf16[64,2048]{1,0:T(8,128)(2,1)S(1)} %constant_dynamic-update-slice_fusion.2), channel_id=1, source_target_pairs={{0,8},{4,12},{8,0},{12,4},{1,9},{5,13},{9,1},{13,5},{2,10},{6,14},... | collective-permute-start | bytes 786440 | tf_op jit(solution)/shard_map/ppermute | solution.py:100
  50.9 1.7 %collective-permute-done.19 = bf16[32,2048]{1,0:T(8,128)(2,1)S(1)} collective-permute-done((bf16[32,2048]{1,0:T(8,128)(2,1)S(1)}, bf16[32,2048]{1,0:T(8,128)(2,1)S(1)}, u32[]{:S(2)}, u32[]{:S(2)}) %collective-permute-start.19) | collective-permute-done | bytes 131104 | tf_op jit(solution)/shard_map/ppermute | solution.py:100
  52.6 0.8 collective-permute-start.21
  53.4 0.8 %convolution_convert_fusion.7 = bf16[128,512]{1,0:T(8,128)(2,1)S(1)} fusion(bf16[128,2048]{1,0:T(8,128)(2,1)S(1)} %collective-permute-done.9, bf16[512,2048]{1,0:T(8,128)(2,1)S(1)} %bitcast.48), kind=kOutput, calls=%fused_computation.8 | convolution fusion | flops 268500992 | bytes 2752512 | tf_op jit(solution)/shard_map/dot_general | solution.py:140
  54.2 0.8 %convolution_convert_fusion.6 = bf16[128,512]{1,0:T(8,128)(2,1)S(1)} fusion(bf16[128,2048]{1,0:T(8,128)(2,1)S(1)} %collective-permute-done.13, bf16[512,2048]{1,0:T(8,128)(2,1)S(1)} %bitcast.49), kind=kOutput, calls=%fused_computation.7 | convolution fusion | flops 268500992 | bytes 2752512 | tf_op jit(solution)/shard_map/dot_general | solution.py:140
  55.2 1.4 %collective-permute-start.16 = (bf16[1,4,32,512]{3,2,1,0:T(8,128)(2,1)S(1)}, bf16[1,4,32,512]{3,2,1,0:T(8,128)(2,1)S(1)}, u32[]{:S(2)}, u32[]{:S(2)}) collective-permute-start(bf16[1,4,32,512]{3,2,1,0:T(8,128)(2,1)S(1)} %get-tuple-element.115), channel_id=1, source_target_pairs={{0,3},{1,2},{2,1},{3,0},{4,7},{5,6},{6,5},{7,4},{8,11},{9,10},{10,... | collective-permute-start | bytes 393224 | tf_op jit(solution)/shard_map/ppermute | solution.py:100
  56.6 2.3 %collective-permute-start.15 = (bf16[1,4,32,512]{3,2,1,0:T(8,128)(2,1)S(1)}, bf16[1,4,32,512]{3,2,1,0:T(8,128)(2,1)S(1)}, u32[]{:S(2)}, u32[]{:S(2)}) collective-permute-start(bf16[1,4,32,512]{3,2,1,0:T(8,128)(2,1)S(1)} %get-tuple-element.85), channel_id=1, source_target_pairs={{0,2},{1,3},{2,0},{3,1},{4,6},{5,7},{6,4},{7,5},{8,10},{9,11},{10,... | collective-permute-start | bytes 393224 | tf_op jit(solution)/shard_map/ppermute | solution.py:100
  58.9 0.8 %collective-permute-start.14 = (bf16[1,4,32,512]{3,2,1,0:T(8,128)(2,1)S(1)}, bf16[1,4,32,512]{3,2,1,0:T(8,128)(2,1)S(1)}, u32[]{:S(2)}, u32[]{:S(2)}) collective-permute-start(bf16[1,4,32,512]{3,2,1,0:T(8,128)(2,1)S(1)} %get-tuple-element.86), channel_id=1, source_target_pairs={{0,1},{1,0},{2,3},{3,2},{4,5},{5,4},{6,7},{7,6},{8,9},{9,8},{10,11... | collective-permute-start | bytes 393224 | tf_op jit(solution)/shard_map/ppermute | solution.py:100
  59.8 0.1 collective-permute-start.18
  59.9 0.8 %convolution_convert_fusion.1 = bf16[128,512]{1,0:T(8,128)(2,1)S(1)} fusion(bf16[128,2048]{1,0:T(8,128)(2,1)S(1)} %pad_maximum_fusion.2, bf16[512,2048]{1,0:T(8,128)(2,1)S(1)} %bitcast.50), kind=kOutput, calls=%fused_computation.2 | convolution fusion | flops 268500992 | bytes 2752512 | tf_op jit(solution)/shard_map/dot_general | solution.py:140
  60.7 3.0 %collective-permute-done.21 = bf16[64,2048]{1,0:T(8,128)(2,1)S(1)} collective-permute-done((bf16[64,2048]{1,0:T(8,128)(2,1)S(1)}, bf16[64,2048]{1,0:T(8,128)(2,1)S(1)}, u32[]{:S(2)}, u32[]{:S(2)}) %collective-permute-start.21) | collective-permute-done | bytes 262176 | tf_op jit(solution)/shard_map/ppermute | solution.py:100
  63.7 0.1 collective-permute-start.22
  63.8 0.8 %convolution_convert_fusion = bf16[128,512]{1,0:T(8,128)(2,1)S(1)} fusion(bf16[128,2048]{1,0:T(8,128)(2,1)S(1)} %pad_maximum_fusion.3, bf16[512,2048]{1,0:T(8,128)(2,1)S(1)} %bitcast.51), kind=kOutput, calls=%fused_computation.1 | convolution fusion | flops 268500992 | bytes 2752512 | tf_op jit(solution)/shard_map/dot_general | solution.py:140
  64.7 0.8 %convolution_convert_fusion.3 = bf16[128,512]{1,0:T(8,128)(2,1)S(1)} fusion(bf16[128,2048]{1,0:T(8,128)(2,1)S(1)} %collective-permute-done.18, bf16[512,2048]{1,0:T(8,128)(2,1)S(1)} %bitcast.52), kind=kOutput, calls=%fused_computation.4 | convolution fusion | flops 268500992 | bytes 2752512 | tf_op jit(solution)/shard_map/dot_general | solution.py:140
  65.5 0.2 collective-permute-done.22
  65.7 0.8 %convolution_convert_fusion.2 = bf16[128,512]{1,0:T(8,128)(2,1)S(1)} fusion(bf16[128,2048]{1,0:T(8,128)(2,1)S(1)} %collective-permute-done.22, bf16[512,2048]{1,0:T(8,128)(2,1)S(1)} %bitcast.53), kind=kOutput, calls=%fused_computation.3 | convolution fusion | flops 268500992 | bytes 2752512 | tf_op jit(solution)/shard_map/dot_general | solution.py:140
  66.6 0.1 broadcast_select_fusion.11
  66.6 0.6 collective-permute-start.23
  67.3 2.1 %collective-permute-start.24 = (bf16[1,4,32,512]{3,2,1,0:T(8,128)(2,1)S(1)}, bf16[1,4,32,512]{3,2,1,0:T(8,128)(2,1)S(1)}, u32[]{:S(2)}, u32[]{:S(2)}) collective-permute-start(bf16[1,4,32,512]{3,2,1,0:T(8,128)(2,1)S(1)} %get-tuple-element.99), channel_id=1, source_target_pairs={{0,2},{1,3},{2,0},{3,1},{4,6},{5,7},{6,4},{7,5},{8,10},{9,11},{10,... | collective-permute-start | bytes 393224 | tf_op jit(solution)/shard_map/ppermute | solution.py:100
  69.4 1.8 %collective-permute-start.25 = (bf16[1,4,32,512]{3,2,1,0:T(8,128)(2,1)S(1)}, bf16[1,4,32,512]{3,2,1,0:T(8,128)(2,1)S(1)}, u32[]{:S(2)}, u32[]{:S(2)}) collective-permute-start(bf16[1,4,32,512]{3,2,1,0:T(8,128)(2,1)S(1)} %get-tuple-element.100), channel_id=1, source_target_pairs={{0,3},{1,2},{2,1},{3,0},{4,7},{5,6},{6,5},{7,4},{8,11},{9,10},{10,... | collective-permute-start | bytes 393224 | tf_op jit(solution)/shard_map/ppermute | solution.py:100
  71.2 0.1 broadcast_select_fusion.31
  71.3 8.0 %collective-permute-done.25 = bf16[1,4,32,512]{3,2,1,0:T(8,128)(2,1)S(1)} collective-permute-done((bf16[1,4,32,512]{3,2,1,0:T(8,128)(2,1)S(1)}, bf16[1,4,32,512]{3,2,1,0:T(8,128)(2,1)S(1)}, u32[]{:S(2)}, u32[]{:S(2)}) %collective-permute-start.25) | collective-permute-done | bytes 131104 | tf_op jit(solution)/shard_map/ppermute | solution.py:100
  79.3 1.0 %collective-permute-done.24 = bf16[1,4,32,512]{3,2,1,0:T(8,128)(2,1)S(1)} collective-permute-done((bf16[1,4,32,512]{3,2,1,0:T(8,128)(2,1)S(1)}, bf16[1,4,32,512]{3,2,1,0:T(8,128)(2,1)S(1)}, u32[]{:S(2)}, u32[]{:S(2)}) %collective-permute-start.24) | collective-permute-done | bytes 131104 | tf_op jit(solution)/shard_map/ppermute | solution.py:100
  80.3 0.1 broadcast_select_fusion.27
  80.4 0.1 broadcast_select_fusion.26
  80.5 0.8 %maximum_bitcast_fusion = f32[256,512]{1,0:T(8,128)} fusion(f32[1,128,512]{2,1,0:T(8,128)S(1)} %bitcast.56, f32[1,128,512]{2,1,0:T(8,128)S(1)} %bitcast.55), kind=kLoop, calls=%fused_computation.13 | loop fusion | flops 131072 | bytes 1048576 | tf_op jit(solution)/shard_map/reshape | solution.py:235
  (53 shorter events, 0.7 us)
Async XLA Ops:
  0.0 1.2 %copy-start = (bf16[256,16,128]{2,1,0:T(8,128)(2,1)S(1)}, bf16[256,16,128]{2,1,0:T(8,128)(2,1)}, u32[]{:S(2)}) copy-start(bf16[256,16,128]{2,1,0:T(8,128)(2,1)} %param.5) | copy-start | bytes 3145732
  1.2 10.8 %collective-permute-start = (bf16[32,16,128]{2,1,0:T(8,128)(2,1)S(1)}, bf16[32,16,128]{2,1,0:T(8,128)(2,1)S(1)}, u32[]{:S(2)}, u32[]{:S(2)}) collective-permute-start(bf16[32,16,128]{2,1,0:T(8,128)(2,1)S(1)} %constant_dynamic-slice_fusion.7), channel_id=1, source_target_pairs={{0,3},{1,2},{2,1},{3,0},{4,7},{5,6},{6,5},{7,4},{8,11},{9,10},{10,... | collective-permute-start | bytes 393224 | tf_op jit(solution)/shard_map/ppermute | solution.py:100
  6.4 10.2 %collective-permute-start.2 = (bf16[32,16,128]{2,1,0:T(8,128)(2,1)S(1)}, bf16[32,16,128]{2,1,0:T(8,128)(2,1)S(1)}, u32[]{:S(2)}, u32[]{:S(2)}) collective-permute-start(bf16[32,16,128]{2,1,0:T(8,128)(2,1)S(1)} %constant_dynamic-slice_fusion.5), channel_id=1, source_target_pairs={{0,1},{1,0},{2,3},{3,2},{4,5},{5,4},{6,7},{7,6},{8,9},{9,8},{10,11... | collective-permute-start | bytes 393224 | tf_op jit(solution)/shard_map/ppermute | solution.py:100
  6.5 17.5 %collective-permute-start.1 = (bf16[32,16,128]{2,1,0:T(8,128)(2,1)S(1)}, bf16[32,16,128]{2,1,0:T(8,128)(2,1)S(1)}, u32[]{:S(2)}, u32[]{:S(2)}) collective-permute-start(bf16[32,16,128]{2,1,0:T(8,128)(2,1)S(1)} %constant_dynamic-slice_fusion.6), channel_id=1, source_target_pairs={{0,2},{1,3},{2,0},{3,1},{4,6},{5,7},{6,4},{7,5},{8,10},{9,11},{10,... | collective-permute-start | bytes 393224 | tf_op jit(solution)/shard_map/ppermute | solution.py:100
  8.2 3.7 %copy-start.1 = (f32[128,128]{1,0:T(8,128)S(1)}, f32[128,128]{1,0:T(8,128)}, u32[]{:S(2)}) copy-start(f32[128,128]{1,0:T(8,128)} %refs_6_.3) | copy-start | bytes 196612
  8.2 15.8 %copy-start.2 = (f32[64,128]{1,0:T(8,128)S(1)}, f32[64,128]{1,0:T(8,128)}, u32[]{:S(2)}) copy-start(f32[64,128]{1,0:T(8,128)} %refs_8_.3) | copy-start | bytes 98308
  12.1 16.3 %collective-permute-start.6 = (bf16[32,16,128]{2,1,0:T(8,128)(2,1)S(1)}, bf16[32,16,128]{2,1,0:T(8,128)(2,1)S(1)}, u32[]{:S(2)}, u32[]{:S(2)}) collective-permute-start(bf16[32,16,128]{2,1,0:T(8,128)(2,1)S(1)} %constant_dynamic-slice_fusion), channel_id=1, source_target_pairs={{0,3},{1,2},{2,1},{3,0},{4,7},{5,6},{6,5},{7,4},{8,11},{9,10},{10,... | collective-permute-start | bytes 393224 | tf_op jit(solution)/shard_map/ppermute | solution.py:100
  16.0 19.4 %collective-permute-start.5 = (bf16[32,16,128]{2,1,0:T(8,128)(2,1)S(1)}, bf16[32,16,128]{2,1,0:T(8,128)(2,1)S(1)}, u32[]{:S(2)}, u32[]{:S(2)}) collective-permute-start(bf16[32,16,128]{2,1,0:T(8,128)(2,1)S(1)} %constant_dynamic-slice_fusion.1), channel_id=1, source_target_pairs={{0,2},{1,3},{2,0},{3,1},{4,6},{5,7},{6,4},{7,5},{8,10},{9,11},{10,... | collective-permute-start | bytes 393224 | tf_op jit(solution)/shard_map/ppermute | solution.py:100
  16.0 19.4 %collective-permute-start.4 = (bf16[32,16,128]{2,1,0:T(8,128)(2,1)S(1)}, bf16[32,16,128]{2,1,0:T(8,128)(2,1)S(1)}, u32[]{:S(2)}, u32[]{:S(2)}) collective-permute-start(bf16[32,16,128]{2,1,0:T(8,128)(2,1)S(1)} %constant_dynamic-slice_fusion.2), channel_id=1, source_target_pairs={{0,1},{1,0},{2,3},{3,2},{4,5},{5,4},{6,7},{7,6},{8,9},{9,8},{10,11... | collective-permute-start | bytes 393224 | tf_op jit(solution)/shard_map/ppermute | solution.py:100
  26.2 9.1 %collective-permute-start.3 = (bf16[32,2048]{1,0:T(8,128)(2,1)S(1)}, bf16[32,2048]{1,0:T(8,128)(2,1)S(1)}, u32[]{:S(2)}, u32[]{:S(2)}) collective-permute-start(bf16[32,2048]{1,0:T(8,128)(2,1)S(1)} %get-tuple-element.63), channel_id=1, source_target_pairs={{0,1},{1,0},{2,3},{3,2},{4,5},{5,4},{6,7},{7,6},{8,9},{9,8},{10,11... | collective-permute-start | bytes 393224 | tf_op jit(solution)/shard_map/ppermute | solution.py:100
  26.3 13.0 %collective-permute-start.10 = (bf16[32,2048]{1,0:T(8,128)(2,1)S(1)}, bf16[32,2048]{1,0:T(8,128)(2,1)S(1)}, u32[]{:S(2)}, u32[]{:S(2)}) collective-permute-start(bf16[32,2048]{1,0:T(8,128)(2,1)S(1)} %get-tuple-element.83), channel_id=1, source_target_pairs={{0,2},{1,3},{2,0},{3,1},{4,6},{5,7},{6,4},{7,5},{8,10},{9,11},{10,... | collective-permute-start | bytes 393224 | tf_op jit(solution)/shard_map/ppermute | solution.py:100
  28.4 10.9 %collective-permute-start.11 = (bf16[32,2048]{1,0:T(8,128)(2,1)S(1)}, bf16[32,2048]{1,0:T(8,128)(2,1)S(1)}, u32[]{:S(2)}, u32[]{:S(2)}) collective-permute-start(bf16[32,2048]{1,0:T(8,128)(2,1)S(1)} %get-tuple-element.84), channel_id=1, source_target_pairs={{0,3},{1,2},{2,1},{3,0},{4,7},{5,6},{6,5},{7,4},{8,11},{9,10},{10,... | collective-permute-start | bytes 393224 | tf_op jit(solution)/shard_map/ppermute | solution.py:100
  35.4 10.0 %collective-permute-start.8 = (bf16[64,2048]{1,0:T(8,128)(2,1)S(1)}, bf16[64,2048]{1,0:T(8,128)(2,1)S(1)}, u32[]{:S(2)}, u32[]{:S(2)}) collective-permute-start(bf16[64,2048]{1,0:T(8,128)(2,1)S(1)} %constant_dynamic-update-slice_fusion), channel_id=1, source_target_pairs={{0,8},{4,12},{8,0},{12,4},{1,9},{5,13},{9,1},{13,5},{2,10},{6,14},... | collective-permute-start | bytes 786440 | tf_op jit(solution)/shard_map/ppermute | solution.py:100
  39.3 6.1 %collective-permute-start.7 = (bf16[32,2048]{1,0:T(8,128)(2,1)S(1)}, bf16[32,2048]{1,0:T(8,128)(2,1)S(1)}, u32[]{:S(2)}, u32[]{:S(2)}) collective-permute-start(bf16[32,2048]{1,0:T(8,128)(2,1)S(1)} %get-tuple-element.77), channel_id=1, source_target_pairs={{0,1},{1,0},{2,3},{3,2},{4,5},{5,4},{6,7},{7,6},{8,9},{9,8},{10,11... | collective-permute-start | bytes 393224 | tf_op jit(solution)/shard_map/ppermute | solution.py:100
  39.4 8.0 %collective-permute-start.12 = (bf16[64,2048]{1,0:T(8,128)(2,1)S(1)}, bf16[64,2048]{1,0:T(8,128)(2,1)S(1)}, u32[]{:S(2)}, u32[]{:S(2)}) collective-permute-start(bf16[64,2048]{1,0:T(8,128)(2,1)S(1)} %pad_maximum_fusion.4), channel_id=1, source_target_pairs={{0,8},{4,12},{8,0},{12,4},{1,9},{5,13},{9,1},{13,5},{2,10},{6,14},... | collective-permute-start | bytes 786440 | tf_op jit(solution)/shard_map/ppermute | solution.py:100
  39.9 7.6 %copy-start.3 = (bf16[64,8,16,128]{3,1,2,0:T(8,128)(2,1)S(1)}, bf16[64,8,16,128]{3,1,2,0:T(8,128)(2,1)}, u32[]{:S(2)}) copy-start(bf16[64,8,16,128]{3,1,2,0:T(8,128)(2,1)} %copy.19) | copy-start | bytes 6291460
  39.9 12.6 %collective-permute-start.19 = (bf16[32,2048]{1,0:T(8,128)(2,1)S(1)}, bf16[32,2048]{1,0:T(8,128)(2,1)S(1)}, u32[]{:S(2)}, u32[]{:S(2)}) collective-permute-start(bf16[32,2048]{1,0:T(8,128)(2,1)S(1)} %get-tuple-element.92), channel_id=1, source_target_pairs={{0,2},{1,3},{2,0},{3,1},{4,6},{5,7},{6,4},{7,5},{8,10},{9,11},{10,... | collective-permute-start | bytes 393224 | tf_op jit(solution)/shard_map/ppermute | solution.py:100
  43.1 9.5 %collective-permute-start.20 = (bf16[32,2048]{1,0:T(8,128)(2,1)S(1)}, bf16[32,2048]{1,0:T(8,128)(2,1)S(1)}, u32[]{:S(2)}, u32[]{:S(2)}) collective-permute-start(bf16[32,2048]{1,0:T(8,128)(2,1)S(1)} %get-tuple-element.93), channel_id=1, source_target_pairs={{0,3},{1,2},{2,1},{3,0},{4,7},{5,6},{6,5},{7,4},{8,11},{9,10},{10,... | collective-permute-start | bytes 393224 | tf_op jit(solution)/shard_map/ppermute | solution.py:100
  45.4 8.0 %collective-permute-start.9 = (bf16[128,2048]{1,0:T(8,128)(2,1)S(1)}, bf16[128,2048]{1,0:T(8,128)(2,1)S(1)}, u32[]{:S(2)}, u32[]{:S(2)}) collective-permute-start(bf16[128,2048]{1,0:T(8,128)(2,1)S(1)} %pad_maximum_fusion), channel_id=1, source_target_pairs={{0,4},{4,0},{8,12},{12,8},{1,5},{5,1},{9,13},{13,9},{2,6},{6,2},{1... | collective-permute-start | bytes 1572872 | tf_op jit(solution)/shard_map/ppermute | solution.py:100
  47.5 6.8 %collective-permute-start.13 = (bf16[128,2048]{1,0:T(8,128)(2,1)S(1)}, bf16[128,2048]{1,0:T(8,128)(2,1)S(1)}, u32[]{:S(2)}, u32[]{:S(2)}) collective-permute-start(bf16[128,2048]{1,0:T(8,128)(2,1)S(1)} %pad_maximum_fusion.1), channel_id=1, source_target_pairs={{0,4},{4,0},{8,12},{12,8},{1,5},{5,1},{9,13},{13,9},{2,6},{6,2},{1... | collective-permute-start | bytes 1572872 | tf_op jit(solution)/shard_map/ppermute | solution.py:100
  49.3 10.4 %collective-permute-start.17 = (bf16[64,2048]{1,0:T(8,128)(2,1)S(1)}, bf16[64,2048]{1,0:T(8,128)(2,1)S(1)}, u32[]{:S(2)}, u32[]{:S(2)}) collective-permute-start(bf16[64,2048]{1,0:T(8,128)(2,1)S(1)} %constant_dynamic-update-slice_fusion.2), channel_id=1, source_target_pairs={{0,8},{4,12},{8,0},{12,4},{1,9},{5,13},{9,1},{13,5},{2,10},{6,14},... | collective-permute-start | bytes 786440 | tf_op jit(solution)/shard_map/ppermute | solution.py:100
  52.6 11.1 %collective-permute-start.21 = (bf16[64,2048]{1,0:T(8,128)(2,1)S(1)}, bf16[64,2048]{1,0:T(8,128)(2,1)S(1)}, u32[]{:S(2)}, u32[]{:S(2)}) collective-permute-start(bf16[64,2048]{1,0:T(8,128)(2,1)S(1)} %constant_dynamic-update-slice_fusion.4), channel_id=1, source_target_pairs={{0,8},{4,12},{8,0},{12,4},{1,9},{5,13},{9,1},{13,5},{2,10},{6,14},... | collective-permute-start | bytes 786440 | tf_op jit(solution)/shard_map/ppermute | solution.py:100
  55.2 16.0 %collective-permute-start.16 = (bf16[1,4,32,512]{3,2,1,0:T(8,128)(2,1)S(1)}, bf16[1,4,32,512]{3,2,1,0:T(8,128)(2,1)S(1)}, u32[]{:S(2)}, u32[]{:S(2)}) collective-permute-start(bf16[1,4,32,512]{3,2,1,0:T(8,128)(2,1)S(1)} %get-tuple-element.115), channel_id=1, source_target_pairs={{0,3},{1,2},{2,1},{3,0},{4,7},{5,6},{6,5},{7,4},{8,11},{9,10},{10,... | collective-permute-start | bytes 393224 | tf_op jit(solution)/shard_map/ppermute | solution.py:100
  56.6 14.6 %collective-permute-start.15 = (bf16[1,4,32,512]{3,2,1,0:T(8,128)(2,1)S(1)}, bf16[1,4,32,512]{3,2,1,0:T(8,128)(2,1)S(1)}, u32[]{:S(2)}, u32[]{:S(2)}) collective-permute-start(bf16[1,4,32,512]{3,2,1,0:T(8,128)(2,1)S(1)} %get-tuple-element.85), channel_id=1, source_target_pairs={{0,2},{1,3},{2,0},{3,1},{4,6},{5,7},{6,4},{7,5},{8,10},{9,11},{10,... | collective-permute-start | bytes 393224 | tf_op jit(solution)/shard_map/ppermute | solution.py:100
  58.9 10.5 %collective-permute-start.14 = (bf16[1,4,32,512]{3,2,1,0:T(8,128)(2,1)S(1)}, bf16[1,4,32,512]{3,2,1,0:T(8,128)(2,1)S(1)}, u32[]{:S(2)}, u32[]{:S(2)}) collective-permute-start(bf16[1,4,32,512]{3,2,1,0:T(8,128)(2,1)S(1)} %get-tuple-element.86), channel_id=1, source_target_pairs={{0,1},{1,0},{2,3},{3,2},{4,5},{5,4},{6,7},{7,6},{8,9},{9,8},{10,11... | collective-permute-start | bytes 393224 | tf_op jit(solution)/shard_map/ppermute | solution.py:100
  59.8 4.9 %collective-permute-start.18 = (bf16[128,2048]{1,0:T(8,128)(2,1)S(1)}, bf16[128,2048]{1,0:T(8,128)(2,1)S(1)}, u32[]{:S(2)}, u32[]{:S(2)}) collective-permute-start(bf16[128,2048]{1,0:T(8,128)(2,1)S(1)} %pad_maximum_fusion.2), channel_id=1, source_target_pairs={{0,4},{4,0},{8,12},{12,8},{1,5},{5,1},{9,13},{13,9},{2,6},{6,2},{1... | collective-permute-start | bytes 1572872 | tf_op jit(solution)/shard_map/ppermute | solution.py:100
  63.7 2.0 %collective-permute-start.22 = (bf16[128,2048]{1,0:T(8,128)(2,1)S(1)}, bf16[128,2048]{1,0:T(8,128)(2,1)S(1)}, u32[]{:S(2)}, u32[]{:S(2)}) collective-permute-start(bf16[128,2048]{1,0:T(8,128)(2,1)S(1)} %pad_maximum_fusion.3), channel_id=1, source_target_pairs={{0,4},{4,0},{8,12},{12,8},{1,5},{5,1},{9,13},{13,9},{2,6},{6,2},{1... | collective-permute-start | bytes 1572872 | tf_op jit(solution)/shard_map/ppermute | solution.py:100
  66.6 13.7 %collective-permute-start.23 = (bf16[1,4,32,512]{3,2,1,0:T(8,128)(2,1)S(1)}, bf16[1,4,32,512]{3,2,1,0:T(8,128)(2,1)S(1)}, u32[]{:S(2)}, u32[]{:S(2)}) collective-permute-start(bf16[1,4,32,512]{3,2,1,0:T(8,128)(2,1)S(1)} %get-tuple-element.98), channel_id=1, source_target_pairs={{0,1},{1,0},{2,3},{3,2},{4,5},{5,4},{6,7},{7,6},{8,9},{9,8},{10,11... | collective-permute-start | bytes 393224 | tf_op jit(solution)/shard_map/ppermute | solution.py:100
  67.3 13.0 %collective-permute-start.24 = (bf16[1,4,32,512]{3,2,1,0:T(8,128)(2,1)S(1)}, bf16[1,4,32,512]{3,2,1,0:T(8,128)(2,1)S(1)}, u32[]{:S(2)}, u32[]{:S(2)}) collective-permute-start(bf16[1,4,32,512]{3,2,1,0:T(8,128)(2,1)S(1)} %get-tuple-element.99), channel_id=1, source_target_pairs={{0,2},{1,3},{2,0},{3,1},{4,6},{5,7},{6,4},{7,5},{8,10},{9,11},{10,... | collective-permute-start | bytes 393224 | tf_op jit(solution)/shard_map/ppermute | solution.py:100
  69.4 9.9 %collective-permute-start.25 = (bf16[1,4,32,512]{3,2,1,0:T(8,128)(2,1)S(1)}, bf16[1,4,32,512]{3,2,1,0:T(8,128)(2,1)S(1)}, u32[]{:S(2)}, u32[]{:S(2)}) collective-permute-start(bf16[1,4,32,512]{3,2,1,0:T(8,128)(2,1)S(1)} %get-tuple-element.100), channel_id=1, source_target_pairs={{0,3},{1,2},{2,1},{3,0},{4,7},{5,6},{6,5},{7,4},{8,11},{9,10},{10,... | collective-permute-start | bytes 393224 | tf_op jit(solution)/shard_map/ppermute | solution.py:100

commit v22 on v20

--- a/solution.py
+++ b/solution.py
@@ -233,7 +233,10 @@
         total = jnp.stack(turned(total, here), axis=1)
         total = jnp.stack(turned([total[at] for at in range(owned)], share % owned))
         results.append(total.reshape(owned, part, train_count))
-    return jnp.concatenate(results, axis=1).reshape(owned * count, train_count)
+    scores = jnp.pad(results[0], ((0, 0), (0, count - parts[0]), (0, 0)))
+    scores = lax.optimization_barrier(scores)
+    scores = lax.dynamic_update_slice_in_dim(scores, results[1], parts[0], 1)
+    return scores.reshape(owned * count, train_count)
 
 
 def solution(mesh):

time: 80.9 us -> 81.7 us (level)
  local copies, waits for them, and re-layouts: 6.27 us -> 7.84 us
  other arithmetic: 1.54 us -> 0.71 us
    pad x0 -> x1, local copies, waits for them, and re-layouts: none -> 0.85 us  [body(): scores = jnp.pad(results[0], ((0, 0), (0, count - parts[0]), (0, 0)))]
    reshape x1 -> x0, other arithmetic: 0.83 us -> none  [body(): return jnp.concatenate(results, axis=1).reshape(owned * count, train_count)]
where the time goes in v22:
time: 81.7 us; the launch traced here: 81.3 us
  starting transfers between devices  33.1 us (41%)
  waiting for transfers between devices  27.9 us (34%)
  local copies, waits for them, and re-layouts  7.84 us (10%)
  matrix products  6.66 us (8%)
  Pallas kernels  4.47 us (5%)
    ppermute x26, starting transfers between devices, crossed(): return lax.ppermute(value, axis, [(at, at ^ mask) for at in range(size)])  33.1 us
    ppermute x26, waiting for transfers between devices, crossed(): return lax.ppermute(value, axis, [(at, at ^ mask) for at in range(size)])  27.9 us
    dot_general x8, matrix products, products(): lax.dot_general(block, train_flat, contract, preferred_element_type=jnp.f...  6.66 us
    unnamed x17, local copies, waits for them, and re-layouts  5.2 us
    pallas_call x2, Pallas kernels, condition_fast(): pl.pallas_call(functools.partial(condition_kernel, slices, rows_here), gr...  4.47 us
  transfers between devices with their start and end apart: 26, of which 8 were waited for; matrix products, arithmetic and copies ran while one was open for 15% of the time, Pallas kernels for 6%

profile of v22, /device:TPU:0, one launch (start us, length us, event | category | flops | bytes accessed | tf_op | source)
XLA Modules:
  0.0 81.3 jit_solution(6790847808347870557)
XLA Ops:
  0.0 1.2 %copy-done = bf16[256,16,128]{2,1,0:T(8,128)(2,1)S(1)} copy-done((bf16[256,16,128]{2,1,0:T(8,128)(2,1)S(1)}, bf16[256,16,128]{2,1,0:T(8,128)(2,1)}, u32[]{:S(2)}) %copy-start) | copy-done | bytes 1048600
  1.2 5.1 %collective-permute-start = (bf16[32,16,128]{2,1,0:T(8,128)(2,1)S(1)}, bf16[32,16,128]{2,1,0:T(8,128)(2,1)S(1)}, u32[]{:S(2)}, u32[]{:S(2)}) collective-permute-start(bf16[32,16,128]{2,1,0:T(8,128)(2,1)S(1)} %constant_dynamic-slice_fusion.7), channel_id=1, source_target_pairs={{0,3},{1,2},{2,1},{3,0},{4,7},{5,6},{6,5},{7,4},{8,11},{9,10},{10,... | collective-permute-start | bytes 393224 | tf_op jit(solution)/shard_map/ppermute | solution.py:100
  6.4 0.1 collective-permute-start.2
  6.5 0.6 collective-permute-start.1
  7.1 0.7 fusion.8
  7.8 0.1 copy.13
  7.9 0.1 copy.14
  8.0 0.1 copy.15
  8.1 0.1 copy.16
  8.2 0.0 copy-start.1
  8.2 0.0 copy-start.2
  8.2 3.5 %copy.19 = bf16[64,8,16,128]{3,1,2,0:T(8,128)(2,1)} copy(bf16[64,8,16,128]{3,2,1,0:T(8,128)(2,1)} %bitcast.53) | data formatting | bytes 4194304
  11.7 0.1 pad_maximum_fusion.15
  11.8 0.1 copy.11.refs_4_
  11.9 0.0 copy-done.1
  11.9 0.1 copy.10
  12.1 3.8 %collective-permute-start.6 = (bf16[32,16,128]{2,1,0:T(8,128)(2,1)S(1)}, bf16[32,16,128]{2,1,0:T(8,128)(2,1)S(1)}, u32[]{:S(2)}, u32[]{:S(2)}) collective-permute-start(bf16[32,16,128]{2,1,0:T(8,128)(2,1)S(1)} %constant_dynamic-slice_fusion), channel_id=1, source_target_pairs={{0,3},{1,2},{2,1},{3,0},{4,7},{5,6},{6,5},{7,4},{8,11},{9,10},{10,... | collective-permute-start | bytes 393224 | tf_op jit(solution)/shard_map/ppermute | solution.py:100
  16.0 0.0 collective-permute-start.5
  16.0 0.6 collective-permute-start.4
  16.6 7.4 %collective-permute-done.1.refs_1_ = bf16[32,16,128]{2,1,0:T(8,128)(2,1)S(1)} collective-permute-done((bf16[32,16,128]{2,1,0:T(8,128)(2,1)S(1)}, bf16[32,16,128]{2,1,0:T(8,128)(2,1)S(1)}, u32[]{:S(2)}, u32[]{:S(2)}) %collective-permute-start.1) | collective-permute-done | bytes 131104 | tf_op jit(solution)/shard_map/ppermute | solution.py:100
  24.0 2.2 %shard_map.55 = (bf16[32,2048]{1,0:T(8,128)(2,1)S(1)}, bf16[32,2048]{1,0:T(8,128)(2,1)S(1)}, bf16[32,2048]{1,0:T(8,128)(2,1)S(1)}, bf16[32,2048]{1,0:T(8,128)(2,1)S(1)}) custom-call(bf16[32,16,128]{2,1,0:T(8,128)(2,1)S(1)} %collective-permute-done.refs_0_, bf16[32,16,128]{2,1,0:T(8,128)(2,1)S(1)} %collective-permute-done.1.refs_1_, ...), custom_call_target="tpu_custom_call" | custom-call | tf_op jit(solution)/shard_map/pallas_call | solution.py:75
  26.2 0.1 collective-permute-start.3
  26.3 2.1 %collective-permute-start.10 = (bf16[32,2048]{1,0:T(8,128)(2,1)S(1)}, bf16[32,2048]{1,0:T(8,128)(2,1)S(1)}, u32[]{:S(2)}, u32[]{:S(2)}) collective-permute-start(bf16[32,2048]{1,0:T(8,128)(2,1)S(1)} %get-tuple-element.87), channel_id=1, source_target_pairs={{0,2},{1,3},{2,0},{3,1},{4,6},{5,7},{6,4},{7,5},{8,10},{9,11},{10,... | collective-permute-start | bytes 393224 | tf_op jit(solution)/shard_map/ppermute | solution.py:100
  28.4 2.3 %collective-permute-start.11 = (bf16[32,2048]{1,0:T(8,128)(2,1)S(1)}, bf16[32,2048]{1,0:T(8,128)(2,1)S(1)}, u32[]{:S(2)}, u32[]{:S(2)}) collective-permute-start(bf16[32,2048]{1,0:T(8,128)(2,1)S(1)} %get-tuple-element.88), channel_id=1, source_target_pairs={{0,3},{1,2},{2,1},{3,0},{4,7},{5,6},{6,5},{7,4},{8,11},{9,10},{10,... | collective-permute-start | bytes 393224 | tf_op jit(solution)/shard_map/ppermute | solution.py:100
  30.7 4.7 %collective-permute-done.5.refs_1_ = bf16[32,16,128]{2,1,0:T(8,128)(2,1)S(1)} collective-permute-done((bf16[32,16,128]{2,1,0:T(8,128)(2,1)S(1)}, bf16[32,16,128]{2,1,0:T(8,128)(2,1)S(1)}, u32[]{:S(2)}, u32[]{:S(2)}) %collective-permute-start.5) | collective-permute-done | bytes 131104 | tf_op jit(solution)/shard_map/ppermute | solution.py:100
  35.4 1.6 %collective-permute-start.8 = (bf16[64,2048]{1,0:T(8,128)(2,1)S(1)}, bf16[64,2048]{1,0:T(8,128)(2,1)S(1)}, u32[]{:S(2)}, u32[]{:S(2)}) collective-permute-start(bf16[64,2048]{1,0:T(8,128)(2,1)S(1)} %constant_dynamic-update-slice_fusion), channel_id=1, source_target_pairs={{0,8},{4,12},{8,0},{12,4},{1,9},{5,13},{9,1},{13,5},{2,10},{6,14},... | collective-permute-start | bytes 786440 | tf_op jit(solution)/shard_map/ppermute | solution.py:100
  37.0 2.2 %shard_map.56 = (bf16[32,2048]{1,0:T(8,128)(2,1)S(1)}, bf16[32,2048]{1,0:T(8,128)(2,1)S(1)}, bf16[32,2048]{1,0:T(8,128)(2,1)S(1)}, bf16[32,2048]{1,0:T(8,128)(2,1)S(1)}) custom-call(bf16[32,16,128]{2,1,0:T(8,128)(2,1)S(1)} %collective-permute-done.6.refs_0_, bf16[32,16,128]{2,1,0:T(8,128)(2,1)S(1)} %collective-permute-done.5.refs_1_, ...), custom_call_target="tpu_custom_call" | custom-call | tf_op jit(solution)/shard_map/pallas_call | solution.py:75
  39.3 0.1 collective-permute-start.7
  39.4 0.5 collective-permute-start.12
  39.9 3.2 %collective-permute-start.19 = (bf16[32,2048]{1,0:T(8,128)(2,1)S(1)}, bf16[32,2048]{1,0:T(8,128)(2,1)S(1)}, u32[]{:S(2)}, u32[]{:S(2)}) collective-permute-start(bf16[32,2048]{1,0:T(8,128)(2,1)S(1)} %get-tuple-element.96), channel_id=1, source_target_pairs={{0,2},{1,3},{2,0},{3,1},{4,6},{5,7},{6,4},{7,5},{8,10},{9,11},{10,... | collective-permute-start | bytes 393224 | tf_op jit(solution)/shard_map/ppermute | solution.py:100
  43.1 1.4 %collective-permute-start.20 = (bf16[32,2048]{1,0:T(8,128)(2,1)S(1)}, bf16[32,2048]{1,0:T(8,128)(2,1)S(1)}, u32[]{:S(2)}, u32[]{:S(2)}) collective-permute-start(bf16[32,2048]{1,0:T(8,128)(2,1)S(1)} %get-tuple-element.97), channel_id=1, source_target_pairs={{0,3},{1,2},{2,1},{3,0},{4,7},{5,6},{6,5},{7,4},{8,11},{9,10},{10,... | collective-permute-start | bytes 393224 | tf_op jit(solution)/shard_map/ppermute | solution.py:100
  44.5 0.8 %collective-permute-done.7 = bf16[32,2048]{1,0:T(8,128)(2,1)S(1)} collective-permute-done((bf16[32,2048]{1,0:T(8,128)(2,1)S(1)}, bf16[32,2048]{1,0:T(8,128)(2,1)S(1)}, u32[]{:S(2)}, u32[]{:S(2)}) %collective-permute-start.7) | collective-permute-done | bytes 131104 | tf_op jit(solution)/shard_map/ppermute | solution.py:100
  45.4 0.1 collective-permute-start.9
  45.5 1.9 %collective-permute-done.12 = bf16[64,2048]{1,0:T(8,128)(2,1)S(1)} collective-permute-done((bf16[64,2048]{1,0:T(8,128)(2,1)S(1)}, bf16[64,2048]{1,0:T(8,128)(2,1)S(1)}, u32[]{:S(2)}, u32[]{:S(2)}) %collective-permute-start.12) | collective-permute-done | bytes 262176 | tf_op jit(solution)/shard_map/ppermute | solution.py:100
  47.5 0.1 collective-permute-start.13
  47.6 0.8 %convolution_convert_fusion.5 = bf16[128,512]{1,0:T(8,128)(2,1)S(1)} fusion(bf16[128,2048]{1,0:T(8,128)(2,1)S(1)} %pad_maximum_fusion, bf16[512,2048]{1,0:T(8,128)(2,1)S(1)} %bitcast.45), kind=kOutput, calls=%fused_computation.6 | convolution fusion | flops 268500992 | bytes 2752512 | tf_op jit(solution)/shard_map/dot_general | solution.py:140
  48.4 0.8 %convolution_convert_fusion.4 = bf16[128,512]{1,0:T(8,128)(2,1)S(1)} fusion(bf16[128,2048]{1,0:T(8,128)(2,1)S(1)} %pad_maximum_fusion.1, bf16[512,2048]{1,0:T(8,128)(2,1)S(1)} %bitcast.46), kind=kOutput, calls=%fused_computation.5 | convolution fusion | flops 268500992 | bytes 2752512 | tf_op jit(solution)/shard_map/dot_general | solution.py:140
  49.3 1.6 %collective-permute-start.17 = (bf16[64,2048]{1,0:T(8,128)(2,1)S(1)}, bf16[64,2048]{1,0:T(8,128)(2,1)S(1)}, u32[]{:S(2)}, u32[]{:S(2)}) collective-permute-start(bf16[64,2048]{1,0:T(8,128)(2,1)S(1)} %constant_dynamic-update-slice_fusion.2), channel_id=1, source_target_pairs={{0,8},{4,12},{8,0},{12,4},{1,9},{5,13},{9,1},{13,5},{2,10},{6,14},... | collective-permute-start | bytes 786440 | tf_op jit(solution)/shard_map/ppermute | solution.py:100
  50.9 1.7 %collective-permute-done.19 = bf16[32,2048]{1,0:T(8,128)(2,1)S(1)} collective-permute-done((bf16[32,2048]{1,0:T(8,128)(2,1)S(1)}, bf16[32,2048]{1,0:T(8,128)(2,1)S(1)}, u32[]{:S(2)}, u32[]{:S(2)}) %collective-permute-start.19) | collective-permute-done | bytes 131104 | tf_op jit(solution)/shard_map/ppermute | solution.py:100
  52.6 0.8 collective-permute-start.21
  53.4 0.8 %convolution_convert_fusion.7 = bf16[128,512]{1,0:T(8,128)(2,1)S(1)} fusion(bf16[128,2048]{1,0:T(8,128)(2,1)S(1)} %collective-permute-done.9, bf16[512,2048]{1,0:T(8,128)(2,1)S(1)} %bitcast.47), kind=kOutput, calls=%fused_computation.8 | convolution fusion | flops 268500992 | bytes 2752512 | tf_op jit(solution)/shard_map/dot_general | solution.py:140
  54.2 0.8 %convolution_convert_fusion.6 = bf16[128,512]{1,0:T(8,128)(2,1)S(1)} fusion(bf16[128,2048]{1,0:T(8,128)(2,1)S(1)} %collective-permute-done.13, bf16[512,2048]{1,0:T(8,128)(2,1)S(1)} %bitcast.48), kind=kOutput, calls=%fused_computation.7 | convolution fusion | flops 268500992 | bytes 2752512 | tf_op jit(solution)/shard_map/dot_general | solution.py:140
  55.2 1.4 %collective-permute-start.16 = (bf16[1,4,32,512]{3,2,1,0:T(8,128)(2,1)S(1)}, bf16[1,4,32,512]{3,2,1,0:T(8,128)(2,1)S(1)}, u32[]{:S(2)}, u32[]{:S(2)}) collective-permute-start(bf16[1,4,32,512]{3,2,1,0:T(8,128)(2,1)S(1)} %get-tuple-element.123), channel_id=1, source_target_pairs={{0,3},{1,2},{2,1},{3,0},{4,7},{5,6},{6,5},{7,4},{8,11},{9,10},{10,... | collective-permute-start | bytes 393224 | tf_op jit(solution)/shard_map/ppermute | solution.py:100
  56.6 2.3 %collective-permute-start.15 = (bf16[1,4,32,512]{3,2,1,0:T(8,128)(2,1)S(1)}, bf16[1,4,32,512]{3,2,1,0:T(8,128)(2,1)S(1)}, u32[]{:S(2)}, u32[]{:S(2)}) collective-permute-start(bf16[1,4,32,512]{3,2,1,0:T(8,128)(2,1)S(1)} %get-tuple-element.89), channel_id=1, source_target_pairs={{0,2},{1,3},{2,0},{3,1},{4,6},{5,7},{6,4},{7,5},{8,10},{9,11},{10,... | collective-permute-start | bytes 393224 | tf_op jit(solution)/shard_map/ppermute | solution.py:100
  58.9 0.8 %collective-permute-start.14 = (bf16[1,4,32,512]{3,2,1,0:T(8,128)(2,1)S(1)}, bf16[1,4,32,512]{3,2,1,0:T(8,128)(2,1)S(1)}, u32[]{:S(2)}, u32[]{:S(2)}) collective-permute-start(bf16[1,4,32,512]{3,2,1,0:T(8,128)(2,1)S(1)} %get-tuple-element.90), channel_id=1, source_target_pairs={{0,1},{1,0},{2,3},{3,2},{4,5},{5,4},{6,7},{7,6},{8,9},{9,8},{10,11... | collective-permute-start | bytes 393224 | tf_op jit(solution)/shard_map/ppermute | solution.py:100
  59.8 0.1 collective-permute-start.18
  59.9 0.8 %convolution_convert_fusion.1 = bf16[128,512]{1,0:T(8,128)(2,1)S(1)} fusion(bf16[128,2048]{1,0:T(8,128)(2,1)S(1)} %pad_maximum_fusion.2, bf16[512,2048]{1,0:T(8,128)(2,1)S(1)} %bitcast.49), kind=kOutput, calls=%fused_computation.2 | convolution fusion | flops 268500992 | bytes 2752512 | tf_op jit(solution)/shard_map/dot_general | solution.py:140
  60.7 3.0 %collective-permute-done.21 = bf16[64,2048]{1,0:T(8,128)(2,1)S(1)} collective-permute-done((bf16[64,2048]{1,0:T(8,128)(2,1)S(1)}, bf16[64,2048]{1,0:T(8,128)(2,1)S(1)}, u32[]{:S(2)}, u32[]{:S(2)}) %collective-permute-start.21) | collective-permute-done | bytes 262176 | tf_op jit(solution)/shard_map/ppermute | solution.py:100
  63.7 0.1 collective-permute-start.22
  63.8 0.8 %convolution_convert_fusion = bf16[128,512]{1,0:T(8,128)(2,1)S(1)} fusion(bf16[128,2048]{1,0:T(8,128)(2,1)S(1)} %pad_maximum_fusion.3, bf16[512,2048]{1,0:T(8,128)(2,1)S(1)} %bitcast.50), kind=kOutput, calls=%fused_computation.1 | convolution fusion | flops 268500992 | bytes 2752512 | tf_op jit(solution)/shard_map/dot_general | solution.py:140
  64.7 0.8 %convolution_convert_fusion.3 = bf16[128,512]{1,0:T(8,128)(2,1)S(1)} fusion(bf16[128,2048]{1,0:T(8,128)(2,1)S(1)} %collective-permute-done.18, bf16[512,2048]{1,0:T(8,128)(2,1)S(1)} %bitcast.51), kind=kOutput, calls=%fused_computation.4 | convolution fusion | flops 268500992 | bytes 2752512 | tf_op jit(solution)/shard_map/dot_general | solution.py:140
  65.5 0.2 collective-permute-done.22
  65.7 0.8 %convolution_convert_fusion.2 = bf16[128,512]{1,0:T(8,128)(2,1)S(1)} fusion(bf16[128,2048]{1,0:T(8,128)(2,1)S(1)} %collective-permute-done.22, bf16[512,2048]{1,0:T(8,128)(2,1)S(1)} %bitcast.52), kind=kOutput, calls=%fused_computation.3 | convolution fusion | flops 268500992 | bytes 2752512 | tf_op jit(solution)/shard_map/dot_general | solution.py:140
  66.6 0.1 broadcast_select_fusion.8
  66.6 0.1 broadcast_select_fusion.9
  66.7 1.8 %collective-permute-start.24 = (bf16[1,4,32,512]{3,2,1,0:T(8,128)(2,1)S(1)}, bf16[1,4,32,512]{3,2,1,0:T(8,128)(2,1)S(1)}, u32[]{:S(2)}, u32[]{:S(2)}) collective-permute-start(bf16[1,4,32,512]{3,2,1,0:T(8,128)(2,1)S(1)} %get-tuple-element.102), channel_id=1, source_target_pairs={{0,2},{1,3},{2,0},{3,1},{4,6},{5,7},{6,4},{7,5},{8,10},{9,11},{10,... | collective-permute-start | bytes 393224 | tf_op jit(solution)/shard_map/ppermute | solution.py:100
  68.5 0.9 %collective-permute-start.23 = (bf16[1,4,32,512]{3,2,1,0:T(8,128)(2,1)S(1)}, bf16[1,4,32,512]{3,2,1,0:T(8,128)(2,1)S(1)}, u32[]{:S(2)}, u32[]{:S(2)}) collective-permute-start(bf16[1,4,32,512]{3,2,1,0:T(8,128)(2,1)S(1)} %get-tuple-element.103), channel_id=1, source_target_pairs={{0,1},{1,0},{2,3},{3,2},{4,5},{5,4},{6,7},{7,6},{8,9},{9,8},{10,11... | collective-permute-start | bytes 393224 | tf_op jit(solution)/shard_map/ppermute | solution.py:100
  69.4 1.8 %collective-permute-start.25 = (bf16[1,4,32,512]{3,2,1,0:T(8,128)(2,1)S(1)}, bf16[1,4,32,512]{3,2,1,0:T(8,128)(2,1)S(1)}, u32[]{:S(2)}, u32[]{:S(2)}) collective-permute-start(bf16[1,4,32,512]{3,2,1,0:T(8,128)(2,1)S(1)} %get-tuple-element.119), channel_id=1, source_target_pairs={{0,3},{1,2},{2,1},{3,0},{4,7},{5,6},{6,5},{7,4},{8,11},{9,10},{10,... | collective-permute-start | bytes 393224 | tf_op jit(solution)/shard_map/ppermute | solution.py:100
  71.1 0.1 broadcast_select_fusion.31
  71.2 8.3 %collective-permute-done.23 = bf16[1,4,32,512]{3,2,1,0:T(8,128)(2,1)S(1)} collective-permute-done((bf16[1,4,32,512]{3,2,1,0:T(8,128)(2,1)S(1)}, bf16[1,4,32,512]{3,2,1,0:T(8,128)(2,1)S(1)}, u32[]{:S(2)}, u32[]{:S(2)}) %collective-permute-start.23) | collective-permute-done | bytes 131104 | tf_op jit(solution)/shard_map/ppermute | solution.py:100
  79.5 0.1 broadcast_select_fusion.27
  79.6 0.1 broadcast_select_fusion.26
  79.7 0.8 %pad.4 = f32[1,256,512]{2,1,0:T(8,128)} pad(f32[1,128,512]{2,1,0:T(8,128)S(1)} %bitcast.55, f32[]{:T(128)} %constant.113.clone.1), padding=0_0x0_128x0_0 | pad | bytes 786436 | tf_op jit(solution)/shard_map/jit(_pad)/pad | solution.py:236
  80.5 0.7 constant_dynamic-update-slice_fusion.6
  (54 shorter events, 0.6 us)
Async XLA Ops:
  0.0 1.2 %copy-start = (bf16[256,16,128]{2,1,0:T(8,128)(2,1)S(1)}, bf16[256,16,128]{2,1,0:T(8,128)(2,1)}, u32[]{:S(2)}) copy-start(bf16[256,16,128]{2,1,0:T(8,128)(2,1)} %param.5) | copy-start | bytes 3145732
  1.2 10.8 %collective-permute-start = (bf16[32,16,128]{2,1,0:T(8,128)(2,1)S(1)}, bf16[32,16,128]{2,1,0:T(8,128)(2,1)S(1)}, u32[]{:S(2)}, u32[]{:S(2)}) collective-permute-start(bf16[32,16,128]{2,1,0:T(8,128)(2,1)S(1)} %constant_dynamic-slice_fusion.7), channel_id=1, source_target_pairs={{0,3},{1,2},{2,1},{3,0},{4,7},{5,6},{6,5},{7,4},{8,11},{9,10},{10,... | collective-permute-start | bytes 393224 | tf_op jit(solution)/shard_map/ppermute | solution.py:100
  6.4 10.2 %collective-permute-start.2 = (bf16[32,16,128]{2,1,0:T(8,128)(2,1)S(1)}, bf16[32,16,128]{2,1,0:T(8,128)(2,1)S(1)}, u32[]{:S(2)}, u32[]{:S(2)}) collective-permute-start(bf16[32,16,128]{2,1,0:T(8,128)(2,1)S(1)} %constant_dynamic-slice_fusion.5), channel_id=1, source_target_pairs={{0,1},{1,0},{2,3},{3,2},{4,5},{5,4},{6,7},{7,6},{8,9},{9,8},{10,11... | collective-permute-start | bytes 393224 | tf_op jit(solution)/shard_map/ppermute | solution.py:100
  6.5 17.5 %collective-permute-start.1 = (bf16[32,16,128]{2,1,0:T(8,128)(2,1)S(1)}, bf16[32,16,128]{2,1,0:T(8,128)(2,1)S(1)}, u32[]{:S(2)}, u32[]{:S(2)}) collective-permute-start(bf16[32,16,128]{2,1,0:T(8,128)(2,1)S(1)} %constant_dynamic-slice_fusion.6), channel_id=1, source_target_pairs={{0,2},{1,3},{2,0},{3,1},{4,6},{5,7},{6,4},{7,5},{8,10},{9,11},{10,... | collective-permute-start | bytes 393224 | tf_op jit(solution)/shard_map/ppermute | solution.py:100
  8.2 3.7 %copy-start.1 = (f32[128,128]{1,0:T(8,128)S(1)}, f32[128,128]{1,0:T(8,128)}, u32[]{:S(2)}) copy-start(f32[128,128]{1,0:T(8,128)} %refs_6_.3) | copy-start | bytes 196612
  8.2 15.8 %copy-start.2 = (f32[64,128]{1,0:T(8,128)S(1)}, f32[64,128]{1,0:T(8,128)}, u32[]{:S(2)}) copy-start(f32[64,128]{1,0:T(8,128)} %refs_8_.3) | copy-start | bytes 98308
  12.1 16.3 %collective-permute-start.6 = (bf16[32,16,128]{2,1,0:T(8,128)(2,1)S(1)}, bf16[32,16,128]{2,1,0:T(8,128)(2,1)S(1)}, u32[]{:S(2)}, u32[]{:S(2)}) collective-permute-start(bf16[32,16,128]{2,1,0:T(8,128)(2,1)S(1)} %constant_dynamic-slice_fusion), channel_id=1, source_target_pairs={{0,3},{1,2},{2,1},{3,0},{4,7},{5,6},{6,5},{7,4},{8,11},{9,10},{10,... | collective-permute-start | bytes 393224 | tf_op jit(solution)/shard_map/ppermute | solution.py:100
  16.0 19.4 %collective-permute-start.5 = (bf16[32,16,128]{2,1,0:T(8,128)(2,1)S(1)}, bf16[32,16,128]{2,1,0:T(8,128)(2,1)S(1)}, u32[]{:S(2)}, u32[]{:S(2)}) collective-permute-start(bf16[32,16,128]{2,1,0:T(8,128)(2,1)S(1)} %constant_dynamic-slice_fusion.1), channel_id=1, source_target_pairs={{0,2},{1,3},{2,0},{3,1},{4,6},{5,7},{6,4},{7,5},{8,10},{9,11},{10,... | collective-permute-start | bytes 393224 | tf_op jit(solution)/shard_map/ppermute | solution.py:100
  16.0 19.4 %collective-permute-start.4 = (bf16[32,16,128]{2,1,0:T(8,128)(2,1)S(1)}, bf16[32,16,128]{2,1,0:T(8,128)(2,1)S(1)}, u32[]{:S(2)}, u32[]{:S(2)}) collective-permute-start(bf16[32,16,128]{2,1,0:T(8,128)(2,1)S(1)} %constant_dynamic-slice_fusion.2), channel_id=1, source_target_pairs={{0,1},{1,0},{2,3},{3,2},{4,5},{5,4},{6,7},{7,6},{8,9},{9,8},{10,11... | collective-permute-start | bytes 393224 | tf_op jit(solution)/shard_map/ppermute | solution.py:100
  26.2 9.1 %collective-permute-start.3 = (bf16[32,2048]{1,0:T(8,128)(2,1)S(1)}, bf16[32,2048]{1,0:T(8,128)(2,1)S(1)}, u32[]{:S(2)}, u32[]{:S(2)}) collective-permute-start(bf16[32,2048]{1,0:T(8,128)(2,1)S(1)} %get-tuple-element.67), channel_id=1, source_target_pairs={{0,1},{1,0},{2,3},{3,2},{4,5},{5,4},{6,7},{7,6},{8,9},{9,8},{10,11... | collective-permute-start | bytes 393224 | tf_op jit(solution)/shard_map/ppermute | solution.py:100
  26.3 13.0 %collective-permute-start.10 = (bf16[32,2048]{1,0:T(8,128)(2,1)S(1)}, bf16[32,2048]{1,0:T(8,128)(2,1)S(1)}, u32[]{:S(2)}, u32[]{:S(2)}) collective-permute-start(bf16[32,2048]{1,0:T(8,128)(2,1)S(1)} %get-tuple-element.87), channel_id=1, source_target_pairs={{0,2},{1,3},{2,0},{3,1},{4,6},{5,7},{6,4},{7,5},{8,10},{9,11},{10,... | collective-permute-start | bytes 393224 | tf_op jit(solution)/shard_map/ppermute | solution.py:100
  28.4 10.9 %collective-permute-start.11 = (bf16[32,2048]{1,0:T(8,128)(2,1)S(1)}, bf16[32,2048]{1,0:T(8,128)(2,1)S(1)}, u32[]{:S(2)}, u32[]{:S(2)}) collective-permute-start(bf16[32,2048]{1,0:T(8,128)(2,1)S(1)} %get-tuple-element.88), channel_id=1, source_target_pairs={{0,3},{1,2},{2,1},{3,0},{4,7},{5,6},{6,5},{7,4},{8,11},{9,10},{10,... | collective-permute-start | bytes 393224 | tf_op jit(solution)/shard_map/ppermute | solution.py:100
  35.4 10.0 %collective-permute-start.8 = (bf16[64,2048]{1,0:T(8,128)(2,1)S(1)}, bf16[64,2048]{1,0:T(8,128)(2,1)S(1)}, u32[]{:S(2)}, u32[]{:S(2)}) collective-permute-start(bf16[64,2048]{1,0:T(8,128)(2,1)S(1)} %constant_dynamic-update-slice_fusion), channel_id=1, source_target_pairs={{0,8},{4,12},{8,0},{12,4},{1,9},{5,13},{9,1},{13,5},{2,10},{6,14},... | collective-permute-start | bytes 786440 | tf_op jit(solution)/shard_map/ppermute | solution.py:100
  39.3 6.1 %collective-permute-start.7 = (bf16[32,2048]{1,0:T(8,128)(2,1)S(1)}, bf16[32,2048]{1,0:T(8,128)(2,1)S(1)}, u32[]{:S(2)}, u32[]{:S(2)}) collective-permute-start(bf16[32,2048]{1,0:T(8,128)(2,1)S(1)} %get-tuple-element.81), channel_id=1, source_target_pairs={{0,1},{1,0},{2,3},{3,2},{4,5},{5,4},{6,7},{7,6},{8,9},{9,8},{10,11... | collective-permute-start | bytes 393224 | tf_op jit(solution)/shard_map/ppermute | solution.py:100
  39.4 8.0 %collective-permute-start.12 = (bf16[64,2048]{1,0:T(8,128)(2,1)S(1)}, bf16[64,2048]{1,0:T(8,128)(2,1)S(1)}, u32[]{:S(2)}, u32[]{:S(2)}) collective-permute-start(bf16[64,2048]{1,0:T(8,128)(2,1)S(1)} %pad_maximum_fusion.4), channel_id=1, source_target_pairs={{0,8},{4,12},{8,0},{12,4},{1,9},{5,13},{9,1},{13,5},{2,10},{6,14},... | collective-permute-start | bytes 786440 | tf_op jit(solution)/shard_map/ppermute | solution.py:100
  39.9 7.6 %copy-start.3 = (bf16[64,8,16,128]{3,1,2,0:T(8,128)(2,1)S(1)}, bf16[64,8,16,128]{3,1,2,0:T(8,128)(2,1)}, u32[]{:S(2)}) copy-start(bf16[64,8,16,128]{3,1,2,0:T(8,128)(2,1)} %copy.19) | copy-start | bytes 6291460
  39.9 12.6 %collective-permute-start.19 = (bf16[32,2048]{1,0:T(8,128)(2,1)S(1)}, bf16[32,2048]{1,0:T(8,128)(2,1)S(1)}, u32[]{:S(2)}, u32[]{:S(2)}) collective-permute-start(bf16[32,2048]{1,0:T(8,128)(2,1)S(1)} %get-tuple-element.96), channel_id=1, source_target_pairs={{0,2},{1,3},{2,0},{3,1},{4,6},{5,7},{6,4},{7,5},{8,10},{9,11},{10,... | collective-permute-start | bytes 393224 | tf_op jit(solution)/shard_map/ppermute | solution.py:100
  43.1 9.5 %collective-permute-start.20 = (bf16[32,2048]{1,0:T(8,128)(2,1)S(1)}, bf16[32,2048]{1,0:T(8,128)(2,1)S(1)}, u32[]{:S(2)}, u32[]{:S(2)}) collective-permute-start(bf16[32,2048]{1,0:T(8,128)(2,1)S(1)} %get-tuple-element.97), channel_id=1, source_target_pairs={{0,3},{1,2},{2,1},{3,0},{4,7},{5,6},{6,5},{7,4},{8,11},{9,10},{10,... | collective-permute-start | bytes 393224 | tf_op jit(solution)/shard_map/ppermute | solution.py:100
  45.4 8.0 %collective-permute-start.9 = (bf16[128,2048]{1,0:T(8,128)(2,1)S(1)}, bf16[128,2048]{1,0:T(8,128)(2,1)S(1)}, u32[]{:S(2)}, u32[]{:S(2)}) collective-permute-start(bf16[128,2048]{1,0:T(8,128)(2,1)S(1)} %pad_maximum_fusion), channel_id=1, source_target_pairs={{0,4},{4,0},{8,12},{12,8},{1,5},{5,1},{9,13},{13,9},{2,6},{6,2},{1... | collective-permute-start | bytes 1572872 | tf_op jit(solution)/shard_map/ppermute | solution.py:100
  47.5 6.8 %collective-permute-start.13 = (bf16[128,2048]{1,0:T(8,128)(2,1)S(1)}, bf16[128,2048]{1,0:T(8,128)(2,1)S(1)}, u32[]{:S(2)}, u32[]{:S(2)}) collective-permute-start(bf16[128,2048]{1,0:T(8,128)(2,1)S(1)} %pad_maximum_fusion.1), channel_id=1, source_target_pairs={{0,4},{4,0},{8,12},{12,8},{1,5},{5,1},{9,13},{13,9},{2,6},{6,2},{1... | collective-permute-start | bytes 1572872 | tf_op jit(solution)/shard_map/ppermute | solution.py:100
  49.3 10.4 %collective-permute-start.17 = (bf16[64,2048]{1,0:T(8,128)(2,1)S(1)}, bf16[64,2048]{1,0:T(8,128)(2,1)S(1)}, u32[]{:S(2)}, u32[]{:S(2)}) collective-permute-start(bf16[64,2048]{1,0:T(8,128)(2,1)S(1)} %constant_dynamic-update-slice_fusion.2), channel_id=1, source_target_pairs={{0,8},{4,12},{8,0},{12,4},{1,9},{5,13},{9,1},{13,5},{2,10},{6,14},... | collective-permute-start | bytes 786440 | tf_op jit(solution)/shard_map/ppermute | solution.py:100
  52.6 11.1 %collective-permute-start.21 = (bf16[64,2048]{1,0:T(8,128)(2,1)S(1)}, bf16[64,2048]{1,0:T(8,128)(2,1)S(1)}, u32[]{:S(2)}, u32[]{:S(2)}) collective-permute-start(bf16[64,2048]{1,0:T(8,128)(2,1)S(1)} %constant_dynamic-update-slice_fusion.4), channel_id=1, source_target_pairs={{0,8},{4,12},{8,0},{12,4},{1,9},{5,13},{9,1},{13,5},{2,10},{6,14},... | collective-permute-start | bytes 786440 | tf_op jit(solution)/shard_map/ppermute | solution.py:100
  55.2 16.0 %collective-permute-start.16 = (bf16[1,4,32,512]{3,2,1,0:T(8,128)(2,1)S(1)}, bf16[1,4,32,512]{3,2,1,0:T(8,128)(2,1)S(1)}, u32[]{:S(2)}, u32[]{:S(2)}) collective-permute-start(bf16[1,4,32,512]{3,2,1,0:T(8,128)(2,1)S(1)} %get-tuple-element.123), channel_id=1, source_target_pairs={{0,3},{1,2},{2,1},{3,0},{4,7},{5,6},{6,5},{7,4},{8,11},{9,10},{10,... | collective-permute-start | bytes 393224 | tf_op jit(solution)/shard_map/ppermute | solution.py:100
  56.6 14.5 %collective-permute-start.15 = (bf16[1,4,32,512]{3,2,1,0:T(8,128)(2,1)S(1)}, bf16[1,4,32,512]{3,2,1,0:T(8,128)(2,1)S(1)}, u32[]{:S(2)}, u32[]{:S(2)}) collective-permute-start(bf16[1,4,32,512]{3,2,1,0:T(8,128)(2,1)S(1)} %get-tuple-element.89), channel_id=1, source_target_pairs={{0,2},{1,3},{2,0},{3,1},{4,6},{5,7},{6,4},{7,5},{8,10},{9,11},{10,... | collective-permute-start | bytes 393224 | tf_op jit(solution)/shard_map/ppermute | solution.py:100
  58.9 10.5 %collective-permute-start.14 = (bf16[1,4,32,512]{3,2,1,0:T(8,128)(2,1)S(1)}, bf16[1,4,32,512]{3,2,1,0:T(8,128)(2,1)S(1)}, u32[]{:S(2)}, u32[]{:S(2)}) collective-permute-start(bf16[1,4,32,512]{3,2,1,0:T(8,128)(2,1)S(1)} %get-tuple-element.90), channel_id=1, source_target_pairs={{0,1},{1,0},{2,3},{3,2},{4,5},{5,4},{6,7},{7,6},{8,9},{9,8},{10,11... | collective-permute-start | bytes 393224 | tf_op jit(solution)/shard_map/ppermute | solution.py:100
  59.8 4.9 %collective-permute-start.18 = (bf16[128,2048]{1,0:T(8,128)(2,1)S(1)}, bf16[128,2048]{1,0:T(8,128)(2,1)S(1)}, u32[]{:S(2)}, u32[]{:S(2)}) collective-permute-start(bf16[128,2048]{1,0:T(8,128)(2,1)S(1)} %pad_maximum_fusion.2), channel_id=1, source_target_pairs={{0,4},{4,0},{8,12},{12,8},{1,5},{5,1},{9,13},{13,9},{2,6},{6,2},{1... | collective-permute-start | bytes 1572872 | tf_op jit(solution)/shard_map/ppermute | solution.py:100
  63.7 2.0 %collective-permute-start.22 = (bf16[128,2048]{1,0:T(8,128)(2,1)S(1)}, bf16[128,2048]{1,0:T(8,128)(2,1)S(1)}, u32[]{:S(2)}, u32[]{:S(2)}) collective-permute-start(bf16[128,2048]{1,0:T(8,128)(2,1)S(1)} %pad_maximum_fusion.3), channel_id=1, source_target_pairs={{0,4},{4,0},{8,12},{12,8},{1,5},{5,1},{9,13},{13,9},{2,6},{6,2},{1... | collective-permute-start | bytes 1572872 | tf_op jit(solution)/shard_map/ppermute | solution.py:100
  66.7 12.8 %collective-permute-start.24 = (bf16[1,4,32,512]{3,2,1,0:T(8,128)(2,1)S(1)}, bf16[1,4,32,512]{3,2,1,0:T(8,128)(2,1)S(1)}, u32[]{:S(2)}, u32[]{:S(2)}) collective-permute-start(bf16[1,4,32,512]{3,2,1,0:T(8,128)(2,1)S(1)} %get-tuple-element.102), channel_id=1, source_target_pairs={{0,2},{1,3},{2,0},{3,1},{4,6},{5,7},{6,4},{7,5},{8,10},{9,11},{10,... | collective-permute-start | bytes 393224 | tf_op jit(solution)/shard_map/ppermute | solution.py:100
  68.5 11.0 %collective-permute-start.23 = (bf16[1,4,32,512]{3,2,1,0:T(8,128)(2,1)S(1)}, bf16[1,4,32,512]{3,2,1,0:T(8,128)(2,1)S(1)}, u32[]{:S(2)}, u32[]{:S(2)}) collective-permute-start(bf16[1,4,32,512]{3,2,1,0:T(8,128)(2,1)S(1)} %get-tuple-element.103), channel_id=1, source_target_pairs={{0,1},{1,0},{2,3},{3,2},{4,5},{5,4},{6,7},{7,6},{8,9},{9,8},{10,11... | collective-permute-start | bytes 393224 | tf_op jit(solution)/shard_map/ppermute | solution.py:100
  69.4 10.1 %collective-permute-start.25 = (bf16[1,4,32,512]{3,2,1,0:T(8,128)(2,1)S(1)}, bf16[1,4,32,512]{3,2,1,0:T(8,128)(2,1)S(1)}, u32[]{:S(2)}, u32[]{:S(2)}) collective-permute-start(bf16[1,4,32,512]{3,2,1,0:T(8,128)(2,1)S(1)} %get-tuple-element.119), channel_id=1, source_target_pairs={{0,3},{1,2},{2,1},{3,0},{4,7},{5,6},{6,5},{7,4},{8,11},{9,10},{10,... | collective-permute-start | bytes 393224 | tf_op jit(solution)/shard_map/ppermute | solution.py:100

commit v23 on v20

--- a/solution.py
+++ b/solution.py
@@ -212,11 +212,14 @@
     spread_b1 = after(spread_b1, came[0])
     near_b1 = lax.optimization_barrier(jnp.concatenate(spread_b1, axis=0))
     far_b1 = crossed(near_b1, "dp", shares, 1)
-    val_b1 = products(near_b1, far_b1, train_flat, shares)
     spread_b2 = after(spread_b2, came[0])
     near_b2 = lax.optimization_barrier(jnp.concatenate(spread_b2, axis=0))
     far_b2 = crossed(near_b2, "dp", shares, 1)
-    val_b2 = products(near_b2, far_b2, train_flat, shares)
+    both = lax.optimization_barrier(jnp.concatenate([far_b1, near_b2], axis=0))
+    joint = products(both, far_b2, train_flat, shares)
+    cut = far_b1.shape[0]
+    val_b1 = [products(near_b1, near_b1, train_flat, shares)[0], joint[0][:cut]]
+    val_b2 = [joint[0][cut:], joint[1]]
     part_b1 = split_shares(val_b1, shares)
     part_b1 = [jnp.concatenate(part_b1[at * owned:(at + 1) * owned]) for at in range(slices)]
     part_b1 = [value.reshape(owned, half, -1, train_count) for value in part_b1]

time: 80.9 us -> 81.5 us (level)
  waiting for transfers between devices: 27.9 us -> 29 us
  matrix products: 6.67 us -> 5.74 us
    ppermute x26, waiting for transfers between devices: 27.9 us -> 29 us  [crossed(): return lax.ppermute(value, axis, [(at, at ^ mask) for at in range(size)])]
    dot_general x8 -> x7, matrix products: 6.67 us -> 5.74 us  [products(): lax.dot_general(block, train_flat, contract, preferred_element_type=jnp.f...]
  transfers between devices with their start and end apart: 26 -> 26, of which waited for: 8 -> 8; matrix products, arithmetic and copies ran while one was open for 15% -> 14% of each run, Pallas kernels for 6% -> 6%
where the time goes in v23:
time: 81.5 us; the launch traced here: 81.2 us
  starting transfers between devices  33.6 us (41%)
  waiting for transfers between devices  29 us (36%)
  local copies, waits for them, and re-layouts  6.27 us (8%)
  matrix products  5.74 us (7%)
  Pallas kernels  4.47 us (5%)
  other arithmetic  1.62 us (2%)
    ppermute x26, starting transfers between devices, crossed(): return lax.ppermute(value, axis, [(at, at ^ mask) for at in range(size)])  33.6 us
    ppermute x26, waiting for transfers between devices, crossed(): return lax.ppermute(value, axis, [(at, at ^ mask) for at in range(size)])  29 us
    dot_general x7, matrix products, products(): lax.dot_general(block, train_flat, contract, preferred_element_type=jnp.f...  5.74 us
    unnamed x17, local copies, waits for them, and re-layouts  5.2 us
    pallas_call x2, Pallas kernels, condition_fast(): pl.pallas_call(functools.partial(condition_kernel, slices, rows_here), gr...  4.47 us
  transfers between devices with their start and end apart: 26, of which 8 were waited for; matrix products, arithmetic and copies ran while one was open for 14% of the time, Pallas kernels for 6%

profile of v23, /device:TPU:0, one launch (start us, length us, event | category | flops | bytes accessed | tf_op | source)
XLA Modules:
  0.0 81.2 jit_solution(3325499094507974464)
XLA Ops:
  0.0 1.2 %copy-done = bf16[256,16,128]{2,1,0:T(8,128)(2,1)S(1)} copy-done((bf16[256,16,128]{2,1,0:T(8,128)(2,1)S(1)}, bf16[256,16,128]{2,1,0:T(8,128)(2,1)}, u32[]{:S(2)}) %copy-start) | copy-done | bytes 1048600
  1.2 5.1 %collective-permute-start = (bf16[32,16,128]{2,1,0:T(8,128)(2,1)S(1)}, bf16[32,16,128]{2,1,0:T(8,128)(2,1)S(1)}, u32[]{:S(2)}, u32[]{:S(2)}) collective-permute-start(bf16[32,16,128]{2,1,0:T(8,128)(2,1)S(1)} %constant_dynamic-slice_fusion.7), channel_id=1, source_target_pairs={{0,3},{1,2},{2,1},{3,0},{4,7},{5,6},{6,5},{7,4},{8,11},{9,10},{10,... | collective-permute-start | bytes 393224 | tf_op jit(solution)/shard_map/ppermute | solution.py:100
  6.4 0.1 collective-permute-start.2
  6.5 0.6 collective-permute-start.1
  7.1 0.7 fusion.7
  7.8 0.1 copy.13
  7.9 0.1 copy.14
  8.0 0.1 copy.15
  8.1 0.1 copy.16
  8.2 0.0 copy-start.1
  8.2 0.0 copy-start.2
  8.2 3.5 %copy.19 = bf16[64,8,16,128]{3,1,2,0:T(8,128)(2,1)} copy(bf16[64,8,16,128]{3,2,1,0:T(8,128)(2,1)} %bitcast.51) | data formatting | bytes 4194304
  11.7 0.1 pad_maximum_fusion.16
  11.8 0.1 copy.11.refs_4_
  11.9 0.0 copy-done.1
  11.9 0.1 copy.10
  12.0 0.0 collective-permute-done.refs_0_
  12.2 3.8 %collective-permute-start.6 = (bf16[32,16,128]{2,1,0:T(8,128)(2,1)S(1)}, bf16[32,16,128]{2,1,0:T(8,128)(2,1)S(1)}, u32[]{:S(2)}, u32[]{:S(2)}) collective-permute-start(bf16[32,16,128]{2,1,0:T(8,128)(2,1)S(1)} %constant_dynamic-slice_fusion), channel_id=1, source_target_pairs={{0,3},{1,2},{2,1},{3,0},{4,7},{5,6},{6,5},{7,4},{8,11},{9,10},{10,... | collective-permute-start | bytes 393224 | tf_op jit(solution)/shard_map/ppermute | solution.py:100
  16.0 0.0 collective-permute-start.5
  16.0 0.6 collective-permute-start.4
  16.6 7.4 %collective-permute-done.1.refs_1_ = bf16[32,16,128]{2,1,0:T(8,128)(2,1)S(1)} collective-permute-done((bf16[32,16,128]{2,1,0:T(8,128)(2,1)S(1)}, bf16[32,16,128]{2,1,0:T(8,128)(2,1)S(1)}, u32[]{:S(2)}, u32[]{:S(2)}) %collective-permute-start.1) | collective-permute-done | bytes 131104 | tf_op jit(solution)/shard_map/ppermute | solution.py:100
  24.0 2.2 %shard_map.55 = (bf16[32,2048]{1,0:T(8,128)(2,1)S(1)}, bf16[32,2048]{1,0:T(8,128)(2,1)S(1)}, bf16[32,2048]{1,0:T(8,128)(2,1)S(1)}, bf16[32,2048]{1,0:T(8,128)(2,1)S(1)}) custom-call(bf16[32,16,128]{2,1,0:T(8,128)(2,1)S(1)} %collective-permute-done.refs_0_, bf16[32,16,128]{2,1,0:T(8,128)(2,1)S(1)} %collective-permute-done.1.refs_1_, ...), custom_call_target="tpu_custom_call" | custom-call | tf_op jit(solution)/shard_map/pallas_call | solution.py:75
  26.2 0.1 collective-permute-start.3
  26.3 2.1 %collective-permute-start.10 = (bf16[32,2048]{1,0:T(8,128)(2,1)S(1)}, bf16[32,2048]{1,0:T(8,128)(2,1)S(1)}, u32[]{:S(2)}, u32[]{:S(2)}) collective-permute-start(bf16[32,2048]{1,0:T(8,128)(2,1)S(1)} %get-tuple-element.87), channel_id=1, source_target_pairs={{0,2},{1,3},{2,0},{3,1},{4,6},{5,7},{6,4},{7,5},{8,10},{9,11},{10,... | collective-permute-start | bytes 393224 | tf_op jit(solution)/shard_map/ppermute | solution.py:100
  28.4 2.3 %collective-permute-start.11 = (bf16[32,2048]{1,0:T(8,128)(2,1)S(1)}, bf16[32,2048]{1,0:T(8,128)(2,1)S(1)}, u32[]{:S(2)}, u32[]{:S(2)}) collective-permute-start(bf16[32,2048]{1,0:T(8,128)(2,1)S(1)} %get-tuple-element.88), channel_id=1, source_target_pairs={{0,3},{1,2},{2,1},{3,0},{4,7},{5,6},{6,5},{7,4},{8,11},{9,10},{10,... | collective-permute-start | bytes 393224 | tf_op jit(solution)/shard_map/ppermute | solution.py:100
  30.7 4.7 %collective-permute-done.5.refs_1_ = bf16[32,16,128]{2,1,0:T(8,128)(2,1)S(1)} collective-permute-done((bf16[32,16,128]{2,1,0:T(8,128)(2,1)S(1)}, bf16[32,16,128]{2,1,0:T(8,128)(2,1)S(1)}, u32[]{:S(2)}, u32[]{:S(2)}) %collective-permute-start.5) | collective-permute-done | bytes 131104 | tf_op jit(solution)/shard_map/ppermute | solution.py:100
  35.4 1.6 %collective-permute-start.8 = (bf16[64,2048]{1,0:T(8,128)(2,1)S(1)}, bf16[64,2048]{1,0:T(8,128)(2,1)S(1)}, u32[]{:S(2)}, u32[]{:S(2)}) collective-permute-start(bf16[64,2048]{1,0:T(8,128)(2,1)S(1)} %constant_dynamic-update-slice_fusion), channel_id=1, source_target_pairs={{0,8},{4,12},{8,0},{12,4},{1,9},{5,13},{9,1},{13,5},{2,10},{6,14},... | collective-permute-start | bytes 786440 | tf_op jit(solution)/shard_map/ppermute | solution.py:100
  37.0 2.2 %shard_map.56 = (bf16[32,2048]{1,0:T(8,128)(2,1)S(1)}, bf16[32,2048]{1,0:T(8,128)(2,1)S(1)}, bf16[32,2048]{1,0:T(8,128)(2,1)S(1)}, bf16[32,2048]{1,0:T(8,128)(2,1)S(1)}) custom-call(bf16[32,16,128]{2,1,0:T(8,128)(2,1)S(1)} %collective-permute-done.6.refs_0_, bf16[32,16,128]{2,1,0:T(8,128)(2,1)S(1)} %collective-permute-done.5.refs_1_, ...), custom_call_target="tpu_custom_call" | custom-call | tf_op jit(solution)/shard_map/pallas_call | solution.py:75
  39.2 0.1 collective-permute-start.7
  39.4 0.5 collective-permute-start.12
  39.9 3.2 %collective-permute-start.19 = (bf16[32,2048]{1,0:T(8,128)(2,1)S(1)}, bf16[32,2048]{1,0:T(8,128)(2,1)S(1)}, u32[]{:S(2)}, u32[]{:S(2)}) collective-permute-start(bf16[32,2048]{1,0:T(8,128)(2,1)S(1)} %get-tuple-element.96), channel_id=1, source_target_pairs={{0,2},{1,3},{2,0},{3,1},{4,6},{5,7},{6,4},{7,5},{8,10},{9,11},{10,... | collective-permute-start | bytes 393224 | tf_op jit(solution)/shard_map/ppermute | solution.py:100
  43.1 1.4 %collective-permute-start.20 = (bf16[32,2048]{1,0:T(8,128)(2,1)S(1)}, bf16[32,2048]{1,0:T(8,128)(2,1)S(1)}, u32[]{:S(2)}, u32[]{:S(2)}) collective-permute-start(bf16[32,2048]{1,0:T(8,128)(2,1)S(1)} %get-tuple-element.97), channel_id=1, source_target_pairs={{0,3},{1,2},{2,1},{3,0},{4,7},{5,6},{6,5},{7,4},{8,11},{9,10},{10,... | collective-permute-start | bytes 393224 | tf_op jit(solution)/shard_map/ppermute | solution.py:100
  44.5 0.8 %collective-permute-done.7 = bf16[32,2048]{1,0:T(8,128)(2,1)S(1)} collective-permute-done((bf16[32,2048]{1,0:T(8,128)(2,1)S(1)}, bf16[32,2048]{1,0:T(8,128)(2,1)S(1)}, u32[]{:S(2)}, u32[]{:S(2)}) %collective-permute-start.7) | collective-permute-done | bytes 131104 | tf_op jit(solution)/shard_map/ppermute | solution.py:100
  45.4 0.1 collective-permute-start.9
  45.4 2.0 %collective-permute-done.12 = bf16[64,2048]{1,0:T(8,128)(2,1)S(1)} collective-permute-done((bf16[64,2048]{1,0:T(8,128)(2,1)S(1)}, bf16[64,2048]{1,0:T(8,128)(2,1)S(1)}, u32[]{:S(2)}, u32[]{:S(2)}) %collective-permute-start.12) | collective-permute-done | bytes 262176 | tf_op jit(solution)/shard_map/ppermute | solution.py:100
  47.5 0.1 collective-permute-start.13
  47.6 0.8 %convolution_convert_fusion.4 = bf16[128,512]{1,0:T(8,128)(2,1)S(1)} fusion(bf16[128,2048]{1,0:T(8,128)(2,1)S(1)} %pad_maximum_fusion.1, bf16[512,2048]{1,0:T(8,128)(2,1)S(1)} %bitcast.44), kind=kOutput, calls=%fused_computation.5 | convolution fusion | flops 268500992 | bytes 2752512 | tf_op jit(solution)/shard_map/dot_general | solution.py:140
  48.4 0.8 %convolution_convert_fusion.3 = bf16[128,512]{1,0:T(8,128)(2,1)S(1)} fusion(bf16[128,2048]{1,0:T(8,128)(2,1)S(1)} %pad_maximum_fusion.2, bf16[512,2048]{1,0:T(8,128)(2,1)S(1)} %bitcast.45), kind=kOutput, calls=%fused_computation.4 | convolution fusion | flops 268500992 | bytes 2752512 | tf_op jit(solution)/shard_map/dot_general | solution.py:140
  49.3 1.6 %collective-permute-start.17 = (bf16[64,2048]{1,0:T(8,128)(2,1)S(1)}, bf16[64,2048]{1,0:T(8,128)(2,1)S(1)}, u32[]{:S(2)}, u32[]{:S(2)}) collective-permute-start(bf16[64,2048]{1,0:T(8,128)(2,1)S(1)} %constant_dynamic-update-slice_fusion.2), channel_id=1, source_target_pairs={{0,8},{4,12},{8,0},{12,4},{1,9},{5,13},{9,1},{13,5},{2,10},{6,14},... | collective-permute-start | bytes 786440 | tf_op jit(solution)/shard_map/ppermute | solution.py:100
  50.9 1.7 %collective-permute-done.19 = bf16[32,2048]{1,0:T(8,128)(2,1)S(1)} collective-permute-done((bf16[32,2048]{1,0:T(8,128)(2,1)S(1)}, bf16[32,2048]{1,0:T(8,128)(2,1)S(1)}, u32[]{:S(2)}, u32[]{:S(2)}) %collective-permute-start.19) | collective-permute-done | bytes 131104 | tf_op jit(solution)/shard_map/ppermute | solution.py:100
  52.6 0.8 collective-permute-start.21
  53.4 0.8 %convolution_convert_fusion.6 = bf16[128,512]{1,0:T(8,128)(2,1)S(1)} fusion(bf16[128,2048]{1,0:T(8,128)(2,1)S(1)} %collective-permute-done.9, bf16[512,2048]{1,0:T(8,128)(2,1)S(1)} %bitcast.46), kind=kOutput, calls=%fused_computation.7 | convolution fusion | flops 268500992 | bytes 2752512 | tf_op jit(solution)/shard_map/dot_general | solution.py:140
  54.2 0.8 %convolution_convert_fusion.5 = bf16[128,512]{1,0:T(8,128)(2,1)S(1)} fusion(bf16[128,2048]{1,0:T(8,128)(2,1)S(1)} %collective-permute-done.13, bf16[512,2048]{1,0:T(8,128)(2,1)S(1)} %bitcast.47), kind=kOutput, calls=%fused_computation.6 | convolution fusion | flops 268500992 | bytes 2752512 | tf_op jit(solution)/shard_map/dot_general | solution.py:140
  55.1 1.4 %collective-permute-start.16 = (bf16[1,4,32,512]{3,2,1,0:T(8,128)(2,1)S(1)}, bf16[1,4,32,512]{3,2,1,0:T(8,128)(2,1)S(1)}, u32[]{:S(2)}, u32[]{:S(2)}) collective-permute-start(bf16[1,4,32,512]{3,2,1,0:T(8,128)(2,1)S(1)} %get-tuple-element.123), channel_id=1, source_target_pairs={{0,3},{1,2},{2,1},{3,0},{4,7},{5,6},{6,5},{7,4},{8,11},{9,10},{10,... | collective-permute-start | bytes 393224 | tf_op jit(solution)/shard_map/ppermute | solution.py:100
  56.6 2.3 %collective-permute-start.15 = (bf16[1,4,32,512]{3,2,1,0:T(8,128)(2,1)S(1)}, bf16[1,4,32,512]{3,2,1,0:T(8,128)(2,1)S(1)}, u32[]{:S(2)}, u32[]{:S(2)}) collective-permute-start(bf16[1,4,32,512]{3,2,1,0:T(8,128)(2,1)S(1)} %get-tuple-element.89), channel_id=1, source_target_pairs={{0,2},{1,3},{2,0},{3,1},{4,6},{5,7},{6,4},{7,5},{8,10},{9,11},{10,... | collective-permute-start | bytes 393224 | tf_op jit(solution)/shard_map/ppermute | solution.py:100
  58.9 0.8 %collective-permute-start.14 = (bf16[1,4,32,512]{3,2,1,0:T(8,128)(2,1)S(1)}, bf16[1,4,32,512]{3,2,1,0:T(8,128)(2,1)S(1)}, u32[]{:S(2)}, u32[]{:S(2)}) collective-permute-start(bf16[1,4,32,512]{3,2,1,0:T(8,128)(2,1)S(1)} %get-tuple-element.90), channel_id=1, source_target_pairs={{0,1},{1,0},{2,3},{3,2},{4,5},{5,4},{6,7},{7,6},{8,9},{9,8},{10,11... | collective-permute-start | bytes 393224 | tf_op jit(solution)/shard_map/ppermute | solution.py:100
  59.7 4.0 %collective-permute-done.21 = bf16[64,2048]{1,0:T(8,128)(2,1)S(1)} collective-permute-done((bf16[64,2048]{1,0:T(8,128)(2,1)S(1)}, bf16[64,2048]{1,0:T(8,128)(2,1)S(1)}, u32[]{:S(2)}, u32[]{:S(2)}) %collective-permute-start.21) | collective-permute-done | bytes 262176 | tf_op jit(solution)/shard_map/ppermute | solution.py:100
  63.7 0.1 collective-permute-start.22
  63.8 0.6 collective-permute-start.18
  64.4 0.8 %convolution_convert_fusion.1 = bf16[128,512]{1,0:T(8,128)(2,1)S(1)} fusion(bf16[128,2048]{1,0:T(8,128)(2,1)S(1)} %pad_maximum_fusion.3, bf16[512,2048]{1,0:T(8,128)(2,1)S(1)} %bitcast.48), kind=kOutput, calls=%fused_computation.2 | convolution fusion | flops 268500992 | bytes 2752512 | tf_op jit(solution)/shard_map/dot_general | solution.py:140
  65.3 0.4 collective-permute-done.22
  65.7 0.8 %convolution_convert_fusion.2 = bf16[128,512]{1,0:T(8,128)(2,1)S(1)} fusion(bf16[128,2048]{1,0:T(8,128)(2,1)S(1)} %collective-permute-done.22, bf16[512,2048]{1,0:T(8,128)(2,1)S(1)} %bitcast.49), kind=kOutput, calls=%fused_computation.3 | convolution fusion | flops 268500992 | bytes 2752512 | tf_op jit(solution)/shard_map/dot_general | solution.py:140
  66.6 0.1 pad_maximum_fusion
  66.6 0.7 convolution_convert_fusion
  67.4 0.1 broadcast_select_fusion.9
  67.5 1.8 %collective-permute-start.24 = (bf16[1,4,32,512]{3,2,1,0:T(8,128)(2,1)S(1)}, bf16[1,4,32,512]{3,2,1,0:T(8,128)(2,1)S(1)}, u32[]{:S(2)}, u32[]{:S(2)}) collective-permute-start(bf16[1,4,32,512]{3,2,1,0:T(8,128)(2,1)S(1)} %get-tuple-element.102), channel_id=1, source_target_pairs={{0,2},{1,3},{2,0},{3,1},{4,6},{5,7},{6,4},{7,5},{8,10},{9,11},{10,... | collective-permute-start | bytes 393224 | tf_op jit(solution)/shard_map/ppermute | solution.py:100
  69.3 0.1 broadcast_select_fusion.11
  69.3 0.9 %collective-permute-start.23 = (bf16[1,4,32,512]{3,2,1,0:T(8,128)(2,1)S(1)}, bf16[1,4,32,512]{3,2,1,0:T(8,128)(2,1)S(1)}, u32[]{:S(2)}, u32[]{:S(2)}) collective-permute-start(bf16[1,4,32,512]{3,2,1,0:T(8,128)(2,1)S(1)} %get-tuple-element.103), channel_id=1, source_target_pairs={{0,1},{1,0},{2,3},{3,2},{4,5},{5,4},{6,7},{7,6},{8,9},{9,8},{10,11... | collective-permute-start | bytes 393224 | tf_op jit(solution)/shard_map/ppermute | solution.py:100
  70.3 1.8 %collective-permute-start.25 = (bf16[1,4,32,512]{3,2,1,0:T(8,128)(2,1)S(1)}, bf16[1,4,32,512]{3,2,1,0:T(8,128)(2,1)S(1)}, u32[]{:S(2)}, u32[]{:S(2)}) collective-permute-start(bf16[1,4,32,512]{3,2,1,0:T(8,128)(2,1)S(1)} %get-tuple-element.122), channel_id=1, source_target_pairs={{0,3},{1,2},{2,1},{3,0},{4,7},{5,6},{6,5},{7,4},{8,11},{9,10},{10,... | collective-permute-start | bytes 393224 | tf_op jit(solution)/shard_map/ppermute | solution.py:100
  72.1 0.1 broadcast_select_fusion.31
  72.1 8.0 %collective-permute-done.23 = bf16[1,4,32,512]{3,2,1,0:T(8,128)(2,1)S(1)} collective-permute-done((bf16[1,4,32,512]{3,2,1,0:T(8,128)(2,1)S(1)}, bf16[1,4,32,512]{3,2,1,0:T(8,128)(2,1)S(1)}, u32[]{:S(2)}, u32[]{:S(2)}) %collective-permute-start.23) | collective-permute-done | bytes 131104 | tf_op jit(solution)/shard_map/ppermute | solution.py:100
  80.2 0.1 broadcast_select_fusion.27
  80.3 0.1 broadcast_select_fusion.26
  80.4 0.8 %maximum_bitcast_fusion = f32[256,512]{1,0:T(8,128)} fusion(f32[1,128,512]{2,1,0:T(8,128)S(1)} %bitcast.53, f32[1,128,512]{2,1,0:T(8,128)S(1)} %bitcast.52), kind=kLoop, calls=%fused_computation.13 | loop fusion | flops 131072 | bytes 1048576 | tf_op jit(solution)/shard_map/reshape | solution.py:239
  (52 shorter events, 0.6 us)
Async XLA Ops:
  0.0 1.2 %copy-start = (bf16[256,16,128]{2,1,0:T(8,128)(2,1)S(1)}, bf16[256,16,128]{2,1,0:T(8,128)(2,1)}, u32[]{:S(2)}) copy-start(bf16[256,16,128]{2,1,0:T(8,128)(2,1)} %param.5) | copy-start | bytes 3145732
  1.2 10.8 %collective-permute-start = (bf16[32,16,128]{2,1,0:T(8,128)(2,1)S(1)}, bf16[32,16,128]{2,1,0:T(8,128)(2,1)S(1)}, u32[]{:S(2)}, u32[]{:S(2)}) collective-permute-start(bf16[32,16,128]{2,1,0:T(8,128)(2,1)S(1)} %constant_dynamic-slice_fusion.7), channel_id=1, source_target_pairs={{0,3},{1,2},{2,1},{3,0},{4,7},{5,6},{6,5},{7,4},{8,11},{9,10},{10,... | collective-permute-start | bytes 393224 | tf_op jit(solution)/shard_map/ppermute | solution.py:100
  6.4 10.2 %collective-permute-start.2 = (bf16[32,16,128]{2,1,0:T(8,128)(2,1)S(1)}, bf16[32,16,128]{2,1,0:T(8,128)(2,1)S(1)}, u32[]{:S(2)}, u32[]{:S(2)}) collective-permute-start(bf16[32,16,128]{2,1,0:T(8,128)(2,1)S(1)} %constant_dynamic-slice_fusion.5), channel_id=1, source_target_pairs={{0,1},{1,0},{2,3},{3,2},{4,5},{5,4},{6,7},{7,6},{8,9},{9,8},{10,11... | collective-permute-start | bytes 393224 | tf_op jit(solution)/shard_map/ppermute | solution.py:100
  6.5 17.5 %collective-permute-start.1 = (bf16[32,16,128]{2,1,0:T(8,128)(2,1)S(1)}, bf16[32,16,128]{2,1,0:T(8,128)(2,1)S(1)}, u32[]{:S(2)}, u32[]{:S(2)}) collective-permute-start(bf16[32,16,128]{2,1,0:T(8,128)(2,1)S(1)} %constant_dynamic-slice_fusion.6), channel_id=1, source_target_pairs={{0,2},{1,3},{2,0},{3,1},{4,6},{5,7},{6,4},{7,5},{8,10},{9,11},{10,... | collective-permute-start | bytes 393224 | tf_op jit(solution)/shard_map/ppermute | solution.py:100
  8.2 3.7 %copy-start.1 = (f32[128,128]{1,0:T(8,128)S(1)}, f32[128,128]{1,0:T(8,128)}, u32[]{:S(2)}) copy-start(f32[128,128]{1,0:T(8,128)} %refs_6_.3) | copy-start | bytes 196612
  8.2 15.8 %copy-start.2 = (f32[64,128]{1,0:T(8,128)S(1)}, f32[64,128]{1,0:T(8,128)}, u32[]{:S(2)}) copy-start(f32[64,128]{1,0:T(8,128)} %refs_8_.3) | copy-start | bytes 98308
  12.2 16.3 %collective-permute-start.6 = (bf16[32,16,128]{2,1,0:T(8,128)(2,1)S(1)}, bf16[32,16,128]{2,1,0:T(8,128)(2,1)S(1)}, u32[]{:S(2)}, u32[]{:S(2)}) collective-permute-start(bf16[32,16,128]{2,1,0:T(8,128)(2,1)S(1)} %constant_dynamic-slice_fusion), channel_id=1, source_target_pairs={{0,3},{1,2},{2,1},{3,0},{4,7},{5,6},{6,5},{7,4},{8,11},{9,10},{10,... | collective-permute-start | bytes 393224 | tf_op jit(solution)/shard_map/ppermute | solution.py:100
  16.0 19.4 %collective-permute-start.5 = (bf16[32,16,128]{2,1,0:T(8,128)(2,1)S(1)}, bf16[32,16,128]{2,1,0:T(8,128)(2,1)S(1)}, u32[]{:S(2)}, u32[]{:S(2)}) collective-permute-start(bf16[32,16,128]{2,1,0:T(8,128)(2,1)S(1)} %constant_dynamic-slice_fusion.1), channel_id=1, source_target_pairs={{0,2},{1,3},{2,0},{3,1},{4,6},{5,7},{6,4},{7,5},{8,10},{9,11},{10,... | collective-permute-start | bytes 393224 | tf_op jit(solution)/shard_map/ppermute | solution.py:100
  16.0 19.4 %collective-permute-start.4 = (bf16[32,16,128]{2,1,0:T(8,128)(2,1)S(1)}, bf16[32,16,128]{2,1,0:T(8,128)(2,1)S(1)}, u32[]{:S(2)}, u32[]{:S(2)}) collective-permute-start(bf16[32,16,128]{2,1,0:T(8,128)(2,1)S(1)} %constant_dynamic-slice_fusion.2), channel_id=1, source_target_pairs={{0,1},{1,0},{2,3},{3,2},{4,5},{5,4},{6,7},{7,6},{8,9},{9,8},{10,11... | collective-permute-start | bytes 393224 | tf_op jit(solution)/shard_map/ppermute | solution.py:100
  26.2 9.1 %collective-permute-start.3 = (bf16[32,2048]{1,0:T(8,128)(2,1)S(1)}, bf16[32,2048]{1,0:T(8,128)(2,1)S(1)}, u32[]{:S(2)}, u32[]{:S(2)}) collective-permute-start(bf16[32,2048]{1,0:T(8,128)(2,1)S(1)} %get-tuple-element.67), channel_id=1, source_target_pairs={{0,1},{1,0},{2,3},{3,2},{4,5},{5,4},{6,7},{7,6},{8,9},{9,8},{10,11... | collective-permute-start | bytes 393224 | tf_op jit(solution)/shard_map/ppermute | solution.py:100
  26.3 13.0 %collective-permute-start.10 = (bf16[32,2048]{1,0:T(8,128)(2,1)S(1)}, bf16[32,2048]{1,0:T(8,128)(2,1)S(1)}, u32[]{:S(2)}, u32[]{:S(2)}) collective-permute-start(bf16[32,2048]{1,0:T(8,128)(2,1)S(1)} %get-tuple-element.87), channel_id=1, source_target_pairs={{0,2},{1,3},{2,0},{3,1},{4,6},{5,7},{6,4},{7,5},{8,10},{9,11},{10,... | collective-permute-start | bytes 393224 | tf_op jit(solution)/shard_map/ppermute | solution.py:100
  28.4 10.9 %collective-permute-start.11 = (bf16[32,2048]{1,0:T(8,128)(2,1)S(1)}, bf16[32,2048]{1,0:T(8,128)(2,1)S(1)}, u32[]{:S(2)}, u32[]{:S(2)}) collective-permute-start(bf16[32,2048]{1,0:T(8,128)(2,1)S(1)} %get-tuple-element.88), channel_id=1, source_target_pairs={{0,3},{1,2},{2,1},{3,0},{4,7},{5,6},{6,5},{7,4},{8,11},{9,10},{10,... | collective-permute-start | bytes 393224 | tf_op jit(solution)/shard_map/ppermute | solution.py:100
  35.4 9.9 %collective-permute-start.8 = (bf16[64,2048]{1,0:T(8,128)(2,1)S(1)}, bf16[64,2048]{1,0:T(8,128)(2,1)S(1)}, u32[]{:S(2)}, u32[]{:S(2)}) collective-permute-start(bf16[64,2048]{1,0:T(8,128)(2,1)S(1)} %constant_dynamic-update-slice_fusion), channel_id=1, source_target_pairs={{0,8},{4,12},{8,0},{12,4},{1,9},{5,13},{9,1},{13,5},{2,10},{6,14},... | collective-permute-start | bytes 786440 | tf_op jit(solution)/shard_map/ppermute | solution.py:100
  39.2 6.1 %collective-permute-start.7 = (bf16[32,2048]{1,0:T(8,128)(2,1)S(1)}, bf16[32,2048]{1,0:T(8,128)(2,1)S(1)}, u32[]{:S(2)}, u32[]{:S(2)}) collective-permute-start(bf16[32,2048]{1,0:T(8,128)(2,1)S(1)} %get-tuple-element.81), channel_id=1, source_target_pairs={{0,1},{1,0},{2,3},{3,2},{4,5},{5,4},{6,7},{7,6},{8,9},{9,8},{10,11... | collective-permute-start | bytes 393224 | tf_op jit(solution)/shard_map/ppermute | solution.py:100
  39.4 8.1 %collective-permute-start.12 = (bf16[64,2048]{1,0:T(8,128)(2,1)S(1)}, bf16[64,2048]{1,0:T(8,128)(2,1)S(1)}, u32[]{:S(2)}, u32[]{:S(2)}) collective-permute-start(bf16[64,2048]{1,0:T(8,128)(2,1)S(1)} %pad_maximum_fusion.5), channel_id=1, source_target_pairs={{0,8},{4,12},{8,0},{12,4},{1,9},{5,13},{9,1},{13,5},{2,10},{6,14},... | collective-permute-start | bytes 786440 | tf_op jit(solution)/shard_map/ppermute | solution.py:100
  39.9 7.6 %copy-start.3 = (bf16[64,8,16,128]{3,1,2,0:T(8,128)(2,1)S(1)}, bf16[64,8,16,128]{3,1,2,0:T(8,128)(2,1)}, u32[]{:S(2)}) copy-start(bf16[64,8,16,128]{3,1,2,0:T(8,128)(2,1)} %copy.19) | copy-start | bytes 6291460
  39.9 12.6 %collective-permute-start.19 = (bf16[32,2048]{1,0:T(8,128)(2,1)S(1)}, bf16[32,2048]{1,0:T(8,128)(2,1)S(1)}, u32[]{:S(2)}, u32[]{:S(2)}) collective-permute-start(bf16[32,2048]{1,0:T(8,128)(2,1)S(1)} %get-tuple-element.96), channel_id=1, source_target_pairs={{0,2},{1,3},{2,0},{3,1},{4,6},{5,7},{6,4},{7,5},{8,10},{9,11},{10,... | collective-permute-start | bytes 393224 | tf_op jit(solution)/shard_map/ppermute | solution.py:100
  43.1 9.4 %collective-permute-start.20 = (bf16[32,2048]{1,0:T(8,128)(2,1)S(1)}, bf16[32,2048]{1,0:T(8,128)(2,1)S(1)}, u32[]{:S(2)}, u32[]{:S(2)}) collective-permute-start(bf16[32,2048]{1,0:T(8,128)(2,1)S(1)} %get-tuple-element.97), channel_id=1, source_target_pairs={{0,3},{1,2},{2,1},{3,0},{4,7},{5,6},{6,5},{7,4},{8,11},{9,10},{10,... | collective-permute-start | bytes 393224 | tf_op jit(solution)/shard_map/ppermute | solution.py:100
  45.4 8.0 %collective-permute-start.9 = (bf16[128,2048]{1,0:T(8,128)(2,1)S(1)}, bf16[128,2048]{1,0:T(8,128)(2,1)S(1)}, u32[]{:S(2)}, u32[]{:S(2)}) collective-permute-start(bf16[128,2048]{1,0:T(8,128)(2,1)S(1)} %pad_maximum_fusion.1), channel_id=1, source_target_pairs={{0,4},{4,0},{8,12},{12,8},{1,5},{5,1},{9,13},{13,9},{2,6},{6,2},{1... | collective-permute-start | bytes 1572872 | tf_op jit(solution)/shard_map/ppermute | solution.py:100
  47.5 6.7 %collective-permute-start.13 = (bf16[128,2048]{1,0:T(8,128)(2,1)S(1)}, bf16[128,2048]{1,0:T(8,128)(2,1)S(1)}, u32[]{:S(2)}, u32[]{:S(2)}) collective-permute-start(bf16[128,2048]{1,0:T(8,128)(2,1)S(1)} %pad_maximum_fusion.2), channel_id=1, source_target_pairs={{0,4},{4,0},{8,12},{12,8},{1,5},{5,1},{9,13},{13,9},{2,6},{6,2},{1... | collective-permute-start | bytes 1572872 | tf_op jit(solution)/shard_map/ppermute | solution.py:100
  49.3 10.4 %collective-permute-start.17 = (bf16[64,2048]{1,0:T(8,128)(2,1)S(1)}, bf16[64,2048]{1,0:T(8,128)(2,1)S(1)}, u32[]{:S(2)}, u32[]{:S(2)}) collective-permute-start(bf16[64,2048]{1,0:T(8,128)(2,1)S(1)} %constant_dynamic-update-slice_fusion.2), channel_id=1, source_target_pairs={{0,8},{4,12},{8,0},{12,4},{1,9},{5,13},{9,1},{13,5},{2,10},{6,14},... | collective-permute-start | bytes 786440 | tf_op jit(solution)/shard_map/ppermute | solution.py:100
  52.6 11.1 %collective-permute-start.21 = (bf16[64,2048]{1,0:T(8,128)(2,1)S(1)}, bf16[64,2048]{1,0:T(8,128)(2,1)S(1)}, u32[]{:S(2)}, u32[]{:S(2)}) collective-permute-start(bf16[64,2048]{1,0:T(8,128)(2,1)S(1)} %constant_dynamic-update-slice_fusion.4), channel_id=1, source_target_pairs={{0,8},{4,12},{8,0},{12,4},{1,9},{5,13},{9,1},{13,5},{2,10},{6,14},... | collective-permute-start | bytes 786440 | tf_op jit(solution)/shard_map/ppermute | solution.py:100
  55.1 16.9 %collective-permute-start.16 = (bf16[1,4,32,512]{3,2,1,0:T(8,128)(2,1)S(1)}, bf16[1,4,32,512]{3,2,1,0:T(8,128)(2,1)S(1)}, u32[]{:S(2)}, u32[]{:S(2)}) collective-permute-start(bf16[1,4,32,512]{3,2,1,0:T(8,128)(2,1)S(1)} %get-tuple-element.123), channel_id=1, source_target_pairs={{0,3},{1,2},{2,1},{3,0},{4,7},{5,6},{6,5},{7,4},{8,11},{9,10},{10,... | collective-permute-start | bytes 393224 | tf_op jit(solution)/shard_map/ppermute | solution.py:100
  56.6 15.4 %collective-permute-start.15 = (bf16[1,4,32,512]{3,2,1,0:T(8,128)(2,1)S(1)}, bf16[1,4,32,512]{3,2,1,0:T(8,128)(2,1)S(1)}, u32[]{:S(2)}, u32[]{:S(2)}) collective-permute-start(bf16[1,4,32,512]{3,2,1,0:T(8,128)(2,1)S(1)} %get-tuple-element.89), channel_id=1, source_target_pairs={{0,2},{1,3},{2,0},{3,1},{4,6},{5,7},{6,4},{7,5},{8,10},{9,11},{10,... | collective-permute-start | bytes 393224 | tf_op jit(solution)/shard_map/ppermute | solution.py:100
  58.9 11.4 %collective-permute-start.14 = (bf16[1,4,32,512]{3,2,1,0:T(8,128)(2,1)S(1)}, bf16[1,4,32,512]{3,2,1,0:T(8,128)(2,1)S(1)}, u32[]{:S(2)}, u32[]{:S(2)}) collective-permute-start(bf16[1,4,32,512]{3,2,1,0:T(8,128)(2,1)S(1)} %get-tuple-element.90), channel_id=1, source_target_pairs={{0,1},{1,0},{2,3},{3,2},{4,5},{5,4},{6,7},{7,6},{8,9},{9,8},{10,11... | collective-permute-start | bytes 393224 | tf_op jit(solution)/shard_map/ppermute | solution.py:100
  63.7 2.0 %collective-permute-start.22 = (bf16[128,2048]{1,0:T(8,128)(2,1)S(1)}, bf16[128,2048]{1,0:T(8,128)(2,1)S(1)}, u32[]{:S(2)}, u32[]{:S(2)}) collective-permute-start(bf16[128,2048]{1,0:T(8,128)(2,1)S(1)} %pad_maximum_fusion.4), channel_id=1, source_target_pairs={{0,4},{4,0},{8,12},{12,8},{1,5},{5,1},{9,13},{13,9},{2,6},{6,2},{1... | collective-permute-start | bytes 1572872 | tf_op jit(solution)/shard_map/ppermute | solution.py:100
  63.8 2.7 %collective-permute-start.18 = (bf16[128,2048]{1,0:T(8,128)(2,1)S(1)}, bf16[128,2048]{1,0:T(8,128)(2,1)S(1)}, u32[]{:S(2)}, u32[]{:S(2)}) collective-permute-start(bf16[128,2048]{1,0:T(8,128)(2,1)S(1)} %pad_maximum_fusion.3), channel_id=1, source_target_pairs={{0,4},{4,0},{8,12},{12,8},{1,5},{5,1},{9,13},{13,9},{2,6},{6,2},{1... | collective-permute-start | bytes 1572872 | tf_op jit(solution)/shard_map/ppermute | solution.py:100
  67.5 12.7 %collective-permute-start.24 = (bf16[1,4,32,512]{3,2,1,0:T(8,128)(2,1)S(1)}, bf16[1,4,32,512]{3,2,1,0:T(8,128)(2,1)S(1)}, u32[]{:S(2)}, u32[]{:S(2)}) collective-permute-start(bf16[1,4,32,512]{3,2,1,0:T(8,128)(2,1)S(1)} %get-tuple-element.102), channel_id=1, source_target_pairs={{0,2},{1,3},{2,0},{3,1},{4,6},{5,7},{6,4},{7,5},{8,10},{9,11},{10,... | collective-permute-start | bytes 393224 | tf_op jit(solution)/shard_map/ppermute | solution.py:100
  69.3 10.9 %collective-permute-start.23 = (bf16[1,4,32,512]{3,2,1,0:T(8,128)(2,1)S(1)}, bf16[1,4,32,512]{3,2,1,0:T(8,128)(2,1)S(1)}, u32[]{:S(2)}, u32[]{:S(2)}) collective-permute-start(bf16[1,4,32,512]{3,2,1,0:T(8,128)(2,1)S(1)} %get-tuple-element.103), channel_id=1, source_target_pairs={{0,1},{1,0},{2,3},{3,2},{4,5},{5,4},{6,7},{7,6},{8,9},{9,8},{10,11... | collective-permute-start | bytes 393224 | tf_op jit(solution)/shard_map/ppermute | solution.py:100
  70.3 9.9 %collective-permute-start.25 = (bf16[1,4,32,512]{3,2,1,0:T(8,128)(2,1)S(1)}, bf16[1,4,32,512]{3,2,1,0:T(8,128)(2,1)S(1)}, u32[]{:S(2)}, u32[]{:S(2)}) collective-permute-start(bf16[1,4,32,512]{3,2,1,0:T(8,128)(2,1)S(1)} %get-tuple-element.122), channel_id=1, source_target_pairs={{0,3},{1,2},{2,1},{3,0},{4,7},{5,6},{6,5},{7,4},{8,11},{9,10},{10,... | collective-permute-start | bytes 393224 | tf_op jit(solution)/shard_map/ppermute | solution.py:100

commit v24 on v20

--- a/solution.py
+++ b/solution.py
@@ -178,7 +178,7 @@
         if chunk:
             source, pieces[0][-1], train_flat = lax.optimization_barrier((source, pieces[0][-1], train_flat))
         raw = {}
-        for mask in (range(slices) if chunk else reversed(range(slices))):
+        for mask in (reversed(range(slices)) if chunk else reversed(range(slices))):
             block = lax.dynamic_slice_in_dim(source, first + (here ^ mask) * each, each, 0)
             raw[mask], source = lax.optimization_barrier((block, source))
         pieces.append(exchanged(raw, slices))
@@ -227,7 +227,6 @@
     blocks = in_turn(blocks)
     left = exchanged(blocks, slices)
     last = [sum(left[mask][:, at ^ mask].astype(jnp.float32) for mask in range(slices)) for at in range(slices)]
-    came = after(came, *left[:1])
     whole = [sum(came[mask][:, at ^ mask].astype(jnp.float32) for mask in range(slices)) for at in range(slices)]
     for part, total in zip(parts, (whole, last)):
         total = jnp.stack(turned(total, here), axis=1)

time: 80.9 us -> 82.2 us (1.016)
  starting transfers between devices: 33.2 us -> 39.4 us
  waiting for transfers between devices: 27.9 us -> 23.1 us
    ppermute x26, starting transfers between devices: 33.2 us -> 39.4 us  [crossed(): return lax.ppermute(value, axis, [(at, at ^ mask) for at in range(size)])]
    ppermute x26, waiting for transfers between devices: 27.9 us -> 23.1 us  [crossed(): return lax.ppermute(value, axis, [(at, at ^ mask) for at in range(size)])]
  transfers between devices with their start and end apart: 26 -> 26, of which waited for: 8 -> 8; matrix products, arithmetic and copies ran while one was open for 15% -> 15% of each run, Pallas kernels for 6% -> 5%
where the time goes in v24:
time: 82.2 us; the launch traced here: 81.9 us
  starting transfers between devices  39.4 us (48%)
  waiting for transfers between devices  23.1 us (28%)
  matrix products  6.66 us (8%)
  local copies, waits for them, and re-layouts  6.26 us (8%)
  Pallas kernels  4.49 us (5%)
  other arithmetic  1.54 us (2%)
    ppermute x26, starting transfers between devices, crossed(): return lax.ppermute(value, axis, [(at, at ^ mask) for at in range(size)])  39.4 us
    ppermute x26, waiting for transfers between devices, crossed(): return lax.ppermute(value, axis, [(at, at ^ mask) for at in range(size)])  23.1 us
    dot_general x8, matrix products, products(): lax.dot_general(block, train_flat, contract, preferred_element_type=jnp.f...  6.66 us
    unnamed x17, local copies, waits for them, and re-layouts  5.2 us
    pallas_call x2, Pallas kernels, condition_fast(): pl.pallas_call(functools.partial(condition_kernel, slices, rows_here), gr...  4.49 us
  transfers between devices with their start and end apart: 26, of which 8 were waited for; matrix products, arithmetic and copies ran while one was open for 15% of the time, Pallas kernels for 5%

profile of v24, /device:TPU:0, one launch (start us, length us, event | category | flops | bytes accessed | tf_op | source)
XLA Modules:
  0.0 81.9 jit_solution(6240985159019173808)
XLA Ops:
  0.0 1.2 %copy-done = bf16[256,16,128]{2,1,0:T(8,128)(2,1)S(1)} copy-done((bf16[256,16,128]{2,1,0:T(8,128)(2,1)S(1)}, bf16[256,16,128]{2,1,0:T(8,128)(2,1)}, u32[]{:S(2)}) %copy-start) | copy-done | bytes 1048600
  1.2 5.1 %collective-permute-start = (bf16[32,16,128]{2,1,0:T(8,128)(2,1)S(1)}, bf16[32,16,128]{2,1,0:T(8,128)(2,1)S(1)}, u32[]{:S(2)}, u32[]{:S(2)}) collective-permute-start(bf16[32,16,128]{2,1,0:T(8,128)(2,1)S(1)} %constant_dynamic-slice_fusion.7), channel_id=1, source_target_pairs={{0,3},{1,2},{2,1},{3,0},{4,7},{5,6},{6,5},{7,4},{8,11},{9,10},{10,... | collective-permute-start | bytes 393224 | tf_op jit(solution)/shard_map/ppermute | solution.py:100
  6.4 0.1 collective-permute-start.2
  6.5 0.6 collective-permute-start.1
  7.1 0.7 fusion.8
  7.8 0.1 copy.13
  7.9 0.1 copy.14
  8.0 0.1 copy.15
  8.1 0.1 copy.16
  8.2 0.0 copy-start.1
  8.2 0.0 copy-start.2
  8.2 3.5 %copy.19 = bf16[64,8,16,128]{3,1,2,0:T(8,128)(2,1)} copy(bf16[64,8,16,128]{3,2,1,0:T(8,128)(2,1)} %bitcast.54) | data formatting | bytes 4194304
  11.7 0.1 pad_maximum_fusion.15
  11.8 0.1 copy.11.refs_4_
  11.9 0.0 copy-done.1
  11.9 0.1 copy.10
  12.1 2.2 %collective-permute-start.4 = (bf16[32,16,128]{2,1,0:T(8,128)(2,1)S(1)}, bf16[32,16,128]{2,1,0:T(8,128)(2,1)S(1)}, u32[]{:S(2)}, u32[]{:S(2)}) collective-permute-start(bf16[32,16,128]{2,1,0:T(8,128)(2,1)S(1)} %constant_dynamic-slice_fusion.1), channel_id=1, source_target_pairs={{0,1},{1,0},{2,3},{3,2},{4,5},{5,4},{6,7},{7,6},{8,9},{9,8},{10,11... | collective-permute-start | bytes 393224 | tf_op jit(solution)/shard_map/ppermute | solution.py:100
  14.3 2.2 %collective-permute-start.5 = (bf16[32,16,128]{2,1,0:T(8,128)(2,1)S(1)}, bf16[32,16,128]{2,1,0:T(8,128)(2,1)S(1)}, u32[]{:S(2)}, u32[]{:S(2)}) collective-permute-start(bf16[32,16,128]{2,1,0:T(8,128)(2,1)S(1)} %constant_dynamic-slice_fusion.2), channel_id=1, source_target_pairs={{0,2},{1,3},{2,0},{3,1},{4,6},{5,7},{6,4},{7,5},{8,10},{9,11},{10,... | collective-permute-start | bytes 393224 | tf_op jit(solution)/shard_map/ppermute | solution.py:100
  16.5 0.2 collective-permute-start.6
  16.7 0.0 collective-permute-done.2.refs_2_
  16.7 3.1 %collective-permute-done.1.refs_1_ = bf16[32,16,128]{2,1,0:T(8,128)(2,1)S(1)} collective-permute-done((bf16[32,16,128]{2,1,0:T(8,128)(2,1)S(1)}, bf16[32,16,128]{2,1,0:T(8,128)(2,1)S(1)}, u32[]{:S(2)}, u32[]{:S(2)}) %collective-permute-start.1) | collective-permute-done | bytes 131104 | tf_op jit(solution)/shard_map/ppermute | solution.py:100
  19.8 2.2 %shard_map.55 = (bf16[32,2048]{1,0:T(8,128)(2,1)S(1)}, bf16[32,2048]{1,0:T(8,128)(2,1)S(1)}, bf16[32,2048]{1,0:T(8,128)(2,1)S(1)}, bf16[32,2048]{1,0:T(8,128)(2,1)S(1)}) custom-call(bf16[32,16,128]{2,1,0:T(8,128)(2,1)S(1)} %collective-permute-done.refs_0_, bf16[32,16,128]{2,1,0:T(8,128)(2,1)S(1)} %collective-permute-done.1.refs_1_, ...), custom_call_target="tpu_custom_call" | custom-call | tf_op jit(solution)/shard_map/pallas_call | solution.py:75
  22.1 0.1 collective-permute-start.3
  22.2 1.3 %collective-permute-start.10 = (bf16[32,2048]{1,0:T(8,128)(2,1)S(1)}, bf16[32,2048]{1,0:T(8,128)(2,1)S(1)}, u32[]{:S(2)}, u32[]{:S(2)}) collective-permute-start(bf16[32,2048]{1,0:T(8,128)(2,1)S(1)} %get-tuple-element.83), channel_id=1, source_target_pairs={{0,2},{1,3},{2,0},{3,1},{4,6},{5,7},{6,4},{7,5},{8,10},{9,11},{10,... | collective-permute-start | bytes 393224 | tf_op jit(solution)/shard_map/ppermute | solution.py:100
  23.5 0.0 collective-permute-done.4.refs_2_
  23.5 3.2 %collective-permute-start.11 = (bf16[32,2048]{1,0:T(8,128)(2,1)S(1)}, bf16[32,2048]{1,0:T(8,128)(2,1)S(1)}, u32[]{:S(2)}, u32[]{:S(2)}) collective-permute-start(bf16[32,2048]{1,0:T(8,128)(2,1)S(1)} %get-tuple-element.84), channel_id=1, source_target_pairs={{0,3},{1,2},{2,1},{3,0},{4,7},{5,6},{6,5},{7,4},{8,11},{9,10},{10,... | collective-permute-start | bytes 393224 | tf_op jit(solution)/shard_map/ppermute | solution.py:100
  26.6 1.6 %collective-permute-done.5.refs_1_ = bf16[32,16,128]{2,1,0:T(8,128)(2,1)S(1)} collective-permute-done((bf16[32,16,128]{2,1,0:T(8,128)(2,1)S(1)}, bf16[32,16,128]{2,1,0:T(8,128)(2,1)S(1)}, u32[]{:S(2)}, u32[]{:S(2)}) %collective-permute-start.5) | collective-permute-done | bytes 131104 | tf_op jit(solution)/shard_map/ppermute | solution.py:100
  28.3 1.6 %collective-permute-start.8 = (bf16[64,2048]{1,0:T(8,128)(2,1)S(1)}, bf16[64,2048]{1,0:T(8,128)(2,1)S(1)}, u32[]{:S(2)}, u32[]{:S(2)}) collective-permute-start(bf16[64,2048]{1,0:T(8,128)(2,1)S(1)} %constant_dynamic-update-slice_fusion), channel_id=1, source_target_pairs={{0,8},{4,12},{8,0},{12,4},{1,9},{5,13},{9,1},{13,5},{2,10},{6,14},... | collective-permute-start | bytes 786440 | tf_op jit(solution)/shard_map/ppermute | solution.py:100
  29.9 2.2 %shard_map.56 = (bf16[32,2048]{1,0:T(8,128)(2,1)S(1)}, bf16[32,2048]{1,0:T(8,128)(2,1)S(1)}, bf16[32,2048]{1,0:T(8,128)(2,1)S(1)}, bf16[32,2048]{1,0:T(8,128)(2,1)S(1)}) custom-call(bf16[32,16,128]{2,1,0:T(8,128)(2,1)S(1)} %collective-permute-done.6.refs_0_, bf16[32,16,128]{2,1,0:T(8,128)(2,1)S(1)} %collective-permute-done.5.refs_1_, ...), custom_call_target="tpu_custom_call" | custom-call | tf_op jit(solution)/shard_map/pallas_call | solution.py:75
  32.1 7.6 %collective-permute-start.7 = (bf16[32,2048]{1,0:T(8,128)(2,1)S(1)}, bf16[32,2048]{1,0:T(8,128)(2,1)S(1)}, u32[]{:S(2)}, u32[]{:S(2)}) collective-permute-start(bf16[32,2048]{1,0:T(8,128)(2,1)S(1)} %get-tuple-element.77), channel_id=1, source_target_pairs={{0,1},{1,0},{2,3},{3,2},{4,5},{5,4},{6,7},{7,6},{8,9},{9,8},{10,11... | collective-permute-start | bytes 393224 | tf_op jit(solution)/shard_map/ppermute | solution.py:100
  39.7 0.6 collective-permute-start.12
  40.3 2.7 %collective-permute-start.19 = (bf16[32,2048]{1,0:T(8,128)(2,1)S(1)}, bf16[32,2048]{1,0:T(8,128)(2,1)S(1)}, u32[]{:S(2)}, u32[]{:S(2)}) collective-permute-start(bf16[32,2048]{1,0:T(8,128)(2,1)S(1)} %get-tuple-element.92), channel_id=1, source_target_pairs={{0,2},{1,3},{2,0},{3,1},{4,6},{5,7},{6,4},{7,5},{8,10},{9,11},{10,... | collective-permute-start | bytes 393224 | tf_op jit(solution)/shard_map/ppermute | solution.py:100
  43.1 1.3 %collective-permute-start.20 = (bf16[32,2048]{1,0:T(8,128)(2,1)S(1)}, bf16[32,2048]{1,0:T(8,128)(2,1)S(1)}, u32[]{:S(2)}, u32[]{:S(2)}) collective-permute-start(bf16[32,2048]{1,0:T(8,128)(2,1)S(1)} %get-tuple-element.93), channel_id=1, source_target_pairs={{0,3},{1,2},{2,1},{3,0},{4,7},{5,6},{6,5},{7,4},{8,11},{9,10},{10,... | collective-permute-start | bytes 393224 | tf_op jit(solution)/shard_map/ppermute | solution.py:100
  44.5 0.1 collective-permute-start.9
  44.5 1.6 %collective-permute-done.12 = bf16[64,2048]{1,0:T(8,128)(2,1)S(1)} collective-permute-done((bf16[64,2048]{1,0:T(8,128)(2,1)S(1)}, bf16[64,2048]{1,0:T(8,128)(2,1)S(1)}, u32[]{:S(2)}, u32[]{:S(2)}) %collective-permute-start.12) | collective-permute-done | bytes 262176 | tf_op jit(solution)/shard_map/ppermute | solution.py:100
  46.2 0.1 collective-permute-start.13
  46.3 0.8 %convolution_convert_fusion.5 = bf16[128,512]{1,0:T(8,128)(2,1)S(1)} fusion(bf16[128,2048]{1,0:T(8,128)(2,1)S(1)} %pad_maximum_fusion, bf16[512,2048]{1,0:T(8,128)(2,1)S(1)} %bitcast.46), kind=kOutput, calls=%fused_computation.6 | convolution fusion | flops 268500992 | bytes 2752512 | tf_op jit(solution)/shard_map/dot_general | solution.py:140
  47.1 0.8 %convolution_convert_fusion.4 = bf16[128,512]{1,0:T(8,128)(2,1)S(1)} fusion(bf16[128,2048]{1,0:T(8,128)(2,1)S(1)} %pad_maximum_fusion.1, bf16[512,2048]{1,0:T(8,128)(2,1)S(1)} %bitcast.47), kind=kOutput, calls=%fused_computation.5 | convolution fusion | flops 268500992 | bytes 2752512 | tf_op jit(solution)/shard_map/dot_general | solution.py:140
  48.0 0.6 collective-permute-start.17
  48.6 4.1 %collective-permute-done.19 = bf16[32,2048]{1,0:T(8,128)(2,1)S(1)} collective-permute-done((bf16[32,2048]{1,0:T(8,128)(2,1)S(1)}, bf16[32,2048]{1,0:T(8,128)(2,1)S(1)}, u32[]{:S(2)}, u32[]{:S(2)}) %collective-permute-start.19) | collective-permute-done | bytes 131104 | tf_op jit(solution)/shard_map/ppermute | solution.py:100
  52.8 0.7 collective-permute-start.21
  53.6 0.8 %convolution_convert_fusion.7 = bf16[128,512]{1,0:T(8,128)(2,1)S(1)} fusion(bf16[128,2048]{1,0:T(8,128)(2,1)S(1)} %collective-permute-done.9, bf16[512,2048]{1,0:T(8,128)(2,1)S(1)} %bitcast.48), kind=kOutput, calls=%fused_computation.8 | convolution fusion | flops 268500992 | bytes 2752512 | tf_op jit(solution)/shard_map/dot_general | solution.py:140
  54.4 0.8 %convolution_convert_fusion.6 = bf16[128,512]{1,0:T(8,128)(2,1)S(1)} fusion(bf16[128,2048]{1,0:T(8,128)(2,1)S(1)} %collective-permute-done.13, bf16[512,2048]{1,0:T(8,128)(2,1)S(1)} %bitcast.49), kind=kOutput, calls=%fused_computation.7 | convolution fusion | flops 268500992 | bytes 2752512 | tf_op jit(solution)/shard_map/dot_general | solution.py:140
  55.3 1.9 %collective-permute-start.16 = (bf16[1,4,32,512]{3,2,1,0:T(8,128)(2,1)S(1)}, bf16[1,4,32,512]{3,2,1,0:T(8,128)(2,1)S(1)}, u32[]{:S(2)}, u32[]{:S(2)}) collective-permute-start(bf16[1,4,32,512]{3,2,1,0:T(8,128)(2,1)S(1)} %get-tuple-element.115), channel_id=1, source_target_pairs={{0,3},{1,2},{2,1},{3,0},{4,7},{5,6},{6,5},{7,4},{8,11},{9,10},{10,... | collective-permute-start | bytes 393224 | tf_op jit(solution)/shard_map/ppermute | solution.py:100
  57.3 1.7 %collective-permute-start.15 = (bf16[1,4,32,512]{3,2,1,0:T(8,128)(2,1)S(1)}, bf16[1,4,32,512]{3,2,1,0:T(8,128)(2,1)S(1)}, u32[]{:S(2)}, u32[]{:S(2)}) collective-permute-start(bf16[1,4,32,512]{3,2,1,0:T(8,128)(2,1)S(1)} %get-tuple-element.85), channel_id=1, source_target_pairs={{0,2},{1,3},{2,0},{3,1},{4,6},{5,7},{6,4},{7,5},{8,10},{9,11},{10,... | collective-permute-start | bytes 393224 | tf_op jit(solution)/shard_map/ppermute | solution.py:100
  59.0 1.0 %collective-permute-start.14 = (bf16[1,4,32,512]{3,2,1,0:T(8,128)(2,1)S(1)}, bf16[1,4,32,512]{3,2,1,0:T(8,128)(2,1)S(1)}, u32[]{:S(2)}, u32[]{:S(2)}) collective-permute-start(bf16[1,4,32,512]{3,2,1,0:T(8,128)(2,1)S(1)} %get-tuple-element.86), channel_id=1, source_target_pairs={{0,1},{1,0},{2,3},{3,2},{4,5},{5,4},{6,7},{7,6},{8,9},{9,8},{10,11... | collective-permute-start | bytes 393224 | tf_op jit(solution)/shard_map/ppermute | solution.py:100
  60.0 0.1 collective-permute-start.18
  60.0 0.8 %convolution_convert_fusion.1 = bf16[128,512]{1,0:T(8,128)(2,1)S(1)} fusion(bf16[128,2048]{1,0:T(8,128)(2,1)S(1)} %pad_maximum_fusion.2, bf16[512,2048]{1,0:T(8,128)(2,1)S(1)} %bitcast.50), kind=kOutput, calls=%fused_computation.2 | convolution fusion | flops 268500992 | bytes 2752512 | tf_op jit(solution)/shard_map/dot_general | solution.py:140
  60.9 1.5 %collective-permute-done.21 = bf16[64,2048]{1,0:T(8,128)(2,1)S(1)} collective-permute-done((bf16[64,2048]{1,0:T(8,128)(2,1)S(1)}, bf16[64,2048]{1,0:T(8,128)(2,1)S(1)}, u32[]{:S(2)}, u32[]{:S(2)}) %collective-permute-start.21) | collective-permute-done | bytes 262176 | tf_op jit(solution)/shard_map/ppermute | solution.py:100
  62.5 0.1 collective-permute-start.22
  62.6 0.8 %convolution_convert_fusion = bf16[128,512]{1,0:T(8,128)(2,1)S(1)} fusion(bf16[128,2048]{1,0:T(8,128)(2,1)S(1)} %pad_maximum_fusion.3, bf16[512,2048]{1,0:T(8,128)(2,1)S(1)} %bitcast.51), kind=kOutput, calls=%fused_computation.1 | convolution fusion | flops 268500992 | bytes 2752512 | tf_op jit(solution)/shard_map/dot_general | solution.py:140
  63.4 0.8 %convolution_convert_fusion.3 = bf16[128,512]{1,0:T(8,128)(2,1)S(1)} fusion(bf16[128,2048]{1,0:T(8,128)(2,1)S(1)} %collective-permute-done.18, bf16[512,2048]{1,0:T(8,128)(2,1)S(1)} %bitcast.52), kind=kOutput, calls=%fused_computation.4 | convolution fusion | flops 268500992 | bytes 2752512 | tf_op jit(solution)/shard_map/dot_general | solution.py:140
  64.3 0.2 collective-permute-done.22
  64.4 0.8 %convolution_convert_fusion.2 = bf16[128,512]{1,0:T(8,128)(2,1)S(1)} fusion(bf16[128,2048]{1,0:T(8,128)(2,1)S(1)} %collective-permute-done.22, bf16[512,2048]{1,0:T(8,128)(2,1)S(1)} %bitcast.53), kind=kOutput, calls=%fused_computation.3 | convolution fusion | flops 268500992 | bytes 2752512 | tf_op jit(solution)/shard_map/dot_general | solution.py:140
  65.3 0.1 broadcast_select_fusion.9
  65.4 2.3 %collective-permute-start.25 = (bf16[1,4,32,512]{3,2,1,0:T(8,128)(2,1)S(1)}, bf16[1,4,32,512]{3,2,1,0:T(8,128)(2,1)S(1)}, u32[]{:S(2)}, u32[]{:S(2)}) collective-permute-start(bf16[1,4,32,512]{3,2,1,0:T(8,128)(2,1)S(1)} %get-tuple-element.114), channel_id=1, source_target_pairs={{0,3},{1,2},{2,1},{3,0},{4,7},{5,6},{6,5},{7,4},{8,11},{9,10},{10,... | collective-permute-start | bytes 393224 | tf_op jit(solution)/shard_map/ppermute | solution.py:100
  67.6 1.0 %collective-permute-start.24 = (bf16[1,4,32,512]{3,2,1,0:T(8,128)(2,1)S(1)}, bf16[1,4,32,512]{3,2,1,0:T(8,128)(2,1)S(1)}, u32[]{:S(2)}, u32[]{:S(2)}) collective-permute-start(bf16[1,4,32,512]{3,2,1,0:T(8,128)(2,1)S(1)} %get-tuple-element.98), channel_id=1, source_target_pairs={{0,2},{1,3},{2,0},{3,1},{4,6},{5,7},{6,4},{7,5},{8,10},{9,11},{10,... | collective-permute-start | bytes 393224 | tf_op jit(solution)/shard_map/ppermute | solution.py:100
  68.7 1.2 %collective-permute-start.23 = (bf16[1,4,32,512]{3,2,1,0:T(8,128)(2,1)S(1)}, bf16[1,4,32,512]{3,2,1,0:T(8,128)(2,1)S(1)}, u32[]{:S(2)}, u32[]{:S(2)}) collective-permute-start(bf16[1,4,32,512]{3,2,1,0:T(8,128)(2,1)S(1)} %get-tuple-element.99), channel_id=1, source_target_pairs={{0,1},{1,0},{2,3},{3,2},{4,5},{5,4},{6,7},{7,6},{8,9},{9,8},{10,11... | collective-permute-start | bytes 393224 | tf_op jit(solution)/shard_map/ppermute | solution.py:100
  69.9 0.1 broadcast_select_fusion.31
  70.0 6.5 %collective-permute-done.23 = bf16[1,4,32,512]{3,2,1,0:T(8,128)(2,1)S(1)} collective-permute-done((bf16[1,4,32,512]{3,2,1,0:T(8,128)(2,1)S(1)}, bf16[1,4,32,512]{3,2,1,0:T(8,128)(2,1)S(1)}, u32[]{:S(2)}, u32[]{:S(2)}) %collective-permute-start.23) | collective-permute-done | bytes 131104 | tf_op jit(solution)/shard_map/ppermute | solution.py:100
  76.6 4.3 %collective-permute-done.24 = bf16[1,4,32,512]{3,2,1,0:T(8,128)(2,1)S(1)} collective-permute-done((bf16[1,4,32,512]{3,2,1,0:T(8,128)(2,1)S(1)}, bf16[1,4,32,512]{3,2,1,0:T(8,128)(2,1)S(1)}, u32[]{:S(2)}, u32[]{:S(2)}) %collective-permute-start.24) | collective-permute-done | bytes 131104 | tf_op jit(solution)/shard_map/ppermute | solution.py:100
  80.9 0.1 broadcast_select_fusion.27
  81.0 0.1 broadcast_select_fusion.26
  81.1 0.8 %maximum_bitcast_fusion = f32[256,512]{1,0:T(8,128)} fusion(f32[1,128,512]{2,1,0:T(8,128)S(1)} %bitcast.56, f32[1,128,512]{2,1,0:T(8,128)S(1)} %bitcast.55), kind=kLoop, calls=%fused_computation.13 | loop fusion | flops 131072 | bytes 1048576 | tf_op jit(solution)/shard_map/reshape | solution.py:235
  (53 shorter events, 0.7 us)
Async XLA Ops:
  0.0 1.2 %copy-start = (bf16[256,16,128]{2,1,0:T(8,128)(2,1)S(1)}, bf16[256,16,128]{2,1,0:T(8,128)(2,1)}, u32[]{:S(2)}) copy-start(bf16[256,16,128]{2,1,0:T(8,128)(2,1)} %param.5) | copy-start | bytes 3145732
  1.2 10.8 %collective-permute-start = (bf16[32,16,128]{2,1,0:T(8,128)(2,1)S(1)}, bf16[32,16,128]{2,1,0:T(8,128)(2,1)S(1)}, u32[]{:S(2)}, u32[]{:S(2)}) collective-permute-start(bf16[32,16,128]{2,1,0:T(8,128)(2,1)S(1)} %constant_dynamic-slice_fusion.7), channel_id=1, source_target_pairs={{0,3},{1,2},{2,1},{3,0},{4,7},{5,6},{6,5},{7,4},{8,11},{9,10},{10,... | collective-permute-start | bytes 393224 | tf_op jit(solution)/shard_map/ppermute | solution.py:100
  6.4 10.4 %collective-permute-start.2 = (bf16[32,16,128]{2,1,0:T(8,128)(2,1)S(1)}, bf16[32,16,128]{2,1,0:T(8,128)(2,1)S(1)}, u32[]{:S(2)}, u32[]{:S(2)}) collective-permute-start(bf16[32,16,128]{2,1,0:T(8,128)(2,1)S(1)} %constant_dynamic-slice_fusion.5), channel_id=1, source_target_pairs={{0,1},{1,0},{2,3},{3,2},{4,5},{5,4},{6,7},{7,6},{8,9},{9,8},{10,11... | collective-permute-start | bytes 393224 | tf_op jit(solution)/shard_map/ppermute | solution.py:100
  6.5 13.4 %collective-permute-start.1 = (bf16[32,16,128]{2,1,0:T(8,128)(2,1)S(1)}, bf16[32,16,128]{2,1,0:T(8,128)(2,1)S(1)}, u32[]{:S(2)}, u32[]{:S(2)}) collective-permute-start(bf16[32,16,128]{2,1,0:T(8,128)(2,1)S(1)} %constant_dynamic-slice_fusion.6), channel_id=1, source_target_pairs={{0,2},{1,3},{2,0},{3,1},{4,6},{5,7},{6,4},{7,5},{8,10},{9,11},{10,... | collective-permute-start | bytes 393224 | tf_op jit(solution)/shard_map/ppermute | solution.py:100
  8.2 3.7 %copy-start.1 = (f32[128,128]{1,0:T(8,128)S(1)}, f32[128,128]{1,0:T(8,128)}, u32[]{:S(2)}) copy-start(f32[128,128]{1,0:T(8,128)} %refs_6_.3) | copy-start | bytes 196612
  8.2 11.6 %copy-start.2 = (f32[64,128]{1,0:T(8,128)S(1)}, f32[64,128]{1,0:T(8,128)}, u32[]{:S(2)}) copy-start(f32[64,128]{1,0:T(8,128)} %refs_8_.3) | copy-start | bytes 98308
  12.1 11.3 %collective-permute-start.4 = (bf16[32,16,128]{2,1,0:T(8,128)(2,1)S(1)}, bf16[32,16,128]{2,1,0:T(8,128)(2,1)S(1)}, u32[]{:S(2)}, u32[]{:S(2)}) collective-permute-start(bf16[32,16,128]{2,1,0:T(8,128)(2,1)S(1)} %constant_dynamic-slice_fusion.1), channel_id=1, source_target_pairs={{0,1},{1,0},{2,3},{3,2},{4,5},{5,4},{6,7},{7,6},{8,9},{9,8},{10,11... | collective-permute-start | bytes 393224 | tf_op jit(solution)/shard_map/ppermute | solution.py:100
  14.3 14.0 %collective-permute-start.5 = (bf16[32,16,128]{2,1,0:T(8,128)(2,1)S(1)}, bf16[32,16,128]{2,1,0:T(8,128)(2,1)S(1)}, u32[]{:S(2)}, u32[]{:S(2)}) collective-permute-start(bf16[32,16,128]{2,1,0:T(8,128)(2,1)S(1)} %constant_dynamic-slice_fusion.2), channel_id=1, source_target_pairs={{0,2},{1,3},{2,0},{3,1},{4,6},{5,7},{6,4},{7,5},{8,10},{9,11},{10,... | collective-permute-start | bytes 393224 | tf_op jit(solution)/shard_map/ppermute | solution.py:100
  16.5 11.7 %collective-permute-start.6 = (bf16[32,16,128]{2,1,0:T(8,128)(2,1)S(1)}, bf16[32,16,128]{2,1,0:T(8,128)(2,1)S(1)}, u32[]{:S(2)}, u32[]{:S(2)}) collective-permute-start(bf16[32,16,128]{2,1,0:T(8,128)(2,1)S(1)} %constant_dynamic-slice_fusion.3), channel_id=1, source_target_pairs={{0,3},{1,2},{2,1},{3,0},{4,7},{5,6},{6,5},{7,4},{8,11},{9,10},{10,... | collective-permute-start | bytes 393224 | tf_op jit(solution)/shard_map/ppermute | solution.py:100
  22.1 6.2 %collective-permute-start.3 = (bf16[32,2048]{1,0:T(8,128)(2,1)S(1)}, bf16[32,2048]{1,0:T(8,128)(2,1)S(1)}, u32[]{:S(2)}, u32[]{:S(2)}) collective-permute-start(bf16[32,2048]{1,0:T(8,128)(2,1)S(1)} %get-tuple-element.63), channel_id=1, source_target_pairs={{0,1},{1,0},{2,3},{3,2},{4,5},{5,4},{6,7},{7,6},{8,9},{9,8},{10,11... | collective-permute-start | bytes 393224 | tf_op jit(solution)/shard_map/ppermute | solution.py:100
  22.2 17.5 %collective-permute-start.10 = (bf16[32,2048]{1,0:T(8,128)(2,1)S(1)}, bf16[32,2048]{1,0:T(8,128)(2,1)S(1)}, u32[]{:S(2)}, u32[]{:S(2)}) collective-permute-start(bf16[32,2048]{1,0:T(8,128)(2,1)S(1)} %get-tuple-element.83), channel_id=1, source_target_pairs={{0,2},{1,3},{2,0},{3,1},{4,6},{5,7},{6,4},{7,5},{8,10},{9,11},{10,... | collective-permute-start | bytes 393224 | tf_op jit(solution)/shard_map/ppermute | solution.py:100
  23.5 16.3 %collective-permute-start.11 = (bf16[32,2048]{1,0:T(8,128)(2,1)S(1)}, bf16[32,2048]{1,0:T(8,128)(2,1)S(1)}, u32[]{:S(2)}, u32[]{:S(2)}) collective-permute-start(bf16[32,2048]{1,0:T(8,128)(2,1)S(1)} %get-tuple-element.84), channel_id=1, source_target_pairs={{0,3},{1,2},{2,1},{3,0},{4,7},{5,6},{6,5},{7,4},{8,11},{9,10},{10,... | collective-permute-start | bytes 393224 | tf_op jit(solution)/shard_map/ppermute | solution.py:100
  28.3 16.1 %collective-permute-start.8 = (bf16[64,2048]{1,0:T(8,128)(2,1)S(1)}, bf16[64,2048]{1,0:T(8,128)(2,1)S(1)}, u32[]{:S(2)}, u32[]{:S(2)}) collective-permute-start(bf16[64,2048]{1,0:T(8,128)(2,1)S(1)} %constant_dynamic-update-slice_fusion), channel_id=1, source_target_pairs={{0,8},{4,12},{8,0},{12,4},{1,9},{5,13},{9,1},{13,5},{2,10},{6,14},... | collective-permute-start | bytes 786440 | tf_op jit(solution)/shard_map/ppermute | solution.py:100
  32.1 12.3 %collective-permute-start.7 = (bf16[32,2048]{1,0:T(8,128)(2,1)S(1)}, bf16[32,2048]{1,0:T(8,128)(2,1)S(1)}, u32[]{:S(2)}, u32[]{:S(2)}) collective-permute-start(bf16[32,2048]{1,0:T(8,128)(2,1)S(1)} %get-tuple-element.77), channel_id=1, source_target_pairs={{0,1},{1,0},{2,3},{3,2},{4,5},{5,4},{6,7},{7,6},{8,9},{9,8},{10,11... | collective-permute-start | bytes 393224 | tf_op jit(solution)/shard_map/ppermute | solution.py:100
  39.7 6.4 %collective-permute-start.12 = (bf16[64,2048]{1,0:T(8,128)(2,1)S(1)}, bf16[64,2048]{1,0:T(8,128)(2,1)S(1)}, u32[]{:S(2)}, u32[]{:S(2)}) collective-permute-start(bf16[64,2048]{1,0:T(8,128)(2,1)S(1)} %pad_maximum_fusion.4), channel_id=1, source_target_pairs={{0,8},{4,12},{8,0},{12,4},{1,9},{5,13},{9,1},{13,5},{2,10},{6,14},... | collective-permute-start | bytes 786440 | tf_op jit(solution)/shard_map/ppermute | solution.py:100
  40.3 6.0 %copy-start.3 = (bf16[64,8,16,128]{3,1,2,0:T(8,128)(2,1)S(1)}, bf16[64,8,16,128]{3,1,2,0:T(8,128)(2,1)}, u32[]{:S(2)}) copy-start(bf16[64,8,16,128]{3,1,2,0:T(8,128)(2,1)} %copy.19) | copy-start | bytes 6291460
  40.3 12.4 %collective-permute-start.19 = (bf16[32,2048]{1,0:T(8,128)(2,1)S(1)}, bf16[32,2048]{1,0:T(8,128)(2,1)S(1)}, u32[]{:S(2)}, u32[]{:S(2)}) collective-permute-start(bf16[32,2048]{1,0:T(8,128)(2,1)S(1)} %get-tuple-element.92), channel_id=1, source_target_pairs={{0,2},{1,3},{2,0},{3,1},{4,6},{5,7},{6,4},{7,5},{8,10},{9,11},{10,... | collective-permute-start | bytes 393224 | tf_op jit(solution)/shard_map/ppermute | solution.py:100
  43.1 9.7 %collective-permute-start.20 = (bf16[32,2048]{1,0:T(8,128)(2,1)S(1)}, bf16[32,2048]{1,0:T(8,128)(2,1)S(1)}, u32[]{:S(2)}, u32[]{:S(2)}) collective-permute-start(bf16[32,2048]{1,0:T(8,128)(2,1)S(1)} %get-tuple-element.93), channel_id=1, source_target_pairs={{0,3},{1,2},{2,1},{3,0},{4,7},{5,6},{6,5},{7,4},{8,11},{9,10},{10,... | collective-permute-start | bytes 393224 | tf_op jit(solution)/shard_map/ppermute | solution.py:100
  44.5 9.1 %collective-permute-start.9 = (bf16[128,2048]{1,0:T(8,128)(2,1)S(1)}, bf16[128,2048]{1,0:T(8,128)(2,1)S(1)}, u32[]{:S(2)}, u32[]{:S(2)}) collective-permute-start(bf16[128,2048]{1,0:T(8,128)(2,1)S(1)} %pad_maximum_fusion), channel_id=1, source_target_pairs={{0,4},{4,0},{8,12},{12,8},{1,5},{5,1},{9,13},{13,9},{2,6},{6,2},{1... | collective-permute-start | bytes 1572872 | tf_op jit(solution)/shard_map/ppermute | solution.py:100
  46.2 8.2 %collective-permute-start.13 = (bf16[128,2048]{1,0:T(8,128)(2,1)S(1)}, bf16[128,2048]{1,0:T(8,128)(2,1)S(1)}, u32[]{:S(2)}, u32[]{:S(2)}) collective-permute-start(bf16[128,2048]{1,0:T(8,128)(2,1)S(1)} %pad_maximum_fusion.1), channel_id=1, source_target_pairs={{0,4},{4,0},{8,12},{12,8},{1,5},{5,1},{9,13},{13,9},{2,6},{6,2},{1... | collective-permute-start | bytes 1572872 | tf_op jit(solution)/shard_map/ppermute | solution.py:100
  48.0 11.9 %collective-permute-start.17 = (bf16[64,2048]{1,0:T(8,128)(2,1)S(1)}, bf16[64,2048]{1,0:T(8,128)(2,1)S(1)}, u32[]{:S(2)}, u32[]{:S(2)}) collective-permute-start(bf16[64,2048]{1,0:T(8,128)(2,1)S(1)} %constant_dynamic-update-slice_fusion.2), channel_id=1, source_target_pairs={{0,8},{4,12},{8,0},{12,4},{1,9},{5,13},{9,1},{13,5},{2,10},{6,14},... | collective-permute-start | bytes 786440 | tf_op jit(solution)/shard_map/ppermute | solution.py:100
  52.8 9.6 %collective-permute-start.21 = (bf16[64,2048]{1,0:T(8,128)(2,1)S(1)}, bf16[64,2048]{1,0:T(8,128)(2,1)S(1)}, u32[]{:S(2)}, u32[]{:S(2)}) collective-permute-start(bf16[64,2048]{1,0:T(8,128)(2,1)S(1)} %constant_dynamic-update-slice_fusion.4), channel_id=1, source_target_pairs={{0,8},{4,12},{8,0},{12,4},{1,9},{5,13},{9,1},{13,5},{2,10},{6,14},... | collective-permute-start | bytes 786440 | tf_op jit(solution)/shard_map/ppermute | solution.py:100
  55.3 14.6 %collective-permute-start.16 = (bf16[1,4,32,512]{3,2,1,0:T(8,128)(2,1)S(1)}, bf16[1,4,32,512]{3,2,1,0:T(8,128)(2,1)S(1)}, u32[]{:S(2)}, u32[]{:S(2)}) collective-permute-start(bf16[1,4,32,512]{3,2,1,0:T(8,128)(2,1)S(1)} %get-tuple-element.115), channel_id=1, source_target_pairs={{0,3},{1,2},{2,1},{3,0},{4,7},{5,6},{6,5},{7,4},{8,11},{9,10},{10,... | collective-permute-start | bytes 393224 | tf_op jit(solution)/shard_map/ppermute | solution.py:100
  57.3 12.7 %collective-permute-start.15 = (bf16[1,4,32,512]{3,2,1,0:T(8,128)(2,1)S(1)}, bf16[1,4,32,512]{3,2,1,0:T(8,128)(2,1)S(1)}, u32[]{:S(2)}, u32[]{:S(2)}) collective-permute-start(bf16[1,4,32,512]{3,2,1,0:T(8,128)(2,1)S(1)} %get-tuple-element.85), channel_id=1, source_target_pairs={{0,2},{1,3},{2,0},{3,1},{4,6},{5,7},{6,4},{7,5},{8,10},{9,11},{10,... | collective-permute-start | bytes 393224 | tf_op jit(solution)/shard_map/ppermute | solution.py:100
  59.0 9.7 %collective-permute-start.14 = (bf16[1,4,32,512]{3,2,1,0:T(8,128)(2,1)S(1)}, bf16[1,4,32,512]{3,2,1,0:T(8,128)(2,1)S(1)}, u32[]{:S(2)}, u32[]{:S(2)}) collective-permute-start(bf16[1,4,32,512]{3,2,1,0:T(8,128)(2,1)S(1)} %get-tuple-element.86), channel_id=1, source_target_pairs={{0,1},{1,0},{2,3},{3,2},{4,5},{5,4},{6,7},{7,6},{8,9},{9,8},{10,11... | collective-permute-start | bytes 393224 | tf_op jit(solution)/shard_map/ppermute | solution.py:100
  60.0 3.5 %collective-permute-start.18 = (bf16[128,2048]{1,0:T(8,128)(2,1)S(1)}, bf16[128,2048]{1,0:T(8,128)(2,1)S(1)}, u32[]{:S(2)}, u32[]{:S(2)}) collective-permute-start(bf16[128,2048]{1,0:T(8,128)(2,1)S(1)} %pad_maximum_fusion.2), channel_id=1, source_target_pairs={{0,4},{4,0},{8,12},{12,8},{1,5},{5,1},{9,13},{13,9},{2,6},{6,2},{1... | collective-permute-start | bytes 1572872 | tf_op jit(solution)/shard_map/ppermute | solution.py:100
  62.5 2.0 %collective-permute-start.22 = (bf16[128,2048]{1,0:T(8,128)(2,1)S(1)}, bf16[128,2048]{1,0:T(8,128)(2,1)S(1)}, u32[]{:S(2)}, u32[]{:S(2)}) collective-permute-start(bf16[128,2048]{1,0:T(8,128)(2,1)S(1)} %pad_maximum_fusion.3), channel_id=1, source_target_pairs={{0,4},{4,0},{8,12},{12,8},{1,5},{5,1},{9,13},{13,9},{2,6},{6,2},{1... | collective-permute-start | bytes 1572872 | tf_op jit(solution)/shard_map/ppermute | solution.py:100
  65.4 15.6 %collective-permute-start.25 = (bf16[1,4,32,512]{3,2,1,0:T(8,128)(2,1)S(1)}, bf16[1,4,32,512]{3,2,1,0:T(8,128)(2,1)S(1)}, u32[]{:S(2)}, u32[]{:S(2)}) collective-permute-start(bf16[1,4,32,512]{3,2,1,0:T(8,128)(2,1)S(1)} %get-tuple-element.114), channel_id=1, source_target_pairs={{0,3},{1,2},{2,1},{3,0},{4,7},{5,6},{6,5},{7,4},{8,11},{9,10},{10,... | collective-permute-start | bytes 393224 | tf_op jit(solution)/shard_map/ppermute | solution.py:100
  67.6 13.3 %collective-permute-start.24 = (bf16[1,4,32,512]{3,2,1,0:T(8,128)(2,1)S(1)}, bf16[1,4,32,512]{3,2,1,0:T(8,128)(2,1)S(1)}, u32[]{:S(2)}, u32[]{:S(2)}) collective-permute-start(bf16[1,4,32,512]{3,2,1,0:T(8,128)(2,1)S(1)} %get-tuple-element.98), channel_id=1, source_target_pairs={{0,2},{1,3},{2,0},{3,1},{4,6},{5,7},{6,4},{7,5},{8,10},{9,11},{10,... | collective-permute-start | bytes 393224 | tf_op jit(solution)/shard_map/ppermute | solution.py:100
  68.7 7.9 %collective-permute-start.23 = (bf16[1,4,32,512]{3,2,1,0:T(8,128)(2,1)S(1)}, bf16[1,4,32,512]{3,2,1,0:T(8,128)(2,1)S(1)}, u32[]{:S(2)}, u32[]{:S(2)}) collective-permute-start(bf16[1,4,32,512]{3,2,1,0:T(8,128)(2,1)S(1)} %get-tuple-element.99), channel_id=1, source_target_pairs={{0,1},{1,0},{2,3},{3,2},{4,5},{5,4},{6,7},{7,6},{8,9},{9,8},{10,11... | collective-permute-start | bytes 393224 | tf_op jit(solution)/shard_map/ppermute | solution.py:100
